TPU v7x, 32 devices: a whole 2x2x4 slice. The times are simulated.
32 devices in a mesh: expert: 8 (over y, x, core), feat: 4 (over z).
Axes of the slice: x: 2, y: 2, z: 4, core: 2. Of those that a mesh axis runs over, the one named last changes fastest.
Arguments:
- tokens: bfloat16 [512, 2304], P('expert'), may hold values from -6 to 6
- expert_ids: int32 [512, 8], P(('expert', 'feat')), may hold values from 0 to 31, all different within a row; in each aligned block of 16 rows (0 to 15, 16 to 31, ...) at most 8 rows name the same one
- gate_weights: float32 [512, 8], P(('expert', 'feat')), may hold values from 0.1 to 0.6
- expert_gate: bfloat16 [32, 2304, 1024], P(('expert', 'feat')), may hold values from -0.125 to 0.125
- expert_up: bfloat16 [32, 2304, 1024], P(('expert', 'feat')), may hold values from -0.125 to 0.125
- expert_down: bfloat16 [32, 1024, 2304], P(('expert', 'feat')), may hold values from -0.1875 to 0.1875
- shared_gate: bfloat16 [2304, 1024], P(None, 'feat'), may hold values from -0.125 to 0.125
- shared_up: bfloat16 [2304, 1024], P(None, 'feat'), may hold values from -0.125 to 0.125
- shared_down: bfloat16 [1024, 2304], P('feat'), may hold values from -0.1875 to 0.1875
- encoder: bfloat16 [2304, 16384], P(None, ('expert', 'feat')), may hold values from -0.125 to 0.125
- encoder_bias: float32 [16384], P(('expert', 'feat')), may hold values from -0.6 to 0.2
- decoder: bfloat16 [16384, 2304], P(('expert', 'feat')), may hold values from -0.046875 to 0.046875
- decoder_bias: float32 [2304], replicated, may hold values from -3 to 3
Outputs:
- features: bfloat16 [512, 16384], P(None, ('expert', 'feat'))
- reconstruction: float32 [512, 2304], P(('expert', 'feat'))
Inputs may be any that keep to these rules, and one draw needn't show every extreme that they name: `expert_ids`: each row names 8 different experts. Within each aligned block of 16 rows (the rows of one device) no expert is named by more than 8 rows, a bound that some block reaches.
All inputs are finite; a program needn't handle non-finite values.
Results may differ from a plain program's by a relative error of at most 0.012.
Values may be sent and summed in bfloat16 or wider, within the bound.
No kernel may reach another device: no remote copies, remote signals or barrier semaphores. Data moves between devices by JAX's collectives and lax.ppermute only.
A program may use at most 128 MiB of HBM per device.

v0:
```python
import jax
import jax.numpy as jnp
from jax import lax
from jax.sharding import PartitionSpec as P


def run_experts(received, expert_gate, expert_up, expert_down):
    gate_proj = jnp.einsum(
        "sjcd,jdh->sjch", received, expert_gate, preferred_element_type=jnp.float32
    )
    up_proj = jnp.einsum("sjcd,jdh->sjch", received, expert_up, preferred_element_type=jnp.float32)
    hidden = (jax.nn.silu(gate_proj) * up_proj).astype(jnp.bfloat16)
    return jnp.einsum(
        "sjch,jhd->sjcd", hidden, expert_down, preferred_element_type=jnp.float32
    ).astype(jnp.bfloat16)


def shards(
    tokens,
    expert_ids,
    gate_weights,
    expert_gate,
    expert_up,
    expert_down,
    shared_gate,
    shared_up,
    shared_down,
    encoder,
    encoder_bias,
    decoder,
    decoder_bias,
):
    devices = lax.axis_size(("expert", "feat"))
    own_rows = expert_ids.shape[0]
    top_count = expert_ids.shape[1]
    width = tokens.shape[1]
    local_experts = expert_gate.shape[0]
    experts = local_experts * devices
    cap_slots = max(2, 2 * own_rows * top_count // experts)
    my_tokens = lax.dynamic_slice_in_dim(tokens, lax.axis_index("feat") * own_rows, own_rows, 0)
    flat_ids = expert_ids.reshape(-1)
    onehot = (flat_ids[:, None] == jnp.arange(experts, dtype=jnp.int32)[None, :]).astype(jnp.int32)
    earlier = jnp.cumsum(onehot, axis=0) - onehot
    slot_index = jnp.sum(earlier * onehot, axis=1)
    places = flat_ids * cap_slots + slot_index
    token_owner = jnp.repeat(jnp.arange(own_rows, dtype=jnp.int32), top_count)
    place_hot = (
        places[:, None] == jnp.arange(experts * cap_slots, dtype=jnp.int32)[None, :]
    ).astype(jnp.float32)
    token_hot = (token_owner[:, None] == jnp.arange(own_rows, dtype=jnp.int32)[None, :]).astype(
        jnp.float32
    )
    dispatch_map = jnp.einsum("ps,pt->st", place_hot, token_hot).astype(jnp.bfloat16)
    weighted_hot = token_hot * gate_weights.reshape(-1)[:, None]
    combine_map = jnp.einsum("pt,ps->ts", weighted_hot, place_hot, precision=lax.Precision.HIGHEST)
    outgoing = jnp.dot(dispatch_map, my_tokens, preferred_element_type=jnp.float32).astype(
        jnp.bfloat16
    )
    outgoing = outgoing.reshape(devices, local_experts, cap_slots, width)
    served = run_experts(
        lax.all_to_all(outgoing, ("expert", "feat"), split_axis=0, concat_axis=0, tiled=True),
        expert_gate,
        expert_up,
        expert_down,
    )
    returned = lax.all_to_all(served, ("expert", "feat"), split_axis=0, concat_axis=0, tiled=True)
    returned_rows = returned.reshape(experts * cap_slots, width).astype(jnp.float32)
    routed = jnp.dot(combine_map, returned_rows, precision=lax.Precision.HIGHEST).astype(
        jnp.bfloat16
    )
    shared_gate_proj = jnp.dot(tokens, shared_gate, preferred_element_type=jnp.float32)
    shared_up_proj = jnp.dot(tokens, shared_up, preferred_element_type=jnp.float32)
    shared_hidden = (jax.nn.silu(shared_gate_proj) * shared_up_proj).astype(jnp.bfloat16)
    block_rows = shared_hidden
    shared_out = lax.psum_scatter(
        jnp.dot(block_rows, shared_down, preferred_element_type=jnp.float32),
        "feat",
        scatter_dimension=0,
        tiled=True,
    ).astype(jnp.bfloat16)
    moe_out = (routed.astype(jnp.float32) + shared_out.astype(jnp.float32)).astype(jnp.bfloat16)
    scores = (
        jnp.dot(
            lax.all_gather(moe_out, ("expert", "feat"), axis=0, tiled=True),
            encoder,
            preferred_element_type=jnp.float32,
        )
        + encoder_bias[None, :]
    )
    features = jax.nn.relu(scores).astype(jnp.bfloat16)
    block_rows = features
    reconstruction = (
        lax.psum_scatter(
            jnp.dot(block_rows, decoder, preferred_element_type=jnp.float32),
            ("expert", "feat"),
            scatter_dimension=0,
            tiled=True,
        )
        + decoder_bias[None, :]
    )
    return (features, reconstruction)


def solution(mesh):
    return jax.shard_map(
        shards,
        mesh=mesh,
        in_specs=(
            P("expert", None),
            P(("expert", "feat"), None),
            P(("expert", "feat"), None),
            P(("expert", "feat"), None, None),
            P(("expert", "feat"), None, None),
            P(("expert", "feat"), None, None),
            P(None, "feat"),
            P(None, "feat"),
            P("feat", None),
            P(None, ("expert", "feat")),
            P(("expert", "feat")),
            P(("expert", "feat"), None),
            P(),
        ),
        out_specs=(P(None, ("expert", "feat")), P(("expert", "feat"), None)),
        check_vma=False,
    )
```

profile of v0, /device:TPU:0, one launch (start us, length us, event | category | flops | bytes accessed | tf_op | source)
XLA Modules:
  0.0 281.2 jit_solution(2259884633903007152)
XLA Ops:
  7.2 0.0 copy-start
  7.2 0.9 copy.20
  8.1 0.1 reshape.46
  8.2 0.1 eq.49
  8.3 0.0 copy-start.5
  8.3 0.1 fusion.53
  8.4 0.2 reduce_window_sum.11
  8.6 0.2 select_reduce_fusion
  8.7 0.0 copy-start.6
  8.8 1.7 fusion.12
  10.4 37.2 %all_to_all.10 = bf16[32,1,8,2304]{3,2,1,0:T(8,128)(2,1)S(1)} all-to-all(bf16[32,1,8,2304]{3,2,1,0:T(8,128)(2,1)S(1)} %fusion.12), channel_id=1, replica_groups=mesh['expert'=8,'feat'=4] {'expert','feat'}, dimensions={0} | all-to-all | bytes 2359296 | tf_op jit(solution)/shard_map/all_to_all | solution.py:61
  47.6 0.0 copy-start.1
  47.6 1.0 copy-done.1
  48.6 3.7 %fusion.16 = f32[32,1,8,1024]{3,2,0,1:T(8,128)S(1)} fusion(bf16[1,2304,1024]{2,1,0:T(8,128)(2,1)} %param.16, bf16[32,1,8,2304]{3,2,1,0:T(8,128)(2,1)S(1)} %all_to_all.10), kind=kOutput, calls=%fused_computation.14 | convolution fusion | flops 1207959552 | bytes 6946816 | tf_op jit(solution)/shard_map/sjcd,jdh->sjch/dot_general | solution.py:8
  52.4 0.0 copy-done.5
  52.4 0.0 copy-done.6
  52.4 7.9 %fusion.9 = bf16[32,1,8,2304]{3,2,1,0:T(8,128)(2,1)} fusion(bf16[1,1024,2304]{2,1,0:T(8,128)(2,1)} %param.18, bf16[1,2304,1024]{2,1,0:T(8,128)(2,1)} %param.17, bf16[32,1,8,2304]{3,2,1,0:T(8,128)(2,1)} %copy-done.1, f32[32,1,8,1024]{3,2,0,1:T(8,128)S(1)} %fusion.16), kind=kOutput, calls=%fused_computation.8 | convolution fusion | flops 2418081792 | bytes 12845056 | tf_op jit(solution)/shard_map/sjch,jhd->sjcd/dot_general | solution.py:13
  60.3 2.7 all-to-all-start.1
  63.0 0.0 copy-start.4
  63.0 0.0 reduce-scatter.3.cloned.1.call-start
  63.0 2.3 fusion.65
  65.4 3.5 %fusion.37 = f32[64,2304]{1,0:T(8,128)} fusion(bf16[256,2304]{1,0:T(8,128)(2,1)} %param.21, bf16[64,2304]{1,0:T(8,128)(2,1)} %param.13, bf16[2304,256]{1,0:T(8,128)(2,1)} %param.20, f32[64,256]{1,0:T(8,128)} %fusion.65), kind=kOutput, calls=%fused_computation.27 | convolution fusion | flops 151093248 | bytes 3309568 | tf_op jit(solution)/shard_map/dot_general | solution.py:76
  68.8 0.0 reduce-scatter.3.cloned.1.call-update
  68.9 0.0 all-gather.2.cloned.1.call-start
  68.9 0.0 copy-done.4
  68.9 0.1 copy.19
  69.0 0.6 mul.40
  69.6 1.0 fusion.43
  70.5 27.1 %reduce-scatter.3.cloned.1.call-done = f32[16,2304]{1,0:T(8,128)} async-done(((f32[64,2304]{1,0:T(8,128)}), f32[16,2304]{1,0:T(8,128)}) %reduce-scatter.3.cloned.1.call-update) | async-done | bytes 147472 | tf_op jit(solution)/shard_map/reduce_scatter | solution.py:75
  97.6 2.6 all-to-all-done.1
  100.2 2.1 fusion.15
  102.3 0.0 all-gather.2.cloned.1.call-update
  102.4 0.0 reduce-scatter.5.cloned.1.call-start
  102.4 57.3 %all-gather.2.cloned.1.call-done = bf16[512,2304]{1,0:T(8,128)(2,1)} async-done(((bf16[16,2304]{1,0:T(8,128)(2,1)}), bf16[512,2304]{1,0:T(8,128)(2,1)}) %all-gather.2.cloned.1.call-update) | async-done | bytes 2359312 | tf_op jit(solution)/shard_map/all_gather | solution.py:84
  159.7 3.8 %fusion.26 = bf16[512,512]{1,0:T(8,128)(2,1)S(1)} fusion(bf16[512,2304]{1,0:T(8,128)(2,1)} %all-gather.2.cloned.1.call-done, bf16[2304,512]{1,0:T(8,128)(2,1)} %param.22, f32[512]{0:T(512)} %param.23), kind=kOutput, calls=%fused_computation.19 | convolution fusion | flops 1208745984 | bytes 5244928 | tf_op jit(solution)/shard_map/dot_general | solution.py:83
  163.5 0.0 copy-done
  163.5 0.0 copy-start.2
  163.5 3.5 %fusion.66 = f32[512,2304]{1,0:T(8,128)} fusion(bf16[512,512]{1,0:T(8,128)(2,1)S(1)} %fusion.26, bf16[512,2304]{1,0:T(8,128)(2,1)S(1)} %copy-done), kind=kOutput, calls=%fused_computation.57 | convolution fusion | flops 1207959552 | bytes 7602176 | tf_op jit(solution)/shard_map/dot_general | solution.py:94
  167.0 0.0 copy-done.2
  167.0 0.0 copy-start.3
  167.0 0.0 reduce-scatter.5.cloned.1.call-update
  167.0 106.0 %reduce-scatter.5.cloned.1.call-done = f32[16,2304]{1,0:T(8,128)} async-done(((f32[512,2304]{1,0:T(8,128)}), f32[16,2304]{1,0:T(8,128)}) %reduce-scatter.5.cloned.1.call-update) | async-done | bytes 147472 | tf_op jit(solution)/shard_map/reduce_scatter | solution.py:93
  273.1 0.0 copy-done.3
  273.1 1.6 broadcast_add_fusion
  (2 shorter events, 0.0 us)
Async XLA Ops:
  7.2 156.3 %copy-start = (bf16[512,2304]{1,0:T(8,128)(2,1)S(1)}, bf16[512,2304]{1,0:T(8,128)(2,1)}, u32[]{:S(2)}) copy-start(bf16[512,2304]{1,0:T(8,128)(2,1)} %param.24) | copy-start | bytes 7077892
  8.3 44.1 %copy-start.5 = (s32[128]{0:T(128)}, s32[128]{0:T(128)S(1)}, u32[]{:S(2)}) copy-start(s32[128]{0:T(128)S(1)} %eq.49) | copy-start | bytes 1540
  8.7 43.7 %copy-start.6 = (s32[128]{0:T(128)}, s32[128]{0:T(128)S(1)}, u32[]{:S(2)}) copy-start(s32[128]{0:T(128)S(1)} %multiply_add_fusion) | copy-start | bytes 1540
  47.6 1.0 copy-start.1
  60.3 39.9 %all-to-all-start.1 = ((bf16[32,1,8,2304]{3,2,1,0:T(8,128)(2,1)}), bf16[32,1,8,2304]{3,2,1,0:T(8,128)(2,1)S(1)}, u32[]{:S(2)}, u32[]{:S(2)}) async-start(bf16[32,1,8,2304]{3,2,1,0:T(8,128)(2,1)} %fusion.9), calls=%async_computation.1 | async-start | bytes 2359296 | tf_op jit(solution)/shard_map/all_to_all | solution.py:66
  63.0 5.9 %copy-start.4 = (f32[16,8]{0,1:T(8,128)S(1)}, f32[16,8]{0,1:T(8,128)}, u32[]{:S(2)}) copy-start(f32[16,8]{0,1:T(8,128)} %param.15) | copy-start | bytes 1540
  63.0 34.7 %reduce-scatter.3.cloned.1.call-start = ((), (), s32[]{:S(2)}) async-start(), calls=%async_computation.4 | async-start | bytes 737280 | tf_op jit(solution)/shard_map/reduce_scatter | solution.py:75
  68.9 90.8 %all-gather.2.cloned.1.call-start = ((), (), s32[]{:S(2)}) async-start(), calls=%async_computation.5 | async-start | bytes 2433024 | tf_op jit(solution)/shard_map/all_gather | solution.py:84
  102.4 170.7 %reduce-scatter.5.cloned.1.call-start = ((), (), s32[]{:S(2)}) async-start(), calls=%async_computation.6 | async-start | bytes 4866048 | tf_op jit(solution)/shard_map/reduce_scatter | solution.py:93
  163.5 3.5 %copy-start.2 = (bf16[512,512]{1,0:T(8,128)(2,1)}, bf16[512,512]{1,0:T(8,128)(2,1)S(1)}, u32[]{:S(2)}) copy-start(bf16[512,512]{1,0:T(8,128)(2,1)S(1)} %fusion.26) | copy-start | bytes 1572868
  167.0 106.1 %copy-start.3 = (f32[2304]{0:T(1024)S(1)}, f32[2304]{0:T(1024)}, u32[]{:S(2)}) copy-start(f32[2304]{0:T(1024)} %param.25) | copy-start | bytes 27652
Sparse Core Ops, SparseCore 0:
  69.0 28.6 reduce-scatter.2
  102.5 57.1 all-gather.1
  167.1 105.8 reduce-scatter.4
where the time goes:
time: 282 us; the launch traced here: 281 us
  waiting for transfers between devices  193 us (68%)
  blocking collectives  37.2 us (13%)
  matrix products  29.4 us (10%)
  between operations  13.9 us (5%)
    reduce_scatter x1, waiting for transfers between devices, shards(): lax.psum_scatter(jnp.dot(block_rows, decoder, preferred_element_type=jnp....  106 us
    all_gather x1, waiting for transfers between devices, shards(): lax.all_gather(moe_out, ('expert', 'feat'), axis=0, tiled=True)  57.3 us
    all_to_all x1, blocking collectives, shards(): lax.all_to_all(outgoing, ('expert', 'feat'), split_axis=0, concat_axis=0,...  37.2 us
    reduce_scatter x1, waiting for transfers between devices, shards(): lax.psum_scatter(jnp.dot(block_rows, shared_down, preferred_element_type=...  27.1 us
    dot_general x1, matrix products, run_experts(): jnp.einsum('sjch,jhd->sjcd', hidden, expert_down, preferred_element_type=...  7.88 us
  transfers between devices with their start and end apart: 4, of which 4 were waited for; matrix products, arithmetic and copies ran while one was open for 3% of the time, Pallas kernels for 0%

commit v1 on v0

v1 whole, which is shorter than its diff:
```python
import jax
import jax.numpy as jnp
from jax import lax
from jax.sharding import PartitionSpec as P


def swap(value, axis, bit):
    count = lax.axis_size(axis)
    return lax.ppermute(value, axis, [(i, i ^ bit) for i in range(count)])


def bits_of(axis):
    count = lax.axis_size(axis)
    assert count & (count - 1) == 0
    return [(axis, 1 << b) for b in range(count.bit_length() - 1)]


def gather(value, held, order, dims):
    held = list(held)
    for bit in order:
        held = [d for d in dims if d in held or d == bit]
        value = jnp.stack([value, swap(value, *bit)], axis=held.index(bit))
    return value


def reduce_bits(value, held, order):
    held = list(held)
    for bit in order:
        place = held.index(bit)
        sent = lax.index_in_dim(value, 1, place, keepdims=False).astype(jnp.bfloat16)
        kept = lax.index_in_dim(value, 0, place, keepdims=False)
        value = kept + swap(sent, *bit).astype(jnp.float32)
        held.remove(bit)
    return value


def relative(value, axis):
    me = lax.axis_index(axis)
    blocks = [lax.dynamic_index_in_dim(value, i ^ me, 0) for i in range(value.shape[0])]
    return jnp.concatenate(blocks, axis=0)


def dot(a, b):
    return jnp.dot(a, b, preferred_element_type=jnp.float32)


def shards(
    tokens,
    expert_ids,
    gate_weights,
    expert_gate,
    expert_up,
    expert_down,
    shared_gate,
    shared_up,
    shared_down,
    encoder,
    encoder_bias,
    decoder,
    decoder_bias,
):
    own, top = expert_ids.shape
    width = tokens.shape[1]
    e_bits, f_bits = bits_of("expert"), bits_of("feat")
    devices = lax.axis_size(("expert", "feat"))
    dims = e_bits + f_bits[::-1]
    feat_dims = f_bits[::-1]
    first, plane = e_bits[0], e_bits[1:]
    half = (width // 2 + 127) // 128 * 128
    streams = [(slice(0, half), plane), (slice(half, width), plane[::-1])]
    local_experts = expert_gate.shape[0]
    me = lax.axis_index(("expert", "feat"))

    table = jnp.concatenate([expert_ids.astype(jnp.float32), gate_weights], axis=1)
    table = gather(table, [], f_bits + plane + [first], dims).reshape(-1, 2 * top)
    ids, weights = table[:, :top].astype(jnp.int32), table[:, top:]

    mine = relative(tokens.reshape(-1, own, width), "feat")
    mine = mine.reshape((2,) * len(f_bits) + (own, width))
    parts = [gather(mine[..., cols], feat_dims, order, dims) for cols, order in streams]
    near = jnp.concatenate(parts, axis=-1).reshape(-1, width)
    far = swap(near, *first)

    def expert(rows):
        out = []
        for j in range(local_experts):
            hidden = (
                jax.nn.silu(dot(rows, expert_gate[j])) * dot(rows, expert_up[j])
            ).astype(jnp.bfloat16)
            out.append(hidden)
        return out

    n = near.shape[0]
    hidden_near, hidden_far = expert(near), expert(far)
    shared_rows = mine.reshape(-1, width)
    shared_rows = (
        jax.nn.silu(dot(shared_rows, shared_gate)) * dot(shared_rows, shared_up)
    ).astype(jnp.bfloat16)
    scale = [
        jnp.sum(jnp.where(ids == me * local_experts + j, weights, 0.0), axis=1)[:, None]
        for j in range(local_experts)
    ]
    moe = []
    rest = [d for d in dims if d != first]
    for cols, order in streams:
        far_out = sum(
            dot(hidden_far[j], expert_down[j][:, cols]) * scale[j][n:] for j in range(local_experts)
        )
        far_out = swap(far_out.astype(jnp.bfloat16), *first)
        near_out = sum(
            dot(hidden_near[j], expert_down[j][:, cols]) * scale[j][:n] for j in range(local_experts)
        )
        total = near_out + far_out.astype(jnp.float32)
        total = total.reshape((2,) * len(rest) + (own, -1))
        total = reduce_bits(total, rest, order)
        shared_out = dot(shared_rows, shared_down[:, cols])
        total = total + shared_out.reshape(total.shape)
        total = reduce_bits(total, feat_dims, f_bits)
        out = total.astype(jnp.bfloat16)
        out = gather(out, [], f_bits[::-1] + order[::-1], dims)
        moe.append(out)
    near = jnp.concatenate(moe, axis=-1).reshape(-1, width)
    far = swap(near, *first)

    features_near = jax.nn.relu(dot(near, encoder) + encoder_bias[None, :]).astype(jnp.bfloat16)
    features_far = jax.nn.relu(dot(far, encoder) + encoder_bias[None, :]).astype(jnp.bfloat16)

    recon = []
    for cols, order in streams:
        far_out = swap(dot(features_far, decoder[:, cols]).astype(jnp.bfloat16), *first)
        total = dot(features_near, decoder[:, cols]) + far_out.astype(jnp.float32)
        total = total.reshape((2,) * len(rest) + (own, -1))
        recon.append(reduce_bits(total, rest, order + f_bits))
    reconstruction = jnp.concatenate(recon, axis=-1) + decoder_bias[None, :]

    features = jnp.concatenate([features_near, features_far], axis=0)
    features = features.reshape((2,) * len(dims) + (own, -1))
    wanted = e_bits[::-1] + f_bits[::-1]
    features = jnp.transpose(
        features, [dims.index(d) for d in wanted] + [len(dims), len(dims) + 1]
    ).reshape(devices, own, -1)
    features = relative(features, ("expert", "feat")).reshape(devices * own, -1)
    return (features, reconstruction)


def solution(mesh):
    return jax.shard_map(
        shards,
        mesh=mesh,
        in_specs=(
            P("expert", None),
            P(("expert", "feat"), None),
            P(("expert", "feat"), None),
            P(("expert", "feat"), None, None),
            P(("expert", "feat"), None, None),
            P(("expert", "feat"), None, None),
            P(None, "feat"),
            P(None, "feat"),
            P("feat", None),
            P(None, ("expert", "feat")),
            P(("expert", "feat")),
            P(("expert", "feat"), None),
            P(),
        ),
        out_specs=(P(None, ("expert", "feat")), P(("expert", "feat"), None)),
        check_vma=False,
    )
```

time: 282 us -> 135 us (0.48)
  waiting for transfers between devices: 193 us -> 60.4 us
  blocking collectives: 37.2 us -> 0 us
  starting transfers between devices: 2.78 us -> 36.3 us
  between operations: 13.9 us -> 1.93 us
  matrix products: 29.4 us -> 23.1 us
  other arithmetic: 2.01 us -> 6.48 us
  local copies, waits for them, and re-layouts: 2.81 us -> 6.56 us
    reduce_scatter x2 -> x0, waiting for transfers between devices: 133 us -> none  [the longest x1 106 us: shards(): lax.psum_scatter(jnp.dot(block_rows, decoder, preferred_element_type=jnp....]
    ppermute x0 -> x39, waiting for transfers between devices: none -> 60.4 us  [swap(): return lax.ppermute(value, axis, [(i, i ^ bit) for i in range(count)])]
    all_gather x1 -> x0, waiting for transfers between devices: 57.3 us -> none  [shards(): lax.all_gather(moe_out, ('expert', 'feat'), axis=0, tiled=True)]
    all_to_all x1 -> x0, blocking collectives: 37.2 us -> none  [shards(): lax.all_to_all(outgoing, ('expert', 'feat'), split_axis=0, concat_axis=0,...]
    ppermute x0 -> x39, starting transfers between devices: none -> 36.3 us  [swap(): return lax.ppermute(value, axis, [(i, i ^ bit) for i in range(count)])]
    dot_general x9 -> x18, matrix products: 29.4 us -> 23.1 us  [dot(): return jnp.dot(a, b, preferred_element_type=jnp.float32)]
    another operation x1 -> x14, other arithmetic: 0.17 us -> 3.46 us  [gather(): value = jnp.stack([value, swap(value, *bit)], axis=held.index(bit))]
  transfers between devices with their start and end apart: 4 -> 39, of which waited for: 4 -> 30; matrix products, arithmetic and copies ran while one was open for 3% -> 15% of each run, Pallas kernels for 0% -> 0%
where the time goes in v1:
time: 135 us
  waiting for transfers between devices  60.4 us (45%)
  starting transfers between devices  36.3 us (27%)
  matrix products  23.1 us (17%)
  local copies, waits for them, and re-layouts  6.56 us (5%)
  other arithmetic  6.48 us (5%)
  between operations  1.93 us (1%)
    ppermute x39, waiting for transfers between devices, swap(): return lax.ppermute(value, axis, [(i, i ^ bit) for i in range(count)])  60.4 us
    ppermute x39, starting transfers between devices, swap(): return lax.ppermute(value, axis, [(i, i ^ bit) for i in range(count)])  36.3 us
    dot_general x18, matrix products, dot(): return jnp.dot(a, b, preferred_element_type=jnp.float32)  23.1 us
    another operation x14, other arithmetic, gather(): value = jnp.stack([value, swap(value, *bit)], axis=held.index(bit))  3.46 us
  transfers between devices with their start and end apart: 39, of which 30 were waited for; matrix products, arithmetic and copies ran while one was open for 15% of the time, Pallas kernels for 0%

profile of v1, /device:TPU:0, one launch (start us, length us, event | category | flops | bytes accessed | tf_op | source)
XLA Modules:
  0.0 134.8 jit_solution(14549146650347283753)
XLA Ops:
  2.3 3.0 %collective-permute-start.4 = (f32[16,16]{0,1:T(8,128)S(1)}, f32[16,16]{0,1:T(8,128)}, u32[]{:S(2)}, u32[]{:S(2)}) collective-permute-start(f32[16,16]{0,1:T(8,128)S(1)} %get-tuple-element.35), channel_id=1, source_target_pairs={{0,1},{1,0},{2,3},{3,2},{4,5},{5,4},{6,7},{7,6},{8,9},{9,8},{10,11... | collective-permute-start | bytes 3080 | tf_op jit(solution)/shard_map/ppermute | solution.py:9
  5.3 1.0 constant_dynamic-slice_fusion.3
  6.4 1.6 %collective-permute-start.2 = (bf16[2,2,16,1152]{3,2,1,0:T(8,128)(2,1)S(1)}, bf16[2,2,16,1152]{3,2,1,0:T(8,128)(2,1)S(1)}, u32[]{:S(2)}, u32[]{:S(2)}) collective-permute-start(bf16[2,2,16,1152]{3,2,1,0:T(8,128)(2,1)S(1)} %get-tuple-element.10), channel_id=1, source_target_pairs={{0,16},{4,20},{8,24},{12,28},{16,0},{20,4},{24,8},{28,12},{1,17},{... | collective-permute-start | bytes 442376 | tf_op jit(solution)/shard_map/ppermute | solution.py:9
  8.0 1.5 %collective-permute-start = (bf16[2,2,16,1152]{3,2,1,0:T(8,128)(2,1)S(1)}, bf16[2,2,16,1152]{3,2,1,0:T(8,128)(2,1)S(1)}, u32[]{:S(2)}, u32[]{:S(2)}) collective-permute-start(bf16[2,2,16,1152]{3,2,1,0:T(8,128)(2,1)S(1)} %get-tuple-element.11), channel_id=1, source_target_pairs={{0,8},{4,12},{8,0},{12,4},{16,24},{20,28},{24,16},{28,20},{1,9},{5... | collective-permute-start | bytes 442376 | tf_op jit(solution)/shard_map/ppermute | solution.py:9
  10.5 2.6 %collective-permute-start.5 = (f32[2,16,16]{1,2,0:T(8,128)S(1)}, f32[2,16,16]{1,2,0:T(8,128)S(1)}, u32[]{:S(2)}, u32[]{:S(2)}) collective-permute-start(f32[2,16,16]{1,2,0:T(8,128)S(1)} %get-tuple-element.33), channel_id=1, source_target_pairs={{0,2},{1,3},{2,0},{3,1},{4,6},{5,7},{6,4},{7,5},{8,10},{9,11},{10,... | collective-permute-start | bytes 6152 | tf_op jit(solution)/shard_map/ppermute | solution.py:9
  13.5 1.8 %collective-permute-done.5 = f32[2,16,16]{1,2,0:T(8,128)S(1)} collective-permute-done((f32[2,16,16]{1,2,0:T(8,128)S(1)}, f32[2,16,16]{1,2,0:T(8,128)S(1)}, u32[]{:S(2)}, u32[]{:S(2)}) %collective-permute-start.5) | collective-permute-done | bytes 2080 | tf_op jit(solution)/shard_map/ppermute | solution.py:9
  15.9 1.6 %collective-permute-start.3 = (bf16[2,2,2,16,1152]{4,3,2,1,0:T(8,128)(2,1)S(1)}, bf16[2,2,2,16,1152]{4,3,2,1,0:T(8,128)(2,1)S(1)}, u32[]{:S(2)}, u32[]{:S(2)}) collective-permute-start(bf16[2,2,2,16,1152]{4,3,2,1,0:T(8,128)(2,1)S(1)} %get-tuple-element.13), channel_id=1, source_target_pairs={{0,8},{4,12},{8,0},{12,4},{16,24},{20,28},{24,16},{28,20},{1,9},{5... | collective-permute-start | bytes 884744 | tf_op jit(solution)/shard_map/ppermute | solution.py:9
  19.7 1.0 collective-permute-start.7
  20.6 2.2 %collective-permute-done.3 = bf16[2,2,2,16,1152]{4,3,2,1,0:T(8,128)(2,1)S(1)} collective-permute-done((bf16[2,2,2,16,1152]{4,3,2,1,0:T(8,128)(2,1)S(1)}, bf16[2,2,2,16,1152]{4,3,2,1,0:T(8,128)(2,1)S(1)}, u32[]{:S(2)}, u32[]{:S(2)}) %collective-permute-start.3) | collective-permute-done | bytes 294944 | tf_op jit(solution)/shard_map/ppermute | solution.py:9
  22.8 1.7 %collective-permute-done.1 = bf16[2,2,2,16,1152]{4,3,2,1,0:T(8,128)(2,1)S(1)} collective-permute-done((bf16[2,2,2,16,1152]{4,3,2,1,0:T(8,128)(2,1)S(1)}, bf16[2,2,2,16,1152]{4,3,2,1,0:T(8,128)(2,1)S(1)}, u32[]{:S(2)}, u32[]{:S(2)}) %collective-permute-start.1) | collective-permute-done | bytes 294944 | tf_op jit(solution)/shard_map/ppermute | solution.py:9
  25.9 0.9 fusion.39
  26.9 1.2 collective-permute-done.8
  28.0 1.0 pad_maximum_fusion.6
  29.9 1.9 %reshape.75 = f32[512,16]{0,1:T(8,128)} reshape(f32[2,2,2,2,2,16,16]{5,4,3,2,1,0,6:T(2,128)} %copy.26) | data formatting | bytes 65536 | tf_op jit(solution)/shard_map/reshape | solution.py:75
  32.5 3.9 %fusion.6 = f32[256,1024]{1,0:T(8,128)S(1)} fusion(bf16[256,2304]{1,0:T(8,128)(2,1)S(1)} %bitcast.251, bf16[1,2304,1024]{2,1,0:T(8,128)(2,1)} %param.16), kind=kOutput, calls=%fused_computation.6 | convolution fusion | flops 1207959552 | bytes 6946816 | tf_op jit(solution)/shard_map/dot_general | solution.py:44
  36.5 4.2 %fusion.4 = f32[256,1024]{1,0:T(8,128)S(1)} fusion(bf16[256,2304]{1,0:T(8,128)(2,1)} %collective-permute-done.9, bf16[1,2304,1024]{2,1,0:T(8,128)(2,1)} %param.16), kind=kOutput, calls=%fused_computation.4 | convolution fusion | flops 1207959552 | bytes 6946816 | tf_op jit(solution)/shard_map/dot_general | solution.py:44
  40.7 2.8 %multiply_convert_fusion = bf16[256,1024]{1,0:T(8,128)(2,1)S(1)} fusion(f32[256,1024]{1,0:T(8,128)S(1)} %fusion.4, bf16[256,2304]{1,0:T(8,128)(2,1)} %collective-permute-done.9, bf16[1,2304,1024]{2,1,0:T(8,128)(2,1)S(1)} %bitcast.279), kind=kOutput, calls=%fused_computation.36 | convolution fusion | flops 1209532416 | bytes 7471104 | tf_op jit(solution)/shard_map/dot_general | solution.py:44
  45.8 1.5 %fusion.17 = bf16[256,1024]{1,0:T(8,128)(2,1)S(1)} fusion(bf16[256,2304]{1,0:T(8,128)(2,1)S(1)} %bitcast.252, bf16[1,2304,1024]{2,1,0:T(8,128)(2,1)S(1)} %bitcast.279, f32[256,1024]{1,0:T(8,128)S(1)} %fusion.6), kind=kOutput, calls=%fused_computation.21 | convolution fusion | flops 1209532416 | bytes 7471104 | tf_op jit(solution)/shard_map/dot_general | solution.py:44
  48.3 0.9 copy-done.3
  51.1 7.1 %collective-permute-done.11 = bf16[2,2,2,16,1152]{4,3,1,2,0:T(8,128)(2,1)S(1)} collective-permute-done((bf16[2,2,2,16,1152]{4,3,1,2,0:T(8,128)(2,1)S(1)}, bf16[2,2,2,16,1152]{4,3,1,2,0:T(8,128)(2,1)S(1)}, u32[]{:S(2)}, u32[]{:S(2)}) %collective-permute-start.11) | collective-permute-done | bytes 294944 | tf_op jit(solution)/shard_map/ppermute | solution.py:9
  59.6 1.6 %collective-permute-start.21 = (bf16[2,2,16,1152]{3,2,0,1:T(8,128)(2,1)S(1)}, bf16[2,2,16,1152]{3,2,0,1:T(8,128)(2,1)S(1)}, u32[]{:S(2)}, u32[]{:S(2)}) collective-permute-start(bf16[2,2,16,1152]{3,2,0,1:T(8,128)(2,1)S(1)} %fusion.54), channel_id=1, source_target_pairs={{0,8},{4,12},{8,0},{12,4},{16,24},{20,28},{24,16},{28,20},{1,9},{5... | collective-permute-start | bytes 442376 | tf_op jit(solution)/shard_map/ppermute | solution.py:9
  61.2 2.4 %collective-permute-done.12 = bf16[2,2,16,1152]{3,2,0,1:T(8,128)(2,1)S(1)} collective-permute-done((bf16[2,2,16,1152]{3,2,0,1:T(8,128)(2,1)S(1)}, bf16[2,2,16,1152]{3,2,0,1:T(8,128)(2,1)S(1)}, u32[]{:S(2)}, u32[]{:S(2)}) %collective-permute-start.12) | collective-permute-done | bytes 147488 | tf_op jit(solution)/shard_map/ppermute | solution.py:9
  64.8 1.0 collective-permute-start.22
  65.9 2.2 %collective-permute-done.13 = bf16[2,16,1152]{2,1,0:T(8,128)(2,1)S(1)} collective-permute-done((bf16[2,16,1152]{2,1,0:T(8,128)(2,1)S(1)}, bf16[2,16,1152]{2,1,0:T(8,128)(2,1)S(1)}, u32[]{:S(2)}, u32[]{:S(2)}) %collective-permute-start.13) | collective-permute-done | bytes 73760 | tf_op jit(solution)/shard_map/ppermute | solution.py:9
  68.1 2.6 %collective-permute-start.14 = (bf16[16,1152]{1,0:T(8,128)(2,1)S(1)}, bf16[16,1152]{1,0:T(8,128)(2,1)S(1)}, u32[]{:S(2)}, u32[]{:S(2)}) collective-permute-start(bf16[16,1152]{1,0:T(8,128)(2,1)S(1)} %fusion.71), channel_id=1, source_target_pairs={{0,2},{1,3},{2,0},{3,1},{4,6},{5,7},{6,4},{7,5},{8,10},{9,11},{10,... | collective-permute-start | bytes 110600 | tf_op jit(solution)/shard_map/ppermute | solution.py:9
  70.7 1.6 %collective-permute-start.23 = (bf16[16,1152]{1,0:T(8,128)(2,1)S(1)}, bf16[16,1152]{1,0:T(8,128)(2,1)S(1)}, u32[]{:S(2)}, u32[]{:S(2)}) collective-permute-start(bf16[16,1152]{1,0:T(8,128)(2,1)S(1)} %fusion.72), channel_id=1, source_target_pairs={{0,2},{1,3},{2,0},{3,1},{4,6},{5,7},{6,4},{7,5},{8,10},{9,11},{10,... | collective-permute-start | bytes 110600 | tf_op jit(solution)/shard_map/ppermute | solution.py:9
  72.3 1.6 %collective-permute-done.14 = bf16[16,1152]{1,0:T(8,128)(2,1)S(1)} collective-permute-done((bf16[16,1152]{1,0:T(8,128)(2,1)S(1)}, bf16[16,1152]{1,0:T(8,128)(2,1)S(1)}, u32[]{:S(2)}, u32[]{:S(2)}) %collective-permute-start.14) | collective-permute-done | bytes 36896 | tf_op jit(solution)/shard_map/ppermute | solution.py:9
  73.9 2.0 %collective-permute-start.15 = (bf16[16,1152]{1,0:T(8,128)(2,1)S(1)}, bf16[16,1152]{1,0:T(8,128)(2,1)S(1)}, u32[]{:S(2)}, u32[]{:S(2)}) collective-permute-start(bf16[16,1152]{1,0:T(8,128)(2,1)S(1)} %fusion.70), channel_id=1, source_target_pairs={{0,2},{1,3},{2,0},{3,1},{4,6},{5,7},{6,4},{7,5},{8,10},{9,11},{10,... | collective-permute-start | bytes 110600 | tf_op jit(solution)/shard_map/ppermute | solution.py:9
  77.2 1.6 %collective-permute-done.15 = bf16[16,1152]{1,0:T(8,128)(2,1)S(1)} collective-permute-done((bf16[16,1152]{1,0:T(8,128)(2,1)S(1)}, bf16[16,1152]{1,0:T(8,128)(2,1)S(1)}, u32[]{:S(2)}, u32[]{:S(2)}) %collective-permute-start.15) | collective-permute-done | bytes 36896 | tf_op jit(solution)/shard_map/ppermute | solution.py:9
  79.0 2.5 %collective-permute-done.24 = bf16[16,1152]{1,0:T(8,128)(2,1)S(1)} collective-permute-done((bf16[16,1152]{1,0:T(8,128)(2,1)S(1)}, bf16[16,1152]{1,0:T(8,128)(2,1)S(1)}, u32[]{:S(2)}, u32[]{:S(2)}) %collective-permute-start.24) | collective-permute-done | bytes 36896 | tf_op jit(solution)/shard_map/ppermute | solution.py:9
  81.6 1.6 %collective-permute-done.16 = bf16[2,16,1152]{2,1,0:T(8,128)(2,1)S(1)} collective-permute-done((bf16[2,16,1152]{2,1,0:T(8,128)(2,1)S(1)}, bf16[2,16,1152]{2,1,0:T(8,128)(2,1)S(1)}, u32[]{:S(2)}, u32[]{:S(2)}) %collective-permute-start.16) | collective-permute-done | bytes 73760 | tf_op jit(solution)/shard_map/ppermute | solution.py:9
  83.9 2.0 %collective-permute-done.25 = bf16[2,16,1152]{2,1,0:T(8,128)(2,1)S(1)} collective-permute-done((bf16[2,16,1152]{2,1,0:T(8,128)(2,1)S(1)}, bf16[2,16,1152]{2,1,0:T(8,128)(2,1)S(1)}, u32[]{:S(2)}, u32[]{:S(2)}) %collective-permute-start.25) | collective-permute-done | bytes 73760 | tf_op jit(solution)/shard_map/ppermute | solution.py:9
  86.7 3.3 %collective-permute-done.17 = bf16[2,2,16,1152]{3,2,1,0:T(8,128)(2,1)S(1)} collective-permute-done((bf16[2,2,16,1152]{3,2,1,0:T(8,128)(2,1)S(1)}, bf16[2,2,16,1152]{3,2,1,0:T(8,128)(2,1)S(1)}, u32[]{:S(2)}, u32[]{:S(2)}) %collective-permute-start.17) | collective-permute-done | bytes 147488 | tf_op jit(solution)/shard_map/ppermute | solution.py:9
  91.9 5.0 %collective-permute-done.18 = bf16[2,2,2,16,1152]{4,3,2,1,0:T(8,128)(2,1)S(1)} collective-permute-done((bf16[2,2,2,16,1152]{4,3,2,1,0:T(8,128)(2,1)S(1)}, bf16[2,2,2,16,1152]{4,3,2,1,0:T(8,128)(2,1)S(1)}, u32[]{:S(2)}, u32[]{:S(2)}) %collective-permute-start.18) | collective-permute-done | bytes 294944 | tf_op jit(solution)/shard_map/ppermute | solution.py:9
  96.9 1.1 collective-permute-done.27
  99.5 1.7 %collective-permute-done.28 = bf16[256,2304]{1,0:T(8,128)(2,1)} collective-permute-done((bf16[256,2304]{1,0:T(8,128)(2,1)S(1)}, bf16[256,2304]{1,0:T(8,128)(2,1)}, u32[]{:S(2)}, u32[]{:S(2)}) %collective-permute-start.28) | collective-permute-done | bytes 1179680 | tf_op jit(solution)/shard_map/ppermute | solution.py:9
  101.2 2.0 %fusion.22 = bf16[256,512]{1,0:T(8,128)(2,1)S(1)} fusion(bf16[256,2304]{1,0:T(8,128)(2,1)} %collective-permute-done.28, bf16[2304,512]{1,0:T(8,128)(2,1)S(1)} %copy-done, f32[512]{0:T(512)S(1)} %copy-done.11), kind=kOutput, calls=%fused_computation.26 | convolution fusion | flops 604372992 | bytes 3803136 | tf_op jit(solution)/shard_map/dot_general | solution.py:44
  105.5 0.9 collective-permute-done.29
  107.0 0.9 copy-done.1
  108.0 1.0 collective-permute-start.30
  110.2 6.8 %collective-permute-done.30 = bf16[2,2,2,16,1152]{4,3,1,2,0:T(8,128)(2,1)S(1)} collective-permute-done((bf16[2,2,2,16,1152]{4,3,1,2,0:T(8,128)(2,1)S(1)}, bf16[2,2,2,16,1152]{4,3,1,2,0:T(8,128)(2,1)S(1)}, u32[]{:S(2)}, u32[]{:S(2)}) %collective-permute-start.30) | collective-permute-done | bytes 294944 | tf_op jit(solution)/shard_map/ppermute | solution.py:9
  118.5 1.1 collective-permute-start.36
  119.6 2.8 %collective-permute-done.31 = bf16[2,2,16,1152]{3,2,0,1:T(8,128)(2,1)S(1)} collective-permute-done((bf16[2,2,16,1152]{3,2,0,1:T(8,128)(2,1)S(1)}, bf16[2,2,16,1152]{3,2,0,1:T(8,128)(2,1)S(1)}, u32[]{:S(2)}, u32[]{:S(2)}) %collective-permute-start.31) | collective-permute-done | bytes 147488 | tf_op jit(solution)/shard_map/ppermute | solution.py:9
  122.5 1.2 collective-permute-done.36
  124.6 2.2 %collective-permute-done.32 = bf16[2,16,1152]{2,1,0:T(8,128)(2,1)S(1)} collective-permute-done((bf16[2,16,1152]{2,1,0:T(8,128)(2,1)S(1)}, bf16[2,16,1152]{2,1,0:T(8,128)(2,1)S(1)}, u32[]{:S(2)}, u32[]{:S(2)}) %collective-permute-start.32) | collective-permute-done | bytes 73760 | tf_op jit(solution)/shard_map/ppermute | solution.py:9
  126.8 2.0 %collective-permute-start.33 = (bf16[16,1152]{1,0:T(8,128)(2,1)S(1)}, bf16[16,1152]{1,0:T(8,128)(2,1)S(1)}, u32[]{:S(2)}, u32[]{:S(2)}) collective-permute-start(bf16[16,1152]{1,0:T(8,128)(2,1)S(1)} %fusion.73), channel_id=1, source_target_pairs={{0,2},{1,3},{2,0},{3,1},{4,6},{5,7},{6,4},{7,5},{8,10},{9,11},{10,... | collective-permute-start | bytes 110600 | tf_op jit(solution)/shard_map/ppermute | solution.py:9
  128.9 1.9 %collective-permute-start.38 = (bf16[16,1152]{1,0:T(8,128)(2,1)S(1)}, bf16[16,1152]{1,0:T(8,128)(2,1)S(1)}, u32[]{:S(2)}, u32[]{:S(2)}) collective-permute-start(bf16[16,1152]{1,0:T(8,128)(2,1)S(1)} %fusion.74), channel_id=1, source_target_pairs={{0,2},{1,3},{2,0},{3,1},{4,6},{5,7},{6,4},{7,5},{8,10},{9,11},{10,... | collective-permute-start | bytes 110600 | tf_op jit(solution)/shard_map/ppermute | solution.py:9
  131.8 2.4 %collective-permute-done.38 = bf16[16,1152]{1,0:T(8,128)(2,1)S(1)} collective-permute-done((bf16[16,1152]{1,0:T(8,128)(2,1)S(1)}, bf16[16,1152]{1,0:T(8,128)(2,1)S(1)}, u32[]{:S(2)}, u32[]{:S(2)}) %collective-permute-start.38) | collective-permute-done | bytes 36896 | tf_op jit(solution)/shard_map/ppermute | solution.py:9
  (179 shorter events, 30.6 us)
Async XLA Ops:
  0.6 98.0 %copy-start = (bf16[2304,512]{1,0:T(8,128)(2,1)S(1)}, bf16[2304,512]{1,0:T(8,128)(2,1)}, u32[]{:S(2)}) copy-start(bf16[2304,512]{1,0:T(8,128)(2,1)} %param.22) | copy-start | bytes 7077892
  0.6 8.9 %copy-start.4 = (bf16[2304,256]{1,0:T(8,128)(2,1)S(1)}, bf16[2304,256]{1,0:T(8,128)(2,1)}, u32[]{:S(2)}) copy-start(bf16[2304,256]{1,0:T(8,128)(2,1)} %param.19) | copy-start | bytes 3538948
  2.3 7.6 %collective-permute-start.4 = (f32[16,16]{0,1:T(8,128)S(1)}, f32[16,16]{0,1:T(8,128)}, u32[]{:S(2)}, u32[]{:S(2)}) collective-permute-start(f32[16,16]{0,1:T(8,128)S(1)} %get-tuple-element.35), channel_id=1, source_target_pairs={{0,1},{1,0},{2,3},{3,2},{4,5},{5,4},{6,7},{7,6},{8,9},{9,8},{10,11... | collective-permute-start | bytes 3080 | tf_op jit(solution)/shard_map/ppermute | solution.py:9
  6.4 6.8 %copy-start.5 = (bf16[2304,256]{1,0:T(8,128)(2,1)S(1)}, bf16[2304,256]{1,0:T(8,128)(2,1)}, u32[]{:S(2)}) copy-start(bf16[2304,256]{1,0:T(8,128)(2,1)} %param.20) | copy-start | bytes 3538948
  6.4 9.4 %collective-permute-start.2 = (bf16[2,2,16,1152]{3,2,1,0:T(8,128)(2,1)S(1)}, bf16[2,2,16,1152]{3,2,1,0:T(8,128)(2,1)S(1)}, u32[]{:S(2)}, u32[]{:S(2)}) collective-permute-start(bf16[2,2,16,1152]{3,2,1,0:T(8,128)(2,1)S(1)} %get-tuple-element.10), channel_id=1, source_target_pairs={{0,16},{4,20},{8,24},{12,28},{16,0},{20,4},{24,8},{28,12},{1,17},{... | collective-permute-start | bytes 442376 | tf_op jit(solution)/shard_map/ppermute | solution.py:9
  8.0 9.5 %collective-permute-start = (bf16[2,2,16,1152]{3,2,1,0:T(8,128)(2,1)S(1)}, bf16[2,2,16,1152]{3,2,1,0:T(8,128)(2,1)S(1)}, u32[]{:S(2)}, u32[]{:S(2)}) collective-permute-start(bf16[2,2,16,1152]{3,2,1,0:T(8,128)(2,1)S(1)} %get-tuple-element.11), channel_id=1, source_target_pairs={{0,8},{4,12},{8,0},{12,4},{16,24},{20,28},{24,16},{28,20},{1,9},{5... | collective-permute-start | bytes 442376 | tf_op jit(solution)/shard_map/ppermute | solution.py:9
  10.5 4.7 %collective-permute-start.5 = (f32[2,16,16]{1,2,0:T(8,128)S(1)}, f32[2,16,16]{1,2,0:T(8,128)S(1)}, u32[]{:S(2)}, u32[]{:S(2)}) collective-permute-start(f32[2,16,16]{1,2,0:T(8,128)S(1)} %get-tuple-element.33), channel_id=1, source_target_pairs={{0,2},{1,3},{2,0},{3,1},{4,6},{5,7},{6,4},{7,5},{8,10},{9,11},{10,... | collective-permute-start | bytes 6152 | tf_op jit(solution)/shard_map/ppermute | solution.py:9
  15.3 4.4 %collective-permute-start.6 = (f32[2,2,16,16]{2,3,1,0:T(8,128)S(1)}, f32[2,2,16,16]{2,3,1,0:T(8,128)S(1)}, u32[]{:S(2)}, u32[]{:S(2)}) collective-permute-start(f32[2,2,16,16]{2,3,1,0:T(8,128)S(1)} %get-tuple-element.31), channel_id=1, source_target_pairs={{0,8},{4,12},{8,0},{12,4},{16,24},{20,28},{24,16},{28,20},{1,9},{5... | collective-permute-start | bytes 12296 | tf_op jit(solution)/shard_map/ppermute | solution.py:9
  15.9 6.9 %collective-permute-start.3 = (bf16[2,2,2,16,1152]{4,3,2,1,0:T(8,128)(2,1)S(1)}, bf16[2,2,2,16,1152]{4,3,2,1,0:T(8,128)(2,1)S(1)}, u32[]{:S(2)}, u32[]{:S(2)}) collective-permute-start(bf16[2,2,2,16,1152]{4,3,2,1,0:T(8,128)(2,1)S(1)} %get-tuple-element.13), channel_id=1, source_target_pairs={{0,8},{4,12},{8,0},{12,4},{16,24},{20,28},{24,16},{28,20},{1,9},{5... | collective-permute-start | bytes 884744 | tf_op jit(solution)/shard_map/ppermute | solution.py:9
  17.5 7.0 %collective-permute-start.1 = (bf16[2,2,2,16,1152]{4,3,2,1,0:T(8,128)(2,1)S(1)}, bf16[2,2,2,16,1152]{4,3,2,1,0:T(8,128)(2,1)S(1)}, u32[]{:S(2)}, u32[]{:S(2)}) collective-permute-start(bf16[2,2,2,16,1152]{4,3,2,1,0:T(8,128)(2,1)S(1)} %get-tuple-element.7), channel_id=1, source_target_pairs={{0,16},{4,20},{8,24},{12,28},{16,0},{20,4},{24,8},{28,12},{1,17},{... | collective-permute-start | bytes 884744 | tf_op jit(solution)/shard_map/ppermute | solution.py:9
  19.7 5.5 %collective-permute-start.7 = (f32[2,2,2,16,16]{3,4,2,1,0:T(8,128)S(1)}, f32[2,2,2,16,16]{3,4,2,1,0:T(8,128)S(1)}, u32[]{:S(2)}, u32[]{:S(2)}) collective-permute-start(f32[2,2,2,16,16]{3,4,2,1,0:T(8,128)S(1)} %get-tuple-element.29), channel_id=1, source_target_pairs={{0,16},{4,20},{8,24},{12,28},{16,0},{20,4},{24,8},{28,12},{1,17},{... | collective-permute-start | bytes 24584 | tf_op jit(solution)/shard_map/ppermute | solution.py:9
  24.6 11.8 %collective-permute-start.9 = (bf16[256,2304]{1,0:T(8,128)(2,1)S(1)}, bf16[256,2304]{1,0:T(8,128)(2,1)}, u32[]{:S(2)}, u32[]{:S(2)}) collective-permute-start(bf16[256,2304]{1,0:T(8,128)(2,1)S(1)} %bitcast.250), channel_id=1, source_target_pairs={{0,4},{4,0},{8,12},{12,8},{16,20},{20,16},{24,28},{28,24},{1,5},{5... | collective-permute-start | bytes 3538952 | tf_op jit(solution)/shard_map/ppermute | solution.py:9
  25.9 2.1 %collective-permute-start.8 = (f32[2,2,2,2,16,16]{4,5,3,2,0,1:T(8,128)}, f32[2,2,2,2,16,16]{4,5,3,2,0,1:T(8,128)}, u32[]{:S(2)}, u32[]{:S(2)}) collective-permute-start(f32[2,2,2,2,16,16]{4,5,3,2,0,1:T(8,128)} %get-tuple-element.23), channel_id=1, source_target_pairs={{0,4},{4,0},{8,12},{12,8},{16,20},{20,16},{24,28},{28,24},{1,5},{5... | collective-permute-start | bytes 49160 | tf_op jit(solution)/shard_map/ppermute | solution.py:9
  32.5 8.2 %slice-start.2 = ((s8[4718592]{0:T(1024)(128)(4,1)}), s8[4194304]{0:T(1024)(128)(4,1)S(1)}, s32[]{:S(2)}) async-start(s8[4718592]{0:T(1024)(128)(4,1)} %bitcast.278), calls=%async_computation.2 | async-start | bytes 8388608
  36.4 7.1 %slice-start.4 = ((s8[4718592]{0:T(1024)(128)(4,1)}), s8[4194304]{0:T(1024)(128)(4,1)S(1)}, s32[]{:S(2)}) async-start(s8[4718592]{0:T(1024)(128)(4,1)} %bitcast.280), calls=%async_computation.4 | async-start | bytes 8388608
  45.2 2.1 %collective-permute-start.10 = (bf16[256,1152]{1,0:T(8,128)(2,1)S(1)}, bf16[256,1152]{1,0:T(8,128)(2,1)S(1)}, u32[]{:S(2)}, u32[]{:S(2)}) collective-permute-start(bf16[256,1152]{1,0:T(8,128)(2,1)S(1)} %fusion.8), channel_id=1, source_target_pairs={{0,4},{4,0},{8,12},{12,8},{16,20},{20,16},{24,28},{28,24},{1,5},{5... | collective-permute-start | bytes 1769480 | tf_op jit(solution)/shard_map/ppermute | solution.py:9
  45.5 4.3 %collective-permute-start.19 = (bf16[256,1152]{1,0:T(8,128)(2,1)S(1)}, bf16[256,1152]{1,0:T(8,128)(2,1)S(1)}, u32[]{:S(2)}, u32[]{:S(2)}) collective-permute-start(bf16[256,1152]{1,0:T(8,128)(2,1)S(1)} %fusion.9), channel_id=1, source_target_pairs={{0,4},{4,0},{8,12},{12,8},{16,20},{20,16},{24,28},{28,24},{1,5},{5... | collective-permute-start | bytes 1769480 | tf_op jit(solution)/shard_map/ppermute | solution.py:9
  49.2 9.0 %collective-permute-start.11 = (bf16[2,2,2,16,1152]{4,3,1,2,0:T(8,128)(2,1)S(1)}, bf16[2,2,2,16,1152]{4,3,1,2,0:T(8,128)(2,1)S(1)}, u32[]{:S(2)}, u32[]{:S(2)}) collective-permute-start(bf16[2,2,2,16,1152]{4,3,1,2,0:T(8,128)(2,1)S(1)} %copy.27), channel_id=1, source_target_pairs={{0,8},{4,12},{8,0},{12,4},{16,24},{20,28},{24,16},{28,20},{1,9},{5... | collective-permute-start | bytes 884744 | tf_op jit(solution)/shard_map/ppermute | solution.py:9
  49.7 8.5 %slice-start.1 = ((f32[256,1152]{1,0:T(8,128)}), f32[128,1152]{1,0:T(8,128)S(1)}, s32[]{:S(2)}) async-start(f32[256,1152]{1,0:T(8,128)} %copy-done.3), calls=%async_computation.1 | async-start | bytes 1179648 | tf_op jit(solution)/shard_map/slice | solution.py:31
  50.6 8.8 %collective-permute-start.20 = (bf16[2,2,2,16,1152]{4,3,1,2,0:T(8,128)(2,1)S(1)}, bf16[2,2,2,16,1152]{4,3,1,2,0:T(8,128)(2,1)S(1)}, u32[]{:S(2)}, u32[]{:S(2)}) collective-permute-start(bf16[2,2,2,16,1152]{4,3,1,2,0:T(8,128)(2,1)S(1)} %fusion.45), channel_id=1, source_target_pairs={{0,16},{4,20},{8,24},{12,28},{16,0},{20,4},{24,8},{28,12},{1,17},{... | collective-permute-start | bytes 884744 | tf_op jit(solution)/shard_map/ppermute | solution.py:9
  58.3 6.4 %copy-start.7 = (f32[64,1152]{1,0:T(8,128)S(1)}, f32[64,1152]{1,0:T(8,128)}, u32[]{:S(2)}) copy-start(f32[64,1152]{1,0:T(8,128)} %fusion.37) | copy-start | bytes 884740
  58.4 5.2 %collective-permute-start.12 = (bf16[2,2,16,1152]{3,2,0,1:T(8,128)(2,1)S(1)}, bf16[2,2,16,1152]{3,2,0,1:T(8,128)(2,1)S(1)}, u32[]{:S(2)}, u32[]{:S(2)}) collective-permute-start(bf16[2,2,16,1152]{3,2,0,1:T(8,128)(2,1)S(1)} %fusion.53), channel_id=1, source_target_pairs={{0,16},{4,20},{8,24},{12,28},{16,0},{20,4},{24,8},{28,12},{1,17},{... | collective-permute-start | bytes 442376 | tf_op jit(solution)/shard_map/ppermute | solution.py:9
  59.6 5.2 %collective-permute-start.21 = (bf16[2,2,16,1152]{3,2,0,1:T(8,128)(2,1)S(1)}, bf16[2,2,16,1152]{3,2,0,1:T(8,128)(2,1)S(1)}, u32[]{:S(2)}, u32[]{:S(2)}) collective-permute-start(bf16[2,2,16,1152]{3,2,0,1:T(8,128)(2,1)S(1)} %fusion.54), channel_id=1, source_target_pairs={{0,8},{4,12},{8,0},{12,4},{16,24},{20,28},{24,16},{28,20},{1,9},{5... | collective-permute-start | bytes 442376 | tf_op jit(solution)/shard_map/ppermute | solution.py:9
  63.6 4.4 %collective-permute-start.13 = (bf16[2,16,1152]{2,1,0:T(8,128)(2,1)S(1)}, bf16[2,16,1152]{2,1,0:T(8,128)(2,1)S(1)}, u32[]{:S(2)}, u32[]{:S(2)}) collective-permute-start(bf16[2,16,1152]{2,1,0:T(8,128)(2,1)S(1)} %fusion.61), channel_id=1, source_target_pairs={{0,1},{1,0},{2,3},{3,2},{4,5},{5,4},{6,7},{7,6},{8,9},{9,8},{10,11... | collective-permute-start | bytes 221192 | tf_op jit(solution)/shard_map/ppermute | solution.py:9
  64.8 5.8 %collective-permute-start.22 = (bf16[2,16,1152]{2,1,0:T(8,128)(2,1)S(1)}, bf16[2,16,1152]{2,1,0:T(8,128)(2,1)S(1)}, u32[]{:S(2)}, u32[]{:S(2)}) collective-permute-start(bf16[2,16,1152]{2,1,0:T(8,128)(2,1)S(1)} %fusion.62), channel_id=1, source_target_pairs={{0,1},{1,0},{2,3},{3,2},{4,5},{5,4},{6,7},{7,6},{8,9},{9,8},{10,11... | collective-permute-start | bytes 221192 | tf_op jit(solution)/shard_map/ppermute | solution.py:9
  68.1 5.8 %collective-permute-start.14 = (bf16[16,1152]{1,0:T(8,128)(2,1)S(1)}, bf16[16,1152]{1,0:T(8,128)(2,1)S(1)}, u32[]{:S(2)}, u32[]{:S(2)}) collective-permute-start(bf16[16,1152]{1,0:T(8,128)(2,1)S(1)} %fusion.71), channel_id=1, source_target_pairs={{0,2},{1,3},{2,0},{3,1},{4,6},{5,7},{6,4},{7,5},{8,10},{9,11},{10,... | collective-permute-start | bytes 110600 | tf_op jit(solution)/shard_map/ppermute | solution.py:9
  70.7 5.8 %collective-permute-start.23 = (bf16[16,1152]{1,0:T(8,128)(2,1)S(1)}, bf16[16,1152]{1,0:T(8,128)(2,1)S(1)}, u32[]{:S(2)}, u32[]{:S(2)}) collective-permute-start(bf16[16,1152]{1,0:T(8,128)(2,1)S(1)} %fusion.72), channel_id=1, source_target_pairs={{0,2},{1,3},{2,0},{3,1},{4,6},{5,7},{6,4},{7,5},{8,10},{9,11},{10,... | collective-permute-start | bytes 110600 | tf_op jit(solution)/shard_map/ppermute | solution.py:9
  73.9 4.9 %collective-permute-start.15 = (bf16[16,1152]{1,0:T(8,128)(2,1)S(1)}, bf16[16,1152]{1,0:T(8,128)(2,1)S(1)}, u32[]{:S(2)}, u32[]{:S(2)}) collective-permute-start(bf16[16,1152]{1,0:T(8,128)(2,1)S(1)} %fusion.70), channel_id=1, source_target_pairs={{0,2},{1,3},{2,0},{3,1},{4,6},{5,7},{6,4},{7,5},{8,10},{9,11},{10,... | collective-permute-start | bytes 110600 | tf_op jit(solution)/shard_map/ppermute | solution.py:9
  76.6 4.9 %collective-permute-start.24 = (bf16[16,1152]{1,0:T(8,128)(2,1)S(1)}, bf16[16,1152]{1,0:T(8,128)(2,1)S(1)}, u32[]{:S(2)}, u32[]{:S(2)}) collective-permute-start(bf16[16,1152]{1,0:T(8,128)(2,1)S(1)} %fusion.68), channel_id=1, source_target_pairs={{0,2},{1,3},{2,0},{3,1},{4,6},{5,7},{6,4},{7,5},{8,10},{9,11},{10,... | collective-permute-start | bytes 110600 | tf_op jit(solution)/shard_map/ppermute | solution.py:9
  78.8 4.4 %collective-permute-start.16 = (bf16[2,16,1152]{2,1,0:T(8,128)(2,1)S(1)}, bf16[2,16,1152]{2,1,0:T(8,128)(2,1)S(1)}, u32[]{:S(2)}, u32[]{:S(2)}) collective-permute-start(bf16[2,16,1152]{2,1,0:T(8,128)(2,1)S(1)} %get-tuple-element.25), channel_id=1, source_target_pairs={{0,1},{1,0},{2,3},{3,2},{4,5},{5,4},{6,7},{7,6},{8,9},{9,8},{10,11... | collective-permute-start | bytes 221192 | tf_op jit(solution)/shard_map/ppermute | solution.py:9
  81.5 4.4 %collective-permute-start.25 = (bf16[2,16,1152]{2,1,0:T(8,128)(2,1)S(1)}, bf16[2,16,1152]{2,1,0:T(8,128)(2,1)S(1)}, u32[]{:S(2)}, u32[]{:S(2)}) collective-permute-start(bf16[2,16,1152]{2,1,0:T(8,128)(2,1)S(1)} %get-tuple-element.27), channel_id=1, source_target_pairs={{0,1},{1,0},{2,3},{3,2},{4,5},{5,4},{6,7},{7,6},{8,9},{9,8},{10,11... | collective-permute-start | bytes 221192 | tf_op jit(solution)/shard_map/ppermute | solution.py:9
  83.3 6.8 %collective-permute-start.17 = (bf16[2,2,16,1152]{3,2,1,0:T(8,128)(2,1)S(1)}, bf16[2,2,16,1152]{3,2,1,0:T(8,128)(2,1)S(1)}, u32[]{:S(2)}, u32[]{:S(2)}) collective-permute-start(bf16[2,2,16,1152]{3,2,1,0:T(8,128)(2,1)S(1)} %get-tuple-element.19), channel_id=1, source_target_pairs={{0,16},{4,20},{8,24},{12,28},{16,0},{20,4},{24,8},{28,12},{1,17},{... | collective-permute-start | bytes 442376 | tf_op jit(solution)/shard_map/ppermute | solution.py:9
  86.0 5.2 %collective-permute-start.26 = (bf16[2,2,16,1152]{3,2,1,0:T(8,128)(2,1)S(1)}, bf16[2,2,16,1152]{3,2,1,0:T(8,128)(2,1)S(1)}, u32[]{:S(2)}, u32[]{:S(2)}) collective-permute-start(bf16[2,2,16,1152]{3,2,1,0:T(8,128)(2,1)S(1)} %get-tuple-element.21), channel_id=1, source_target_pairs={{0,8},{4,12},{8,0},{12,4},{16,24},{20,28},{24,16},{28,20},{1,9},{5... | collective-permute-start | bytes 442376 | tf_op jit(solution)/shard_map/ppermute | solution.py:9
  90.1 6.8 %collective-permute-start.18 = (bf16[2,2,2,16,1152]{4,3,2,1,0:T(8,128)(2,1)S(1)}, bf16[2,2,2,16,1152]{4,3,2,1,0:T(8,128)(2,1)S(1)}, u32[]{:S(2)}, u32[]{:S(2)}) collective-permute-start(bf16[2,2,2,16,1152]{4,3,2,1,0:T(8,128)(2,1)S(1)} %get-tuple-element.3), channel_id=1, source_target_pairs={{0,8},{4,12},{8,0},{12,4},{16,24},{20,28},{24,16},{28,20},{1,9},{5... | collective-permute-start | bytes 884744 | tf_op jit(solution)/shard_map/ppermute | solution.py:9
  91.2 6.8 %collective-permute-start.27 = (bf16[2,2,2,16,1152]{4,3,2,1,0:T(8,128)(2,1)S(1)}, bf16[2,2,2,16,1152]{4,3,2,1,0:T(8,128)(2,1)S(1)}, u32[]{:S(2)}, u32[]{:S(2)}) collective-permute-start(bf16[2,2,2,16,1152]{4,3,2,1,0:T(8,128)(2,1)S(1)} %get-tuple-element.5), channel_id=1, source_target_pairs={{0,16},{4,20},{8,24},{12,28},{16,0},{20,4},{24,8},{28,12},{1,17},{... | collective-permute-start | bytes 884744 | tf_op jit(solution)/shard_map/ppermute | solution.py:9
  98.1 3.0 %collective-permute-start.28 = (bf16[256,2304]{1,0:T(8,128)(2,1)S(1)}, bf16[256,2304]{1,0:T(8,128)(2,1)}, u32[]{:S(2)}, u32[]{:S(2)}) collective-permute-start(bf16[256,2304]{1,0:T(8,128)(2,1)S(1)} %bitcast.248), channel_id=1, source_target_pairs={{0,4},{4,0},{8,12},{12,8},{16,20},{20,16},{24,28},{28,24},{1,5},{5... | collective-permute-start | bytes 3538952 | tf_op jit(solution)/shard_map/ppermute | solution.py:9
  104.3 2.1 %collective-permute-start.29 = (bf16[256,1152]{1,0:T(8,128)(2,1)S(1)}, bf16[256,1152]{1,0:T(8,128)(2,1)S(1)}, u32[]{:S(2)}, u32[]{:S(2)}) collective-permute-start(bf16[256,1152]{1,0:T(8,128)(2,1)S(1)} %convolution_convert_fusion.1), channel_id=1, source_target_pairs={{0,4},{4,0},{8,12},{12,8},{16,20},{20,16},{24,28},{28,24},{1,5},{5... | collective-permute-start | bytes 1769480 | tf_op jit(solution)/shard_map/ppermute | solution.py:9
  104.5 4.4 %collective-permute-start.34 = (bf16[256,1152]{1,0:T(8,128)(2,1)S(1)}, bf16[256,1152]{1,0:T(8,128)(2,1)S(1)}, u32[]{:S(2)}, u32[]{:S(2)}) collective-permute-start(bf16[256,1152]{1,0:T(8,128)(2,1)S(1)} %convolution_convert_fusion), channel_id=1, source_target_pairs={{0,4},{4,0},{8,12},{12,8},{16,20},{20,16},{24,28},{28,24},{1,5},{5... | collective-permute-start | bytes 1769480 | tf_op jit(solution)/shard_map/ppermute | solution.py:9
  108.0 9.1 %collective-permute-start.30 = (bf16[2,2,2,16,1152]{4,3,1,2,0:T(8,128)(2,1)S(1)}, bf16[2,2,2,16,1152]{4,3,1,2,0:T(8,128)(2,1)S(1)}, u32[]{:S(2)}, u32[]{:S(2)}) collective-permute-start(bf16[2,2,2,16,1152]{4,3,1,2,0:T(8,128)(2,1)S(1)} %copy.37), channel_id=1, source_target_pairs={{0,8},{4,12},{8,0},{12,4},{16,24},{20,28},{24,16},{28,20},{1,9},{5... | collective-permute-start | bytes 884744 | tf_op jit(solution)/shard_map/ppermute | solution.py:9
  109.0 8.0 %slice-start = ((f32[256,1152]{1,0:T(8,128)}), f32[128,1152]{1,0:T(8,128)S(1)}, s32[]{:S(2)}) async-start(f32[256,1152]{1,0:T(8,128)} %copy-done.1), calls=%async_computation | async-start | bytes 1179648 | tf_op jit(solution)/shard_map/slice | solution.py:31
  109.5 8.8 %collective-permute-start.35 = (bf16[2,2,2,16,1152]{4,3,1,2,0:T(8,128)(2,1)S(1)}, bf16[2,2,2,16,1152]{4,3,1,2,0:T(8,128)(2,1)S(1)}, u32[]{:S(2)}, u32[]{:S(2)}) collective-permute-start(bf16[2,2,2,16,1152]{4,3,1,2,0:T(8,128)(2,1)S(1)} %fusion.46), channel_id=1, source_target_pairs={{0,16},{4,20},{8,24},{12,28},{16,0},{20,4},{24,8},{28,12},{1,17},{... | collective-permute-start | bytes 884744 | tf_op jit(solution)/shard_map/ppermute | solution.py:9
  117.1 5.2 %collective-permute-start.31 = (bf16[2,2,16,1152]{3,2,0,1:T(8,128)(2,1)S(1)}, bf16[2,2,16,1152]{3,2,0,1:T(8,128)(2,1)S(1)}, u32[]{:S(2)}, u32[]{:S(2)}) collective-permute-start(bf16[2,2,16,1152]{3,2,0,1:T(8,128)(2,1)S(1)} %fusion.55), channel_id=1, source_target_pairs={{0,16},{4,20},{8,24},{12,28},{16,0},{20,4},{24,8},{28,12},{1,17},{... | collective-permute-start | bytes 442376 | tf_op jit(solution)/shard_map/ppermute | solution.py:9
  118.5 5.2 %collective-permute-start.36 = (bf16[2,2,16,1152]{3,2,0,1:T(8,128)(2,1)S(1)}, bf16[2,2,16,1152]{3,2,0,1:T(8,128)(2,1)S(1)}, u32[]{:S(2)}, u32[]{:S(2)}) collective-permute-start(bf16[2,2,16,1152]{3,2,0,1:T(8,128)(2,1)S(1)} %fusion.56), channel_id=1, source_target_pairs={{0,8},{4,12},{8,0},{12,4},{16,24},{20,28},{24,16},{28,20},{1,9},{5... | collective-permute-start | bytes 442376 | tf_op jit(solution)/shard_map/ppermute | solution.py:9
  122.3 11.8 %copy-start.9 = (f32[2304]{0:T(1024)S(1)}, f32[2304]{0:T(1024)}, u32[]{:S(2)}) copy-start(f32[2304]{0:T(1024)} %param.25) | copy-start | bytes 27652
  122.4 4.4 %collective-permute-start.32 = (bf16[2,16,1152]{2,1,0:T(8,128)(2,1)S(1)}, bf16[2,16,1152]{2,1,0:T(8,128)(2,1)S(1)}, u32[]{:S(2)}, u32[]{:S(2)}) collective-permute-start(bf16[2,16,1152]{2,1,0:T(8,128)(2,1)S(1)} %fusion.63), channel_id=1, source_target_pairs={{0,1},{1,0},{2,3},{3,2},{4,5},{5,4},{6,7},{7,6},{8,9},{9,8},{10,11... | collective-permute-start | bytes 221192 | tf_op jit(solution)/shard_map/ppermute | solution.py:9
  123.7 5.1 %collective-permute-start.37 = (bf16[2,16,1152]{2,1,0:T(8,128)(2,1)S(1)}, bf16[2,16,1152]{2,1,0:T(8,128)(2,1)S(1)}, u32[]{:S(2)}, u32[]{:S(2)}) collective-permute-start(bf16[2,16,1152]{2,1,0:T(8,128)(2,1)S(1)} %fusion.64), channel_id=1, source_target_pairs={{0,1},{1,0},{2,3},{3,2},{4,5},{5,4},{6,7},{7,6},{8,9},{9,8},{10,11... | collective-permute-start | bytes 221192 | tf_op jit(solution)/shard_map/ppermute | solution.py:9
  126.8 4.9 %collective-permute-start.33 = (bf16[16,1152]{1,0:T(8,128)(2,1)S(1)}, bf16[16,1152]{1,0:T(8,128)(2,1)S(1)}, u32[]{:S(2)}, u32[]{:S(2)}) collective-permute-start(bf16[16,1152]{1,0:T(8,128)(2,1)S(1)} %fusion.73), channel_id=1, source_target_pairs={{0,2},{1,3},{2,0},{3,1},{4,6},{5,7},{6,4},{7,5},{8,10},{9,11},{10,... | collective-permute-start | bytes 110600 | tf_op jit(solution)/shard_map/ppermute | solution.py:9
  128.9 5.2 %collective-permute-start.38 = (bf16[16,1152]{1,0:T(8,128)(2,1)S(1)}, bf16[16,1152]{1,0:T(8,128)(2,1)S(1)}, u32[]{:S(2)}, u32[]{:S(2)}) collective-permute-start(bf16[16,1152]{1,0:T(8,128)(2,1)S(1)} %fusion.74), channel_id=1, source_target_pairs={{0,2},{1,3},{2,0},{3,1},{4,6},{5,7},{6,4},{7,5},{8,10},{9,11},{10,... | collective-permute-start | bytes 110600 | tf_op jit(solution)/shard_map/ppermute | solution.py:9
  (9 other events, 24.9 us)

commit v2 on v0

v2 whole, which is shorter than its diff:
```python
import jax
import jax.numpy as jnp
from jax import lax
from jax.sharding import PartitionSpec as P

CHUNKS = 2


def swap(value, axis, r):
    return lax.ppermute(value, axis, [(i, i ^ r) for i in range(lax.axis_size(axis))])


def dot(a, b):
    return jnp.dot(a, b, preferred_element_type=jnp.float32)


def half(value):
    return value.astype(jnp.bfloat16)


def full(value):
    return value.astype(jnp.float32)


def routing_table(expert_ids, gate_weights, planes, feats):
    own, top = expert_ids.shape
    high = half(gate_weights)
    low = half(gate_weights - full(high))
    row = jnp.concatenate([half(expert_ids), high, low], axis=1)
    row = jnp.pad(row, ((0, 0), (0, 128 - 3 * top)))
    mine = jnp.arange(feats, dtype=jnp.int32)[:, None, None] == lax.axis_index("feat")
    table = jnp.where(mine, row[None], jnp.zeros_like(row)[None])
    bit = 1
    while bit < feats:
        table = table + swap(table, "feat", bit)
        bit *= 2
    table = table[None]
    bit = 1
    while bit < planes:
        table = jnp.concatenate([table, swap(table, "expert", 2 * bit)], axis=0)
        bit *= 2
    return table, swap(table, "expert", 1)


def chunk_rows(value, planes, feats):
    own = value.shape[2]
    value = value.reshape(planes, feats, CHUNKS, own // CHUNKS, value.shape[-1])
    return value.transpose(2, 0, 1, 3, 4).reshape(-1, value.shape[-1])


def shards(
    tokens,
    expert_ids,
    gate_weights,
    expert_gate,
    expert_up,
    expert_down,
    shared_gate,
    shared_up,
    shared_down,
    encoder,
    encoder_bias,
    decoder,
    decoder_bias,
):
    own, top = expert_ids.shape
    width = tokens.shape[1]
    feats = lax.axis_size("feat")
    planes = lax.axis_size("expert") // 2
    devices = 2 * planes * feats
    local_experts = expert_gate.shape[0]
    me = lax.axis_index(("expert", "feat"))
    my_feat = lax.axis_index("feat")
    step = own // CHUNKS
    rows = planes * feats * step

    table_near, table_far = routing_table(expert_ids, gate_weights, planes, feats)

    pieces = [tokens] + [swap(tokens, "expert", 2 * p) for p in range(1, planes)]
    near = chunk_rows(jnp.stack(pieces).reshape(planes, feats, own, width), planes, feats)
    far = swap(near, "expert", 1)

    def scales(table):
        table = chunk_rows(table, planes, feats)
        ids = table[:, :top].astype(jnp.int32)
        weights = full(table[:, top : 2 * top]) + full(table[:, 2 * top : 3 * top])
        return [
            jnp.sum(jnp.where(ids == me * local_experts + j, weights, 0.0), axis=1)[:, None]
            for j in range(local_experts)
        ]

    def swiglu(x, gate, up):
        return half(jax.nn.silu(dot(x, gate)) * dot(x, up))

    def expert_hidden(x):
        return [swiglu(x, expert_gate[j], expert_up[j]) for j in range(local_experts)]

    def expert_out(hidden, scale, c):
        cut = slice(c * rows, (c + 1) * rows)
        return sum(
            dot(hidden[j][cut], expert_down[j]) * scale[j][cut] for j in range(local_experts)
        )

    hidden_near = expert_hidden(near)
    scale_near, scale_far = scales(table_near), scales(table_far)
    received = [
        swap(half(expert_out(hidden_near, scale_near, c)), "expert", 1) for c in range(CHUNKS)
    ]
    hidden_far = expert_hidden(far)
    shared_rows = far.reshape(CHUNKS, planes, feats * step, width)[:, 0]
    shared_rows = shared_rows.reshape(CHUNKS * feats * step, width)
    shared_out = dot(swiglu(shared_rows, shared_gate, shared_up), shared_down)
    shared_out = shared_out.reshape(CHUNKS, feats, step, width)

    near_rows = []
    for c in range(CHUNKS):
        total = expert_out(hidden_far, scale_far, c) + full(received[c])
        total = total.reshape(planes, feats, step, width)
        arrived = [swap(half(total[p]), "expert", 2 * p) for p in range(1, planes)]
        total = total[0] + shared_out[c] + sum(full(a) for a in arrived)
        block = [lax.dynamic_index_in_dim(total, my_feat ^ r, 0, False) for r in range(feats)]
        arrived = [swap(half(block[r]), "feat", r) for r in range(1, feats)]
        moe_out = half(block[0] + sum(full(a) for a in arrived))
        pieces = jnp.stack([moe_out] + [swap(moe_out, "feat", r) for r in range(1, feats)])
        pieces = [pieces] + [swap(pieces, "expert", 2 * p) for p in range(1, planes)]
        near_rows.append(jnp.stack(pieces).reshape(rows, width))

    def encode(x):
        return half(jax.nn.relu(dot(x, encoder) + encoder_bias[None, :]))

    features, reconstruction = [], []
    for c in range(CHUNKS):
        near, far = near_rows[c], swap(near_rows[c], "expert", 1)
        features_near = encode(near)
        arrived = swap(half(dot(features_near, decoder)), "expert", 1)
        features_far = encode(far)
        total = dot(features_far, decoder) + full(arrived)
        total = total.reshape(planes, feats, step, width)
        arrived = [swap(half(total[p]), "expert", 2 * p) for p in range(1, planes)]
        total = total[0] + sum(full(a) for a in arrived)
        arrived = [swap(half(total[r]), "feat", r) for r in range(1, feats)]
        reconstruction.append(total[0] + sum(full(a) for a in arrived) + decoder_bias[None, :])
        both = jnp.stack([features_far, features_near])
        features.append(both.reshape(2, planes, feats, step, -1))
    reconstruction = jnp.concatenate(reconstruction, axis=0)

    features = jnp.stack(features).transpose(2, 1, 3, 0, 4, 5).reshape(devices, own, -1)
    blocks = [lax.dynamic_index_in_dim(features, i ^ me, 0) for i in range(devices)]
    features = jnp.concatenate(blocks, axis=0).reshape(devices * own, -1)
    return (features, reconstruction)


def solution(mesh):
    return jax.shard_map(
        shards,
        mesh=mesh,
        in_specs=(
            P("expert", None),
            P(("expert", "feat"), None),
            P(("expert", "feat"), None),
            P(("expert", "feat"), None, None),
            P(("expert", "feat"), None, None),
            P(("expert", "feat"), None, None),
            P(None, "feat"),
            P(None, "feat"),
            P("feat", None),
            P(None, ("expert", "feat")),
            P(("expert", "feat")),
            P(("expert", "feat"), None),
            P(),
        ),
        out_specs=(P(None, ("expert", "feat")), P(("expert", "feat"), None)),
        check_vma=False,
    )
```

time: 282 us -> 127 us (0.45)
  waiting for transfers between devices: 193 us -> 29.5 us
  starting transfers between devices: 2.78 us -> 62.1 us
  blocking collectives: 37.2 us -> 0 us
  between operations: 13.9 us -> 1.37 us
  matrix products: 29.4 us -> 20.4 us
  other arithmetic: 2.01 us -> 7.7 us
  local copies, waits for them, and re-layouts: 2.81 us -> 5.68 us
    reduce_scatter x2 -> x0, waiting for transfers between devices: 133 us -> none  [the longest x1 106 us: shards(): lax.psum_scatter(jnp.dot(block_rows, decoder, preferred_element_type=jnp....]
    ppermute x0 -> x51, starting transfers between devices: none -> 62.1 us  [swap(): lax.ppermute(value, axis, [(i, i ^ r) for i in range(lax.axis_size(axis))])]
    all_gather x1 -> x0, waiting for transfers between devices: 57.3 us -> none  [shards(): lax.all_gather(moe_out, ('expert', 'feat'), axis=0, tiled=True)]
    all_to_all x1 -> x0, blocking collectives: 37.2 us -> none  [shards(): lax.all_to_all(outgoing, ('expert', 'feat'), split_axis=0, concat_axis=0,...]
    ppermute x0 -> x51, waiting for transfers between devices: none -> 29.5 us  [swap(): lax.ppermute(value, axis, [(i, i ^ r) for i in range(lax.axis_size(axis))])]
    dot_general x9 -> x18, matrix products: 29.4 us -> 20.4 us  [dot(): return jnp.dot(a, b, preferred_element_type=jnp.float32)]
  transfers between devices with their start and end apart: 4 -> 51, of which waited for: 4 -> 21; matrix products, arithmetic and copies ran while one was open for 3% -> 19% of each run, Pallas kernels for 0% -> 0%
where the time goes in v2:
time: 127 us
  starting transfers between devices  62.1 us (49%)
  waiting for transfers between devices  29.5 us (23%)
  matrix products  20.4 us (16%)
  other arithmetic  7.7 us (6%)
  local copies, waits for them, and re-layouts  5.68 us (4%)
  between operations  1.37 us (1%)
    ppermute x51, starting transfers between devices, swap(): lax.ppermute(value, axis, [(i, i ^ r) for i in range(lax.axis_size(axis))])  62.1 us
    ppermute x51, waiting for transfers between devices, swap(): lax.ppermute(value, axis, [(i, i ^ r) for i in range(lax.axis_size(axis))])  29.5 us
    dot_general x18, matrix products, dot(): return jnp.dot(a, b, preferred_element_type=jnp.float32)  20.4 us
    unnamed x60, local copies, waits for them, and re-layouts  3.93 us
  transfers between devices with their start and end apart: 51, of which 21 were waited for; matrix products, arithmetic and copies ran while one was open for 19% of the time, Pallas kernels for 0%

profile of v2, /device:TPU:0, one launch (start us, length us, event | category | flops | bytes accessed | tf_op | source)
XLA Modules:
  0.0 126.8 jit_solution(8991617356217389479)
XLA Ops:
  2.4 3.0 %collective-permute-start.4 = (bf16[4,16,128]{2,1,0:T(8,128)(2,1)S(1)}, bf16[4,16,128]{2,1,0:T(8,128)(2,1)S(1)}, u32[]{:S(2)}, u32[]{:S(2)}) collective-permute-start(bf16[4,16,128]{2,1,0:T(8,128)(2,1)S(1)} %broadcast_select_fusion), channel_id=1, source_target_pairs={{0,1},{1,0},{2,3},{3,2},{4,5},{5,4},{6,7},{7,6},{8,9},{9,8},{10,11... | collective-permute-start | bytes 49160 | tf_op jit(solution)/shard_map/ppermute | solution.py:10
  5.4 1.7 %collective-permute-done.4 = bf16[4,16,128]{2,1,0:T(8,128)(2,1)S(1)} collective-permute-done((bf16[4,16,128]{2,1,0:T(8,128)(2,1)S(1)}, bf16[4,16,128]{2,1,0:T(8,128)(2,1)S(1)}, u32[]{:S(2)}, u32[]{:S(2)}) %collective-permute-start.4) | collective-permute-done | bytes 16416 | tf_op jit(solution)/shard_map/ppermute | solution.py:10
  7.2 3.0 %collective-permute-start.5 = (bf16[4,16,128]{2,1,0:T(8,128)(2,1)S(1)}, bf16[4,16,128]{2,1,0:T(8,128)(2,1)S(1)}, u32[]{:S(2)}, u32[]{:S(2)}) collective-permute-start(bf16[4,16,128]{2,1,0:T(8,128)(2,1)S(1)} %fusion.76), channel_id=1, source_target_pairs={{0,2},{1,3},{2,0},{3,1},{4,6},{5,7},{6,4},{7,5},{8,10},{9,11},{10,... | collective-permute-start | bytes 49160 | tf_op jit(solution)/shard_map/ppermute | solution.py:10
  10.3 1.7 %collective-permute-done.5 = bf16[4,16,128]{2,1,0:T(8,128)(2,1)S(1)} collective-permute-done((bf16[4,16,128]{2,1,0:T(8,128)(2,1)S(1)}, bf16[4,16,128]{2,1,0:T(8,128)(2,1)S(1)}, u32[]{:S(2)}, u32[]{:S(2)}) %collective-permute-start.5) | collective-permute-done | bytes 16416 | tf_op jit(solution)/shard_map/ppermute | solution.py:10
  12.7 1.8 %collective-permute-start.6 = (bf16[1,4,16,128]{3,2,1,0:T(8,128)(2,1)S(1)}, bf16[1,4,16,128]{3,2,1,0:T(8,128)(2,1)S(1)}, u32[]{:S(2)}, u32[]{:S(2)}) collective-permute-start(bf16[1,4,16,128]{3,2,1,0:T(8,128)(2,1)S(1)} %get-tuple-element.43), channel_id=1, source_target_pairs={{0,8},{4,12},{8,0},{12,4},{16,24},{20,28},{24,16},{28,20},{1,9},{5... | collective-permute-start | bytes 49160 | tf_op jit(solution)/shard_map/ppermute | solution.py:10
  14.5 1.9 %collective-permute-done.6 = bf16[1,4,16,128]{3,2,1,0:T(8,128)(2,1)S(1)} collective-permute-done((bf16[1,4,16,128]{3,2,1,0:T(8,128)(2,1)S(1)}, bf16[1,4,16,128]{3,2,1,0:T(8,128)(2,1)S(1)}, u32[]{:S(2)}, u32[]{:S(2)}) %collective-permute-start.6) | collective-permute-done | bytes 16416 | tf_op jit(solution)/shard_map/ppermute | solution.py:10
  17.1 1.8 %collective-permute-start.7 = (bf16[2,4,16,128]{3,2,1,0:T(8,128)(2,1)}, bf16[2,4,16,128]{3,2,1,0:T(8,128)(2,1)}, u32[]{:S(2)}, u32[]{:S(2)}) collective-permute-start(bf16[2,4,16,128]{3,2,1,0:T(8,128)(2,1)} %pad_maximum_fusion.6), channel_id=1, source_target_pairs={{0,16},{4,20},{8,24},{12,28},{16,0},{20,4},{24,8},{28,12},{1,17},{... | collective-permute-start | bytes 98312 | tf_op jit(solution)/shard_map/ppermute | solution.py:10
  18.9 1.4 %collective-permute-start.2 = (bf16[64,2304]{1,0:T(8,128)(2,1)}, bf16[64,2304]{1,0:T(8,128)(2,1)S(1)}, u32[]{:S(2)}, u32[]{:S(2)}) collective-permute-start(bf16[64,2304]{1,0:T(8,128)(2,1)} %param.13), channel_id=1, source_target_pairs={{0,24},{4,28},{8,16},{12,20},{16,8},{20,12},{24,0},{28,4},{1,25},{... | collective-permute-start | bytes 884744 | tf_op jit(solution)/shard_map/ppermute | solution.py:10
  20.3 1.5 %collective-permute-start.1 = (bf16[64,2304]{1,0:T(8,128)(2,1)}, bf16[64,2304]{1,0:T(8,128)(2,1)S(1)}, u32[]{:S(2)}, u32[]{:S(2)}) collective-permute-start(bf16[64,2304]{1,0:T(8,128)(2,1)} %param.13), channel_id=1, source_target_pairs={{0,16},{4,20},{8,24},{12,28},{16,0},{20,4},{24,8},{28,12},{1,17},{... | collective-permute-start | bytes 884744 | tf_op jit(solution)/shard_map/ppermute | solution.py:10
  25.2 3.2 %collective-permute-done.2 = bf16[64,2304]{1,0:T(8,128)(2,1)S(1)} collective-permute-done((bf16[64,2304]{1,0:T(8,128)(2,1)}, bf16[64,2304]{1,0:T(8,128)(2,1)S(1)}, u32[]{:S(2)}, u32[]{:S(2)}) %collective-permute-start.2) | collective-permute-done | bytes 294944 | tf_op jit(solution)/shard_map/ppermute | solution.py:10
  28.3 3.4 %collective-permute-done.1 = bf16[64,2304]{1,0:T(8,128)(2,1)S(1)} collective-permute-done((bf16[64,2304]{1,0:T(8,128)(2,1)}, bf16[64,2304]{1,0:T(8,128)(2,1)S(1)}, u32[]{:S(2)}, u32[]{:S(2)}) %collective-permute-start.1) | collective-permute-done | bytes 294944 | tf_op jit(solution)/shard_map/ppermute | solution.py:10
  32.0 2.0 %copy-done.9 = bf16[1,2304,1024]{2,1,0:T(8,128)(2,1)S(1)} copy-done((bf16[1,2304,1024]{2,1,0:T(8,128)(2,1)S(1)}, bf16[1,2304,1024]{2,1,0:T(8,128)(2,1)}, u32[]{:S(2)}) %copy-start.9) | copy-done | bytes 4718616
  34.0 1.4 %fusion.12 = f32[256,1024]{1,0:T(8,128)S(1)} fusion(bf16[256,2304]{1,0:T(8,128)(2,1)S(1)} %bitcast.255, bf16[1,2304,1024]{2,1,0:T(8,128)(2,1)S(1)} %copy-done.9), kind=kOutput, calls=%fused_computation.12 | convolution fusion | flops 1207959552 | bytes 6946816 | tf_op jit(solution)/shard_map/dot_general | solution.py:14
  35.5 4.0 %fusion.37 = bf16[256,1024]{1,0:T(8,128)(2,1)S(1)} fusion(bf16[256,2304]{1,0:T(8,128)(2,1)S(1)} %bitcast.256, bf16[1,2304,1024]{2,1,0:T(8,128)(2,1)} %param.17, f32[256,1024]{1,0:T(8,128)S(1)} %fusion.12), kind=kOutput, calls=%fused_computation.25 | convolution fusion | flops 1209532416 | bytes 7471104 | tf_op jit(solution)/shard_map/dot_general | solution.py:14
  41.8 1.4 %fusion.14 = f32[256,1024]{1,0:T(8,128)S(1)} fusion(bf16[256,2304]{1,0:T(8,128)(2,1)S(1)} %collective-permute-done.3, bf16[1,2304,1024]{2,1,0:T(8,128)(2,1)S(1)} %copy-done.9), kind=kOutput, calls=%fused_computation.14 | convolution fusion | flops 1207959552 | bytes 6946816 | tf_op jit(solution)/shard_map/dot_general | solution.py:14
  44.1 1.6 %multiply_convert_fusion = bf16[256,1024]{1,0:T(8,128)(2,1)S(1)} fusion(f32[256,1024]{1,0:T(8,128)S(1)} %fusion.14, bf16[256,2304]{1,0:T(8,128)(2,1)S(1)} %collective-permute-done.3, bf16[1,2304,1024]{2,1,0:T(8,128)(2,1)S(1)} %bitcast.286), kind=kOutput, calls=%fused_computation.43 | convolution fusion | flops 1209532416 | bytes 7471104 | tf_op jit(solution)/shard_map/dot_general | solution.py:14
  45.7 1.9 %fusion.88 = (bf16[128,2304]{1,0:T(8,128)(2,1)S(1)}, f32[128,2304]{1,0:T(8,128)}) fusion(bf16[128,2304]{1,0:T(8,128)(2,1)S(1)} %collective-permute-done.9, f32[128]{0:T(128)S(1)} %get-tuple-element.46, bf16[1,1024,2304]{2,1,0:T(8,128)(2,1)S(1)} %bitcast.215, bf16[256,1024]{1,0:T(8,128)(2,1)S(1)} %multiply_convert_fusion), kind=kOutput, calls=%fused_computation.162 | convolution fusion | flops 605159424 | bytes 7340544 | tf_op jit(solution)/shard_map/dot_general | solution.py:14
  48.2 1.4 %collective-permute-start.12 = (bf16[4,8,2304]{2,1,0:T(8,128)(2,1)S(1)}, bf16[4,8,2304]{2,1,0:T(8,128)(2,1)S(1)}, u32[]{:S(2)}, u32[]{:S(2)}) collective-permute-start(bf16[4,8,2304]{2,1,0:T(8,128)(2,1)S(1)} %get-tuple-element.21), channel_id=1, source_target_pairs={{0,24},{4,28},{8,16},{12,20},{16,8},{20,12},{24,0},{28,4},{1,25},{... | collective-permute-start | bytes 442376 | tf_op jit(solution)/shard_map/ppermute | solution.py:10
  50.4 1.3 %collective-permute-start.10 = (bf16[4,8,2304]{2,1,0:T(8,128)(2,1)S(1)}, bf16[4,8,2304]{2,1,0:T(8,128)(2,1)}, u32[]{:S(2)}, u32[]{:S(2)}) collective-permute-start(bf16[4,8,2304]{2,1,0:T(8,128)(2,1)S(1)} %get-tuple-element.20), channel_id=1, source_target_pairs={{0,8},{4,12},{8,0},{12,4},{16,24},{20,28},{24,16},{28,20},{1,9},{5... | collective-permute-start | bytes 442376 | tf_op jit(solution)/shard_map/ppermute | solution.py:10
  51.7 1.9 %fusion.89 = (bf16[128,2304]{1,0:T(8,128)(2,1)S(1)}, f32[128,2304]{1,0:T(8,128)}) fusion(bf16[128,2304]{1,0:T(8,128)(2,1)S(1)} %collective-permute-done.23, f32[128]{0:T(128)S(1)} %get-tuple-element.47, bf16[1,1024,2304]{2,1,0:T(8,128)(2,1)S(1)} %bitcast.215, bf16[256,1024]{1,0:T(8,128)(2,1)S(1)} %multiply_convert_fusion), kind=kOutput, calls=%fused_computation.163 | convolution fusion | flops 605159424 | bytes 7340544 | tf_op jit(solution)/shard_map/dot_general | solution.py:14
  54.4 1.4 %collective-permute-start.26 = (bf16[4,8,2304]{2,1,0:T(8,128)(2,1)}, bf16[4,8,2304]{2,1,0:T(8,128)(2,1)}, u32[]{:S(2)}, u32[]{:S(2)}) collective-permute-start(bf16[4,8,2304]{2,1,0:T(8,128)(2,1)} %get-tuple-element.24), channel_id=1, source_target_pairs={{0,24},{4,28},{8,16},{12,20},{16,8},{20,12},{24,0},{28,4},{1,25},{... | collective-permute-start | bytes 442376 | tf_op jit(solution)/shard_map/ppermute | solution.py:10
  57.6 1.3 %collective-permute-start.24 = (bf16[4,8,2304]{2,1,0:T(8,128)(2,1)}, bf16[4,8,2304]{2,1,0:T(8,128)(2,1)}, u32[]{:S(2)}, u32[]{:S(2)}) collective-permute-start(bf16[4,8,2304]{2,1,0:T(8,128)(2,1)} %get-tuple-element.23), channel_id=1, source_target_pairs={{0,8},{4,12},{8,0},{12,4},{16,24},{20,28},{24,16},{28,20},{1,9},{5... | collective-permute-start | bytes 442376 | tf_op jit(solution)/shard_map/ppermute | solution.py:10
  58.9 2.5 %fusion.74 = f32[64,2304]{1,0:T(8,128)S(1)} fusion(bf16[256,2304]{1,0:T(8,128)(2,1)} %param.21, f32[64,256]{1,0:T(8,128)S(1)} %fusion.92, bf16[64,2304]{1,0:T(8,128)(2,1)S(1)} %bitcast.217, bf16[2304,256]{1,0:T(8,128)(2,1)} %param.20), kind=kOutput, calls=%fused_computation.143 | convolution fusion | flops 151093248 | bytes 3309568 | tf_op jit(solution)/shard_map/dot_general | solution.py:14
  62.4 2.1 %collective-permute-done.25 = bf16[4,8,2304]{2,1,0:T(8,128)(2,1)} collective-permute-done((bf16[4,8,2304]{2,1,0:T(8,128)(2,1)}, bf16[4,8,2304]{2,1,0:T(8,128)(2,1)}, u32[]{:S(2)}, u32[]{:S(2)}) %collective-permute-start.25) | collective-permute-done | bytes 147488 | tf_op jit(solution)/shard_map/ppermute | solution.py:10
  64.5 1.5 %fusion.57 = (f32[4,8,2304]{2,1,0:T(8,128)S(1)}, f32[4,8,2304]{2,1,0:T(8,128)S(1)}) fusion(f32[64,2304]{1,0:T(8,128)S(1)} %fusion.74, f32[128,2304]{1,0:T(8,128)} %get-tuple-element.51, bf16[4,8,2304]{2,1,0:T(8,128)(2,1)} %copy-done.5, bf16[4,8,2304]{2,1,0:T(8,128)(2,1)} %collective-permute-done.11, bf16[4,8,2304]{2,1,0:T(8,128)(2,1)} %collective-permute-done.10, ...), kind=kLoop, calls=%fused_computation.56 | loop fusion | flops 1032192 | bytes 2654208 | tf_op jit(solution)/shard_map/add | solution.py:120
  66.1 3.7 %collective-permute-start.29 = (bf16[8,2304]{1,0:T(8,128)(2,1)S(1)}, bf16[8,2304]{1,0:T(8,128)(2,1)S(1)}, u32[]{:S(2)}, u32[]{:S(2)}) collective-permute-start(bf16[8,2304]{1,0:T(8,128)(2,1)S(1)} %get-tuple-element.30), channel_id=1, source_target_pairs={{0,3},{1,2},{2,1},{3,0},{4,7},{5,6},{6,5},{7,4},{8,11},{9,10},{10,... | collective-permute-start | bytes 110600 | tf_op jit(solution)/shard_map/ppermute | solution.py:10
  70.6 3.7 %collective-permute-start.15 = (bf16[8,2304]{1,0:T(8,128)(2,1)S(1)}, bf16[8,2304]{1,0:T(8,128)(2,1)S(1)}, u32[]{:S(2)}, u32[]{:S(2)}) collective-permute-start(bf16[8,2304]{1,0:T(8,128)(2,1)S(1)} %get-tuple-element.27), channel_id=1, source_target_pairs={{0,3},{1,2},{2,1},{3,0},{4,7},{5,6},{6,5},{7,4},{8,11},{9,10},{10,... | collective-permute-start | bytes 110600 | tf_op jit(solution)/shard_map/ppermute | solution.py:10
  75.1 3.7 %collective-permute-start.32 = (bf16[8,2304]{1,0:T(8,128)(2,1)S(1)}, bf16[8,2304]{1,0:T(8,128)(2,1)S(1)}, u32[]{:S(2)}, u32[]{:S(2)}) collective-permute-start(bf16[8,2304]{1,0:T(8,128)(2,1)S(1)} %fusion.66), channel_id=1, source_target_pairs={{0,3},{1,2},{2,1},{3,0},{4,7},{5,6},{6,5},{7,4},{8,11},{9,10},{10,... | collective-permute-start | bytes 110600 | tf_op jit(solution)/shard_map/ppermute | solution.py:10
  79.6 3.7 %collective-permute-start.18 = (bf16[8,2304]{1,0:T(8,128)(2,1)S(1)}, bf16[8,2304]{1,0:T(8,128)(2,1)S(1)}, u32[]{:S(2)}, u32[]{:S(2)}) collective-permute-start(bf16[8,2304]{1,0:T(8,128)(2,1)S(1)} %fusion.67), channel_id=1, source_target_pairs={{0,3},{1,2},{2,1},{3,0},{4,7},{5,6},{6,5},{7,4},{8,11},{9,10},{10,... | collective-permute-start | bytes 110600 | tf_op jit(solution)/shard_map/ppermute | solution.py:10
  84.1 1.5 %collective-permute-start.35 = (bf16[4,8,2304]{2,1,0:T(8,128)(2,1)S(1)}, bf16[4,8,2304]{2,1,0:T(8,128)(2,1)S(1)}, u32[]{:S(2)}, u32[]{:S(2)}) collective-permute-start(bf16[4,8,2304]{2,1,0:T(8,128)(2,1)S(1)} %get-tuple-element.41), channel_id=1, source_target_pairs={{0,24},{4,28},{8,16},{12,20},{16,8},{20,12},{24,0},{28,4},{1,25},{... | collective-permute-start | bytes 442376 | tf_op jit(solution)/shard_map/ppermute | solution.py:10
  86.4 1.2 collective-permute-start.33
  88.2 1.5 %collective-permute-start.21 = (bf16[4,8,2304]{2,1,0:T(8,128)(2,1)S(1)}, bf16[4,8,2304]{2,1,0:T(8,128)(2,1)S(1)}, u32[]{:S(2)}, u32[]{:S(2)}) collective-permute-start(bf16[4,8,2304]{2,1,0:T(8,128)(2,1)S(1)} %get-tuple-element.39), channel_id=1, source_target_pairs={{0,24},{4,28},{8,16},{12,20},{16,8},{20,12},{24,0},{28,4},{1,25},{... | collective-permute-start | bytes 442376 | tf_op jit(solution)/shard_map/ppermute | solution.py:10
  90.5 1.3 %collective-permute-done.35 = bf16[4,8,2304]{2,1,0:T(8,128)(2,1)S(1)} collective-permute-done((bf16[4,8,2304]{2,1,0:T(8,128)(2,1)S(1)}, bf16[4,8,2304]{2,1,0:T(8,128)(2,1)S(1)}, u32[]{:S(2)}, u32[]{:S(2)}) %collective-permute-start.35) | collective-permute-done | bytes 147488 | tf_op jit(solution)/shard_map/ppermute | solution.py:10
  92.6 1.8 %collective-permute-done.34 = bf16[4,8,2304]{2,1,0:T(8,128)(2,1)S(1)} collective-permute-done((bf16[4,8,2304]{2,1,0:T(8,128)(2,1)S(1)}, bf16[4,8,2304]{2,1,0:T(8,128)(2,1)S(1)}, u32[]{:S(2)}, u32[]{:S(2)}) %collective-permute-start.34) | collective-permute-done | bytes 147488 | tf_op jit(solution)/shard_map/ppermute | solution.py:10
  94.6 1.6 %collective-permute-done.21 = bf16[4,8,2304]{2,1,0:T(8,128)(2,1)S(1)} collective-permute-done((bf16[4,8,2304]{2,1,0:T(8,128)(2,1)S(1)}, bf16[4,8,2304]{2,1,0:T(8,128)(2,1)S(1)}, u32[]{:S(2)}, u32[]{:S(2)}) %collective-permute-start.21) | collective-permute-done | bytes 147488 | tf_op jit(solution)/shard_map/ppermute | solution.py:10
  96.1 1.4 %collective-permute-done.20 = bf16[4,8,2304]{2,1,0:T(8,128)(2,1)S(1)} collective-permute-done((bf16[4,8,2304]{2,1,0:T(8,128)(2,1)S(1)}, bf16[4,8,2304]{2,1,0:T(8,128)(2,1)S(1)}, u32[]{:S(2)}, u32[]{:S(2)}) %collective-permute-start.20) | collective-permute-done | bytes 147488 | tf_op jit(solution)/shard_map/ppermute | solution.py:10
  101.4 1.5 %collective-permute-start.40 = (bf16[4,8,2304]{2,1,0:T(8,128)(2,1)S(1)}, bf16[4,8,2304]{2,1,0:T(8,128)(2,1)S(1)}, u32[]{:S(2)}, u32[]{:S(2)}) collective-permute-start(bf16[4,8,2304]{2,1,0:T(8,128)(2,1)S(1)} %get-tuple-element.13), channel_id=1, source_target_pairs={{0,24},{4,28},{8,16},{12,20},{16,8},{20,12},{24,0},{28,4},{1,25},{... | collective-permute-start | bytes 442376 | tf_op jit(solution)/shard_map/ppermute | solution.py:10
  103.7 1.3 %collective-permute-start.38 = (bf16[4,8,2304]{2,1,0:T(8,128)(2,1)S(1)}, bf16[4,8,2304]{2,1,0:T(8,128)(2,1)S(1)}, u32[]{:S(2)}, u32[]{:S(2)}) collective-permute-start(bf16[4,8,2304]{2,1,0:T(8,128)(2,1)S(1)} %get-tuple-element.12), channel_id=1, source_target_pairs={{0,8},{4,12},{8,0},{12,4},{16,24},{20,28},{24,16},{28,20},{1,9},{5... | collective-permute-start | bytes 442376 | tf_op jit(solution)/shard_map/ppermute | solution.py:10
  106.0 1.5 %collective-permute-start.47 = (bf16[4,8,2304]{2,1,0:T(8,128)(2,1)S(1)}, bf16[4,8,2304]{2,1,0:T(8,128)(2,1)S(1)}, u32[]{:S(2)}, u32[]{:S(2)}) collective-permute-start(bf16[4,8,2304]{2,1,0:T(8,128)(2,1)S(1)} %get-tuple-element.16), channel_id=1, source_target_pairs={{0,24},{4,28},{8,16},{12,20},{16,8},{20,12},{24,0},{28,4},{1,25},{... | collective-permute-start | bytes 442376 | tf_op jit(solution)/shard_map/ppermute | solution.py:10
  109.1 1.2 collective-permute-start.45
  110.3 2.0 %collective-permute-done.39 = bf16[4,8,2304]{2,1,0:T(8,128)(2,1)S(1)} collective-permute-done((bf16[4,8,2304]{2,1,0:T(8,128)(2,1)S(1)}, bf16[4,8,2304]{2,1,0:T(8,128)(2,1)S(1)}, u32[]{:S(2)}, u32[]{:S(2)}) %collective-permute-start.39) | collective-permute-done | bytes 147488 | tf_op jit(solution)/shard_map/ppermute | solution.py:10
  112.4 3.1 %collective-permute-start.43 = (bf16[8,2304]{1,0:T(8,128)(2,1)S(1)}, bf16[8,2304]{1,0:T(8,128)(2,1)S(1)}, u32[]{:S(2)}, u32[]{:S(2)}) collective-permute-start(bf16[8,2304]{1,0:T(8,128)(2,1)S(1)} %get-tuple-element.33), channel_id=1, source_target_pairs={{0,3},{1,2},{2,1},{3,0},{4,7},{5,6},{6,5},{7,4},{8,11},{9,10},{10,... | collective-permute-start | bytes 110600 | tf_op jit(solution)/shard_map/ppermute | solution.py:10
  115.5 1.4 %collective-permute-start.41 = (bf16[8,2304]{1,0:T(8,128)(2,1)S(1)}, bf16[8,2304]{1,0:T(8,128)(2,1)S(1)}, u32[]{:S(2)}, u32[]{:S(2)}) collective-permute-start(bf16[8,2304]{1,0:T(8,128)(2,1)S(1)} %get-tuple-element.32), channel_id=1, source_target_pairs={{0,1},{1,0},{2,3},{3,2},{4,5},{5,4},{6,7},{7,6},{8,9},{9,8},{10,11... | collective-permute-start | bytes 110600 | tf_op jit(solution)/shard_map/ppermute | solution.py:10
  116.8 1.2 collective-permute-done.46
  118.2 3.1 %collective-permute-start.50 = (bf16[8,2304]{1,0:T(8,128)(2,1)S(1)}, bf16[8,2304]{1,0:T(8,128)(2,1)S(1)}, u32[]{:S(2)}, u32[]{:S(2)}) collective-permute-start(bf16[8,2304]{1,0:T(8,128)(2,1)S(1)} %get-tuple-element.36), channel_id=1, source_target_pairs={{0,3},{1,2},{2,1},{3,0},{4,7},{5,6},{6,5},{7,4},{8,11},{9,10},{10,... | collective-permute-start | bytes 110600 | tf_op jit(solution)/shard_map/ppermute | solution.py:10
  121.3 1.4 %collective-permute-start.48 = (bf16[8,2304]{1,0:T(8,128)(2,1)S(1)}, bf16[8,2304]{1,0:T(8,128)(2,1)S(1)}, u32[]{:S(2)}, u32[]{:S(2)}) collective-permute-start(bf16[8,2304]{1,0:T(8,128)(2,1)S(1)} %get-tuple-element.35), channel_id=1, source_target_pairs={{0,1},{1,0},{2,3},{3,2},{4,5},{5,4},{6,7},{7,6},{8,9},{9,8},{10,11... | collective-permute-start | bytes 110600 | tf_op jit(solution)/shard_map/ppermute | solution.py:10
  122.6 1.4 %collective-permute-done.50 = bf16[8,2304]{1,0:T(8,128)(2,1)S(1)} collective-permute-done((bf16[8,2304]{1,0:T(8,128)(2,1)S(1)}, bf16[8,2304]{1,0:T(8,128)(2,1)S(1)}, u32[]{:S(2)}, u32[]{:S(2)}) %collective-permute-start.50) | collective-permute-done | bytes 36896 | tf_op jit(solution)/shard_map/ppermute | solution.py:10
  124.0 2.1 %collective-permute-done.49 = bf16[8,2304]{1,0:T(8,128)(2,1)S(1)} collective-permute-done((bf16[8,2304]{1,0:T(8,128)(2,1)S(1)}, bf16[8,2304]{1,0:T(8,128)(2,1)S(1)}, u32[]{:S(2)}, u32[]{:S(2)}) %collective-permute-start.49) | collective-permute-done | bytes 36896 | tf_op jit(solution)/shard_map/ppermute | solution.py:10
  (174 shorter events, 29.0 us)
Async XLA Ops:
  2.4 4.7 %collective-permute-start.4 = (bf16[4,16,128]{2,1,0:T(8,128)(2,1)S(1)}, bf16[4,16,128]{2,1,0:T(8,128)(2,1)S(1)}, u32[]{:S(2)}, u32[]{:S(2)}) collective-permute-start(bf16[4,16,128]{2,1,0:T(8,128)(2,1)S(1)} %broadcast_select_fusion), channel_id=1, source_target_pairs={{0,1},{1,0},{2,3},{3,2},{4,5},{5,4},{6,7},{7,6},{8,9},{9,8},{10,11... | collective-permute-start | bytes 49160 | tf_op jit(solution)/shard_map/ppermute | solution.py:10
  7.2 4.8 %collective-permute-start.5 = (bf16[4,16,128]{2,1,0:T(8,128)(2,1)S(1)}, bf16[4,16,128]{2,1,0:T(8,128)(2,1)S(1)}, u32[]{:S(2)}, u32[]{:S(2)}) collective-permute-start(bf16[4,16,128]{2,1,0:T(8,128)(2,1)S(1)} %fusion.76), channel_id=1, source_target_pairs={{0,2},{1,3},{2,0},{3,1},{4,6},{5,7},{6,4},{7,5},{8,10},{9,11},{10,... | collective-permute-start | bytes 49160 | tf_op jit(solution)/shard_map/ppermute | solution.py:10
  12.7 3.7 %collective-permute-start.6 = (bf16[1,4,16,128]{3,2,1,0:T(8,128)(2,1)S(1)}, bf16[1,4,16,128]{3,2,1,0:T(8,128)(2,1)S(1)}, u32[]{:S(2)}, u32[]{:S(2)}) collective-permute-start(bf16[1,4,16,128]{3,2,1,0:T(8,128)(2,1)S(1)} %get-tuple-element.43), channel_id=1, source_target_pairs={{0,8},{4,12},{8,0},{12,4},{16,24},{20,28},{24,16},{28,20},{1,9},{5... | collective-permute-start | bytes 49160 | tf_op jit(solution)/shard_map/ppermute | solution.py:10
  17.1 5.7 %collective-permute-start.7 = (bf16[2,4,16,128]{3,2,1,0:T(8,128)(2,1)}, bf16[2,4,16,128]{3,2,1,0:T(8,128)(2,1)}, u32[]{:S(2)}, u32[]{:S(2)}) collective-permute-start(bf16[2,4,16,128]{3,2,1,0:T(8,128)(2,1)} %pad_maximum_fusion.6), channel_id=1, source_target_pairs={{0,16},{4,20},{8,24},{12,28},{16,0},{20,4},{24,8},{28,12},{1,17},{... | collective-permute-start | bytes 98312 | tf_op jit(solution)/shard_map/ppermute | solution.py:10
  18.9 9.4 %collective-permute-start.2 = (bf16[64,2304]{1,0:T(8,128)(2,1)}, bf16[64,2304]{1,0:T(8,128)(2,1)S(1)}, u32[]{:S(2)}, u32[]{:S(2)}) collective-permute-start(bf16[64,2304]{1,0:T(8,128)(2,1)} %param.13), channel_id=1, source_target_pairs={{0,24},{4,28},{8,16},{12,20},{16,8},{20,12},{24,0},{28,4},{1,25},{... | collective-permute-start | bytes 884744 | tf_op jit(solution)/shard_map/ppermute | solution.py:10
  20.3 11.4 %collective-permute-start.1 = (bf16[64,2304]{1,0:T(8,128)(2,1)}, bf16[64,2304]{1,0:T(8,128)(2,1)S(1)}, u32[]{:S(2)}, u32[]{:S(2)}) collective-permute-start(bf16[64,2304]{1,0:T(8,128)(2,1)} %param.13), channel_id=1, source_target_pairs={{0,16},{4,20},{8,24},{12,28},{16,0},{20,4},{24,8},{28,12},{1,17},{... | collective-permute-start | bytes 884744 | tf_op jit(solution)/shard_map/ppermute | solution.py:10
  21.9 9.8 %collective-permute-start = (bf16[64,2304]{1,0:T(8,128)(2,1)}, bf16[64,2304]{1,0:T(8,128)(2,1)S(1)}, u32[]{:S(2)}, u32[]{:S(2)}) collective-permute-start(bf16[64,2304]{1,0:T(8,128)(2,1)} %param.13), channel_id=1, source_target_pairs={{0,8},{4,12},{8,0},{12,4},{16,24},{20,28},{24,16},{28,20},{1,9},{5... | collective-permute-start | bytes 884744 | tf_op jit(solution)/shard_map/ppermute | solution.py:10
  32.0 9.8 %collective-permute-start.3 = (bf16[256,2304]{1,0:T(8,128)(2,1)S(1)}, bf16[256,2304]{1,0:T(8,128)(2,1)S(1)}, u32[]{:S(2)}, u32[]{:S(2)}) collective-permute-start(bf16[256,2304]{1,0:T(8,128)(2,1)S(1)} %bitcast.254), channel_id=1, source_target_pairs={{0,4},{4,0},{8,12},{12,8},{16,20},{20,16},{24,28},{28,24},{1,5},{5... | collective-permute-start | bytes 3538952 | tf_op jit(solution)/shard_map/ppermute | solution.py:10
  40.3 5.3 %collective-permute-start.9 = (bf16[128,2304]{1,0:T(8,128)(2,1)S(1)}, bf16[128,2304]{1,0:T(8,128)(2,1)S(1)}, u32[]{:S(2)}, u32[]{:S(2)}) collective-permute-start(bf16[128,2304]{1,0:T(8,128)(2,1)S(1)} %fusion.31), channel_id=1, source_target_pairs={{0,4},{4,0},{8,12},{12,8},{16,20},{20,16},{24,28},{28,24},{1,5},{5... | collective-permute-start | bytes 1769480 | tf_op jit(solution)/shard_map/ppermute | solution.py:10
  41.2 10.5 %collective-permute-start.23 = (bf16[128,2304]{1,0:T(8,128)(2,1)S(1)}, bf16[128,2304]{1,0:T(8,128)(2,1)S(1)}, u32[]{:S(2)}, u32[]{:S(2)}) collective-permute-start(bf16[128,2304]{1,0:T(8,128)(2,1)S(1)} %fusion.28), channel_id=1, source_target_pairs={{0,4},{4,0},{8,12},{12,8},{16,20},{20,16},{24,28},{28,24},{1,5},{5... | collective-permute-start | bytes 1769480 | tf_op jit(solution)/shard_map/ppermute | solution.py:10
  48.2 8.7 %collective-permute-start.12 = (bf16[4,8,2304]{2,1,0:T(8,128)(2,1)S(1)}, bf16[4,8,2304]{2,1,0:T(8,128)(2,1)S(1)}, u32[]{:S(2)}, u32[]{:S(2)}) collective-permute-start(bf16[4,8,2304]{2,1,0:T(8,128)(2,1)S(1)} %get-tuple-element.21), channel_id=1, source_target_pairs={{0,24},{4,28},{8,16},{12,20},{16,8},{20,12},{24,0},{28,4},{1,25},{... | collective-permute-start | bytes 442376 | tf_op jit(solution)/shard_map/ppermute | solution.py:10
  49.7 11.7 %collective-permute-start.11 = (bf16[4,8,2304]{2,1,0:T(8,128)(2,1)}, bf16[4,8,2304]{2,1,0:T(8,128)(2,1)}, u32[]{:S(2)}, u32[]{:S(2)}) collective-permute-start(bf16[4,8,2304]{2,1,0:T(8,128)(2,1)} %get-tuple-element.22), channel_id=1, source_target_pairs={{0,16},{4,20},{8,24},{12,28},{16,0},{20,4},{24,8},{28,12},{1,17},{... | collective-permute-start | bytes 442376 | tf_op jit(solution)/shard_map/ppermute | solution.py:10
  50.4 11.0 %collective-permute-start.10 = (bf16[4,8,2304]{2,1,0:T(8,128)(2,1)S(1)}, bf16[4,8,2304]{2,1,0:T(8,128)(2,1)}, u32[]{:S(2)}, u32[]{:S(2)}) collective-permute-start(bf16[4,8,2304]{2,1,0:T(8,128)(2,1)S(1)} %get-tuple-element.20), channel_id=1, source_target_pairs={{0,8},{4,12},{8,0},{12,4},{16,24},{20,28},{24,16},{28,20},{1,9},{5... | collective-permute-start | bytes 442376 | tf_op jit(solution)/shard_map/ppermute | solution.py:10
  54.4 8.0 %collective-permute-start.26 = (bf16[4,8,2304]{2,1,0:T(8,128)(2,1)}, bf16[4,8,2304]{2,1,0:T(8,128)(2,1)}, u32[]{:S(2)}, u32[]{:S(2)}) collective-permute-start(bf16[4,8,2304]{2,1,0:T(8,128)(2,1)} %get-tuple-element.24), channel_id=1, source_target_pairs={{0,24},{4,28},{8,16},{12,20},{16,8},{20,12},{24,0},{28,4},{1,25},{... | collective-permute-start | bytes 442376 | tf_op jit(solution)/shard_map/ppermute | solution.py:10
  55.8 8.7 %collective-permute-start.25 = (bf16[4,8,2304]{2,1,0:T(8,128)(2,1)}, bf16[4,8,2304]{2,1,0:T(8,128)(2,1)}, u32[]{:S(2)}, u32[]{:S(2)}) collective-permute-start(bf16[4,8,2304]{2,1,0:T(8,128)(2,1)} %get-tuple-element.25), channel_id=1, source_target_pairs={{0,16},{4,20},{8,24},{12,28},{16,0},{20,4},{24,8},{28,12},{1,17},{... | collective-permute-start | bytes 442376 | tf_op jit(solution)/shard_map/ppermute | solution.py:10
  57.6 6.9 %collective-permute-start.24 = (bf16[4,8,2304]{2,1,0:T(8,128)(2,1)}, bf16[4,8,2304]{2,1,0:T(8,128)(2,1)}, u32[]{:S(2)}, u32[]{:S(2)}) collective-permute-start(bf16[4,8,2304]{2,1,0:T(8,128)(2,1)} %get-tuple-element.23), channel_id=1, source_target_pairs={{0,8},{4,12},{8,0},{12,4},{16,24},{20,28},{24,16},{28,20},{1,9},{5... | collective-permute-start | bytes 442376 | tf_op jit(solution)/shard_map/ppermute | solution.py:10
  66.1 8.2 %collective-permute-start.29 = (bf16[8,2304]{1,0:T(8,128)(2,1)S(1)}, bf16[8,2304]{1,0:T(8,128)(2,1)S(1)}, u32[]{:S(2)}, u32[]{:S(2)}) collective-permute-start(bf16[8,2304]{1,0:T(8,128)(2,1)S(1)} %get-tuple-element.30), channel_id=1, source_target_pairs={{0,3},{1,2},{2,1},{3,0},{4,7},{5,6},{6,5},{7,4},{8,11},{9,10},{10,... | collective-permute-start | bytes 110600 | tf_op jit(solution)/shard_map/ppermute | solution.py:10
  69.8 5.3 %collective-permute-start.28 = (bf16[8,2304]{1,0:T(8,128)(2,1)S(1)}, bf16[8,2304]{1,0:T(8,128)(2,1)S(1)}, u32[]{:S(2)}, u32[]{:S(2)}) collective-permute-start(bf16[8,2304]{1,0:T(8,128)(2,1)S(1)} %get-tuple-element.31), channel_id=1, source_target_pairs={{0,2},{1,3},{2,0},{3,1},{4,6},{5,7},{6,4},{7,5},{8,10},{9,11},{10,... | collective-permute-start | bytes 110600 | tf_op jit(solution)/shard_map/ppermute | solution.py:10
  69.8 5.3 %collective-permute-start.27 = (bf16[8,2304]{1,0:T(8,128)(2,1)S(1)}, bf16[8,2304]{1,0:T(8,128)(2,1)S(1)}, u32[]{:S(2)}, u32[]{:S(2)}) collective-permute-start(bf16[8,2304]{1,0:T(8,128)(2,1)S(1)} %get-tuple-element.29), channel_id=1, source_target_pairs={{0,1},{1,0},{2,3},{3,2},{4,5},{5,4},{6,7},{7,6},{8,9},{9,8},{10,11... | collective-permute-start | bytes 110600 | tf_op jit(solution)/shard_map/ppermute | solution.py:10
  70.6 8.2 %collective-permute-start.15 = (bf16[8,2304]{1,0:T(8,128)(2,1)S(1)}, bf16[8,2304]{1,0:T(8,128)(2,1)S(1)}, u32[]{:S(2)}, u32[]{:S(2)}) collective-permute-start(bf16[8,2304]{1,0:T(8,128)(2,1)S(1)} %get-tuple-element.27), channel_id=1, source_target_pairs={{0,3},{1,2},{2,1},{3,0},{4,7},{5,6},{6,5},{7,4},{8,11},{9,10},{10,... | collective-permute-start | bytes 110600 | tf_op jit(solution)/shard_map/ppermute | solution.py:10
  74.3 5.3 %collective-permute-start.14 = (bf16[8,2304]{1,0:T(8,128)(2,1)S(1)}, bf16[8,2304]{1,0:T(8,128)(2,1)S(1)}, u32[]{:S(2)}, u32[]{:S(2)}) collective-permute-start(bf16[8,2304]{1,0:T(8,128)(2,1)S(1)} %get-tuple-element.28), channel_id=1, source_target_pairs={{0,2},{1,3},{2,0},{3,1},{4,6},{5,7},{6,4},{7,5},{8,10},{9,11},{10,... | collective-permute-start | bytes 110600 | tf_op jit(solution)/shard_map/ppermute | solution.py:10
  74.3 5.3 %collective-permute-start.13 = (bf16[8,2304]{1,0:T(8,128)(2,1)S(1)}, bf16[8,2304]{1,0:T(8,128)(2,1)S(1)}, u32[]{:S(2)}, u32[]{:S(2)}) collective-permute-start(bf16[8,2304]{1,0:T(8,128)(2,1)S(1)} %get-tuple-element.26), channel_id=1, source_target_pairs={{0,1},{1,0},{2,3},{3,2},{4,5},{5,4},{6,7},{7,6},{8,9},{9,8},{10,11... | collective-permute-start | bytes 110600 | tf_op jit(solution)/shard_map/ppermute | solution.py:10
  75.1 8.2 %collective-permute-start.32 = (bf16[8,2304]{1,0:T(8,128)(2,1)S(1)}, bf16[8,2304]{1,0:T(8,128)(2,1)S(1)}, u32[]{:S(2)}, u32[]{:S(2)}) collective-permute-start(bf16[8,2304]{1,0:T(8,128)(2,1)S(1)} %fusion.66), channel_id=1, source_target_pairs={{0,3},{1,2},{2,1},{3,0},{4,7},{5,6},{6,5},{7,4},{8,11},{9,10},{10,... | collective-permute-start | bytes 110600 | tf_op jit(solution)/shard_map/ppermute | solution.py:10
  78.8 5.3 %collective-permute-start.31 = (bf16[8,2304]{1,0:T(8,128)(2,1)S(1)}, bf16[8,2304]{1,0:T(8,128)(2,1)S(1)}, u32[]{:S(2)}, u32[]{:S(2)}) collective-permute-start(bf16[8,2304]{1,0:T(8,128)(2,1)S(1)} %fusion.66), channel_id=1, source_target_pairs={{0,2},{1,3},{2,0},{3,1},{4,6},{5,7},{6,4},{7,5},{8,10},{9,11},{10,... | collective-permute-start | bytes 110600 | tf_op jit(solution)/shard_map/ppermute | solution.py:10
  78.8 5.3 %collective-permute-start.30 = (bf16[8,2304]{1,0:T(8,128)(2,1)S(1)}, bf16[8,2304]{1,0:T(8,128)(2,1)S(1)}, u32[]{:S(2)}, u32[]{:S(2)}) collective-permute-start(bf16[8,2304]{1,0:T(8,128)(2,1)S(1)} %fusion.66), channel_id=1, source_target_pairs={{0,1},{1,0},{2,3},{3,2},{4,5},{5,4},{6,7},{7,6},{8,9},{9,8},{10,11... | collective-permute-start | bytes 110600 | tf_op jit(solution)/shard_map/ppermute | solution.py:10
  79.6 6.8 %collective-permute-start.18 = (bf16[8,2304]{1,0:T(8,128)(2,1)S(1)}, bf16[8,2304]{1,0:T(8,128)(2,1)S(1)}, u32[]{:S(2)}, u32[]{:S(2)}) collective-permute-start(bf16[8,2304]{1,0:T(8,128)(2,1)S(1)} %fusion.67), channel_id=1, source_target_pairs={{0,3},{1,2},{2,1},{3,0},{4,7},{5,6},{6,5},{7,4},{8,11},{9,10},{10,... | collective-permute-start | bytes 110600 | tf_op jit(solution)/shard_map/ppermute | solution.py:10
  83.3 4.9 %collective-permute-start.17 = (bf16[8,2304]{1,0:T(8,128)(2,1)S(1)}, bf16[8,2304]{1,0:T(8,128)(2,1)S(1)}, u32[]{:S(2)}, u32[]{:S(2)}) collective-permute-start(bf16[8,2304]{1,0:T(8,128)(2,1)S(1)} %fusion.67), channel_id=1, source_target_pairs={{0,2},{1,3},{2,0},{3,1},{4,6},{5,7},{6,4},{7,5},{8,10},{9,11},{10,... | collective-permute-start | bytes 110600 | tf_op jit(solution)/shard_map/ppermute | solution.py:10
  83.3 4.9 %collective-permute-start.16 = (bf16[8,2304]{1,0:T(8,128)(2,1)S(1)}, bf16[8,2304]{1,0:T(8,128)(2,1)S(1)}, u32[]{:S(2)}, u32[]{:S(2)}) collective-permute-start(bf16[8,2304]{1,0:T(8,128)(2,1)S(1)} %fusion.67), channel_id=1, source_target_pairs={{0,1},{1,0},{2,3},{3,2},{4,5},{5,4},{6,7},{7,6},{8,9},{9,8},{10,11... | collective-permute-start | bytes 110600 | tf_op jit(solution)/shard_map/ppermute | solution.py:10
  84.1 7.7 %collective-permute-start.35 = (bf16[4,8,2304]{2,1,0:T(8,128)(2,1)S(1)}, bf16[4,8,2304]{2,1,0:T(8,128)(2,1)S(1)}, u32[]{:S(2)}, u32[]{:S(2)}) collective-permute-start(bf16[4,8,2304]{2,1,0:T(8,128)(2,1)S(1)} %get-tuple-element.41), channel_id=1, source_target_pairs={{0,24},{4,28},{8,16},{12,20},{16,8},{20,12},{24,0},{28,4},{1,25},{... | collective-permute-start | bytes 442376 | tf_op jit(solution)/shard_map/ppermute | solution.py:10
  85.6 8.8 %collective-permute-start.34 = (bf16[4,8,2304]{2,1,0:T(8,128)(2,1)S(1)}, bf16[4,8,2304]{2,1,0:T(8,128)(2,1)S(1)}, u32[]{:S(2)}, u32[]{:S(2)}) collective-permute-start(bf16[4,8,2304]{2,1,0:T(8,128)(2,1)S(1)} %get-tuple-element.41), channel_id=1, source_target_pairs={{0,16},{4,20},{8,24},{12,28},{16,0},{20,4},{24,8},{28,12},{1,17},{... | collective-permute-start | bytes 442376 | tf_op jit(solution)/shard_map/ppermute | solution.py:10
  86.4 8.0 %collective-permute-start.33 = (bf16[4,8,2304]{2,1,0:T(8,128)(2,1)S(1)}, bf16[4,8,2304]{2,1,0:T(8,128)(2,1)S(1)}, u32[]{:S(2)}, u32[]{:S(2)}) collective-permute-start(bf16[4,8,2304]{2,1,0:T(8,128)(2,1)S(1)} %get-tuple-element.41), channel_id=1, source_target_pairs={{0,8},{4,12},{8,0},{12,4},{16,24},{20,28},{24,16},{28,20},{1,9},{5... | collective-permute-start | bytes 442376 | tf_op jit(solution)/shard_map/ppermute | solution.py:10
  88.2 8.0 %collective-permute-start.21 = (bf16[4,8,2304]{2,1,0:T(8,128)(2,1)S(1)}, bf16[4,8,2304]{2,1,0:T(8,128)(2,1)S(1)}, u32[]{:S(2)}, u32[]{:S(2)}) collective-permute-start(bf16[4,8,2304]{2,1,0:T(8,128)(2,1)S(1)} %get-tuple-element.39), channel_id=1, source_target_pairs={{0,24},{4,28},{8,16},{12,20},{16,8},{20,12},{24,0},{28,4},{1,25},{... | collective-permute-start | bytes 442376 | tf_op jit(solution)/shard_map/ppermute | solution.py:10
  89.7 7.9 %collective-permute-start.20 = (bf16[4,8,2304]{2,1,0:T(8,128)(2,1)S(1)}, bf16[4,8,2304]{2,1,0:T(8,128)(2,1)S(1)}, u32[]{:S(2)}, u32[]{:S(2)}) collective-permute-start(bf16[4,8,2304]{2,1,0:T(8,128)(2,1)S(1)} %get-tuple-element.39), channel_id=1, source_target_pairs={{0,16},{4,20},{8,24},{12,28},{16,0},{20,4},{24,8},{28,12},{1,17},{... | collective-permute-start | bytes 442376 | tf_op jit(solution)/shard_map/ppermute | solution.py:10
  91.7 5.8 %collective-permute-start.19 = (bf16[4,8,2304]{2,1,0:T(8,128)(2,1)S(1)}, bf16[4,8,2304]{2,1,0:T(8,128)(2,1)S(1)}, u32[]{:S(2)}, u32[]{:S(2)}) collective-permute-start(bf16[4,8,2304]{2,1,0:T(8,128)(2,1)S(1)} %get-tuple-element.39), channel_id=1, source_target_pairs={{0,8},{4,12},{8,0},{12,4},{16,24},{20,28},{24,16},{28,20},{1,9},{5... | collective-permute-start | bytes 442376 | tf_op jit(solution)/shard_map/ppermute | solution.py:10
  94.5 10.5 %collective-permute-start.36 = (bf16[128,2304]{1,0:T(8,128)(2,1)S(1)}, bf16[128,2304]{1,0:T(8,128)(2,1)S(1)}, u32[]{:S(2)}, u32[]{:S(2)}) collective-permute-start(bf16[128,2304]{1,0:T(8,128)(2,1)S(1)} %bitcast.218), channel_id=1, source_target_pairs={{0,4},{4,0},{8,12},{12,8},{16,20},{20,16},{24,28},{28,24},{1,5},{5... | collective-permute-start | bytes 1769480 | tf_op jit(solution)/shard_map/ppermute | solution.py:10
  100.2 5.2 %collective-permute-start.44 = (bf16[128,2304]{1,0:T(8,128)(2,1)S(1)}, bf16[128,2304]{1,0:T(8,128)(2,1)S(1)}, u32[]{:S(2)}, u32[]{:S(2)}) collective-permute-start(bf16[128,2304]{1,0:T(8,128)(2,1)S(1)} %convolution_convert_fusion), channel_id=1, source_target_pairs={{0,4},{4,0},{8,12},{12,8},{16,20},{20,16},{24,28},{28,24},{1,5},{5... | collective-permute-start | bytes 1769480 | tf_op jit(solution)/shard_map/ppermute | solution.py:10
  101.4 7.7 %collective-permute-start.40 = (bf16[4,8,2304]{2,1,0:T(8,128)(2,1)S(1)}, bf16[4,8,2304]{2,1,0:T(8,128)(2,1)S(1)}, u32[]{:S(2)}, u32[]{:S(2)}) collective-permute-start(bf16[4,8,2304]{2,1,0:T(8,128)(2,1)S(1)} %get-tuple-element.13), channel_id=1, source_target_pairs={{0,24},{4,28},{8,16},{12,20},{16,8},{20,12},{24,0},{28,4},{1,25},{... | collective-permute-start | bytes 442376 | tf_op jit(solution)/shard_map/ppermute | solution.py:10
  102.9 9.4 %collective-permute-start.39 = (bf16[4,8,2304]{2,1,0:T(8,128)(2,1)S(1)}, bf16[4,8,2304]{2,1,0:T(8,128)(2,1)S(1)}, u32[]{:S(2)}, u32[]{:S(2)}) collective-permute-start(bf16[4,8,2304]{2,1,0:T(8,128)(2,1)S(1)} %get-tuple-element.14), channel_id=1, source_target_pairs={{0,16},{4,20},{8,24},{12,28},{16,0},{20,4},{24,8},{28,12},{1,17},{... | collective-permute-start | bytes 442376 | tf_op jit(solution)/shard_map/ppermute | solution.py:10
  103.7 8.6 %collective-permute-start.38 = (bf16[4,8,2304]{2,1,0:T(8,128)(2,1)S(1)}, bf16[4,8,2304]{2,1,0:T(8,128)(2,1)S(1)}, u32[]{:S(2)}, u32[]{:S(2)}) collective-permute-start(bf16[4,8,2304]{2,1,0:T(8,128)(2,1)S(1)} %get-tuple-element.12), channel_id=1, source_target_pairs={{0,8},{4,12},{8,0},{12,4},{16,24},{20,28},{24,16},{28,20},{1,9},{5... | collective-permute-start | bytes 442376 | tf_op jit(solution)/shard_map/ppermute | solution.py:10
  106.0 9.5 %collective-permute-start.47 = (bf16[4,8,2304]{2,1,0:T(8,128)(2,1)S(1)}, bf16[4,8,2304]{2,1,0:T(8,128)(2,1)S(1)}, u32[]{:S(2)}, u32[]{:S(2)}) collective-permute-start(bf16[4,8,2304]{2,1,0:T(8,128)(2,1)S(1)} %get-tuple-element.16), channel_id=1, source_target_pairs={{0,24},{4,28},{8,16},{12,20},{16,8},{20,12},{24,0},{28,4},{1,25},{... | collective-permute-start | bytes 442376 | tf_op jit(solution)/shard_map/ppermute | solution.py:10
  107.5 10.5 %collective-permute-start.46 = (bf16[4,8,2304]{2,1,0:T(8,128)(2,1)S(1)}, bf16[4,8,2304]{2,1,0:T(8,128)(2,1)S(1)}, u32[]{:S(2)}, u32[]{:S(2)}) collective-permute-start(bf16[4,8,2304]{2,1,0:T(8,128)(2,1)S(1)} %get-tuple-element.17), channel_id=1, source_target_pairs={{0,16},{4,20},{8,24},{12,28},{16,0},{20,4},{24,8},{28,12},{1,17},{... | collective-permute-start | bytes 442376 | tf_op jit(solution)/shard_map/ppermute | solution.py:10
  109.1 9.0 %collective-permute-start.45 = (bf16[4,8,2304]{2,1,0:T(8,128)(2,1)S(1)}, bf16[4,8,2304]{2,1,0:T(8,128)(2,1)S(1)}, u32[]{:S(2)}, u32[]{:S(2)}) collective-permute-start(bf16[4,8,2304]{2,1,0:T(8,128)(2,1)S(1)} %get-tuple-element.15), channel_id=1, source_target_pairs={{0,8},{4,12},{8,0},{12,4},{16,24},{20,28},{24,16},{28,20},{1,9},{5... | collective-permute-start | bytes 442376 | tf_op jit(solution)/shard_map/ppermute | solution.py:10
  112.4 8.9 %collective-permute-start.43 = (bf16[8,2304]{1,0:T(8,128)(2,1)S(1)}, bf16[8,2304]{1,0:T(8,128)(2,1)S(1)}, u32[]{:S(2)}, u32[]{:S(2)}) collective-permute-start(bf16[8,2304]{1,0:T(8,128)(2,1)S(1)} %get-tuple-element.33), channel_id=1, source_target_pairs={{0,3},{1,2},{2,1},{3,0},{4,7},{5,6},{6,5},{7,4},{8,11},{9,10},{10,... | collective-permute-start | bytes 110600 | tf_op jit(solution)/shard_map/ppermute | solution.py:10
  115.5 7.1 %collective-permute-start.42 = (bf16[8,2304]{1,0:T(8,128)(2,1)S(1)}, bf16[8,2304]{1,0:T(8,128)(2,1)S(1)}, u32[]{:S(2)}, u32[]{:S(2)}) collective-permute-start(bf16[8,2304]{1,0:T(8,128)(2,1)S(1)} %get-tuple-element.34), channel_id=1, source_target_pairs={{0,2},{1,3},{2,0},{3,1},{4,6},{5,7},{6,4},{7,5},{8,10},{9,11},{10,... | collective-permute-start | bytes 110600 | tf_op jit(solution)/shard_map/ppermute | solution.py:10
  115.5 7.1 %collective-permute-start.41 = (bf16[8,2304]{1,0:T(8,128)(2,1)S(1)}, bf16[8,2304]{1,0:T(8,128)(2,1)S(1)}, u32[]{:S(2)}, u32[]{:S(2)}) collective-permute-start(bf16[8,2304]{1,0:T(8,128)(2,1)S(1)} %get-tuple-element.32), channel_id=1, source_target_pairs={{0,1},{1,0},{2,3},{3,2},{4,5},{5,4},{6,7},{7,6},{8,9},{9,8},{10,11... | collective-permute-start | bytes 110600 | tf_op jit(solution)/shard_map/ppermute | solution.py:10
  118.2 5.9 %collective-permute-start.50 = (bf16[8,2304]{1,0:T(8,128)(2,1)S(1)}, bf16[8,2304]{1,0:T(8,128)(2,1)S(1)}, u32[]{:S(2)}, u32[]{:S(2)}) collective-permute-start(bf16[8,2304]{1,0:T(8,128)(2,1)S(1)} %get-tuple-element.36), channel_id=1, source_target_pairs={{0,3},{1,2},{2,1},{3,0},{4,7},{5,6},{6,5},{7,4},{8,11},{9,10},{10,... | collective-permute-start | bytes 110600 | tf_op jit(solution)/shard_map/ppermute | solution.py:10
  121.3 4.9 %collective-permute-start.49 = (bf16[8,2304]{1,0:T(8,128)(2,1)S(1)}, bf16[8,2304]{1,0:T(8,128)(2,1)S(1)}, u32[]{:S(2)}, u32[]{:S(2)}) collective-permute-start(bf16[8,2304]{1,0:T(8,128)(2,1)S(1)} %get-tuple-element.37), channel_id=1, source_target_pairs={{0,2},{1,3},{2,0},{3,1},{4,6},{5,7},{6,4},{7,5},{8,10},{9,11},{10,... | collective-permute-start | bytes 110600 | tf_op jit(solution)/shard_map/ppermute | solution.py:10
  121.3 4.9 %collective-permute-start.48 = (bf16[8,2304]{1,0:T(8,128)(2,1)S(1)}, bf16[8,2304]{1,0:T(8,128)(2,1)S(1)}, u32[]{:S(2)}, u32[]{:S(2)}) collective-permute-start(bf16[8,2304]{1,0:T(8,128)(2,1)S(1)} %get-tuple-element.35), channel_id=1, source_target_pairs={{0,1},{1,0},{2,3},{3,2},{4,5},{5,4},{6,7},{7,6},{8,9},{9,8},{10,11... | collective-permute-start | bytes 110600 | tf_op jit(solution)/shard_map/ppermute | solution.py:10
  (17 other events, 182.0 us)

commit v3 on v2

v3 whole, which is shorter than its diff:
```python
import jax
import jax.numpy as jnp
from jax import lax
from jax.sharding import PartitionSpec as P

CHUNKS = 2


def pair_swap(value):
    return lax.ppermute(value, "expert", [(i, i ^ 1) for i in range(lax.axis_size("expert"))])


def exchange_pairs(blocks):
    count = lax.axis_size("expert")
    groups = [list(range(parity, count, 2)) for parity in range(2)]
    return lax.all_to_all(
        blocks, "expert", split_axis=0, concat_axis=0, axis_index_groups=groups, tiled=True
    )


def exchange_feats(blocks):
    return lax.all_to_all(blocks, "feat", split_axis=0, concat_axis=0, tiled=True)


def copies(value, count):
    return jnp.broadcast_to(value[None], (count,) + value.shape)


def dot(a, b):
    return jnp.dot(a, b, preferred_element_type=jnp.float32)


def half(value):
    return value.astype(jnp.bfloat16)


def full(value):
    return value.astype(jnp.float32)


def shards(
    tokens,
    expert_ids,
    gate_weights,
    expert_gate,
    expert_up,
    expert_down,
    shared_gate,
    shared_up,
    shared_down,
    encoder,
    encoder_bias,
    decoder,
    decoder_bias,
):
    own, top = expert_ids.shape
    width = tokens.shape[1]
    feats = lax.axis_size("feat")
    pairs = lax.axis_size("expert") // 2
    devices = 2 * pairs * feats
    local_experts = expert_gate.shape[0]
    parity = lax.axis_index("expert") % 2
    step = own // CHUNKS
    rows = pairs * feats * step

    names = jnp.arange(devices * local_experts, dtype=jnp.int32)
    weights = jnp.sum(
        jnp.where(expert_ids[None] == names[:, None, None], gate_weights[None], 0.0), axis=2
    )
    weights = lax.all_to_all(
        weights.reshape(devices, local_experts, own),
        ("expert", "feat"),
        split_axis=0,
        concat_axis=0,
        tiled=True,
    )

    def chunk_rows(value):
        value = value.reshape(pairs, feats, CHUNKS, step, value.shape[-1])
        return value.transpose(2, 0, 1, 3, 4).reshape(-1, value.shape[-1])

    near = chunk_rows(exchange_pairs(copies(tokens, pairs)).reshape(pairs, feats, own, width))
    far = pair_swap(near)

    weights = weights.reshape(pairs, 2, feats, local_experts, own)
    even, odd = weights[:, 0], weights[:, 1]

    def scales(own_parity):
        value = jnp.where((parity == 0) == own_parity, even, odd)
        value = chunk_rows(value.transpose(0, 1, 3, 2))
        return [value[:, j : j + 1] for j in range(local_experts)]

    def swiglu(x, gate, up):
        return half(jax.nn.silu(dot(x, gate)) * dot(x, up))

    def expert_hidden(x):
        return [swiglu(x, expert_gate[j], expert_up[j]) for j in range(local_experts)]

    def expert_out(hidden, scale, c):
        cut = slice(c * rows, (c + 1) * rows)
        return sum(
            dot(hidden[j][cut], expert_down[j]) * scale[j][cut] for j in range(local_experts)
        )

    hidden_near = expert_hidden(near)
    scale_near, scale_far = scales(True), scales(False)
    received = [pair_swap(half(expert_out(hidden_near, scale_near, c))) for c in range(CHUNKS)]
    hidden_far = expert_hidden(far)
    my_pair = lax.axis_index("expert") // 2
    shared_rows = far.reshape(CHUNKS, pairs, feats * step, width)
    shared_rows = lax.dynamic_index_in_dim(shared_rows, my_pair, 1, False)
    shared_rows = shared_rows.reshape(CHUNKS * feats * step, width)
    shared_out = dot(swiglu(shared_rows, shared_gate, shared_up), shared_down)
    shared_out = shared_out.reshape(CHUNKS, feats, step, width)

    near_rows = []
    for c in range(CHUNKS):
        total = half(expert_out(hidden_far, scale_far, c) + full(received[c]))
        total = exchange_pairs(total.reshape(pairs, feats, step, width))
        total = half(jnp.sum(full(total), axis=0) + shared_out[c])
        moe_out = half(jnp.sum(full(exchange_feats(total)), axis=0))
        gathered = exchange_feats(copies(moe_out, feats))
        gathered = exchange_pairs(copies(gathered, pairs))
        near_rows.append(gathered.reshape(rows, width))

    def encode(x):
        return half(jax.nn.relu(dot(x, encoder) + encoder_bias[None, :]))

    features, reconstruction = [], []
    for c in range(CHUNKS):
        near, far = near_rows[c], pair_swap(near_rows[c])
        features_near = encode(near)
        arrived = pair_swap(half(dot(features_near, decoder)))
        features_far = encode(far)
        total = half(dot(features_far, decoder) + full(arrived))
        total = exchange_pairs(total.reshape(pairs, feats, step, width))
        total = exchange_feats(half(jnp.sum(full(total), axis=0)))
        reconstruction.append(jnp.sum(full(total), axis=0) + decoder_bias[None, :])
        both = [
            jnp.where(parity == 0, features_far, features_near),
            jnp.where(parity == 0, features_near, features_far),
        ]
        features.append(jnp.stack(both).reshape(2, pairs, feats, step, -1))
    reconstruction = jnp.concatenate(reconstruction, axis=0)
    features = jnp.stack(features).transpose(2, 1, 3, 0, 4, 5).reshape(devices * own, -1)
    return (features, reconstruction)


def solution(mesh):
    return jax.shard_map(
        shards,
        mesh=mesh,
        in_specs=(
            P("expert", None),
            P(("expert", "feat"), None),
            P(("expert", "feat"), None),
            P(("expert", "feat"), None, None),
            P(("expert", "feat"), None, None),
            P(("expert", "feat"), None, None),
            P(None, "feat"),
            P(None, "feat"),
            P("feat", None),
            P(None, ("expert", "feat")),
            P(("expert", "feat")),
            P(("expert", "feat"), None),
            P(),
        ),
        out_specs=(P(None, ("expert", "feat")), P(("expert", "feat"), None)),
        check_vma=False,
    )
```

time: 127 us -> 193 us (1.52)
  blocking collectives: 0 us -> 42.8 us
  starting transfers between devices: 62.1 us -> 36.8 us
  waiting for transfers between devices: 29.5 us -> 51 us
  matrix products: 20.4 us -> 38.5 us
  local copies, waits for them, and re-layouts: 5.68 us -> 15.1 us
    ppermute x51 -> x7, starting transfers between devices: 62.1 us -> 1.71 us  [pair_swap(): lax.ppermute(value, 'expert', [(i, i ^ 1) for i in range(lax.axis_size('e...]
    all_to_all x0 -> x10, waiting for transfers between devices: none -> 51 us  [the longest x6 30 us: exchange_pairs(): lax.all_to_all(blocks, 'expert', split_axis=0, concat_axis=0, axis_index_...]
    all_to_all x0 -> x4, blocking collectives: none -> 42.8 us  [the longest x2 18.3 us: exchange_feats(): lax.all_to_all(blocks, 'feat', split_axis=0, concat_axis=0, tiled=True)]
    all_to_all x0 -> x10, starting transfers between devices: none -> 35.1 us  [the longest x6 21.8 us: exchange_pairs(): lax.all_to_all(blocks, 'expert', split_axis=0, concat_axis=0, axis_index_...]
    ppermute x51 -> x7, waiting for transfers between devices: 29.5 us -> 0.02 us  [pair_swap(): lax.ppermute(value, 'expert', [(i, i ^ 1) for i in range(lax.axis_size('e...]
    dot_general x18, matrix products: 20.4 us -> 38.5 us  [dot(): return jnp.dot(a, b, preferred_element_type=jnp.float32)]
    broadcast_in_dim x0 -> x5, local copies, waits for them, and re-layouts: none -> 3.67 us  [copies(): return jnp.broadcast_to(value[None], (count,) + value.shape)]
    mul x0 -> x4, local copies, waits for them, and re-layouts: none -> 3.15 us  [expert_out(): dot(hidden[j][cut], expert_down[j]) * scale[j][cut]]
  transfers between devices with their start and end apart: 51 -> 17, of which waited for: 21 -> 10; matrix products, arithmetic and copies ran while one was open for 19% -> 26% of each run, Pallas kernels for 0% -> 0%
where the time goes in v3:
time: 193 us; the launch traced here: 191 us
  waiting for transfers between devices  51 us (26%)
  blocking collectives  42.8 us (22%)
  matrix products  38.5 us (20%)
  starting transfers between devices  36.8 us (19%)
  local copies, waits for them, and re-layouts  15.1 us (8%)
  other arithmetic  5.96 us (3%)
    dot_general x18, matrix products, dot(): return jnp.dot(a, b, preferred_element_type=jnp.float32)  38.5 us
    all_to_all x6, waiting for transfers between devices, exchange_pairs(): lax.all_to_all(blocks, 'expert', split_axis=0, concat_axis=0, axis_index_...  30 us
    all_to_all x6, starting transfers between devices, exchange_pairs(): lax.all_to_all(blocks, 'expert', split_axis=0, concat_axis=0, axis_index_...  21.8 us
    all_to_all x4, waiting for transfers between devices, exchange_feats(): lax.all_to_all(blocks, 'feat', split_axis=0, concat_axis=0, tiled=True)  21 us
    all_to_all x2, blocking collectives, exchange_feats(): lax.all_to_all(blocks, 'feat', split_axis=0, concat_axis=0, tiled=True)  18.3 us
    all_to_all x1, blocking collectives, shards(): lax.all_to_all(weights.reshape(devices, local_experts, own), ('expert', '...  14.3 us
    all_to_all x4, starting transfers between devices, exchange_feats(): lax.all_to_all(blocks, 'feat', split_axis=0, concat_axis=0, tiled=True)  13.3 us
    all_to_all x1, blocking collectives, exchange_pairs(): lax.all_to_all(blocks, 'expert', split_axis=0, concat_axis=0, axis_index_...  10.2 us
  transfers between devices with their start and end apart: 17, of which 10 were waited for; matrix products, arithmetic and copies ran while one was open for 26% of the time, Pallas kernels for 0%

profile of v3, /device:TPU:0, one launch (start us, length us, event | category | flops | bytes accessed | tf_op | source)
XLA Modules:
  0.0 191.4 jit_solution(3027627626844867082)
XLA Ops:
  0.6 0.9 copy.30
  2.5 14.3 %all_to_all.70 = f32[32,1,16]{2,1,0:T(1,128)S(1)} all-to-all(f32[32,1,16]{2,1,0:T(1,128)S(1)} %copy.32), channel_id=1, replica_groups=mesh['expert'=8,'feat'=4] {'expert','feat'}, dimensions={0} | all-to-all | bytes 4096 | tf_op jit(solution)/shard_map/all_to_all | solution.py:70
  16.8 2.1 %broadcast_in_dim.22 = bf16[4,64,2304]{2,1,0:T(8,128)(2,1)} broadcast(bf16[64,2304]{1,0:T(8,128)(2,1)} %param.13), dimensions={1,2} | broadcast | bytes 1474560 | tf_op jit(solution)/shard_map/broadcast_in_dim | solution.py:26
  18.9 3.5 %all-to-all-start = ((bf16[4,64,2304]{2,1,0:T(8,128)(2,1)}), bf16[4,64,2304]{2,1,0:T(8,128)(2,1)S(1)}, u32[]{:S(2)}, u32[]{:S(2)}) async-start(bf16[4,64,2304]{2,1,0:T(8,128)(2,1)} %broadcast_in_dim.22), calls=%async_computation | async-start | bytes 2359296 | tf_op jit(solution)/shard_map/all_to_all | solution.py:16
  23.8 1.4 select_n.85
  25.2 1.5 slice_reduce_fusion.2
  29.8 7.8 %all-to-all-done = bf16[4,64,2304]{2,1,0:T(8,128)(2,1)S(1)} async-done(((bf16[4,64,2304]{2,1,0:T(8,128)(2,1)}), bf16[4,64,2304]{2,1,0:T(8,128)(2,1)S(1)}, u32[]{:S(2)}, u32[]{:S(2)}) %all-to-all-start) | async-done | bytes 1179680 | tf_op jit(solution)/shard_map/all_to_all | solution.py:16
  37.8 3.9 %fusion.12 = f32[256,1024]{1,0:T(8,128)S(1)} fusion(bf16[256,2304]{1,0:T(8,128)(2,1)S(1)} %bitcast.115, bf16[1,2304,1024]{2,1,0:T(8,128)(2,1)} %param.16), kind=kOutput, calls=%fused_computation.12 | convolution fusion | flops 1207959552 | bytes 6946816 | tf_op jit(solution)/shard_map/dot_general | solution.py:30
  41.8 1.5 fusion.37
  45.0 1.6 fusion.31
  47.1 1.4 fusion.14
  48.5 1.5 multiply_convert_fusion
  50.1 1.6 add_convert_fusion.2
  51.7 3.5 %all-to-all-start.6 = ((bf16[4,4,8,2304]{3,2,1,0:T(8,128)(2,1)}), bf16[4,4,8,2304]{3,2,1,0:T(8,128)(2,1)S(1)}, u32[]{:S(2)}, u32[]{:S(2)}) async-start(bf16[4,4,8,2304]{3,2,1,0:T(8,128)(2,1)} %bitcast.17), calls=%async_computation.6 | async-start | bytes 1179648 | tf_op jit(solution)/shard_map/all_to_all | solution.py:16
  55.2 1.0 constant_dynamic-slice_fusion
  56.3 1.6 fusion.65
  57.9 4.1 %add_convert_fusion.3 = bf16[128,2304]{1,0:T(8,128)(2,1)} fusion(bf16[128,2304]{1,0:T(8,128)(2,1)} %collective-permute-done.1, f32[128]{0:T(128)S(1)} %mul.62, bf16[1,1024,2304]{2,1,0:T(8,128)(2,1)} %param.18, bf16[256,1024]{1,0:T(8,128)(2,1)S(1)} %copy-done.7), kind=kOutput, calls=%fused_computation.31 | convolution fusion | flops 605159424 | bytes 6160896 | tf_op jit(solution)/shard_map/dot_general | solution.py:30
  62.0 2.3 %all-to-all-done.6 = bf16[4,4,8,2304]{3,2,1,0:T(8,128)(2,1)S(1)} async-done(((bf16[4,4,8,2304]{3,2,1,0:T(8,128)(2,1)}), bf16[4,4,8,2304]{3,2,1,0:T(8,128)(2,1)S(1)}, u32[]{:S(2)}, u32[]{:S(2)}) %all-to-all-start.6) | async-done | bytes 589856 | tf_op jit(solution)/shard_map/all_to_all | solution.py:16
  64.3 4.2 %all-to-all-start.2 = ((bf16[4,4,8,2304]{3,2,1,0:T(8,128)(2,1)}), bf16[4,4,8,2304]{3,2,1,0:T(8,128)(2,1)}, u32[]{:S(2)}, u32[]{:S(2)}) async-start(bf16[4,4,8,2304]{3,2,1,0:T(8,128)(2,1)} %bitcast.10), calls=%async_computation.2 | async-start | bytes 1179648 | tf_op jit(solution)/shard_map/all_to_all | solution.py:16
  68.5 3.3 %fusion.60 = f32[64,2304]{1,0:T(8,128)} fusion(bf16[256,2304]{1,0:T(8,128)(2,1)} %param.21, f32[64,256]{1,0:T(8,128)S(1)} %fusion.65, bf16[64,2304]{1,0:T(8,128)(2,1)S(1)} %bitcast.109, bf16[2304,256]{1,0:T(8,128)(2,1)} %param.20), kind=kOutput, calls=%fused_computation.68 | convolution fusion | flops 151093248 | bytes 3309568 | tf_op jit(solution)/shard_map/dot_general | solution.py:30
  71.9 5.0 %all-to-all-done.2 = bf16[4,4,8,2304]{3,2,1,0:T(8,128)(2,1)} async-done(((bf16[4,4,8,2304]{3,2,1,0:T(8,128)(2,1)}), bf16[4,4,8,2304]{3,2,1,0:T(8,128)(2,1)}, u32[]{:S(2)}, u32[]{:S(2)}) %all-to-all-start.2) | async-done | bytes 589856 | tf_op jit(solution)/shard_map/all_to_all | solution.py:16
  76.9 1.2 convert_reduce_fusion.1
  78.8 9.0 %all_to_all.71 = bf16[4,8,2304]{2,1,0:T(8,128)(2,1)S(1)} all-to-all(bf16[4,8,2304]{2,1,0:T(8,128)(2,1)S(1)} %get-tuple-element.7), channel_id=1, replica_groups=mesh['expert'=8,'feat'=4] {'feat'}, dimensions={0} | all-to-all | bytes 294912 | tf_op jit(solution)/shard_map/all_to_all | solution.py:22
  87.8 3.3 %all-to-all-start.3 = ((bf16[4,8,2304]{2,1,0:T(8,128)(2,1)}), bf16[4,8,2304]{2,1,0:T(8,128)(2,1)S(1)}, u32[]{:S(2)}, u32[]{:S(2)}) async-start(bf16[4,8,2304]{2,1,0:T(8,128)(2,1)} %get-tuple-element.6), calls=%async_computation.3 | async-start | bytes 294912 | tf_op jit(solution)/shard_map/all_to_all | solution.py:22
  91.2 5.9 %all-to-all-done.3 = bf16[4,8,2304]{2,1,0:T(8,128)(2,1)S(1)} async-done(((bf16[4,8,2304]{2,1,0:T(8,128)(2,1)}), bf16[4,8,2304]{2,1,0:T(8,128)(2,1)S(1)}, u32[]{:S(2)}, u32[]{:S(2)}) %all-to-all-start.3) | async-done | bytes 147488 | tf_op jit(solution)/shard_map/all_to_all | solution.py:22
  97.7 3.3 %all-to-all-start.8 = ((bf16[4,8,2304]{2,1,0:T(8,128)(2,1)}), bf16[4,8,2304]{2,1,0:T(8,128)(2,1)S(1)}, u32[]{:S(2)}, u32[]{:S(2)}) async-start(bf16[4,8,2304]{2,1,0:T(8,128)(2,1)} %broadcast_in_dim.27), calls=%async_computation.8 | async-start | bytes 294912 | tf_op jit(solution)/shard_map/all_to_all | solution.py:22
  101.1 5.9 %all-to-all-done.8 = bf16[4,8,2304]{2,1,0:T(8,128)(2,1)S(1)} async-done(((bf16[4,8,2304]{2,1,0:T(8,128)(2,1)}), bf16[4,8,2304]{2,1,0:T(8,128)(2,1)S(1)}, u32[]{:S(2)}, u32[]{:S(2)}) %all-to-all-start.8) | async-done | bytes 147488 | tf_op jit(solution)/shard_map/all_to_all | solution.py:22
  107.0 9.3 %all_to_all.72 = bf16[4,8,2304]{2,1,0:T(8,128)(2,1)S(1)} all-to-all(bf16[4,8,2304]{2,1,0:T(8,128)(2,1)S(1)} %broadcast_in_dim.25), channel_id=1, replica_groups=mesh['expert'=8,'feat'=4] {'feat'}, dimensions={0} | all-to-all | bytes 294912 | tf_op jit(solution)/shard_map/all_to_all | solution.py:22
  116.4 10.2 %all_to_all.73 = bf16[4,4,8,2304]{3,2,1,0:T(8,128)(2,1)S(1)} all-to-all(bf16[4,4,8,2304]{3,2,1,0:T(8,128)(2,1)S(1)} %broadcast_in_dim.28), channel_id=1, replica_groups={{0,8,16,24},{4,12,20,28},{1,9,17,25},{5,13,21,29},{2,10,18,26},{6,14,22..., dimensions={0} | all-to-all | bytes 1179648 | tf_op jit(solution)/shard_map/all_to_all | solution.py:16
  127.5 3.7 %all-to-all-start.5 = ((bf16[4,4,8,2304]{3,2,1,0:T(8,128)(2,1)}), bf16[4,4,8,2304]{3,2,1,0:T(8,128)(2,1)S(1)}, u32[]{:S(2)}, u32[]{:S(2)}) async-start(bf16[4,4,8,2304]{3,2,1,0:T(8,128)(2,1)} %broadcast_in_dim.26), calls=%async_computation.5 | async-start | bytes 1179648 | tf_op jit(solution)/shard_map/all_to_all | solution.py:16
  131.2 2.1 %fusion.44 = bf16[128,512]{1,0:T(8,128)(2,1)S(1)} fusion(bf16[128,2304]{1,0:T(8,128)(2,1)S(1)} %bitcast.113, bf16[2304,512]{1,0:T(8,128)(2,1)} %param.22, f32[512]{0:T(512)S(1)} %copy-done.12), kind=kOutput, calls=%fused_computation.40 | convolution fusion | flops 302186496 | bytes 3082240 | tf_op jit(solution)/shard_map/dot_general | solution.py:30
  133.4 1.3 convolution_convert_fusion
  135.2 2.7 %all-to-all-done.5 = bf16[4,4,8,2304]{3,2,1,0:T(8,128)(2,1)S(1)} async-done(((bf16[4,4,8,2304]{3,2,1,0:T(8,128)(2,1)}), bf16[4,4,8,2304]{3,2,1,0:T(8,128)(2,1)S(1)}, u32[]{:S(2)}, u32[]{:S(2)}) %all-to-all-start.5) | async-done | bytes 589856 | tf_op jit(solution)/shard_map/all_to_all | solution.py:16
  137.9 2.1 %fusion.46 = bf16[128,512]{1,0:T(8,128)(2,1)S(1)} fusion(bf16[128,2304]{1,0:T(8,128)(2,1)S(1)} %bitcast.111, bf16[2304,512]{1,0:T(8,128)(2,1)} %param.22, f32[512]{0:T(512)S(1)} %copy-done.12), kind=kOutput, calls=%fused_computation.42 | convolution fusion | flops 302186496 | bytes 3082240 | tf_op jit(solution)/shard_map/dot_general | solution.py:30
  140.1 1.3 convolution_convert_fusion.1
  142.0 2.3 %broadcast_select_fusion.1 = (bf16[128,512]{1,0:T(8,128)(2,1)}, bf16[128,512]{1,0:T(8,128)(2,1)}, bf16[128,512]{1,0:T(8,128)(2,1)S(1)}) fusion(bf16[128,512]{1,0:T(8,128)(2,1)S(1)} %copy-done.5, pred[]{:T(512)S(6)} %eq.12, f32[512]{0:T(512)S(1)} %copy-done.12, bf16[128,2304]{1,0:T(8,128)(2,1)} %collective-permute-done.4, bf16[2304,512]{1,0:T(8,128)(2,1)S(1)} %copy-done.1), kind=kOutput, calls=%fused_computation.60 | convolution fusion | flops 302317568 | bytes 3475457 | tf_op jit(solution)/shard_map/dot_general | solution.py:30
  144.3 2.4 %add_convert_fusion = bf16[128,2304]{1,0:T(8,128)(2,1)} fusion(bf16[128,2304]{1,0:T(8,128)(2,1)} %collective-permute-done.6, bf16[128,512]{1,0:T(8,128)(2,1)S(1)} %get-tuple-element.16, bf16[512,2304]{1,0:T(8,128)(2,1)S(1)} %copy-done), kind=kOutput, calls=%fused_computation.26 | convolution fusion | flops 302874624 | bytes 3670016 | tf_op jit(solution)/shard_map/dot_general | solution.py:30
  146.7 3.5 %all-to-all-start.12 = ((bf16[4,4,8,2304]{3,2,1,0:T(8,128)(2,1)}), bf16[4,4,8,2304]{3,2,1,0:T(8,128)(2,1)S(1)}, u32[]{:S(2)}, u32[]{:S(2)}) async-start(bf16[4,4,8,2304]{3,2,1,0:T(8,128)(2,1)} %bitcast.25), calls=%async_computation.12 | async-start | bytes 1179648 | tf_op jit(solution)/shard_map/all_to_all | solution.py:16
  150.2 3.0 %broadcast_select_fusion.3 = (bf16[128,512]{1,0:T(8,128)(2,1)}, bf16[128,512]{1,0:T(8,128)(2,1)}, bf16[128,512]{1,0:T(8,128)(2,1)S(1)}) fusion(bf16[128,512]{1,0:T(8,128)(2,1)} %copy-done.3, pred[]{:T(512)S(6)} %eq.12, f32[512]{0:T(512)S(1)} %copy-done.12, bf16[128,2304]{1,0:T(8,128)(2,1)} %collective-permute-done.2, bf16[2304,512]{1,0:T(8,128)(2,1)} %param.22), kind=kOutput, calls=%fused_computation.62 | convolution fusion | flops 302317568 | bytes 3475457 | tf_op jit(solution)/shard_map/dot_general | solution.py:30
  153.2 2.4 %add_convert_fusion.1 = bf16[128,2304]{1,0:T(8,128)(2,1)} fusion(bf16[128,2304]{1,0:T(8,128)(2,1)} %collective-permute-done.5, bf16[128,512]{1,0:T(8,128)(2,1)S(1)} %get-tuple-element.17, bf16[512,2304]{1,0:T(8,128)(2,1)S(1)} %copy-done), kind=kOutput, calls=%fused_computation.27 | convolution fusion | flops 302874624 | bytes 3670016 | tf_op jit(solution)/shard_map/dot_general | solution.py:30
  155.6 4.2 %all-to-all-done.12 = bf16[4,4,8,2304]{3,2,1,0:T(8,128)(2,1)S(1)} async-done(((bf16[4,4,8,2304]{3,2,1,0:T(8,128)(2,1)}), bf16[4,4,8,2304]{3,2,1,0:T(8,128)(2,1)S(1)}, u32[]{:S(2)}, u32[]{:S(2)}) %all-to-all-start.12) | async-done | bytes 589856 | tf_op jit(solution)/shard_map/all_to_all | solution.py:16
  159.8 3.5 %all-to-all-start.10 = ((bf16[4,4,8,2304]{3,2,1,0:T(8,128)(2,1)}), bf16[4,4,8,2304]{3,2,1,0:T(8,128)(2,1)S(1)}, u32[]{:S(2)}, u32[]{:S(2)}) async-start(bf16[4,4,8,2304]{3,2,1,0:T(8,128)(2,1)} %bitcast.24), calls=%async_computation.10 | async-start | bytes 1179648 | tf_op jit(solution)/shard_map/all_to_all | solution.py:16
  164.0 8.1 %all-to-all-done.10 = bf16[4,4,8,2304]{3,2,1,0:T(8,128)(2,1)S(1)} async-done(((bf16[4,4,8,2304]{3,2,1,0:T(8,128)(2,1)}), bf16[4,4,8,2304]{3,2,1,0:T(8,128)(2,1)S(1)}, u32[]{:S(2)}, u32[]{:S(2)}) %all-to-all-start.10) | async-done | bytes 589856 | tf_op jit(solution)/shard_map/all_to_all | solution.py:16
  172.1 3.3 %all-to-all-start.13 = ((bf16[4,8,2304]{2,1,0:T(8,128)(2,1)}), bf16[4,8,2304]{2,1,0:T(8,128)(2,1)S(1)}, u32[]{:S(2)}, u32[]{:S(2)}) async-start(bf16[4,8,2304]{2,1,0:T(8,128)(2,1)} %reduce_sum.100), calls=%async_computation.13 | async-start | bytes 294912 | tf_op jit(solution)/shard_map/all_to_all | solution.py:22
  176.2 5.2 %all-to-all-done.13 = bf16[4,8,2304]{2,1,0:T(8,128)(2,1)S(1)} async-done(((bf16[4,8,2304]{2,1,0:T(8,128)(2,1)}), bf16[4,8,2304]{2,1,0:T(8,128)(2,1)S(1)}, u32[]{:S(2)}, u32[]{:S(2)}) %all-to-all-start.13) | async-done | bytes 147488 | tf_op jit(solution)/shard_map/all_to_all | solution.py:22
  181.4 3.3 %all-to-all-start.11 = ((bf16[4,8,2304]{2,1,0:T(8,128)(2,1)}), bf16[4,8,2304]{2,1,0:T(8,128)(2,1)S(1)}, u32[]{:S(2)}, u32[]{:S(2)}) async-start(bf16[4,8,2304]{2,1,0:T(8,128)(2,1)} %reduce_sum.98), calls=%async_computation.11 | async-start | bytes 294912 | tf_op jit(solution)/shard_map/all_to_all | solution.py:22
  184.8 1.0 maximum_bitcast_fusion
  186.6 4.0 %all-to-all-done.11 = bf16[4,8,2304]{2,1,0:T(8,128)(2,1)S(1)} async-done(((bf16[4,8,2304]{2,1,0:T(8,128)(2,1)}), bf16[4,8,2304]{2,1,0:T(8,128)(2,1)S(1)}, u32[]{:S(2)}, u32[]{:S(2)}) %all-to-all-start.11) | async-done | bytes 147488 | tf_op jit(solution)/shard_map/all_to_all | solution.py:22
  (83 shorter events, 14.6 us)
Async XLA Ops:
  0.6 132.8 %copy-start = (bf16[512,2304]{1,0:T(8,128)(2,1)S(1)}, bf16[512,2304]{1,0:T(8,128)(2,1)}, u32[]{:S(2)}) copy-start(bf16[512,2304]{1,0:T(8,128)(2,1)} %param.24) | copy-start | bytes 7077892
  18.9 18.8 %all-to-all-start = ((bf16[4,64,2304]{2,1,0:T(8,128)(2,1)}), bf16[4,64,2304]{2,1,0:T(8,128)(2,1)S(1)}, u32[]{:S(2)}, u32[]{:S(2)}) async-start(bf16[4,64,2304]{2,1,0:T(8,128)(2,1)} %broadcast_in_dim.22), calls=%async_computation | async-start | bytes 2359296 | tf_op jit(solution)/shard_map/all_to_all | solution.py:16
  37.6 4.2 %slice-start.4 = ((s8[4718592]{0:T(1024)(128)(4,1)}), s8[4194304]{0:T(1024)(128)(4,1)S(1)}, s32[]{:S(2)}) async-start(s8[4718592]{0:T(1024)(128)(4,1)} %bitcast.129), calls=%async_computation.18 | async-start | bytes 8388608
  37.7 4.1 %slice-start.5 = ((s8[4718592]{0:T(1024)(128)(4,1)}), s8[524288]{0:T(1024)(128)(4,1)S(1)}, s32[]{:S(2)}) async-start(s8[4718592]{0:T(1024)(128)(4,1)} %bitcast.129), calls=%async_computation.19 | async-start | bytes 1048576
  37.7 9.4 %collective-permute-start = (bf16[256,2304]{1,0:T(8,128)(2,1)S(1)}, bf16[256,2304]{1,0:T(8,128)(2,1)S(1)}, u32[]{:S(2)}, u32[]{:S(2)}) collective-permute-start(bf16[256,2304]{1,0:T(8,128)(2,1)S(1)} %bitcast.114), channel_id=1, source_target_pairs={{0,4},{4,0},{8,12},{12,8},{16,20},{20,16},{24,28},{28,24},{1,5},{5... | collective-permute-start | bytes 3538952 | tf_op jit(solution)/shard_map/ppermute | solution.py:10
  37.8 5.5 %slice-start = ((s8[4718592]{0:T(1024)(128)(4,1)}), s8[4194304]{0:T(1024)(128)(4,1)S(1)}, s32[]{:S(2)}) async-start(s8[4718592]{0:T(1024)(128)(4,1)} %bitcast.105), calls=%async_computation.14 | async-start | bytes 8388608
  37.8 9.3 %slice-start.2 = ((s8[4718592]{0:T(1024)(128)(4,1)}), s8[4194304]{0:T(1024)(128)(4,1)S(1)}, s32[]{:S(2)}) async-start(s8[4718592]{0:T(1024)(128)(4,1)} %bitcast.127), calls=%async_computation.16 | async-start | bytes 8388608
  41.8 2.3 %slice-start.1 = ((s8[4718592]{0:T(1024)(128)(4,1)}), s8[524288]{0:T(1024)(128)(4,1)S(1)}, s32[]{:S(2)}) async-start(s8[4718592]{0:T(1024)(128)(4,1)} %bitcast.105), calls=%async_computation.15 | async-start | bytes 1048576
  41.8 5.3 %slice-start.3 = ((s8[4718592]{0:T(1024)(128)(4,1)}), s8[524288]{0:T(1024)(128)(4,1)S(1)}, s32[]{:S(2)}) async-start(s8[4718592]{0:T(1024)(128)(4,1)} %bitcast.127), calls=%async_computation.17 | async-start | bytes 1048576
  44.9 5.2 %collective-permute-start.3 = (bf16[128,2304]{1,0:T(8,128)(2,1)S(1)}, bf16[128,2304]{1,0:T(8,128)(2,1)S(1)}, u32[]{:S(2)}, u32[]{:S(2)}) collective-permute-start(bf16[128,2304]{1,0:T(8,128)(2,1)S(1)} %fusion.28), channel_id=1, source_target_pairs={{0,4},{4,0},{8,12},{12,8},{16,20},{20,16},{24,28},{28,24},{1,5},{5... | collective-permute-start | bytes 1769480 | tf_op jit(solution)/shard_map/ppermute | solution.py:10
  46.6 11.3 %collective-permute-start.1 = (bf16[128,2304]{1,0:T(8,128)(2,1)}, bf16[128,2304]{1,0:T(8,128)(2,1)}, u32[]{:S(2)}, u32[]{:S(2)}) collective-permute-start(bf16[128,2304]{1,0:T(8,128)(2,1)} %fusion.31), channel_id=1, source_target_pairs={{0,4},{4,0},{8,12},{12,8},{16,20},{20,16},{24,28},{28,24},{1,5},{5... | collective-permute-start | bytes 1769480 | tf_op jit(solution)/shard_map/ppermute | solution.py:10
  47.1 1.4 copy-start.11
  50.0 1.7 copy-start.6
  51.7 12.6 %all-to-all-start.6 = ((bf16[4,4,8,2304]{3,2,1,0:T(8,128)(2,1)}), bf16[4,4,8,2304]{3,2,1,0:T(8,128)(2,1)S(1)}, u32[]{:S(2)}, u32[]{:S(2)}) async-start(bf16[4,4,8,2304]{3,2,1,0:T(8,128)(2,1)} %bitcast.17), calls=%async_computation.6 | async-start | bytes 1179648 | tf_op jit(solution)/shard_map/all_to_all | solution.py:16
  55.2 2.7 %copy-start.7 = (bf16[256,1024]{1,0:T(8,128)(2,1)S(1)}, bf16[256,1024]{1,0:T(8,128)(2,1)}, u32[]{:S(2)}) copy-start(bf16[256,1024]{1,0:T(8,128)(2,1)} %copy-done.6) | copy-start | bytes 1572868
  64.3 12.5 %all-to-all-start.2 = ((bf16[4,4,8,2304]{3,2,1,0:T(8,128)(2,1)}), bf16[4,4,8,2304]{3,2,1,0:T(8,128)(2,1)}, u32[]{:S(2)}, u32[]{:S(2)}) async-start(bf16[4,4,8,2304]{3,2,1,0:T(8,128)(2,1)} %bitcast.10), calls=%async_computation.2 | async-start | bytes 1179648 | tf_op jit(solution)/shard_map/all_to_all | solution.py:16
  71.9 6.2 %copy-start.2 = (f32[64,2304]{1,0:T(8,128)S(1)}, f32[64,2304]{1,0:T(8,128)}, u32[]{:S(2)}) copy-start(f32[64,2304]{1,0:T(8,128)} %fusion.60) | copy-start | bytes 1769476
  87.8 9.3 %all-to-all-start.3 = ((bf16[4,8,2304]{2,1,0:T(8,128)(2,1)}), bf16[4,8,2304]{2,1,0:T(8,128)(2,1)S(1)}, u32[]{:S(2)}, u32[]{:S(2)}) async-start(bf16[4,8,2304]{2,1,0:T(8,128)(2,1)} %get-tuple-element.6), calls=%async_computation.3 | async-start | bytes 294912 | tf_op jit(solution)/shard_map/all_to_all | solution.py:22
  97.7 9.3 %all-to-all-start.8 = ((bf16[4,8,2304]{2,1,0:T(8,128)(2,1)}), bf16[4,8,2304]{2,1,0:T(8,128)(2,1)S(1)}, u32[]{:S(2)}, u32[]{:S(2)}) async-start(bf16[4,8,2304]{2,1,0:T(8,128)(2,1)} %broadcast_in_dim.27), calls=%async_computation.8 | async-start | bytes 294912 | tf_op jit(solution)/shard_map/all_to_all | solution.py:22
  126.6 4.6 %copy-start.12 = (f32[512]{0:T(512)S(1)}, f32[512]{0:T(512)}, u32[]{:S(2)}) copy-start(f32[512]{0:T(512)} %param.23) | copy-start | bytes 6148
  127.5 10.4 %all-to-all-start.5 = ((bf16[4,4,8,2304]{3,2,1,0:T(8,128)(2,1)}), bf16[4,4,8,2304]{3,2,1,0:T(8,128)(2,1)S(1)}, u32[]{:S(2)}, u32[]{:S(2)}) async-start(bf16[4,4,8,2304]{3,2,1,0:T(8,128)(2,1)} %broadcast_in_dim.26), calls=%async_computation.5 | async-start | bytes 1179648 | tf_op jit(solution)/shard_map/all_to_all | solution.py:16
  131.2 10.8 %collective-permute-start.4 = (bf16[128,2304]{1,0:T(8,128)(2,1)S(1)}, bf16[128,2304]{1,0:T(8,128)(2,1)}, u32[]{:S(2)}, u32[]{:S(2)}) collective-permute-start(bf16[128,2304]{1,0:T(8,128)(2,1)S(1)} %bitcast.112), channel_id=1, source_target_pairs={{0,4},{4,0},{8,12},{12,8},{16,20},{20,16},{24,28},{28,24},{1,5},{5... | collective-permute-start | bytes 1769480 | tf_op jit(solution)/shard_map/ppermute | solution.py:10
  133.4 1.3 copy-start.4
  134.7 9.6 %collective-permute-start.6 = (bf16[128,2304]{1,0:T(8,128)(2,1)}, bf16[128,2304]{1,0:T(8,128)(2,1)}, u32[]{:S(2)}, u32[]{:S(2)}) collective-permute-start(bf16[128,2304]{1,0:T(8,128)(2,1)} %convolution_convert_fusion), channel_id=1, source_target_pairs={{0,4},{4,0},{8,12},{12,8},{16,20},{20,16},{24,28},{28,24},{1,5},{5... | collective-permute-start | bytes 1769480 | tf_op jit(solution)/shard_map/ppermute | solution.py:10
  137.9 12.3 %collective-permute-start.2 = (bf16[128,2304]{1,0:T(8,128)(2,1)S(1)}, bf16[128,2304]{1,0:T(8,128)(2,1)}, u32[]{:S(2)}, u32[]{:S(2)}) collective-permute-start(bf16[128,2304]{1,0:T(8,128)(2,1)S(1)} %bitcast.110), channel_id=1, source_target_pairs={{0,4},{4,0},{8,12},{12,8},{16,20},{20,16},{24,28},{28,24},{1,5},{5... | collective-permute-start | bytes 1769480 | tf_op jit(solution)/shard_map/ppermute | solution.py:10
  140.1 1.4 copy-start.3
  140.1 1.9 %copy-start.1 = (bf16[2304,512]{1,0:T(8,128)(2,1)S(1)}, bf16[2304,512]{1,0:T(8,128)(2,1)}, u32[]{:S(2)}) copy-start(bf16[2304,512]{1,0:T(8,128)(2,1)} %param.22) | copy-start | bytes 7077892
  140.1 1.9 %copy-start.5 = (bf16[128,512]{1,0:T(8,128)(2,1)S(1)}, bf16[128,512]{1,0:T(8,128)(2,1)}, u32[]{:S(2)}) copy-start(bf16[128,512]{1,0:T(8,128)(2,1)} %copy-done.4) | copy-start | bytes 393220
  141.4 11.8 %collective-permute-start.5 = (bf16[128,2304]{1,0:T(8,128)(2,1)}, bf16[128,2304]{1,0:T(8,128)(2,1)}, u32[]{:S(2)}, u32[]{:S(2)}) collective-permute-start(bf16[128,2304]{1,0:T(8,128)(2,1)} %convolution_convert_fusion.1), channel_id=1, source_target_pairs={{0,4},{4,0},{8,12},{12,8},{16,20},{20,16},{24,28},{28,24},{1,5},{5... | collective-permute-start | bytes 1769480 | tf_op jit(solution)/shard_map/ppermute | solution.py:10
  146.7 13.1 %all-to-all-start.12 = ((bf16[4,4,8,2304]{3,2,1,0:T(8,128)(2,1)}), bf16[4,4,8,2304]{3,2,1,0:T(8,128)(2,1)S(1)}, u32[]{:S(2)}, u32[]{:S(2)}) async-start(bf16[4,4,8,2304]{3,2,1,0:T(8,128)(2,1)} %bitcast.25), calls=%async_computation.12 | async-start | bytes 1179648 | tf_op jit(solution)/shard_map/all_to_all | solution.py:16
  159.8 12.3 %all-to-all-start.10 = ((bf16[4,4,8,2304]{3,2,1,0:T(8,128)(2,1)}), bf16[4,4,8,2304]{3,2,1,0:T(8,128)(2,1)S(1)}, u32[]{:S(2)}, u32[]{:S(2)}) async-start(bf16[4,4,8,2304]{3,2,1,0:T(8,128)(2,1)} %bitcast.24), calls=%async_computation.10 | async-start | bytes 1179648 | tf_op jit(solution)/shard_map/all_to_all | solution.py:16
  164.0 20.7 %copy-start.8 = (bf16[128,512]{1,0:T(8,128)(2,1)S(1)}, bf16[128,512]{1,0:T(8,128)(2,1)}, u32[]{:S(2)}) copy-start(bf16[128,512]{1,0:T(8,128)(2,1)} %get-tuple-element.10) | copy-start | bytes 393220
  164.0 20.7 %copy-start.9 = (bf16[128,512]{1,0:T(8,128)(2,1)S(1)}, bf16[128,512]{1,0:T(8,128)(2,1)}, u32[]{:S(2)}) copy-start(bf16[128,512]{1,0:T(8,128)(2,1)} %get-tuple-element.11) | copy-start | bytes 393220
  164.0 20.7 %copy-start.10 = (bf16[128,512]{1,0:T(8,128)(2,1)S(1)}, bf16[128,512]{1,0:T(8,128)(2,1)}, u32[]{:S(2)}) copy-start(bf16[128,512]{1,0:T(8,128)(2,1)} %get-tuple-element.8) | copy-start | bytes 393220
  172.1 9.3 %all-to-all-start.13 = ((bf16[4,8,2304]{2,1,0:T(8,128)(2,1)}), bf16[4,8,2304]{2,1,0:T(8,128)(2,1)S(1)}, u32[]{:S(2)}, u32[]{:S(2)}) async-start(bf16[4,8,2304]{2,1,0:T(8,128)(2,1)} %reduce_sum.100), calls=%async_computation.13 | async-start | bytes 294912 | tf_op jit(solution)/shard_map/all_to_all | solution.py:22
  181.4 9.3 %all-to-all-start.11 = ((bf16[4,8,2304]{2,1,0:T(8,128)(2,1)}), bf16[4,8,2304]{2,1,0:T(8,128)(2,1)S(1)}, u32[]{:S(2)}, u32[]{:S(2)}) async-start(bf16[4,8,2304]{2,1,0:T(8,128)(2,1)} %reduce_sum.98), calls=%async_computation.11 | async-start | bytes 294912 | tf_op jit(solution)/shard_map/all_to_all | solution.py:22
  184.8 5.9 %copy-start.13 = (f32[2304]{0:T(1024)S(1)}, f32[2304]{0:T(1024)}, u32[]{:S(2)}) copy-start(f32[2304]{0:T(1024)} %param.25) | copy-start | bytes 27652

commit v4 on v2

v4 whole, which is shorter than its diff:
```python
import jax
import jax.numpy as jnp
from jax import lax
from jax.sharding import PartitionSpec as P

CHUNKS = 2


def swap(value, axis, r):
    return lax.ppermute(value, axis, [(i, i ^ r) for i in range(lax.axis_size(axis))])


def dot(a, b):
    return jnp.dot(a, b, preferred_element_type=jnp.float32)


def half(value):
    return value.astype(jnp.bfloat16)


def full(value):
    return value.astype(jnp.float32)


def bits_of(count):
    assert count & (count - 1) == 0
    return [1 << b for b in range(count.bit_length() - 1)]


def take(value, index, dim):
    return lax.dynamic_index_in_dim(value, index, dim, keepdims=False)


def gather_pairs(value):
    pairs = lax.axis_size("expert") // 2
    return jnp.stack([value] + [swap(value, "expert", 2 * p) for p in range(1, pairs)])


def reduce_pairs(value):
    arrived = [swap(half(value[p]), "expert", 2 * p) for p in range(1, value.shape[0])]
    return value[0] + sum(full(a) for a in arrived)


def shards(
    tokens,
    expert_ids,
    gate_weights,
    expert_gate,
    expert_up,
    expert_down,
    shared_gate,
    shared_up,
    shared_down,
    encoder,
    encoder_bias,
    decoder,
    decoder_bias,
):
    own, top = expert_ids.shape
    width = tokens.shape[1]
    feats = lax.axis_size("feat")
    pairs = lax.axis_size("expert") // 2
    devices = 2 * pairs * feats
    local_experts = expert_gate.shape[0]
    me = lax.axis_index(("expert", "feat"))
    my_feat = lax.axis_index("feat")
    feat_bits = bits_of(feats)
    step = own // CHUNKS
    rows = pairs * feats * step

    high = half(gate_weights)
    low = half(gate_weights - full(high))
    row = jnp.concatenate([half(expert_ids), high, low], axis=1)
    mine = jnp.arange(feats, dtype=jnp.int32)[:, None, None] == my_feat
    table = jnp.where(mine, row[None], jnp.zeros_like(row)[None])
    table = table.reshape(feats, CHUNKS, step, 3 * top).transpose(0, 2, 1, 3)
    lanes = -(-CHUNKS * 3 * top // 128) * 128
    table = table.reshape(feats * step, CHUNKS * 3 * top)
    table = jnp.pad(table, ((0, 0), (0, lanes - table.shape[1])))
    for bit in feat_bits:
        table = table + swap(table, "feat", bit)

    parts = tokens.reshape(feats, CHUNKS, step, width)
    parts = [parts[:, c].reshape(feats * step, width) for c in range(CHUNKS)]
    parts[-1] = jnp.concatenate([parts[-1], table], axis=1)
    both = []
    for part in parts:
        near = gather_pairs(part).reshape(rows, -1)
        both.append(jnp.concatenate([near, swap(near, "expert", 1)], axis=0))
    tables = both[-1][:, width:]
    both[-1] = both[-1][:, :width]

    def scales(c):
        ids = tables[:, c * 3 * top :][:, :top].astype(jnp.int32)
        weights = full(tables[:, (c * 3 + 1) * top :][:, :top])
        weights = weights + full(tables[:, (c * 3 + 2) * top :][:, :top])
        return [
            jnp.sum(jnp.where(ids == me * local_experts + j, weights, 0.0), axis=1)[:, None]
            for j in range(local_experts)
        ]

    def swiglu(x, gate, up):
        return half(jax.nn.silu(dot(x, gate)) * dot(x, up))

    def run_experts(x, scale):
        out = 0.0
        for j in range(local_experts):
            hidden = swiglu(x, expert_gate[j], expert_up[j])
            out = out + dot(hidden, expert_down[j]) * scale[j]
        return out

    near_rows = []
    for c in range(CHUNKS):
        out = run_experts(both[c], scales(c))
        shared_rows = both[c][rows : rows + feats * step]
        shared_out = dot(swiglu(shared_rows, shared_gate, shared_up), shared_down)
        total = out[rows:] + full(swap(half(out[:rows]), "expert", 1))
        total = reduce_pairs(total.reshape(pairs, feats * step, width)) + shared_out
        total = total.reshape((2,) * len(feat_bits) + (step, width))
        place = [(my_feat // bit) % 2 for bit in feat_bits]
        for i, bit in enumerate(feat_bits[:-1]):
            dim = len(feat_bits) - 1 - i
            arrived = swap(half(take(total, 1 - place[i], dim)), "feat", bit)
            total = take(total, place[i], dim) + full(arrived)
        total = half(total)
        moe_out = half(full(total) + full(swap(total, "feat", feat_bits[-1])))
        for i, bit in reversed(list(enumerate(feat_bits[:-1]))):
            moe_out = jnp.stack([moe_out, swap(moe_out, "feat", bit)], axis=1)
        near_rows.append(gather_pairs(moe_out).reshape(rows, width))

    def encode(x):
        return half(jax.nn.relu(dot(x, encoder) + encoder_bias[None, :]))

    features, reconstruction = [], []
    for c in range(CHUNKS):
        near, far = near_rows[c], swap(near_rows[c], "expert", 1)
        features_near = encode(near)
        arrived = swap(half(dot(features_near, decoder)), "expert", 1)
        features_far = encode(far)
        total = dot(features_far, decoder) + full(arrived)
        total = reduce_pairs(total.reshape(pairs, feats * step, width))
        total = total.reshape((2,) * len(feat_bits) + (step, width))
        for bit in feat_bits[:-1]:
            dim = len(total.shape) - 3
            arrived = swap(half(lax.index_in_dim(total, 1, dim, False)), "feat", bit)
            total = lax.index_in_dim(total, 0, dim, False) + full(arrived)
        arrived = swap(half(take(total, 1 - place[-1], 0)), "feat", feat_bits[-1])
        reconstruction.append(take(total, place[-1], 0) + full(arrived) + decoder_bias[None, :])
        both = jnp.stack([features_far, features_near])
        features.append(both.reshape(2, pairs, feats, step, -1))
    reconstruction = jnp.concatenate(reconstruction, axis=0)

    features = jnp.stack(features).transpose(2, 1, 3, 0, 4, 5).reshape(devices, own, -1)
    relative = me - me % feats + my_feat % (feats // 2)
    blocks = [lax.dynamic_index_in_dim(features, i ^ relative, 0) for i in range(devices)]
    features = jnp.concatenate(blocks, axis=0).reshape(devices * own, -1)
    return (features, reconstruction)


def solution(mesh):
    return jax.shard_map(
        shards,
        mesh=mesh,
        in_specs=(
            P("expert", None),
            P(("expert", "feat"), None),
            P(("expert", "feat"), None),
            P(("expert", "feat"), None, None),
            P(("expert", "feat"), None, None),
            P(("expert", "feat"), None, None),
            P(None, "feat"),
            P(None, "feat"),
            P("feat", None),
            P(None, ("expert", "feat")),
            P(("expert", "feat")),
            P(("expert", "feat"), None),
            P(),
        ),
        out_specs=(P(None, ("expert", "feat")), P(("expert", "feat"), None)),
        check_vma=False,
    )
```

time: 127 us -> 147 us (1.16)
  matrix products: 20.4 us -> 38.6 us
  starting transfers between devices: 62.1 us -> 54 us
  other arithmetic: 7.7 us -> 12.2 us
  local copies, waits for them, and re-layouts: 5.68 us -> 9.52 us
    dot_general x18 -> x16, matrix products: 20.4 us -> 38.6 us  [dot(): return jnp.dot(a, b, preferred_element_type=jnp.float32)]
    ppermute x51 -> x44, starting transfers between devices: 62.1 us -> 54 us  [swap(): lax.ppermute(value, axis, [(i, i ^ r) for i in range(lax.axis_size(axis))])]
    another operation x6 -> x9, other arithmetic: 0.35 us -> 6.64 us  [the longest x4 0.21 us: shards(): near_rows.append(jnp.stack(pieces).reshape(rows, width))]
    slice x3 -> x6, local copies, waits for them, and re-layouts: 0.03 us -> 4.49 us  [the longest x2 3.63 us: shards(): total = out[rows:] + full(swap(half(out[:rows]), 'expert', 1))]
    unnamed x60 -> x57, local copies, waits for them, and re-layouts: 3.93 us -> 0.39 us
    concatenate x4 -> x1, other arithmetic: 2.08 us -> 0.01 us  [shards(): row = jnp.concatenate([half(expert_ids), high, low], axis=1)]
    convert_element_type x4 -> x6, other arithmetic: 1.61 us -> 3.56 us  [half(): return value.astype(jnp.bfloat16)]
    add x3 -> x7, other arithmetic: 1.67 us -> 0.19 us  [the longest x2 0.12 us: reduce_pairs(): return value[0] + sum((full(a) for a in arrived))]
  transfers between devices with their start and end apart: 51 -> 44, of which waited for: 21 -> 20; matrix products, arithmetic and copies ran while one was open for 19% -> 29% of each run, Pallas kernels for 0% -> 0%
where the time goes in v4:
time: 147 us; the launch traced here: 146 us
  starting transfers between devices  54 us (37%)
  matrix products  38.6 us (26%)
  waiting for transfers between devices  30.6 us (21%)
  other arithmetic  12.2 us (8%)
  local copies, waits for them, and re-layouts  9.52 us (6%)
    ppermute x44, starting transfers between devices, swap(): lax.ppermute(value, axis, [(i, i ^ r) for i in range(lax.axis_size(axis))])  54 us
    dot_general x16, matrix products, dot(): return jnp.dot(a, b, preferred_element_type=jnp.float32)  38.6 us
    ppermute x44, waiting for transfers between devices, swap(): lax.ppermute(value, axis, [(i, i ^ r) for i in range(lax.axis_size(axis))])  30.6 us
    slice x2, local copies, waits for them, and re-layouts, shards(): total = out[rows:] + full(swap(half(out[:rows]), 'expert', 1))  3.63 us
    convert_element_type x6, other arithmetic, half(): return value.astype(jnp.bfloat16)  3.56 us
    another operation x2, other arithmetic  3.54 us
    another operation x7, other arithmetic, gather_pairs(): jnp.stack([value] + [swap(value, 'expert', 2 * p) for p in range(1, pairs)])  3.1 us
  transfers between devices with their start and end apart: 44, of which 20 were waited for; matrix products, arithmetic and copies ran while one was open for 29% of the time, Pallas kernels for 0%

profile of v4, /device:TPU:0, one launch (start us, length us, event | category | flops | bytes accessed | tf_op | source)
XLA Modules:
  0.0 146.3 jit_solution(2420531054850218168)
XLA Ops:
  4.1 3.1 %collective-permute-start.4 = (bf16[32,128]{1,0:T(8,128)(2,1)S(1)}, bf16[32,128]{1,0:T(8,128)(2,1)S(1)}, u32[]{:S(2)}, u32[]{:S(2)}) collective-permute-start(bf16[32,128]{1,0:T(8,128)(2,1)S(1)} %pad.4), channel_id=1, source_target_pairs={{0,1},{1,0},{2,3},{3,2},{4,5},{5,4},{6,7},{7,6},{8,9},{9,8},{10,11... | collective-permute-start | bytes 24584 | tf_op jit(solution)/shard_map/ppermute | solution.py:10
  8.2 2.5 %collective-permute-start.2 = (bf16[32,2304]{1,0:T(8,128)(2,1)S(1)}, bf16[32,2304]{1,0:T(8,128)(2,1)S(1)}, u32[]{:S(2)}, u32[]{:S(2)}) collective-permute-start(bf16[32,2304]{1,0:T(8,128)(2,1)S(1)} %get-tuple-element.27), channel_id=1, source_target_pairs={{0,24},{4,28},{8,16},{12,20},{16,8},{20,12},{24,0},{28,4},{1,25},{... | collective-permute-start | bytes 442376 | tf_op jit(solution)/shard_map/ppermute | solution.py:10
  11.7 2.7 %collective-permute-start.5 = (bf16[32,128]{1,0:T(8,128)(2,1)S(1)}, bf16[32,128]{1,0:T(8,128)(2,1)S(1)}, u32[]{:S(2)}, u32[]{:S(2)}) collective-permute-start(bf16[32,128]{1,0:T(8,128)(2,1)S(1)} %pad_add_fusion), channel_id=1, source_target_pairs={{0,2},{1,3},{2,0},{3,1},{4,6},{5,7},{6,4},{7,5},{8,10},{9,11},{10,... | collective-permute-start | bytes 24584 | tf_op jit(solution)/shard_map/ppermute | solution.py:10
  14.4 2.0 %collective-permute-done.5 = bf16[32,128]{1,0:T(8,128)(2,1)S(1)} collective-permute-done((bf16[32,128]{1,0:T(8,128)(2,1)S(1)}, bf16[32,128]{1,0:T(8,128)(2,1)S(1)}, u32[]{:S(2)}, u32[]{:S(2)}) %collective-permute-start.5) | collective-permute-done | bytes 8224 | tf_op jit(solution)/shard_map/ppermute | solution.py:10
  16.3 1.2 collective-permute-done.1
  19.3 1.7 %collective-permute-start.8 = (bf16[32,2432]{1,0:T(8,128)(2,1)}, bf16[32,2432]{1,0:T(8,128)(2,1)}, u32[]{:S(2)}, u32[]{:S(2)}) collective-permute-start(bf16[32,2432]{1,0:T(8,128)(2,1)} %get-tuple-element.30), channel_id=1, source_target_pairs={{0,24},{4,28},{8,16},{12,20},{16,8},{20,12},{24,0},{28,4},{1,25},{... | collective-permute-start | bytes 466952 | tf_op jit(solution)/shard_map/ppermute | solution.py:10
  21.0 1.3 collective-permute-start.7
  22.8 4.6 %collective-permute-done.8 = bf16[32,2432]{1,0:T(8,128)(2,1)} collective-permute-done((bf16[32,2432]{1,0:T(8,128)(2,1)}, bf16[32,2432]{1,0:T(8,128)(2,1)}, u32[]{:S(2)}, u32[]{:S(2)}) %collective-permute-start.8) | collective-permute-done | bytes 155680 | tf_op jit(solution)/shard_map/ppermute | solution.py:10
  27.4 2.9 %collective-permute-done.7 = bf16[32,2432]{1,0:T(8,128)(2,1)} collective-permute-done((bf16[32,2432]{1,0:T(8,128)(2,1)}, bf16[32,2432]{1,0:T(8,128)(2,1)}, u32[]{:S(2)}, u32[]{:S(2)}) %collective-permute-start.7) | collective-permute-done | bytes 155680 | tf_op jit(solution)/shard_map/ppermute | solution.py:10
  31.7 2.0 %fusion.47 = f32[32,256]{1,0:T(8,128)} fusion(bf16[2304,256]{1,0:T(8,128)(2,1)S(1)} %copy-done.3, bf16[128,2304]{1,0:T(8,128)(2,1)} %collective-permute-done.3), kind=kOutput, calls=%fused_computation.84 | convolution fusion | flops 37748736 | bytes 1359872 | tf_op jit(solution)/shard_map/dot_general | solution.py:14
  33.7 5.1 %fusion.10 = f32[256,1024]{1,0:T(8,128)} fusion(bf16[1,2304,1024]{2,1,0:T(8,128)(2,1)} %param.16, bf16[128,2304]{1,0:T(8,128)(2,1)} %collective-permute-done.3, bf16[128,2304]{1,0:T(8,128)(2,1)} %bitcast.6), kind=kOutput, calls=%fused_computation.10 | convolution fusion | flops 1210318848 | bytes 6946816 | tf_op jit(solution)/shard_map/dot_general | solution.py:14
  39.2 2.4 %fusion.4 = f32[256,1024]{1,0:T(8,128)} fusion(bf16[1,2304,1024]{2,1,0:T(8,128)(2,1)S(1)} %bitcast.222, bf16[128,2432]{1,0:T(8,128)(2,1)S(1)} %bitcast.155, bf16[128,2432]{1,0:T(8,128)(2,1)S(1)} %collective-permute-done.9), kind=kOutput, calls=%fused_computation.4 | convolution fusion | flops 1210318848 | bytes 7012352 | tf_op jit(solution)/shard_map/dot_general | solution.py:14
  41.6 8.7 %fusion.15 = f32[256,2304]{1,0:T(8,128)} fusion(bf16[1,1024,2304]{2,1,0:T(8,128)(2,1)} %param.18, f32[256]{0:T(256)S(1)} %get-tuple-element.3, f32[256,1024]{1,0:T(8,128)} %fusion.4, bf16[1,2304,1024]{2,1,0:T(8,128)(2,1)} %param.16, bf16[128,2432]{1,0:T(8,128)(2,1)} %bitcast.156, bf16[128,2432]{1,0:T(8,128)(2,1)} %copy-done.5), kind=kOutput, calls=%fused_computation.13 | convolution fusion | flops 2420441088 | bytes 14091264 | tf_op jit(solution)/shard_map/dot_general | solution.py:14
  50.3 2.1 %slice.292 = bf16[128,2304]{1,0:T(8,128)(2,1)} slice(f32[256,2304]{1,0:T(8,128)} %fusion.15), slice={[0:128], [0:2304]} | slice | bytes 1179648 | tf_op jit(solution)/shard_map/slice | solution.py:117
  52.9 8.6 %fusion.12 = f32[256,2304]{1,0:T(8,128)} fusion(bf16[1,1024,2304]{2,1,0:T(8,128)(2,1)} %param.18, f32[256]{0:T(256)S(1)} %get-tuple-element.2, f32[256,1024]{1,0:T(8,128)} %fusion.10, bf16[1,2304,1024]{2,1,0:T(8,128)(2,1)} %param.17, bf16[128,2304]{1,0:T(8,128)(2,1)} %collective-permute-done.3, bf16[128,2304]{1,0:T(8,128)(2,1)} %bitcast.6), kind=kOutput, calls=%fused_computation.12 | convolution fusion | flops 2420441088 | bytes 14025728 | tf_op jit(solution)/shard_map/dot_general | solution.py:14
  61.4 1.5 %slice.293 = bf16[128,2304]{1,0:T(8,128)(2,1)S(1)} slice(f32[256,2304]{1,0:T(8,128)} %fusion.12), slice={[0:128], [0:2304]} | slice | bytes 1179648 | tf_op jit(solution)/shard_map/slice | solution.py:117
  63.0 1.9 %fusion.43 = f32[32,256]{1,0:T(8,128)} fusion(bf16[2304,256]{1,0:T(8,128)(2,1)S(1)} %copy-done.3, bf16[128,2432]{1,0:T(8,128)(2,1)} %copy-done.5), kind=kOutput, calls=%fused_computation.80 | convolution fusion | flops 37748736 | bytes 1359872 | tf_op jit(solution)/shard_map/dot_general | solution.py:14
  64.9 2.4 %fusion.93 = (bf16[128,2304]{1,0:T(8,128)(2,1)S(1)}, f32[128,2304]{1,0:T(8,128)}) fusion(bf16[128,2304]{1,0:T(8,128)(2,1)} %collective-permute-done.21, f32[256,2304]{1,0:T(8,128)S(1)} %copy-done.7), kind=kLoop, calls=%fused_computation.160 | loop fusion | flops 884736 | bytes 3538944 | tf_op jit(solution)/shard_map/convert.10
  67.3 1.7 %collective-permute-start.24 = (bf16[32,2304]{1,0:T(8,128)(2,1)S(1)}, bf16[32,2304]{1,0:T(8,128)(2,1)}, u32[]{:S(2)}, u32[]{:S(2)}) collective-permute-start(bf16[32,2304]{1,0:T(8,128)(2,1)S(1)} %get-tuple-element.24), channel_id=1, source_target_pairs={{0,24},{4,28},{8,16},{12,20},{16,8},{20,12},{24,0},{28,4},{1,25},{... | collective-permute-start | bytes 442376 | tf_op jit(solution)/shard_map/ppermute | solution.py:10
  69.0 1.3 collective-permute-start.23
  72.8 1.7 %collective-permute-start.13 = (bf16[32,2304]{1,0:T(8,128)(2,1)}, bf16[32,2304]{1,0:T(8,128)(2,1)}, u32[]{:S(2)}, u32[]{:S(2)}) collective-permute-start(bf16[32,2304]{1,0:T(8,128)(2,1)} %get-tuple-element.21), channel_id=1, source_target_pairs={{0,24},{4,28},{8,16},{12,20},{16,8},{20,12},{24,0},{28,4},{1,25},{... | collective-permute-start | bytes 442376 | tf_op jit(solution)/shard_map/ppermute | solution.py:10
  74.5 1.3 collective-permute-start.12
  76.6 1.7 %collective-permute-done.23 = bf16[32,2304]{1,0:T(8,128)(2,1)} collective-permute-done((bf16[32,2304]{1,0:T(8,128)(2,1)S(1)}, bf16[32,2304]{1,0:T(8,128)(2,1)}, u32[]{:S(2)}, u32[]{:S(2)}) %collective-permute-start.23) | collective-permute-done | bytes 147488 | tf_op jit(solution)/shard_map/ppermute | solution.py:10
  78.3 3.0 %fusion.37 = f32[32,2304]{1,0:T(8,128)} fusion(f32[128,2304]{1,0:T(8,128)} %get-tuple-element.11, bf16[32,2304]{1,0:T(8,128)(2,1)} %collective-permute-done.24, bf16[32,2304]{1,0:T(8,128)(2,1)} %collective-permute-done.23, bf16[32,2304]{1,0:T(8,128)(2,1)} %collective-permute-done.22, bf16[256,2304]{1,0:T(8,128)(2,1)S(1)} %copy-done.2, ...), kind=kOutput, calls=%fused_computation.54 | convolution fusion | flops 76062720 | bytes 3571712 | tf_op jit(solution)/shard_map/dot_general | solution.py:14
  81.3 1.5 %fusion.52 = bf16[2,8,2304]{2,1,0:T(8,128)(2,1)} fusion(f32[2,2,8,2304]{3,2,1,0:T(8,128)} %bitcast.197, s32[]{:T(128)S(6)} %select_n.158), kind=kLoop, calls=%fused_computation.91 | loop fusion | bytes 147460 | tf_op jit(solution)/shard_map/convert_element_type | solution.py:18
  84.1 3.0 %fusion.38 = f32[32,2304]{1,0:T(8,128)} fusion(f32[128,2304]{1,0:T(8,128)} %get-tuple-element.9, bf16[32,2304]{1,0:T(8,128)(2,1)} %collective-permute-done.13, bf16[32,2304]{1,0:T(8,128)(2,1)} %collective-permute-done.12, bf16[32,2304]{1,0:T(8,128)(2,1)} %collective-permute-done.11, bf16[256,2304]{1,0:T(8,128)(2,1)S(1)} %copy-done.2, ...), kind=kOutput, calls=%fused_computation.56 | convolution fusion | flops 76062720 | bytes 3571712 | tf_op jit(solution)/shard_map/dot_general | solution.py:14
  90.1 2.7 %collective-permute-start.26 = (bf16[2,8,2304]{2,1,0:T(8,128)(2,1)S(1)}, bf16[2,8,2304]{2,1,0:T(8,128)(2,1)S(1)}, u32[]{:S(2)}, u32[]{:S(2)}) collective-permute-start(bf16[2,8,2304]{2,1,0:T(8,128)(2,1)S(1)} %fusion.41), channel_id=1, source_target_pairs={{0,2},{1,3},{2,0},{3,1},{4,6},{5,7},{6,4},{7,5},{8,10},{9,11},{10,... | collective-permute-start | bytes 221192 | tf_op jit(solution)/shard_map/ppermute | solution.py:10
  93.7 3.3 %collective-permute-start.15 = (bf16[2,8,2304]{2,1,0:T(8,128)(2,1)S(1)}, bf16[2,8,2304]{2,1,0:T(8,128)(2,1)S(1)}, u32[]{:S(2)}, u32[]{:S(2)}) collective-permute-start(bf16[2,8,2304]{2,1,0:T(8,128)(2,1)S(1)} %fusion.42), channel_id=1, source_target_pairs={{0,2},{1,3},{2,0},{3,1},{4,6},{5,7},{6,4},{7,5},{8,10},{9,11},{10,... | collective-permute-start | bytes 221192 | tf_op jit(solution)/shard_map/ppermute | solution.py:10
  98.1 2.0 %collective-permute-done.15 = bf16[2,8,2304]{2,1,0:T(8,128)(2,1)S(1)} collective-permute-done((bf16[2,8,2304]{2,1,0:T(8,128)(2,1)S(1)}, bf16[2,8,2304]{2,1,0:T(8,128)(2,1)S(1)}, u32[]{:S(2)}, u32[]{:S(2)}) %collective-permute-start.15) | collective-permute-done | bytes 73760 | tf_op jit(solution)/shard_map/ppermute | solution.py:10
  100.9 1.3 collective-permute-done.27
  102.2 1.5 %collective-permute-start.30 = (bf16[2,2,8,2304]{3,2,1,0:T(8,128)(2,1)S(1)}, bf16[2,2,8,2304]{3,2,1,0:T(8,128)(2,1)S(1)}, u32[]{:S(2)}, u32[]{:S(2)}) collective-permute-start(bf16[2,2,8,2304]{3,2,1,0:T(8,128)(2,1)S(1)} %get-tuple-element.34), channel_id=1, source_target_pairs={{0,24},{4,28},{8,16},{12,20},{16,8},{20,12},{24,0},{28,4},{1,25},{... | collective-permute-start | bytes 442376 | tf_op jit(solution)/shard_map/ppermute | solution.py:10
  103.7 1.3 collective-permute-start.29
  105.8 1.5 %collective-permute-start.19 = (bf16[2,2,8,2304]{3,2,1,0:T(8,128)(2,1)S(1)}, bf16[2,2,8,2304]{3,2,1,0:T(8,128)(2,1)S(1)}, u32[]{:S(2)}, u32[]{:S(2)}) collective-permute-start(bf16[2,2,8,2304]{3,2,1,0:T(8,128)(2,1)S(1)} %get-tuple-element.32), channel_id=1, source_target_pairs={{0,24},{4,28},{8,16},{12,20},{16,8},{20,12},{24,0},{28,4},{1,25},{... | collective-permute-start | bytes 442376 | tf_op jit(solution)/shard_map/ppermute | solution.py:10
  107.3 1.3 collective-permute-start.18
  108.6 1.3 collective-permute-done.30
  109.9 1.3 collective-permute-start.17
  112.4 1.6 %collective-permute-done.19 = bf16[2,2,8,2304]{3,2,1,0:T(8,128)(2,1)S(1)} collective-permute-done((bf16[2,2,8,2304]{3,2,1,0:T(8,128)(2,1)S(1)}, bf16[2,2,8,2304]{3,2,1,0:T(8,128)(2,1)S(1)}, u32[]{:S(2)}, u32[]{:S(2)}) %collective-permute-start.19) | collective-permute-done | bytes 147488 | tf_op jit(solution)/shard_map/ppermute | solution.py:10
  113.9 1.4 collective-permute-done.18
  119.2 1.5 %collective-permute-start.35 = (bf16[32,2304]{1,0:T(8,128)(2,1)S(1)}, bf16[32,2304]{1,0:T(8,128)(2,1)S(1)}, u32[]{:S(2)}, u32[]{:S(2)}) collective-permute-start(bf16[32,2304]{1,0:T(8,128)(2,1)S(1)} %get-tuple-element.15), channel_id=1, source_target_pairs={{0,24},{4,28},{8,16},{12,20},{16,8},{20,12},{24,0},{28,4},{1,25},{... | collective-permute-start | bytes 442376 | tf_op jit(solution)/shard_map/ppermute | solution.py:10
  120.8 1.3 collective-permute-start.34
  123.8 1.5 %collective-permute-start.41 = (bf16[32,2304]{1,0:T(8,128)(2,1)S(1)}, bf16[32,2304]{1,0:T(8,128)(2,1)S(1)}, u32[]{:S(2)}, u32[]{:S(2)}) collective-permute-start(bf16[32,2304]{1,0:T(8,128)(2,1)S(1)} %get-tuple-element.18), channel_id=1, source_target_pairs={{0,24},{4,28},{8,16},{12,20},{16,8},{20,12},{24,0},{28,4},{1,25},{... | collective-permute-start | bytes 442376 | tf_op jit(solution)/shard_map/ppermute | solution.py:10
  125.3 1.3 collective-permute-start.40
  128.2 1.9 %collective-permute-done.34 = bf16[32,2304]{1,0:T(8,128)(2,1)S(1)} collective-permute-done((bf16[32,2304]{1,0:T(8,128)(2,1)S(1)}, bf16[32,2304]{1,0:T(8,128)(2,1)S(1)}, u32[]{:S(2)}, u32[]{:S(2)}) %collective-permute-start.34) | collective-permute-done | bytes 147488 | tf_op jit(solution)/shard_map/ppermute | solution.py:10
  131.2 2.1 %collective-permute-done.41 = bf16[32,2304]{1,0:T(8,128)(2,1)S(1)} collective-permute-done((bf16[32,2304]{1,0:T(8,128)(2,1)S(1)}, bf16[32,2304]{1,0:T(8,128)(2,1)S(1)}, u32[]{:S(2)}, u32[]{:S(2)}) %collective-permute-start.41) | collective-permute-done | bytes 147488 | tf_op jit(solution)/shard_map/ppermute | solution.py:10
  133.3 2.6 %collective-permute-done.40 = bf16[32,2304]{1,0:T(8,128)(2,1)S(1)} collective-permute-done((bf16[32,2304]{1,0:T(8,128)(2,1)S(1)}, bf16[32,2304]{1,0:T(8,128)(2,1)S(1)}, u32[]{:S(2)}, u32[]{:S(2)}) %collective-permute-start.40) | collective-permute-done | bytes 147488 | tf_op jit(solution)/shard_map/ppermute | solution.py:10
  137.0 3.3 %collective-permute-start.37 = (bf16[8,2304]{1,0:T(8,128)(2,1)S(1)}, bf16[8,2304]{1,0:T(8,128)(2,1)S(1)}, u32[]{:S(2)}, u32[]{:S(2)}) collective-permute-start(bf16[8,2304]{1,0:T(8,128)(2,1)S(1)} %fusion.59), channel_id=1, source_target_pairs={{0,2},{1,3},{2,0},{3,1},{4,6},{5,7},{6,4},{7,5},{8,10},{9,11},{10,... | collective-permute-start | bytes 110600 | tf_op jit(solution)/shard_map/ppermute | solution.py:10
  140.4 3.2 %collective-permute-start.43 = (bf16[8,2304]{1,0:T(8,128)(2,1)S(1)}, bf16[8,2304]{1,0:T(8,128)(2,1)S(1)}, u32[]{:S(2)}, u32[]{:S(2)}) collective-permute-start(bf16[8,2304]{1,0:T(8,128)(2,1)S(1)} %fusion.60), channel_id=1, source_target_pairs={{0,2},{1,3},{2,0},{3,1},{4,6},{5,7},{6,4},{7,5},{8,10},{9,11},{10,... | collective-permute-start | bytes 110600 | tf_op jit(solution)/shard_map/ppermute | solution.py:10
  143.6 1.9 %collective-permute-done.43 = bf16[8,2304]{1,0:T(8,128)(2,1)S(1)} collective-permute-done((bf16[8,2304]{1,0:T(8,128)(2,1)S(1)}, bf16[8,2304]{1,0:T(8,128)(2,1)S(1)}, u32[]{:S(2)}, u32[]{:S(2)}) %collective-permute-start.43) | collective-permute-done | bytes 36896 | tf_op jit(solution)/shard_map/ppermute | solution.py:10
  (163 shorter events, 31.9 us)
Async XLA Ops:
  0.6 115.4 %copy-start = (bf16[512,2304]{1,0:T(8,128)(2,1)S(1)}, bf16[512,2304]{1,0:T(8,128)(2,1)}, u32[]{:S(2)}) copy-start(bf16[512,2304]{1,0:T(8,128)(2,1)} %param.24) | copy-start | bytes 7077892
  0.6 31.0 %copy-start.3 = (bf16[2304,256]{1,0:T(8,128)(2,1)S(1)}, bf16[2304,256]{1,0:T(8,128)(2,1)}, u32[]{:S(2)}) copy-start(bf16[2304,256]{1,0:T(8,128)(2,1)} %param.20) | copy-start | bytes 3538948
  4.1 7.7 %collective-permute-start.4 = (bf16[32,128]{1,0:T(8,128)(2,1)S(1)}, bf16[32,128]{1,0:T(8,128)(2,1)S(1)}, u32[]{:S(2)}, u32[]{:S(2)}) collective-permute-start(bf16[32,128]{1,0:T(8,128)(2,1)S(1)} %pad.4), channel_id=1, source_target_pairs={{0,1},{1,0},{2,3},{3,2},{4,5},{5,4},{6,7},{7,6},{8,9},{9,8},{10,11... | collective-permute-start | bytes 24584 | tf_op jit(solution)/shard_map/ppermute | solution.py:10
  8.2 8.2 %collective-permute-start.2 = (bf16[32,2304]{1,0:T(8,128)(2,1)S(1)}, bf16[32,2304]{1,0:T(8,128)(2,1)S(1)}, u32[]{:S(2)}, u32[]{:S(2)}) collective-permute-start(bf16[32,2304]{1,0:T(8,128)(2,1)S(1)} %get-tuple-element.27), channel_id=1, source_target_pairs={{0,24},{4,28},{8,16},{12,20},{16,8},{20,12},{24,0},{28,4},{1,25},{... | collective-permute-start | bytes 442376 | tf_op jit(solution)/shard_map/ppermute | solution.py:10
  10.7 6.9 %collective-permute-start.1 = (bf16[32,2304]{1,0:T(8,128)(2,1)S(1)}, bf16[32,2304]{1,0:T(8,128)(2,1)S(1)}, u32[]{:S(2)}, u32[]{:S(2)}) collective-permute-start(bf16[32,2304]{1,0:T(8,128)(2,1)S(1)} %get-tuple-element.27), channel_id=1, source_target_pairs={{0,16},{4,20},{8,24},{12,28},{16,0},{20,4},{24,8},{28,12},{1,17},{... | collective-permute-start | bytes 442376 | tf_op jit(solution)/shard_map/ppermute | solution.py:10
  11.2 6.5 %collective-permute-start = (bf16[32,2304]{1,0:T(8,128)(2,1)S(1)}, bf16[32,2304]{1,0:T(8,128)(2,1)S(1)}, u32[]{:S(2)}, u32[]{:S(2)}) collective-permute-start(bf16[32,2304]{1,0:T(8,128)(2,1)S(1)} %get-tuple-element.27), channel_id=1, source_target_pairs={{0,8},{4,12},{8,0},{12,4},{16,24},{20,28},{24,16},{28,20},{1,9},{5... | collective-permute-start | bytes 442376 | tf_op jit(solution)/shard_map/ppermute | solution.py:10
  11.7 4.6 %collective-permute-start.5 = (bf16[32,128]{1,0:T(8,128)(2,1)S(1)}, bf16[32,128]{1,0:T(8,128)(2,1)S(1)}, u32[]{:S(2)}, u32[]{:S(2)}) collective-permute-start(bf16[32,128]{1,0:T(8,128)(2,1)S(1)} %pad_add_fusion), channel_id=1, source_target_pairs={{0,2},{1,3},{2,0},{3,1},{4,6},{5,7},{6,4},{7,5},{8,10},{9,11},{10,... | collective-permute-start | bytes 24584 | tf_op jit(solution)/shard_map/ppermute | solution.py:10
  18.6 13.1 %collective-permute-start.3 = (bf16[128,2304]{1,0:T(8,128)(2,1)}, bf16[128,2304]{1,0:T(8,128)(2,1)}, u32[]{:S(2)}, u32[]{:S(2)}) collective-permute-start(bf16[128,2304]{1,0:T(8,128)(2,1)} %bitcast.6), channel_id=1, source_target_pairs={{0,4},{4,0},{8,12},{12,8},{16,20},{20,16},{24,28},{28,24},{1,5},{5... | collective-permute-start | bytes 1769480 | tf_op jit(solution)/shard_map/ppermute | solution.py:10
  19.3 8.1 %collective-permute-start.8 = (bf16[32,2432]{1,0:T(8,128)(2,1)}, bf16[32,2432]{1,0:T(8,128)(2,1)}, u32[]{:S(2)}, u32[]{:S(2)}) collective-permute-start(bf16[32,2432]{1,0:T(8,128)(2,1)} %get-tuple-element.30), channel_id=1, source_target_pairs={{0,24},{4,28},{8,16},{12,20},{16,8},{20,12},{24,0},{28,4},{1,25},{... | collective-permute-start | bytes 466952 | tf_op jit(solution)/shard_map/ppermute | solution.py:10
  21.0 9.3 %collective-permute-start.7 = (bf16[32,2432]{1,0:T(8,128)(2,1)}, bf16[32,2432]{1,0:T(8,128)(2,1)}, u32[]{:S(2)}, u32[]{:S(2)}) collective-permute-start(bf16[32,2432]{1,0:T(8,128)(2,1)} %get-tuple-element.30), channel_id=1, source_target_pairs={{0,16},{4,20},{8,24},{12,28},{16,0},{20,4},{24,8},{28,12},{1,17},{... | collective-permute-start | bytes 466952 | tf_op jit(solution)/shard_map/ppermute | solution.py:10
  22.3 8.0 %collective-permute-start.6 = (bf16[32,2432]{1,0:T(8,128)(2,1)}, bf16[32,2432]{1,0:T(8,128)(2,1)}, u32[]{:S(2)}, u32[]{:S(2)}) collective-permute-start(bf16[32,2432]{1,0:T(8,128)(2,1)} %get-tuple-element.30), channel_id=1, source_target_pairs={{0,8},{4,12},{8,0},{12,4},{16,24},{20,28},{24,16},{28,20},{1,9},{5... | collective-permute-start | bytes 466952 | tf_op jit(solution)/shard_map/ppermute | solution.py:10
  31.6 7.3 %collective-permute-start.9 = (bf16[128,2432]{1,0:T(8,128)(2,1)S(1)}, bf16[128,2432]{1,0:T(8,128)(2,1)S(1)}, u32[]{:S(2)}, u32[]{:S(2)}) collective-permute-start(bf16[128,2432]{1,0:T(8,128)(2,1)S(1)} %bitcast.153), channel_id=1, source_target_pairs={{0,4},{4,0},{8,12},{12,8},{16,20},{20,16},{24,28},{28,24},{1,5},{5... | collective-permute-start | bytes 1867784 | tf_op jit(solution)/shard_map/ppermute | solution.py:10
  52.4 12.5 %collective-permute-start.21 = (bf16[128,2304]{1,0:T(8,128)(2,1)}, bf16[128,2304]{1,0:T(8,128)(2,1)}, u32[]{:S(2)}, u32[]{:S(2)}) collective-permute-start(bf16[128,2304]{1,0:T(8,128)(2,1)} %slice.292), channel_id=1, source_target_pairs={{0,4},{4,0},{8,12},{12,8},{16,20},{20,16},{24,28},{28,24},{1,5},{5... | collective-permute-start | bytes 1769480 | tf_op jit(solution)/shard_map/ppermute | solution.py:10
  62.9 7.9 %collective-permute-start.10 = (bf16[128,2304]{1,0:T(8,128)(2,1)S(1)}, bf16[128,2304]{1,0:T(8,128)(2,1)S(1)}, u32[]{:S(2)}, u32[]{:S(2)}) collective-permute-start(bf16[128,2304]{1,0:T(8,128)(2,1)S(1)} %slice.293), channel_id=1, source_target_pairs={{0,4},{4,0},{8,12},{12,8},{16,20},{20,16},{24,28},{28,24},{1,5},{5... | collective-permute-start | bytes 1769480 | tf_op jit(solution)/shard_map/ppermute | solution.py:10
  67.3 8.5 %collective-permute-start.24 = (bf16[32,2304]{1,0:T(8,128)(2,1)S(1)}, bf16[32,2304]{1,0:T(8,128)(2,1)}, u32[]{:S(2)}, u32[]{:S(2)}) collective-permute-start(bf16[32,2304]{1,0:T(8,128)(2,1)S(1)} %get-tuple-element.24), channel_id=1, source_target_pairs={{0,24},{4,28},{8,16},{12,20},{16,8},{20,12},{24,0},{28,4},{1,25},{... | collective-permute-start | bytes 442376 | tf_op jit(solution)/shard_map/ppermute | solution.py:10
  69.0 9.2 %collective-permute-start.23 = (bf16[32,2304]{1,0:T(8,128)(2,1)S(1)}, bf16[32,2304]{1,0:T(8,128)(2,1)}, u32[]{:S(2)}, u32[]{:S(2)}) collective-permute-start(bf16[32,2304]{1,0:T(8,128)(2,1)S(1)} %get-tuple-element.25), channel_id=1, source_target_pairs={{0,16},{4,20},{8,24},{12,28},{16,0},{20,4},{24,8},{28,12},{1,17},{... | collective-permute-start | bytes 442376 | tf_op jit(solution)/shard_map/ppermute | solution.py:10
  70.3 7.9 %collective-permute-start.22 = (bf16[32,2304]{1,0:T(8,128)(2,1)S(1)}, bf16[32,2304]{1,0:T(8,128)(2,1)}, u32[]{:S(2)}, u32[]{:S(2)}) collective-permute-start(bf16[32,2304]{1,0:T(8,128)(2,1)S(1)} %get-tuple-element.23), channel_id=1, source_target_pairs={{0,8},{4,12},{8,0},{12,4},{16,24},{20,28},{24,16},{28,20},{1,9},{5... | collective-permute-start | bytes 442376 | tf_op jit(solution)/shard_map/ppermute | solution.py:10
  72.8 10.5 %collective-permute-start.13 = (bf16[32,2304]{1,0:T(8,128)(2,1)}, bf16[32,2304]{1,0:T(8,128)(2,1)}, u32[]{:S(2)}, u32[]{:S(2)}) collective-permute-start(bf16[32,2304]{1,0:T(8,128)(2,1)} %get-tuple-element.21), channel_id=1, source_target_pairs={{0,24},{4,28},{8,16},{12,20},{16,8},{20,12},{24,0},{28,4},{1,25},{... | collective-permute-start | bytes 442376 | tf_op jit(solution)/shard_map/ppermute | solution.py:10
  74.5 9.6 %collective-permute-start.12 = (bf16[32,2304]{1,0:T(8,128)(2,1)}, bf16[32,2304]{1,0:T(8,128)(2,1)}, u32[]{:S(2)}, u32[]{:S(2)}) collective-permute-start(bf16[32,2304]{1,0:T(8,128)(2,1)} %get-tuple-element.22), channel_id=1, source_target_pairs={{0,16},{4,20},{8,24},{12,28},{16,0},{20,4},{24,8},{28,12},{1,17},{... | collective-permute-start | bytes 442376 | tf_op jit(solution)/shard_map/ppermute | solution.py:10
  75.8 8.3 %collective-permute-start.11 = (bf16[32,2304]{1,0:T(8,128)(2,1)}, bf16[32,2304]{1,0:T(8,128)(2,1)}, u32[]{:S(2)}, u32[]{:S(2)}) collective-permute-start(bf16[32,2304]{1,0:T(8,128)(2,1)} %get-tuple-element.20), channel_id=1, source_target_pairs={{0,8},{4,12},{8,0},{12,4},{16,24},{20,28},{24,16},{28,20},{1,9},{5... | collective-permute-start | bytes 442376 | tf_op jit(solution)/shard_map/ppermute | solution.py:10
  82.9 6.2 %collective-permute-start.25 = (bf16[2,8,2304]{2,1,0:T(8,128)(2,1)}, bf16[2,8,2304]{2,1,0:T(8,128)(2,1)}, u32[]{:S(2)}, u32[]{:S(2)}) collective-permute-start(bf16[2,8,2304]{2,1,0:T(8,128)(2,1)} %fusion.52), channel_id=1, source_target_pairs={{0,1},{1,0},{2,3},{3,2},{4,5},{5,4},{6,7},{7,6},{8,9},{9,8},{10,11... | collective-permute-start | bytes 221192 | tf_op jit(solution)/shard_map/ppermute | solution.py:10
  87.2 28.3 %copy-start.1 = (bf16[2304,512]{1,0:T(8,128)(2,1)S(1)}, bf16[2304,512]{1,0:T(8,128)(2,1)}, u32[]{:S(2)}) copy-start(bf16[2304,512]{1,0:T(8,128)(2,1)} %param.22) | copy-start | bytes 7077892
  87.2 28.4 %copy-start.8 = (f32[512]{0:T(512)S(1)}, f32[512]{0:T(512)}, u32[]{:S(2)}) copy-start(f32[512]{0:T(512)} %param.23) | copy-start | bytes 6148
  88.3 4.5 %collective-permute-start.14 = (bf16[2,8,2304]{2,1,0:T(8,128)(2,1)S(1)}, bf16[2,8,2304]{2,1,0:T(8,128)(2,1)S(1)}, u32[]{:S(2)}, u32[]{:S(2)}) collective-permute-start(bf16[2,8,2304]{2,1,0:T(8,128)(2,1)S(1)} %fusion.51), channel_id=1, source_target_pairs={{0,1},{1,0},{2,3},{3,2},{4,5},{5,4},{6,7},{7,6},{8,9},{9,8},{10,11... | collective-permute-start | bytes 221192 | tf_op jit(solution)/shard_map/ppermute | solution.py:10
  90.1 7.0 %collective-permute-start.26 = (bf16[2,8,2304]{2,1,0:T(8,128)(2,1)S(1)}, bf16[2,8,2304]{2,1,0:T(8,128)(2,1)S(1)}, u32[]{:S(2)}, u32[]{:S(2)}) collective-permute-start(bf16[2,8,2304]{2,1,0:T(8,128)(2,1)S(1)} %fusion.41), channel_id=1, source_target_pairs={{0,2},{1,3},{2,0},{3,1},{4,6},{5,7},{6,4},{7,5},{8,10},{9,11},{10,... | collective-permute-start | bytes 221192 | tf_op jit(solution)/shard_map/ppermute | solution.py:10
  93.7 6.4 %collective-permute-start.15 = (bf16[2,8,2304]{2,1,0:T(8,128)(2,1)S(1)}, bf16[2,8,2304]{2,1,0:T(8,128)(2,1)S(1)}, u32[]{:S(2)}, u32[]{:S(2)}) collective-permute-start(bf16[2,8,2304]{2,1,0:T(8,128)(2,1)S(1)} %fusion.42), channel_id=1, source_target_pairs={{0,2},{1,3},{2,0},{3,1},{4,6},{5,7},{6,4},{7,5},{8,10},{9,11},{10,... | collective-permute-start | bytes 221192 | tf_op jit(solution)/shard_map/ppermute | solution.py:10
  97.1 5.1 %collective-permute-start.27 = (bf16[2,8,2304]{2,1,0:T(8,128)(2,1)S(1)}, bf16[2,8,2304]{2,1,0:T(8,128)(2,1)S(1)}, u32[]{:S(2)}, u32[]{:S(2)}) collective-permute-start(bf16[2,8,2304]{2,1,0:T(8,128)(2,1)S(1)} %add_convert_fusion), channel_id=1, source_target_pairs={{0,1},{1,0},{2,3},{3,2},{4,5},{5,4},{6,7},{7,6},{8,9},{9,8},{10,11... | collective-permute-start | bytes 221192 | tf_op jit(solution)/shard_map/ppermute | solution.py:10
  100.1 5.7 %collective-permute-start.16 = (bf16[2,8,2304]{2,1,0:T(8,128)(2,1)S(1)}, bf16[2,8,2304]{2,1,0:T(8,128)(2,1)S(1)}, u32[]{:S(2)}, u32[]{:S(2)}) collective-permute-start(bf16[2,8,2304]{2,1,0:T(8,128)(2,1)S(1)} %add_convert_fusion.1), channel_id=1, source_target_pairs={{0,1},{1,0},{2,3},{3,2},{4,5},{5,4},{6,7},{7,6},{8,9},{9,8},{10,11... | collective-permute-start | bytes 221192 | tf_op jit(solution)/shard_map/ppermute | solution.py:10
  102.2 7.7 %collective-permute-start.30 = (bf16[2,2,8,2304]{3,2,1,0:T(8,128)(2,1)S(1)}, bf16[2,2,8,2304]{3,2,1,0:T(8,128)(2,1)S(1)}, u32[]{:S(2)}, u32[]{:S(2)}) collective-permute-start(bf16[2,2,8,2304]{3,2,1,0:T(8,128)(2,1)S(1)} %get-tuple-element.34), channel_id=1, source_target_pairs={{0,24},{4,28},{8,16},{12,20},{16,8},{20,12},{24,0},{28,4},{1,25},{... | collective-permute-start | bytes 442376 | tf_op jit(solution)/shard_map/ppermute | solution.py:10
  103.7 8.5 %collective-permute-start.29 = (bf16[2,2,8,2304]{3,2,1,0:T(8,128)(2,1)S(1)}, bf16[2,2,8,2304]{3,2,1,0:T(8,128)(2,1)S(1)}, u32[]{:S(2)}, u32[]{:S(2)}) collective-permute-start(bf16[2,2,8,2304]{3,2,1,0:T(8,128)(2,1)S(1)} %get-tuple-element.34), channel_id=1, source_target_pairs={{0,16},{4,20},{8,24},{12,28},{16,0},{20,4},{24,8},{28,12},{1,17},{... | collective-permute-start | bytes 442376 | tf_op jit(solution)/shard_map/ppermute | solution.py:10
  105.0 7.2 %collective-permute-start.28 = (bf16[2,2,8,2304]{3,2,1,0:T(8,128)(2,1)S(1)}, bf16[2,2,8,2304]{3,2,1,0:T(8,128)(2,1)S(1)}, u32[]{:S(2)}, u32[]{:S(2)}) collective-permute-start(bf16[2,2,8,2304]{3,2,1,0:T(8,128)(2,1)S(1)} %get-tuple-element.34), channel_id=1, source_target_pairs={{0,8},{4,12},{8,0},{12,4},{16,24},{20,28},{24,16},{28,20},{1,9},{5... | collective-permute-start | bytes 442376 | tf_op jit(solution)/shard_map/ppermute | solution.py:10
  105.8 8.1 %collective-permute-start.19 = (bf16[2,2,8,2304]{3,2,1,0:T(8,128)(2,1)S(1)}, bf16[2,2,8,2304]{3,2,1,0:T(8,128)(2,1)S(1)}, u32[]{:S(2)}, u32[]{:S(2)}) collective-permute-start(bf16[2,2,8,2304]{3,2,1,0:T(8,128)(2,1)S(1)} %get-tuple-element.32), channel_id=1, source_target_pairs={{0,24},{4,28},{8,16},{12,20},{16,8},{20,12},{24,0},{28,4},{1,25},{... | collective-permute-start | bytes 442376 | tf_op jit(solution)/shard_map/ppermute | solution.py:10
  107.3 8.1 %collective-permute-start.18 = (bf16[2,2,8,2304]{3,2,1,0:T(8,128)(2,1)S(1)}, bf16[2,2,8,2304]{3,2,1,0:T(8,128)(2,1)S(1)}, u32[]{:S(2)}, u32[]{:S(2)}) collective-permute-start(bf16[2,2,8,2304]{3,2,1,0:T(8,128)(2,1)S(1)} %get-tuple-element.32), channel_id=1, source_target_pairs={{0,16},{4,20},{8,24},{12,28},{16,0},{20,4},{24,8},{28,12},{1,17},{... | collective-permute-start | bytes 442376 | tf_op jit(solution)/shard_map/ppermute | solution.py:10
  109.9 5.5 %collective-permute-start.17 = (bf16[2,2,8,2304]{3,2,1,0:T(8,128)(2,1)S(1)}, bf16[2,2,8,2304]{3,2,1,0:T(8,128)(2,1)S(1)}, u32[]{:S(2)}, u32[]{:S(2)}) collective-permute-start(bf16[2,2,8,2304]{3,2,1,0:T(8,128)(2,1)S(1)} %get-tuple-element.32), channel_id=1, source_target_pairs={{0,8},{4,12},{8,0},{12,4},{16,24},{20,28},{24,16},{28,20},{1,9},{5... | collective-permute-start | bytes 442376 | tf_op jit(solution)/shard_map/ppermute | solution.py:10
  112.3 10.5 %collective-permute-start.31 = (bf16[128,2304]{1,0:T(8,128)(2,1)S(1)}, bf16[128,2304]{1,0:T(8,128)(2,1)S(1)}, u32[]{:S(2)}, u32[]{:S(2)}) collective-permute-start(bf16[128,2304]{1,0:T(8,128)(2,1)S(1)} %bitcast.157), channel_id=1, source_target_pairs={{0,4},{4,0},{8,12},{12,8},{16,20},{20,16},{24,28},{28,24},{1,5},{5... | collective-permute-start | bytes 1769480 | tf_op jit(solution)/shard_map/ppermute | solution.py:10
  115.4 2.7 %collective-permute-start.20 = (bf16[128,2304]{1,0:T(8,128)(2,1)S(1)}, bf16[128,2304]{1,0:T(8,128)(2,1)S(1)}, u32[]{:S(2)}, u32[]{:S(2)}) collective-permute-start(bf16[128,2304]{1,0:T(8,128)(2,1)S(1)} %bitcast.159), channel_id=1, source_target_pairs={{0,4},{4,0},{8,12},{12,8},{16,20},{20,16},{24,28},{28,24},{1,5},{5... | collective-permute-start | bytes 1769480 | tf_op jit(solution)/shard_map/ppermute | solution.py:10
  116.5 2.2 %collective-permute-start.32 = (bf16[128,2304]{1,0:T(8,128)(2,1)S(1)}, bf16[128,2304]{1,0:T(8,128)(2,1)S(1)}, u32[]{:S(2)}, u32[]{:S(2)}) collective-permute-start(bf16[128,2304]{1,0:T(8,128)(2,1)S(1)} %convolution_convert_fusion.1), channel_id=1, source_target_pairs={{0,4},{4,0},{8,12},{12,8},{16,20},{20,16},{24,28},{28,24},{1,5},{5... | collective-permute-start | bytes 1769480 | tf_op jit(solution)/shard_map/ppermute | solution.py:10
  118.0 5.2 %collective-permute-start.38 = (bf16[128,2304]{1,0:T(8,128)(2,1)S(1)}, bf16[128,2304]{1,0:T(8,128)(2,1)S(1)}, u32[]{:S(2)}, u32[]{:S(2)}) collective-permute-start(bf16[128,2304]{1,0:T(8,128)(2,1)S(1)} %convolution_convert_fusion), channel_id=1, source_target_pairs={{0,4},{4,0},{8,12},{12,8},{16,20},{20,16},{24,28},{28,24},{1,5},{5... | collective-permute-start | bytes 1769480 | tf_op jit(solution)/shard_map/ppermute | solution.py:10
  119.2 8.1 %collective-permute-start.35 = (bf16[32,2304]{1,0:T(8,128)(2,1)S(1)}, bf16[32,2304]{1,0:T(8,128)(2,1)S(1)}, u32[]{:S(2)}, u32[]{:S(2)}) collective-permute-start(bf16[32,2304]{1,0:T(8,128)(2,1)S(1)} %get-tuple-element.15), channel_id=1, source_target_pairs={{0,24},{4,28},{8,16},{12,20},{16,8},{20,12},{24,0},{28,4},{1,25},{... | collective-permute-start | bytes 442376 | tf_op jit(solution)/shard_map/ppermute | solution.py:10
  120.8 9.3 %collective-permute-start.34 = (bf16[32,2304]{1,0:T(8,128)(2,1)S(1)}, bf16[32,2304]{1,0:T(8,128)(2,1)S(1)}, u32[]{:S(2)}, u32[]{:S(2)}) collective-permute-start(bf16[32,2304]{1,0:T(8,128)(2,1)S(1)} %get-tuple-element.16), channel_id=1, source_target_pairs={{0,16},{4,20},{8,24},{12,28},{16,0},{20,4},{24,8},{28,12},{1,17},{... | collective-permute-start | bytes 442376 | tf_op jit(solution)/shard_map/ppermute | solution.py:10
  122.1 8.0 %collective-permute-start.33 = (bf16[32,2304]{1,0:T(8,128)(2,1)S(1)}, bf16[32,2304]{1,0:T(8,128)(2,1)S(1)}, u32[]{:S(2)}, u32[]{:S(2)}) collective-permute-start(bf16[32,2304]{1,0:T(8,128)(2,1)S(1)} %get-tuple-element.14), channel_id=1, source_target_pairs={{0,8},{4,12},{8,0},{12,4},{16,24},{20,28},{24,16},{28,20},{1,9},{5... | collective-permute-start | bytes 442376 | tf_op jit(solution)/shard_map/ppermute | solution.py:10
  123.8 9.4 %collective-permute-start.41 = (bf16[32,2304]{1,0:T(8,128)(2,1)S(1)}, bf16[32,2304]{1,0:T(8,128)(2,1)S(1)}, u32[]{:S(2)}, u32[]{:S(2)}) collective-permute-start(bf16[32,2304]{1,0:T(8,128)(2,1)S(1)} %get-tuple-element.18), channel_id=1, source_target_pairs={{0,24},{4,28},{8,16},{12,20},{16,8},{20,12},{24,0},{28,4},{1,25},{... | collective-permute-start | bytes 442376 | tf_op jit(solution)/shard_map/ppermute | solution.py:10
  125.3 10.5 %collective-permute-start.40 = (bf16[32,2304]{1,0:T(8,128)(2,1)S(1)}, bf16[32,2304]{1,0:T(8,128)(2,1)S(1)}, u32[]{:S(2)}, u32[]{:S(2)}) collective-permute-start(bf16[32,2304]{1,0:T(8,128)(2,1)S(1)} %get-tuple-element.19), channel_id=1, source_target_pairs={{0,16},{4,20},{8,24},{12,28},{16,0},{20,4},{24,8},{28,12},{1,17},{... | collective-permute-start | bytes 442376 | tf_op jit(solution)/shard_map/ppermute | solution.py:10
  127.3 8.6 %collective-permute-start.39 = (bf16[32,2304]{1,0:T(8,128)(2,1)S(1)}, bf16[32,2304]{1,0:T(8,128)(2,1)S(1)}, u32[]{:S(2)}, u32[]{:S(2)}) collective-permute-start(bf16[32,2304]{1,0:T(8,128)(2,1)S(1)} %get-tuple-element.17), channel_id=1, source_target_pairs={{0,8},{4,12},{8,0},{12,4},{16,24},{20,28},{24,16},{28,20},{1,9},{5... | collective-permute-start | bytes 442376 | tf_op jit(solution)/shard_map/ppermute | solution.py:10
  130.2 6.8 %collective-permute-start.36 = (bf16[2,8,2304]{2,1,0:T(8,128)(2,1)S(1)}, bf16[2,8,2304]{2,1,0:T(8,128)(2,1)S(1)}, u32[]{:S(2)}, u32[]{:S(2)}) collective-permute-start(bf16[2,8,2304]{2,1,0:T(8,128)(2,1)S(1)} %fusion.53), channel_id=1, source_target_pairs={{0,1},{1,0},{2,3},{3,2},{4,5},{5,4},{6,7},{7,6},{8,9},{9,8},{10,11... | collective-permute-start | bytes 221192 | tf_op jit(solution)/shard_map/ppermute | solution.py:10
  136.0 4.4 %collective-permute-start.42 = (bf16[2,8,2304]{2,1,0:T(8,128)(2,1)S(1)}, bf16[2,8,2304]{2,1,0:T(8,128)(2,1)S(1)}, u32[]{:S(2)}, u32[]{:S(2)}) collective-permute-start(bf16[2,8,2304]{2,1,0:T(8,128)(2,1)S(1)} %fusion.54), channel_id=1, source_target_pairs={{0,1},{1,0},{2,3},{3,2},{4,5},{5,4},{6,7},{7,6},{8,9},{9,8},{10,11... | collective-permute-start | bytes 221192 | tf_op jit(solution)/shard_map/ppermute | solution.py:10
  137.0 6.6 %collective-permute-start.37 = (bf16[8,2304]{1,0:T(8,128)(2,1)S(1)}, bf16[8,2304]{1,0:T(8,128)(2,1)S(1)}, u32[]{:S(2)}, u32[]{:S(2)}) collective-permute-start(bf16[8,2304]{1,0:T(8,128)(2,1)S(1)} %fusion.59), channel_id=1, source_target_pairs={{0,2},{1,3},{2,0},{3,1},{4,6},{5,7},{6,4},{7,5},{8,10},{9,11},{10,... | collective-permute-start | bytes 110600 | tf_op jit(solution)/shard_map/ppermute | solution.py:10
  140.4 5.1 %collective-permute-start.43 = (bf16[8,2304]{1,0:T(8,128)(2,1)S(1)}, bf16[8,2304]{1,0:T(8,128)(2,1)S(1)}, u32[]{:S(2)}, u32[]{:S(2)}) collective-permute-start(bf16[8,2304]{1,0:T(8,128)(2,1)S(1)} %fusion.60), channel_id=1, source_target_pairs={{0,2},{1,3},{2,0},{3,1},{4,6},{5,7},{6,4},{7,5},{8,10},{9,11},{10,... | collective-permute-start | bytes 110600 | tf_op jit(solution)/shard_map/ppermute | solution.py:10
  (9 other events, 65.1 us)

commit v5 on v4

--- a/solution.py
+++ b/solution.py
@@ -1,9 +1,15 @@
+import functools
+
 import jax
 import jax.numpy as jnp
 from jax import lax
+from jax.experimental import pallas as pl
+from jax.experimental.pallas import tpu as pltpu
 from jax.sharding import PartitionSpec as P
 
 CHUNKS = 2
+LANES = 128
+VMEM = 24 * 1024 * 1024
 
 
 def swap(value, axis, r):
@@ -39,6 +45,163 @@
 def reduce_pairs(value):
     arrived = [swap(half(value[p]), "expert", 2 * p) for p in range(1, value.shape[0])]
     return value[0] + sum(full(a) for a in arrived)
+
+
+def hidden_kernel(count, *refs):
+    pieces, (gate, up, out, rows) = refs[:count], refs[count:]
+    size = pieces[0].shape[0]
+
+    @pl.when((pl.program_id(0) == 0) & (pl.program_id(1) == 0))
+    def _():
+        for i, piece in enumerate(pieces):
+            rows[i * size : (i + 1) * size, :] = piece[...]
+
+    value = dot(rows[...], gate[...])
+    out[...] = half(value / (1.0 + jnp.exp(-value)) * dot(rows[...], up[...]))
+
+
+def run_hidden(pieces, gate, up):
+    count, (size, width) = len(pieces), pieces[0].shape
+    experts, _, units = gate.shape
+    tile = min(256, units)
+    weight = pl.BlockSpec((None, width, tile), lambda e, j: (e, 0, j))
+    return pl.pallas_call(
+        functools.partial(hidden_kernel, count),
+        grid=(experts, units // tile),
+        in_specs=[pl.BlockSpec((size, width), lambda e, j: (0, 0))] * count + [weight] * 2,
+        out_specs=pl.BlockSpec((None, count * size, tile), lambda e, j: (e, 0, j)),
+        out_shape=jax.ShapeDtypeStruct((experts, count * size, units), jnp.bfloat16),
+        scratch_shapes=[pltpu.VMEM((count * size, width), jnp.bfloat16)],
+        compiler_params=pltpu.CompilerParams(vmem_limit_bytes=VMEM),
+        cost_estimate=pl.CostEstimate(
+            flops=4 * experts * count * size * width * units,
+            bytes_accessed=4 * experts * width * units,
+            transcendentals=experts * count * size * units,
+        ),
+    )(*pieces, gate, up)
+
+
+def down_kernel(top, experts, parts, me, hidden, down, table, *refs):
+    e = pl.program_id(1)
+    entries = full(table[...])
+    lane = lax.broadcasted_iota(jnp.int32, entries.shape, 1)
+    expert = (me[0] * experts + e).astype(jnp.float32)
+    chosen = jnp.where((entries == expert) & (lane < top), 1.0, 0.0)
+    chosen = pltpu.roll(chosen, top, 1) + pltpu.roll(chosen, 2 * top, 1)
+    scale = jnp.sum(chosen * entries, axis=1, keepdims=True)
+    value = dot(hidden[...], down[...]) * scale
+    if parts is None:
+        outs, total = refs[:1], refs[1]
+    else:
+        arrived, outs, total = refs[0], refs[1:-1], refs[-1]
+
+    @pl.when(e == 0)
+    def _():
+        total[...] = value if parts is None else value + full(arrived[...])
+
+    @pl.when(e > 0)
+    def _():
+        total[...] += value
+
+    @pl.when(e == experts - 1)
+    def _():
+        if parts is None:
+            outs[0][...] = half(total[...])
+        else:
+            pairs, feats, step = parts
+            split = total[...].reshape(pairs, feats, CHUNKS, step, -1)
+            for i, out in enumerate(outs):
+                block = split[i % pairs, :, i // pairs].reshape(feats * step, -1)
+                out[...] = block.astype(out.dtype)
+
+
+def run_down(hidden, down, table, me, top, arrived=None, parts=None):
+    experts, rows, units = hidden.shape
+    width = down.shape[2]
+    tile = max(t for t in range(128, 769, 128) if width % t == 0)
+    whole = pl.BlockSpec((rows, tile), lambda j, e: (0, j))
+    in_specs = [
+        pl.BlockSpec(memory_space=pltpu.SMEM),
+        pl.BlockSpec((None, rows, units), lambda j, e: (e, 0, 0)),
+        pl.BlockSpec((None, units, tile), lambda j, e: (e, 0, j)),
+        pl.BlockSpec((rows, LANES), lambda j, e: (0, 0)),
+    ]
+    operands = [me.reshape(1), hidden, down, table]
+    if arrived is None:
+        out_specs = whole
+        out_shape = jax.ShapeDtypeStruct((rows, width), jnp.bfloat16)
+    else:
+        in_specs.append(whole)
+        operands.append(arrived)
+        pairs, feats, step = parts
+        out_specs = [pl.BlockSpec((feats * step, tile), lambda j, e: (0, j))] * (pairs * CHUNKS)
+        out_shape = [
+            jax.ShapeDtypeStruct((feats * step, width), jnp.bfloat16 if i % pairs else jnp.float32)
+            for i in range(pairs * CHUNKS)
+        ]
+    return pl.pallas_call(
+        functools.partial(down_kernel, top, experts, parts),
+        grid=(width // tile, experts),
+        in_specs=in_specs,
+        out_specs=out_specs,
+        out_shape=out_shape,
+        scratch_shapes=[pltpu.VMEM((rows, tile), jnp.float32)],
+        compiler_params=pltpu.CompilerParams(vmem_limit_bytes=VMEM),
+        cost_estimate=pl.CostEstimate(
+            flops=2 * experts * rows * width * units,
+            bytes_accessed=2 * experts * width * units,
+            transcendentals=0,
+        ),
+    )(*operands)
+
+
+def shared_kernel(feats, x, gate, up, down, *outs):
+    value = dot(x[...], gate[...])
+    hidden = half(value / (1.0 + jnp.exp(-value)) * dot(x[...], up[...]))
+    value = dot(hidden, down[...])
+    rows, width = value.shape
+    value = value.reshape(feats, CHUNKS, rows // feats // CHUNKS, width)
+    for c, out in enumerate(outs):
+        out[...] = value[:, c].reshape(rows // CHUNKS, width)
+
+
+def run_shared(x, gate, up, down, feats):
+    rows, width = x.shape
+    return pl.pallas_call(
+        functools.partial(shared_kernel, feats),
+        out_shape=[jax.ShapeDtypeStruct((rows // CHUNKS, width), jnp.float32)] * CHUNKS,
+        compiler_params=pltpu.CompilerParams(vmem_limit_bytes=VMEM),
+        cost_estimate=pl.CostEstimate(
+            flops=6 * rows * gate.size, bytes_accessed=6 * gate.size, transcendentals=0
+        ),
+    )(x, gate, up, down)
+
+
+def sum_kernel(step, place, *refs):
+    parts, (kept, sent) = refs[:-2], refs[-2:]
+    total = sum(full(part[...]) for part in parts)
+    rows, width = total.shape
+    total = total.reshape(rows // step // 2, 2, step, width)
+    low, high = total[:, 0].reshape(-1, width), total[:, 1].reshape(-1, width)
+    kept[...] = jnp.where(place[0] == 0, low, high)
+    sent[...] = half(jnp.where(place[0] == 0, high, low))
+
+
+def run_sum(parts, place, step):
+    rows, width = parts[0].shape
+    vmem = pl.BlockSpec(memory_space=pltpu.VMEM)
+    return pl.pallas_call(
+        functools.partial(sum_kernel, step),
+        in_specs=[pl.BlockSpec(memory_space=pltpu.SMEM)] + [vmem] * len(parts),
+        out_shape=[
+            jax.ShapeDtypeStruct((rows // 2, width), jnp.float32),
+            jax.ShapeDtypeStruct((rows // 2, width), jnp.bfloat16),
+        ],
+        compiler_params=pltpu.CompilerParams(vmem_limit_bytes=VMEM),
+        cost_estimate=pl.CostEstimate(
+            flops=rows * width * len(parts), bytes_accessed=2 * rows * width, transcendentals=0
+        ),
+    )(place.reshape(1), *parts)
 
 
 def shards(
@@ -61,7 +224,6 @@
     feats = lax.axis_size("feat")
     pairs = lax.axis_size("expert") // 2
     devices = 2 * pairs * feats
-    local_experts = expert_gate.shape[0]
     me = lax.axis_index(("expert", "feat"))
     my_feat = lax.axis_index("feat")
     feat_bits = bits_of(feats)
@@ -71,61 +233,41 @@
     high = half(gate_weights)
     low = half(gate_weights - full(high))
     row = jnp.concatenate([half(expert_ids), high, low], axis=1)
+    row = jnp.pad(row, ((0, 0), (0, LANES - 3 * top)))
     mine = jnp.arange(feats, dtype=jnp.int32)[:, None, None] == my_feat
-    table = jnp.where(mine, row[None], jnp.zeros_like(row)[None])
-    table = table.reshape(feats, CHUNKS, step, 3 * top).transpose(0, 2, 1, 3)
-    lanes = -(-CHUNKS * 3 * top // 128) * 128
-    table = table.reshape(feats * step, CHUNKS * 3 * top)
-    table = jnp.pad(table, ((0, 0), (0, lanes - table.shape[1])))
+    table = jnp.where(mine, row[None], jnp.zeros_like(row)[None]).reshape(-1, LANES)
     for bit in feat_bits:
         table = table + swap(table, "feat", bit)
-
-    parts = tokens.reshape(feats, CHUNKS, step, width)
-    parts = [parts[:, c].reshape(feats * step, width) for c in range(CHUNKS)]
-    parts[-1] = jnp.concatenate([parts[-1], table], axis=1)
-    both = []
-    for part in parts:
-        near = gather_pairs(part).reshape(rows, -1)
-        both.append(jnp.concatenate([near, swap(near, "expert", 1)], axis=0))
-    tables = both[-1][:, width:]
-    both[-1] = both[-1][:, :width]
-
-    def scales(c):
-        ids = tables[:, c * 3 * top :][:, :top].astype(jnp.int32)
-        weights = full(tables[:, (c * 3 + 1) * top :][:, :top])
-        weights = weights + full(tables[:, (c * 3 + 2) * top :][:, :top])
-        return [
-            jnp.sum(jnp.where(ids == me * local_experts + j, weights, 0.0), axis=1)[:, None]
-            for j in range(local_experts)
-        ]
-
-    def swiglu(x, gate, up):
-        return half(jax.nn.silu(dot(x, gate)) * dot(x, up))
-
-    def run_experts(x, scale):
-        out = 0.0
-        for j in range(local_experts):
-            hidden = swiglu(x, expert_gate[j], expert_up[j])
-            out = out + dot(hidden, expert_down[j]) * scale[j]
-        return out
+    for bit in bits_of(pairs):
+        table = jnp.concatenate([table, swap(table, "expert", 2 * bit)], axis=0)
+    table_far = swap(table, "expert", 1)
+
+    near = [tokens] + [swap(tokens, "expert", 2 * p) for p in range(1, pairs)]
+    far = [swap(piece, "expert", 1) for piece in near]
+    shared_out = run_shared(far[0], shared_gate, shared_up, shared_down, feats)
+
+    hidden_near = run_hidden(near, expert_gate, expert_up)
+    out_near = run_down(hidden_near, expert_down, table, me, top)
+    arrived = swap(out_near, "expert", 1)
+    hidden_far = run_hidden(far, expert_gate, expert_up)
+    blocks = run_down(hidden_far, expert_down, table_far, me, top, arrived, (pairs, feats, step))
 
     near_rows = []
+    place = [(my_feat // bit) % 2 for bit in feat_bits]
     for c in range(CHUNKS):
-        out = run_experts(both[c], scales(c))
-        shared_rows = both[c][rows : rows + feats * step]
-        shared_out = dot(swiglu(shared_rows, shared_gate, shared_up), shared_down)
-        total = out[rows:] + full(swap(half(out[:rows]), "expert", 1))
-        total = reduce_pairs(total.reshape(pairs, feats * step, width)) + shared_out
-        total = total.reshape((2,) * len(feat_bits) + (step, width))
-        place = [(my_feat // bit) % 2 for bit in feat_bits]
-        for i, bit in enumerate(feat_bits[:-1]):
-            dim = len(feat_bits) - 1 - i
-            arrived = swap(half(take(total, 1 - place[i], dim)), "feat", bit)
-            total = take(total, place[i], dim) + full(arrived)
+        mine = blocks[c * pairs : (c + 1) * pairs]
+        arrived = [swap(mine[p], "expert", 2 * p) for p in range(1, pairs)]
+        total, sent = run_sum([mine[0], shared_out[c]] + arrived, place[0], step)
+        total = total + full(swap(sent, "feat", feat_bits[0]))
+        total = total.reshape((2,) * (len(feat_bits) - 1) + (step, width))
+        for i, bit in enumerate(feat_bits[1:-1]):
+            dim = len(feat_bits) - 2 - i
+            arrived = swap(half(take(total, 1 - place[i + 1], dim)), "feat", bit)
+            total = take(total, place[i + 1], dim) + full(arrived)
         total = half(total)
         moe_out = half(full(total) + full(swap(total, "feat", feat_bits[-1])))
-        for i, bit in reversed(list(enumerate(feat_bits[:-1]))):
-            moe_out = jnp.stack([moe_out, swap(moe_out, "feat", bit)], axis=1)
+        for bit in feat_bits[-2::-1]:
+            moe_out = jnp.stack([moe_out, swap(moe_out, "feat", bit)], axis=moe_out.ndim - 2)
         near_rows.append(gather_pairs(moe_out).reshape(rows, width))
 
     def encode(x):

time: 147 us -> 128 us (0.87)
  matrix products: 38.6 us -> 3.85 us
  Pallas kernels: 0 us -> 17.5 us
  other arithmetic: 12.2 us -> 2.97 us
  local copies, waits for them, and re-layouts: 9.52 us -> 15.1 us
  waiting for transfers between devices: 30.6 us -> 34.9 us
  starting transfers between devices: 54 us -> 52.3 us
    dot_general x16 -> x8, matrix products: 38.6 us -> 3.85 us  [dot(): return jnp.dot(a, b, preferred_element_type=jnp.float32)]
    pallas_call x0 -> x7, Pallas kernels: none -> 17.5 us  [the longest x2 9.22 us: run_hidden(): pl.pallas_call(functools.partial(hidden_kernel, count), grid=(experts, un...]
    unnamed x57 -> x84, local copies, waits for them, and re-layouts: 0.39 us -> 14.8 us
    ppermute x44 -> x45, waiting for transfers between devices: 30.6 us -> 34.9 us  [swap(): lax.ppermute(value, axis, [(i, i ^ r) for i in range(lax.axis_size(axis))])]
    slice x2 -> x0, local copies, waits for them, and re-layouts: 3.63 us -> none  [shards(): total = out[rows:] + full(swap(half(out[:rows]), 'expert', 1))]
    another operation x2, other arithmetic: 3.54 us -> 0.06 us  [shards(): jnp.stack([moe_out, swap(moe_out, 'feat', bit)], axis=moe_out.ndim - 2)]
    another operation x7 -> x4, other arithmetic: 3.1 us -> 0.19 us  [gather_pairs(): jnp.stack([value] + [swap(value, 'expert', 2 * p) for p in range(1, pairs)])]
    convert_element_type x6 -> x4, local copies, waits for them, and re-layouts: 2.67 us -> 0.05 us  [half(): return value.astype(jnp.bfloat16)]
  transfers between devices with their start and end apart: 44 -> 45, of which waited for: 20 -> 25; matrix products, arithmetic and copies ran while one was open for 29% -> 4% of each run, Pallas kernels for 0% -> 6%
where the time goes in v5:
time: 128 us
  starting transfers between devices  52.3 us (41%)
  waiting for transfers between devices  34.9 us (27%)
  Pallas kernels  17.5 us (14%)
  local copies, waits for them, and re-layouts  15.1 us (12%)
  matrix products  3.85 us (3%)
  other arithmetic  2.97 us (2%)
  between operations  1.38 us (1%)
    ppermute x45, starting transfers between devices, swap(): lax.ppermute(value, axis, [(i, i ^ r) for i in range(lax.axis_size(axis))])  52.3 us
    ppermute x45, waiting for transfers between devices, swap(): lax.ppermute(value, axis, [(i, i ^ r) for i in range(lax.axis_size(axis))])  34.9 us
    unnamed x84, local copies, waits for them, and re-layouts  14.8 us
    pallas_call x2, Pallas kernels, run_hidden(): pl.pallas_call(functools.partial(hidden_kernel, count), grid=(experts, un...  9.22 us
    pallas_call x2, Pallas kernels, run_down(): pl.pallas_call(functools.partial(down_kernel, top, experts, parts), grid=...  5.26 us
    dot_general x8, matrix products, dot(): return jnp.dot(a, b, preferred_element_type=jnp.float32)  3.85 us
  transfers between devices with their start and end apart: 45, of which 25 were waited for; matrix products, arithmetic and copies ran while one was open for 4% of the time, Pallas kernels for 6%

profile of v5, /device:TPU:0, one launch (start us, length us, event | category | flops | bytes accessed | tf_op | source)
XLA Modules:
  0.0 127.9 jit_solution(1186723674544925126)
XLA Ops:
  2.5 3.1 %collective-permute-start.7 = (bf16[64,128]{1,0:T(8,128)(2,1)S(1)}, bf16[64,128]{1,0:T(8,128)(2,1)S(1)}, u32[]{:S(2)}, u32[]{:S(2)}) collective-permute-start(bf16[64,128]{1,0:T(8,128)(2,1)S(1)} %bitcast_select_fusion), channel_id=1, source_target_pairs={{0,1},{1,0},{2,3},{3,2},{4,5},{5,4},{6,7},{7,6},{8,9},{9,8},{10,11... | collective-permute-start | bytes 49160 | tf_op jit(solution)/shard_map/ppermute | solution.py:16
  5.6 1.5 %collective-permute-start.1 = (bf16[64,2304]{1,0:T(8,128)(2,1)}, bf16[64,2304]{1,0:T(8,128)(2,1)S(1)}, u32[]{:S(2)}, u32[]{:S(2)}) collective-permute-start(bf16[64,2304]{1,0:T(8,128)(2,1)} %refs_0_.1), channel_id=1, source_target_pairs={{0,8},{4,12},{8,0},{12,4},{16,24},{20,28},{24,16},{28,20},{1,9},{5... | collective-permute-start | bytes 884744 | tf_op jit(solution)/shard_map/ppermute | solution.py:16
  7.1 1.5 %collective-permute-start.3 = (bf16[64,2304]{1,0:T(8,128)(2,1)}, bf16[64,2304]{1,0:T(8,128)(2,1)S(1)}, u32[]{:S(2)}, u32[]{:S(2)}) collective-permute-start(bf16[64,2304]{1,0:T(8,128)(2,1)} %refs_0_.1), channel_id=1, source_target_pairs={{0,16},{4,20},{8,24},{12,28},{16,0},{20,4},{24,8},{28,12},{1,17},{... | collective-permute-start | bytes 884744 | tf_op jit(solution)/shard_map/ppermute | solution.py:16
  9.2 2.6 %collective-permute-start.8 = (bf16[64,128]{1,0:T(8,128)(2,1)S(1)}, bf16[64,128]{1,0:T(8,128)(2,1)S(1)}, u32[]{:S(2)}, u32[]{:S(2)}) collective-permute-start(bf16[64,128]{1,0:T(8,128)(2,1)S(1)} %fusion.18), channel_id=1, source_target_pairs={{0,2},{1,3},{2,0},{3,1},{4,6},{5,7},{6,4},{7,5},{8,10},{9,11},{10,... | collective-permute-start | bytes 49160 | tf_op jit(solution)/shard_map/ppermute | solution.py:16
  11.8 2.0 %collective-permute-done.8 = bf16[64,128]{1,0:T(8,128)(2,1)S(1)} collective-permute-done((bf16[64,128]{1,0:T(8,128)(2,1)S(1)}, bf16[64,128]{1,0:T(8,128)(2,1)S(1)}, u32[]{:S(2)}, u32[]{:S(2)}) %collective-permute-start.8) | collective-permute-done | bytes 16416 | tf_op jit(solution)/shard_map/ppermute | solution.py:16
  13.9 1.6 %collective-permute-start.9 = (bf16[64,128]{1,0:T(8,128)(2,1)S(1)}, bf16[64,128]{1,0:T(8,128)(2,1)S(1)}, u32[]{:S(2)}, u32[]{:S(2)}) collective-permute-start(bf16[64,128]{1,0:T(8,128)(2,1)S(1)} %add.225), channel_id=1, source_target_pairs={{0,8},{4,12},{8,0},{12,4},{16,24},{20,28},{24,16},{28,20},{1,9},{5... | collective-permute-start | bytes 49160 | tf_op jit(solution)/shard_map/ppermute | solution.py:16
  15.5 5.5 %collective-permute-done.9 = bf16[64,128]{1,0:T(8,128)(2,1)S(1)} collective-permute-done((bf16[64,128]{1,0:T(8,128)(2,1)S(1)}, bf16[64,128]{1,0:T(8,128)(2,1)S(1)}, u32[]{:S(2)}, u32[]{:S(2)}) %collective-permute-start.9) | collective-permute-done | bytes 16416 | tf_op jit(solution)/shard_map/ppermute | solution.py:16
  21.0 1.5 %collective-permute-start.10 = (bf16[128,128]{1,0:T(8,128)(2,1)S(1)}, bf16[128,128]{1,0:T(8,128)(2,1)S(1)}, u32[]{:S(2)}, u32[]{:S(2)}) collective-permute-start(bf16[128,128]{1,0:T(8,128)(2,1)S(1)} %pad_maximum_fusion.6), channel_id=1, source_target_pairs={{0,16},{4,20},{8,24},{12,28},{16,0},{20,4},{24,8},{28,12},{1,17},{... | collective-permute-start | bytes 98312 | tf_op jit(solution)/shard_map/ppermute | solution.py:16
  22.5 2.4 %collective-permute-done.10 = bf16[128,128]{1,0:T(8,128)(2,1)S(1)} collective-permute-done((bf16[128,128]{1,0:T(8,128)(2,1)S(1)}, bf16[128,128]{1,0:T(8,128)(2,1)S(1)}, u32[]{:S(2)}, u32[]{:S(2)}) %collective-permute-start.10) | collective-permute-done | bytes 32800 | tf_op jit(solution)/shard_map/ppermute | solution.py:16
  25.0 2.5 %copy-done.1 = bf16[1,2304,1024]{2,1,0:T(8,128)(2,1)S(1)} copy-done((bf16[1,2304,1024]{2,1,0:T(8,128)(2,1)S(1)}, bf16[1,2304,1024]{2,1,0:T(8,128)(2,1)}, u32[]{:S(2)}) %copy-start.1) | copy-done | bytes 4718616
  27.5 2.6 %copy-done.3 = bf16[1,2304,1024]{2,1,0:T(8,128)(2,1)S(1)} copy-done((bf16[1,2304,1024]{2,1,0:T(8,128)(2,1)S(1)}, bf16[1,2304,1024]{2,1,0:T(8,128)(2,1)}, u32[]{:S(2)}) %copy-start.3) | copy-done | bytes 4718616
  31.0 4.6 %shard_map.141.hidden = bf16[1,256,1024]{2,1,0:T(8,128)(2,1)S(1)} custom-call(bf16[64,2304]{1,0:T(8,128)(2,1)S(1)} %copy-done.10, bf16[64,2304]{1,0:T(8,128)(2,1)S(1)} %collective-permute-done.1.refs_1_, bf16[64,2304]{1,0:T(8,128)(2,1)S(1)} %collective-permute-done.3.refs_2_, bf16[64,2304]{1,0:T(8,128)(2,1)S(1)} %collective-permute-done.5.refs_3_, ...), custom_call_target="tpu_custom_call" | custom-call | flops 2415919104 | bytes 9437184 | tf_op jit(solution)/shard_map/pallas_call | solution.py:68
  35.7 2.2 %shard_map.142 = bf16[256,2304]{1,0:T(8,128)(2,1)S(1)} custom-call(s32[1]{0:T(128)} %bitcast.1.me, bf16[1,256,1024]{2,1,0:T(8,128)(2,1)S(1)} %shard_map.141.hidden, bf16[1,1024,2304]{2,1,0:T(8,128)(2,1)S(1)} %bitcast.99, bf16[256,128]{1,0:T(8,128)(2,1)S(1)} %pad_maximum_fusion.5.table), custom_call_target="tpu_custom_call" | custom-call | flops 1207959552 | bytes 4718592 | tf_op jit(solution)/shard_map/pallas_call | solution.py:142
  39.1 2.2 %collective-permute-done.refs_0_.x = bf16[64,2304]{1,0:T(8,128)(2,1)S(1)} collective-permute-done((bf16[64,2304]{1,0:T(8,128)(2,1)S(1)}, bf16[64,2304]{1,0:T(8,128)(2,1)S(1)}, u32[]{:S(2)}, u32[]{:S(2)}) %collective-permute-start) | collective-permute-done | bytes 294944 | tf_op jit(solution)/shard_map/ppermute | solution.py:16
  42.5 4.6 %shard_map.140.hidden = bf16[1,256,1024]{2,1,0:T(8,128)(2,1)S(1)} custom-call(bf16[64,2304]{1,0:T(8,128)(2,1)S(1)} %collective-permute-done.refs_0_.x, bf16[64,2304]{1,0:T(8,128)(2,1)S(1)} %collective-permute-done.2.refs_1_, bf16[64,2304]{1,0:T(8,128)(2,1)S(1)} %collective-permute-done.4.refs_2_, bf16[64,2304]{1,0:T(8,128)(2,1)S(1)} %collective-permute-done.6.refs_3_, ...), custom_call_target="tpu_custom_call" | custom-call | flops 2415919104 | bytes 9437184 | tf_op jit(solution)/shard_map/pallas_call | solution.py:68
  47.2 3.1 %shard_map.143 = (f32[32,2304]{1,0:T(8,128)S(1)}, bf16[32,2304]{1,0:T(8,128)(2,1)}, bf16[32,2304]{1,0:T(8,128)(2,1)}, bf16[32,2304]{1,0:T(8,128)(2,1)}, f32[32,2...) custom-call(s32[1]{0:T(128)} %bitcast.1.me, ...), custom_call_target="tpu_custom_call" | custom-call | flops 1207959552 | bytes 4718592 | tf_op jit(solution)/shard_map/pallas_call | solution.py:142
  51.7 1.5 %collective-permute-start.23 = (bf16[32,2304]{1,0:T(8,128)(2,1)S(1)}, bf16[32,2304]{1,0:T(8,128)(2,1)S(1)}, u32[]{:S(2)}, u32[]{:S(2)}) collective-permute-start(bf16[32,2304]{1,0:T(8,128)(2,1)S(1)} %get-tuple-element.25), channel_id=1, source_target_pairs={{0,8},{4,12},{8,0},{12,4},{16,24},{20,28},{24,16},{28,20},{1,9},{5... | collective-permute-start | bytes 442376 | tf_op jit(solution)/shard_map/ppermute | solution.py:16
  53.2 1.5 %collective-permute-start.24 = (bf16[32,2304]{1,0:T(8,128)(2,1)}, bf16[32,2304]{1,0:T(8,128)(2,1)}, u32[]{:S(2)}, u32[]{:S(2)}) collective-permute-start(bf16[32,2304]{1,0:T(8,128)(2,1)} %get-tuple-element.26), channel_id=1, source_target_pairs={{0,16},{4,20},{8,24},{12,28},{16,0},{20,4},{24,8},{28,12},{1,17},{... | collective-permute-start | bytes 442376 | tf_op jit(solution)/shard_map/ppermute | solution.py:16
  55.2 1.5 %collective-permute-start.13 = (bf16[32,2304]{1,0:T(8,128)(2,1)}, bf16[32,2304]{1,0:T(8,128)(2,1)}, u32[]{:S(2)}, u32[]{:S(2)}) collective-permute-start(bf16[32,2304]{1,0:T(8,128)(2,1)} %get-tuple-element.18), channel_id=1, source_target_pairs={{0,8},{4,12},{8,0},{12,4},{16,24},{20,28},{24,16},{28,20},{1,9},{5... | collective-permute-start | bytes 442376 | tf_op jit(solution)/shard_map/ppermute | solution.py:16
  56.7 1.5 %collective-permute-start.14 = (bf16[32,2304]{1,0:T(8,128)(2,1)}, bf16[32,2304]{1,0:T(8,128)(2,1)}, u32[]{:S(2)}, u32[]{:S(2)}) collective-permute-start(bf16[32,2304]{1,0:T(8,128)(2,1)} %get-tuple-element.19), channel_id=1, source_target_pairs={{0,16},{4,20},{8,24},{12,28},{16,0},{20,4},{24,8},{28,12},{1,17},{... | collective-permute-start | bytes 442376 | tf_op jit(solution)/shard_map/ppermute | solution.py:16
  58.8 2.6 %collective-permute-start.15 = (bf16[32,2304]{1,0:T(8,128)(2,1)}, bf16[32,2304]{1,0:T(8,128)(2,1)}, u32[]{:S(2)}, u32[]{:S(2)}) collective-permute-start(bf16[32,2304]{1,0:T(8,128)(2,1)} %get-tuple-element.20), channel_id=1, source_target_pairs={{0,24},{4,28},{8,16},{12,20},{16,8},{20,12},{24,0},{28,4},{1,25},{... | collective-permute-start | bytes 442376 | tf_op jit(solution)/shard_map/ppermute | solution.py:16
  61.4 1.3 copy-done.6
  62.7 1.3 copy-done.7
  66.5 1.1 shard_map.146
  68.6 1.0 copy-done.13
  70.5 1.1 shard_map.145
  71.6 1.2 collective-permute-start.16
  72.8 2.6 %collective-permute-start.27 = (bf16[2,8,2304]{2,1,0:T(8,128)(2,1)S(1)}, bf16[2,8,2304]{2,1,0:T(8,128)(2,1)S(1)}, u32[]{:S(2)}, u32[]{:S(2)}) collective-permute-start(bf16[2,8,2304]{2,1,0:T(8,128)(2,1)S(1)} %fusion.11), channel_id=1, source_target_pairs={{0,2},{1,3},{2,0},{3,1},{4,6},{5,7},{6,4},{7,5},{8,10},{9,11},{10,... | collective-permute-start | bytes 221192 | tf_op jit(solution)/shard_map/ppermute | solution.py:16
  76.1 3.0 %collective-permute-start.17 = (bf16[2,8,2304]{2,1,0:T(8,128)(2,1)S(1)}, bf16[2,8,2304]{2,1,0:T(8,128)(2,1)S(1)}, u32[]{:S(2)}, u32[]{:S(2)}) collective-permute-start(bf16[2,8,2304]{2,1,0:T(8,128)(2,1)S(1)} %fusion.10), channel_id=1, source_target_pairs={{0,2},{1,3},{2,0},{3,1},{4,6},{5,7},{6,4},{7,5},{8,10},{9,11},{10,... | collective-permute-start | bytes 221192 | tf_op jit(solution)/shard_map/ppermute | solution.py:16
  79.1 1.4 %collective-permute-done.27 = bf16[2,8,2304]{2,1,0:T(8,128)(2,1)S(1)} collective-permute-done((bf16[2,8,2304]{2,1,0:T(8,128)(2,1)S(1)}, bf16[2,8,2304]{2,1,0:T(8,128)(2,1)S(1)}, u32[]{:S(2)}, u32[]{:S(2)}) %collective-permute-start.27) | collective-permute-done | bytes 73760 | tf_op jit(solution)/shard_map/ppermute | solution.py:16
  81.5 1.8 %collective-permute-start.18 = (bf16[2,8,2304]{2,1,0:T(8,128)(2,1)S(1)}, bf16[2,8,2304]{2,1,0:T(8,128)(2,1)S(1)}, u32[]{:S(2)}, u32[]{:S(2)}) collective-permute-start(bf16[2,8,2304]{2,1,0:T(8,128)(2,1)S(1)} %add_convert_fusion.2), channel_id=1, source_target_pairs={{0,1},{1,0},{2,3},{3,2},{4,5},{5,4},{6,7},{7,6},{8,9},{9,8},{10,11... | collective-permute-start | bytes 221192 | tf_op jit(solution)/shard_map/ppermute | solution.py:16
  83.4 1.6 %collective-permute-done.28 = bf16[2,8,2304]{2,1,0:T(8,128)(2,1)S(1)} collective-permute-done((bf16[2,8,2304]{2,1,0:T(8,128)(2,1)S(1)}, bf16[2,8,2304]{2,1,0:T(8,128)(2,1)S(1)}, u32[]{:S(2)}, u32[]{:S(2)}) %collective-permute-start.28) | collective-permute-done | bytes 73760 | tf_op jit(solution)/shard_map/ppermute | solution.py:16
  86.1 2.5 %collective-permute-start.29 = (bf16[2,2,8,2304]{3,2,1,0:T(8,128)(2,1)S(1)}, bf16[2,2,8,2304]{3,2,1,0:T(8,128)(2,1)S(1)}, u32[]{:S(2)}, u32[]{:S(2)}) collective-permute-start(bf16[2,2,8,2304]{3,2,1,0:T(8,128)(2,1)S(1)} %get-tuple-element.45), channel_id=1, source_target_pairs={{0,8},{4,12},{8,0},{12,4},{16,24},{20,28},{24,16},{28,20},{1,9},{5... | collective-permute-start | bytes 442376 | tf_op jit(solution)/shard_map/ppermute | solution.py:16
  90.1 2.3 %collective-permute-done.31 = bf16[2,2,8,2304]{3,2,1,0:T(8,128)(2,1)S(1)} collective-permute-done((bf16[2,2,8,2304]{3,2,1,0:T(8,128)(2,1)S(1)}, bf16[2,2,8,2304]{3,2,1,0:T(8,128)(2,1)S(1)}, u32[]{:S(2)}, u32[]{:S(2)}) %collective-permute-start.31) | collective-permute-done | bytes 147488 | tf_op jit(solution)/shard_map/ppermute | solution.py:16
  92.4 1.5 %collective-permute-done.30 = bf16[2,2,8,2304]{3,2,1,0:T(8,128)(2,1)S(1)} collective-permute-done((bf16[2,2,8,2304]{3,2,1,0:T(8,128)(2,1)S(1)}, bf16[2,2,8,2304]{3,2,1,0:T(8,128)(2,1)S(1)}, u32[]{:S(2)}, u32[]{:S(2)}) %collective-permute-start.30) | collective-permute-done | bytes 147488 | tf_op jit(solution)/shard_map/ppermute | solution.py:16
  94.4 1.2 collective-permute-done.21
  95.6 1.5 %collective-permute-done.20 = bf16[2,2,8,2304]{3,2,1,0:T(8,128)(2,1)S(1)} collective-permute-done((bf16[2,2,8,2304]{3,2,1,0:T(8,128)(2,1)S(1)}, bf16[2,2,8,2304]{3,2,1,0:T(8,128)(2,1)S(1)}, u32[]{:S(2)}, u32[]{:S(2)}) %collective-permute-start.20) | collective-permute-done | bytes 147488 | tf_op jit(solution)/shard_map/ppermute | solution.py:16
  101.4 1.0 collective-permute-start.36
  103.3 1.7 %collective-permute-start.34 = (bf16[32,2304]{1,0:T(8,128)(2,1)S(1)}, bf16[32,2304]{1,0:T(8,128)(2,1)S(1)}, u32[]{:S(2)}, u32[]{:S(2)}) collective-permute-start(bf16[32,2304]{1,0:T(8,128)(2,1)S(1)} %get-tuple-element.36), channel_id=1, source_target_pairs={{0,8},{4,12},{8,0},{12,4},{16,24},{20,28},{24,16},{28,20},{1,9},{5... | collective-permute-start | bytes 442376 | tf_op jit(solution)/shard_map/ppermute | solution.py:16
  106.0 1.0 collective-permute-start.42
  109.1 1.2 collective-permute-start.40
  110.3 2.0 %collective-permute-done.35 = bf16[32,2304]{1,0:T(8,128)(2,1)S(1)} collective-permute-done((bf16[32,2304]{1,0:T(8,128)(2,1)S(1)}, bf16[32,2304]{1,0:T(8,128)(2,1)S(1)}, u32[]{:S(2)}, u32[]{:S(2)}) %collective-permute-start.35) | collective-permute-done | bytes 147488 | tf_op jit(solution)/shard_map/ppermute | solution.py:16
  113.1 2.3 %collective-permute-done.42 = bf16[32,2304]{1,0:T(8,128)(2,1)S(1)} collective-permute-done((bf16[32,2304]{1,0:T(8,128)(2,1)S(1)}, bf16[32,2304]{1,0:T(8,128)(2,1)S(1)}, u32[]{:S(2)}, u32[]{:S(2)}) %collective-permute-start.42) | collective-permute-done | bytes 147488 | tf_op jit(solution)/shard_map/ppermute | solution.py:16
  115.5 2.3 %collective-permute-done.41 = bf16[32,2304]{1,0:T(8,128)(2,1)S(1)} collective-permute-done((bf16[32,2304]{1,0:T(8,128)(2,1)S(1)}, bf16[32,2304]{1,0:T(8,128)(2,1)S(1)}, u32[]{:S(2)}, u32[]{:S(2)}) %collective-permute-start.41) | collective-permute-done | bytes 147488 | tf_op jit(solution)/shard_map/ppermute | solution.py:16
  117.9 1.0 collective-permute-start.43
  118.9 3.3 %collective-permute-start.38 = (bf16[8,2304]{1,0:T(8,128)(2,1)S(1)}, bf16[8,2304]{1,0:T(8,128)(2,1)S(1)}, u32[]{:S(2)}, u32[]{:S(2)}) collective-permute-start(bf16[8,2304]{1,0:T(8,128)(2,1)S(1)} %fusion.16), channel_id=1, source_target_pairs={{0,2},{1,3},{2,0},{3,1},{4,6},{5,7},{6,4},{7,5},{8,10},{9,11},{10,... | collective-permute-start | bytes 110600 | tf_op jit(solution)/shard_map/ppermute | solution.py:16
  122.3 2.8 %collective-permute-start.44 = (bf16[8,2304]{1,0:T(8,128)(2,1)S(1)}, bf16[8,2304]{1,0:T(8,128)(2,1)S(1)}, u32[]{:S(2)}, u32[]{:S(2)}) collective-permute-start(bf16[8,2304]{1,0:T(8,128)(2,1)S(1)} %fusion.17), channel_id=1, source_target_pairs={{0,2},{1,3},{2,0},{3,1},{4,6},{5,7},{6,4},{7,5},{8,10},{9,11},{10,... | collective-permute-start | bytes 110600 | tf_op jit(solution)/shard_map/ppermute | solution.py:16
  125.1 2.1 %collective-permute-done.44 = bf16[8,2304]{1,0:T(8,128)(2,1)S(1)} collective-permute-done((bf16[8,2304]{1,0:T(8,128)(2,1)S(1)}, bf16[8,2304]{1,0:T(8,128)(2,1)S(1)}, u32[]{:S(2)}, u32[]{:S(2)}) %collective-permute-start.44) | collective-permute-done | bytes 36896 | tf_op jit(solution)/shard_map/ppermute | solution.py:16
  (178 shorter events, 27.5 us)
Async XLA Ops:
  0.6 97.6 %copy-start = (bf16[512,2304]{1,0:T(8,128)(2,1)S(1)}, bf16[512,2304]{1,0:T(8,128)(2,1)}, u32[]{:S(2)}) copy-start(bf16[512,2304]{1,0:T(8,128)(2,1)} %param.24) | copy-start | bytes 7077892
  2.5 6.6 %collective-permute-start.7 = (bf16[64,128]{1,0:T(8,128)(2,1)S(1)}, bf16[64,128]{1,0:T(8,128)(2,1)S(1)}, u32[]{:S(2)}, u32[]{:S(2)}) collective-permute-start(bf16[64,128]{1,0:T(8,128)(2,1)S(1)} %bitcast_select_fusion), channel_id=1, source_target_pairs={{0,1},{1,0},{2,3},{3,2},{4,5},{5,4},{6,7},{7,6},{8,9},{9,8},{10,11... | collective-permute-start | bytes 49160 | tf_op jit(solution)/shard_map/ppermute | solution.py:16
  5.6 19.3 %collective-permute-start.1 = (bf16[64,2304]{1,0:T(8,128)(2,1)}, bf16[64,2304]{1,0:T(8,128)(2,1)S(1)}, u32[]{:S(2)}, u32[]{:S(2)}) collective-permute-start(bf16[64,2304]{1,0:T(8,128)(2,1)} %refs_0_.1), channel_id=1, source_target_pairs={{0,8},{4,12},{8,0},{12,4},{16,24},{20,28},{24,16},{28,20},{1,9},{5... | collective-permute-start | bytes 884744 | tf_op jit(solution)/shard_map/ppermute | solution.py:16
  7.1 17.9 %collective-permute-start.3 = (bf16[64,2304]{1,0:T(8,128)(2,1)}, bf16[64,2304]{1,0:T(8,128)(2,1)S(1)}, u32[]{:S(2)}, u32[]{:S(2)}) collective-permute-start(bf16[64,2304]{1,0:T(8,128)(2,1)} %refs_0_.1), channel_id=1, source_target_pairs={{0,16},{4,20},{8,24},{12,28},{16,0},{20,4},{24,8},{28,12},{1,17},{... | collective-permute-start | bytes 884744 | tf_op jit(solution)/shard_map/ppermute | solution.py:16
  8.6 16.4 %collective-permute-start.5 = (bf16[64,2304]{1,0:T(8,128)(2,1)}, bf16[64,2304]{1,0:T(8,128)(2,1)S(1)}, u32[]{:S(2)}, u32[]{:S(2)}) collective-permute-start(bf16[64,2304]{1,0:T(8,128)(2,1)} %refs_0_.1), channel_id=1, source_target_pairs={{0,24},{4,28},{8,16},{12,20},{16,8},{20,12},{24,0},{28,4},{1,25},{... | collective-permute-start | bytes 884744 | tf_op jit(solution)/shard_map/ppermute | solution.py:16
  9.2 4.7 %collective-permute-start.8 = (bf16[64,128]{1,0:T(8,128)(2,1)S(1)}, bf16[64,128]{1,0:T(8,128)(2,1)S(1)}, u32[]{:S(2)}, u32[]{:S(2)}) collective-permute-start(bf16[64,128]{1,0:T(8,128)(2,1)S(1)} %fusion.18), channel_id=1, source_target_pairs={{0,2},{1,3},{2,0},{3,1},{4,6},{5,7},{6,4},{7,5},{8,10},{9,11},{10,... | collective-permute-start | bytes 49160 | tf_op jit(solution)/shard_map/ppermute | solution.py:16
  13.9 7.1 %collective-permute-start.9 = (bf16[64,128]{1,0:T(8,128)(2,1)S(1)}, bf16[64,128]{1,0:T(8,128)(2,1)S(1)}, u32[]{:S(2)}, u32[]{:S(2)}) collective-permute-start(bf16[64,128]{1,0:T(8,128)(2,1)S(1)} %add.225), channel_id=1, source_target_pairs={{0,8},{4,12},{8,0},{12,4},{16,24},{20,28},{24,16},{28,20},{1,9},{5... | collective-permute-start | bytes 49160 | tf_op jit(solution)/shard_map/ppermute | solution.py:16
  21.0 3.9 %collective-permute-start.10 = (bf16[128,128]{1,0:T(8,128)(2,1)S(1)}, bf16[128,128]{1,0:T(8,128)(2,1)S(1)}, u32[]{:S(2)}, u32[]{:S(2)}) collective-permute-start(bf16[128,128]{1,0:T(8,128)(2,1)S(1)} %pad_maximum_fusion.6), channel_id=1, source_target_pairs={{0,16},{4,20},{8,24},{12,28},{16,0},{20,4},{24,8},{28,12},{1,17},{... | collective-permute-start | bytes 98312 | tf_op jit(solution)/shard_map/ppermute | solution.py:16
  37.9 9.2 %collective-permute-start.12 = (bf16[256,2304]{1,0:T(8,128)(2,1)S(1)}, bf16[256,2304]{1,0:T(8,128)(2,1)S(1)}, u32[]{:S(2)}, u32[]{:S(2)}) collective-permute-start(bf16[256,2304]{1,0:T(8,128)(2,1)S(1)} %shard_map.142), channel_id=1, source_target_pairs={{0,4},{4,0},{8,12},{12,8},{16,20},{20,16},{24,28},{28,24},{1,5},{5... | collective-permute-start | bytes 3538952 | tf_op jit(solution)/shard_map/ppermute | solution.py:16
  38.0 3.2 %collective-permute-start = (bf16[64,2304]{1,0:T(8,128)(2,1)S(1)}, bf16[64,2304]{1,0:T(8,128)(2,1)S(1)}, u32[]{:S(2)}, u32[]{:S(2)}) collective-permute-start(bf16[64,2304]{1,0:T(8,128)(2,1)S(1)} %copy-done.11), channel_id=1, source_target_pairs={{0,4},{4,0},{8,12},{12,8},{16,20},{20,16},{24,28},{28,24},{1,5},{5... | collective-permute-start | bytes 884744 | tf_op jit(solution)/shard_map/ppermute | solution.py:16
  38.5 3.2 %collective-permute-start.2 = (bf16[64,2304]{1,0:T(8,128)(2,1)S(1)}, bf16[64,2304]{1,0:T(8,128)(2,1)S(1)}, u32[]{:S(2)}, u32[]{:S(2)}) collective-permute-start(bf16[64,2304]{1,0:T(8,128)(2,1)S(1)} %collective-permute-done.1.refs_1_), channel_id=1, source_target_pairs={{0,4},{4,0},{8,12},{12,8},{16,20},{20,16},{24,28},{28,24},{1,5},{5... | collective-permute-start | bytes 884744 | tf_op jit(solution)/shard_map/ppermute | solution.py:16
  38.6 3.5 %collective-permute-start.4 = (bf16[64,2304]{1,0:T(8,128)(2,1)S(1)}, bf16[64,2304]{1,0:T(8,128)(2,1)S(1)}, u32[]{:S(2)}, u32[]{:S(2)}) collective-permute-start(bf16[64,2304]{1,0:T(8,128)(2,1)S(1)} %collective-permute-done.3.refs_2_), channel_id=1, source_target_pairs={{0,4},{4,0},{8,12},{12,8},{16,20},{20,16},{24,28},{28,24},{1,5},{5... | collective-permute-start | bytes 884744 | tf_op jit(solution)/shard_map/ppermute | solution.py:16
  39.0 3.5 %collective-permute-start.6 = (bf16[64,2304]{1,0:T(8,128)(2,1)S(1)}, bf16[64,2304]{1,0:T(8,128)(2,1)S(1)}, u32[]{:S(2)}, u32[]{:S(2)}) collective-permute-start(bf16[64,2304]{1,0:T(8,128)(2,1)S(1)} %collective-permute-done.5.refs_3_), channel_id=1, source_target_pairs={{0,4},{4,0},{8,12},{12,8},{16,20},{20,16},{24,28},{28,24},{1,5},{5... | collective-permute-start | bytes 884744 | tf_op jit(solution)/shard_map/ppermute | solution.py:16
  41.3 5.9 %collective-permute-start.11 = (bf16[256,128]{1,0:T(8,128)(2,1)S(1)}, bf16[256,128]{1,0:T(8,128)(2,1)S(1)}, u32[]{:S(2)}, u32[]{:S(2)}) collective-permute-start(bf16[256,128]{1,0:T(8,128)(2,1)S(1)} %pad_maximum_fusion.5.table), channel_id=1, source_target_pairs={{0,4},{4,0},{8,12},{12,8},{16,20},{20,16},{24,28},{28,24},{1,5},{5... | collective-permute-start | bytes 196616 | tf_op jit(solution)/shard_map/ppermute | solution.py:16
  51.7 6.5 %collective-permute-start.23 = (bf16[32,2304]{1,0:T(8,128)(2,1)S(1)}, bf16[32,2304]{1,0:T(8,128)(2,1)S(1)}, u32[]{:S(2)}, u32[]{:S(2)}) collective-permute-start(bf16[32,2304]{1,0:T(8,128)(2,1)S(1)} %get-tuple-element.25), channel_id=1, source_target_pairs={{0,8},{4,12},{8,0},{12,4},{16,24},{20,28},{24,16},{28,20},{1,9},{5... | collective-permute-start | bytes 442376 | tf_op jit(solution)/shard_map/ppermute | solution.py:16
  53.2 13.3 %collective-permute-start.24 = (bf16[32,2304]{1,0:T(8,128)(2,1)}, bf16[32,2304]{1,0:T(8,128)(2,1)}, u32[]{:S(2)}, u32[]{:S(2)}) collective-permute-start(bf16[32,2304]{1,0:T(8,128)(2,1)} %get-tuple-element.26), channel_id=1, source_target_pairs={{0,16},{4,20},{8,24},{12,28},{16,0},{20,4},{24,8},{28,12},{1,17},{... | collective-permute-start | bytes 442376 | tf_op jit(solution)/shard_map/ppermute | solution.py:16
  54.7 11.9 %collective-permute-start.25 = (bf16[32,2304]{1,0:T(8,128)(2,1)}, bf16[32,2304]{1,0:T(8,128)(2,1)}, u32[]{:S(2)}, u32[]{:S(2)}) collective-permute-start(bf16[32,2304]{1,0:T(8,128)(2,1)} %get-tuple-element.27), channel_id=1, source_target_pairs={{0,24},{4,28},{8,16},{12,20},{16,8},{20,12},{24,0},{28,4},{1,25},{... | collective-permute-start | bytes 442376 | tf_op jit(solution)/shard_map/ppermute | solution.py:16
  55.2 12.9 %collective-permute-start.13 = (bf16[32,2304]{1,0:T(8,128)(2,1)}, bf16[32,2304]{1,0:T(8,128)(2,1)}, u32[]{:S(2)}, u32[]{:S(2)}) collective-permute-start(bf16[32,2304]{1,0:T(8,128)(2,1)} %get-tuple-element.18), channel_id=1, source_target_pairs={{0,8},{4,12},{8,0},{12,4},{16,24},{20,28},{24,16},{28,20},{1,9},{5... | collective-permute-start | bytes 442376 | tf_op jit(solution)/shard_map/ppermute | solution.py:16
  56.7 11.9 %collective-permute-start.14 = (bf16[32,2304]{1,0:T(8,128)(2,1)}, bf16[32,2304]{1,0:T(8,128)(2,1)}, u32[]{:S(2)}, u32[]{:S(2)}) collective-permute-start(bf16[32,2304]{1,0:T(8,128)(2,1)} %get-tuple-element.19), channel_id=1, source_target_pairs={{0,16},{4,20},{8,24},{12,28},{16,0},{20,4},{24,8},{28,12},{1,17},{... | collective-permute-start | bytes 442376 | tf_op jit(solution)/shard_map/ppermute | solution.py:16
  58.8 9.8 %collective-permute-start.15 = (bf16[32,2304]{1,0:T(8,128)(2,1)}, bf16[32,2304]{1,0:T(8,128)(2,1)}, u32[]{:S(2)}, u32[]{:S(2)}) collective-permute-start(bf16[32,2304]{1,0:T(8,128)(2,1)} %get-tuple-element.20), channel_id=1, source_target_pairs={{0,24},{4,28},{8,16},{12,20},{16,8},{20,12},{24,0},{28,4},{1,25},{... | collective-permute-start | bytes 442376 | tf_op jit(solution)/shard_map/ppermute | solution.py:16
  67.6 5.2 %collective-permute-start.26 = (bf16[16,2304]{1,0:T(8,128)(2,1)S(1)}, bf16[16,2304]{1,0:T(8,128)(2,1)S(1)}, u32[]{:S(2)}, u32[]{:S(2)}) collective-permute-start(bf16[16,2304]{1,0:T(8,128)(2,1)S(1)} %get-tuple-element.29), channel_id=1, source_target_pairs={{0,1},{1,0},{2,3},{3,2},{4,5},{5,4},{6,7},{7,6},{8,9},{9,8},{10,11... | collective-permute-start | bytes 221192 | tf_op jit(solution)/shard_map/ppermute | solution.py:16
  71.6 4.4 %collective-permute-start.16 = (bf16[16,2304]{1,0:T(8,128)(2,1)S(1)}, bf16[16,2304]{1,0:T(8,128)(2,1)S(1)}, u32[]{:S(2)}, u32[]{:S(2)}) collective-permute-start(bf16[16,2304]{1,0:T(8,128)(2,1)S(1)} %get-tuple-element.22), channel_id=1, source_target_pairs={{0,1},{1,0},{2,3},{3,2},{4,5},{5,4},{6,7},{7,6},{8,9},{9,8},{10,11... | collective-permute-start | bytes 221192 | tf_op jit(solution)/shard_map/ppermute | solution.py:16
  72.8 7.7 %collective-permute-start.27 = (bf16[2,8,2304]{2,1,0:T(8,128)(2,1)S(1)}, bf16[2,8,2304]{2,1,0:T(8,128)(2,1)S(1)}, u32[]{:S(2)}, u32[]{:S(2)}) collective-permute-start(bf16[2,8,2304]{2,1,0:T(8,128)(2,1)S(1)} %fusion.11), channel_id=1, source_target_pairs={{0,2},{1,3},{2,0},{3,1},{4,6},{5,7},{6,4},{7,5},{8,10},{9,11},{10,... | collective-permute-start | bytes 221192 | tf_op jit(solution)/shard_map/ppermute | solution.py:16
  76.1 21.6 %copy-start.20 = (bf16[2304,512]{1,0:T(8,128)(2,1)S(1)}, bf16[2304,512]{1,0:T(8,128)(2,1)}, u32[]{:S(2)}) copy-start(bf16[2304,512]{1,0:T(8,128)(2,1)} %param.22) | copy-start | bytes 7077892
  76.1 21.6 %copy-start.21 = (f32[512]{0:T(512)S(1)}, f32[512]{0:T(512)}, u32[]{:S(2)}) copy-start(f32[512]{0:T(512)} %param.23) | copy-start | bytes 6148
  76.1 5.4 %collective-permute-start.17 = (bf16[2,8,2304]{2,1,0:T(8,128)(2,1)S(1)}, bf16[2,8,2304]{2,1,0:T(8,128)(2,1)S(1)}, u32[]{:S(2)}, u32[]{:S(2)}) collective-permute-start(bf16[2,8,2304]{2,1,0:T(8,128)(2,1)S(1)} %fusion.10), channel_id=1, source_target_pairs={{0,2},{1,3},{2,0},{3,1},{4,6},{5,7},{6,4},{7,5},{8,10},{9,11},{10,... | collective-permute-start | bytes 221192 | tf_op jit(solution)/shard_map/ppermute | solution.py:16
  80.6 4.4 %collective-permute-start.28 = (bf16[2,8,2304]{2,1,0:T(8,128)(2,1)S(1)}, bf16[2,8,2304]{2,1,0:T(8,128)(2,1)S(1)}, u32[]{:S(2)}, u32[]{:S(2)}) collective-permute-start(bf16[2,8,2304]{2,1,0:T(8,128)(2,1)S(1)} %add_convert_fusion), channel_id=1, source_target_pairs={{0,1},{1,0},{2,3},{3,2},{4,5},{5,4},{6,7},{7,6},{8,9},{9,8},{10,11... | collective-permute-start | bytes 221192 | tf_op jit(solution)/shard_map/ppermute | solution.py:16
  81.5 7.1 %collective-permute-start.18 = (bf16[2,8,2304]{2,1,0:T(8,128)(2,1)S(1)}, bf16[2,8,2304]{2,1,0:T(8,128)(2,1)S(1)}, u32[]{:S(2)}, u32[]{:S(2)}) collective-permute-start(bf16[2,8,2304]{2,1,0:T(8,128)(2,1)S(1)} %add_convert_fusion.2), channel_id=1, source_target_pairs={{0,1},{1,0},{2,3},{3,2},{4,5},{5,4},{6,7},{7,6},{8,9},{9,8},{10,11... | collective-permute-start | bytes 221192 | tf_op jit(solution)/shard_map/ppermute | solution.py:16
  85.0 7.4 %collective-permute-start.31 = (bf16[2,2,8,2304]{3,2,1,0:T(8,128)(2,1)S(1)}, bf16[2,2,8,2304]{3,2,1,0:T(8,128)(2,1)S(1)}, u32[]{:S(2)}, u32[]{:S(2)}) collective-permute-start(bf16[2,2,8,2304]{3,2,1,0:T(8,128)(2,1)S(1)} %get-tuple-element.45), channel_id=1, source_target_pairs={{0,24},{4,28},{8,16},{12,20},{16,8},{20,12},{24,0},{28,4},{1,25},{... | collective-permute-start | bytes 442376 | tf_op jit(solution)/shard_map/ppermute | solution.py:16
  85.6 8.3 %collective-permute-start.30 = (bf16[2,2,8,2304]{3,2,1,0:T(8,128)(2,1)S(1)}, bf16[2,2,8,2304]{3,2,1,0:T(8,128)(2,1)S(1)}, u32[]{:S(2)}, u32[]{:S(2)}) collective-permute-start(bf16[2,2,8,2304]{3,2,1,0:T(8,128)(2,1)S(1)} %get-tuple-element.45), channel_id=1, source_target_pairs={{0,16},{4,20},{8,24},{12,28},{16,0},{20,4},{24,8},{28,12},{1,17},{... | collective-permute-start | bytes 442376 | tf_op jit(solution)/shard_map/ppermute | solution.py:16
  86.1 8.2 %collective-permute-start.29 = (bf16[2,2,8,2304]{3,2,1,0:T(8,128)(2,1)S(1)}, bf16[2,2,8,2304]{3,2,1,0:T(8,128)(2,1)S(1)}, u32[]{:S(2)}, u32[]{:S(2)}) collective-permute-start(bf16[2,2,8,2304]{3,2,1,0:T(8,128)(2,1)S(1)} %get-tuple-element.45), channel_id=1, source_target_pairs={{0,8},{4,12},{8,0},{12,4},{16,24},{20,28},{24,16},{28,20},{1,9},{5... | collective-permute-start | bytes 442376 | tf_op jit(solution)/shard_map/ppermute | solution.py:16
  88.6 7.0 %collective-permute-start.21 = (bf16[2,2,8,2304]{3,2,1,0:T(8,128)(2,1)S(1)}, bf16[2,2,8,2304]{3,2,1,0:T(8,128)(2,1)S(1)}, u32[]{:S(2)}, u32[]{:S(2)}) collective-permute-start(bf16[2,2,8,2304]{3,2,1,0:T(8,128)(2,1)S(1)} %get-tuple-element.43), channel_id=1, source_target_pairs={{0,24},{4,28},{8,16},{12,20},{16,8},{20,12},{24,0},{28,4},{1,25},{... | collective-permute-start | bytes 442376 | tf_op jit(solution)/shard_map/ppermute | solution.py:16
  89.2 7.9 %collective-permute-start.20 = (bf16[2,2,8,2304]{3,2,1,0:T(8,128)(2,1)S(1)}, bf16[2,2,8,2304]{3,2,1,0:T(8,128)(2,1)S(1)}, u32[]{:S(2)}, u32[]{:S(2)}) collective-permute-start(bf16[2,2,8,2304]{3,2,1,0:T(8,128)(2,1)S(1)} %get-tuple-element.43), channel_id=1, source_target_pairs={{0,16},{4,20},{8,24},{12,28},{16,0},{20,4},{24,8},{28,12},{1,17},{... | collective-permute-start | bytes 442376 | tf_op jit(solution)/shard_map/ppermute | solution.py:16
  92.4 5.1 %collective-permute-start.19 = (bf16[2,2,8,2304]{3,2,1,0:T(8,128)(2,1)S(1)}, bf16[2,2,8,2304]{3,2,1,0:T(8,128)(2,1)S(1)}, u32[]{:S(2)}, u32[]{:S(2)}) collective-permute-start(bf16[2,2,8,2304]{3,2,1,0:T(8,128)(2,1)S(1)} %get-tuple-element.43), channel_id=1, source_target_pairs={{0,8},{4,12},{8,0},{12,4},{16,24},{20,28},{24,16},{28,20},{1,9},{5... | collective-permute-start | bytes 442376 | tf_op jit(solution)/shard_map/ppermute | solution.py:16
  94.4 10.6 %collective-permute-start.32 = (bf16[128,2304]{1,0:T(8,128)(2,1)S(1)}, bf16[128,2304]{1,0:T(8,128)(2,1)S(1)}, u32[]{:S(2)}, u32[]{:S(2)}) collective-permute-start(bf16[128,2304]{1,0:T(8,128)(2,1)S(1)} %bitcast.100), channel_id=1, source_target_pairs={{0,4},{4,0},{8,12},{12,8},{16,20},{20,16},{24,28},{28,24},{1,5},{5... | collective-permute-start | bytes 1769480 | tf_op jit(solution)/shard_map/ppermute | solution.py:16
  97.6 2.7 %collective-permute-start.22 = (bf16[128,2304]{1,0:T(8,128)(2,1)S(1)}, bf16[128,2304]{1,0:T(8,128)(2,1)S(1)}, u32[]{:S(2)}, u32[]{:S(2)}) collective-permute-start(bf16[128,2304]{1,0:T(8,128)(2,1)S(1)} %bitcast.102), channel_id=1, source_target_pairs={{0,4},{4,0},{8,12},{12,8},{16,20},{20,16},{24,28},{28,24},{1,5},{5... | collective-permute-start | bytes 1769480 | tf_op jit(solution)/shard_map/ppermute | solution.py:16
  98.7 2.2 %collective-permute-start.33 = (bf16[128,2304]{1,0:T(8,128)(2,1)S(1)}, bf16[128,2304]{1,0:T(8,128)(2,1)S(1)}, u32[]{:S(2)}, u32[]{:S(2)}) collective-permute-start(bf16[128,2304]{1,0:T(8,128)(2,1)S(1)} %convolution_convert_fusion.1), channel_id=1, source_target_pairs={{0,4},{4,0},{8,12},{12,8},{16,20},{20,16},{24,28},{28,24},{1,5},{5... | collective-permute-start | bytes 1769480 | tf_op jit(solution)/shard_map/ppermute | solution.py:16
  100.2 5.2 %collective-permute-start.39 = (bf16[128,2304]{1,0:T(8,128)(2,1)S(1)}, bf16[128,2304]{1,0:T(8,128)(2,1)S(1)}, u32[]{:S(2)}, u32[]{:S(2)}) collective-permute-start(bf16[128,2304]{1,0:T(8,128)(2,1)S(1)} %convolution_convert_fusion), channel_id=1, source_target_pairs={{0,4},{4,0},{8,12},{12,8},{16,20},{20,16},{24,28},{28,24},{1,5},{5... | collective-permute-start | bytes 1769480 | tf_op jit(solution)/shard_map/ppermute | solution.py:16
  101.4 7.7 %collective-permute-start.36 = (bf16[32,2304]{1,0:T(8,128)(2,1)S(1)}, bf16[32,2304]{1,0:T(8,128)(2,1)S(1)}, u32[]{:S(2)}, u32[]{:S(2)}) collective-permute-start(bf16[32,2304]{1,0:T(8,128)(2,1)S(1)} %get-tuple-element.37), channel_id=1, source_target_pairs={{0,24},{4,28},{8,16},{12,20},{16,8},{20,12},{24,0},{28,4},{1,25},{... | collective-permute-start | bytes 442376 | tf_op jit(solution)/shard_map/ppermute | solution.py:16
  102.4 9.9 %collective-permute-start.35 = (bf16[32,2304]{1,0:T(8,128)(2,1)S(1)}, bf16[32,2304]{1,0:T(8,128)(2,1)S(1)}, u32[]{:S(2)}, u32[]{:S(2)}) collective-permute-start(bf16[32,2304]{1,0:T(8,128)(2,1)S(1)} %get-tuple-element.38), channel_id=1, source_target_pairs={{0,16},{4,20},{8,24},{12,28},{16,0},{20,4},{24,8},{28,12},{1,17},{... | collective-permute-start | bytes 442376 | tf_op jit(solution)/shard_map/ppermute | solution.py:16
  103.3 9.0 %collective-permute-start.34 = (bf16[32,2304]{1,0:T(8,128)(2,1)S(1)}, bf16[32,2304]{1,0:T(8,128)(2,1)S(1)}, u32[]{:S(2)}, u32[]{:S(2)}) collective-permute-start(bf16[32,2304]{1,0:T(8,128)(2,1)S(1)} %get-tuple-element.36), channel_id=1, source_target_pairs={{0,8},{4,12},{8,0},{12,4},{16,24},{20,28},{24,16},{28,20},{1,9},{5... | collective-permute-start | bytes 442376 | tf_op jit(solution)/shard_map/ppermute | solution.py:16
  106.0 9.4 %collective-permute-start.42 = (bf16[32,2304]{1,0:T(8,128)(2,1)S(1)}, bf16[32,2304]{1,0:T(8,128)(2,1)S(1)}, u32[]{:S(2)}, u32[]{:S(2)}) collective-permute-start(bf16[32,2304]{1,0:T(8,128)(2,1)S(1)} %get-tuple-element.40), channel_id=1, source_target_pairs={{0,24},{4,28},{8,16},{12,20},{16,8},{20,12},{24,0},{28,4},{1,25},{... | collective-permute-start | bytes 442376 | tf_op jit(solution)/shard_map/ppermute | solution.py:16
  107.0 10.8 %collective-permute-start.41 = (bf16[32,2304]{1,0:T(8,128)(2,1)S(1)}, bf16[32,2304]{1,0:T(8,128)(2,1)S(1)}, u32[]{:S(2)}, u32[]{:S(2)}) collective-permute-start(bf16[32,2304]{1,0:T(8,128)(2,1)S(1)} %get-tuple-element.41), channel_id=1, source_target_pairs={{0,16},{4,20},{8,24},{12,28},{16,0},{20,4},{24,8},{28,12},{1,17},{... | collective-permute-start | bytes 442376 | tf_op jit(solution)/shard_map/ppermute | solution.py:16
  109.1 8.7 %collective-permute-start.40 = (bf16[32,2304]{1,0:T(8,128)(2,1)S(1)}, bf16[32,2304]{1,0:T(8,128)(2,1)S(1)}, u32[]{:S(2)}, u32[]{:S(2)}) collective-permute-start(bf16[32,2304]{1,0:T(8,128)(2,1)S(1)} %get-tuple-element.39), channel_id=1, source_target_pairs={{0,8},{4,12},{8,0},{12,4},{16,24},{20,28},{24,16},{28,20},{1,9},{5... | collective-permute-start | bytes 442376 | tf_op jit(solution)/shard_map/ppermute | solution.py:16
  112.4 6.5 %collective-permute-start.37 = (bf16[2,8,2304]{2,1,0:T(8,128)(2,1)S(1)}, bf16[2,8,2304]{2,1,0:T(8,128)(2,1)S(1)}, u32[]{:S(2)}, u32[]{:S(2)}) collective-permute-start(bf16[2,8,2304]{2,1,0:T(8,128)(2,1)S(1)} %fusion.12), channel_id=1, source_target_pairs={{0,1},{1,0},{2,3},{3,2},{4,5},{5,4},{6,7},{7,6},{8,9},{9,8},{10,11... | collective-permute-start | bytes 221192 | tf_op jit(solution)/shard_map/ppermute | solution.py:16
  117.9 4.4 %collective-permute-start.43 = (bf16[2,8,2304]{2,1,0:T(8,128)(2,1)S(1)}, bf16[2,8,2304]{2,1,0:T(8,128)(2,1)S(1)}, u32[]{:S(2)}, u32[]{:S(2)}) collective-permute-start(bf16[2,8,2304]{2,1,0:T(8,128)(2,1)S(1)} %fusion.13), channel_id=1, source_target_pairs={{0,1},{1,0},{2,3},{3,2},{4,5},{5,4},{6,7},{7,6},{8,9},{9,8},{10,11... | collective-permute-start | bytes 221192 | tf_op jit(solution)/shard_map/ppermute | solution.py:16
  118.9 6.2 %collective-permute-start.38 = (bf16[8,2304]{1,0:T(8,128)(2,1)S(1)}, bf16[8,2304]{1,0:T(8,128)(2,1)S(1)}, u32[]{:S(2)}, u32[]{:S(2)}) collective-permute-start(bf16[8,2304]{1,0:T(8,128)(2,1)S(1)} %fusion.16), channel_id=1, source_target_pairs={{0,2},{1,3},{2,0},{3,1},{4,6},{5,7},{6,4},{7,5},{8,10},{9,11},{10,... | collective-permute-start | bytes 110600 | tf_op jit(solution)/shard_map/ppermute | solution.py:16
  122.3 4.9 %collective-permute-start.44 = (bf16[8,2304]{1,0:T(8,128)(2,1)S(1)}, bf16[8,2304]{1,0:T(8,128)(2,1)S(1)}, u32[]{:S(2)}, u32[]{:S(2)}) collective-permute-start(bf16[8,2304]{1,0:T(8,128)(2,1)S(1)} %fusion.17), channel_id=1, source_target_pairs={{0,2},{1,3},{2,0},{3,1},{4,6},{5,7},{6,4},{7,5},{8,10},{9,11},{10,... | collective-permute-start | bytes 110600 | tf_op jit(solution)/shard_map/ppermute | solution.py:16
  (23 other events, 101.9 us)

commit v6 on v4

v6 whole, which is shorter than its diff:
```python
import functools

import jax
import jax.numpy as jnp
from jax import lax
from jax.experimental import pallas as pl
from jax.experimental.pallas import tpu as pltpu
from jax.sharding import PartitionSpec as P

CHUNKS = 2
LANES = 128
MIB = 1024 * 1024
LOAD_MIB = 36
VMEM_SPEC = pl.BlockSpec(memory_space=pltpu.VMEM)
SMEM_SPEC = pl.BlockSpec(memory_space=pltpu.SMEM)
HBM_SPEC = pl.BlockSpec(memory_space=pltpu.HBM)


def swap(value, axis, r):
    return lax.ppermute(value, axis, [(i, i ^ r) for i in range(lax.axis_size(axis))])


def dot(a, b):
    return jnp.dot(a, b, preferred_element_type=jnp.float32)


def half(value):
    return value.astype(jnp.bfloat16)


def full(value):
    return value.astype(jnp.float32)


def silu(value):
    return value / (1.0 + jnp.exp(-value))


def bits_of(count):
    assert count & (count - 1) == 0
    return [1 << b for b in range(count.bit_length() - 1)]


def take(value, index, dim):
    return lax.dynamic_index_in_dim(value, index, dim, keepdims=False)


def gather_pairs(value):
    pairs = lax.axis_size("expert") // 2
    return jnp.stack([value] + [swap(value, "expert", 2 * p) for p in range(1, pairs)])


def call(body, operands, specs, outs, scratch, mib, cost):
    flops, moved = cost
    return pl.pallas_call(
        body,
        in_specs=specs,
        out_specs=[VMEM_SPEC] * len(outs),
        out_shape=[jax.ShapeDtypeStruct(shape, dtype) for shape, dtype in outs],
        scratch_shapes=scratch,
        compiler_params=pltpu.CompilerParams(vmem_limit_bytes=mib * MIB),
        cost_estimate=pl.CostEstimate(flops=flops, bytes_accessed=moved, transcendentals=0),
    )(*operands)


def start_all(pairs, sems):
    copies = [pltpu.make_async_copy(a, b, sems.at[i]) for i, (a, b) in enumerate(pairs)]
    for copy in copies:
        copy.start()
    return copies


def pack_kernel(feats, feat, ids, weights, out):
    top, own = ids.shape
    lane = lax.broadcasted_iota(jnp.int32, (top, LANES), 1)
    row = lax.broadcasted_iota(jnp.int32, (top, LANES), 0)
    high = half(weights[...])
    low = half(weights[...] - full(high))
    values = jnp.zeros((own, LANES), jnp.float32)
    for i, part in enumerate([half(full(ids[...])), high, low]):
        places = half(jnp.where(lane == row + i * top, 1.0, 0.0))
        values += lax.dot_general(
            part, places, (((0,), (0,)), ((), ())), preferred_element_type=jnp.float32
        )
    for f in range(feats):
        out[f * own : (f + 1) * own, :] = half(jnp.where(feat[0] == f, values, 0.0))


def run_pack(feat, expert_ids, gate_weights, feats):
    own, top = expert_ids.shape
    return call(
        functools.partial(pack_kernel, feats),
        [feat.reshape(1), expert_ids.T, gate_weights.T],
        [SMEM_SPEC, VMEM_SPEC, VMEM_SPEC],
        [((feats * own, LANES), jnp.bfloat16)],
        [],
        2,
        (6 * own * top * LANES, 2 * feats * own * LANES),
    )[0]


def load_kernel(count, *refs):
    copies = start_all(list(zip(refs[:count], refs[count:-1])), refs[-1])
    for copy in copies:
        copy.wait()


def run_load(values, mib):
    count = len(values)
    return call(
        functools.partial(load_kernel, count),
        values,
        [HBM_SPEC] * count,
        [(value.shape, value.dtype) for value in values],
        [pltpu.SemaphoreType.DMA((count,))],
        mib,
        (0, 4 * sum(value.size for value in values)),
    )


def hidden_kernel(count, e, tile, *refs):
    pieces, (gate, up, out, rows) = refs[:count], refs[count:]
    size = pieces[0].shape[0]
    for i in range(count):
        rows[i * size : (i + 1) * size, :] = pieces[i][...]
    for j in range(0, out.shape[1], tile):
        cut = slice(j, j + tile)
        value = silu(dot(rows[...], gate[e, :, cut]))
        out[:, cut] = half(value * dot(rows[...], up[e, :, cut]))


def run_hidden(pieces, gate, up, e):
    count, (size, width) = len(pieces), pieces[0].shape
    units = gate.shape[2]
    return call(
        functools.partial(hidden_kernel, count, e, min(256, units)),
        [*pieces, gate, up],
        [VMEM_SPEC] * (count + 2),
        [((count * size, units), jnp.bfloat16)],
        [pltpu.VMEM((count * size, width), jnp.bfloat16)],
        8,
        (4 * count * size * width * units, 4 * width * units),
    )[0]


def down_kernel(top, e, start, tile, more, me, hidden, down, table, *refs):
    arrived, outs = refs[:more], refs[more:]
    entries = full(table[...])
    lane = lax.broadcasted_iota(jnp.int32, entries.shape, 1)
    expert = (me[0] * down.shape[0] + e).astype(jnp.float32)
    chosen = jnp.where((entries == expert) & (lane < top), 1.0, 0.0)
    chosen = pltpu.roll(chosen, top, 1) + pltpu.roll(chosen, 2 * top, 1)
    scale = jnp.sum(chosen * entries, axis=1, keepdims=True)
    size, columns = outs[0].shape
    for j in range(0, columns, tile):
        cut = slice(j, j + tile)
        value = dot(hidden[...], down[e, :, start + j : start + j + tile]) * scale
        if more:
            value += full(arrived[0][:, cut])
        for p, out in enumerate(outs):
            out[:, cut] = value[p * size : (p + 1) * size].astype(out.dtype)


def run_down(hidden, down, e, c, table, me, top, arrived=None, pairs=None):
    rows, units = hidden.shape
    columns = down.shape[2] // CHUNKS
    tile = max(t for t in range(128, 513, 128) if columns % t == 0)
    outs = [((rows, columns), jnp.bfloat16)]
    if pairs is not None:
        outs = [
            ((rows // pairs, columns), jnp.bfloat16 if p else jnp.float32) for p in range(pairs)
        ]
    more = [] if arrived is None else [arrived]
    result = call(
        functools.partial(down_kernel, top, e, c * columns, tile, len(more)),
        [me.reshape(1), hidden, down, table, *more],
        [SMEM_SPEC] + [VMEM_SPEC] * (3 + len(more)),
        outs,
        [],
        8,
        (2 * rows * units * columns, 2 * units * columns),
    )
    return result if pairs is not None else result[0]


def shared_kernel(x, gate, up, down, *outs):
    hidden = half(silu(dot(x[...], gate[...])) * dot(x[...], up[...]))
    columns = outs[0].shape[1]
    for c, out in enumerate(outs):
        out[...] = dot(hidden, down[:, c * columns : (c + 1) * columns])


def run_shared(x, gate, up, down):
    rows, width = x.shape
    return call(
        shared_kernel,
        [x, gate, up, down],
        [VMEM_SPEC] * 4,
        [((rows, width // CHUNKS), jnp.float32)] * CHUNKS,
        [],
        8,
        (6 * rows * gate.size, 6 * gate.size),
    )


def sum_kernel(step, place, *refs):
    parts, (kept, sent) = refs[:-2], refs[-2:]
    total = sum(full(part[...]) for part in parts)
    rows, width = total.shape
    total = total.reshape(rows // step // 2, 2, step, width)
    low, high = total[:, 0].reshape(-1, width), total[:, 1].reshape(-1, width)
    kept[...] = jnp.where(place[0] == 0, low, high)
    sent[...] = half(jnp.where(place[0] == 0, high, low))


def run_sum(parts, place, step):
    rows, width = parts[0].shape
    return call(
        functools.partial(sum_kernel, step),
        [place.reshape(1), *parts],
        [SMEM_SPEC] + [VMEM_SPEC] * len(parts),
        [((rows // 2, width), jnp.float32), ((rows // 2, width), jnp.bfloat16)],
        [],
        6,
        (rows * width * len(parts), 2 * rows * width),
    )


def encode_kernel(*refs):
    parts, (encoder, bias, out) = refs[:-3], refs[-3:]
    columns = parts[0].shape[1]
    total = bias[...]
    for c, part in enumerate(parts):
        total = total + dot(part[...], encoder[c * columns : (c + 1) * columns, :])
    out[...] = half(jnp.maximum(total, 0.0))


def run_encode(parts, encoder, bias):
    rows = parts[0].shape[0]
    return call(
        encode_kernel,
        [*parts, encoder, bias[None, :]],
        [VMEM_SPEC] * (len(parts) + 2),
        [((rows, encoder.shape[1]), jnp.bfloat16)],
        [],
        8,
        (2 * rows * encoder.size, 2 * encoder.size),
    )[0]


def decode_kernel(c, more, features, decoder, *refs):
    arrived, outs = refs[:more], refs[more:]
    size, columns = outs[0].shape
    value = dot(features[...], decoder[:, c * columns : (c + 1) * columns])
    if more:
        value += full(arrived[0][...])
    for p, out in enumerate(outs):
        out[...] = value[p * size : (p + 1) * size].astype(out.dtype)


def run_decode(features, decoder, c, arrived=None, pairs=None):
    rows, columns = features.shape[0], decoder.shape[1] // CHUNKS
    outs = [((rows, columns), jnp.bfloat16)]
    if pairs is not None:
        outs = [
            ((rows // pairs, columns), jnp.bfloat16 if p else jnp.float32) for p in range(pairs)
        ]
    more = [] if arrived is None else [arrived]
    result = call(
        functools.partial(decode_kernel, c, len(more)),
        [features, decoder, *more],
        [VMEM_SPEC] * (2 + len(more)),
        outs,
        [],
        8,
        (2 * rows * decoder.size // CHUNKS, 2 * decoder.size // CHUNKS),
    )
    return result if pairs is not None else result[0]


def shards(
    tokens,
    expert_ids,
    gate_weights,
    expert_gate,
    expert_up,
    expert_down,
    shared_gate,
    shared_up,
    shared_down,
    encoder,
    encoder_bias,
    decoder,
    decoder_bias,
):
    own, top = expert_ids.shape
    width = tokens.shape[1]
    feats = lax.axis_size("feat")
    pairs = lax.axis_size("expert") // 2
    devices = 2 * pairs * feats
    local_experts = range(expert_gate.shape[0])
    chunks = range(CHUNKS)
    me = lax.axis_index(("expert", "feat"))
    my_feat = lax.axis_index("feat")
    feat_bits = bits_of(feats)
    place = [(my_feat // bit) % 2 for bit in feat_bits]

    table = run_pack(my_feat, expert_ids, gate_weights, feats)
    for bit in feat_bits:
        table = table + swap(table, "feat", bit)
    for bit in bits_of(pairs):
        table = jnp.concatenate([table, swap(table, "expert", 2 * bit)], axis=0)
    table_far = swap(table, "expert", 1)

    near = [tokens] + [swap(tokens, "expert", 2 * p) for p in range(1, pairs)]
    far = [swap(piece, "expert", 1) for piece in near]
    near[0], expert_gate, expert_up, expert_down = run_load(
        [tokens, expert_gate, expert_up, expert_down], LOAD_MIB
    )
    shared_out = run_shared(far[0], shared_gate, shared_up, shared_down)

    hidden_near = [run_hidden(near, expert_gate, expert_up, e) for e in local_experts]
    hidden_far = [run_hidden(far, expert_gate, expert_up, e) for e in local_experts]

    def over_experts(hidden, rows_table, c, total, last_pairs):
        for e in local_experts:
            last = last_pairs if e == local_experts[-1] else None
            total = run_down(hidden[e], expert_down, e, c, rows_table, me, top, total, last)
        return total

    arrived = [swap(over_experts(hidden_near, table, c, None, None), "expert", 1) for c in chunks]
    blocks = [over_experts(hidden_far, table_far, c, arrived[c], pairs) for c in chunks]

    near = []
    for c in chunks:
        arrived = [swap(blocks[c][p], "expert", 2 * p) for p in range(1, pairs)]
        total, sent = run_sum([blocks[c][0], shared_out[c]] + arrived, place[0], own)
        total = total + full(swap(sent, "feat", feat_bits[0]))
        total = total.reshape((2,) * (len(feat_bits) - 1) + (own, -1))
        for i, bit in enumerate(feat_bits[1:-1]):
            dim = len(feat_bits) - 2 - i
            arrived = swap(half(take(total, 1 - place[i + 1], dim)), "feat", bit)
            total = take(total, place[i + 1], dim) + full(arrived)
        total = half(total)
        moe_out = half(full(total) + full(swap(total, "feat", feat_bits[-1])))
        for bit in feat_bits[-2::-1]:
            moe_out = jnp.stack([moe_out, swap(moe_out, "feat", bit)], axis=moe_out.ndim - 2)
        near.append(gather_pairs(moe_out).reshape(pairs * feats * own, -1))

    far = [swap(part, "expert", 1) for part in near]
    features_near = run_encode(near, encoder, encoder_bias)
    arrived = [swap(run_decode(features_near, decoder, c), "expert", 1) for c in chunks]
    features_far = run_encode(far, encoder, encoder_bias)
    blocks = [run_decode(features_far, decoder, c, arrived[c], pairs) for c in chunks]

    reconstruction = []
    for c in chunks:
        arrived = [swap(blocks[c][p], "expert", 2 * p) for p in range(1, pairs)]
        total = blocks[c][0] + sum(full(a) for a in arrived)
        total = total.reshape((2,) * len(feat_bits) + (own, -1))
        for bit in feat_bits[:-1]:
            dim = len(total.shape) - 3
            arrived = swap(half(lax.index_in_dim(total, 1, dim, False)), "feat", bit)
            total = lax.index_in_dim(total, 0, dim, False) + full(arrived)
        arrived = swap(half(take(total, 1 - place[-1], 0)), "feat", feat_bits[-1])
        reconstruction.append(take(total, place[-1], 0) + full(arrived))
    reconstruction = jnp.concatenate(reconstruction, axis=1) + decoder_bias[None, :]

    features = jnp.stack([features_far, features_near]).reshape(2, pairs, feats, own, -1)
    features = features.transpose(1, 0, 2, 3, 4).reshape(devices, own, -1)
    relative = me - me % feats + my_feat % (feats // 2)
    blocks = [lax.dynamic_index_in_dim(features, i ^ relative, 0) for i in range(devices)]
    features = jnp.concatenate(blocks, axis=0).reshape(devices * own, -1)
    return (features, reconstruction)


def solution(mesh):
    return jax.shard_map(
        shards,
        mesh=mesh,
        in_specs=(
            P("expert", None),
            P(("expert", "feat"), None),
            P(("expert", "feat"), None),
            P(("expert", "feat"), None, None),
            P(("expert", "feat"), None, None),
            P(("expert", "feat"), None, None),
            P(None, "feat"),
            P(None, "feat"),
            P("feat", None),
            P(None, ("expert", "feat")),
            P(("expert", "feat")),
            P(("expert", "feat"), None),
            P(),
        ),
        out_specs=(P(None, ("expert", "feat")), P(("expert", "feat"), None)),
        check_vma=False,
    )
```

time: 147 us -> 124 us (0.84)
  matrix products: 38.6 us -> 0 us
  Pallas kernels: 0 us -> 29.2 us
  other arithmetic: 12.2 us -> 2.05 us
  starting transfers between devices: 54 us -> 52.4 us
    dot_general x16 -> x0, matrix products: 38.6 us -> none  [dot(): return jnp.dot(a, b, preferred_element_type=jnp.float32)]
    pallas_call x0 -> x17, Pallas kernels: none -> 29.2 us  [call(): pl.pallas_call(body, in_specs=specs, out_specs=[VMEM_SPEC] * len(outs), o...]
    unnamed x57 -> x71, local copies, waits for them, and re-layouts: 0.39 us -> 9.28 us
    slice x6 -> x0, local copies, waits for them, and re-layouts: 4.49 us -> none  [the longest x2 3.63 us: shards(): total = out[rows:] + full(swap(half(out[:rows]), 'expert', 1))]
    another operation x3 -> x1, other arithmetic: 3.59 us -> 0.05 us  [shards(): jnp.stack([features_far, features_near]).reshape(2, pairs, feats, own, -1)]
    convert_element_type x6 -> x4, other arithmetic: 3.56 us -> 0.08 us  [half(): return value.astype(jnp.bfloat16)]
    convert_element_type x6 -> x4, local copies, waits for them, and re-layouts: 2.67 us -> 0.05 us  [half(): return value.astype(jnp.bfloat16)]
    another operation x7 -> x4, other arithmetic: 3.1 us -> 1.05 us  [gather_pairs(): jnp.stack([value] + [swap(value, 'expert', 2 * p) for p in range(1, pairs)])]
  transfers between devices with their start and end apart: 44 -> 46, of which waited for: 20 -> 18; matrix products, arithmetic and copies ran while one was open for 29% -> 1% of each run, Pallas kernels for 0% -> 23%
where the time goes in v6:
time: 124 us; the launch traced here: 123 us
  starting transfers between devices  52.4 us (42%)
  Pallas kernels  29.2 us (24%)
  waiting for transfers between devices  29.2 us (24%)
  local copies, waits for them, and re-layouts  9.34 us (8%)
  other arithmetic  2.05 us (2%)
  between operations  1.28 us (1%)
    ppermute x46, starting transfers between devices, swap(): lax.ppermute(value, axis, [(i, i ^ r) for i in range(lax.axis_size(axis))])  52.4 us
    ppermute x46, waiting for transfers between devices, swap(): lax.ppermute(value, axis, [(i, i ^ r) for i in range(lax.axis_size(axis))])  29.2 us
    pallas_call x17, Pallas kernels, call(): pl.pallas_call(body, in_specs=specs, out_specs=[VMEM_SPEC] * len(outs), o...  29.2 us
    unnamed x71, local copies, waits for them, and re-layouts  9.28 us
  transfers between devices with their start and end apart: 46, of which 18 were waited for; matrix products, arithmetic and copies ran while one was open for 1% of the time, Pallas kernels for 23%

profile of v6, /device:TPU:0, one launch (start us, length us, event | category | flops | bytes accessed | tf_op | source)
XLA Modules:
  0.0 123.4 jit_solution(13973361249080357985)
XLA Ops:
  2.2 3.0 %collective-permute-start.7 = (bf16[64,128]{1,0:T(8,128)(2,1)S(1)}, bf16[64,128]{1,0:T(8,128)(2,1)S(1)}, u32[]{:S(2)}, u32[]{:S(2)}) collective-permute-start(bf16[64,128]{1,0:T(8,128)(2,1)S(1)} %shard_map.142), channel_id=1, source_target_pairs={{0,1},{1,0},{2,3},{3,2},{4,5},{5,4},{6,7},{7,6},{8,9},{9,8},{10,11... | collective-permute-start | bytes 49160 | tf_op jit(solution)/shard_map/ppermute | solution.py:20
  5.2 1.5 %collective-permute-start.1 = (bf16[64,2304]{1,0:T(8,128)(2,1)}, bf16[64,2304]{1,0:T(8,128)(2,1)S(1)}, u32[]{:S(2)}, u32[]{:S(2)}) collective-permute-start(bf16[64,2304]{1,0:T(8,128)(2,1)} %refs_0_.1), channel_id=1, source_target_pairs={{0,8},{4,12},{8,0},{12,4},{16,24},{20,28},{24,16},{28,20},{1,9},{5... | collective-permute-start | bytes 884744 | tf_op jit(solution)/shard_map/ppermute | solution.py:20
  6.7 1.5 %collective-permute-start.3 = (bf16[64,2304]{1,0:T(8,128)(2,1)}, bf16[64,2304]{1,0:T(8,128)(2,1)S(1)}, u32[]{:S(2)}, u32[]{:S(2)}) collective-permute-start(bf16[64,2304]{1,0:T(8,128)(2,1)} %refs_0_.1), channel_id=1, source_target_pairs={{0,16},{4,20},{8,24},{12,28},{16,0},{20,4},{24,8},{28,12},{1,17},{... | collective-permute-start | bytes 884744 | tf_op jit(solution)/shard_map/ppermute | solution.py:20
  8.7 2.7 %collective-permute-start.8 = (bf16[64,128]{1,0:T(8,128)(2,1)S(1)}, bf16[64,128]{1,0:T(8,128)(2,1)S(1)}, u32[]{:S(2)}, u32[]{:S(2)}) collective-permute-start(bf16[64,128]{1,0:T(8,128)(2,1)S(1)} %add.184), channel_id=1, source_target_pairs={{0,2},{1,3},{2,0},{3,1},{4,6},{5,7},{6,4},{7,5},{8,10},{9,11},{10,... | collective-permute-start | bytes 49160 | tf_op jit(solution)/shard_map/ppermute | solution.py:20
  11.4 2.0 %collective-permute-done.8 = bf16[64,128]{1,0:T(8,128)(2,1)S(1)} collective-permute-done((bf16[64,128]{1,0:T(8,128)(2,1)S(1)}, bf16[64,128]{1,0:T(8,128)(2,1)S(1)}, u32[]{:S(2)}, u32[]{:S(2)}) %collective-permute-start.8) | collective-permute-done | bytes 16416 | tf_op jit(solution)/shard_map/ppermute | solution.py:20
  13.4 1.6 %collective-permute-start.9 = (bf16[64,128]{1,0:T(8,128)(2,1)S(1)}, bf16[64,128]{1,0:T(8,128)(2,1)S(1)}, u32[]{:S(2)}, u32[]{:S(2)}) collective-permute-start(bf16[64,128]{1,0:T(8,128)(2,1)S(1)} %add.185), channel_id=1, source_target_pairs={{0,8},{4,12},{8,0},{12,4},{16,24},{20,28},{24,16},{28,20},{1,9},{5... | collective-permute-start | bytes 49160 | tf_op jit(solution)/shard_map/ppermute | solution.py:20
  15.1 5.6 %collective-permute-done.9 = bf16[64,128]{1,0:T(8,128)(2,1)S(1)} collective-permute-done((bf16[64,128]{1,0:T(8,128)(2,1)S(1)}, bf16[64,128]{1,0:T(8,128)(2,1)S(1)}, u32[]{:S(2)}, u32[]{:S(2)}) %collective-permute-start.9) | collective-permute-done | bytes 16416 | tf_op jit(solution)/shard_map/ppermute | solution.py:20
  20.6 1.5 %collective-permute-start.10 = (bf16[128,128]{1,0:T(8,128)(2,1)S(1)}, bf16[128,128]{1,0:T(8,128)(2,1)S(1)}, u32[]{:S(2)}, u32[]{:S(2)}) collective-permute-start(bf16[128,128]{1,0:T(8,128)(2,1)S(1)} %pad_maximum_fusion.6), channel_id=1, source_target_pairs={{0,16},{4,20},{8,24},{12,28},{16,0},{20,4},{24,8},{28,12},{1,17},{... | collective-permute-start | bytes 98312 | tf_op jit(solution)/shard_map/ppermute | solution.py:20
  23.1 5.2 %shard_map.140 = (bf16[64,2304]{1,0:T(8,128)(2,1)S(1)}, bf16[1,2304,1024]{2,1,0:T(8,128)(2,1)S(1)}, bf16[1,2304,1024]{2,1,0:T(8,128)(2,1)S(1)}, bf16[1,1024,2304]{2,1,0:T(8,128)(2,1)S(1)}) custom-call(bf16[64,2304]{1,0:T(8,128)(2,1)S(1)} %copy-done.12, bf16[1,2304,1024]{2,1,0:T(8,128)(2,1)} %refs_1_.1, bf16[1,2304,1024]{2,1,0:T(8,128)(2,1)} %refs_2_.3, ...), custom_call_target="tpu_custom_call" | custom-call | bytes 28901376 | tf_op jit(solution)/shard_map/pallas_call | solution.py:55
  28.4 2.7 %shard_map.143.hidden = bf16[256,1024]{1,0:T(8,128)(2,1)S(1)} custom-call(bf16[64,2304]{1,0:T(8,128)(2,1)S(1)} %get-tuple-element.31.refs_0_, bf16[64,2304]{1,0:T(8,128)(2,1)S(1)} %collective-permute-done.1.refs_1_, bf16[64,2304]{1,0:T(8,128)(2,1)S(1)} %collective-permute-done.3.refs_2_, bf16[64,2304]{1,0:T(8,128)(2,1)S(1)} %collective-permute-done.5.refs_3_, ...), custom_call_target="tpu_custom_call" | custom-call | flops 2415919104 | bytes 9437184 | tf_op jit(solution)/shard_map/pallas_call | solution.py:55
  35.5 2.7 %shard_map.141.hidden = bf16[256,1024]{1,0:T(8,128)(2,1)S(1)} custom-call(bf16[64,2304]{1,0:T(8,128)(2,1)S(1)} %collective-permute-done.refs_0_.x, bf16[64,2304]{1,0:T(8,128)(2,1)S(1)} %collective-permute-done.2.refs_1_, bf16[64,2304]{1,0:T(8,128)(2,1)S(1)} %collective-permute-done.4.refs_2_, bf16[64,2304]{1,0:T(8,128)(2,1)S(1)} %collective-permute-done.6.refs_3_, ...), custom_call_target="tpu_custom_call" | custom-call | flops 2415919104 | bytes 9437184 | tf_op jit(solution)/shard_map/pallas_call | solution.py:55
  39.0 1.7 %shard_map.145 = (f32[64,1152]{1,0:T(8,128)S(1)}, bf16[64,1152]{1,0:T(8,128)(2,1)S(1)}, bf16[64,1152]{1,0:T(8,128)(2,1)}, bf16[64,1152]{1,0:T(8,128)(2,1)}) custom-call(s32[1]{0:T(128)} %bitcast.1.me, bf16[256,1024]{1,0:T(8,128)(2,1)S(1)} %shard_map.141.hidden, bf16[1,1024,2304]{2,1,0:T(8,128)(2,1)S(1)} %get-tuple-element.30.down, ...), custom_call_target="tpu_custom_call" | custom-call | flops 603979776 | bytes 2359296 | tf_op jit(solution)/shard_map/pallas_call | solution.py:55
  40.7 1.5 %collective-permute-start.13 = (bf16[64,1152]{1,0:T(8,128)(2,1)S(1)}, bf16[64,1152]{1,0:T(8,128)(2,1)S(1)}, u32[]{:S(2)}, u32[]{:S(2)}) collective-permute-start(bf16[64,1152]{1,0:T(8,128)(2,1)S(1)} %get-tuple-element.34), channel_id=1, source_target_pairs={{0,8},{4,12},{8,0},{12,4},{16,24},{20,28},{24,16},{28,20},{1,9},{5... | collective-permute-start | bytes 442376 | tf_op jit(solution)/shard_map/ppermute | solution.py:20
  42.7 1.5 %collective-permute-start.15 = (bf16[64,1152]{1,0:T(8,128)(2,1)}, bf16[64,1152]{1,0:T(8,128)(2,1)}, u32[]{:S(2)}, u32[]{:S(2)}) collective-permute-start(bf16[64,1152]{1,0:T(8,128)(2,1)} %get-tuple-element.36), channel_id=1, source_target_pairs={{0,24},{4,28},{8,16},{12,20},{16,8},{20,12},{24,0},{28,4},{1,25},{... | collective-permute-start | bytes 442376 | tf_op jit(solution)/shard_map/ppermute | solution.py:20
  44.2 1.7 %shard_map.149 = (f32[64,1152]{1,0:T(8,128)S(1)}, bf16[64,1152]{1,0:T(8,128)(2,1)}, bf16[64,1152]{1,0:T(8,128)(2,1)}, bf16[64,1152]{1,0:T(8,128)(2,1)}) custom-call(s32[1]{0:T(128)} %bitcast.1.me, bf16[256,1024]{1,0:T(8,128)(2,1)S(1)} %shard_map.141.hidden, bf16[1,1024,2304]{2,1,0:T(8,128)(2,1)S(1)} %get-tuple-element.30.down, ...), custom_call_target="tpu_custom_call" | custom-call | flops 603979776 | bytes 2359296 | tf_op jit(solution)/shard_map/pallas_call | solution.py:55
  46.6 1.4 %collective-permute-start.24 = (bf16[64,1152]{1,0:T(8,128)(2,1)}, bf16[64,1152]{1,0:T(8,128)(2,1)}, u32[]{:S(2)}, u32[]{:S(2)}) collective-permute-start(bf16[64,1152]{1,0:T(8,128)(2,1)} %get-tuple-element.41), channel_id=1, source_target_pairs={{0,8},{4,12},{8,0},{12,4},{16,24},{20,28},{24,16},{28,20},{1,9},{5... | collective-permute-start | bytes 442376 | tf_op jit(solution)/shard_map/ppermute | solution.py:20
  49.3 1.5 %collective-permute-start.26 = (bf16[64,1152]{1,0:T(8,128)(2,1)}, bf16[64,1152]{1,0:T(8,128)(2,1)}, u32[]{:S(2)}, u32[]{:S(2)}) collective-permute-start(bf16[64,1152]{1,0:T(8,128)(2,1)} %get-tuple-element.43), channel_id=1, source_target_pairs={{0,24},{4,28},{8,16},{12,20},{16,8},{20,12},{24,0},{28,4},{1,25},{... | collective-permute-start | bytes 442376 | tf_op jit(solution)/shard_map/ppermute | solution.py:20
  54.5 1.1 shard_map.147
  56.1 1.7 %collective-permute-done.25.refs_3_ = bf16[64,1152]{1,0:T(8,128)(2,1)} collective-permute-done((bf16[64,1152]{1,0:T(8,128)(2,1)}, bf16[64,1152]{1,0:T(8,128)(2,1)}, u32[]{:S(2)}, u32[]{:S(2)}) %collective-permute-start.25) | collective-permute-done | bytes 147488 | tf_op jit(solution)/shard_map/ppermute | solution.py:20
  57.8 1.1 shard_map.150
  60.0 2.6 %collective-permute-start.17 = (bf16[2,16,1152]{2,1,0:T(8,128)(2,1)S(1)}, bf16[2,16,1152]{2,1,0:T(8,128)(2,1)S(1)}, u32[]{:S(2)}, u32[]{:S(2)}) collective-permute-start(bf16[2,16,1152]{2,1,0:T(8,128)(2,1)S(1)} %bitcast.106), channel_id=1, source_target_pairs={{0,2},{1,3},{2,0},{3,1},{4,6},{5,7},{6,4},{7,5},{8,10},{9,11},{10,... | collective-permute-start | bytes 221192 | tf_op jit(solution)/shard_map/ppermute | solution.py:20
  63.5 2.4 %collective-permute-start.28 = (bf16[2,16,1152]{2,1,0:T(8,128)(2,1)S(1)}, bf16[2,16,1152]{2,1,0:T(8,128)(2,1)S(1)}, u32[]{:S(2)}, u32[]{:S(2)}) collective-permute-start(bf16[2,16,1152]{2,1,0:T(8,128)(2,1)S(1)} %bitcast.108), channel_id=1, source_target_pairs={{0,2},{1,3},{2,0},{3,1},{4,6},{5,7},{6,4},{7,5},{8,10},{9,11},{10,... | collective-permute-start | bytes 221192 | tf_op jit(solution)/shard_map/ppermute | solution.py:20
  66.0 1.4 %collective-permute-done.17 = bf16[2,16,1152]{2,1,0:T(8,128)(2,1)S(1)} collective-permute-done((bf16[2,16,1152]{2,1,0:T(8,128)(2,1)S(1)}, bf16[2,16,1152]{2,1,0:T(8,128)(2,1)S(1)}, u32[]{:S(2)}, u32[]{:S(2)}) %collective-permute-start.17) | collective-permute-done | bytes 73760 | tf_op jit(solution)/shard_map/ppermute | solution.py:20
  67.9 1.7 %collective-permute-done.28 = bf16[2,16,1152]{2,1,0:T(8,128)(2,1)S(1)} collective-permute-done((bf16[2,16,1152]{2,1,0:T(8,128)(2,1)S(1)}, bf16[2,16,1152]{2,1,0:T(8,128)(2,1)S(1)}, u32[]{:S(2)}, u32[]{:S(2)}) %collective-permute-start.28) | collective-permute-done | bytes 73760 | tf_op jit(solution)/shard_map/ppermute | solution.py:20
  70.2 1.7 %collective-permute-done.18 = bf16[2,16,1152]{2,1,0:T(8,128)(2,1)S(1)} collective-permute-done((bf16[2,16,1152]{2,1,0:T(8,128)(2,1)S(1)}, bf16[2,16,1152]{2,1,0:T(8,128)(2,1)S(1)}, u32[]{:S(2)}, u32[]{:S(2)}) %collective-permute-start.18) | collective-permute-done | bytes 73760 | tf_op jit(solution)/shard_map/ppermute | solution.py:20
  71.9 2.6 %collective-permute-start.21 = (bf16[2,2,16,1152]{3,2,1,0:T(8,128)(2,1)S(1)}, bf16[2,2,16,1152]{3,2,1,0:T(8,128)(2,1)S(1)}, u32[]{:S(2)}, u32[]{:S(2)}) collective-permute-start(bf16[2,2,16,1152]{3,2,1,0:T(8,128)(2,1)S(1)} %get-tuple-element.57), channel_id=1, source_target_pairs={{0,24},{4,28},{8,16},{12,20},{16,8},{20,12},{24,0},{28,4},{1,25},{... | collective-permute-start | bytes 442376 | tf_op jit(solution)/shard_map/ppermute | solution.py:20
  75.5 2.6 %collective-permute-start.32 = (bf16[2,2,16,1152]{3,2,1,0:T(8,128)(2,1)S(1)}, bf16[2,2,16,1152]{3,2,1,0:T(8,128)(2,1)S(1)}, u32[]{:S(2)}, u32[]{:S(2)}) collective-permute-start(bf16[2,2,16,1152]{3,2,1,0:T(8,128)(2,1)S(1)} %get-tuple-element.55), channel_id=1, source_target_pairs={{0,24},{4,28},{8,16},{12,20},{16,8},{20,12},{24,0},{28,4},{1,25},{... | collective-permute-start | bytes 442376 | tf_op jit(solution)/shard_map/ppermute | solution.py:20
  79.1 1.7 %collective-permute-start.30 = (bf16[2,2,16,1152]{3,2,1,0:T(8,128)(2,1)S(1)}, bf16[2,2,16,1152]{3,2,1,0:T(8,128)(2,1)S(1)}, u32[]{:S(2)}, u32[]{:S(2)}) collective-permute-start(bf16[2,2,16,1152]{3,2,1,0:T(8,128)(2,1)S(1)} %get-tuple-element.55), channel_id=1, source_target_pairs={{0,8},{4,12},{8,0},{12,4},{16,24},{20,28},{24,16},{28,20},{1,9},{5... | collective-permute-start | bytes 442376 | tf_op jit(solution)/shard_map/ppermute | solution.py:20
  80.8 1.1 collective-permute-done.20
  82.0 1.5 %collective-permute-done.32 = bf16[2,2,16,1152]{3,2,1,0:T(8,128)(2,1)S(1)} collective-permute-done((bf16[2,2,16,1152]{3,2,1,0:T(8,128)(2,1)S(1)}, bf16[2,2,16,1152]{3,2,1,0:T(8,128)(2,1)S(1)}, u32[]{:S(2)}, u32[]{:S(2)}) %collective-permute-start.32) | collective-permute-done | bytes 147488 | tf_op jit(solution)/shard_map/ppermute | solution.py:20
  83.5 1.5 %collective-permute-done.31 = bf16[2,2,16,1152]{3,2,1,0:T(8,128)(2,1)S(1)} collective-permute-done((bf16[2,2,16,1152]{3,2,1,0:T(8,128)(2,1)S(1)}, bf16[2,2,16,1152]{3,2,1,0:T(8,128)(2,1)S(1)}, u32[]{:S(2)}, u32[]{:S(2)}) %collective-permute-start.31) | collective-permute-done | bytes 147488 | tf_op jit(solution)/shard_map/ppermute | solution.py:20
  85.9 1.9 %shard_map.152.features = bf16[256,512]{1,0:T(8,128)(2,1)S(1)} custom-call(bf16[256,1152]{1,0:T(8,128)(2,1)S(1)} %bitcast.63, bf16[256,1152]{1,0:T(8,128)(2,1)} %bitcast.22.refs_1_, bf16[2304,512]{1,0:T(8,128)(2,1)S(1)} %copy-done.1, f32[1,512]{1,0:T(1,128)S(1)} %bitcast.64), custom_call_target="tpu_custom_call" | custom-call | flops 603979776 | bytes 2359296 | tf_op jit(solution)/shard_map/pallas_call | solution.py:55
  87.8 1.5 %shard_map.155 = bf16[256,1152]{1,0:T(8,128)(2,1)} custom-call(bf16[256,512]{1,0:T(8,128)(2,1)S(1)} %shard_map.152.features, bf16[512,2304]{1,0:T(8,128)(2,1)S(1)} %copy-done), custom_call_target="tpu_custom_call" | custom-call | flops 301989888 | bytes 1179648 | tf_op jit(solution)/shard_map/pallas_call | solution.py:55
  89.8 1.3 %shard_map.153 = bf16[256,1152]{1,0:T(8,128)(2,1)} custom-call(bf16[256,512]{1,0:T(8,128)(2,1)S(1)} %shard_map.152.features, bf16[512,2304]{1,0:T(8,128)(2,1)S(1)} %copy-done), custom_call_target="tpu_custom_call" | custom-call | flops 301989888 | bytes 1179648 | tf_op jit(solution)/shard_map/pallas_call | solution.py:55
  91.2 1.7 %copy-done.2 = bf16[2304,512]{1,0:T(8,128)(2,1)S(1)} copy-done((bf16[2304,512]{1,0:T(8,128)(2,1)S(1)}, bf16[2304,512]{1,0:T(8,128)(2,1)}, u32[]{:S(2)}) %copy-start.2) | copy-done | bytes 2359320
  92.9 2.1 %shard_map.151.features = bf16[256,512]{1,0:T(8,128)(2,1)S(1)} custom-call(bf16[256,1152]{1,0:T(8,128)(2,1)} %collective-permute-done.22.refs_0_, bf16[256,1152]{1,0:T(8,128)(2,1)} %collective-permute-done.33.refs_1_, bf16[2304,512]{1,0:T(8,128)(2,1)S(1)} %copy-done.2, f32[1,512]{1,0:T(1,128)S(1)} %bitcast.65), custom_call_target="tpu_custom_call" | custom-call | flops 603979776 | bytes 2359296 | tf_op jit(solution)/shard_map/pallas_call | solution.py:55
  94.9 1.6 %shard_map.156 = (f32[64,1152]{1,0:T(8,128)S(1)}, bf16[64,1152]{1,0:T(8,128)(2,1)S(1)}, bf16[64,1152]{1,0:T(8,128)(2,1)S(1)}, bf16[64,1152]{1,0:T(8,128)(2,1)S(1)}) custom-call(bf16[256,512]{1,0:T(8,128)(2,1)S(1)} %shard_map.151.features, bf16[512,2304]{1,0:T(8,128)(2,1)S(1)} %copy-done, bf16[256,1152]{1,0:T(8,128)(2,1)} %collective-permute-done.40.refs_0_), custom_call_target="tpu_custom_call" | custom-call | flops 301989888 | bytes 1179648 | tf_op jit(solution)/shard_map/pallas_call | solution.py:55
  96.5 2.4 %collective-permute-start.43 = (bf16[64,1152]{1,0:T(8,128)(2,1)S(1)}, bf16[64,1152]{1,0:T(8,128)(2,1)S(1)}, u32[]{:S(2)}, u32[]{:S(2)}) collective-permute-start(bf16[64,1152]{1,0:T(8,128)(2,1)S(1)} %get-tuple-element.53), channel_id=1, source_target_pairs={{0,24},{4,28},{8,16},{12,20},{16,8},{20,12},{24,0},{28,4},{1,25},{... | collective-permute-start | bytes 442376 | tf_op jit(solution)/shard_map/ppermute | solution.py:20
  100.1 1.6 %shard_map.154 = (f32[64,1152]{1,0:T(8,128)S(1)}, bf16[64,1152]{1,0:T(8,128)(2,1)S(1)}, bf16[64,1152]{1,0:T(8,128)(2,1)S(1)}, bf16[64,1152]{1,0:T(8,128)(2,1)S(1)}) custom-call(bf16[256,512]{1,0:T(8,128)(2,1)S(1)} %shard_map.151.features, bf16[512,2304]{1,0:T(8,128)(2,1)S(1)} %copy-done, bf16[256,1152]{1,0:T(8,128)(2,1)} %collective-permute-done.34.refs_0_), custom_call_target="tpu_custom_call" | custom-call | flops 301989888 | bytes 1179648 | tf_op jit(solution)/shard_map/pallas_call | solution.py:55
  101.7 2.4 %collective-permute-start.37 = (bf16[64,1152]{1,0:T(8,128)(2,1)S(1)}, bf16[64,1152]{1,0:T(8,128)(2,1)S(1)}, u32[]{:S(2)}, u32[]{:S(2)}) collective-permute-start(bf16[64,1152]{1,0:T(8,128)(2,1)S(1)} %get-tuple-element.49), channel_id=1, source_target_pairs={{0,24},{4,28},{8,16},{12,20},{16,8},{20,12},{24,0},{28,4},{1,25},{... | collective-permute-start | bytes 442376 | tf_op jit(solution)/shard_map/ppermute | solution.py:20
  106.0 1.4 %collective-permute-done.42 = bf16[64,1152]{1,0:T(8,128)(2,1)S(1)} collective-permute-done((bf16[64,1152]{1,0:T(8,128)(2,1)S(1)}, bf16[64,1152]{1,0:T(8,128)(2,1)S(1)}, u32[]{:S(2)}, u32[]{:S(2)}) %collective-permute-start.42) | collective-permute-done | bytes 147488 | tf_op jit(solution)/shard_map/ppermute | solution.py:20
  107.5 1.6 %collective-permute-start.44 = (bf16[2,16,1152]{2,1,0:T(8,128)(2,1)S(1)}, bf16[2,16,1152]{2,1,0:T(8,128)(2,1)S(1)}, u32[]{:S(2)}, u32[]{:S(2)}) collective-permute-start(bf16[2,16,1152]{2,1,0:T(8,128)(2,1)S(1)} %fusion.3), channel_id=1, source_target_pairs={{0,1},{1,0},{2,3},{3,2},{4,5},{5,4},{6,7},{7,6},{8,9},{9,8},{10,11... | collective-permute-start | bytes 221192 | tf_op jit(solution)/shard_map/ppermute | solution.py:20
  109.1 1.5 %collective-permute-done.37 = bf16[64,1152]{1,0:T(8,128)(2,1)S(1)} collective-permute-done((bf16[64,1152]{1,0:T(8,128)(2,1)S(1)}, bf16[64,1152]{1,0:T(8,128)(2,1)S(1)}, u32[]{:S(2)}, u32[]{:S(2)}) %collective-permute-start.37) | collective-permute-done | bytes 147488 | tf_op jit(solution)/shard_map/ppermute | solution.py:20
  110.5 2.7 %collective-permute-done.36 = bf16[64,1152]{1,0:T(8,128)(2,1)S(1)} collective-permute-done((bf16[64,1152]{1,0:T(8,128)(2,1)S(1)}, bf16[64,1152]{1,0:T(8,128)(2,1)S(1)}, u32[]{:S(2)}, u32[]{:S(2)}) %collective-permute-start.36) | collective-permute-done | bytes 147488 | tf_op jit(solution)/shard_map/ppermute | solution.py:20
  113.3 1.3 %collective-permute-start.38 = (bf16[2,16,1152]{2,1,0:T(8,128)(2,1)S(1)}, bf16[2,16,1152]{2,1,0:T(8,128)(2,1)S(1)}, u32[]{:S(2)}, u32[]{:S(2)}) collective-permute-start(bf16[2,16,1152]{2,1,0:T(8,128)(2,1)S(1)} %fusion.2), channel_id=1, source_target_pairs={{0,1},{1,0},{2,3},{3,2},{4,5},{5,4},{6,7},{7,6},{8,9},{9,8},{10,11... | collective-permute-start | bytes 221192 | tf_op jit(solution)/shard_map/ppermute | solution.py:20
  114.7 2.5 %collective-permute-start.45 = (bf16[16,1152]{1,0:T(8,128)(2,1)S(1)}, bf16[16,1152]{1,0:T(8,128)(2,1)S(1)}, u32[]{:S(2)}, u32[]{:S(2)}) collective-permute-start(bf16[16,1152]{1,0:T(8,128)(2,1)S(1)} %fusion.5), channel_id=1, source_target_pairs={{0,2},{1,3},{2,0},{3,1},{4,6},{5,7},{6,4},{7,5},{8,10},{9,11},{10,... | collective-permute-start | bytes 110600 | tf_op jit(solution)/shard_map/ppermute | solution.py:20
  117.8 2.6 %collective-permute-start.39 = (bf16[16,1152]{1,0:T(8,128)(2,1)S(1)}, bf16[16,1152]{1,0:T(8,128)(2,1)S(1)}, u32[]{:S(2)}, u32[]{:S(2)}) collective-permute-start(bf16[16,1152]{1,0:T(8,128)(2,1)S(1)} %fusion.4), channel_id=1, source_target_pairs={{0,2},{1,3},{2,0},{3,1},{4,6},{5,7},{6,4},{7,5},{8,10},{9,11},{10,... | collective-permute-start | bytes 110600 | tf_op jit(solution)/shard_map/ppermute | solution.py:20
  120.4 2.3 %collective-permute-done.39 = bf16[16,1152]{1,0:T(8,128)(2,1)S(1)} collective-permute-done((bf16[16,1152]{1,0:T(8,128)(2,1)S(1)}, bf16[16,1152]{1,0:T(8,128)(2,1)S(1)}, u32[]{:S(2)}, u32[]{:S(2)}) %collective-permute-start.39) | collective-permute-done | bytes 36896 | tf_op jit(solution)/shard_map/ppermute | solution.py:20
  (157 shorter events, 26.0 us)
Async XLA Ops:
  2.2 6.5 %collective-permute-start.7 = (bf16[64,128]{1,0:T(8,128)(2,1)S(1)}, bf16[64,128]{1,0:T(8,128)(2,1)S(1)}, u32[]{:S(2)}, u32[]{:S(2)}) collective-permute-start(bf16[64,128]{1,0:T(8,128)(2,1)S(1)} %shard_map.142), channel_id=1, source_target_pairs={{0,1},{1,0},{2,3},{3,2},{4,5},{5,4},{6,7},{7,6},{8,9},{9,8},{10,11... | collective-permute-start | bytes 49160 | tf_op jit(solution)/shard_map/ppermute | solution.py:20
  5.2 23.1 %collective-permute-start.1 = (bf16[64,2304]{1,0:T(8,128)(2,1)}, bf16[64,2304]{1,0:T(8,128)(2,1)S(1)}, u32[]{:S(2)}, u32[]{:S(2)}) collective-permute-start(bf16[64,2304]{1,0:T(8,128)(2,1)} %refs_0_.1), channel_id=1, source_target_pairs={{0,8},{4,12},{8,0},{12,4},{16,24},{20,28},{24,16},{28,20},{1,9},{5... | collective-permute-start | bytes 884744 | tf_op jit(solution)/shard_map/ppermute | solution.py:20
  6.7 21.6 %collective-permute-start.3 = (bf16[64,2304]{1,0:T(8,128)(2,1)}, bf16[64,2304]{1,0:T(8,128)(2,1)S(1)}, u32[]{:S(2)}, u32[]{:S(2)}) collective-permute-start(bf16[64,2304]{1,0:T(8,128)(2,1)} %refs_0_.1), channel_id=1, source_target_pairs={{0,16},{4,20},{8,24},{12,28},{16,0},{20,4},{24,8},{28,12},{1,17},{... | collective-permute-start | bytes 884744 | tf_op jit(solution)/shard_map/ppermute | solution.py:20
  8.2 20.1 %collective-permute-start.5 = (bf16[64,2304]{1,0:T(8,128)(2,1)}, bf16[64,2304]{1,0:T(8,128)(2,1)S(1)}, u32[]{:S(2)}, u32[]{:S(2)}) collective-permute-start(bf16[64,2304]{1,0:T(8,128)(2,1)} %refs_0_.1), channel_id=1, source_target_pairs={{0,24},{4,28},{8,16},{12,20},{16,8},{20,12},{24,0},{28,4},{1,25},{... | collective-permute-start | bytes 884744 | tf_op jit(solution)/shard_map/ppermute | solution.py:20
  8.7 4.7 %collective-permute-start.8 = (bf16[64,128]{1,0:T(8,128)(2,1)S(1)}, bf16[64,128]{1,0:T(8,128)(2,1)S(1)}, u32[]{:S(2)}, u32[]{:S(2)}) collective-permute-start(bf16[64,128]{1,0:T(8,128)(2,1)S(1)} %add.184), channel_id=1, source_target_pairs={{0,2},{1,3},{2,0},{3,1},{4,6},{5,7},{6,4},{7,5},{8,10},{9,11},{10,... | collective-permute-start | bytes 49160 | tf_op jit(solution)/shard_map/ppermute | solution.py:20
  13.4 7.2 %collective-permute-start.9 = (bf16[64,128]{1,0:T(8,128)(2,1)S(1)}, bf16[64,128]{1,0:T(8,128)(2,1)S(1)}, u32[]{:S(2)}, u32[]{:S(2)}) collective-permute-start(bf16[64,128]{1,0:T(8,128)(2,1)S(1)} %add.185), channel_id=1, source_target_pairs={{0,8},{4,12},{8,0},{12,4},{16,24},{20,28},{24,16},{28,20},{1,9},{5... | collective-permute-start | bytes 49160 | tf_op jit(solution)/shard_map/ppermute | solution.py:20
  20.6 7.7 %collective-permute-start.10 = (bf16[128,128]{1,0:T(8,128)(2,1)S(1)}, bf16[128,128]{1,0:T(8,128)(2,1)S(1)}, u32[]{:S(2)}, u32[]{:S(2)}) collective-permute-start(bf16[128,128]{1,0:T(8,128)(2,1)S(1)} %pad_maximum_fusion.6), channel_id=1, source_target_pairs={{0,16},{4,20},{8,24},{12,28},{16,0},{20,4},{24,8},{28,12},{1,17},{... | collective-permute-start | bytes 98312 | tf_op jit(solution)/shard_map/ppermute | solution.py:20
  22.1 12.1 %collective-permute-start = (bf16[64,2304]{1,0:T(8,128)(2,1)}, bf16[64,2304]{1,0:T(8,128)(2,1)S(1)}, u32[]{:S(2)}, u32[]{:S(2)}) collective-permute-start(bf16[64,2304]{1,0:T(8,128)(2,1)} %refs_0_.1), channel_id=1, source_target_pairs={{0,4},{4,0},{8,12},{12,8},{16,20},{20,16},{24,28},{28,24},{1,5},{5... | collective-permute-start | bytes 884744 | tf_op jit(solution)/shard_map/ppermute | solution.py:20
  32.1 6.9 %collective-permute-start.12 = (bf16[256,1152]{1,0:T(8,128)(2,1)S(1)}, bf16[256,1152]{1,0:T(8,128)(2,1)S(1)}, u32[]{:S(2)}, u32[]{:S(2)}) collective-permute-start(bf16[256,1152]{1,0:T(8,128)(2,1)S(1)} %shard_map.144), channel_id=1, source_target_pairs={{0,4},{4,0},{8,12},{12,8},{16,20},{20,16},{24,28},{28,24},{1,5},{5... | collective-permute-start | bytes 1769480 | tf_op jit(solution)/shard_map/ppermute | solution.py:20
  32.6 2.1 %collective-permute-start.2 = (bf16[64,2304]{1,0:T(8,128)(2,1)S(1)}, bf16[64,2304]{1,0:T(8,128)(2,1)S(1)}, u32[]{:S(2)}, u32[]{:S(2)}) collective-permute-start(bf16[64,2304]{1,0:T(8,128)(2,1)S(1)} %collective-permute-done.1.refs_1_), channel_id=1, source_target_pairs={{0,4},{4,0},{8,12},{12,8},{16,20},{20,16},{24,28},{28,24},{1,5},{5... | collective-permute-start | bytes 884744 | tf_op jit(solution)/shard_map/ppermute | solution.py:20
  32.7 2.4 %collective-permute-start.4 = (bf16[64,2304]{1,0:T(8,128)(2,1)S(1)}, bf16[64,2304]{1,0:T(8,128)(2,1)S(1)}, u32[]{:S(2)}, u32[]{:S(2)}) collective-permute-start(bf16[64,2304]{1,0:T(8,128)(2,1)S(1)} %collective-permute-done.3.refs_2_), channel_id=1, source_target_pairs={{0,4},{4,0},{8,12},{12,8},{16,20},{20,16},{24,28},{28,24},{1,5},{5... | collective-permute-start | bytes 884744 | tf_op jit(solution)/shard_map/ppermute | solution.py:20
  33.1 2.4 %collective-permute-start.6 = (bf16[64,2304]{1,0:T(8,128)(2,1)S(1)}, bf16[64,2304]{1,0:T(8,128)(2,1)S(1)}, u32[]{:S(2)}, u32[]{:S(2)}) collective-permute-start(bf16[64,2304]{1,0:T(8,128)(2,1)S(1)} %collective-permute-done.5.refs_3_), channel_id=1, source_target_pairs={{0,4},{4,0},{8,12},{12,8},{16,20},{20,16},{24,28},{28,24},{1,5},{5... | collective-permute-start | bytes 884744 | tf_op jit(solution)/shard_map/ppermute | solution.py:20
  34.2 10.0 %collective-permute-start.23 = (bf16[256,1152]{1,0:T(8,128)(2,1)S(1)}, bf16[256,1152]{1,0:T(8,128)(2,1)S(1)}, u32[]{:S(2)}, u32[]{:S(2)}) collective-permute-start(bf16[256,1152]{1,0:T(8,128)(2,1)S(1)} %shard_map.148), channel_id=1, source_target_pairs={{0,4},{4,0},{8,12},{12,8},{16,20},{20,16},{24,28},{28,24},{1,5},{5... | collective-permute-start | bytes 1769480 | tf_op jit(solution)/shard_map/ppermute | solution.py:20
  34.7 4.2 %collective-permute-start.11 = (bf16[256,128]{1,0:T(8,128)(2,1)S(1)}, bf16[256,128]{1,0:T(8,128)(2,1)S(1)}, u32[]{:S(2)}, u32[]{:S(2)}) collective-permute-start(bf16[256,128]{1,0:T(8,128)(2,1)S(1)} %pad_maximum_fusion.5.table), channel_id=1, source_target_pairs={{0,4},{4,0},{8,12},{12,8},{16,20},{20,16},{24,28},{28,24},{1,5},{5... | collective-permute-start | bytes 196616 | tf_op jit(solution)/shard_map/ppermute | solution.py:20
  40.7 8.0 %collective-permute-start.13 = (bf16[64,1152]{1,0:T(8,128)(2,1)S(1)}, bf16[64,1152]{1,0:T(8,128)(2,1)S(1)}, u32[]{:S(2)}, u32[]{:S(2)}) collective-permute-start(bf16[64,1152]{1,0:T(8,128)(2,1)S(1)} %get-tuple-element.34), channel_id=1, source_target_pairs={{0,8},{4,12},{8,0},{12,4},{16,24},{20,28},{24,16},{28,20},{1,9},{5... | collective-permute-start | bytes 442376 | tf_op jit(solution)/shard_map/ppermute | solution.py:20
  42.1 10.5 %collective-permute-start.14 = (bf16[64,1152]{1,0:T(8,128)(2,1)}, bf16[64,1152]{1,0:T(8,128)(2,1)}, u32[]{:S(2)}, u32[]{:S(2)}) collective-permute-start(bf16[64,1152]{1,0:T(8,128)(2,1)} %get-tuple-element.35), channel_id=1, source_target_pairs={{0,16},{4,20},{8,24},{12,28},{16,0},{20,4},{24,8},{28,12},{1,17},{... | collective-permute-start | bytes 442376 | tf_op jit(solution)/shard_map/ppermute | solution.py:20
  42.7 9.9 %collective-permute-start.15 = (bf16[64,1152]{1,0:T(8,128)(2,1)}, bf16[64,1152]{1,0:T(8,128)(2,1)}, u32[]{:S(2)}, u32[]{:S(2)}) collective-permute-start(bf16[64,1152]{1,0:T(8,128)(2,1)} %get-tuple-element.36), channel_id=1, source_target_pairs={{0,24},{4,28},{8,16},{12,20},{16,8},{20,12},{24,0},{28,4},{1,25},{... | collective-permute-start | bytes 442376 | tf_op jit(solution)/shard_map/ppermute | solution.py:20
  46.6 9.4 %collective-permute-start.24 = (bf16[64,1152]{1,0:T(8,128)(2,1)}, bf16[64,1152]{1,0:T(8,128)(2,1)}, u32[]{:S(2)}, u32[]{:S(2)}) collective-permute-start(bf16[64,1152]{1,0:T(8,128)(2,1)} %get-tuple-element.41), channel_id=1, source_target_pairs={{0,8},{4,12},{8,0},{12,4},{16,24},{20,28},{24,16},{28,20},{1,9},{5... | collective-permute-start | bytes 442376 | tf_op jit(solution)/shard_map/ppermute | solution.py:20
  48.1 9.7 %collective-permute-start.25 = (bf16[64,1152]{1,0:T(8,128)(2,1)}, bf16[64,1152]{1,0:T(8,128)(2,1)}, u32[]{:S(2)}, u32[]{:S(2)}) collective-permute-start(bf16[64,1152]{1,0:T(8,128)(2,1)} %get-tuple-element.42), channel_id=1, source_target_pairs={{0,16},{4,20},{8,24},{12,28},{16,0},{20,4},{24,8},{28,12},{1,17},{... | collective-permute-start | bytes 442376 | tf_op jit(solution)/shard_map/ppermute | solution.py:20
  49.3 8.5 %collective-permute-start.26 = (bf16[64,1152]{1,0:T(8,128)(2,1)}, bf16[64,1152]{1,0:T(8,128)(2,1)}, u32[]{:S(2)}, u32[]{:S(2)}) collective-permute-start(bf16[64,1152]{1,0:T(8,128)(2,1)} %get-tuple-element.43), channel_id=1, source_target_pairs={{0,24},{4,28},{8,16},{12,20},{16,8},{20,12},{24,0},{28,4},{1,25},{... | collective-permute-start | bytes 442376 | tf_op jit(solution)/shard_map/ppermute | solution.py:20
  51.8 34.1 %copy-start.1 = (bf16[2304,512]{1,0:T(8,128)(2,1)S(1)}, bf16[2304,512]{1,0:T(8,128)(2,1)}, u32[]{:S(2)}) copy-start(bf16[2304,512]{1,0:T(8,128)(2,1)} %refs_2_.5) | copy-start | bytes 7077892
  51.8 34.1 %copy-start.15 = (f32[512]{0:T(512)S(1)}, f32[512]{0:T(512)}, u32[]{:S(2)}) copy-start(f32[512]{0:T(512)} %param.23) | copy-start | bytes 6148
  55.6 4.4 %collective-permute-start.16 = (bf16[32,1152]{1,0:T(8,128)(2,1)S(1)}, bf16[32,1152]{1,0:T(8,128)(2,1)S(1)}, u32[]{:S(2)}, u32[]{:S(2)}) collective-permute-start(bf16[32,1152]{1,0:T(8,128)(2,1)S(1)} %get-tuple-element.38), channel_id=1, source_target_pairs={{0,1},{1,0},{2,3},{3,2},{4,5},{5,4},{6,7},{7,6},{8,9},{9,8},{10,11... | collective-permute-start | bytes 221192 | tf_op jit(solution)/shard_map/ppermute | solution.py:20
  58.9 4.6 %collective-permute-start.27 = (bf16[32,1152]{1,0:T(8,128)(2,1)S(1)}, bf16[32,1152]{1,0:T(8,128)(2,1)S(1)}, u32[]{:S(2)}, u32[]{:S(2)}) collective-permute-start(bf16[32,1152]{1,0:T(8,128)(2,1)S(1)} %get-tuple-element.45), channel_id=1, source_target_pairs={{0,1},{1,0},{2,3},{3,2},{4,5},{5,4},{6,7},{7,6},{8,9},{9,8},{10,11... | collective-permute-start | bytes 221192 | tf_op jit(solution)/shard_map/ppermute | solution.py:20
  60.0 7.4 %collective-permute-start.17 = (bf16[2,16,1152]{2,1,0:T(8,128)(2,1)S(1)}, bf16[2,16,1152]{2,1,0:T(8,128)(2,1)S(1)}, u32[]{:S(2)}, u32[]{:S(2)}) collective-permute-start(bf16[2,16,1152]{2,1,0:T(8,128)(2,1)S(1)} %bitcast.106), channel_id=1, source_target_pairs={{0,2},{1,3},{2,0},{3,1},{4,6},{5,7},{6,4},{7,5},{8,10},{9,11},{10,... | collective-permute-start | bytes 221192 | tf_op jit(solution)/shard_map/ppermute | solution.py:20
  63.5 6.0 %collective-permute-start.28 = (bf16[2,16,1152]{2,1,0:T(8,128)(2,1)S(1)}, bf16[2,16,1152]{2,1,0:T(8,128)(2,1)S(1)}, u32[]{:S(2)}, u32[]{:S(2)}) collective-permute-start(bf16[2,16,1152]{2,1,0:T(8,128)(2,1)S(1)} %bitcast.108), channel_id=1, source_target_pairs={{0,2},{1,3},{2,0},{3,1},{4,6},{5,7},{6,4},{7,5},{8,10},{9,11},{10,... | collective-permute-start | bytes 221192 | tf_op jit(solution)/shard_map/ppermute | solution.py:20
  67.4 4.4 %collective-permute-start.18 = (bf16[2,16,1152]{2,1,0:T(8,128)(2,1)S(1)}, bf16[2,16,1152]{2,1,0:T(8,128)(2,1)S(1)}, u32[]{:S(2)}, u32[]{:S(2)}) collective-permute-start(bf16[2,16,1152]{2,1,0:T(8,128)(2,1)S(1)} %add_convert_fusion.2), channel_id=1, source_target_pairs={{0,1},{1,0},{2,3},{3,2},{4,5},{5,4},{6,7},{7,6},{8,9},{9,8},{10,11... | collective-permute-start | bytes 221192 | tf_op jit(solution)/shard_map/ppermute | solution.py:20
  69.6 5.9 %collective-permute-start.29 = (bf16[2,16,1152]{2,1,0:T(8,128)(2,1)S(1)}, bf16[2,16,1152]{2,1,0:T(8,128)(2,1)S(1)}, u32[]{:S(2)}, u32[]{:S(2)}) collective-permute-start(bf16[2,16,1152]{2,1,0:T(8,128)(2,1)S(1)} %add_convert_fusion), channel_id=1, source_target_pairs={{0,1},{1,0},{2,3},{3,2},{4,5},{5,4},{6,7},{7,6},{8,9},{9,8},{10,11... | collective-permute-start | bytes 221192 | tf_op jit(solution)/shard_map/ppermute | solution.py:20
  71.9 7.2 %collective-permute-start.21 = (bf16[2,2,16,1152]{3,2,1,0:T(8,128)(2,1)S(1)}, bf16[2,2,16,1152]{3,2,1,0:T(8,128)(2,1)S(1)}, u32[]{:S(2)}, u32[]{:S(2)}) collective-permute-start(bf16[2,2,16,1152]{3,2,1,0:T(8,128)(2,1)S(1)} %get-tuple-element.57), channel_id=1, source_target_pairs={{0,24},{4,28},{8,16},{12,20},{16,8},{20,12},{24,0},{28,4},{1,25},{... | collective-permute-start | bytes 442376 | tf_op jit(solution)/shard_map/ppermute | solution.py:20
  74.5 7.3 %collective-permute-start.20 = (bf16[2,2,16,1152]{3,2,1,0:T(8,128)(2,1)S(1)}, bf16[2,2,16,1152]{3,2,1,0:T(8,128)(2,1)S(1)}, u32[]{:S(2)}, u32[]{:S(2)}) collective-permute-start(bf16[2,2,16,1152]{3,2,1,0:T(8,128)(2,1)S(1)} %get-tuple-element.57), channel_id=1, source_target_pairs={{0,16},{4,20},{8,24},{12,28},{16,0},{20,4},{24,8},{28,12},{1,17},{... | collective-permute-start | bytes 442376 | tf_op jit(solution)/shard_map/ppermute | solution.py:20
  74.9 7.0 %collective-permute-start.19 = (bf16[2,2,16,1152]{3,2,1,0:T(8,128)(2,1)S(1)}, bf16[2,2,16,1152]{3,2,1,0:T(8,128)(2,1)S(1)}, u32[]{:S(2)}, u32[]{:S(2)}) collective-permute-start(bf16[2,2,16,1152]{3,2,1,0:T(8,128)(2,1)S(1)} %get-tuple-element.57), channel_id=1, source_target_pairs={{0,8},{4,12},{8,0},{12,4},{16,24},{20,28},{24,16},{28,20},{1,9},{5... | collective-permute-start | bytes 442376 | tf_op jit(solution)/shard_map/ppermute | solution.py:20
  75.5 8.0 %collective-permute-start.32 = (bf16[2,2,16,1152]{3,2,1,0:T(8,128)(2,1)S(1)}, bf16[2,2,16,1152]{3,2,1,0:T(8,128)(2,1)S(1)}, u32[]{:S(2)}, u32[]{:S(2)}) collective-permute-start(bf16[2,2,16,1152]{3,2,1,0:T(8,128)(2,1)S(1)} %get-tuple-element.55), channel_id=1, source_target_pairs={{0,24},{4,28},{8,16},{12,20},{16,8},{20,12},{24,0},{28,4},{1,25},{... | collective-permute-start | bytes 442376 | tf_op jit(solution)/shard_map/ppermute | solution.py:20
  78.1 6.9 %collective-permute-start.31 = (bf16[2,2,16,1152]{3,2,1,0:T(8,128)(2,1)S(1)}, bf16[2,2,16,1152]{3,2,1,0:T(8,128)(2,1)S(1)}, u32[]{:S(2)}, u32[]{:S(2)}) collective-permute-start(bf16[2,2,16,1152]{3,2,1,0:T(8,128)(2,1)S(1)} %get-tuple-element.55), channel_id=1, source_target_pairs={{0,16},{4,20},{8,24},{12,28},{16,0},{20,4},{24,8},{28,12},{1,17},{... | collective-permute-start | bytes 442376 | tf_op jit(solution)/shard_map/ppermute | solution.py:20
  79.1 5.9 %collective-permute-start.30 = (bf16[2,2,16,1152]{3,2,1,0:T(8,128)(2,1)S(1)}, bf16[2,2,16,1152]{3,2,1,0:T(8,128)(2,1)S(1)}, u32[]{:S(2)}, u32[]{:S(2)}) collective-permute-start(bf16[2,2,16,1152]{3,2,1,0:T(8,128)(2,1)S(1)} %get-tuple-element.55), channel_id=1, source_target_pairs={{0,8},{4,12},{8,0},{12,4},{16,24},{20,28},{24,16},{28,20},{1,9},{5... | collective-permute-start | bytes 442376 | tf_op jit(solution)/shard_map/ppermute | solution.py:20
  81.9 9.3 %collective-permute-start.22 = (bf16[256,1152]{1,0:T(8,128)(2,1)S(1)}, bf16[256,1152]{1,0:T(8,128)(2,1)}, u32[]{:S(2)}, u32[]{:S(2)}) collective-permute-start(bf16[256,1152]{1,0:T(8,128)(2,1)S(1)} %bitcast.62), channel_id=1, source_target_pairs={{0,4},{4,0},{8,12},{12,8},{16,20},{20,16},{24,28},{28,24},{1,5},{5... | collective-permute-start | bytes 1769480 | tf_op jit(solution)/shard_map/ppermute | solution.py:20
  85.9 5.3 %collective-permute-start.33 = (bf16[256,1152]{1,0:T(8,128)(2,1)}, bf16[256,1152]{1,0:T(8,128)(2,1)}, u32[]{:S(2)}, u32[]{:S(2)}) collective-permute-start(bf16[256,1152]{1,0:T(8,128)(2,1)} %bitcast.22.refs_1_), channel_id=1, source_target_pairs={{0,4},{4,0},{8,12},{12,8},{16,20},{20,16},{24,28},{28,24},{1,5},{5... | collective-permute-start | bytes 1769480 | tf_op jit(solution)/shard_map/ppermute | solution.py:20
  89.3 5.6 %collective-permute-start.40 = (bf16[256,1152]{1,0:T(8,128)(2,1)}, bf16[256,1152]{1,0:T(8,128)(2,1)}, u32[]{:S(2)}, u32[]{:S(2)}) collective-permute-start(bf16[256,1152]{1,0:T(8,128)(2,1)} %shard_map.155), channel_id=1, source_target_pairs={{0,4},{4,0},{8,12},{12,8},{16,20},{20,16},{24,28},{28,24},{1,5},{5... | collective-permute-start | bytes 1769480 | tf_op jit(solution)/shard_map/ppermute | solution.py:20
  91.2 8.9 %collective-permute-start.34 = (bf16[256,1152]{1,0:T(8,128)(2,1)}, bf16[256,1152]{1,0:T(8,128)(2,1)}, u32[]{:S(2)}, u32[]{:S(2)}) collective-permute-start(bf16[256,1152]{1,0:T(8,128)(2,1)} %shard_map.153), channel_id=1, source_target_pairs={{0,4},{4,0},{8,12},{12,8},{16,20},{20,16},{24,28},{28,24},{1,5},{5... | collective-permute-start | bytes 1769480 | tf_op jit(solution)/shard_map/ppermute | solution.py:20
  96.5 9.2 %collective-permute-start.43 = (bf16[64,1152]{1,0:T(8,128)(2,1)S(1)}, bf16[64,1152]{1,0:T(8,128)(2,1)S(1)}, u32[]{:S(2)}, u32[]{:S(2)}) collective-permute-start(bf16[64,1152]{1,0:T(8,128)(2,1)S(1)} %get-tuple-element.53), channel_id=1, source_target_pairs={{0,24},{4,28},{8,16},{12,20},{16,8},{20,12},{24,0},{28,4},{1,25},{... | collective-permute-start | bytes 442376 | tf_op jit(solution)/shard_map/ppermute | solution.py:20
  98.9 8.5 %collective-permute-start.42 = (bf16[64,1152]{1,0:T(8,128)(2,1)S(1)}, bf16[64,1152]{1,0:T(8,128)(2,1)S(1)}, u32[]{:S(2)}, u32[]{:S(2)}) collective-permute-start(bf16[64,1152]{1,0:T(8,128)(2,1)S(1)} %get-tuple-element.52), channel_id=1, source_target_pairs={{0,16},{4,20},{8,24},{12,28},{16,0},{20,4},{24,8},{28,12},{1,17},{... | collective-permute-start | bytes 442376 | tf_op jit(solution)/shard_map/ppermute | solution.py:20
  99.9 7.5 %collective-permute-start.41 = (bf16[64,1152]{1,0:T(8,128)(2,1)S(1)}, bf16[64,1152]{1,0:T(8,128)(2,1)S(1)}, u32[]{:S(2)}, u32[]{:S(2)}) collective-permute-start(bf16[64,1152]{1,0:T(8,128)(2,1)S(1)} %get-tuple-element.51), channel_id=1, source_target_pairs={{0,8},{4,12},{8,0},{12,4},{16,24},{20,28},{24,16},{28,20},{1,9},{5... | collective-permute-start | bytes 442376 | tf_op jit(solution)/shard_map/ppermute | solution.py:20
  101.7 8.8 %collective-permute-start.37 = (bf16[64,1152]{1,0:T(8,128)(2,1)S(1)}, bf16[64,1152]{1,0:T(8,128)(2,1)S(1)}, u32[]{:S(2)}, u32[]{:S(2)}) collective-permute-start(bf16[64,1152]{1,0:T(8,128)(2,1)S(1)} %get-tuple-element.49), channel_id=1, source_target_pairs={{0,24},{4,28},{8,16},{12,20},{16,8},{20,12},{24,0},{28,4},{1,25},{... | collective-permute-start | bytes 442376 | tf_op jit(solution)/shard_map/ppermute | solution.py:20
  104.0 9.2 %collective-permute-start.36 = (bf16[64,1152]{1,0:T(8,128)(2,1)S(1)}, bf16[64,1152]{1,0:T(8,128)(2,1)S(1)}, u32[]{:S(2)}, u32[]{:S(2)}) collective-permute-start(bf16[64,1152]{1,0:T(8,128)(2,1)S(1)} %get-tuple-element.48), channel_id=1, source_target_pairs={{0,16},{4,20},{8,24},{12,28},{16,0},{20,4},{24,8},{28,12},{1,17},{... | collective-permute-start | bytes 442376 | tf_op jit(solution)/shard_map/ppermute | solution.py:20
  105.7 7.5 %collective-permute-start.35 = (bf16[64,1152]{1,0:T(8,128)(2,1)S(1)}, bf16[64,1152]{1,0:T(8,128)(2,1)S(1)}, u32[]{:S(2)}, u32[]{:S(2)}) collective-permute-start(bf16[64,1152]{1,0:T(8,128)(2,1)S(1)} %get-tuple-element.47), channel_id=1, source_target_pairs={{0,8},{4,12},{8,0},{12,4},{16,24},{20,28},{24,16},{28,20},{1,9},{5... | collective-permute-start | bytes 442376 | tf_op jit(solution)/shard_map/ppermute | solution.py:20
  107.5 7.2 %collective-permute-start.44 = (bf16[2,16,1152]{2,1,0:T(8,128)(2,1)S(1)}, bf16[2,16,1152]{2,1,0:T(8,128)(2,1)S(1)}, u32[]{:S(2)}, u32[]{:S(2)}) collective-permute-start(bf16[2,16,1152]{2,1,0:T(8,128)(2,1)S(1)} %fusion.3), channel_id=1, source_target_pairs={{0,1},{1,0},{2,3},{3,2},{4,5},{5,4},{6,7},{7,6},{8,9},{9,8},{10,11... | collective-permute-start | bytes 221192 | tf_op jit(solution)/shard_map/ppermute | solution.py:20
  113.3 4.4 %collective-permute-start.38 = (bf16[2,16,1152]{2,1,0:T(8,128)(2,1)S(1)}, bf16[2,16,1152]{2,1,0:T(8,128)(2,1)S(1)}, u32[]{:S(2)}, u32[]{:S(2)}) collective-permute-start(bf16[2,16,1152]{2,1,0:T(8,128)(2,1)S(1)} %fusion.2), channel_id=1, source_target_pairs={{0,1},{1,0},{2,3},{3,2},{4,5},{5,4},{6,7},{7,6},{8,9},{9,8},{10,11... | collective-permute-start | bytes 221192 | tf_op jit(solution)/shard_map/ppermute | solution.py:20
  114.7 5.7 %collective-permute-start.45 = (bf16[16,1152]{1,0:T(8,128)(2,1)S(1)}, bf16[16,1152]{1,0:T(8,128)(2,1)S(1)}, u32[]{:S(2)}, u32[]{:S(2)}) collective-permute-start(bf16[16,1152]{1,0:T(8,128)(2,1)S(1)} %fusion.5), channel_id=1, source_target_pairs={{0,2},{1,3},{2,0},{3,1},{4,6},{5,7},{6,4},{7,5},{8,10},{9,11},{10,... | collective-permute-start | bytes 110600 | tf_op jit(solution)/shard_map/ppermute | solution.py:20
  117.8 4.9 %collective-permute-start.39 = (bf16[16,1152]{1,0:T(8,128)(2,1)S(1)}, bf16[16,1152]{1,0:T(8,128)(2,1)S(1)}, u32[]{:S(2)}, u32[]{:S(2)}) collective-permute-start(bf16[16,1152]{1,0:T(8,128)(2,1)S(1)} %fusion.4), channel_id=1, source_target_pairs={{0,2},{1,3},{2,0},{3,1},{4,6},{5,7},{6,4},{7,5},{8,10},{9,11},{10,... | collective-permute-start | bytes 110600 | tf_op jit(solution)/shard_map/ppermute | solution.py:20
  (18 other events, 131.9 us)

commit v7 on v6

v7 whole, which is shorter than its diff:
```python
import functools

import jax
import jax.numpy as jnp
from jax import lax
from jax.experimental import pallas as pl
from jax.experimental.pallas import tpu as pltpu
from jax.sharding import PartitionSpec as P

LANES = 128
MIB = 1024 * 1024
LOAD_MIB = 34
VMEM_SPEC = pl.BlockSpec(memory_space=pltpu.VMEM)
SMEM_SPEC = pl.BlockSpec(memory_space=pltpu.SMEM)
HBM_SPEC = pl.BlockSpec(memory_space=pltpu.HBM)


def swap(value, axis, r):
    return lax.ppermute(value, axis, [(i, i ^ r) for i in range(lax.axis_size(axis))])


def dot(a, b):
    return jnp.dot(a, b, preferred_element_type=jnp.float32)


def half(value):
    return value.astype(jnp.bfloat16)


def full(value):
    return value.astype(jnp.float32)


def silu(value):
    return value / (1.0 + jnp.exp(-value))


def bits_of(count):
    assert count & (count - 1) == 0
    return [1 << b for b in range(count.bit_length() - 1)]


def take(value, index, dim):
    return lax.dynamic_index_in_dim(value, index, dim, keepdims=False)


def call(body, operands, specs, outs, scratch, mib, cost):
    flops, moved = cost
    return pl.pallas_call(
        body,
        in_specs=specs,
        out_specs=[VMEM_SPEC] * len(outs),
        out_shape=[jax.ShapeDtypeStruct(shape, dtype) for shape, dtype in outs],
        scratch_shapes=scratch,
        compiler_params=pltpu.CompilerParams(vmem_limit_bytes=mib * MIB),
        cost_estimate=pl.CostEstimate(flops=flops, bytes_accessed=moved, transcendentals=0),
    )(*operands)


def start_all(pairs, sems):
    copies = [pltpu.make_async_copy(a, b, sems.at[i]) for i, (a, b) in enumerate(pairs)]
    for copy in copies:
        copy.start()
    return copies


def pack_kernel(feats, feat, ids, weights, out):
    top, own = ids.shape
    lane = lax.broadcasted_iota(jnp.int32, (top, LANES), 1)
    row = lax.broadcasted_iota(jnp.int32, (top, LANES), 0)
    high = half(weights[...])
    low = half(weights[...] - full(high))
    values = jnp.zeros((own, LANES), jnp.float32)
    for i, part in enumerate([half(full(ids[...])), high, low]):
        places = half(jnp.where(lane == row + i * top, 1.0, 0.0))
        values += lax.dot_general(
            part, places, (((0,), (0,)), ((), ())), preferred_element_type=jnp.float32
        )
    for f in range(feats):
        out[f * own : (f + 1) * own, :] = half(jnp.where(feat[0] == f, values, 0.0))


def run_pack(feat, expert_ids, gate_weights, feats):
    own, top = expert_ids.shape
    return call(
        functools.partial(pack_kernel, feats),
        [feat.reshape(1), expert_ids.T, gate_weights.T],
        [SMEM_SPEC, VMEM_SPEC, VMEM_SPEC],
        [((feats * own, LANES), jnp.bfloat16)],
        [],
        2,
        (6 * own * top * LANES, 2 * feats * own * LANES),
    )[0]


def load_kernel(count, x, table, *refs):
    sources, refs = refs[: count + 3], refs[count + 3 :]
    (shared_out, table_out), loaded = refs[:2], refs[2 : 2 + count]
    gate, up, down, sems = refs[2 + count :]
    copies = start_all(list(zip(sources, (gate, up, down) + loaded)), sems)
    table_out[...] = table[...]
    copies[0].wait()
    value = silu(dot(x[...], gate[...]))
    copies[1].wait()
    hidden = half(value * dot(x[...], up[...]))
    copies[2].wait()
    for j in range(0, shared_out.shape[1], 256):
        shared_out[:, j : j + 256] = dot(hidden, down[:, j : j + 256])
    for copy in copies[3:]:
        copy.wait()


def run_load(x, table, shared, values):
    count = len(values)
    outs = [((x.shape[0], shared[2].shape[1]), jnp.float32)]
    outs += [(value.shape, value.dtype) for value in [table] + values]
    return call(
        functools.partial(load_kernel, count),
        [x, table, *shared, *values],
        [VMEM_SPEC] * 2 + [HBM_SPEC] * (3 + count),
        outs,
        [pltpu.VMEM(w.shape, jnp.bfloat16) for w in shared]
        + [pltpu.SemaphoreType.DMA((3 + count,))],
        LOAD_MIB,
        (6 * x.shape[0] * shared[0].size, 4 * sum(value.size for value in values)),
    )


def hidden_kernel(count, e, tile, *refs):
    pieces, (gate, up, out, rows) = refs[:count], refs[count:]
    size = pieces[0].shape[0]
    for i in range(count):
        rows[i * size : (i + 1) * size, :] = pieces[i][...]
    for j in range(0, out.shape[1], tile):
        cut = slice(j, j + tile)
        value = silu(dot(rows[...], gate[e, :, cut]))
        out[:, cut] = half(value * dot(rows[...], up[e, :, cut]))


def run_hidden(pieces, gate, up, e):
    count, (size, width) = len(pieces), pieces[0].shape
    units = gate.shape[2]
    return call(
        functools.partial(hidden_kernel, count, e, min(256, units)),
        [*pieces, gate, up],
        [VMEM_SPEC] * (count + 2),
        [((count * size, units), jnp.bfloat16)],
        [pltpu.VMEM((count * size, width), jnp.bfloat16)],
        8,
        (4 * count * size * width * units, 4 * width * units),
    )[0]


def down_kernel(top, e, tile, kind, scalars, hidden, down, table, *refs):
    count = 1 if kind is None else 2 * kind[0]
    more, outs = refs[:-count], refs[-count:]
    entries = full(table[...])
    lane = lax.broadcasted_iota(jnp.int32, entries.shape, 1)
    expert = (scalars[0] * down.shape[0] + e).astype(jnp.float32)
    chosen = jnp.where((entries == expert) & (lane < top), 1.0, 0.0)
    chosen = pltpu.roll(chosen, top, 1) + pltpu.roll(chosen, 2 * top, 1)
    scale = jnp.sum(chosen * entries, axis=1, keepdims=True)
    for j in range(0, down.shape[2], tile):
        cut = slice(j, j + tile)
        value = dot(hidden[...], down[e, :, cut]) * scale
        if more:
            value += full(more[0][:, cut])
        if kind is None:
            outs[0][:, cut] = half(value)
            continue
        pairs, own = kind
        size = value.shape[0] // pairs
        for p in range(pairs):
            block = value[p * size : (p + 1) * size]
            if p == 0:
                block += more[1][:, cut]
            block = block.reshape(size // own // 2, 2, own, tile)
            low, high = block[:, 0].reshape(-1, tile), block[:, 1].reshape(-1, tile)
            outs[p][:, cut] = half(jnp.where(scalars[1] == 0, low, high))
            outs[pairs + p][:, cut] = half(jnp.where(scalars[1] == 0, high, low))


def run_down(hidden, down, e, scalars, table, top, more=(), kind=None):
    rows, units = hidden.shape
    width = down.shape[2]
    tile = 256 if width % 256 == 0 else 128
    outs = [((rows, width), jnp.bfloat16)]
    if kind is not None:
        outs = [((rows // kind[0] // 2, width), jnp.bfloat16)] * (2 * kind[0])
    return call(
        functools.partial(down_kernel, top, e, tile, kind),
        [scalars, hidden, down, table, *more],
        [SMEM_SPEC] + [VMEM_SPEC] * (3 + len(more)),
        outs,
        [],
        8,
        (2 * rows * units * width, 2 * units * width),
    )


def shards(
    tokens,
    expert_ids,
    gate_weights,
    expert_gate,
    expert_up,
    expert_down,
    shared_gate,
    shared_up,
    shared_down,
    encoder,
    encoder_bias,
    decoder,
    decoder_bias,
):
    own, top = expert_ids.shape
    width = tokens.shape[1]
    feats = lax.axis_size("feat")
    pairs = lax.axis_size("expert") // 2
    devices = 2 * pairs * feats
    local_experts = range(expert_gate.shape[0])
    me = lax.axis_index(("expert", "feat"))
    my_feat = lax.axis_index("feat")
    feat_bits = bits_of(feats)
    place = [(my_feat // bit) % 2 for bit in feat_bits]
    scalars = jnp.stack([me, place[0]])
    chunk_rows = pairs * feats // 2 * own

    table = run_pack(my_feat, expert_ids, gate_weights, feats)
    for bit in feat_bits:
        table = table + swap(table, "feat", bit)

    near = [tokens] + [swap(tokens, "expert", 2 * p) for p in range(1, pairs)]
    far = [swap(piece, "expert", 1) for piece in near]
    arrived = swap(table, "expert", 2)
    shared_out, table, near[0], expert_gate, expert_up, expert_down = run_load(
        far[0],
        table,
        [shared_gate, shared_up, shared_down],
        [tokens, expert_gate, expert_up, expert_down],
    )
    table = jnp.concatenate([table, arrived], axis=0)
    for bit in bits_of(pairs)[1:]:
        table = jnp.concatenate([table, swap(table, "expert", 2 * bit)], axis=0)
    table_far = swap(table, "expert", 1)

    arrived = None
    for e in local_experts:
        hidden = run_hidden(near, expert_gate, expert_up, e)
        more = [] if arrived is None else [arrived]
        arrived = run_down(hidden, expert_down, e, scalars, table, top, more)[0]
    arrived = swap(arrived, "expert", 1)
    for e in local_experts:
        hidden = run_hidden(far, expert_gate, expert_up, e)
        if e < local_experts[-1]:
            more = [arrived]
            arrived = run_down(hidden, expert_down, e, scalars, table_far, top, more)[0]
    blocks = run_down(
        hidden, expert_down, e, scalars, table_far, top, [arrived, shared_out], (pairs, own)
    )

    def reduce_pairs(parts):
        arrived = [swap(parts[p], "expert", 2 * p) for p in range(1, pairs)]
        return sum(full(part) for part in [parts[0]] + arrived)

    def gather_pairs(value):
        parts = [value] + [swap(value, "expert", 2 * p) for p in range(1, pairs)]
        return jnp.stack(parts).reshape(chunk_rows, width)

    arrived = swap(half(reduce_pairs(blocks[:pairs])), "feat", feat_bits[0])
    total = reduce_pairs(blocks[pairs:]) + full(arrived)
    total = total.reshape((2,) * (len(feat_bits) - 1) + (own, width))
    for i, bit in enumerate(feat_bits[1:-1]):
        dim = len(feat_bits) - 2 - i
        arrived = swap(half(take(total, 1 - place[i + 1], dim)), "feat", bit)
        total = take(total, place[i + 1], dim) + full(arrived)
    total = half(total)
    moe_out = half(full(total) + full(swap(total, "feat", feat_bits[-1])))
    for bit in feat_bits[-2:0:-1]:
        moe_out = jnp.stack([moe_out, swap(moe_out, "feat", bit)], axis=moe_out.ndim - 2)
    moe_out = moe_out.reshape(-1, width)
    near = [None, gather_pairs(moe_out)]
    near[0] = gather_pairs(swap(moe_out, "feat", feat_bits[0]))

    def encode(x):
        return half(jax.nn.relu(dot(x, encoder) + encoder_bias[None, :]))

    features = [None, None]
    arrived = None
    for chunk in (1, 0):
        far = swap(near[chunk], "expert", 1)
        features_near = encode(near[chunk])
        decoded = swap(half(dot(features_near, decoder)), "expert", 1)
        features_far = encode(far)
        total = dot(features_far, decoder) + full(decoded)
        total = total.reshape(pairs, feats // 2 * own, width)
        total = reduce_pairs([total[0]] + [half(total[p]) for p in range(1, pairs)])
        both = jnp.stack([features_far, features_near])
        features[chunk] = both.reshape(2, pairs, feats // 2, 1, own, -1)
        if chunk == 1:
            arrived = swap(half(total), "feat", feat_bits[0])
    total = (total + full(arrived)).reshape((2,) * (len(feat_bits) - 1) + (own, width))
    for bit in feat_bits[1:-1]:
        dim = len(total.shape) - 3
        arrived = swap(half(lax.index_in_dim(total, 1, dim, False)), "feat", bit)
        total = lax.index_in_dim(total, 0, dim, False) + full(arrived)
    arrived = swap(half(take(total, 1 - place[-1], 0)), "feat", feat_bits[-1])
    reconstruction = take(total, place[-1], 0) + full(arrived) + decoder_bias[None, :]

    features = jnp.concatenate(features, axis=3).transpose(1, 0, 2, 3, 4, 5)
    features = features.reshape(devices, own, -1)
    relative = me - me % feats + my_feat % (feats // 2)
    blocks = [lax.dynamic_index_in_dim(features, i ^ relative, 0) for i in range(devices)]
    features = jnp.concatenate(blocks, axis=0).reshape(devices * own, -1)
    return (features, reconstruction)


def solution(mesh):
    return jax.shard_map(
        shards,
        mesh=mesh,
        in_specs=(
            P("expert", None),
            P(("expert", "feat"), None),
            P(("expert", "feat"), None),
            P(("expert", "feat"), None, None),
            P(("expert", "feat"), None, None),
            P(("expert", "feat"), None, None),
            P(None, "feat"),
            P(None, "feat"),
            P("feat", None),
            P(None, ("expert", "feat")),
            P(("expert", "feat")),
            P(("expert", "feat"), None),
            P(),
        ),
        out_specs=(P(None, ("expert", "feat")), P(("expert", "feat"), None)),
        check_vma=False,
    )
```

time: 124 us -> 122 us (0.984)
  waiting for transfers between devices: 29.2 us -> 51.2 us
  Pallas kernels: 29.2 us -> 15.6 us
  starting transfers between devices: 52.4 us -> 39.2 us
  matrix products: 0 us -> 5.52 us
  local copies, waits for them, and re-layouts: 9.34 us -> 6.79 us
    ppermute x46 -> x40, waiting for transfers between devices: 29.2 us -> 51.2 us  [swap(): lax.ppermute(value, axis, [(i, i ^ r) for i in range(lax.axis_size(axis))])]
    pallas_call x17 -> x6, Pallas kernels: 29.2 us -> 15.6 us  [call(): pl.pallas_call(body, in_specs=specs, out_specs=[VMEM_SPEC] * len(outs), o...]
    ppermute x46 -> x40, starting transfers between devices: 52.4 us -> 39.2 us  [swap(): lax.ppermute(value, axis, [(i, i ^ r) for i in range(lax.axis_size(axis))])]
    dot_general x0 -> x8, matrix products: none -> 5.52 us  [dot(): return jnp.dot(a, b, preferred_element_type=jnp.float32)]
    unnamed x71 -> x55, local copies, waits for them, and re-layouts: 9.28 us -> 6.7 us
  transfers between devices with their start and end apart: 46 -> 40, of which waited for: 18 -> 19; matrix products, arithmetic and copies ran while one was open for 1% -> 6% of each run, Pallas kernels for 23% -> 10%
where the time goes in v7:
time: 122 us
  waiting for transfers between devices  51.2 us (42%)
  starting transfers between devices  39.2 us (32%)
  Pallas kernels  15.6 us (13%)
  local copies, waits for them, and re-layouts  6.79 us (6%)
  matrix products  5.52 us (5%)
  other arithmetic  2.05 us (2%)
  between operations  1.24 us (1%)
    ppermute x40, waiting for transfers between devices, swap(): lax.ppermute(value, axis, [(i, i ^ r) for i in range(lax.axis_size(axis))])  51.2 us
    ppermute x40, starting transfers between devices, swap(): lax.ppermute(value, axis, [(i, i ^ r) for i in range(lax.axis_size(axis))])  39.2 us
    pallas_call x6, Pallas kernels, call(): pl.pallas_call(body, in_specs=specs, out_specs=[VMEM_SPEC] * len(outs), o...  15.6 us
    unnamed x55, local copies, waits for them, and re-layouts  6.7 us
    dot_general x8, matrix products, dot(): return jnp.dot(a, b, preferred_element_type=jnp.float32)  5.52 us
  transfers between devices with their start and end apart: 40, of which 19 were waited for; matrix products, arithmetic and copies ran while one was open for 6% of the time, Pallas kernels for 10%

profile of v7, /device:TPU:0, one launch (start us, length us, event | category | flops | bytes accessed | tf_op | source)
XLA Modules:
  0.0 121.6 jit_solution(10716880636596204104)
XLA Ops:
  2.9 2.6 %collective-permute-start.7 = (bf16[64,128]{1,0:T(8,128)(2,1)S(1)}, bf16[64,128]{1,0:T(8,128)(2,1)}, u32[]{:S(2)}, u32[]{:S(2)}) collective-permute-start(bf16[64,128]{1,0:T(8,128)(2,1)S(1)} %shard_map.140), channel_id=1, source_target_pairs={{0,1},{1,0},{2,3},{3,2},{4,5},{5,4},{6,7},{7,6},{8,9},{9,8},{10,11... | collective-permute-start | bytes 49160 | tf_op jit(solution)/shard_map/ppermute | solution.py:19
  5.5 1.5 %collective-permute-start.1 = (bf16[64,2304]{1,0:T(8,128)(2,1)}, bf16[64,2304]{1,0:T(8,128)(2,1)S(1)}, u32[]{:S(2)}, u32[]{:S(2)}) collective-permute-start(bf16[64,2304]{1,0:T(8,128)(2,1)} %refs_3_.1), channel_id=1, source_target_pairs={{0,8},{4,12},{8,0},{12,4},{16,24},{20,28},{24,16},{28,20},{1,9},{5... | collective-permute-start | bytes 884744 | tf_op jit(solution)/shard_map/ppermute | solution.py:19
  7.0 1.5 %collective-permute-start.3 = (bf16[64,2304]{1,0:T(8,128)(2,1)}, bf16[64,2304]{1,0:T(8,128)(2,1)S(1)}, u32[]{:S(2)}, u32[]{:S(2)}) collective-permute-start(bf16[64,2304]{1,0:T(8,128)(2,1)} %refs_3_.1), channel_id=1, source_target_pairs={{0,16},{4,20},{8,24},{12,28},{16,0},{20,4},{24,8},{28,12},{1,17},{... | collective-permute-start | bytes 884744 | tf_op jit(solution)/shard_map/ppermute | solution.py:19
  9.7 2.6 %collective-permute-start.8 = (bf16[64,128]{1,0:T(8,128)(2,1)S(1)}, bf16[64,128]{1,0:T(8,128)(2,1)S(1)}, u32[]{:S(2)}, u32[]{:S(2)}) collective-permute-start(bf16[64,128]{1,0:T(8,128)(2,1)S(1)} %add.220), channel_id=1, source_target_pairs={{0,2},{1,3},{2,0},{3,1},{4,6},{5,7},{6,4},{7,5},{8,10},{9,11},{10,... | collective-permute-start | bytes 49160 | tf_op jit(solution)/shard_map/ppermute | solution.py:19
  12.3 2.0 %collective-permute-done.8 = bf16[64,128]{1,0:T(8,128)(2,1)S(1)} collective-permute-done((bf16[64,128]{1,0:T(8,128)(2,1)S(1)}, bf16[64,128]{1,0:T(8,128)(2,1)S(1)}, u32[]{:S(2)}, u32[]{:S(2)}) %collective-permute-start.8) | collective-permute-done | bytes 16416 | tf_op jit(solution)/shard_map/ppermute | solution.py:19
  14.3 1.6 %collective-permute-start.9 = (bf16[64,128]{1,0:T(8,128)(2,1)S(1)}, bf16[64,128]{1,0:T(8,128)(2,1)S(1)}, u32[]{:S(2)}, u32[]{:S(2)}) collective-permute-start(bf16[64,128]{1,0:T(8,128)(2,1)S(1)} %add.221.table), channel_id=1, source_target_pairs={{0,8},{4,12},{8,0},{12,4},{16,24},{20,28},{24,16},{28,20},{1,9},{5... | collective-permute-start | bytes 49160 | tf_op jit(solution)/shard_map/ppermute | solution.py:19
  16.0 1.3 %copy-done.1 = bf16[2304,256]{1,0:T(8,128)(2,1)S(1)} copy-done((bf16[2304,256]{1,0:T(8,128)(2,1)S(1)}, bf16[2304,256]{1,0:T(8,128)(2,1)}, u32[]{:S(2)}) %copy-start.1) | copy-done | bytes 1179672
  17.2 1.3 %copy-done.2 = bf16[2304,256]{1,0:T(8,128)(2,1)S(1)} copy-done((bf16[2304,256]{1,0:T(8,128)(2,1)S(1)}, bf16[2304,256]{1,0:T(8,128)(2,1)}, u32[]{:S(2)}) %copy-start.2) | copy-done | bytes 1179672
  18.5 1.3 %copy-done.3 = bf16[256,2304]{1,0:T(8,128)(2,1)S(1)} copy-done((bf16[256,2304]{1,0:T(8,128)(2,1)S(1)}, bf16[256,2304]{1,0:T(8,128)(2,1)}, u32[]{:S(2)}) %copy-start.3) | copy-done | bytes 1179672
  19.8 1.0 copy-done.4
  20.7 6.0 %shard_map.141 = (f32[64,2304]{1,0:T(8,128)S(1)}, bf16[64,128]{1,0:T(8,128)(2,1)S(1)}, bf16[64,2304]{1,0:T(8,128)(2,1)S(1)}, bf16[1,2304,1024]{2,1,0:T(8,128)(2,...) custom-call(bf16[64,2304]{1,0:T(8,128)(2,1)S(1)} %collective-permute-done.x.refs_0_, ...), custom_call_target="tpu_custom_call" | custom-call | flops 226492416 | bytes 28901376 | tf_op jit(solution)/shard_map/pallas_call | solution.py:49
  26.7 1.6 %collective-permute-start.10 = (bf16[128,128]{1,0:T(8,128)(2,1)S(1)}, bf16[128,128]{1,0:T(8,128)(2,1)S(1)}, u32[]{:S(2)}, u32[]{:S(2)}) collective-permute-start(bf16[128,128]{1,0:T(8,128)(2,1)S(1)} %pad_maximum_fusion.2), channel_id=1, source_target_pairs={{0,16},{4,20},{8,24},{12,28},{16,0},{20,4},{24,8},{28,12},{1,17},{... | collective-permute-start | bytes 98312 | tf_op jit(solution)/shard_map/ppermute | solution.py:19
  28.3 2.7 %shard_map.143.hidden = bf16[256,1024]{1,0:T(8,128)(2,1)S(1)} custom-call(bf16[64,2304]{1,0:T(8,128)(2,1)S(1)} %get-tuple-element.20.refs_0_, bf16[64,2304]{1,0:T(8,128)(2,1)S(1)} %collective-permute-done.1.refs_1_, bf16[64,2304]{1,0:T(8,128)(2,1)S(1)} %collective-permute-done.3.refs_2_, bf16[64,2304]{1,0:T(8,128)(2,1)S(1)} %collective-permute-done.5.refs_3_, ...), custom_call_target="tpu_custom_call" | custom-call | flops 2415919104 | bytes 9437184 | tf_op jit(solution)/shard_map/pallas_call | solution.py:49
  31.1 1.9 %shard_map.144 = bf16[256,2304]{1,0:T(8,128)(2,1)S(1)} custom-call(s32[2]{0:T(128)S(1)} %pad_add_fusion.scalars, bf16[256,1024]{1,0:T(8,128)(2,1)S(1)} %shard_map.143.hidden, bf16[1,1024,2304]{2,1,0:T(8,128)(2,1)S(1)} %get-tuple-element.18.down, bf16[256,128]{1,0:T(8,128)(2,1)S(1)} %constant_dynamic-update-slice_fusion.table), custom_call_target="tpu_custom_call" | custom-call | flops 1207959552 | bytes 4718592 | tf_op jit(solution)/shard_map/pallas_call | solution.py:49
  34.2 2.2 %collective-permute-done.2.refs_1_ = bf16[64,2304]{1,0:T(8,128)(2,1)S(1)} collective-permute-done((bf16[64,2304]{1,0:T(8,128)(2,1)S(1)}, bf16[64,2304]{1,0:T(8,128)(2,1)S(1)}, u32[]{:S(2)}, u32[]{:S(2)}) %collective-permute-start.2) | collective-permute-done | bytes 294944 | tf_op jit(solution)/shard_map/ppermute | solution.py:19
  37.2 2.7 %shard_map.142.hidden = bf16[256,1024]{1,0:T(8,128)(2,1)S(1)} custom-call(bf16[64,2304]{1,0:T(8,128)(2,1)S(1)} %collective-permute-done.x.refs_0_, bf16[64,2304]{1,0:T(8,128)(2,1)S(1)} %collective-permute-done.2.refs_1_, bf16[64,2304]{1,0:T(8,128)(2,1)S(1)} %collective-permute-done.4.refs_2_, bf16[64,2304]{1,0:T(8,128)(2,1)S(1)} %collective-permute-done.6.refs_3_, ...), custom_call_target="tpu_custom_call" | custom-call | flops 2415919104 | bytes 9437184 | tf_op jit(solution)/shard_map/pallas_call | solution.py:49
  40.0 2.1 %shard_map.145 = (bf16[32,2304]{1,0:T(8,128)(2,1)S(1)}, bf16[32,2304]{1,0:T(8,128)(2,1)S(1)}, bf16[32,2304]{1,0:T(8,128)(2,1)S(1)}, bf16[32,2304]{1,0:T(8,128)(2...) custom-call(s32[2]{0:T(128)S(1)} %pad_add_fusion.scalars, ...), custom_call_target="tpu_custom_call" | custom-call | flops 1207959552 | bytes 4718592 | tf_op jit(solution)/shard_map/pallas_call | solution.py:49
  42.1 1.1 collective-permute-start.18
  44.1 1.5 %collective-permute-start.16 = (bf16[32,2304]{1,0:T(8,128)(2,1)S(1)}, bf16[32,2304]{1,0:T(8,128)(2,1)S(1)}, u32[]{:S(2)}, u32[]{:S(2)}) collective-permute-start(bf16[32,2304]{1,0:T(8,128)(2,1)S(1)} %get-tuple-element.27), channel_id=1, source_target_pairs={{0,8},{4,12},{8,0},{12,4},{16,24},{20,28},{24,16},{28,20},{1,9},{5... | collective-permute-start | bytes 442376 | tf_op jit(solution)/shard_map/ppermute | solution.py:19
  45.6 1.1 collective-permute-start.15
  47.6 2.2 %collective-permute-done.18 = bf16[32,2304]{1,0:T(8,128)(2,1)S(1)} collective-permute-done((bf16[32,2304]{1,0:T(8,128)(2,1)S(1)}, bf16[32,2304]{1,0:T(8,128)(2,1)S(1)}, u32[]{:S(2)}, u32[]{:S(2)}) %collective-permute-start.18) | collective-permute-done | bytes 147488 | tf_op jit(solution)/shard_map/ppermute | solution.py:19
  50.3 2.7 %collective-permute-done.17 = bf16[32,2304]{1,0:T(8,128)(2,1)S(1)} collective-permute-done((bf16[32,2304]{1,0:T(8,128)(2,1)S(1)}, bf16[32,2304]{1,0:T(8,128)(2,1)S(1)}, u32[]{:S(2)}, u32[]{:S(2)}) %collective-permute-start.17) | collective-permute-done | bytes 147488 | tf_op jit(solution)/shard_map/ppermute | solution.py:19
  53.5 2.6 %collective-permute-done.15 = bf16[32,2304]{1,0:T(8,128)(2,1)S(1)} collective-permute-done((bf16[32,2304]{1,0:T(8,128)(2,1)S(1)}, bf16[32,2304]{1,0:T(8,128)(2,1)S(1)}, u32[]{:S(2)}, u32[]{:S(2)}) %collective-permute-start.15) | collective-permute-done | bytes 147488 | tf_op jit(solution)/shard_map/ppermute | solution.py:19
  56.2 2.2 %collective-permute-done.14 = bf16[32,2304]{1,0:T(8,128)(2,1)S(1)} collective-permute-done((bf16[32,2304]{1,0:T(8,128)(2,1)S(1)}, bf16[32,2304]{1,0:T(8,128)(2,1)S(1)}, u32[]{:S(2)}, u32[]{:S(2)}) %collective-permute-start.14) | collective-permute-done | bytes 147488 | tf_op jit(solution)/shard_map/ppermute | solution.py:19
  58.4 2.6 %collective-permute-start.20 = (bf16[2,16,2304]{2,1,0:T(8,128)(2,1)S(1)}, bf16[2,16,2304]{2,1,0:T(8,128)(2,1)S(1)}, u32[]{:S(2)}, u32[]{:S(2)}) collective-permute-start(bf16[2,16,2304]{2,1,0:T(8,128)(2,1)S(1)} %bitcast.105), channel_id=1, source_target_pairs={{0,2},{1,3},{2,0},{3,1},{4,6},{5,7},{6,4},{7,5},{8,10},{9,11},{10,... | collective-permute-start | bytes 442376 | tf_op jit(solution)/shard_map/ppermute | solution.py:19
  61.0 7.0 %collective-permute-done.20 = bf16[2,16,2304]{2,1,0:T(8,128)(2,1)S(1)} collective-permute-done((bf16[2,16,2304]{2,1,0:T(8,128)(2,1)S(1)}, bf16[2,16,2304]{2,1,0:T(8,128)(2,1)S(1)}, u32[]{:S(2)}, u32[]{:S(2)}) %collective-permute-start.20) | collective-permute-done | bytes 147488 | tf_op jit(solution)/shard_map/ppermute | solution.py:19
  68.1 1.3 %collective-permute-start.28 = (bf16[32,2304]{1,0:T(8,128)(2,1)S(1)}, bf16[32,2304]{1,0:T(8,128)(2,1)S(1)}, u32[]{:S(2)}, u32[]{:S(2)}) collective-permute-start(bf16[32,2304]{1,0:T(8,128)(2,1)S(1)} %bitcast.100), channel_id=1, source_target_pairs={{0,24},{4,28},{8,16},{12,20},{16,8},{20,12},{24,0},{28,4},{1,25},{... | collective-permute-start | bytes 442376 | tf_op jit(solution)/shard_map/ppermute | solution.py:19
  69.4 0.9 collective-permute-start.27
  70.4 1.3 %collective-permute-start.26 = (bf16[32,2304]{1,0:T(8,128)(2,1)S(1)}, bf16[32,2304]{1,0:T(8,128)(2,1)S(1)}, u32[]{:S(2)}, u32[]{:S(2)}) collective-permute-start(bf16[32,2304]{1,0:T(8,128)(2,1)S(1)} %bitcast.102), channel_id=1, source_target_pairs={{0,8},{4,12},{8,0},{12,4},{16,24},{20,28},{24,16},{28,20},{1,9},{5... | collective-permute-start | bytes 442376 | tf_op jit(solution)/shard_map/ppermute | solution.py:19
  71.7 4.2 %collective-permute-done.28 = bf16[32,2304]{1,0:T(8,128)(2,1)S(1)} collective-permute-done((bf16[32,2304]{1,0:T(8,128)(2,1)S(1)}, bf16[32,2304]{1,0:T(8,128)(2,1)S(1)}, u32[]{:S(2)}, u32[]{:S(2)}) %collective-permute-start.28) | collective-permute-done | bytes 147488 | tf_op jit(solution)/shard_map/ppermute | solution.py:19
  75.8 2.2 %collective-permute-done.27 = bf16[32,2304]{1,0:T(8,128)(2,1)S(1)} collective-permute-done((bf16[32,2304]{1,0:T(8,128)(2,1)S(1)}, bf16[32,2304]{1,0:T(8,128)(2,1)S(1)}, u32[]{:S(2)}, u32[]{:S(2)}) %collective-permute-start.27) | collective-permute-done | bytes 147488 | tf_op jit(solution)/shard_map/ppermute | solution.py:19
  78.2 2.1 %fusion.4 = bf16[128,512]{1,0:T(8,128)(2,1)S(1)} fusion(bf16[128,2304]{1,0:T(8,128)(2,1)S(1)} %bitcast.61, bf16[2304,512]{1,0:T(8,128)(2,1)} %param.22, f32[512]{0:T(512)S(1)} %copy-done.8), kind=kOutput, calls=%fused_computation.12 | convolution fusion | flops 302186496 | bytes 3082240 | tf_op jit(solution)/shard_map/dot_general | solution.py:23
  80.3 1.3 %collective-permute-start.24 = (bf16[32,2304]{1,0:T(8,128)(2,1)S(1)}, bf16[32,2304]{1,0:T(8,128)(2,1)S(1)}, u32[]{:S(2)}, u32[]{:S(2)}) collective-permute-start(bf16[32,2304]{1,0:T(8,128)(2,1)S(1)} %collective-permute-done.21), channel_id=1, source_target_pairs={{0,24},{4,28},{8,16},{12,20},{16,8},{20,12},{24,0},{28,4},{1,25},{... | collective-permute-start | bytes 442376 | tf_op jit(solution)/shard_map/ppermute | solution.py:19
  81.7 0.9 collective-permute-start.23
  82.6 1.3 %collective-permute-start.22 = (bf16[32,2304]{1,0:T(8,128)(2,1)S(1)}, bf16[32,2304]{1,0:T(8,128)(2,1)S(1)}, u32[]{:S(2)}, u32[]{:S(2)}) collective-permute-start(bf16[32,2304]{1,0:T(8,128)(2,1)S(1)} %collective-permute-done.21), channel_id=1, source_target_pairs={{0,8},{4,12},{8,0},{12,4},{16,24},{20,28},{24,16},{28,20},{1,9},{5... | collective-permute-start | bytes 442376 | tf_op jit(solution)/shard_map/ppermute | solution.py:19
  84.5 3.5 %collective-permute-done.24 = bf16[32,2304]{1,0:T(8,128)(2,1)S(1)} collective-permute-done((bf16[32,2304]{1,0:T(8,128)(2,1)S(1)}, bf16[32,2304]{1,0:T(8,128)(2,1)S(1)}, u32[]{:S(2)}, u32[]{:S(2)}) %collective-permute-start.24) | collective-permute-done | bytes 147488 | tf_op jit(solution)/shard_map/ppermute | solution.py:19
  88.0 2.7 %collective-permute-done.23 = bf16[32,2304]{1,0:T(8,128)(2,1)S(1)} collective-permute-done((bf16[32,2304]{1,0:T(8,128)(2,1)S(1)}, bf16[32,2304]{1,0:T(8,128)(2,1)S(1)}, u32[]{:S(2)}, u32[]{:S(2)}) %collective-permute-start.23) | collective-permute-done | bytes 147488 | tf_op jit(solution)/shard_map/ppermute | solution.py:19
  92.4 1.3 %collective-permute-start.37 = (bf16[32,2304]{1,0:T(8,128)(2,1)S(1)}, bf16[32,2304]{1,0:T(8,128)(2,1)S(1)}, u32[]{:S(2)}, u32[]{:S(2)}) collective-permute-start(bf16[32,2304]{1,0:T(8,128)(2,1)S(1)} %get-tuple-element.38), channel_id=1, source_target_pairs={{0,24},{4,28},{8,16},{12,20},{16,8},{20,12},{24,0},{28,4},{1,25},{... | collective-permute-start | bytes 442376 | tf_op jit(solution)/shard_map/ppermute | solution.py:19
  93.8 0.9 collective-permute-start.36
  94.7 1.3 %collective-permute-start.35 = (bf16[32,2304]{1,0:T(8,128)(2,1)S(1)}, bf16[32,2304]{1,0:T(8,128)(2,1)S(1)}, u32[]{:S(2)}, u32[]{:S(2)}) collective-permute-start(bf16[32,2304]{1,0:T(8,128)(2,1)S(1)} %get-tuple-element.37), channel_id=1, source_target_pairs={{0,8},{4,12},{8,0},{12,4},{16,24},{20,28},{24,16},{28,20},{1,9},{5... | collective-permute-start | bytes 442376 | tf_op jit(solution)/shard_map/ppermute | solution.py:19
  96.5 3.5 %collective-permute-done.37 = bf16[32,2304]{1,0:T(8,128)(2,1)S(1)} collective-permute-done((bf16[32,2304]{1,0:T(8,128)(2,1)S(1)}, bf16[32,2304]{1,0:T(8,128)(2,1)S(1)}, u32[]{:S(2)}, u32[]{:S(2)}) %collective-permute-start.37) | collective-permute-done | bytes 147488 | tf_op jit(solution)/shard_map/ppermute | solution.py:19
  100.1 2.7 %collective-permute-done.36 = bf16[32,2304]{1,0:T(8,128)(2,1)S(1)} collective-permute-done((bf16[32,2304]{1,0:T(8,128)(2,1)S(1)}, bf16[32,2304]{1,0:T(8,128)(2,1)S(1)}, u32[]{:S(2)}, u32[]{:S(2)}) %collective-permute-start.36) | collective-permute-done | bytes 147488 | tf_op jit(solution)/shard_map/ppermute | solution.py:19
  104.0 1.4 %collective-permute-start.33 = (bf16[32,2304]{1,0:T(8,128)(2,1)S(1)}, bf16[32,2304]{1,0:T(8,128)(2,1)S(1)}, u32[]{:S(2)}, u32[]{:S(2)}) collective-permute-start(bf16[32,2304]{1,0:T(8,128)(2,1)S(1)} %get-tuple-element.35), channel_id=1, source_target_pairs={{0,24},{4,28},{8,16},{12,20},{16,8},{20,12},{24,0},{28,4},{1,25},{... | collective-permute-start | bytes 442376 | tf_op jit(solution)/shard_map/ppermute | solution.py:19
  106.2 1.3 %collective-permute-start.31 = (bf16[32,2304]{1,0:T(8,128)(2,1)S(1)}, bf16[32,2304]{1,0:T(8,128)(2,1)S(1)}, u32[]{:S(2)}, u32[]{:S(2)}) collective-permute-start(bf16[32,2304]{1,0:T(8,128)(2,1)S(1)} %get-tuple-element.34), channel_id=1, source_target_pairs={{0,8},{4,12},{8,0},{12,4},{16,24},{20,28},{24,16},{28,20},{1,9},{5... | collective-permute-start | bytes 442376 | tf_op jit(solution)/shard_map/ppermute | solution.py:19
  108.7 3.0 %collective-permute-done.33 = bf16[32,2304]{1,0:T(8,128)(2,1)S(1)} collective-permute-done((bf16[32,2304]{1,0:T(8,128)(2,1)S(1)}, bf16[32,2304]{1,0:T(8,128)(2,1)S(1)}, u32[]{:S(2)}, u32[]{:S(2)}) %collective-permute-start.33) | collective-permute-done | bytes 147488 | tf_op jit(solution)/shard_map/ppermute | solution.py:19
  111.7 2.2 %collective-permute-done.32 = bf16[32,2304]{1,0:T(8,128)(2,1)S(1)} collective-permute-done((bf16[32,2304]{1,0:T(8,128)(2,1)S(1)}, bf16[32,2304]{1,0:T(8,128)(2,1)S(1)}, u32[]{:S(2)}, u32[]{:S(2)}) %collective-permute-start.32) | collective-permute-done | bytes 147488 | tf_op jit(solution)/shard_map/ppermute | solution.py:19
  114.0 2.0 %collective-permute-start.39 = (bf16[16,2304]{1,0:T(8,128)(2,1)S(1)}, bf16[16,2304]{1,0:T(8,128)(2,1)S(1)}, u32[]{:S(2)}, u32[]{:S(2)}) collective-permute-start(bf16[16,2304]{1,0:T(8,128)(2,1)S(1)} %fusion.15), channel_id=1, source_target_pairs={{0,2},{1,3},{2,0},{3,1},{4,6},{5,7},{6,4},{7,5},{8,10},{9,11},{10,... | collective-permute-start | bytes 221192 | tf_op jit(solution)/shard_map/ppermute | solution.py:19
  116.0 4.9 %collective-permute-done.39 = bf16[16,2304]{1,0:T(8,128)(2,1)S(1)} collective-permute-done((bf16[16,2304]{1,0:T(8,128)(2,1)S(1)}, bf16[16,2304]{1,0:T(8,128)(2,1)S(1)}, u32[]{:S(2)}, u32[]{:S(2)}) %collective-permute-start.39) | collective-permute-done | bytes 73760 | tf_op jit(solution)/shard_map/ppermute | solution.py:19
  (119 shorter events, 15.3 us)
Async XLA Ops:
  0.6 83.3 %copy-start = (bf16[512,2304]{1,0:T(8,128)(2,1)S(1)}, bf16[512,2304]{1,0:T(8,128)(2,1)}, u32[]{:S(2)}) copy-start(bf16[512,2304]{1,0:T(8,128)(2,1)} %param.24) | copy-start | bytes 7077892
  0.6 15.3 %collective-permute-start = (bf16[64,2304]{1,0:T(8,128)(2,1)}, bf16[64,2304]{1,0:T(8,128)(2,1)S(1)}, u32[]{:S(2)}, u32[]{:S(2)}) collective-permute-start(bf16[64,2304]{1,0:T(8,128)(2,1)} %refs_3_.1), channel_id=1, source_target_pairs={{0,4},{4,0},{8,12},{12,8},{16,20},{20,16},{24,28},{28,24},{1,5},{5... | collective-permute-start | bytes 884744 | tf_op jit(solution)/shard_map/ppermute | solution.py:19
  2.9 6.1 %collective-permute-start.7 = (bf16[64,128]{1,0:T(8,128)(2,1)S(1)}, bf16[64,128]{1,0:T(8,128)(2,1)}, u32[]{:S(2)}, u32[]{:S(2)}) collective-permute-start(bf16[64,128]{1,0:T(8,128)(2,1)S(1)} %shard_map.140), channel_id=1, source_target_pairs={{0,1},{1,0},{2,3},{3,2},{4,5},{5,4},{6,7},{7,6},{8,9},{9,8},{10,11... | collective-permute-start | bytes 49160 | tf_op jit(solution)/shard_map/ppermute | solution.py:19
  5.5 22.8 %collective-permute-start.1 = (bf16[64,2304]{1,0:T(8,128)(2,1)}, bf16[64,2304]{1,0:T(8,128)(2,1)S(1)}, u32[]{:S(2)}, u32[]{:S(2)}) collective-permute-start(bf16[64,2304]{1,0:T(8,128)(2,1)} %refs_3_.1), channel_id=1, source_target_pairs={{0,8},{4,12},{8,0},{12,4},{16,24},{20,28},{24,16},{28,20},{1,9},{5... | collective-permute-start | bytes 884744 | tf_op jit(solution)/shard_map/ppermute | solution.py:19
  7.0 21.4 %collective-permute-start.3 = (bf16[64,2304]{1,0:T(8,128)(2,1)}, bf16[64,2304]{1,0:T(8,128)(2,1)S(1)}, u32[]{:S(2)}, u32[]{:S(2)}) collective-permute-start(bf16[64,2304]{1,0:T(8,128)(2,1)} %refs_3_.1), channel_id=1, source_target_pairs={{0,16},{4,20},{8,24},{12,28},{16,0},{20,4},{24,8},{28,12},{1,17},{... | collective-permute-start | bytes 884744 | tf_op jit(solution)/shard_map/ppermute | solution.py:19
  8.5 19.8 %collective-permute-start.5 = (bf16[64,2304]{1,0:T(8,128)(2,1)}, bf16[64,2304]{1,0:T(8,128)(2,1)S(1)}, u32[]{:S(2)}, u32[]{:S(2)}) collective-permute-start(bf16[64,2304]{1,0:T(8,128)(2,1)} %refs_3_.1), channel_id=1, source_target_pairs={{0,24},{4,28},{8,16},{12,20},{16,8},{20,12},{24,0},{28,4},{1,25},{... | collective-permute-start | bytes 884744 | tf_op jit(solution)/shard_map/ppermute | solution.py:19
  9.7 4.6 %collective-permute-start.8 = (bf16[64,128]{1,0:T(8,128)(2,1)S(1)}, bf16[64,128]{1,0:T(8,128)(2,1)S(1)}, u32[]{:S(2)}, u32[]{:S(2)}) collective-permute-start(bf16[64,128]{1,0:T(8,128)(2,1)S(1)} %add.220), channel_id=1, source_target_pairs={{0,2},{1,3},{2,0},{3,1},{4,6},{5,7},{6,4},{7,5},{8,10},{9,11},{10,... | collective-permute-start | bytes 49160 | tf_op jit(solution)/shard_map/ppermute | solution.py:19
  14.3 12.4 %collective-permute-start.9 = (bf16[64,128]{1,0:T(8,128)(2,1)S(1)}, bf16[64,128]{1,0:T(8,128)(2,1)S(1)}, u32[]{:S(2)}, u32[]{:S(2)}) collective-permute-start(bf16[64,128]{1,0:T(8,128)(2,1)S(1)} %add.221.table), channel_id=1, source_target_pairs={{0,8},{4,12},{8,0},{12,4},{16,24},{20,28},{24,16},{28,20},{1,9},{5... | collective-permute-start | bytes 49160 | tf_op jit(solution)/shard_map/ppermute | solution.py:19
  16.0 1.3 %copy-start.1 = (bf16[2304,256]{1,0:T(8,128)(2,1)S(1)}, bf16[2304,256]{1,0:T(8,128)(2,1)}, u32[]{:S(2)}) copy-start(bf16[2304,256]{1,0:T(8,128)(2,1)} %refs_0_.1) | copy-start | bytes 3538948
  17.2 1.3 %copy-start.2 = (bf16[2304,256]{1,0:T(8,128)(2,1)S(1)}, bf16[2304,256]{1,0:T(8,128)(2,1)}, u32[]{:S(2)}) copy-start(bf16[2304,256]{1,0:T(8,128)(2,1)} %refs_1_.1) | copy-start | bytes 3538948
  18.5 1.3 %copy-start.3 = (bf16[256,2304]{1,0:T(8,128)(2,1)S(1)}, bf16[256,2304]{1,0:T(8,128)(2,1)}, u32[]{:S(2)}) copy-start(bf16[256,2304]{1,0:T(8,128)(2,1)} %refs_2_.1) | copy-start | bytes 3538948
  26.7 4.4 %collective-permute-start.10 = (bf16[128,128]{1,0:T(8,128)(2,1)S(1)}, bf16[128,128]{1,0:T(8,128)(2,1)S(1)}, u32[]{:S(2)}, u32[]{:S(2)}) collective-permute-start(bf16[128,128]{1,0:T(8,128)(2,1)S(1)} %pad_maximum_fusion.2), channel_id=1, source_target_pairs={{0,16},{4,20},{8,24},{12,28},{16,0},{20,4},{24,8},{28,12},{1,17},{... | collective-permute-start | bytes 98312 | tf_op jit(solution)/shard_map/ppermute | solution.py:19
  33.0 6.9 %collective-permute-start.12 = (bf16[256,2304]{1,0:T(8,128)(2,1)S(1)}, bf16[256,2304]{1,0:T(8,128)(2,1)S(1)}, u32[]{:S(2)}, u32[]{:S(2)}) collective-permute-start(bf16[256,2304]{1,0:T(8,128)(2,1)S(1)} %shard_map.144), channel_id=1, source_target_pairs={{0,4},{4,0},{8,12},{12,8},{16,20},{20,16},{24,28},{28,24},{1,5},{5... | collective-permute-start | bytes 3538952 | tf_op jit(solution)/shard_map/ppermute | solution.py:19
  33.1 3.3 %collective-permute-start.2 = (bf16[64,2304]{1,0:T(8,128)(2,1)S(1)}, bf16[64,2304]{1,0:T(8,128)(2,1)S(1)}, u32[]{:S(2)}, u32[]{:S(2)}) collective-permute-start(bf16[64,2304]{1,0:T(8,128)(2,1)S(1)} %collective-permute-done.1.refs_1_), channel_id=1, source_target_pairs={{0,4},{4,0},{8,12},{12,8},{16,20},{20,16},{24,28},{28,24},{1,5},{5... | collective-permute-start | bytes 884744 | tf_op jit(solution)/shard_map/ppermute | solution.py:19
  33.6 3.2 %collective-permute-start.4 = (bf16[64,2304]{1,0:T(8,128)(2,1)S(1)}, bf16[64,2304]{1,0:T(8,128)(2,1)S(1)}, u32[]{:S(2)}, u32[]{:S(2)}) collective-permute-start(bf16[64,2304]{1,0:T(8,128)(2,1)S(1)} %collective-permute-done.3.refs_2_), channel_id=1, source_target_pairs={{0,4},{4,0},{8,12},{12,8},{16,20},{20,16},{24,28},{28,24},{1,5},{5... | collective-permute-start | bytes 884744 | tf_op jit(solution)/shard_map/ppermute | solution.py:19
  33.7 3.5 %collective-permute-start.6 = (bf16[64,2304]{1,0:T(8,128)(2,1)S(1)}, bf16[64,2304]{1,0:T(8,128)(2,1)S(1)}, u32[]{:S(2)}, u32[]{:S(2)}) collective-permute-start(bf16[64,2304]{1,0:T(8,128)(2,1)S(1)} %collective-permute-done.5.refs_3_), channel_id=1, source_target_pairs={{0,4},{4,0},{8,12},{12,8},{16,20},{20,16},{24,28},{28,24},{1,5},{5... | collective-permute-start | bytes 884744 | tf_op jit(solution)/shard_map/ppermute | solution.py:19
  34.1 5.8 %collective-permute-start.11 = (bf16[256,128]{1,0:T(8,128)(2,1)S(1)}, bf16[256,128]{1,0:T(8,128)(2,1)S(1)}, u32[]{:S(2)}, u32[]{:S(2)}) collective-permute-start(bf16[256,128]{1,0:T(8,128)(2,1)S(1)} %constant_dynamic-update-slice_fusion.table), channel_id=1, source_target_pairs={{0,4},{4,0},{8,12},{12,8},{16,20},{20,16},{24,28},{28,24},{1,5},{5... | collective-permute-start | bytes 196616 | tf_op jit(solution)/shard_map/ppermute | solution.py:19
  42.1 36.1 %copy-start.8 = (f32[512]{0:T(512)S(1)}, f32[512]{0:T(512)}, u32[]{:S(2)}) copy-start(f32[512]{0:T(512)} %param.23) | copy-start | bytes 6148
  42.1 7.7 %collective-permute-start.18 = (bf16[32,2304]{1,0:T(8,128)(2,1)S(1)}, bf16[32,2304]{1,0:T(8,128)(2,1)S(1)}, u32[]{:S(2)}, u32[]{:S(2)}) collective-permute-start(bf16[32,2304]{1,0:T(8,128)(2,1)S(1)} %get-tuple-element.29), channel_id=1, source_target_pairs={{0,24},{4,28},{8,16},{12,20},{16,8},{20,12},{24,0},{28,4},{1,25},{... | collective-permute-start | bytes 442376 | tf_op jit(solution)/shard_map/ppermute | solution.py:19
  43.2 9.8 %collective-permute-start.17 = (bf16[32,2304]{1,0:T(8,128)(2,1)S(1)}, bf16[32,2304]{1,0:T(8,128)(2,1)S(1)}, u32[]{:S(2)}, u32[]{:S(2)}) collective-permute-start(bf16[32,2304]{1,0:T(8,128)(2,1)S(1)} %get-tuple-element.28), channel_id=1, source_target_pairs={{0,16},{4,20},{8,24},{12,28},{16,0},{20,4},{24,8},{28,12},{1,17},{... | collective-permute-start | bytes 442376 | tf_op jit(solution)/shard_map/ppermute | solution.py:19
  44.1 8.9 %collective-permute-start.16 = (bf16[32,2304]{1,0:T(8,128)(2,1)S(1)}, bf16[32,2304]{1,0:T(8,128)(2,1)S(1)}, u32[]{:S(2)}, u32[]{:S(2)}) collective-permute-start(bf16[32,2304]{1,0:T(8,128)(2,1)S(1)} %get-tuple-element.27), channel_id=1, source_target_pairs={{0,8},{4,12},{8,0},{12,4},{16,24},{20,28},{24,16},{28,20},{1,9},{5... | collective-permute-start | bytes 442376 | tf_op jit(solution)/shard_map/ppermute | solution.py:19
  45.6 10.5 %collective-permute-start.15 = (bf16[32,2304]{1,0:T(8,128)(2,1)S(1)}, bf16[32,2304]{1,0:T(8,128)(2,1)S(1)}, u32[]{:S(2)}, u32[]{:S(2)}) collective-permute-start(bf16[32,2304]{1,0:T(8,128)(2,1)S(1)} %get-tuple-element.25), channel_id=1, source_target_pairs={{0,24},{4,28},{8,16},{12,20},{16,8},{20,12},{24,0},{28,4},{1,25},{... | collective-permute-start | bytes 442376 | tf_op jit(solution)/shard_map/ppermute | solution.py:19
  46.7 11.6 %collective-permute-start.14 = (bf16[32,2304]{1,0:T(8,128)(2,1)S(1)}, bf16[32,2304]{1,0:T(8,128)(2,1)S(1)}, u32[]{:S(2)}, u32[]{:S(2)}) collective-permute-start(bf16[32,2304]{1,0:T(8,128)(2,1)S(1)} %get-tuple-element.24), channel_id=1, source_target_pairs={{0,16},{4,20},{8,24},{12,28},{16,0},{20,4},{24,8},{28,12},{1,17},{... | collective-permute-start | bytes 442376 | tf_op jit(solution)/shard_map/ppermute | solution.py:19
  49.8 8.5 %collective-permute-start.13 = (bf16[32,2304]{1,0:T(8,128)(2,1)S(1)}, bf16[32,2304]{1,0:T(8,128)(2,1)S(1)}, u32[]{:S(2)}, u32[]{:S(2)}) collective-permute-start(bf16[32,2304]{1,0:T(8,128)(2,1)S(1)} %get-tuple-element.23), channel_id=1, source_target_pairs={{0,8},{4,12},{8,0},{12,4},{16,24},{20,28},{24,16},{28,20},{1,9},{5... | collective-permute-start | bytes 442376 | tf_op jit(solution)/shard_map/ppermute | solution.py:19
  53.1 5.2 %collective-permute-start.19 = (bf16[32,2304]{1,0:T(8,128)(2,1)S(1)}, bf16[32,2304]{1,0:T(8,128)(2,1)S(1)}, u32[]{:S(2)}, u32[]{:S(2)}) collective-permute-start(bf16[32,2304]{1,0:T(8,128)(2,1)S(1)} %add_convert_fusion.2), channel_id=1, source_target_pairs={{0,1},{1,0},{2,3},{3,2},{4,5},{5,4},{6,7},{7,6},{8,9},{9,8},{10,11... | collective-permute-start | bytes 442376 | tf_op jit(solution)/shard_map/ppermute | solution.py:19
  58.4 9.6 %collective-permute-start.20 = (bf16[2,16,2304]{2,1,0:T(8,128)(2,1)S(1)}, bf16[2,16,2304]{2,1,0:T(8,128)(2,1)S(1)}, u32[]{:S(2)}, u32[]{:S(2)}) collective-permute-start(bf16[2,16,2304]{2,1,0:T(8,128)(2,1)S(1)} %bitcast.105), channel_id=1, source_target_pairs={{0,2},{1,3},{2,0},{3,1},{4,6},{5,7},{6,4},{7,5},{8,10},{9,11},{10,... | collective-permute-start | bytes 442376 | tf_op jit(solution)/shard_map/ppermute | solution.py:19
  68.1 7.7 %collective-permute-start.28 = (bf16[32,2304]{1,0:T(8,128)(2,1)S(1)}, bf16[32,2304]{1,0:T(8,128)(2,1)S(1)}, u32[]{:S(2)}, u32[]{:S(2)}) collective-permute-start(bf16[32,2304]{1,0:T(8,128)(2,1)S(1)} %bitcast.100), channel_id=1, source_target_pairs={{0,24},{4,28},{8,16},{12,20},{16,8},{20,12},{24,0},{28,4},{1,25},{... | collective-permute-start | bytes 442376 | tf_op jit(solution)/shard_map/ppermute | solution.py:19
  69.4 8.6 %collective-permute-start.27 = (bf16[32,2304]{1,0:T(8,128)(2,1)S(1)}, bf16[32,2304]{1,0:T(8,128)(2,1)S(1)}, u32[]{:S(2)}, u32[]{:S(2)}) collective-permute-start(bf16[32,2304]{1,0:T(8,128)(2,1)S(1)} %bitcast.101), channel_id=1, source_target_pairs={{0,16},{4,20},{8,24},{12,28},{16,0},{20,4},{24,8},{28,12},{1,17},{... | collective-permute-start | bytes 442376 | tf_op jit(solution)/shard_map/ppermute | solution.py:19
  70.4 7.6 %collective-permute-start.26 = (bf16[32,2304]{1,0:T(8,128)(2,1)S(1)}, bf16[32,2304]{1,0:T(8,128)(2,1)S(1)}, u32[]{:S(2)}, u32[]{:S(2)}) collective-permute-start(bf16[32,2304]{1,0:T(8,128)(2,1)S(1)} %bitcast.102), channel_id=1, source_target_pairs={{0,8},{4,12},{8,0},{12,4},{16,24},{20,28},{24,16},{28,20},{1,9},{5... | collective-permute-start | bytes 442376 | tf_op jit(solution)/shard_map/ppermute | solution.py:19
  71.6 8.7 %collective-permute-start.21 = (bf16[32,2304]{1,0:T(8,128)(2,1)S(1)}, bf16[32,2304]{1,0:T(8,128)(2,1)S(1)}, u32[]{:S(2)}, u32[]{:S(2)}) collective-permute-start(bf16[32,2304]{1,0:T(8,128)(2,1)S(1)} %bitcast.103), channel_id=1, source_target_pairs={{0,1},{1,0},{2,3},{3,2},{4,5},{5,4},{6,7},{7,6},{8,9},{9,8},{10,11... | collective-permute-start | bytes 442376 | tf_op jit(solution)/shard_map/ppermute | solution.py:19
  78.1 13.3 %collective-permute-start.29 = (bf16[128,2304]{1,0:T(8,128)(2,1)S(1)}, bf16[128,2304]{1,0:T(8,128)(2,1)S(1)}, u32[]{:S(2)}, u32[]{:S(2)}) collective-permute-start(bf16[128,2304]{1,0:T(8,128)(2,1)S(1)} %bitcast.60), channel_id=1, source_target_pairs={{0,4},{4,0},{8,12},{12,8},{16,20},{20,16},{24,28},{28,24},{1,5},{5... | collective-permute-start | bytes 1769480 | tf_op jit(solution)/shard_map/ppermute | solution.py:19
  80.3 10.6 %copy-start.7 = (bf16[2304,512]{1,0:T(8,128)(2,1)S(1)}, bf16[2304,512]{1,0:T(8,128)(2,1)}, u32[]{:S(2)}) copy-start(bf16[2304,512]{1,0:T(8,128)(2,1)} %param.22) | copy-start | bytes 7077892
  80.3 7.7 %collective-permute-start.24 = (bf16[32,2304]{1,0:T(8,128)(2,1)S(1)}, bf16[32,2304]{1,0:T(8,128)(2,1)S(1)}, u32[]{:S(2)}, u32[]{:S(2)}) collective-permute-start(bf16[32,2304]{1,0:T(8,128)(2,1)S(1)} %collective-permute-done.21), channel_id=1, source_target_pairs={{0,24},{4,28},{8,16},{12,20},{16,8},{20,12},{24,0},{28,4},{1,25},{... | collective-permute-start | bytes 442376 | tf_op jit(solution)/shard_map/ppermute | solution.py:19
  81.7 9.0 %collective-permute-start.23 = (bf16[32,2304]{1,0:T(8,128)(2,1)S(1)}, bf16[32,2304]{1,0:T(8,128)(2,1)S(1)}, u32[]{:S(2)}, u32[]{:S(2)}) collective-permute-start(bf16[32,2304]{1,0:T(8,128)(2,1)S(1)} %collective-permute-done.21), channel_id=1, source_target_pairs={{0,16},{4,20},{8,24},{12,28},{16,0},{20,4},{24,8},{28,12},{1,17},{... | collective-permute-start | bytes 442376 | tf_op jit(solution)/shard_map/ppermute | solution.py:19
  82.6 8.1 %collective-permute-start.22 = (bf16[32,2304]{1,0:T(8,128)(2,1)S(1)}, bf16[32,2304]{1,0:T(8,128)(2,1)S(1)}, u32[]{:S(2)}, u32[]{:S(2)}) collective-permute-start(bf16[32,2304]{1,0:T(8,128)(2,1)S(1)} %collective-permute-done.21), channel_id=1, source_target_pairs={{0,8},{4,12},{8,0},{12,4},{16,24},{20,28},{24,16},{28,20},{1,9},{5... | collective-permute-start | bytes 442376 | tf_op jit(solution)/shard_map/ppermute | solution.py:19
  84.4 7.5 %collective-permute-start.34 = (bf16[128,2304]{1,0:T(8,128)(2,1)S(1)}, bf16[128,2304]{1,0:T(8,128)(2,1)S(1)}, u32[]{:S(2)}, u32[]{:S(2)}) collective-permute-start(bf16[128,2304]{1,0:T(8,128)(2,1)S(1)} %convolution_convert_fusion), channel_id=1, source_target_pairs={{0,4},{4,0},{8,12},{12,8},{16,20},{20,16},{24,28},{28,24},{1,5},{5... | collective-permute-start | bytes 1769480 | tf_op jit(solution)/shard_map/ppermute | solution.py:19
  90.8 12.1 %collective-permute-start.25 = (bf16[128,2304]{1,0:T(8,128)(2,1)S(1)}, bf16[128,2304]{1,0:T(8,128)(2,1)S(1)}, u32[]{:S(2)}, u32[]{:S(2)}) collective-permute-start(bf16[128,2304]{1,0:T(8,128)(2,1)S(1)} %bitcast.58), channel_id=1, source_target_pairs={{0,4},{4,0},{8,12},{12,8},{16,20},{20,16},{24,28},{28,24},{1,5},{5... | collective-permute-start | bytes 1769480 | tf_op jit(solution)/shard_map/ppermute | solution.py:19
  92.4 7.7 %collective-permute-start.37 = (bf16[32,2304]{1,0:T(8,128)(2,1)S(1)}, bf16[32,2304]{1,0:T(8,128)(2,1)S(1)}, u32[]{:S(2)}, u32[]{:S(2)}) collective-permute-start(bf16[32,2304]{1,0:T(8,128)(2,1)S(1)} %get-tuple-element.38), channel_id=1, source_target_pairs={{0,24},{4,28},{8,16},{12,20},{16,8},{20,12},{24,0},{28,4},{1,25},{... | collective-permute-start | bytes 442376 | tf_op jit(solution)/shard_map/ppermute | solution.py:19
  93.8 9.0 %collective-permute-start.36 = (bf16[32,2304]{1,0:T(8,128)(2,1)S(1)}, bf16[32,2304]{1,0:T(8,128)(2,1)S(1)}, u32[]{:S(2)}, u32[]{:S(2)}) collective-permute-start(bf16[32,2304]{1,0:T(8,128)(2,1)S(1)} %get-tuple-element.39), channel_id=1, source_target_pairs={{0,16},{4,20},{8,24},{12,28},{16,0},{20,4},{24,8},{28,12},{1,17},{... | collective-permute-start | bytes 442376 | tf_op jit(solution)/shard_map/ppermute | solution.py:19
  94.7 8.1 %collective-permute-start.35 = (bf16[32,2304]{1,0:T(8,128)(2,1)S(1)}, bf16[32,2304]{1,0:T(8,128)(2,1)S(1)}, u32[]{:S(2)}, u32[]{:S(2)}) collective-permute-start(bf16[32,2304]{1,0:T(8,128)(2,1)S(1)} %get-tuple-element.37), channel_id=1, source_target_pairs={{0,8},{4,12},{8,0},{12,4},{16,24},{20,28},{24,16},{28,20},{1,9},{5... | collective-permute-start | bytes 442376 | tf_op jit(solution)/shard_map/ppermute | solution.py:19
  96.5 6.9 %collective-permute-start.30 = (bf16[128,2304]{1,0:T(8,128)(2,1)S(1)}, bf16[128,2304]{1,0:T(8,128)(2,1)S(1)}, u32[]{:S(2)}, u32[]{:S(2)}) collective-permute-start(bf16[128,2304]{1,0:T(8,128)(2,1)S(1)} %convolution_convert_fusion.1), channel_id=1, source_target_pairs={{0,4},{4,0},{8,12},{12,8},{16,20},{20,16},{24,28},{28,24},{1,5},{5... | collective-permute-start | bytes 1769480 | tf_op jit(solution)/shard_map/ppermute | solution.py:19
  102.8 5.9 %collective-permute-start.38 = (bf16[32,2304]{1,0:T(8,128)(2,1)S(1)}, bf16[32,2304]{1,0:T(8,128)(2,1)S(1)}, u32[]{:S(2)}, u32[]{:S(2)}) collective-permute-start(bf16[32,2304]{1,0:T(8,128)(2,1)S(1)} %fusion.10), channel_id=1, source_target_pairs={{0,1},{1,0},{2,3},{3,2},{4,5},{5,4},{6,7},{7,6},{8,9},{9,8},{10,11... | collective-permute-start | bytes 442376 | tf_op jit(solution)/shard_map/ppermute | solution.py:19
  103.9 17.0 %copy-start.9 = (f32[2304]{0:T(1024)S(1)}, f32[2304]{0:T(1024)}, u32[]{:S(2)}) copy-start(f32[2304]{0:T(1024)} %param.25) | copy-start | bytes 27652
  104.0 7.7 %collective-permute-start.33 = (bf16[32,2304]{1,0:T(8,128)(2,1)S(1)}, bf16[32,2304]{1,0:T(8,128)(2,1)S(1)}, u32[]{:S(2)}, u32[]{:S(2)}) collective-permute-start(bf16[32,2304]{1,0:T(8,128)(2,1)S(1)} %get-tuple-element.35), channel_id=1, source_target_pairs={{0,24},{4,28},{8,16},{12,20},{16,8},{20,12},{24,0},{28,4},{1,25},{... | collective-permute-start | bytes 442376 | tf_op jit(solution)/shard_map/ppermute | solution.py:19
  105.3 8.6 %collective-permute-start.32 = (bf16[32,2304]{1,0:T(8,128)(2,1)S(1)}, bf16[32,2304]{1,0:T(8,128)(2,1)S(1)}, u32[]{:S(2)}, u32[]{:S(2)}) collective-permute-start(bf16[32,2304]{1,0:T(8,128)(2,1)S(1)} %get-tuple-element.36), channel_id=1, source_target_pairs={{0,16},{4,20},{8,24},{12,28},{16,0},{20,4},{24,8},{28,12},{1,17},{... | collective-permute-start | bytes 442376 | tf_op jit(solution)/shard_map/ppermute | solution.py:19
  106.2 7.6 %collective-permute-start.31 = (bf16[32,2304]{1,0:T(8,128)(2,1)S(1)}, bf16[32,2304]{1,0:T(8,128)(2,1)S(1)}, u32[]{:S(2)}, u32[]{:S(2)}) collective-permute-start(bf16[32,2304]{1,0:T(8,128)(2,1)S(1)} %get-tuple-element.34), channel_id=1, source_target_pairs={{0,8},{4,12},{8,0},{12,4},{16,24},{20,28},{24,16},{28,20},{1,9},{5... | collective-permute-start | bytes 442376 | tf_op jit(solution)/shard_map/ppermute | solution.py:19
  114.0 6.9 %collective-permute-start.39 = (bf16[16,2304]{1,0:T(8,128)(2,1)S(1)}, bf16[16,2304]{1,0:T(8,128)(2,1)S(1)}, u32[]{:S(2)}, u32[]{:S(2)}) collective-permute-start(bf16[16,2304]{1,0:T(8,128)(2,1)S(1)} %fusion.15), channel_id=1, source_target_pairs={{0,2},{1,3},{2,0},{3,1},{4,6},{5,7},{6,4},{7,5},{8,10},{9,11},{10,... | collective-permute-start | bytes 221192 | tf_op jit(solution)/shard_map/ppermute | solution.py:19
  116.0 5.6 %copy-start.10 = (bf16[32,16,512]{2,1,0:T(8,128)(2,1)}, bf16[32,16,512]{2,1,0:T(8,128)(2,1)S(1)}, u32[]{:S(2)}) copy-start(bf16[32,16,512]{2,1,0:T(8,128)(2,1)S(1)} %constant_dynamic-update-slice_fusion.3) | copy-start | bytes 1572868
  (3 other events, 2.5 us)

commit v8 on v7

--- a/solution.py
+++ b/solution.py
@@ -9,7 +9,7 @@
 
 LANES = 128
 MIB = 1024 * 1024
-LOAD_MIB = 34
+LOAD_MIB = 40
 VMEM_SPEC = pl.BlockSpec(memory_space=pltpu.VMEM)
 SMEM_SPEC = pl.BlockSpec(memory_space=pltpu.SMEM)
 HBM_SPEC = pl.BlockSpec(memory_space=pltpu.HBM)
@@ -93,36 +93,48 @@
     )[0]
 
 
-def load_kernel(count, x, table, *refs):
-    sources, refs = refs[: count + 3], refs[count + 3 :]
-    (shared_out, table_out), loaded = refs[:2], refs[2 : 2 + count]
-    gate, up, down, sems = refs[2 + count :]
-    copies = start_all(list(zip(sources, (gate, up, down) + loaded)), sems)
-    table_out[...] = table[...]
-    copies[0].wait()
-    value = silu(dot(x[...], gate[...]))
-    copies[1].wait()
-    hidden = half(value * dot(x[...], up[...]))
-    copies[2].wait()
-    for j in range(0, shared_out.shape[1], 256):
-        shared_out[:, j : j + 256] = dot(hidden, down[:, j : j + 256])
-    for copy in copies[3:]:
+def load_kernel(table, *refs):
+    count = (len(refs) - 2) // 2
+    copies = start_all(list(zip(refs[:count], refs[count + 1 : -1])), refs[-1])
+    refs[count][...] = table[...]
+    for copy in copies:
         copy.wait()
 
 
-def run_load(x, table, shared, values):
+def run_load(table, values):
     count = len(values)
-    outs = [((x.shape[0], shared[2].shape[1]), jnp.float32)]
-    outs += [(value.shape, value.dtype) for value in [table] + values]
-    return call(
-        functools.partial(load_kernel, count),
-        [x, table, *shared, *values],
-        [VMEM_SPEC] * 2 + [HBM_SPEC] * (3 + count),
-        outs,
-        [pltpu.VMEM(w.shape, jnp.bfloat16) for w in shared]
-        + [pltpu.SemaphoreType.DMA((3 + count,))],
+    return call(
+        load_kernel,
+        [table, *values],
+        [VMEM_SPEC] + [HBM_SPEC] * count,
+        [(value.shape, value.dtype) for value in [table] + values],
+        [pltpu.SemaphoreType.DMA((count,))],
         LOAD_MIB,
-        (6 * x.shape[0] * shared[0].size, 4 * sum(value.size for value in values)),
+        (550 * sum(value.size for value in values), 4 * sum(value.size for value in values)),
+    )
+
+
+def shared_kernel(own, scalars, x, gate, up, down, kept, sent):
+    hidden = half(silu(dot(x[...], gate[...])) * dot(x[...], up[...]))
+    rows, width = x.shape
+    for j in range(0, width, 256):
+        cut = slice(j, j + 256)
+        value = dot(hidden, down[:, cut]).reshape(rows // own // 2, 2, own, -1)
+        low, high = [value[:, i].reshape(rows // 2, -1) for i in range(2)]
+        kept[:, cut] = jnp.where(scalars[1] == 0, low, high)
+        sent[:, cut] = jnp.where(scalars[1] == 0, high, low)
+
+
+def run_shared(scalars, x, weights, own):
+    rows, width = x.shape
+    return call(
+        functools.partial(shared_kernel, own),
+        [scalars, x, *weights],
+        [SMEM_SPEC] + [VMEM_SPEC] * 4,
+        [((rows // 2, width), jnp.float32)] * 2,
+        [],
+        6,
+        (6 * rows * weights[0].size, 6 * weights[0].size),
     )
 
 
@@ -172,8 +184,6 @@
         size = value.shape[0] // pairs
         for p in range(pairs):
             block = value[p * size : (p + 1) * size]
-            if p == 0:
-                block += more[1][:, cut]
             block = block.reshape(size // own // 2, 2, own, tile)
             low, high = block[:, 0].reshape(-1, tile), block[:, 1].reshape(-1, tile)
             outs[p][:, cut] = half(jnp.where(scalars[1] == 0, low, high))
@@ -233,17 +243,16 @@
     near = [tokens] + [swap(tokens, "expert", 2 * p) for p in range(1, pairs)]
     far = [swap(piece, "expert", 1) for piece in near]
     arrived = swap(table, "expert", 2)
-    shared_out, table, near[0], expert_gate, expert_up, expert_down = run_load(
-        far[0],
-        table,
-        [shared_gate, shared_up, shared_down],
-        [tokens, expert_gate, expert_up, expert_down],
-    )
+    table, near[0], expert_gate, expert_up = run_load(
+        table, [tokens, expert_gate, expert_up]
+    )
+    shared_out = run_shared(scalars, far[0], [shared_gate, shared_up, shared_down], own)
     table = jnp.concatenate([table, arrived], axis=0)
     for bit in bits_of(pairs)[1:]:
         table = jnp.concatenate([table, swap(table, "expert", 2 * bit)], axis=0)
     table_far = swap(table, "expert", 1)
 
+    table, *far = lax.optimization_barrier((table, *far))
     arrived = None
     for e in local_experts:
         hidden = run_hidden(near, expert_gate, expert_up, e)
@@ -256,19 +265,15 @@
             more = [arrived]
             arrived = run_down(hidden, expert_down, e, scalars, table_far, top, more)[0]
     blocks = run_down(
-        hidden, expert_down, e, scalars, table_far, top, [arrived, shared_out], (pairs, own)
-    )
-
-    def reduce_pairs(parts):
+        hidden, expert_down, e, scalars, table_far, top, [arrived], (pairs, own)
+    )
+
+    def reduce_pairs(parts, *more):
         arrived = [swap(parts[p], "expert", 2 * p) for p in range(1, pairs)]
-        return sum(full(part) for part in [parts[0]] + arrived)
-
-    def gather_pairs(value):
-        parts = [value] + [swap(value, "expert", 2 * p) for p in range(1, pairs)]
-        return jnp.stack(parts).reshape(chunk_rows, width)
-
-    arrived = swap(half(reduce_pairs(blocks[:pairs])), "feat", feat_bits[0])
-    total = reduce_pairs(blocks[pairs:]) + full(arrived)
+        return sum(full(part) for part in [parts[0], *more] + arrived)
+
+    arrived = swap(half(reduce_pairs(blocks[:pairs], shared_out[0])), "feat", feat_bits[0])
+    total = reduce_pairs(blocks[pairs:], shared_out[1]) + full(arrived)
     total = total.reshape((2,) * (len(feat_bits) - 1) + (own, width))
     for i, bit in enumerate(feat_bits[1:-1]):
         dim = len(feat_bits) - 2 - i
@@ -279,14 +284,17 @@
     for bit in feat_bits[-2:0:-1]:
         moe_out = jnp.stack([moe_out, swap(moe_out, "feat", bit)], axis=moe_out.ndim - 2)
     moe_out = moe_out.reshape(-1, width)
-    near = [None, gather_pairs(moe_out)]
-    near[0] = gather_pairs(swap(moe_out, "feat", feat_bits[0]))
+    other = swap(moe_out, "feat", feat_bits[0])
+    parts = [moe_out] + [swap(moe_out, "expert", 2 * p) for p in range(1, pairs - 1)]
+    mine, other = lax.optimization_barrier((moe_out, other))
+    parts.append(swap(mine, "expert", 2 * (pairs - 1)))
+    sides = [[other] + [swap(other, "expert", 2 * p) for p in range(1, pairs)], parts]
+    near = [jnp.stack(parts).reshape(chunk_rows, width) for parts in sides]
 
     def encode(x):
         return half(jax.nn.relu(dot(x, encoder) + encoder_bias[None, :]))
 
-    features = [None, None]
-    arrived = None
+    features, blocks = [None, None], [None, None]
     for chunk in (1, 0):
         far = swap(near[chunk], "expert", 1)
         features_near = encode(near[chunk])
@@ -294,11 +302,12 @@
         features_far = encode(far)
         total = dot(features_far, decoder) + full(decoded)
         total = total.reshape(pairs, feats // 2 * own, width)
-        total = reduce_pairs([total[0]] + [half(total[p]) for p in range(1, pairs)])
+        blocks[chunk] = [total[0]]
+        blocks[chunk] += [swap(half(total[p]), "expert", 2 * p) for p in range(1, pairs)]
         both = jnp.stack([features_far, features_near])
         features[chunk] = both.reshape(2, pairs, feats // 2, 1, own, -1)
-        if chunk == 1:
-            arrived = swap(half(total), "feat", feat_bits[0])
+    arrived = swap(half(sum(full(block) for block in blocks[1])), "feat", feat_bits[0])
+    total = sum(full(block) for block in blocks[0])
     total = (total + full(arrived)).reshape((2,) * (len(feat_bits) - 1) + (own, width))
     for bit in feat_bits[1:-1]:
         dim = len(total.shape) - 3

time: 122 us -> 108 us (0.89)
  waiting for transfers between devices: 51.2 us -> 42.6 us
  local copies, waits for them, and re-layouts: 6.79 us -> 2.94 us
  matrix products: 5.52 us -> 3.86 us
  starting transfers between devices: 39.2 us -> 40.6 us
    ppermute x40, waiting for transfers between devices: 51.2 us -> 42.6 us  [swap(): lax.ppermute(value, axis, [(i, i ^ r) for i in range(lax.axis_size(axis))])]
    unnamed x55 -> x59, local copies, waits for them, and re-layouts: 6.7 us -> 2.85 us
    dot_general x8, matrix products: 5.52 us -> 3.86 us  [dot(): return jnp.dot(a, b, preferred_element_type=jnp.float32)]
    ppermute x40, starting transfers between devices: 39.2 us -> 40.6 us  [swap(): lax.ppermute(value, axis, [(i, i ^ r) for i in range(lax.axis_size(axis))])]
    pallas_call x6 -> x7, Pallas kernels: 15.6 us -> 14.8 us  [call(): pl.pallas_call(body, in_specs=specs, out_specs=[VMEM_SPEC] * len(outs), o...]
  transfers between devices with their start and end apart: 40 -> 40, of which waited for: 19 -> 20; matrix products, arithmetic and copies ran while one was open for 6% -> 5% of each run, Pallas kernels for 10% -> 10%
where the time goes in v8:
time: 108 us
  waiting for transfers between devices  42.6 us (39%)
  starting transfers between devices  40.6 us (38%)
  Pallas kernels  14.8 us (14%)
  matrix products  3.86 us (4%)
  local copies, waits for them, and re-layouts  2.94 us (3%)
  other arithmetic  2.07 us (2%)
  between operations  1.28 us (1%)
    ppermute x40, waiting for transfers between devices, swap(): lax.ppermute(value, axis, [(i, i ^ r) for i in range(lax.axis_size(axis))])  42.6 us
    ppermute x40, starting transfers between devices, swap(): lax.ppermute(value, axis, [(i, i ^ r) for i in range(lax.axis_size(axis))])  40.6 us
    pallas_call x7, Pallas kernels, call(): pl.pallas_call(body, in_specs=specs, out_specs=[VMEM_SPEC] * len(outs), o...  14.8 us
    dot_general x8, matrix products, dot(): return jnp.dot(a, b, preferred_element_type=jnp.float32)  3.86 us
    unnamed x59, local copies, waits for them, and re-layouts  2.85 us
  transfers between devices with their start and end apart: 40, of which 20 were waited for; matrix products, arithmetic and copies ran while one was open for 5% of the time, Pallas kernels for 10%

profile of v8, /device:TPU:0, one launch (start us, length us, event | category | flops | bytes accessed | tf_op | source)
XLA Modules:
  0.0 108.2 jit_solution(4801937850820346888)
XLA Ops:
  0.7 0.8 copy-done.4
  1.5 0.7 copy-done.5
  2.4 3.0 %collective-permute-start = (bf16[64,128]{1,0:T(8,128)(2,1)S(1)}, bf16[64,128]{1,0:T(8,128)(2,1)}, u32[]{:S(2)}, u32[]{:S(2)}) collective-permute-start(bf16[64,128]{1,0:T(8,128)(2,1)S(1)} %shard_map.140), channel_id=1, source_target_pairs={{0,1},{1,0},{2,3},{3,2},{4,5},{5,4},{6,7},{7,6},{8,9},{9,8},{10,11... | collective-permute-start | bytes 49160 | tf_op jit(solution)/shard_map/ppermute | solution.py:19
  5.4 1.5 %collective-permute-start.5 = (bf16[64,2304]{1,0:T(8,128)(2,1)}, bf16[64,2304]{1,0:T(8,128)(2,1)S(1)}, u32[]{:S(2)}, u32[]{:S(2)}) collective-permute-start(bf16[64,2304]{1,0:T(8,128)(2,1)} %refs_0_.1), channel_id=1, source_target_pairs={{0,8},{4,12},{8,0},{12,4},{16,24},{20,28},{24,16},{28,20},{1,9},{5... | collective-permute-start | bytes 884744 | tf_op jit(solution)/shard_map/ppermute | solution.py:19
  6.9 1.5 %collective-permute-start.7 = (bf16[64,2304]{1,0:T(8,128)(2,1)}, bf16[64,2304]{1,0:T(8,128)(2,1)S(1)}, u32[]{:S(2)}, u32[]{:S(2)}) collective-permute-start(bf16[64,2304]{1,0:T(8,128)(2,1)} %refs_0_.1), channel_id=1, source_target_pairs={{0,16},{4,20},{8,24},{12,28},{16,0},{20,4},{24,8},{28,12},{1,17},{... | collective-permute-start | bytes 884744 | tf_op jit(solution)/shard_map/ppermute | solution.py:19
  8.9 0.7 add.226
  9.6 2.6 %collective-permute-start.1 = (bf16[64,128]{1,0:T(8,128)(2,1)S(1)}, bf16[64,128]{1,0:T(8,128)(2,1)S(1)}, u32[]{:S(2)}, u32[]{:S(2)}) collective-permute-start(bf16[64,128]{1,0:T(8,128)(2,1)S(1)} %add.226), channel_id=1, source_target_pairs={{0,2},{1,3},{2,0},{3,1},{4,6},{5,7},{6,4},{7,5},{8,10},{9,11},{10,... | collective-permute-start | bytes 49160 | tf_op jit(solution)/shard_map/ppermute | solution.py:19
  12.3 2.0 %collective-permute-done.1 = bf16[64,128]{1,0:T(8,128)(2,1)S(1)} collective-permute-done((bf16[64,128]{1,0:T(8,128)(2,1)S(1)}, bf16[64,128]{1,0:T(8,128)(2,1)S(1)}, u32[]{:S(2)}, u32[]{:S(2)}) %collective-permute-start.1) | collective-permute-done | bytes 16416 | tf_op jit(solution)/shard_map/ppermute | solution.py:19
  14.3 1.6 %collective-permute-start.2 = (bf16[64,128]{1,0:T(8,128)(2,1)S(1)}, bf16[64,128]{1,0:T(8,128)(2,1)S(1)}, u32[]{:S(2)}, u32[]{:S(2)}) collective-permute-start(bf16[64,128]{1,0:T(8,128)(2,1)S(1)} %add.227.table), channel_id=1, source_target_pairs={{0,8},{4,12},{8,0},{12,4},{16,24},{20,28},{24,16},{28,20},{1,9},{5... | collective-permute-start | bytes 49160 | tf_op jit(solution)/shard_map/ppermute | solution.py:19
  15.9 1.0 copy-done.6
  16.8 3.9 %shard_map.141 = (bf16[64,128]{1,0:T(8,128)(2,1)S(1)}, bf16[64,2304]{1,0:T(8,128)(2,1)S(1)}, bf16[1,2304,1024]{2,1,0:T(8,128)(2,1)S(1)}, bf16[1,2304,1024]{2,1,0:T(8,128)(2,1)S(1)}) custom-call(bf16[64,128]{1,0:T(8,128)(2,1)S(1)} %add.227.table, bf16[64,2304]{1,0:T(8,128)(2,1)S(1)} %copy-done.6, bf16[1,2304,1024]{2,1,0:T(8,128)(2,1)} %refs_1_.1, ...), custom_call_target="tpu_custom_call" | custom-call | flops 2676326400 | bytes 19464192 | tf_op jit(solution)/shard_map/pallas_call | solution.py:49
  20.7 1.0 collective-permute-done.2
  21.7 1.5 %collective-permute-start.3 = (bf16[128,128]{1,0:T(8,128)(2,1)S(1)}, bf16[128,128]{1,0:T(8,128)(2,1)S(1)}, u32[]{:S(2)}, u32[]{:S(2)}) collective-permute-start(bf16[128,128]{1,0:T(8,128)(2,1)S(1)} %pad_maximum_fusion.2), channel_id=1, source_target_pairs={{0,16},{4,20},{8,24},{12,28},{16,0},{20,4},{24,8},{28,12},{1,17},{... | collective-permute-start | bytes 98312 | tf_op jit(solution)/shard_map/ppermute | solution.py:19
  23.9 1.8 %collective-permute-done.3 = bf16[128,128]{1,0:T(8,128)(2,1)S(1)} collective-permute-done((bf16[128,128]{1,0:T(8,128)(2,1)S(1)}, bf16[128,128]{1,0:T(8,128)(2,1)S(1)}, u32[]{:S(2)}, u32[]{:S(2)}) %collective-permute-start.3) | collective-permute-done | bytes 32800 | tf_op jit(solution)/shard_map/ppermute | solution.py:19
  25.7 2.7 %shard_map.143.hidden = bf16[256,1024]{1,0:T(8,128)(2,1)S(1)} custom-call(bf16[64,2304]{1,0:T(8,128)(2,1)S(1)} %get-tuple-element.30.refs_0_, bf16[64,2304]{1,0:T(8,128)(2,1)S(1)} %collective-permute-done.5.refs_1_, bf16[64,2304]{1,0:T(8,128)(2,1)S(1)} %collective-permute-done.7.refs_2_, bf16[64,2304]{1,0:T(8,128)(2,1)S(1)} %collective-permute-done.9.refs_3_, ...), custom_call_target="tpu_custom_call" | custom-call | flops 2415919104 | bytes 9437184 | tf_op jit(solution)/shard_map/pallas_call | solution.py:49
  28.5 1.9 %shard_map.144 = bf16[256,2304]{1,0:T(8,128)(2,1)S(1)} custom-call(s32[2]{0:T(128)S(1)} %pad_add_fusion.scalars, bf16[256,1024]{1,0:T(8,128)(2,1)S(1)} %shard_map.143.hidden, bf16[1,1024,2304]{2,1,0:T(8,128)(2,1)S(1)} %bitcast.57, bf16[256,128]{1,0:T(8,128)(2,1)S(1)} %constant_dynamic-update-slice_fusion.table), custom_call_target="tpu_custom_call" | custom-call | flops 1207959552 | bytes 4718592 | tf_op jit(solution)/shard_map/pallas_call | solution.py:49
  31.0 2.7 %shard_map.142.hidden = bf16[256,1024]{1,0:T(8,128)(2,1)S(1)} custom-call(bf16[64,2304]{1,0:T(8,128)(2,1)S(1)} %collective-permute-done.4.refs_0_.x, bf16[64,2304]{1,0:T(8,128)(2,1)S(1)} %collective-permute-done.6.refs_1_, bf16[64,2304]{1,0:T(8,128)(2,1)S(1)} %collective-permute-done.8.refs_2_, bf16[64,2304]{1,0:T(8,128)(2,1)S(1)} %collective-permute-done.10.refs_3_, ...), custom_call_target="tpu_custom_call" | custom-call | flops 2415919104 | bytes 9437184 | tf_op jit(solution)/shard_map/pallas_call | solution.py:49
  33.8 2.0 %shard_map.145 = (bf16[32,2304]{1,0:T(8,128)(2,1)S(1)}, bf16[32,2304]{1,0:T(8,128)(2,1)S(1)}, bf16[32,2304]{1,0:T(8,128)(2,1)S(1)}, bf16[32,2304]{1,0:T(8,128)(2...) custom-call(s32[2]{0:T(128)S(1)} %pad_add_fusion.scalars, ...), custom_call_target="tpu_custom_call" | custom-call | flops 1207959552 | bytes 4718592 | tf_op jit(solution)/shard_map/pallas_call | solution.py:49
  35.8 2.5 %collective-permute-start.18 = (bf16[32,2304]{1,0:T(8,128)(2,1)S(1)}, bf16[32,2304]{1,0:T(8,128)(2,1)S(1)}, u32[]{:S(2)}, u32[]{:S(2)}) collective-permute-start(bf16[32,2304]{1,0:T(8,128)(2,1)S(1)} %get-tuple-element.41), channel_id=1, source_target_pairs={{0,24},{4,28},{8,16},{12,20},{16,8},{20,12},{24,0},{28,4},{1,25},{... | collective-permute-start | bytes 442376 | tf_op jit(solution)/shard_map/ppermute | solution.py:19
  38.2 0.6 collective-permute-start.17
  39.3 1.4 %shard_map.146 = (f32[32,2304]{1,0:T(8,128)S(1)}, f32[32,2304]{1,0:T(8,128)S(1)}) custom-call(s32[2]{0:T(128)S(1)} %pad_add_fusion.scalars, bf16[64,2304]{1,0:T(8,128)(2,1)S(1)} %collective-permute-done.4.refs_0_.x, bf16[2304,256]{1,0:T(8,128)(2,1)S(1)} %copy-done.1, bf16[2304,256]{1,0:T(8,128)(2,1)S(1)} %copy-done.2, bf16[256,2304]{1,0:T(8,128)(2,1)S(1)} %copy-done.3), custom_call_target="tpu_custom_call" | custom-call | flops 226492416 | bytes 3538944 | tf_op jit(solution)/shard_map/pallas_call | solution.py:49
  40.7 2.5 %collective-permute-start.15 = (bf16[32,2304]{1,0:T(8,128)(2,1)S(1)}, bf16[32,2304]{1,0:T(8,128)(2,1)S(1)}, u32[]{:S(2)}, u32[]{:S(2)}) collective-permute-start(bf16[32,2304]{1,0:T(8,128)(2,1)S(1)} %get-tuple-element.36), channel_id=1, source_target_pairs={{0,24},{4,28},{8,16},{12,20},{16,8},{20,12},{24,0},{28,4},{1,25},{... | collective-permute-start | bytes 442376 | tf_op jit(solution)/shard_map/ppermute | solution.py:19
  43.7 1.2 %collective-permute-start.13 = (bf16[32,2304]{1,0:T(8,128)(2,1)S(1)}, bf16[32,2304]{1,0:T(8,128)(2,1)S(1)}, u32[]{:S(2)}, u32[]{:S(2)}) collective-permute-start(bf16[32,2304]{1,0:T(8,128)(2,1)S(1)} %get-tuple-element.34), channel_id=1, source_target_pairs={{0,8},{4,12},{8,0},{12,4},{16,24},{20,28},{24,16},{28,20},{1,9},{5... | collective-permute-start | bytes 442376 | tf_op jit(solution)/shard_map/ppermute | solution.py:19
  45.0 1.6 %collective-permute-done.17 = bf16[32,2304]{1,0:T(8,128)(2,1)S(1)} collective-permute-done((bf16[32,2304]{1,0:T(8,128)(2,1)S(1)}, bf16[32,2304]{1,0:T(8,128)(2,1)S(1)}, u32[]{:S(2)}, u32[]{:S(2)}) %collective-permute-start.17) | collective-permute-done | bytes 147488 | tf_op jit(solution)/shard_map/ppermute | solution.py:19
  47.3 2.4 %collective-permute-done.15 = bf16[32,2304]{1,0:T(8,128)(2,1)S(1)} collective-permute-done((bf16[32,2304]{1,0:T(8,128)(2,1)S(1)}, bf16[32,2304]{1,0:T(8,128)(2,1)S(1)}, u32[]{:S(2)}, u32[]{:S(2)}) %collective-permute-start.15) | collective-permute-done | bytes 147488 | tf_op jit(solution)/shard_map/ppermute | solution.py:19
  49.7 2.4 %collective-permute-done.14 = bf16[32,2304]{1,0:T(8,128)(2,1)S(1)} collective-permute-done((bf16[32,2304]{1,0:T(8,128)(2,1)S(1)}, bf16[32,2304]{1,0:T(8,128)(2,1)S(1)}, u32[]{:S(2)}, u32[]{:S(2)}) %collective-permute-start.14) | collective-permute-done | bytes 147488 | tf_op jit(solution)/shard_map/ppermute | solution.py:19
  52.4 2.6 %collective-permute-start.20 = (bf16[2,16,2304]{2,1,0:T(8,128)(2,1)S(1)}, bf16[2,16,2304]{2,1,0:T(8,128)(2,1)S(1)}, u32[]{:S(2)}, u32[]{:S(2)}) collective-permute-start(bf16[2,16,2304]{2,1,0:T(8,128)(2,1)S(1)} %bitcast.107), channel_id=1, source_target_pairs={{0,2},{1,3},{2,0},{3,1},{4,6},{5,7},{6,4},{7,5},{8,10},{9,11},{10,... | collective-permute-start | bytes 442376 | tf_op jit(solution)/shard_map/ppermute | solution.py:19
  55.0 6.8 %collective-permute-done.20 = bf16[2,16,2304]{2,1,0:T(8,128)(2,1)S(1)} collective-permute-done((bf16[2,16,2304]{2,1,0:T(8,128)(2,1)S(1)}, bf16[2,16,2304]{2,1,0:T(8,128)(2,1)S(1)}, u32[]{:S(2)}, u32[]{:S(2)}) %collective-permute-start.20) | collective-permute-done | bytes 147488 | tf_op jit(solution)/shard_map/ppermute | solution.py:19
  62.0 1.7 %collective-permute-start.27 = (bf16[32,2304]{1,0:T(8,128)(2,1)S(1)}, bf16[32,2304]{1,0:T(8,128)(2,1)S(1)}, u32[]{:S(2)}, u32[]{:S(2)}) collective-permute-start(bf16[32,2304]{1,0:T(8,128)(2,1)S(1)} %bitcast.103), channel_id=1, source_target_pairs={{0,16},{4,20},{8,24},{12,28},{16,0},{20,4},{24,8},{28,12},{1,17},{... | collective-permute-start | bytes 442376 | tf_op jit(solution)/shard_map/ppermute | solution.py:19
  63.7 4.0 %collective-permute-done.21 = bf16[32,2304]{1,0:T(8,128)(2,1)S(1)} collective-permute-done((bf16[32,2304]{1,0:T(8,128)(2,1)S(1)}, bf16[32,2304]{1,0:T(8,128)(2,1)S(1)}, u32[]{:S(2)}, u32[]{:S(2)}) %collective-permute-start.21) | collective-permute-done | bytes 147488 | tf_op jit(solution)/shard_map/ppermute | solution.py:19
  68.2 2.4 %collective-permute-start.24 = (bf16[32,2304]{1,0:T(8,128)(2,1)S(1)}, bf16[32,2304]{1,0:T(8,128)(2,1)S(1)}, u32[]{:S(2)}, u32[]{:S(2)}) collective-permute-start(bf16[32,2304]{1,0:T(8,128)(2,1)S(1)} %collective-permute-done.21), channel_id=1, source_target_pairs={{0,24},{4,28},{8,16},{12,20},{16,8},{20,12},{24,0},{28,4},{1,25},{... | collective-permute-start | bytes 442376 | tf_op jit(solution)/shard_map/ppermute | solution.py:19
  70.6 1.6 %collective-permute-start.23 = (bf16[32,2304]{1,0:T(8,128)(2,1)S(1)}, bf16[32,2304]{1,0:T(8,128)(2,1)S(1)}, u32[]{:S(2)}, u32[]{:S(2)}) collective-permute-start(bf16[32,2304]{1,0:T(8,128)(2,1)S(1)} %collective-permute-done.21), channel_id=1, source_target_pairs={{0,16},{4,20},{8,24},{12,28},{16,0},{20,4},{24,8},{28,12},{1,17},{... | collective-permute-start | bytes 442376 | tf_op jit(solution)/shard_map/ppermute | solution.py:19
  72.3 3.2 %collective-permute-done.28 = bf16[32,2304]{1,0:T(8,128)(2,1)S(1)} collective-permute-done((bf16[32,2304]{1,0:T(8,128)(2,1)S(1)}, bf16[32,2304]{1,0:T(8,128)(2,1)S(1)}, u32[]{:S(2)}, u32[]{:S(2)}) %collective-permute-start.28) | collective-permute-done | bytes 147488 | tf_op jit(solution)/shard_map/ppermute | solution.py:19
  75.6 2.7 %collective-permute-done.24 = bf16[32,2304]{1,0:T(8,128)(2,1)S(1)} collective-permute-done((bf16[32,2304]{1,0:T(8,128)(2,1)S(1)}, bf16[32,2304]{1,0:T(8,128)(2,1)S(1)}, u32[]{:S(2)}, u32[]{:S(2)}) %collective-permute-start.24) | collective-permute-done | bytes 147488 | tf_op jit(solution)/shard_map/ppermute | solution.py:19
  78.4 1.5 %collective-permute-done.23 = bf16[32,2304]{1,0:T(8,128)(2,1)S(1)} collective-permute-done((bf16[32,2304]{1,0:T(8,128)(2,1)S(1)}, bf16[32,2304]{1,0:T(8,128)(2,1)S(1)}, u32[]{:S(2)}, u32[]{:S(2)}) %collective-permute-start.23) | collective-permute-done | bytes 147488 | tf_op jit(solution)/shard_map/ppermute | solution.py:19
  84.0 1.5 %collective-permute-start.37 = (bf16[32,2304]{1,0:T(8,128)(2,1)S(1)}, bf16[32,2304]{1,0:T(8,128)(2,1)S(1)}, u32[]{:S(2)}, u32[]{:S(2)}) collective-permute-start(bf16[32,2304]{1,0:T(8,128)(2,1)S(1)} %get-tuple-element.52), channel_id=1, source_target_pairs={{0,24},{4,28},{8,16},{12,20},{16,8},{20,12},{24,0},{28,4},{1,25},{... | collective-permute-start | bytes 442376 | tf_op jit(solution)/shard_map/ppermute | solution.py:19
  85.5 1.4 %collective-permute-start.36 = (bf16[32,2304]{1,0:T(8,128)(2,1)S(1)}, bf16[32,2304]{1,0:T(8,128)(2,1)S(1)}, u32[]{:S(2)}, u32[]{:S(2)}) collective-permute-start(bf16[32,2304]{1,0:T(8,128)(2,1)S(1)} %get-tuple-element.53), channel_id=1, source_target_pairs={{0,16},{4,20},{8,24},{12,28},{16,0},{20,4},{24,8},{28,12},{1,17},{... | collective-permute-start | bytes 442376 | tf_op jit(solution)/shard_map/ppermute | solution.py:19
  86.9 0.6 collective-permute-start.35
  88.6 1.5 %collective-permute-start.33 = (bf16[32,2304]{1,0:T(8,128)(2,1)S(1)}, bf16[32,2304]{1,0:T(8,128)(2,1)S(1)}, u32[]{:S(2)}, u32[]{:S(2)}) collective-permute-start(bf16[32,2304]{1,0:T(8,128)(2,1)S(1)} %get-tuple-element.49), channel_id=1, source_target_pairs={{0,24},{4,28},{8,16},{12,20},{16,8},{20,12},{24,0},{28,4},{1,25},{... | collective-permute-start | bytes 442376 | tf_op jit(solution)/shard_map/ppermute | solution.py:19
  90.1 1.4 %collective-permute-start.32 = (bf16[32,2304]{1,0:T(8,128)(2,1)S(1)}, bf16[32,2304]{1,0:T(8,128)(2,1)S(1)}, u32[]{:S(2)}, u32[]{:S(2)}) collective-permute-start(bf16[32,2304]{1,0:T(8,128)(2,1)S(1)} %get-tuple-element.50), channel_id=1, source_target_pairs={{0,16},{4,20},{8,24},{12,28},{16,0},{20,4},{24,8},{28,12},{1,17},{... | collective-permute-start | bytes 442376 | tf_op jit(solution)/shard_map/ppermute | solution.py:19
  92.1 0.9 collective-permute-start.31
  93.0 1.8 %collective-permute-done.36 = bf16[32,2304]{1,0:T(8,128)(2,1)S(1)} collective-permute-done((bf16[32,2304]{1,0:T(8,128)(2,1)S(1)}, bf16[32,2304]{1,0:T(8,128)(2,1)S(1)}, u32[]{:S(2)}, u32[]{:S(2)}) %collective-permute-start.36) | collective-permute-done | bytes 147488 | tf_op jit(solution)/shard_map/ppermute | solution.py:19
  94.9 0.7 collective-permute-start.38
  95.6 2.4 %collective-permute-done.33 = bf16[32,2304]{1,0:T(8,128)(2,1)S(1)} collective-permute-done((bf16[32,2304]{1,0:T(8,128)(2,1)S(1)}, bf16[32,2304]{1,0:T(8,128)(2,1)S(1)}, u32[]{:S(2)}, u32[]{:S(2)}) %collective-permute-start.33) | collective-permute-done | bytes 147488 | tf_op jit(solution)/shard_map/ppermute | solution.py:19
  98.0 2.6 %collective-permute-done.32 = bf16[32,2304]{1,0:T(8,128)(2,1)S(1)} collective-permute-done((bf16[32,2304]{1,0:T(8,128)(2,1)S(1)}, bf16[32,2304]{1,0:T(8,128)(2,1)S(1)}, u32[]{:S(2)}, u32[]{:S(2)}) %collective-permute-start.32) | collective-permute-done | bytes 147488 | tf_op jit(solution)/shard_map/ppermute | solution.py:19
  100.8 1.0 collective-permute-start.39
  101.7 5.7 %collective-permute-done.39 = bf16[16,2304]{1,0:T(8,128)(2,1)S(1)} collective-permute-done((bf16[16,2304]{1,0:T(8,128)(2,1)S(1)}, bf16[16,2304]{1,0:T(8,128)(2,1)S(1)}, u32[]{:S(2)}, u32[]{:S(2)}) %collective-permute-start.39) | collective-permute-done | bytes 73760 | tf_op jit(solution)/shard_map/ppermute | solution.py:19
  107.5 0.7 fusion.14
  (125 shorter events, 10.6 us)
Async XLA Ops:
  0.6 80.1 %copy-start = (bf16[512,2304]{1,0:T(8,128)(2,1)S(1)}, bf16[512,2304]{1,0:T(8,128)(2,1)}, u32[]{:S(2)}) copy-start(bf16[512,2304]{1,0:T(8,128)(2,1)} %param.24) | copy-start | bytes 7077892
  2.4 6.5 %collective-permute-start = (bf16[64,128]{1,0:T(8,128)(2,1)S(1)}, bf16[64,128]{1,0:T(8,128)(2,1)}, u32[]{:S(2)}, u32[]{:S(2)}) collective-permute-start(bf16[64,128]{1,0:T(8,128)(2,1)S(1)} %shard_map.140), channel_id=1, source_target_pairs={{0,1},{1,0},{2,3},{3,2},{4,5},{5,4},{6,7},{7,6},{8,9},{9,8},{10,11... | collective-permute-start | bytes 49160 | tf_op jit(solution)/shard_map/ppermute | solution.py:19
  5.4 23.0 %collective-permute-start.4 = (bf16[64,2304]{1,0:T(8,128)(2,1)}, bf16[64,2304]{1,0:T(8,128)(2,1)S(1)}, u32[]{:S(2)}, u32[]{:S(2)}) collective-permute-start(bf16[64,2304]{1,0:T(8,128)(2,1)} %refs_0_.1), channel_id=1, source_target_pairs={{0,4},{4,0},{8,12},{12,8},{16,20},{20,16},{24,28},{28,24},{1,5},{5... | collective-permute-start | bytes 884744 | tf_op jit(solution)/shard_map/ppermute | solution.py:19
  5.4 17.9 %collective-permute-start.5 = (bf16[64,2304]{1,0:T(8,128)(2,1)}, bf16[64,2304]{1,0:T(8,128)(2,1)S(1)}, u32[]{:S(2)}, u32[]{:S(2)}) collective-permute-start(bf16[64,2304]{1,0:T(8,128)(2,1)} %refs_0_.1), channel_id=1, source_target_pairs={{0,8},{4,12},{8,0},{12,4},{16,24},{20,28},{24,16},{28,20},{1,9},{5... | collective-permute-start | bytes 884744 | tf_op jit(solution)/shard_map/ppermute | solution.py:19
  6.9 16.4 %collective-permute-start.7 = (bf16[64,2304]{1,0:T(8,128)(2,1)}, bf16[64,2304]{1,0:T(8,128)(2,1)S(1)}, u32[]{:S(2)}, u32[]{:S(2)}) collective-permute-start(bf16[64,2304]{1,0:T(8,128)(2,1)} %refs_0_.1), channel_id=1, source_target_pairs={{0,16},{4,20},{8,24},{12,28},{16,0},{20,4},{24,8},{28,12},{1,17},{... | collective-permute-start | bytes 884744 | tf_op jit(solution)/shard_map/ppermute | solution.py:19
  8.4 15.4 %collective-permute-start.9 = (bf16[64,2304]{1,0:T(8,128)(2,1)}, bf16[64,2304]{1,0:T(8,128)(2,1)S(1)}, u32[]{:S(2)}, u32[]{:S(2)}) collective-permute-start(bf16[64,2304]{1,0:T(8,128)(2,1)} %refs_0_.1), channel_id=1, source_target_pairs={{0,24},{4,28},{8,16},{12,20},{16,8},{20,12},{24,0},{28,4},{1,25},{... | collective-permute-start | bytes 884744 | tf_op jit(solution)/shard_map/ppermute | solution.py:19
  9.6 4.6 %collective-permute-start.1 = (bf16[64,128]{1,0:T(8,128)(2,1)S(1)}, bf16[64,128]{1,0:T(8,128)(2,1)S(1)}, u32[]{:S(2)}, u32[]{:S(2)}) collective-permute-start(bf16[64,128]{1,0:T(8,128)(2,1)S(1)} %add.226), channel_id=1, source_target_pairs={{0,2},{1,3},{2,0},{3,1},{4,6},{5,7},{6,4},{7,5},{8,10},{9,11},{10,... | collective-permute-start | bytes 49160 | tf_op jit(solution)/shard_map/ppermute | solution.py:19
  14.3 7.5 %collective-permute-start.2 = (bf16[64,128]{1,0:T(8,128)(2,1)S(1)}, bf16[64,128]{1,0:T(8,128)(2,1)S(1)}, u32[]{:S(2)}, u32[]{:S(2)}) collective-permute-start(bf16[64,128]{1,0:T(8,128)(2,1)S(1)} %add.227.table), channel_id=1, source_target_pairs={{0,8},{4,12},{8,0},{12,4},{16,24},{20,28},{24,16},{28,20},{1,9},{5... | collective-permute-start | bytes 49160 | tf_op jit(solution)/shard_map/ppermute | solution.py:19
  16.8 11.6 %slice-start = ((s8[4718592]{0:T(1024)(128)(4,1)}), s8[524288]{0:T(1024)(128)(4,1)S(1)}, s32[]{:S(2)}) async-start(s8[4718592]{0:T(1024)(128)(4,1)} %bitcast.56), calls=%async_computation | async-start | bytes 1048576
  21.7 3.9 %collective-permute-start.3 = (bf16[128,128]{1,0:T(8,128)(2,1)S(1)}, bf16[128,128]{1,0:T(8,128)(2,1)S(1)}, u32[]{:S(2)}, u32[]{:S(2)}) collective-permute-start(bf16[128,128]{1,0:T(8,128)(2,1)S(1)} %pad_maximum_fusion.2), channel_id=1, source_target_pairs={{0,16},{4,20},{8,24},{12,28},{16,0},{20,4},{24,8},{28,12},{1,17},{... | collective-permute-start | bytes 98312 | tf_op jit(solution)/shard_map/ppermute | solution.py:19
  23.3 5.2 %collective-permute-start.6 = (bf16[64,2304]{1,0:T(8,128)(2,1)S(1)}, bf16[64,2304]{1,0:T(8,128)(2,1)S(1)}, u32[]{:S(2)}, u32[]{:S(2)}) collective-permute-start(bf16[64,2304]{1,0:T(8,128)(2,1)S(1)} %collective-permute-done.5.refs_1_), channel_id=1, source_target_pairs={{0,4},{4,0},{8,12},{12,8},{16,20},{20,16},{24,28},{28,24},{1,5},{5... | collective-permute-start | bytes 884744 | tf_op jit(solution)/shard_map/ppermute | solution.py:19
  23.3 5.1 %collective-permute-start.8 = (bf16[64,2304]{1,0:T(8,128)(2,1)S(1)}, bf16[64,2304]{1,0:T(8,128)(2,1)S(1)}, u32[]{:S(2)}, u32[]{:S(2)}) collective-permute-start(bf16[64,2304]{1,0:T(8,128)(2,1)S(1)} %collective-permute-done.7.refs_2_), channel_id=1, source_target_pairs={{0,4},{4,0},{8,12},{12,8},{16,20},{20,16},{24,28},{28,24},{1,5},{5... | collective-permute-start | bytes 884744 | tf_op jit(solution)/shard_map/ppermute | solution.py:19
  23.8 4.7 %collective-permute-start.10 = (bf16[64,2304]{1,0:T(8,128)(2,1)S(1)}, bf16[64,2304]{1,0:T(8,128)(2,1)S(1)}, u32[]{:S(2)}, u32[]{:S(2)}) collective-permute-start(bf16[64,2304]{1,0:T(8,128)(2,1)S(1)} %collective-permute-done.9.refs_3_), channel_id=1, source_target_pairs={{0,4},{4,0},{8,12},{12,8},{16,20},{20,16},{24,28},{28,24},{1,5},{5... | collective-permute-start | bytes 884744 | tf_op jit(solution)/shard_map/ppermute | solution.py:19
  30.4 3.3 %collective-permute-start.12 = (bf16[256,2304]{1,0:T(8,128)(2,1)S(1)}, bf16[256,2304]{1,0:T(8,128)(2,1)S(1)}, u32[]{:S(2)}, u32[]{:S(2)}) collective-permute-start(bf16[256,2304]{1,0:T(8,128)(2,1)S(1)} %shard_map.144), channel_id=1, source_target_pairs={{0,4},{4,0},{8,12},{12,8},{16,20},{20,16},{24,28},{28,24},{1,5},{5... | collective-permute-start | bytes 3538952 | tf_op jit(solution)/shard_map/ppermute | solution.py:19
  30.5 3.2 %collective-permute-start.11 = (bf16[256,128]{1,0:T(8,128)(2,1)S(1)}, bf16[256,128]{1,0:T(8,128)(2,1)S(1)}, u32[]{:S(2)}, u32[]{:S(2)}) collective-permute-start(bf16[256,128]{1,0:T(8,128)(2,1)S(1)} %constant_dynamic-update-slice_fusion.table), channel_id=1, source_target_pairs={{0,4},{4,0},{8,12},{12,8},{16,20},{20,16},{24,28},{28,24},{1,5},{5... | collective-permute-start | bytes 196616 | tf_op jit(solution)/shard_map/ppermute | solution.py:19
  33.7 5.6 %copy-start.1 = (bf16[2304,256]{1,0:T(8,128)(2,1)S(1)}, bf16[2304,256]{1,0:T(8,128)(2,1)}, u32[]{:S(2)}) copy-start(bf16[2304,256]{1,0:T(8,128)(2,1)} %gate.1) | copy-start | bytes 3538948
  33.7 5.6 %copy-start.2 = (bf16[2304,256]{1,0:T(8,128)(2,1)S(1)}, bf16[2304,256]{1,0:T(8,128)(2,1)}, u32[]{:S(2)}) copy-start(bf16[2304,256]{1,0:T(8,128)(2,1)} %up.1) | copy-start | bytes 3538948
  35.8 8.0 %collective-permute-start.18 = (bf16[32,2304]{1,0:T(8,128)(2,1)S(1)}, bf16[32,2304]{1,0:T(8,128)(2,1)S(1)}, u32[]{:S(2)}, u32[]{:S(2)}) collective-permute-start(bf16[32,2304]{1,0:T(8,128)(2,1)S(1)} %get-tuple-element.41), channel_id=1, source_target_pairs={{0,24},{4,28},{8,16},{12,20},{16,8},{20,12},{24,0},{28,4},{1,25},{... | collective-permute-start | bytes 442376 | tf_op jit(solution)/shard_map/ppermute | solution.py:19
  38.2 8.3 %collective-permute-start.17 = (bf16[32,2304]{1,0:T(8,128)(2,1)S(1)}, bf16[32,2304]{1,0:T(8,128)(2,1)S(1)}, u32[]{:S(2)}, u32[]{:S(2)}) collective-permute-start(bf16[32,2304]{1,0:T(8,128)(2,1)S(1)} %get-tuple-element.40), channel_id=1, source_target_pairs={{0,16},{4,20},{8,24},{12,28},{16,0},{20,4},{24,8},{28,12},{1,17},{... | collective-permute-start | bytes 442376 | tf_op jit(solution)/shard_map/ppermute | solution.py:19
  38.8 7.9 %collective-permute-start.16 = (bf16[32,2304]{1,0:T(8,128)(2,1)S(1)}, bf16[32,2304]{1,0:T(8,128)(2,1)S(1)}, u32[]{:S(2)}, u32[]{:S(2)}) collective-permute-start(bf16[32,2304]{1,0:T(8,128)(2,1)S(1)} %get-tuple-element.39), channel_id=1, source_target_pairs={{0,8},{4,12},{8,0},{12,4},{16,24},{20,28},{24,16},{28,20},{1,9},{5... | collective-permute-start | bytes 442376 | tf_op jit(solution)/shard_map/ppermute | solution.py:19
  40.7 9.0 %collective-permute-start.15 = (bf16[32,2304]{1,0:T(8,128)(2,1)S(1)}, bf16[32,2304]{1,0:T(8,128)(2,1)S(1)}, u32[]{:S(2)}, u32[]{:S(2)}) collective-permute-start(bf16[32,2304]{1,0:T(8,128)(2,1)S(1)} %get-tuple-element.36), channel_id=1, source_target_pairs={{0,24},{4,28},{8,16},{12,20},{16,8},{20,12},{24,0},{28,4},{1,25},{... | collective-permute-start | bytes 442376 | tf_op jit(solution)/shard_map/ppermute | solution.py:19
  43.2 8.9 %collective-permute-start.14 = (bf16[32,2304]{1,0:T(8,128)(2,1)S(1)}, bf16[32,2304]{1,0:T(8,128)(2,1)S(1)}, u32[]{:S(2)}, u32[]{:S(2)}) collective-permute-start(bf16[32,2304]{1,0:T(8,128)(2,1)S(1)} %get-tuple-element.35), channel_id=1, source_target_pairs={{0,16},{4,20},{8,24},{12,28},{16,0},{20,4},{24,8},{28,12},{1,17},{... | collective-permute-start | bytes 442376 | tf_op jit(solution)/shard_map/ppermute | solution.py:19
  43.7 8.5 %collective-permute-start.13 = (bf16[32,2304]{1,0:T(8,128)(2,1)S(1)}, bf16[32,2304]{1,0:T(8,128)(2,1)S(1)}, u32[]{:S(2)}, u32[]{:S(2)}) collective-permute-start(bf16[32,2304]{1,0:T(8,128)(2,1)S(1)} %get-tuple-element.34), channel_id=1, source_target_pairs={{0,8},{4,12},{8,0},{12,4},{16,24},{20,28},{24,16},{28,20},{1,9},{5... | collective-permute-start | bytes 442376 | tf_op jit(solution)/shard_map/ppermute | solution.py:19
  46.8 33.4 %copy-start.8 = (f32[512]{0:T(512)S(1)}, f32[512]{0:T(512)}, u32[]{:S(2)}) copy-start(f32[512]{0:T(512)} %param.23) | copy-start | bytes 6148
  46.8 5.5 %collective-permute-start.19 = (bf16[32,2304]{1,0:T(8,128)(2,1)S(1)}, bf16[32,2304]{1,0:T(8,128)(2,1)S(1)}, u32[]{:S(2)}, u32[]{:S(2)}) collective-permute-start(bf16[32,2304]{1,0:T(8,128)(2,1)S(1)} %add_convert_fusion.2), channel_id=1, source_target_pairs={{0,1},{1,0},{2,3},{3,2},{4,5},{5,4},{6,7},{7,6},{8,9},{9,8},{10,11... | collective-permute-start | bytes 442376 | tf_op jit(solution)/shard_map/ppermute | solution.py:19
  52.4 9.4 %collective-permute-start.20 = (bf16[2,16,2304]{2,1,0:T(8,128)(2,1)S(1)}, bf16[2,16,2304]{2,1,0:T(8,128)(2,1)S(1)}, u32[]{:S(2)}, u32[]{:S(2)}) collective-permute-start(bf16[2,16,2304]{2,1,0:T(8,128)(2,1)S(1)} %bitcast.107), channel_id=1, source_target_pairs={{0,2},{1,3},{2,0},{3,1},{4,6},{5,7},{6,4},{7,5},{8,10},{9,11},{10,... | collective-permute-start | bytes 442376 | tf_op jit(solution)/shard_map/ppermute | solution.py:19
  61.9 5.8 %collective-permute-start.21 = (bf16[32,2304]{1,0:T(8,128)(2,1)S(1)}, bf16[32,2304]{1,0:T(8,128)(2,1)S(1)}, u32[]{:S(2)}, u32[]{:S(2)}) collective-permute-start(bf16[32,2304]{1,0:T(8,128)(2,1)S(1)} %bitcast.102), channel_id=1, source_target_pairs={{0,1},{1,0},{2,3},{3,2},{4,5},{5,4},{6,7},{7,6},{8,9},{9,8},{10,11... | collective-permute-start | bytes 442376 | tf_op jit(solution)/shard_map/ppermute | solution.py:19
  62.0 10.3 %collective-permute-start.27 = (bf16[32,2304]{1,0:T(8,128)(2,1)S(1)}, bf16[32,2304]{1,0:T(8,128)(2,1)S(1)}, u32[]{:S(2)}, u32[]{:S(2)}) collective-permute-start(bf16[32,2304]{1,0:T(8,128)(2,1)S(1)} %bitcast.103), channel_id=1, source_target_pairs={{0,16},{4,20},{8,24},{12,28},{16,0},{20,4},{24,8},{28,12},{1,17},{... | collective-permute-start | bytes 442376 | tf_op jit(solution)/shard_map/ppermute | solution.py:19
  63.7 8.6 %collective-permute-start.26 = (bf16[32,2304]{1,0:T(8,128)(2,1)S(1)}, bf16[32,2304]{1,0:T(8,128)(2,1)S(1)}, u32[]{:S(2)}, u32[]{:S(2)}) collective-permute-start(bf16[32,2304]{1,0:T(8,128)(2,1)S(1)} %bitcast.104), channel_id=1, source_target_pairs={{0,8},{4,12},{8,0},{12,4},{16,24},{20,28},{24,16},{28,20},{1,9},{5... | collective-permute-start | bytes 442376 | tf_op jit(solution)/shard_map/ppermute | solution.py:19
  67.7 7.7 %collective-permute-start.28 = (bf16[32,2304]{1,0:T(8,128)(2,1)S(1)}, bf16[32,2304]{1,0:T(8,128)(2,1)S(1)}, u32[]{:S(2)}, u32[]{:S(2)}) collective-permute-start(bf16[32,2304]{1,0:T(8,128)(2,1)S(1)} %bitcast.105), channel_id=1, source_target_pairs={{0,24},{4,28},{8,16},{12,20},{16,8},{20,12},{24,0},{28,4},{1,25},{... | collective-permute-start | bytes 442376 | tf_op jit(solution)/shard_map/ppermute | solution.py:19
  68.2 12.0 %copy-start.7 = (bf16[2304,512]{1,0:T(8,128)(2,1)S(1)}, bf16[2304,512]{1,0:T(8,128)(2,1)}, u32[]{:S(2)}) copy-start(bf16[2304,512]{1,0:T(8,128)(2,1)} %param.22) | copy-start | bytes 7077892
  68.2 10.1 %collective-permute-start.24 = (bf16[32,2304]{1,0:T(8,128)(2,1)S(1)}, bf16[32,2304]{1,0:T(8,128)(2,1)S(1)}, u32[]{:S(2)}, u32[]{:S(2)}) collective-permute-start(bf16[32,2304]{1,0:T(8,128)(2,1)S(1)} %collective-permute-done.21), channel_id=1, source_target_pairs={{0,24},{4,28},{8,16},{12,20},{16,8},{20,12},{24,0},{28,4},{1,25},{... | collective-permute-start | bytes 442376 | tf_op jit(solution)/shard_map/ppermute | solution.py:19
  70.6 9.2 %collective-permute-start.23 = (bf16[32,2304]{1,0:T(8,128)(2,1)S(1)}, bf16[32,2304]{1,0:T(8,128)(2,1)S(1)}, u32[]{:S(2)}, u32[]{:S(2)}) collective-permute-start(bf16[32,2304]{1,0:T(8,128)(2,1)S(1)} %collective-permute-done.21), channel_id=1, source_target_pairs={{0,16},{4,20},{8,24},{12,28},{16,0},{20,4},{24,8},{28,12},{1,17},{... | collective-permute-start | bytes 442376 | tf_op jit(solution)/shard_map/ppermute | solution.py:19
  72.3 7.8 %collective-permute-start.22 = (bf16[32,2304]{1,0:T(8,128)(2,1)S(1)}, bf16[32,2304]{1,0:T(8,128)(2,1)S(1)}, u32[]{:S(2)}, u32[]{:S(2)}) collective-permute-start(bf16[32,2304]{1,0:T(8,128)(2,1)S(1)} %collective-permute-done.21), channel_id=1, source_target_pairs={{0,8},{4,12},{8,0},{12,4},{16,24},{20,28},{24,16},{28,20},{1,9},{5... | collective-permute-start | bytes 442376 | tf_op jit(solution)/shard_map/ppermute | solution.py:19
  75.5 7.3 %collective-permute-start.29 = (bf16[128,2304]{1,0:T(8,128)(2,1)S(1)}, bf16[128,2304]{1,0:T(8,128)(2,1)S(1)}, u32[]{:S(2)}, u32[]{:S(2)}) collective-permute-start(bf16[128,2304]{1,0:T(8,128)(2,1)S(1)} %bitcast.62), channel_id=1, source_target_pairs={{0,4},{4,0},{8,12},{12,8},{16,20},{20,16},{24,28},{28,24},{1,5},{5... | collective-permute-start | bytes 1769480 | tf_op jit(solution)/shard_map/ppermute | solution.py:19
  80.2 7.4 %collective-permute-start.25 = (bf16[128,2304]{1,0:T(8,128)(2,1)S(1)}, bf16[128,2304]{1,0:T(8,128)(2,1)S(1)}, u32[]{:S(2)}, u32[]{:S(2)}) collective-permute-start(bf16[128,2304]{1,0:T(8,128)(2,1)S(1)} %bitcast.60), channel_id=1, source_target_pairs={{0,4},{4,0},{8,12},{12,8},{16,20},{20,16},{24,28},{28,24},{1,5},{5... | collective-permute-start | bytes 1769480 | tf_op jit(solution)/shard_map/ppermute | solution.py:19
  81.3 2.2 %collective-permute-start.34 = (bf16[128,2304]{1,0:T(8,128)(2,1)S(1)}, bf16[128,2304]{1,0:T(8,128)(2,1)S(1)}, u32[]{:S(2)}, u32[]{:S(2)}) collective-permute-start(bf16[128,2304]{1,0:T(8,128)(2,1)S(1)} %convolution_convert_fusion), channel_id=1, source_target_pairs={{0,4},{4,0},{8,12},{12,8},{16,20},{20,16},{24,28},{28,24},{1,5},{5... | collective-permute-start | bytes 1769480 | tf_op jit(solution)/shard_map/ppermute | solution.py:19
  82.8 5.2 %collective-permute-start.30 = (bf16[128,2304]{1,0:T(8,128)(2,1)S(1)}, bf16[128,2304]{1,0:T(8,128)(2,1)S(1)}, u32[]{:S(2)}, u32[]{:S(2)}) collective-permute-start(bf16[128,2304]{1,0:T(8,128)(2,1)S(1)} %convolution_convert_fusion.1), channel_id=1, source_target_pairs={{0,4},{4,0},{8,12},{12,8},{16,20},{20,16},{24,28},{28,24},{1,5},{5... | collective-permute-start | bytes 1769480 | tf_op jit(solution)/shard_map/ppermute | solution.py:19
  84.0 8.1 %collective-permute-start.37 = (bf16[32,2304]{1,0:T(8,128)(2,1)S(1)}, bf16[32,2304]{1,0:T(8,128)(2,1)S(1)}, u32[]{:S(2)}, u32[]{:S(2)}) collective-permute-start(bf16[32,2304]{1,0:T(8,128)(2,1)S(1)} %get-tuple-element.52), channel_id=1, source_target_pairs={{0,24},{4,28},{8,16},{12,20},{16,8},{20,12},{24,0},{28,4},{1,25},{... | collective-permute-start | bytes 442376 | tf_op jit(solution)/shard_map/ppermute | solution.py:19
  85.5 9.4 %collective-permute-start.36 = (bf16[32,2304]{1,0:T(8,128)(2,1)S(1)}, bf16[32,2304]{1,0:T(8,128)(2,1)S(1)}, u32[]{:S(2)}, u32[]{:S(2)}) collective-permute-start(bf16[32,2304]{1,0:T(8,128)(2,1)S(1)} %get-tuple-element.53), channel_id=1, source_target_pairs={{0,16},{4,20},{8,24},{12,28},{16,0},{20,4},{24,8},{28,12},{1,17},{... | collective-permute-start | bytes 442376 | tf_op jit(solution)/shard_map/ppermute | solution.py:19
  86.9 7.9 %collective-permute-start.35 = (bf16[32,2304]{1,0:T(8,128)(2,1)S(1)}, bf16[32,2304]{1,0:T(8,128)(2,1)S(1)}, u32[]{:S(2)}, u32[]{:S(2)}) collective-permute-start(bf16[32,2304]{1,0:T(8,128)(2,1)S(1)} %get-tuple-element.51), channel_id=1, source_target_pairs={{0,8},{4,12},{8,0},{12,4},{16,24},{20,28},{24,16},{28,20},{1,9},{5... | collective-permute-start | bytes 442376 | tf_op jit(solution)/shard_map/ppermute | solution.py:19
  88.5 18.9 %copy-start.9 = (f32[2304]{0:T(1024)S(1)}, f32[2304]{0:T(1024)}, u32[]{:S(2)}) copy-start(f32[2304]{0:T(1024)} %param.25) | copy-start | bytes 27652
  88.6 9.4 %collective-permute-start.33 = (bf16[32,2304]{1,0:T(8,128)(2,1)S(1)}, bf16[32,2304]{1,0:T(8,128)(2,1)S(1)}, u32[]{:S(2)}, u32[]{:S(2)}) collective-permute-start(bf16[32,2304]{1,0:T(8,128)(2,1)S(1)} %get-tuple-element.49), channel_id=1, source_target_pairs={{0,24},{4,28},{8,16},{12,20},{16,8},{20,12},{24,0},{28,4},{1,25},{... | collective-permute-start | bytes 442376 | tf_op jit(solution)/shard_map/ppermute | solution.py:19
  90.1 10.5 %collective-permute-start.32 = (bf16[32,2304]{1,0:T(8,128)(2,1)S(1)}, bf16[32,2304]{1,0:T(8,128)(2,1)S(1)}, u32[]{:S(2)}, u32[]{:S(2)}) collective-permute-start(bf16[32,2304]{1,0:T(8,128)(2,1)S(1)} %get-tuple-element.50), channel_id=1, source_target_pairs={{0,16},{4,20},{8,24},{12,28},{16,0},{20,4},{24,8},{28,12},{1,17},{... | collective-permute-start | bytes 442376 | tf_op jit(solution)/shard_map/ppermute | solution.py:19
  92.1 8.6 %collective-permute-start.31 = (bf16[32,2304]{1,0:T(8,128)(2,1)S(1)}, bf16[32,2304]{1,0:T(8,128)(2,1)S(1)}, u32[]{:S(2)}, u32[]{:S(2)}) collective-permute-start(bf16[32,2304]{1,0:T(8,128)(2,1)S(1)} %get-tuple-element.48), channel_id=1, source_target_pairs={{0,8},{4,12},{8,0},{12,4},{16,24},{20,28},{24,16},{28,20},{1,9},{5... | collective-permute-start | bytes 442376 | tf_op jit(solution)/shard_map/ppermute | solution.py:19
  94.9 5.7 %collective-permute-start.38 = (bf16[32,2304]{1,0:T(8,128)(2,1)S(1)}, bf16[32,2304]{1,0:T(8,128)(2,1)S(1)}, u32[]{:S(2)}, u32[]{:S(2)}) collective-permute-start(bf16[32,2304]{1,0:T(8,128)(2,1)S(1)} %fusion.10), channel_id=1, source_target_pairs={{0,1},{1,0},{2,3},{3,2},{4,5},{5,4},{6,7},{7,6},{8,9},{9,8},{10,11... | collective-permute-start | bytes 442376 | tf_op jit(solution)/shard_map/ppermute | solution.py:19
  100.8 6.7 %collective-permute-start.39 = (bf16[16,2304]{1,0:T(8,128)(2,1)S(1)}, bf16[16,2304]{1,0:T(8,128)(2,1)S(1)}, u32[]{:S(2)}, u32[]{:S(2)}) collective-permute-start(bf16[16,2304]{1,0:T(8,128)(2,1)S(1)} %fusion.15), channel_id=1, source_target_pairs={{0,2},{1,3},{2,0},{3,1},{4,6},{5,7},{6,4},{7,5},{8,10},{9,11},{10,... | collective-permute-start | bytes 221192 | tf_op jit(solution)/shard_map/ppermute | solution.py:19
  101.7 6.4 %copy-start.10 = (bf16[32,16,512]{2,1,0:T(8,128)(2,1)}, bf16[32,16,512]{2,1,0:T(8,128)(2,1)S(1)}, u32[]{:S(2)}) copy-start(bf16[32,16,512]{2,1,0:T(8,128)(2,1)S(1)} %constant_dynamic-update-slice_fusion.3) | copy-start | bytes 1572868
  (5 other events, 10.9 us)

commit v9 on v8

--- a/solution.py
+++ b/solution.py
@@ -9,7 +9,7 @@
 
 LANES = 128
 MIB = 1024 * 1024
-LOAD_MIB = 40
+STREAM_MIB = 40
 VMEM_SPEC = pl.BlockSpec(memory_space=pltpu.VMEM)
 SMEM_SPEC = pl.BlockSpec(memory_space=pltpu.SMEM)
 HBM_SPEC = pl.BlockSpec(memory_space=pltpu.HBM)
@@ -93,24 +93,20 @@
     )[0]
 
 
-def load_kernel(table, *refs):
-    count = (len(refs) - 2) // 2
-    copies = start_all(list(zip(refs[:count], refs[count + 1 : -1])), refs[-1])
-    refs[count][...] = table[...]
-    for copy in copies:
-        copy.wait()
-
-
-def run_load(table, values):
-    count = len(values)
+def load_kernel(table, tokens, table_out, tokens_out):
+    table_out[...] = table[...]
+    tokens_out[...] = tokens[...]
+
+
+def run_load(table, tokens):
     return call(
         load_kernel,
-        [table, *values],
-        [VMEM_SPEC] + [HBM_SPEC] * count,
-        [(value.shape, value.dtype) for value in [table] + values],
-        [pltpu.SemaphoreType.DMA((count,))],
-        LOAD_MIB,
-        (550 * sum(value.size for value in values), 4 * sum(value.size for value in values)),
+        [table, tokens],
+        [VMEM_SPEC] * 2,
+        [(value.shape, value.dtype) for value in (table, tokens)],
+        [],
+        2,
+        (0, 4 * tokens.size),
     )
 
 
@@ -138,29 +134,48 @@
     )
 
 
-def hidden_kernel(count, e, tile, *refs):
-    pieces, (gate, up, out, rows) = refs[:count], refs[count:]
-    size = pieces[0].shape[0]
+def hidden_kernel(count, e, tile, stream, *refs):
+    pieces, (gate, up, out), refs = refs[:count], refs[count : count + 3], refs[count + 3 :]
+    size, units = pieces[0].shape[0], out.shape[1]
+    cuts = [slice(j, j + tile) for j in range(0, units, tile)]
+    if stream:
+        gate_held, up_held, rows, sems = refs
+        pairs = []
+        for cut in cuts:
+            pairs.append((gate.at[e, :, cut], gate_held.at[0, :, cut]))
+            pairs.append((up.at[e, :, cut], up_held.at[0, :, cut]))
+        copies = start_all(pairs, sems)
+    else:
+        gate_held, up_held, rows = gate, up, refs[0]
     for i in range(count):
         rows[i * size : (i + 1) * size, :] = pieces[i][...]
-    for j in range(0, out.shape[1], tile):
-        cut = slice(j, j + tile)
-        value = silu(dot(rows[...], gate[e, :, cut]))
-        out[:, cut] = half(value * dot(rows[...], up[e, :, cut]))
-
-
-def run_hidden(pieces, gate, up, e):
+    for i, cut in enumerate(cuts):
+        if stream:
+            copies[2 * i].wait()
+        value = silu(dot(rows[...], gate_held[0, :, cut]))
+        if stream:
+            copies[2 * i + 1].wait()
+        out[:, cut] = half(value * dot(rows[...], up_held[0, :, cut]))
+
+
+def run_hidden(pieces, gate, up, e, stream):
     count, (size, width) = len(pieces), pieces[0].shape
     units = gate.shape[2]
-    return call(
-        functools.partial(hidden_kernel, count, e, min(256, units)),
+    tile = min(256, units)
+    outs = [((count * size, units), jnp.bfloat16)]
+    scratch = [pltpu.VMEM((count * size, width), jnp.bfloat16)]
+    if stream:
+        outs += [((1, width, units), jnp.bfloat16)] * 2
+        scratch.append(pltpu.SemaphoreType.DMA((2 * (units // tile),)))
+    return call(
+        functools.partial(hidden_kernel, count, e, tile, stream),
         [*pieces, gate, up],
-        [VMEM_SPEC] * (count + 2),
-        [((count * size, units), jnp.bfloat16)],
-        [pltpu.VMEM((count * size, width), jnp.bfloat16)],
-        8,
+        [VMEM_SPEC] * count + [HBM_SPEC if stream else VMEM_SPEC] * 2,
+        outs,
+        scratch,
+        STREAM_MIB if stream else 8,
         (4 * count * size * width * units, 4 * width * units),
-    )[0]
+    )
 
 
 def down_kernel(top, e, tile, kind, scalars, hidden, down, table, *refs):
@@ -239,41 +254,40 @@
     table = run_pack(my_feat, expert_ids, gate_weights, feats)
     for bit in feat_bits:
         table = table + swap(table, "feat", bit)
-
-    near = [tokens] + [swap(tokens, "expert", 2 * p) for p in range(1, pairs)]
-    far = [swap(piece, "expert", 1) for piece in near]
-    arrived = swap(table, "expert", 2)
-    table, near[0], expert_gate, expert_up = run_load(
-        table, [tokens, expert_gate, expert_up]
-    )
-    shared_out = run_shared(scalars, far[0], [shared_gate, shared_up, shared_down], own)
-    table = jnp.concatenate([table, arrived], axis=0)
-    for bit in bits_of(pairs)[1:]:
-        table = jnp.concatenate([table, swap(table, "expert", 2 * bit)], axis=0)
+    tables = [swap(table, "expert", 2 * p) for p in range(1, pairs)]
+
+    near = [swap(tokens, "expert", 2 * p) for p in range(1, pairs)]
+    far = [swap(piece, "expert", 1) for piece in [tokens] + near]
+    table, mine = run_load(table, tokens)
+    near = [mine] + near
+
+    hidden = [list(run_hidden(near, expert_gate, expert_up, e, True)) for e in local_experts]
+    hidden[0][0], *rest = lax.optimization_barrier((hidden[0][0], *tables, *far))
+    table = jnp.concatenate([table] + rest[: pairs - 1], axis=0)
+    far = rest[pairs - 1 :]
     table_far = swap(table, "expert", 1)
-
-    table, *far = lax.optimization_barrier((table, *far))
     arrived = None
     for e in local_experts:
-        hidden = run_hidden(near, expert_gate, expert_up, e)
         more = [] if arrived is None else [arrived]
-        arrived = run_down(hidden, expert_down, e, scalars, table, top, more)[0]
+        arrived = run_down(hidden[e][0], expert_down, e, scalars, table, top, more)[0]
     arrived = swap(arrived, "expert", 1)
     for e in local_experts:
-        hidden = run_hidden(far, expert_gate, expert_up, e)
+        hidden_far = run_hidden(far, hidden[e][1], hidden[e][2], e, False)[0]
         if e < local_experts[-1]:
             more = [arrived]
-            arrived = run_down(hidden, expert_down, e, scalars, table_far, top, more)[0]
+            arrived = run_down(hidden_far, expert_down, e, scalars, table_far, top, more)[0]
     blocks = run_down(
-        hidden, expert_down, e, scalars, table_far, top, [arrived], (pairs, own)
-    )
-
-    def reduce_pairs(parts, *more):
-        arrived = [swap(parts[p], "expert", 2 * p) for p in range(1, pairs)]
-        return sum(full(part) for part in [parts[0], *more] + arrived)
-
-    arrived = swap(half(reduce_pairs(blocks[:pairs], shared_out[0])), "feat", feat_bits[0])
-    total = reduce_pairs(blocks[pairs:], shared_out[1]) + full(arrived)
+        hidden_far, expert_down, e, scalars, table_far, top, [arrived], (pairs, own)
+    )
+    blocks = [blocks[:pairs], blocks[pairs:]]
+    blocks = [
+        [mine[0]] + [swap(mine[p], "expert", 2 * p) for p in range(1, pairs)] for mine in blocks
+    ]
+    scalars, blocks[0][-1] = lax.optimization_barrier((scalars, blocks[0][-1]))
+    shared_out = run_shared(scalars, far[0], [shared_gate, shared_up, shared_down], own)
+    totals = [sum(full(part) for part in blocks[i] + [shared_out[i]]) for i in range(2)]
+
+    total = totals[1] + full(swap(half(totals[0]), "feat", feat_bits[0]))
     total = total.reshape((2,) * (len(feat_bits) - 1) + (own, width))
     for i, bit in enumerate(feat_bits[1:-1]):
         dim = len(feat_bits) - 2 - i
@@ -289,21 +303,20 @@
     mine, other = lax.optimization_barrier((moe_out, other))
     parts.append(swap(mine, "expert", 2 * (pairs - 1)))
     sides = [[other] + [swap(other, "expert", 2 * p) for p in range(1, pairs)], parts]
-    near = [jnp.stack(parts).reshape(chunk_rows, width) for parts in sides]
 
     def encode(x):
         return half(jax.nn.relu(dot(x, encoder) + encoder_bias[None, :]))
 
     features, blocks = [None, None], [None, None]
     for chunk in (1, 0):
-        far = swap(near[chunk], "expert", 1)
-        features_near = encode(near[chunk])
+        near = jnp.stack(sides[chunk]).reshape(chunk_rows, width)
+        far = swap(near, "expert", 1)
+        features_near = encode(near)
         decoded = swap(half(dot(features_near, decoder)), "expert", 1)
         features_far = encode(far)
-        total = dot(features_far, decoder) + full(decoded)
+        total = half(dot(features_far, decoder) + full(decoded))
         total = total.reshape(pairs, feats // 2 * own, width)
-        blocks[chunk] = [total[0]]
-        blocks[chunk] += [swap(half(total[p]), "expert", 2 * p) for p in range(1, pairs)]
+        blocks[chunk] = [total[0]] + [swap(total[p], "expert", 2 * p) for p in range(1, pairs)]
         both = jnp.stack([features_far, features_near])
         features[chunk] = both.reshape(2, pairs, feats // 2, 1, own, -1)
     arrived = swap(half(sum(full(block) for block in blocks[1])), "feat", feat_bits[0])

time: 108 us -> 113 us (1.046)
  starting transfers between devices: 40.6 us -> 50.2 us
  waiting for transfers between devices: 42.6 us -> 36.9 us
    ppermute x40 -> x41, starting transfers between devices: 40.6 us -> 50.2 us  [swap(): lax.ppermute(value, axis, [(i, i ^ r) for i in range(lax.axis_size(axis))])]
    ppermute x40 -> x41, waiting for transfers between devices: 42.6 us -> 36.9 us  [swap(): lax.ppermute(value, axis, [(i, i ^ r) for i in range(lax.axis_size(axis))])]
    unnamed x59 -> x60, local copies, waits for them, and re-layouts: 2.85 us -> 2.72 us
  transfers between devices with their start and end apart: 40 -> 41, of which waited for: 20 -> 20; matrix products, arithmetic and copies ran while one was open for 5% -> 5% of each run, Pallas kernels for 10% -> 10%
where the time goes in v9:
time: 113 us
  starting transfers between devices  50.2 us (44%)
  waiting for transfers between devices  36.9 us (33%)
  Pallas kernels  15.8 us (14%)
  matrix products  4.05 us (4%)
  local copies, waits for them, and re-layouts  2.81 us (2%)
  other arithmetic  2.08 us (2%)
  between operations  1.26 us (1%)
    ppermute x41, starting transfers between devices, swap(): lax.ppermute(value, axis, [(i, i ^ r) for i in range(lax.axis_size(axis))])  50.2 us
    ppermute x41, waiting for transfers between devices, swap(): lax.ppermute(value, axis, [(i, i ^ r) for i in range(lax.axis_size(axis))])  36.9 us
    pallas_call x7, Pallas kernels, call(): pl.pallas_call(body, in_specs=specs, out_specs=[VMEM_SPEC] * len(outs), o...  15.8 us
    dot_general x8, matrix products, dot(): return jnp.dot(a, b, preferred_element_type=jnp.float32)  4.05 us
    unnamed x60, local copies, waits for them, and re-layouts  2.72 us
  transfers between devices with their start and end apart: 41, of which 20 were waited for; matrix products, arithmetic and copies ran while one was open for 5% of the time, Pallas kernels for 10%

profile of v9, /device:TPU:0, one launch (start us, length us, event | category | flops | bytes accessed | tf_op | source)
XLA Modules:
  0.0 113.1 jit_solution(16101339102982054025)
XLA Ops:
  0.6 3.0 %collective-permute-start.2 = (bf16[64,2304]{1,0:T(8,128)(2,1)}, bf16[64,2304]{1,0:T(8,128)(2,1)S(1)}, u32[]{:S(2)}, u32[]{:S(2)}) collective-permute-start(bf16[64,2304]{1,0:T(8,128)(2,1)} %tokens.1), channel_id=1, source_target_pairs={{0,8},{4,12},{8,0},{12,4},{16,24},{20,28},{24,16},{28,20},{1,9},{5... | collective-permute-start | bytes 884744 | tf_op jit(solution)/shard_map/ppermute | solution.py:19
  3.6 1.5 %collective-permute-start.3 = (bf16[64,2304]{1,0:T(8,128)(2,1)}, bf16[64,2304]{1,0:T(8,128)(2,1)S(1)}, u32[]{:S(2)}, u32[]{:S(2)}) collective-permute-start(bf16[64,2304]{1,0:T(8,128)(2,1)} %tokens.1), channel_id=1, source_target_pairs={{0,16},{4,20},{8,24},{12,28},{16,0},{20,4},{24,8},{28,12},{1,17},{... | collective-permute-start | bytes 884744 | tf_op jit(solution)/shard_map/ppermute | solution.py:19
  6.7 2.0 %collective-permute-start = (bf16[64,128]{1,0:T(8,128)(2,1)S(1)}, bf16[64,128]{1,0:T(8,128)(2,1)S(1)}, u32[]{:S(2)}, u32[]{:S(2)}) collective-permute-start(bf16[64,128]{1,0:T(8,128)(2,1)S(1)} %shard_map.140), channel_id=1, source_target_pairs={{0,1},{1,0},{2,3},{3,2},{4,5},{5,4},{6,7},{7,6},{8,9},{9,8},{10,11... | collective-permute-start | bytes 49160 | tf_op jit(solution)/shard_map/ppermute | solution.py:19
  8.8 1.7 %collective-permute-done = bf16[64,128]{1,0:T(8,128)(2,1)S(1)} collective-permute-done((bf16[64,128]{1,0:T(8,128)(2,1)S(1)}, bf16[64,128]{1,0:T(8,128)(2,1)S(1)}, u32[]{:S(2)}, u32[]{:S(2)}) %collective-permute-start) | collective-permute-done | bytes 16416 | tf_op jit(solution)/shard_map/ppermute | solution.py:19
  10.5 3.1 %collective-permute-start.1 = (bf16[64,128]{1,0:T(8,128)(2,1)S(1)}, bf16[64,128]{1,0:T(8,128)(2,1)}, u32[]{:S(2)}, u32[]{:S(2)}) collective-permute-start(bf16[64,128]{1,0:T(8,128)(2,1)S(1)} %add.226), channel_id=1, source_target_pairs={{0,2},{1,3},{2,0},{3,1},{4,6},{5,7},{6,4},{7,5},{8,10},{9,11},{10,... | collective-permute-start | bytes 49160 | tf_op jit(solution)/shard_map/ppermute | solution.py:19
  13.6 1.8 %collective-permute-done.1 = bf16[64,128]{1,0:T(8,128)(2,1)} collective-permute-done((bf16[64,128]{1,0:T(8,128)(2,1)S(1)}, bf16[64,128]{1,0:T(8,128)(2,1)}, u32[]{:S(2)}, u32[]{:S(2)}) %collective-permute-start.1) | collective-permute-done | bytes 16416 | tf_op jit(solution)/shard_map/ppermute | solution.py:19
  16.2 1.8 %collective-permute-start.5 = (bf16[64,128]{1,0:T(8,128)(2,1)S(1)}, bf16[64,128]{1,0:T(8,128)(2,1)S(1)}, u32[]{:S(2)}, u32[]{:S(2)}) collective-permute-start(bf16[64,128]{1,0:T(8,128)(2,1)S(1)} %add.227.table), channel_id=1, source_target_pairs={{0,8},{4,12},{8,0},{12,4},{16,24},{20,28},{24,16},{28,20},{1,9},{5... | collective-permute-start | bytes 49160 | tf_op jit(solution)/shard_map/ppermute | solution.py:19
  18.1 1.0 copy-done.4
  19.0 0.9 collective-permute-done.5
  19.9 1.8 %collective-permute-start.6 = (bf16[64,128]{1,0:T(8,128)(2,1)S(1)}, bf16[64,128]{1,0:T(8,128)(2,1)S(1)}, u32[]{:S(2)}, u32[]{:S(2)}) collective-permute-start(bf16[64,128]{1,0:T(8,128)(2,1)S(1)} %add.227.table), channel_id=1, source_target_pairs={{0,16},{4,20},{8,24},{12,28},{16,0},{20,4},{24,8},{28,12},{1,17},{... | collective-permute-start | bytes 49160 | tf_op jit(solution)/shard_map/ppermute | solution.py:19
  22.3 1.3 %collective-permute-done.6 = bf16[64,128]{1,0:T(8,128)(2,1)S(1)} collective-permute-done((bf16[64,128]{1,0:T(8,128)(2,1)S(1)}, bf16[64,128]{1,0:T(8,128)(2,1)S(1)}, u32[]{:S(2)}, u32[]{:S(2)}) %collective-permute-start.6) | collective-permute-done | bytes 16416 | tf_op jit(solution)/shard_map/ppermute | solution.py:19
  23.6 2.8 %collective-permute-start.7 = (bf16[64,128]{1,0:T(8,128)(2,1)S(1)}, bf16[64,128]{1,0:T(8,128)(2,1)S(1)}, u32[]{:S(2)}, u32[]{:S(2)}) collective-permute-start(bf16[64,128]{1,0:T(8,128)(2,1)S(1)} %add.227.table), channel_id=1, source_target_pairs={{0,24},{4,28},{8,16},{12,20},{16,8},{20,12},{24,0},{28,4},{1,25},{... | collective-permute-start | bytes 49160 | tf_op jit(solution)/shard_map/ppermute | solution.py:19
  26.4 7.5 %shard_map.142 = (bf16[256,1024]{1,0:T(8,128)(2,1)S(1)}, bf16[1,2304,1024]{2,1,0:T(8,128)(2,1)S(1)}, bf16[1,2304,1024]{2,1,0:T(8,128)(2,1)S(1)}) custom-call(bf16[64,2304]{1,0:T(8,128)(2,1)S(1)} %get-tuple-element.29.refs_0_, bf16[64,2304]{1,0:T(8,128)(2,1)S(1)} %collective-permute-done.2.refs_1_, bf16[64,2304]{1,0:T(8,128)(2,1)S(1)} %collective-permute-done.3.refs_2_, ...), custom_call_target="tpu_custom_call" | custom-call | flops 2415919104 | bytes 9437184 | tf_op jit(solution)/shard_map/pallas_call | solution.py:49
  34.1 1.9 %shard_map.144 = bf16[256,2304]{1,0:T(8,128)(2,1)S(1)} custom-call(s32[2]{0:T(128)S(1)} %pad_add_fusion.scalars, bf16[256,1024]{1,0:T(8,128)(2,1)S(1)} %get-tuple-element.41.hidden, bf16[1,1024,2304]{2,1,0:T(8,128)(2,1)S(1)} %bitcast.57, bf16[256,128]{1,0:T(8,128)(2,1)S(1)} %constant_dynamic-update-slice_fusion.table), custom_call_target="tpu_custom_call" | custom-call | flops 1207959552 | bytes 4718592 | tf_op jit(solution)/shard_map/pallas_call | solution.py:49
  36.6 2.7 %shard_map.143.hidden = bf16[256,1024]{1,0:T(8,128)(2,1)S(1)} custom-call(bf16[64,2304]{1,0:T(8,128)(2,1)S(1)} %collective-permute-done.8.refs_0_.x, bf16[64,2304]{1,0:T(8,128)(2,1)S(1)} %collective-permute-done.9.refs_1_, bf16[64,2304]{1,0:T(8,128)(2,1)S(1)} %collective-permute-done.10.refs_2_, bf16[64,2304]{1,0:T(8,128)(2,1)S(1)} %collective-permute-done.11.refs_3_, ...), custom_call_target="tpu_custom_call" | custom-call | flops 2415919104 | bytes 9437184 | tf_op jit(solution)/shard_map/pallas_call | solution.py:49
  39.3 2.1 %shard_map.145 = (bf16[32,2304]{1,0:T(8,128)(2,1)S(1)}, bf16[32,2304]{1,0:T(8,128)(2,1)S(1)}, bf16[32,2304]{1,0:T(8,128)(2,1)S(1)}, bf16[32,2304]{1,0:T(8,128)(2...) custom-call(s32[2]{0:T(128)S(1)} %pad_add_fusion.scalars, ...), custom_call_target="tpu_custom_call" | custom-call | flops 1207959552 | bytes 4718592 | tf_op jit(solution)/shard_map/pallas_call | solution.py:49
  41.6 1.8 %collective-permute-start.19 = (bf16[32,2304]{1,0:T(8,128)(2,1)S(1)}, bf16[32,2304]{1,0:T(8,128)(2,1)S(1)}, u32[]{:S(2)}, u32[]{:S(2)}) collective-permute-start(bf16[32,2304]{1,0:T(8,128)(2,1)S(1)} %get-tuple-element.51), channel_id=1, source_target_pairs={{0,16},{4,20},{8,24},{12,28},{16,0},{20,4},{24,8},{28,12},{1,17},{... | collective-permute-start | bytes 442376 | tf_op jit(solution)/shard_map/ppermute | solution.py:19
  43.5 1.5 %collective-permute-start.18 = (bf16[32,2304]{1,0:T(8,128)(2,1)S(1)}, bf16[32,2304]{1,0:T(8,128)(2,1)S(1)}, u32[]{:S(2)}, u32[]{:S(2)}) collective-permute-start(bf16[32,2304]{1,0:T(8,128)(2,1)S(1)} %get-tuple-element.50), channel_id=1, source_target_pairs={{0,8},{4,12},{8,0},{12,4},{16,24},{20,28},{24,16},{28,20},{1,9},{5... | collective-permute-start | bytes 442376 | tf_op jit(solution)/shard_map/ppermute | solution.py:19
  45.1 1.8 %collective-permute-start.15 = (bf16[32,2304]{1,0:T(8,128)(2,1)S(1)}, bf16[32,2304]{1,0:T(8,128)(2,1)S(1)}, u32[]{:S(2)}, u32[]{:S(2)}) collective-permute-start(bf16[32,2304]{1,0:T(8,128)(2,1)S(1)} %get-tuple-element.44), channel_id=1, source_target_pairs={{0,16},{4,20},{8,24},{12,28},{16,0},{20,4},{24,8},{28,12},{1,17},{... | collective-permute-start | bytes 442376 | tf_op jit(solution)/shard_map/ppermute | solution.py:19
  46.9 2.2 %collective-permute-done.17 = bf16[32,2304]{1,0:T(8,128)(2,1)S(1)} collective-permute-done((bf16[32,2304]{1,0:T(8,128)(2,1)S(1)}, bf16[32,2304]{1,0:T(8,128)(2,1)S(1)}, u32[]{:S(2)}, u32[]{:S(2)}) %collective-permute-start.17) | collective-permute-done | bytes 147488 | tf_op jit(solution)/shard_map/ppermute | solution.py:19
  49.6 1.4 %shard_map.146 = (f32[32,2304]{1,0:T(8,128)S(1)}, f32[32,2304]{1,0:T(8,128)S(1)}) custom-call(s32[2]{0:T(128)S(1)} %pad_add_fusion.scalars, bf16[64,2304]{1,0:T(8,128)(2,1)S(1)} %collective-permute-done.8.refs_0_.x, bf16[2304,256]{1,0:T(8,128)(2,1)S(1)} %copy-done.1, bf16[2304,256]{1,0:T(8,128)(2,1)S(1)} %copy-done.2, bf16[256,2304]{1,0:T(8,128)(2,1)S(1)} %copy-done.3), custom_call_target="tpu_custom_call" | custom-call | flops 226492416 | bytes 3538944 | tf_op jit(solution)/shard_map/pallas_call | solution.py:49
  51.0 1.3 %collective-permute-done.19 = bf16[32,2304]{1,0:T(8,128)(2,1)S(1)} collective-permute-done((bf16[32,2304]{1,0:T(8,128)(2,1)S(1)}, bf16[32,2304]{1,0:T(8,128)(2,1)S(1)}, u32[]{:S(2)}, u32[]{:S(2)}) %collective-permute-start.19) | collective-permute-done | bytes 147488 | tf_op jit(solution)/shard_map/ppermute | solution.py:19
  52.4 1.7 %collective-permute-start.20 = (bf16[32,2304]{1,0:T(8,128)(2,1)S(1)}, bf16[32,2304]{1,0:T(8,128)(2,1)S(1)}, u32[]{:S(2)}, u32[]{:S(2)}) collective-permute-start(bf16[32,2304]{1,0:T(8,128)(2,1)S(1)} %add_convert_fusion.5), channel_id=1, source_target_pairs={{0,1},{1,0},{2,3},{3,2},{4,5},{5,4},{6,7},{7,6},{8,9},{9,8},{10,11... | collective-permute-start | bytes 442376 | tf_op jit(solution)/shard_map/ppermute | solution.py:19
  54.1 1.4 %collective-permute-done.16 = bf16[32,2304]{1,0:T(8,128)(2,1)S(1)} collective-permute-done((bf16[32,2304]{1,0:T(8,128)(2,1)S(1)}, bf16[32,2304]{1,0:T(8,128)(2,1)S(1)}, u32[]{:S(2)}, u32[]{:S(2)}) %collective-permute-start.16) | collective-permute-done | bytes 147488 | tf_op jit(solution)/shard_map/ppermute | solution.py:19
  55.5 1.4 %collective-permute-done.15 = bf16[32,2304]{1,0:T(8,128)(2,1)S(1)} collective-permute-done((bf16[32,2304]{1,0:T(8,128)(2,1)S(1)}, bf16[32,2304]{1,0:T(8,128)(2,1)S(1)}, u32[]{:S(2)}, u32[]{:S(2)}) %collective-permute-start.15) | collective-permute-done | bytes 147488 | tf_op jit(solution)/shard_map/ppermute | solution.py:19
  56.9 0.8 collective-permute-done.20
  57.7 2.7 %collective-permute-start.21 = (bf16[2,16,2304]{2,1,0:T(8,128)(2,1)S(1)}, bf16[2,16,2304]{2,1,0:T(8,128)(2,1)S(1)}, u32[]{:S(2)}, u32[]{:S(2)}) collective-permute-start(bf16[2,16,2304]{2,1,0:T(8,128)(2,1)S(1)} %bitcast.107), channel_id=1, source_target_pairs={{0,2},{1,3},{2,0},{3,1},{4,6},{5,7},{6,4},{7,5},{8,10},{9,11},{10,... | collective-permute-start | bytes 442376 | tf_op jit(solution)/shard_map/ppermute | solution.py:19
  60.4 5.8 %collective-permute-done.21 = bf16[2,16,2304]{2,1,0:T(8,128)(2,1)S(1)} collective-permute-done((bf16[2,16,2304]{2,1,0:T(8,128)(2,1)S(1)}, bf16[2,16,2304]{2,1,0:T(8,128)(2,1)S(1)}, u32[]{:S(2)}, u32[]{:S(2)}) %collective-permute-start.21) | collective-permute-done | bytes 147488 | tf_op jit(solution)/shard_map/ppermute | solution.py:19
  66.3 0.8 collective-permute-start.22
  67.1 1.9 %collective-permute-start.28 = (bf16[32,2304]{1,0:T(8,128)(2,1)S(1)}, bf16[32,2304]{1,0:T(8,128)(2,1)S(1)}, u32[]{:S(2)}, u32[]{:S(2)}) collective-permute-start(bf16[32,2304]{1,0:T(8,128)(2,1)S(1)} %bitcast.103), channel_id=1, source_target_pairs={{0,16},{4,20},{8,24},{12,28},{16,0},{20,4},{24,8},{28,12},{1,17},{... | collective-permute-start | bytes 442376 | tf_op jit(solution)/shard_map/ppermute | solution.py:19
  69.5 2.0 %collective-permute-done.22 = bf16[32,2304]{1,0:T(8,128)(2,1)S(1)} collective-permute-done((bf16[32,2304]{1,0:T(8,128)(2,1)S(1)}, bf16[32,2304]{1,0:T(8,128)(2,1)S(1)}, u32[]{:S(2)}, u32[]{:S(2)}) %collective-permute-start.22) | collective-permute-done | bytes 147488 | tf_op jit(solution)/shard_map/ppermute | solution.py:19
  71.5 1.9 %collective-permute-start.29 = (bf16[32,2304]{1,0:T(8,128)(2,1)S(1)}, bf16[32,2304]{1,0:T(8,128)(2,1)S(1)}, u32[]{:S(2)}, u32[]{:S(2)}) collective-permute-start(bf16[32,2304]{1,0:T(8,128)(2,1)S(1)} %bitcast.105), channel_id=1, source_target_pairs={{0,24},{4,28},{8,16},{12,20},{16,8},{20,12},{24,0},{28,4},{1,25},{... | collective-permute-start | bytes 442376 | tf_op jit(solution)/shard_map/ppermute | solution.py:19
  73.4 1.0 collective-permute-start.25
  74.4 2.0 %collective-permute-start.24 = (bf16[32,2304]{1,0:T(8,128)(2,1)S(1)}, bf16[32,2304]{1,0:T(8,128)(2,1)S(1)}, u32[]{:S(2)}, u32[]{:S(2)}) collective-permute-start(bf16[32,2304]{1,0:T(8,128)(2,1)S(1)} %collective-permute-done.22), channel_id=1, source_target_pairs={{0,16},{4,20},{8,24},{12,28},{16,0},{20,4},{24,8},{28,12},{1,17},{... | collective-permute-start | bytes 442376 | tf_op jit(solution)/shard_map/ppermute | solution.py:19
  76.9 2.3 %collective-permute-done.29 = bf16[32,2304]{1,0:T(8,128)(2,1)S(1)} collective-permute-done((bf16[32,2304]{1,0:T(8,128)(2,1)S(1)}, bf16[32,2304]{1,0:T(8,128)(2,1)S(1)}, u32[]{:S(2)}, u32[]{:S(2)}) %collective-permute-start.29) | collective-permute-done | bytes 147488 | tf_op jit(solution)/shard_map/ppermute | solution.py:19
  79.4 2.6 %collective-permute-done.25 = bf16[32,2304]{1,0:T(8,128)(2,1)S(1)} collective-permute-done((bf16[32,2304]{1,0:T(8,128)(2,1)S(1)}, bf16[32,2304]{1,0:T(8,128)(2,1)S(1)}, u32[]{:S(2)}, u32[]{:S(2)}) %collective-permute-start.25) | collective-permute-done | bytes 147488 | tf_op jit(solution)/shard_map/ppermute | solution.py:19
  81.9 1.2 %collective-permute-done.24 = bf16[32,2304]{1,0:T(8,128)(2,1)S(1)} collective-permute-done((bf16[32,2304]{1,0:T(8,128)(2,1)S(1)}, bf16[32,2304]{1,0:T(8,128)(2,1)S(1)}, u32[]{:S(2)}, u32[]{:S(2)}) %collective-permute-start.24) | collective-permute-done | bytes 147488 | tf_op jit(solution)/shard_map/ppermute | solution.py:19
  87.8 1.6 %collective-permute-start.38 = (bf16[32,2304]{1,0:T(8,128)(2,1)S(1)}, bf16[32,2304]{1,0:T(8,128)(2,1)S(1)}, u32[]{:S(2)}, u32[]{:S(2)}) collective-permute-start(bf16[32,2304]{1,0:T(8,128)(2,1)S(1)} %get-tuple-element.60), channel_id=1, source_target_pairs={{0,24},{4,28},{8,16},{12,20},{16,8},{20,12},{24,0},{28,4},{1,25},{... | collective-permute-start | bytes 442376 | tf_op jit(solution)/shard_map/ppermute | solution.py:19
  89.3 1.4 %collective-permute-start.37 = (bf16[32,2304]{1,0:T(8,128)(2,1)S(1)}, bf16[32,2304]{1,0:T(8,128)(2,1)S(1)}, u32[]{:S(2)}, u32[]{:S(2)}) collective-permute-start(bf16[32,2304]{1,0:T(8,128)(2,1)S(1)} %get-tuple-element.61), channel_id=1, source_target_pairs={{0,16},{4,20},{8,24},{12,28},{16,0},{20,4},{24,8},{28,12},{1,17},{... | collective-permute-start | bytes 442376 | tf_op jit(solution)/shard_map/ppermute | solution.py:19
  92.4 1.6 %collective-permute-start.34 = (bf16[32,2304]{1,0:T(8,128)(2,1)S(1)}, bf16[32,2304]{1,0:T(8,128)(2,1)S(1)}, u32[]{:S(2)}, u32[]{:S(2)}) collective-permute-start(bf16[32,2304]{1,0:T(8,128)(2,1)S(1)} %get-tuple-element.57), channel_id=1, source_target_pairs={{0,24},{4,28},{8,16},{12,20},{16,8},{20,12},{24,0},{28,4},{1,25},{... | collective-permute-start | bytes 442376 | tf_op jit(solution)/shard_map/ppermute | solution.py:19
  94.0 1.4 %collective-permute-start.33 = (bf16[32,2304]{1,0:T(8,128)(2,1)S(1)}, bf16[32,2304]{1,0:T(8,128)(2,1)S(1)}, u32[]{:S(2)}, u32[]{:S(2)}) collective-permute-start(bf16[32,2304]{1,0:T(8,128)(2,1)S(1)} %get-tuple-element.58), channel_id=1, source_target_pairs={{0,16},{4,20},{8,24},{12,28},{16,0},{20,4},{24,8},{28,12},{1,17},{... | collective-permute-start | bytes 442376 | tf_op jit(solution)/shard_map/ppermute | solution.py:19
  96.0 0.9 collective-permute-start.32
  96.9 1.7 %collective-permute-done.37 = bf16[32,2304]{1,0:T(8,128)(2,1)S(1)} collective-permute-done((bf16[32,2304]{1,0:T(8,128)(2,1)S(1)}, bf16[32,2304]{1,0:T(8,128)(2,1)S(1)}, u32[]{:S(2)}, u32[]{:S(2)}) %collective-permute-start.37) | collective-permute-done | bytes 147488 | tf_op jit(solution)/shard_map/ppermute | solution.py:19
  98.7 1.8 %collective-permute-start.39 = (bf16[32,2304]{1,0:T(8,128)(2,1)S(1)}, bf16[32,2304]{1,0:T(8,128)(2,1)S(1)}, u32[]{:S(2)}, u32[]{:S(2)}) collective-permute-start(bf16[32,2304]{1,0:T(8,128)(2,1)S(1)} %add_convert_fusion.2), channel_id=1, source_target_pairs={{0,1},{1,0},{2,3},{3,2},{4,5},{5,4},{6,7},{7,6},{8,9},{9,8},{10,11... | collective-permute-start | bytes 442376 | tf_op jit(solution)/shard_map/ppermute | solution.py:19
  100.6 1.3 %collective-permute-done.34 = bf16[32,2304]{1,0:T(8,128)(2,1)S(1)} collective-permute-done((bf16[32,2304]{1,0:T(8,128)(2,1)S(1)}, bf16[32,2304]{1,0:T(8,128)(2,1)S(1)}, u32[]{:S(2)}, u32[]{:S(2)}) %collective-permute-start.34) | collective-permute-done | bytes 147488 | tf_op jit(solution)/shard_map/ppermute | solution.py:19
  101.8 2.6 %collective-permute-done.33 = bf16[32,2304]{1,0:T(8,128)(2,1)S(1)} collective-permute-done((bf16[32,2304]{1,0:T(8,128)(2,1)S(1)}, bf16[32,2304]{1,0:T(8,128)(2,1)S(1)}, u32[]{:S(2)}, u32[]{:S(2)}) %collective-permute-start.33) | collective-permute-done | bytes 147488 | tf_op jit(solution)/shard_map/ppermute | solution.py:19
  104.6 3.8 %collective-permute-start.40 = (bf16[16,2304]{1,0:T(8,128)(2,1)S(1)}, bf16[16,2304]{1,0:T(8,128)(2,1)S(1)}, u32[]{:S(2)}, u32[]{:S(2)}) collective-permute-start(bf16[16,2304]{1,0:T(8,128)(2,1)S(1)} %fusion.9), channel_id=1, source_target_pairs={{0,2},{1,3},{2,0},{3,1},{4,6},{5,7},{6,4},{7,5},{8,10},{9,11},{10,... | collective-permute-start | bytes 221192 | tf_op jit(solution)/shard_map/ppermute | solution.py:19
  108.4 4.0 %collective-permute-done.40 = bf16[16,2304]{1,0:T(8,128)(2,1)S(1)} collective-permute-done((bf16[16,2304]{1,0:T(8,128)(2,1)S(1)}, bf16[16,2304]{1,0:T(8,128)(2,1)S(1)}, u32[]{:S(2)}, u32[]{:S(2)}) %collective-permute-start.40) | collective-permute-done | bytes 73760 | tf_op jit(solution)/shard_map/ppermute | solution.py:19
  (127 shorter events, 13.4 us)
Async XLA Ops:
  0.6 83.9 %copy-start = (bf16[512,2304]{1,0:T(8,128)(2,1)S(1)}, bf16[512,2304]{1,0:T(8,128)(2,1)}, u32[]{:S(2)}) copy-start(bf16[512,2304]{1,0:T(8,128)(2,1)} %param.24) | copy-start | bytes 7077892
  0.6 21.1 %collective-permute-start.2 = (bf16[64,2304]{1,0:T(8,128)(2,1)}, bf16[64,2304]{1,0:T(8,128)(2,1)S(1)}, u32[]{:S(2)}, u32[]{:S(2)}) collective-permute-start(bf16[64,2304]{1,0:T(8,128)(2,1)} %tokens.1), channel_id=1, source_target_pairs={{0,8},{4,12},{8,0},{12,4},{16,24},{20,28},{24,16},{28,20},{1,9},{5... | collective-permute-start | bytes 884744 | tf_op jit(solution)/shard_map/ppermute | solution.py:19
  3.6 18.1 %collective-permute-start.3 = (bf16[64,2304]{1,0:T(8,128)(2,1)}, bf16[64,2304]{1,0:T(8,128)(2,1)S(1)}, u32[]{:S(2)}, u32[]{:S(2)}) collective-permute-start(bf16[64,2304]{1,0:T(8,128)(2,1)} %tokens.1), channel_id=1, source_target_pairs={{0,16},{4,20},{8,24},{12,28},{16,0},{20,4},{24,8},{28,12},{1,17},{... | collective-permute-start | bytes 884744 | tf_op jit(solution)/shard_map/ppermute | solution.py:19
  5.2 17.1 %collective-permute-start.4 = (bf16[64,2304]{1,0:T(8,128)(2,1)}, bf16[64,2304]{1,0:T(8,128)(2,1)S(1)}, u32[]{:S(2)}, u32[]{:S(2)}) collective-permute-start(bf16[64,2304]{1,0:T(8,128)(2,1)} %tokens.1), channel_id=1, source_target_pairs={{0,24},{4,28},{8,16},{12,20},{16,8},{20,12},{24,0},{28,4},{1,25},{... | collective-permute-start | bytes 884744 | tf_op jit(solution)/shard_map/ppermute | solution.py:19
  6.7 3.8 %collective-permute-start = (bf16[64,128]{1,0:T(8,128)(2,1)S(1)}, bf16[64,128]{1,0:T(8,128)(2,1)S(1)}, u32[]{:S(2)}, u32[]{:S(2)}) collective-permute-start(bf16[64,128]{1,0:T(8,128)(2,1)S(1)} %shard_map.140), channel_id=1, source_target_pairs={{0,1},{1,0},{2,3},{3,2},{4,5},{5,4},{6,7},{7,6},{8,9},{9,8},{10,11... | collective-permute-start | bytes 49160 | tf_op jit(solution)/shard_map/ppermute | solution.py:19
  10.5 4.9 %collective-permute-start.1 = (bf16[64,128]{1,0:T(8,128)(2,1)S(1)}, bf16[64,128]{1,0:T(8,128)(2,1)}, u32[]{:S(2)}, u32[]{:S(2)}) collective-permute-start(bf16[64,128]{1,0:T(8,128)(2,1)S(1)} %add.226), channel_id=1, source_target_pairs={{0,2},{1,3},{2,0},{3,1},{4,6},{5,7},{6,4},{7,5},{8,10},{9,11},{10,... | collective-permute-start | bytes 49160 | tf_op jit(solution)/shard_map/ppermute | solution.py:19
  13.6 20.4 %collective-permute-start.8 = (bf16[64,2304]{1,0:T(8,128)(2,1)}, bf16[64,2304]{1,0:T(8,128)(2,1)S(1)}, u32[]{:S(2)}, u32[]{:S(2)}) collective-permute-start(bf16[64,2304]{1,0:T(8,128)(2,1)} %tokens.1), channel_id=1, source_target_pairs={{0,4},{4,0},{8,12},{12,8},{16,20},{20,16},{24,28},{28,24},{1,5},{5... | collective-permute-start | bytes 884744 | tf_op jit(solution)/shard_map/ppermute | solution.py:19
  16.2 3.7 %collective-permute-start.5 = (bf16[64,128]{1,0:T(8,128)(2,1)S(1)}, bf16[64,128]{1,0:T(8,128)(2,1)S(1)}, u32[]{:S(2)}, u32[]{:S(2)}) collective-permute-start(bf16[64,128]{1,0:T(8,128)(2,1)S(1)} %add.227.table), channel_id=1, source_target_pairs={{0,8},{4,12},{8,0},{12,4},{16,24},{20,28},{24,16},{28,20},{1,9},{5... | collective-permute-start | bytes 49160 | tf_op jit(solution)/shard_map/ppermute | solution.py:19
  19.0 15.0 %slice-start = ((s8[4718592]{0:T(1024)(128)(4,1)}), s8[4194304]{0:T(1024)(128)(4,1)S(1)}, s32[]{:S(2)}) async-start(s8[4718592]{0:T(1024)(128)(4,1)} %bitcast.56), calls=%async_computation | async-start | bytes 8388608
  19.9 3.7 %collective-permute-start.6 = (bf16[64,128]{1,0:T(8,128)(2,1)S(1)}, bf16[64,128]{1,0:T(8,128)(2,1)S(1)}, u32[]{:S(2)}, u32[]{:S(2)}) collective-permute-start(bf16[64,128]{1,0:T(8,128)(2,1)S(1)} %add.227.table), channel_id=1, source_target_pairs={{0,16},{4,20},{8,24},{12,28},{16,0},{20,4},{24,8},{28,12},{1,17},{... | collective-permute-start | bytes 49160 | tf_op jit(solution)/shard_map/ppermute | solution.py:19
  21.8 12.2 %collective-permute-start.9 = (bf16[64,2304]{1,0:T(8,128)(2,1)S(1)}, bf16[64,2304]{1,0:T(8,128)(2,1)S(1)}, u32[]{:S(2)}, u32[]{:S(2)}) collective-permute-start(bf16[64,2304]{1,0:T(8,128)(2,1)S(1)} %collective-permute-done.2.refs_1_), channel_id=1, source_target_pairs={{0,4},{4,0},{8,12},{12,8},{16,20},{20,16},{24,28},{28,24},{1,5},{5... | collective-permute-start | bytes 884744 | tf_op jit(solution)/shard_map/ppermute | solution.py:19
  21.8 12.2 %collective-permute-start.10 = (bf16[64,2304]{1,0:T(8,128)(2,1)S(1)}, bf16[64,2304]{1,0:T(8,128)(2,1)S(1)}, u32[]{:S(2)}, u32[]{:S(2)}) collective-permute-start(bf16[64,2304]{1,0:T(8,128)(2,1)S(1)} %collective-permute-done.3.refs_2_), channel_id=1, source_target_pairs={{0,4},{4,0},{8,12},{12,8},{16,20},{20,16},{24,28},{28,24},{1,5},{5... | collective-permute-start | bytes 884744 | tf_op jit(solution)/shard_map/ppermute | solution.py:19
  22.3 11.7 %collective-permute-start.11 = (bf16[64,2304]{1,0:T(8,128)(2,1)S(1)}, bf16[64,2304]{1,0:T(8,128)(2,1)S(1)}, u32[]{:S(2)}, u32[]{:S(2)}) collective-permute-start(bf16[64,2304]{1,0:T(8,128)(2,1)S(1)} %collective-permute-done.4.refs_3_), channel_id=1, source_target_pairs={{0,4},{4,0},{8,12},{12,8},{16,20},{20,16},{24,28},{28,24},{1,5},{5... | collective-permute-start | bytes 884744 | tf_op jit(solution)/shard_map/ppermute | solution.py:19
  23.6 10.3 %collective-permute-start.7 = (bf16[64,128]{1,0:T(8,128)(2,1)S(1)}, bf16[64,128]{1,0:T(8,128)(2,1)S(1)}, u32[]{:S(2)}, u32[]{:S(2)}) collective-permute-start(bf16[64,128]{1,0:T(8,128)(2,1)S(1)} %add.227.table), channel_id=1, source_target_pairs={{0,24},{4,28},{8,16},{12,20},{16,8},{20,12},{24,0},{28,4},{1,25},{... | collective-permute-start | bytes 49160 | tf_op jit(solution)/shard_map/ppermute | solution.py:19
  36.0 3.3 %collective-permute-start.13 = (bf16[256,2304]{1,0:T(8,128)(2,1)S(1)}, bf16[256,2304]{1,0:T(8,128)(2,1)S(1)}, u32[]{:S(2)}, u32[]{:S(2)}) collective-permute-start(bf16[256,2304]{1,0:T(8,128)(2,1)S(1)} %shard_map.144), channel_id=1, source_target_pairs={{0,4},{4,0},{8,12},{12,8},{16,20},{20,16},{24,28},{28,24},{1,5},{5... | collective-permute-start | bytes 3538952 | tf_op jit(solution)/shard_map/ppermute | solution.py:19
  36.1 3.2 %collective-permute-start.12 = (bf16[256,128]{1,0:T(8,128)(2,1)S(1)}, bf16[256,128]{1,0:T(8,128)(2,1)S(1)}, u32[]{:S(2)}, u32[]{:S(2)}) collective-permute-start(bf16[256,128]{1,0:T(8,128)(2,1)S(1)} %constant_dynamic-update-slice_fusion.table), channel_id=1, source_target_pairs={{0,4},{4,0},{8,12},{12,8},{16,20},{20,16},{24,28},{28,24},{1,5},{5... | collective-permute-start | bytes 196616 | tf_op jit(solution)/shard_map/ppermute | solution.py:19
  39.3 10.4 %copy-start.1 = (bf16[2304,256]{1,0:T(8,128)(2,1)S(1)}, bf16[2304,256]{1,0:T(8,128)(2,1)}, u32[]{:S(2)}) copy-start(bf16[2304,256]{1,0:T(8,128)(2,1)} %gate.1) | copy-start | bytes 3538948
  39.3 10.4 %copy-start.2 = (bf16[2304,256]{1,0:T(8,128)(2,1)S(1)}, bf16[2304,256]{1,0:T(8,128)(2,1)}, u32[]{:S(2)}) copy-start(bf16[2304,256]{1,0:T(8,128)(2,1)} %up.1) | copy-start | bytes 3538948
  41.4 7.7 %collective-permute-start.17 = (bf16[32,2304]{1,0:T(8,128)(2,1)S(1)}, bf16[32,2304]{1,0:T(8,128)(2,1)S(1)}, u32[]{:S(2)}, u32[]{:S(2)}) collective-permute-start(bf16[32,2304]{1,0:T(8,128)(2,1)S(1)} %get-tuple-element.46), channel_id=1, source_target_pairs={{0,24},{4,28},{8,16},{12,20},{16,8},{20,12},{24,0},{28,4},{1,25},{... | collective-permute-start | bytes 442376 | tf_op jit(solution)/shard_map/ppermute | solution.py:19
  41.6 10.7 %collective-permute-start.19 = (bf16[32,2304]{1,0:T(8,128)(2,1)S(1)}, bf16[32,2304]{1,0:T(8,128)(2,1)S(1)}, u32[]{:S(2)}, u32[]{:S(2)}) collective-permute-start(bf16[32,2304]{1,0:T(8,128)(2,1)S(1)} %get-tuple-element.51), channel_id=1, source_target_pairs={{0,16},{4,20},{8,24},{12,28},{16,0},{20,4},{24,8},{28,12},{1,17},{... | collective-permute-start | bytes 442376 | tf_op jit(solution)/shard_map/ppermute | solution.py:19
  43.5 8.9 %collective-permute-start.18 = (bf16[32,2304]{1,0:T(8,128)(2,1)S(1)}, bf16[32,2304]{1,0:T(8,128)(2,1)S(1)}, u32[]{:S(2)}, u32[]{:S(2)}) collective-permute-start(bf16[32,2304]{1,0:T(8,128)(2,1)S(1)} %get-tuple-element.50), channel_id=1, source_target_pairs={{0,8},{4,12},{8,0},{12,4},{16,24},{20,28},{24,16},{28,20},{1,9},{5... | collective-permute-start | bytes 442376 | tf_op jit(solution)/shard_map/ppermute | solution.py:19
  45.0 10.5 %collective-permute-start.16 = (bf16[32,2304]{1,0:T(8,128)(2,1)S(1)}, bf16[32,2304]{1,0:T(8,128)(2,1)S(1)}, u32[]{:S(2)}, u32[]{:S(2)}) collective-permute-start(bf16[32,2304]{1,0:T(8,128)(2,1)S(1)} %get-tuple-element.45), channel_id=1, source_target_pairs={{0,24},{4,28},{8,16},{12,20},{16,8},{20,12},{24,0},{28,4},{1,25},{... | collective-permute-start | bytes 442376 | tf_op jit(solution)/shard_map/ppermute | solution.py:19
  45.1 11.8 %collective-permute-start.15 = (bf16[32,2304]{1,0:T(8,128)(2,1)S(1)}, bf16[32,2304]{1,0:T(8,128)(2,1)S(1)}, u32[]{:S(2)}, u32[]{:S(2)}) collective-permute-start(bf16[32,2304]{1,0:T(8,128)(2,1)S(1)} %get-tuple-element.44), channel_id=1, source_target_pairs={{0,16},{4,20},{8,24},{12,28},{16,0},{20,4},{24,8},{28,12},{1,17},{... | collective-permute-start | bytes 442376 | tf_op jit(solution)/shard_map/ppermute | solution.py:19
  49.1 7.8 %collective-permute-start.14 = (bf16[32,2304]{1,0:T(8,128)(2,1)S(1)}, bf16[32,2304]{1,0:T(8,128)(2,1)S(1)}, u32[]{:S(2)}, u32[]{:S(2)}) collective-permute-start(bf16[32,2304]{1,0:T(8,128)(2,1)S(1)} %get-tuple-element.43), channel_id=1, source_target_pairs={{0,8},{4,12},{8,0},{12,4},{16,24},{20,28},{24,16},{28,20},{1,9},{5... | collective-permute-start | bytes 442376 | tf_op jit(solution)/shard_map/ppermute | solution.py:19
  52.4 31.5 %copy-start.8 = (f32[512]{0:T(512)S(1)}, f32[512]{0:T(512)}, u32[]{:S(2)}) copy-start(f32[512]{0:T(512)} %param.23) | copy-start | bytes 6148
  52.4 5.2 %collective-permute-start.20 = (bf16[32,2304]{1,0:T(8,128)(2,1)S(1)}, bf16[32,2304]{1,0:T(8,128)(2,1)S(1)}, u32[]{:S(2)}, u32[]{:S(2)}) collective-permute-start(bf16[32,2304]{1,0:T(8,128)(2,1)S(1)} %add_convert_fusion.5), channel_id=1, source_target_pairs={{0,1},{1,0},{2,3},{3,2},{4,5},{5,4},{6,7},{7,6},{8,9},{9,8},{10,11... | collective-permute-start | bytes 442376 | tf_op jit(solution)/shard_map/ppermute | solution.py:19
  57.7 8.5 %collective-permute-start.21 = (bf16[2,16,2304]{2,1,0:T(8,128)(2,1)S(1)}, bf16[2,16,2304]{2,1,0:T(8,128)(2,1)S(1)}, u32[]{:S(2)}, u32[]{:S(2)}) collective-permute-start(bf16[2,16,2304]{2,1,0:T(8,128)(2,1)S(1)} %bitcast.107), channel_id=1, source_target_pairs={{0,2},{1,3},{2,0},{3,1},{4,6},{5,7},{6,4},{7,5},{8,10},{9,11},{10,... | collective-permute-start | bytes 442376 | tf_op jit(solution)/shard_map/ppermute | solution.py:19
  66.3 5.2 %collective-permute-start.22 = (bf16[32,2304]{1,0:T(8,128)(2,1)S(1)}, bf16[32,2304]{1,0:T(8,128)(2,1)S(1)}, u32[]{:S(2)}, u32[]{:S(2)}) collective-permute-start(bf16[32,2304]{1,0:T(8,128)(2,1)S(1)} %bitcast.102), channel_id=1, source_target_pairs={{0,1},{1,0},{2,3},{3,2},{4,5},{5,4},{6,7},{7,6},{8,9},{9,8},{10,11... | collective-permute-start | bytes 442376 | tf_op jit(solution)/shard_map/ppermute | solution.py:19
  67.1 9.3 %collective-permute-start.28 = (bf16[32,2304]{1,0:T(8,128)(2,1)S(1)}, bf16[32,2304]{1,0:T(8,128)(2,1)S(1)}, u32[]{:S(2)}, u32[]{:S(2)}) collective-permute-start(bf16[32,2304]{1,0:T(8,128)(2,1)S(1)} %bitcast.103), channel_id=1, source_target_pairs={{0,16},{4,20},{8,24},{12,28},{16,0},{20,4},{24,8},{28,12},{1,17},{... | collective-permute-start | bytes 442376 | tf_op jit(solution)/shard_map/ppermute | solution.py:19
  69.0 7.9 %collective-permute-start.27 = (bf16[32,2304]{1,0:T(8,128)(2,1)S(1)}, bf16[32,2304]{1,0:T(8,128)(2,1)S(1)}, u32[]{:S(2)}, u32[]{:S(2)}) collective-permute-start(bf16[32,2304]{1,0:T(8,128)(2,1)S(1)} %bitcast.104), channel_id=1, source_target_pairs={{0,8},{4,12},{8,0},{12,4},{16,24},{20,28},{24,16},{28,20},{1,9},{5... | collective-permute-start | bytes 442376 | tf_op jit(solution)/shard_map/ppermute | solution.py:19
  71.5 7.7 %collective-permute-start.29 = (bf16[32,2304]{1,0:T(8,128)(2,1)S(1)}, bf16[32,2304]{1,0:T(8,128)(2,1)S(1)}, u32[]{:S(2)}, u32[]{:S(2)}) collective-permute-start(bf16[32,2304]{1,0:T(8,128)(2,1)S(1)} %bitcast.105), channel_id=1, source_target_pairs={{0,24},{4,28},{8,16},{12,20},{16,8},{20,12},{24,0},{28,4},{1,25},{... | collective-permute-start | bytes 442376 | tf_op jit(solution)/shard_map/ppermute | solution.py:19
  73.4 10.5 %copy-start.7 = (bf16[2304,512]{1,0:T(8,128)(2,1)S(1)}, bf16[2304,512]{1,0:T(8,128)(2,1)}, u32[]{:S(2)}) copy-start(bf16[2304,512]{1,0:T(8,128)(2,1)} %param.22) | copy-start | bytes 7077892
  73.4 8.6 %collective-permute-start.25 = (bf16[32,2304]{1,0:T(8,128)(2,1)S(1)}, bf16[32,2304]{1,0:T(8,128)(2,1)S(1)}, u32[]{:S(2)}, u32[]{:S(2)}) collective-permute-start(bf16[32,2304]{1,0:T(8,128)(2,1)S(1)} %collective-permute-done.22), channel_id=1, source_target_pairs={{0,24},{4,28},{8,16},{12,20},{16,8},{20,12},{24,0},{28,4},{1,25},{... | collective-permute-start | bytes 442376 | tf_op jit(solution)/shard_map/ppermute | solution.py:19
  74.4 8.7 %collective-permute-start.24 = (bf16[32,2304]{1,0:T(8,128)(2,1)S(1)}, bf16[32,2304]{1,0:T(8,128)(2,1)S(1)}, u32[]{:S(2)}, u32[]{:S(2)}) collective-permute-start(bf16[32,2304]{1,0:T(8,128)(2,1)S(1)} %collective-permute-done.22), channel_id=1, source_target_pairs={{0,16},{4,20},{8,24},{12,28},{16,0},{20,4},{24,8},{28,12},{1,17},{... | collective-permute-start | bytes 442376 | tf_op jit(solution)/shard_map/ppermute | solution.py:19
  76.4 7.3 %collective-permute-start.23 = (bf16[32,2304]{1,0:T(8,128)(2,1)S(1)}, bf16[32,2304]{1,0:T(8,128)(2,1)S(1)}, u32[]{:S(2)}, u32[]{:S(2)}) collective-permute-start(bf16[32,2304]{1,0:T(8,128)(2,1)S(1)} %collective-permute-done.22), channel_id=1, source_target_pairs={{0,8},{4,12},{8,0},{12,4},{16,24},{20,28},{24,16},{28,20},{1,9},{5... | collective-permute-start | bytes 442376 | tf_op jit(solution)/shard_map/ppermute | solution.py:19
  79.3 7.4 %collective-permute-start.30 = (bf16[128,2304]{1,0:T(8,128)(2,1)S(1)}, bf16[128,2304]{1,0:T(8,128)(2,1)S(1)}, u32[]{:S(2)}, u32[]{:S(2)}) collective-permute-start(bf16[128,2304]{1,0:T(8,128)(2,1)S(1)} %bitcast.62), channel_id=1, source_target_pairs={{0,4},{4,0},{8,12},{12,8},{16,20},{20,16},{24,28},{28,24},{1,5},{5... | collective-permute-start | bytes 1769480 | tf_op jit(solution)/shard_map/ppermute | solution.py:19
  83.8 7.6 %collective-permute-start.26 = (bf16[128,2304]{1,0:T(8,128)(2,1)S(1)}, bf16[128,2304]{1,0:T(8,128)(2,1)S(1)}, u32[]{:S(2)}, u32[]{:S(2)}) collective-permute-start(bf16[128,2304]{1,0:T(8,128)(2,1)S(1)} %bitcast.60), channel_id=1, source_target_pairs={{0,4},{4,0},{8,12},{12,8},{16,20},{20,16},{24,28},{28,24},{1,5},{5... | collective-permute-start | bytes 1769480 | tf_op jit(solution)/shard_map/ppermute | solution.py:19
  85.1 2.2 %collective-permute-start.35 = (bf16[128,2304]{1,0:T(8,128)(2,1)S(1)}, bf16[128,2304]{1,0:T(8,128)(2,1)S(1)}, u32[]{:S(2)}, u32[]{:S(2)}) collective-permute-start(bf16[128,2304]{1,0:T(8,128)(2,1)S(1)} %convolution_convert_fusion), channel_id=1, source_target_pairs={{0,4},{4,0},{8,12},{12,8},{16,20},{20,16},{24,28},{28,24},{1,5},{5... | collective-permute-start | bytes 1769480 | tf_op jit(solution)/shard_map/ppermute | solution.py:19
  86.6 5.2 %collective-permute-start.31 = (bf16[128,2304]{1,0:T(8,128)(2,1)S(1)}, bf16[128,2304]{1,0:T(8,128)(2,1)S(1)}, u32[]{:S(2)}, u32[]{:S(2)}) collective-permute-start(bf16[128,2304]{1,0:T(8,128)(2,1)S(1)} %convolution_convert_fusion.1), channel_id=1, source_target_pairs={{0,4},{4,0},{8,12},{12,8},{16,20},{20,16},{24,28},{28,24},{1,5},{5... | collective-permute-start | bytes 1769480 | tf_op jit(solution)/shard_map/ppermute | solution.py:19
  87.8 8.2 %collective-permute-start.38 = (bf16[32,2304]{1,0:T(8,128)(2,1)S(1)}, bf16[32,2304]{1,0:T(8,128)(2,1)S(1)}, u32[]{:S(2)}, u32[]{:S(2)}) collective-permute-start(bf16[32,2304]{1,0:T(8,128)(2,1)S(1)} %get-tuple-element.60), channel_id=1, source_target_pairs={{0,24},{4,28},{8,16},{12,20},{16,8},{20,12},{24,0},{28,4},{1,25},{... | collective-permute-start | bytes 442376 | tf_op jit(solution)/shard_map/ppermute | solution.py:19
  89.3 9.3 %collective-permute-start.37 = (bf16[32,2304]{1,0:T(8,128)(2,1)S(1)}, bf16[32,2304]{1,0:T(8,128)(2,1)S(1)}, u32[]{:S(2)}, u32[]{:S(2)}) collective-permute-start(bf16[32,2304]{1,0:T(8,128)(2,1)S(1)} %get-tuple-element.61), channel_id=1, source_target_pairs={{0,16},{4,20},{8,24},{12,28},{16,0},{20,4},{24,8},{28,12},{1,17},{... | collective-permute-start | bytes 442376 | tf_op jit(solution)/shard_map/ppermute | solution.py:19
  90.8 7.9 %collective-permute-start.36 = (bf16[32,2304]{1,0:T(8,128)(2,1)S(1)}, bf16[32,2304]{1,0:T(8,128)(2,1)S(1)}, u32[]{:S(2)}, u32[]{:S(2)}) collective-permute-start(bf16[32,2304]{1,0:T(8,128)(2,1)S(1)} %get-tuple-element.59), channel_id=1, source_target_pairs={{0,8},{4,12},{8,0},{12,4},{16,24},{20,28},{24,16},{28,20},{1,9},{5... | collective-permute-start | bytes 442376 | tf_op jit(solution)/shard_map/ppermute | solution.py:19
  92.3 20.0 %copy-start.9 = (f32[2304]{0:T(1024)S(1)}, f32[2304]{0:T(1024)}, u32[]{:S(2)}) copy-start(f32[2304]{0:T(1024)} %param.25) | copy-start | bytes 27652
  92.4 9.4 %collective-permute-start.34 = (bf16[32,2304]{1,0:T(8,128)(2,1)S(1)}, bf16[32,2304]{1,0:T(8,128)(2,1)S(1)}, u32[]{:S(2)}, u32[]{:S(2)}) collective-permute-start(bf16[32,2304]{1,0:T(8,128)(2,1)S(1)} %get-tuple-element.57), channel_id=1, source_target_pairs={{0,24},{4,28},{8,16},{12,20},{16,8},{20,12},{24,0},{28,4},{1,25},{... | collective-permute-start | bytes 442376 | tf_op jit(solution)/shard_map/ppermute | solution.py:19
  94.0 10.5 %collective-permute-start.33 = (bf16[32,2304]{1,0:T(8,128)(2,1)S(1)}, bf16[32,2304]{1,0:T(8,128)(2,1)S(1)}, u32[]{:S(2)}, u32[]{:S(2)}) collective-permute-start(bf16[32,2304]{1,0:T(8,128)(2,1)S(1)} %get-tuple-element.58), channel_id=1, source_target_pairs={{0,16},{4,20},{8,24},{12,28},{16,0},{20,4},{24,8},{28,12},{1,17},{... | collective-permute-start | bytes 442376 | tf_op jit(solution)/shard_map/ppermute | solution.py:19
  96.0 8.5 %collective-permute-start.32 = (bf16[32,2304]{1,0:T(8,128)(2,1)S(1)}, bf16[32,2304]{1,0:T(8,128)(2,1)S(1)}, u32[]{:S(2)}, u32[]{:S(2)}) collective-permute-start(bf16[32,2304]{1,0:T(8,128)(2,1)S(1)} %get-tuple-element.56), channel_id=1, source_target_pairs={{0,8},{4,12},{8,0},{12,4},{16,24},{20,28},{24,16},{28,20},{1,9},{5... | collective-permute-start | bytes 442376 | tf_op jit(solution)/shard_map/ppermute | solution.py:19
  98.7 5.7 %collective-permute-start.39 = (bf16[32,2304]{1,0:T(8,128)(2,1)S(1)}, bf16[32,2304]{1,0:T(8,128)(2,1)S(1)}, u32[]{:S(2)}, u32[]{:S(2)}) collective-permute-start(bf16[32,2304]{1,0:T(8,128)(2,1)S(1)} %add_convert_fusion.2), channel_id=1, source_target_pairs={{0,1},{1,0},{2,3},{3,2},{4,5},{5,4},{6,7},{7,6},{8,9},{9,8},{10,11... | collective-permute-start | bytes 442376 | tf_op jit(solution)/shard_map/ppermute | solution.py:19
  104.6 7.8 %collective-permute-start.40 = (bf16[16,2304]{1,0:T(8,128)(2,1)S(1)}, bf16[16,2304]{1,0:T(8,128)(2,1)S(1)}, u32[]{:S(2)}, u32[]{:S(2)}) collective-permute-start(bf16[16,2304]{1,0:T(8,128)(2,1)S(1)} %fusion.9), channel_id=1, source_target_pairs={{0,2},{1,3},{2,0},{3,1},{4,6},{5,7},{6,4},{7,5},{8,10},{9,11},{10,... | collective-permute-start | bytes 221192 | tf_op jit(solution)/shard_map/ppermute | solution.py:19
  (6 other events, 25.0 us)

commit v10 on v8

--- a/solution.py
+++ b/solution.py
@@ -64,7 +64,7 @@
     return copies
 
 
-def pack_kernel(feats, feat, ids, weights, out):
+def pack_kernel(ids, weights, out):
     top, own = ids.shape
     lane = lax.broadcasted_iota(jnp.int32, (top, LANES), 1)
     row = lax.broadcasted_iota(jnp.int32, (top, LANES), 0)
@@ -76,38 +76,36 @@
         values += lax.dot_general(
             part, places, (((0,), (0,)), ((), ())), preferred_element_type=jnp.float32
         )
-    for f in range(feats):
-        out[f * own : (f + 1) * own, :] = half(jnp.where(feat[0] == f, values, 0.0))
-
-
-def run_pack(feat, expert_ids, gate_weights, feats):
+    out[...] = half(values)
+
+
+def run_pack(expert_ids, gate_weights):
     own, top = expert_ids.shape
     return call(
-        functools.partial(pack_kernel, feats),
-        [feat.reshape(1), expert_ids.T, gate_weights.T],
-        [SMEM_SPEC, VMEM_SPEC, VMEM_SPEC],
-        [((feats * own, LANES), jnp.bfloat16)],
+        pack_kernel,
+        [expert_ids.T, gate_weights.T],
+        [VMEM_SPEC] * 2,
+        [((own, LANES), jnp.bfloat16)],
         [],
         2,
-        (6 * own * top * LANES, 2 * feats * own * LANES),
+        (6 * own * top * LANES, 2 * own * LANES),
     )[0]
 
 
-def load_kernel(table, *refs):
-    count = (len(refs) - 2) // 2
-    copies = start_all(list(zip(refs[:count], refs[count + 1 : -1])), refs[-1])
-    refs[count][...] = table[...]
+def load_kernel(*refs):
+    count = (len(refs) - 1) // 2
+    copies = start_all(list(zip(refs[:count], refs[count:-1])), refs[-1])
     for copy in copies:
         copy.wait()
 
 
-def run_load(table, values):
+def run_load(values):
     count = len(values)
     return call(
         load_kernel,
-        [table, *values],
-        [VMEM_SPEC] + [HBM_SPEC] * count,
-        [(value.shape, value.dtype) for value in [table] + values],
+        values,
+        [HBM_SPEC] * count,
+        [(value.shape, value.dtype) for value in values],
         [pltpu.SemaphoreType.DMA((count,))],
         LOAD_MIB,
         (550 * sum(value.size for value in values), 4 * sum(value.size for value in values)),
@@ -163,10 +161,15 @@
     )[0]
 
 
-def down_kernel(top, e, tile, kind, scalars, hidden, down, table, *refs):
+def down_kernel(top, e, tile, pairs, flip, kind, scalars, hidden, down, table, *refs):
     count = 1 if kind is None else 2 * kind[0]
     more, outs = refs[:-count], refs[-count:]
-    entries = full(table[...])
+    size = hidden.shape[0] // pairs
+    entries = []
+    for p in range(pairs):
+        owner = 2 * jnp.bitwise_xor(scalars[2], p) + jnp.bitwise_xor(scalars[3], flip)
+        entries.append(full(table[pl.ds(pl.multiple_of(owner * size, size), size), :]))
+    entries = jnp.concatenate(entries, axis=0)
     lane = lax.broadcasted_iota(jnp.int32, entries.shape, 1)
     expert = (scalars[0] * down.shape[0] + e).astype(jnp.float32)
     chosen = jnp.where((entries == expert) & (lane < top), 1.0, 0.0)
@@ -180,8 +183,7 @@
         if kind is None:
             outs[0][:, cut] = half(value)
             continue
-        pairs, own = kind
-        size = value.shape[0] // pairs
+        own = kind[1]
         for p in range(pairs):
             block = value[p * size : (p + 1) * size]
             block = block.reshape(size // own // 2, 2, own, tile)
@@ -190,7 +192,7 @@
             outs[pairs + p][:, cut] = half(jnp.where(scalars[1] == 0, high, low))
 
 
-def run_down(hidden, down, e, scalars, table, top, more=(), kind=None):
+def run_down(hidden, down, e, scalars, table, top, pairs, flip, more=(), kind=None):
     rows, units = hidden.shape
     width = down.shape[2]
     tile = 256 if width % 256 == 0 else 128
@@ -198,7 +200,7 @@
     if kind is not None:
         outs = [((rows // kind[0] // 2, width), jnp.bfloat16)] * (2 * kind[0])
     return call(
-        functools.partial(down_kernel, top, e, tile, kind),
+        functools.partial(down_kernel, top, e, tile, pairs, flip, kind),
         [scalars, hidden, down, table, *more],
         [SMEM_SPEC] + [VMEM_SPEC] * (3 + len(more)),
         outs,
@@ -233,47 +235,42 @@
     my_feat = lax.axis_index("feat")
     feat_bits = bits_of(feats)
     place = [(my_feat // bit) % 2 for bit in feat_bits]
-    scalars = jnp.stack([me, place[0]])
+    my_expert = lax.axis_index("expert")
+    scalars = jnp.stack([me, place[0], my_expert // 2, my_expert % 2])
     chunk_rows = pairs * feats // 2 * own
 
-    table = run_pack(my_feat, expert_ids, gate_weights, feats)
-    for bit in feat_bits:
-        table = table + swap(table, "feat", bit)
-
-    near = [tokens] + [swap(tokens, "expert", 2 * p) for p in range(1, pairs)]
-    far = [swap(piece, "expert", 1) for piece in near]
-    arrived = swap(table, "expert", 2)
-    table, near[0], expert_gate, expert_up = run_load(
-        table, [tokens, expert_gate, expert_up]
-    )
-    shared_out = run_shared(scalars, far[0], [shared_gate, shared_up, shared_down], own)
-    table = jnp.concatenate([table, arrived], axis=0)
-    for bit in bits_of(pairs)[1:]:
-        table = jnp.concatenate([table, swap(table, "expert", 2 * bit)], axis=0)
-    table_far = swap(table, "expert", 1)
-
-    table, *far = lax.optimization_barrier((table, *far))
+    table = run_pack(expert_ids, gate_weights)
+    table = lax.all_gather(table, ("expert", "feat"), axis=0, tiled=True)
+
+    near = [swap(tokens, "expert", 2 * p) for p in range(1, pairs)]
+    far = [swap(piece, "expert", 1) for piece in [tokens] + near]
+    mine, expert_gate, expert_up = run_load([tokens, expert_gate, expert_up])
+    near = [mine] + near
+
+    hidden = [run_hidden(near, expert_gate, expert_up, e) for e in local_experts]
+    hidden[0], *far = lax.optimization_barrier((hidden[0], *far))
     arrived = None
     for e in local_experts:
-        hidden = run_hidden(near, expert_gate, expert_up, e)
         more = [] if arrived is None else [arrived]
-        arrived = run_down(hidden, expert_down, e, scalars, table, top, more)[0]
+        arrived = run_down(hidden[e], expert_down, e, scalars, table, top, pairs, 0, more)[0]
     arrived = swap(arrived, "expert", 1)
     for e in local_experts:
         hidden = run_hidden(far, expert_gate, expert_up, e)
         if e < local_experts[-1]:
             more = [arrived]
-            arrived = run_down(hidden, expert_down, e, scalars, table_far, top, more)[0]
+            arrived = run_down(hidden, expert_down, e, scalars, table, top, pairs, 1, more)[0]
     blocks = run_down(
-        hidden, expert_down, e, scalars, table_far, top, [arrived], (pairs, own)
-    )
-
-    def reduce_pairs(parts, *more):
-        arrived = [swap(parts[p], "expert", 2 * p) for p in range(1, pairs)]
-        return sum(full(part) for part in [parts[0], *more] + arrived)
-
-    arrived = swap(half(reduce_pairs(blocks[:pairs], shared_out[0])), "feat", feat_bits[0])
-    total = reduce_pairs(blocks[pairs:], shared_out[1]) + full(arrived)
+        hidden, expert_down, e, scalars, table, top, pairs, 1, [arrived], (pairs, own)
+    )
+    blocks = [blocks[:pairs], blocks[pairs:]]
+    blocks = [
+        [mine[0]] + [swap(mine[p], "expert", 2 * p) for p in range(1, pairs)] for mine in blocks
+    ]
+    scalars, blocks[0][-1] = lax.optimization_barrier((scalars, blocks[0][-1]))
+    shared_out = run_shared(scalars, far[0], [shared_gate, shared_up, shared_down], own)
+    totals = [sum(full(part) for part in blocks[i] + [shared_out[i]]) for i in range(2)]
+
+    total = totals[1] + full(swap(half(totals[0]), "feat", feat_bits[0]))
     total = total.reshape((2,) * (len(feat_bits) - 1) + (own, width))
     for i, bit in enumerate(feat_bits[1:-1]):
         dim = len(feat_bits) - 2 - i
@@ -289,21 +286,20 @@
     mine, other = lax.optimization_barrier((moe_out, other))
     parts.append(swap(mine, "expert", 2 * (pairs - 1)))
     sides = [[other] + [swap(other, "expert", 2 * p) for p in range(1, pairs)], parts]
-    near = [jnp.stack(parts).reshape(chunk_rows, width) for parts in sides]
 
     def encode(x):
         return half(jax.nn.relu(dot(x, encoder) + encoder_bias[None, :]))
 
     features, blocks = [None, None], [None, None]
     for chunk in (1, 0):
-        far = swap(near[chunk], "expert", 1)
-        features_near = encode(near[chunk])
+        near = jnp.stack(sides[chunk]).reshape(chunk_rows, width)
+        far = swap(near, "expert", 1)
+        features_near = encode(near)
         decoded = swap(half(dot(features_near, decoder)), "expert", 1)
         features_far = encode(far)
-        total = dot(features_far, decoder) + full(decoded)
+        total = half(dot(features_far, decoder) + full(decoded))
         total = total.reshape(pairs, feats // 2 * own, width)
-        blocks[chunk] = [total[0]]
-        blocks[chunk] += [swap(half(total[p]), "expert", 2 * p) for p in range(1, pairs)]
+        blocks[chunk] = [total[0]] + [swap(total[p], "expert", 2 * p) for p in range(1, pairs)]
         both = jnp.stack([features_far, features_near])
         features[chunk] = both.reshape(2, pairs, feats // 2, 1, own, -1)
     arrived = swap(half(sum(full(block) for block in blocks[1])), "feat", feat_bits[0])

time: 108 us -> 168 us (1.56)
  blocking collectives: 0 us -> 68.4 us
  starting transfers between devices: 40.6 us -> 26.1 us
  waiting for transfers between devices: 42.6 us -> 50.3 us
    all_gather x0 -> x1, blocking collectives: none -> 68.4 us  [shards(): table = lax.all_gather(table, ('expert', 'feat'), axis=0, tiled=True)]
    ppermute x40 -> x35, starting transfers between devices: 40.6 us -> 26.1 us  [swap(): lax.ppermute(value, axis, [(i, i ^ r) for i in range(lax.axis_size(axis))])]
    ppermute x40 -> x35, waiting for transfers between devices: 42.6 us -> 50.3 us  [swap(): lax.ppermute(value, axis, [(i, i ^ r) for i in range(lax.axis_size(axis))])]
  transfers between devices with their start and end apart: 40 -> 35, of which waited for: 20 -> 19; matrix products, arithmetic and copies ran while one was open for 5% -> 3% of each run, Pallas kernels for 10% -> 6%
where the time goes in v10:
time: 168 us
  blocking collectives  68.4 us (41%)
  waiting for transfers between devices  50.3 us (30%)
  starting transfers between devices  26.1 us (16%)
  Pallas kernels  14.8 us (9%)
  matrix products  3.85 us (2%)
    all_gather x1, blocking collectives, shards(): table = lax.all_gather(table, ('expert', 'feat'), axis=0, tiled=True)  68.4 us
    ppermute x35, waiting for transfers between devices, swap(): lax.ppermute(value, axis, [(i, i ^ r) for i in range(lax.axis_size(axis))])  50.3 us
    ppermute x35, starting transfers between devices, swap(): lax.ppermute(value, axis, [(i, i ^ r) for i in range(lax.axis_size(axis))])  26.1 us
    pallas_call x7, Pallas kernels, call(): pl.pallas_call(body, in_specs=specs, out_specs=[VMEM_SPEC] * len(outs), o...  14.8 us
    dot_general x8, matrix products, dot(): return jnp.dot(a, b, preferred_element_type=jnp.float32)  3.85 us
  transfers between devices with their start and end apart: 35, of which 19 were waited for; matrix products, arithmetic and copies ran while one was open for 3% of the time, Pallas kernels for 6%

profile of v10, /device:TPU:0, one launch (start us, length us, event | category | flops | bytes accessed | tf_op | source)
XLA Modules:
  0.0 167.6 jit_solution(6011851897866807457)
XLA Ops:
  0.6 3.0 %collective-permute-start = (bf16[64,2304]{1,0:T(8,128)(2,1)}, bf16[64,2304]{1,0:T(8,128)(2,1)S(1)}, u32[]{:S(2)}, u32[]{:S(2)}) collective-permute-start(bf16[64,2304]{1,0:T(8,128)(2,1)} %refs_0_.1), channel_id=1, source_target_pairs={{0,8},{4,12},{8,0},{12,4},{16,24},{20,28},{24,16},{28,20},{1,9},{5... | collective-permute-start | bytes 884744 | tf_op jit(solution)/shard_map/ppermute | solution.py:19
  3.7 1.5 collective-permute-start.1
  5.2 1.0 copy-done.6
  6.2 3.9 %shard_map.140 = (bf16[64,2304]{1,0:T(8,128)(2,1)S(1)}, bf16[1,2304,1024]{2,1,0:T(8,128)(2,1)S(1)}, bf16[1,2304,1024]{2,1,0:T(8,128)(2,1)S(1)}) custom-call(bf16[64,2304]{1,0:T(8,128)(2,1)S(1)} %copy-done.6, bf16[1,2304,1024]{2,1,0:T(8,128)(2,1)} %refs_1_.1, bf16[1,2304,1024]{2,1,0:T(8,128)(2,1)} %refs_2_.1), custom_call_target="tpu_custom_call" | custom-call | flops 2676326400 | bytes 19464192 | tf_op jit(solution)/shard_map/pallas_call | solution.py:49
  10.1 1.6 collective-permute-done.refs_1_
  11.7 6.9 %collective-permute-done.1.refs_2_ = bf16[64,2304]{1,0:T(8,128)(2,1)S(1)} collective-permute-done((bf16[64,2304]{1,0:T(8,128)(2,1)}, bf16[64,2304]{1,0:T(8,128)(2,1)S(1)}, u32[]{:S(2)}, u32[]{:S(2)}) %collective-permute-start.1) | collective-permute-done | bytes 294944 | tf_op jit(solution)/shard_map/ppermute | solution.py:19
  18.7 0.5 collective-permute-start.6
  19.4 68.4 %all_gather.3.table = bf16[512,128]{1,0:T(8,128)(2,1)S(1)} all-gather(bf16[16,128]{1,0:T(8,128)(2,1)S(1)} %shard_map.143), channel_id=1, replica_groups=mesh['expert'=8,'feat'=4] {'expert','feat'}, dimensions={0}, use_global_device_ids=true | all-gather | bytes 135168 | tf_op jit(solution)/shard_map/all_gather | solution.py:243
  87.9 2.7 %shard_map.141.hidden = bf16[256,1024]{1,0:T(8,128)(2,1)S(1)} custom-call(bf16[64,2304]{1,0:T(8,128)(2,1)S(1)} %get-tuple-element.24.refs_0_, bf16[64,2304]{1,0:T(8,128)(2,1)S(1)} %collective-permute-done.refs_1_, bf16[64,2304]{1,0:T(8,128)(2,1)S(1)} %collective-permute-done.1.refs_2_, bf16[64,2304]{1,0:T(8,128)(2,1)S(1)} %collective-permute-done.2.refs_3_, ...), custom_call_target="tpu_custom_call" | custom-call | flops 2415919104 | bytes 9437184 | tf_op jit(solution)/shard_map/pallas_call | solution.py:49
  90.6 1.9 %shard_map.144 = bf16[256,2304]{1,0:T(8,128)(2,1)S(1)} custom-call(s32[4]{0:T(128)S(1)} %pad_add_fusion.scalars, bf16[256,1024]{1,0:T(8,128)(2,1)S(1)} %shard_map.141.hidden, bf16[1,1024,2304]{2,1,0:T(8,128)(2,1)S(1)} %bitcast.58, bf16[512,128]{1,0:T(8,128)(2,1)S(1)} %all_gather.3.table), custom_call_target="tpu_custom_call" | custom-call | flops 1207959552 | bytes 4718592 | tf_op jit(solution)/shard_map/pallas_call | solution.py:49
  92.6 2.7 %shard_map.142.hidden = bf16[256,1024]{1,0:T(8,128)(2,1)S(1)} custom-call(bf16[64,2304]{1,0:T(8,128)(2,1)S(1)} %collective-permute-done.3.refs_0_.x, bf16[64,2304]{1,0:T(8,128)(2,1)S(1)} %collective-permute-done.4.refs_1_, bf16[64,2304]{1,0:T(8,128)(2,1)S(1)} %collective-permute-done.5.refs_2_, bf16[64,2304]{1,0:T(8,128)(2,1)S(1)} %collective-permute-done.6.refs_3_, ...), custom_call_target="tpu_custom_call" | custom-call | flops 2415919104 | bytes 9437184 | tf_op jit(solution)/shard_map/pallas_call | solution.py:49
  95.5 2.0 %shard_map.145 = (bf16[32,2304]{1,0:T(8,128)(2,1)S(1)}, bf16[32,2304]{1,0:T(8,128)(2,1)S(1)}, bf16[32,2304]{1,0:T(8,128)(2,1)S(1)}, bf16[32,2304]{1,0:T(8,128)(2...) custom-call(s32[4]{0:T(128)S(1)} %pad_add_fusion.scalars, ...), custom_call_target="tpu_custom_call" | custom-call | flops 1207959552 | bytes 4718592 | tf_op jit(solution)/shard_map/pallas_call | solution.py:49
  97.6 1.3 collective-permute-start.13
  98.8 2.2 %collective-permute-start.12 = (bf16[32,2304]{1,0:T(8,128)(2,1)S(1)}, bf16[32,2304]{1,0:T(8,128)(2,1)S(1)}, u32[]{:S(2)}, u32[]{:S(2)}) collective-permute-start(bf16[32,2304]{1,0:T(8,128)(2,1)S(1)} %get-tuple-element.40), channel_id=1, source_target_pairs={{0,8},{4,12},{8,0},{12,4},{16,24},{20,28},{24,16},{28,20},{1,9},{5... | collective-permute-start | bytes 442376 | tf_op jit(solution)/shard_map/ppermute | solution.py:19
  101.0 0.6 collective-permute-start.10
  101.7 0.8 collective-permute-start.9
  102.5 2.6 %collective-permute-done.11 = bf16[32,2304]{1,0:T(8,128)(2,1)S(1)} collective-permute-done((bf16[32,2304]{1,0:T(8,128)(2,1)S(1)}, bf16[32,2304]{1,0:T(8,128)(2,1)S(1)}, u32[]{:S(2)}, u32[]{:S(2)}) %collective-permute-start.11) | collective-permute-done | bytes 147488 | tf_op jit(solution)/shard_map/ppermute | solution.py:19
  105.2 1.4 shard_map.146
  106.6 0.9 collective-permute-done.13
  107.5 0.6 collective-permute-done.12
  108.2 3.3 %collective-permute-done.10 = bf16[32,2304]{1,0:T(8,128)(2,1)S(1)} collective-permute-done((bf16[32,2304]{1,0:T(8,128)(2,1)S(1)}, bf16[32,2304]{1,0:T(8,128)(2,1)S(1)}, u32[]{:S(2)}, u32[]{:S(2)}) %collective-permute-start.10) | collective-permute-done | bytes 147488 | tf_op jit(solution)/shard_map/ppermute | solution.py:19
  111.5 1.8 %collective-permute-done.9 = bf16[32,2304]{1,0:T(8,128)(2,1)S(1)} collective-permute-done((bf16[32,2304]{1,0:T(8,128)(2,1)S(1)}, bf16[32,2304]{1,0:T(8,128)(2,1)S(1)}, u32[]{:S(2)}, u32[]{:S(2)}) %collective-permute-start.9) | collective-permute-done | bytes 147488 | tf_op jit(solution)/shard_map/ppermute | solution.py:19
  113.3 0.7 collective-permute-done.8
  114.2 7.9 %collective-permute-done.15 = bf16[2,16,2304]{2,1,0:T(8,128)(2,1)S(1)} collective-permute-done((bf16[2,16,2304]{2,1,0:T(8,128)(2,1)S(1)}, bf16[2,16,2304]{2,1,0:T(8,128)(2,1)S(1)}, u32[]{:S(2)}, u32[]{:S(2)}) %collective-permute-start.15) | collective-permute-done | bytes 147488 | tf_op jit(solution)/shard_map/ppermute | solution.py:19
  122.1 0.9 collective-permute-start.22
  123.0 0.9 collective-permute-start.21
  123.9 3.7 %collective-permute-done.16 = bf16[32,2304]{1,0:T(8,128)(2,1)S(1)} collective-permute-done((bf16[32,2304]{1,0:T(8,128)(2,1)S(1)}, bf16[32,2304]{1,0:T(8,128)(2,1)S(1)}, u32[]{:S(2)}, u32[]{:S(2)}) %collective-permute-start.16) | collective-permute-done | bytes 147488 | tf_op jit(solution)/shard_map/ppermute | solution.py:19
  127.6 0.8 collective-permute-start.23
  128.5 2.1 %collective-permute-start.19 = (bf16[32,2304]{1,0:T(8,128)(2,1)S(1)}, bf16[32,2304]{1,0:T(8,128)(2,1)S(1)}, u32[]{:S(2)}, u32[]{:S(2)}) collective-permute-start(bf16[32,2304]{1,0:T(8,128)(2,1)S(1)} %collective-permute-done.16), channel_id=1, source_target_pairs={{0,24},{4,28},{8,16},{12,20},{16,8},{20,12},{24,0},{28,4},{1,25},{... | collective-permute-start | bytes 442376 | tf_op jit(solution)/shard_map/ppermute | solution.py:19
  130.6 0.8 collective-permute-start.18
  131.4 0.7 collective-permute-start.17
  132.2 3.2 %collective-permute-done.23 = bf16[32,2304]{1,0:T(8,128)(2,1)S(1)} collective-permute-done((bf16[32,2304]{1,0:T(8,128)(2,1)S(1)}, bf16[32,2304]{1,0:T(8,128)(2,1)S(1)}, u32[]{:S(2)}, u32[]{:S(2)}) %collective-permute-start.23) | collective-permute-done | bytes 147488 | tf_op jit(solution)/shard_map/ppermute | solution.py:19
  135.5 2.5 %collective-permute-done.19 = bf16[32,2304]{1,0:T(8,128)(2,1)S(1)} collective-permute-done((bf16[32,2304]{1,0:T(8,128)(2,1)S(1)}, bf16[32,2304]{1,0:T(8,128)(2,1)S(1)}, u32[]{:S(2)}, u32[]{:S(2)}) %collective-permute-start.19) | collective-permute-done | bytes 147488 | tf_op jit(solution)/shard_map/ppermute | solution.py:19
  138.0 1.5 collective-permute-done.18
  140.2 0.5 convolution_convert_fusion
  140.7 0.6 collective-permute-start.29
  143.4 1.9 %collective-permute-start.32 = (bf16[32,2304]{1,0:T(8,128)(2,1)S(1)}, bf16[32,2304]{1,0:T(8,128)(2,1)S(1)}, u32[]{:S(2)}, u32[]{:S(2)}) collective-permute-start(bf16[32,2304]{1,0:T(8,128)(2,1)S(1)} %get-tuple-element.50), channel_id=1, source_target_pairs={{0,24},{4,28},{8,16},{12,20},{16,8},{20,12},{24,0},{28,4},{1,25},{... | collective-permute-start | bytes 442376 | tf_op jit(solution)/shard_map/ppermute | solution.py:19
  145.3 1.4 collective-permute-start.31
  147.4 0.5 add_convert_fusion.1
  148.0 1.9 %collective-permute-start.28 = (bf16[32,2304]{1,0:T(8,128)(2,1)S(1)}, bf16[32,2304]{1,0:T(8,128)(2,1)S(1)}, u32[]{:S(2)}, u32[]{:S(2)}) collective-permute-start(bf16[32,2304]{1,0:T(8,128)(2,1)S(1)} %get-tuple-element.47), channel_id=1, source_target_pairs={{0,24},{4,28},{8,16},{12,20},{16,8},{20,12},{24,0},{28,4},{1,25},{... | collective-permute-start | bytes 442376 | tf_op jit(solution)/shard_map/ppermute | solution.py:19
  149.9 1.4 collective-permute-start.27
  151.9 0.9 collective-permute-start.26
  152.9 1.4 collective-permute-done.31
  154.3 0.8 collective-permute-start.33
  155.1 2.3 %collective-permute-done.28 = bf16[32,2304]{1,0:T(8,128)(2,1)S(1)} collective-permute-done((bf16[32,2304]{1,0:T(8,128)(2,1)S(1)}, bf16[32,2304]{1,0:T(8,128)(2,1)S(1)}, u32[]{:S(2)}, u32[]{:S(2)}) %collective-permute-start.28) | collective-permute-done | bytes 147488 | tf_op jit(solution)/shard_map/ppermute | solution.py:19
  157.4 2.6 %collective-permute-done.27 = bf16[32,2304]{1,0:T(8,128)(2,1)S(1)} collective-permute-done((bf16[32,2304]{1,0:T(8,128)(2,1)S(1)}, bf16[32,2304]{1,0:T(8,128)(2,1)S(1)}, u32[]{:S(2)}, u32[]{:S(2)}) %collective-permute-start.27) | collective-permute-done | bytes 147488 | tf_op jit(solution)/shard_map/ppermute | solution.py:19
  160.3 6.6 %collective-permute-done.34 = bf16[16,2304]{1,0:T(8,128)(2,1)S(1)} collective-permute-done((bf16[16,2304]{1,0:T(8,128)(2,1)S(1)}, bf16[16,2304]{1,0:T(8,128)(2,1)S(1)}, u32[]{:S(2)}, u32[]{:S(2)}) %collective-permute-start.34) | collective-permute-done | bytes 73760 | tf_op jit(solution)/shard_map/ppermute | solution.py:19
  166.9 0.7 fusion.8
  (110 shorter events, 5.3 us)
Async XLA Ops:
  0.6 139.5 %copy-start = (bf16[512,2304]{1,0:T(8,128)(2,1)S(1)}, bf16[512,2304]{1,0:T(8,128)(2,1)}, u32[]{:S(2)}) copy-start(bf16[512,2304]{1,0:T(8,128)(2,1)} %param.24) | copy-start | bytes 7077892
  0.6 11.1 %collective-permute-start = (bf16[64,2304]{1,0:T(8,128)(2,1)}, bf16[64,2304]{1,0:T(8,128)(2,1)S(1)}, u32[]{:S(2)}, u32[]{:S(2)}) collective-permute-start(bf16[64,2304]{1,0:T(8,128)(2,1)} %refs_0_.1), channel_id=1, source_target_pairs={{0,8},{4,12},{8,0},{12,4},{16,24},{20,28},{24,16},{28,20},{1,9},{5... | collective-permute-start | bytes 884744 | tf_op jit(solution)/shard_map/ppermute | solution.py:19
  3.7 15.0 %collective-permute-start.1 = (bf16[64,2304]{1,0:T(8,128)(2,1)}, bf16[64,2304]{1,0:T(8,128)(2,1)S(1)}, u32[]{:S(2)}, u32[]{:S(2)}) collective-permute-start(bf16[64,2304]{1,0:T(8,128)(2,1)} %refs_0_.1), channel_id=1, source_target_pairs={{0,16},{4,20},{8,24},{12,28},{16,0},{20,4},{24,8},{28,12},{1,17},{... | collective-permute-start | bytes 884744 | tf_op jit(solution)/shard_map/ppermute | solution.py:19
  5.2 13.5 %collective-permute-start.2 = (bf16[64,2304]{1,0:T(8,128)(2,1)}, bf16[64,2304]{1,0:T(8,128)(2,1)S(1)}, u32[]{:S(2)}, u32[]{:S(2)}) collective-permute-start(bf16[64,2304]{1,0:T(8,128)(2,1)} %refs_0_.1), channel_id=1, source_target_pairs={{0,24},{4,28},{8,16},{12,20},{16,8},{20,12},{24,0},{28,4},{1,25},{... | collective-permute-start | bytes 884744 | tf_op jit(solution)/shard_map/ppermute | solution.py:19
  5.2 85.4 %collective-permute-start.3 = (bf16[64,2304]{1,0:T(8,128)(2,1)}, bf16[64,2304]{1,0:T(8,128)(2,1)S(1)}, u32[]{:S(2)}, u32[]{:S(2)}) collective-permute-start(bf16[64,2304]{1,0:T(8,128)(2,1)} %refs_0_.1), channel_id=1, source_target_pairs={{0,4},{4,0},{8,12},{12,8},{16,20},{20,16},{24,28},{28,24},{1,5},{5... | collective-permute-start | bytes 884744 | tf_op jit(solution)/shard_map/ppermute | solution.py:19
  5.2 1.0 copy-start.6
  6.2 13.0 %copy-start.4 = (s32[16,8]{0,1:T(8,128)S(1)}, s32[16,8]{0,1:T(8,128)}, u32[]{:S(2)}) copy-start(s32[16,8]{0,1:T(8,128)} %param.14) | copy-start | bytes 1540
  6.2 13.0 %copy-start.5 = (f32[16,8]{0,1:T(8,128)S(1)}, f32[16,8]{0,1:T(8,128)}, u32[]{:S(2)}) copy-start(f32[16,8]{0,1:T(8,128)} %param.15) | copy-start | bytes 1540
  6.2 84.4 %slice-start = ((s8[4718592]{0:T(1024)(128)(4,1)}), s8[524288]{0:T(1024)(128)(4,1)S(1)}, s32[]{:S(2)}) async-start(s8[4718592]{0:T(1024)(128)(4,1)} %bitcast.57), calls=%async_computation | async-start | bytes 1048576
  11.7 78.9 %collective-permute-start.4 = (bf16[64,2304]{1,0:T(8,128)(2,1)S(1)}, bf16[64,2304]{1,0:T(8,128)(2,1)S(1)}, u32[]{:S(2)}, u32[]{:S(2)}) collective-permute-start(bf16[64,2304]{1,0:T(8,128)(2,1)S(1)} %collective-permute-done.refs_1_), channel_id=1, source_target_pairs={{0,4},{4,0},{8,12},{12,8},{16,20},{20,16},{24,28},{28,24},{1,5},{5... | collective-permute-start | bytes 884744 | tf_op jit(solution)/shard_map/ppermute | solution.py:19
  18.6 71.9 %collective-permute-start.5 = (bf16[64,2304]{1,0:T(8,128)(2,1)S(1)}, bf16[64,2304]{1,0:T(8,128)(2,1)S(1)}, u32[]{:S(2)}, u32[]{:S(2)}) collective-permute-start(bf16[64,2304]{1,0:T(8,128)(2,1)S(1)} %collective-permute-done.1.refs_2_), channel_id=1, source_target_pairs={{0,4},{4,0},{8,12},{12,8},{16,20},{20,16},{24,28},{28,24},{1,5},{5... | collective-permute-start | bytes 884744 | tf_op jit(solution)/shard_map/ppermute | solution.py:19
  18.7 71.9 %collective-permute-start.6 = (bf16[64,2304]{1,0:T(8,128)(2,1)S(1)}, bf16[64,2304]{1,0:T(8,128)(2,1)S(1)}, u32[]{:S(2)}, u32[]{:S(2)}) collective-permute-start(bf16[64,2304]{1,0:T(8,128)(2,1)S(1)} %collective-permute-done.2.refs_3_), channel_id=1, source_target_pairs={{0,4},{4,0},{8,12},{12,8},{16,20},{20,16},{24,28},{28,24},{1,5},{5... | collective-permute-start | bytes 884744 | tf_op jit(solution)/shard_map/ppermute | solution.py:19
  87.9 2.7 %slice-start.1 = ((s8[4718592]{0:T(1024)(128)(4,1)}), s8[4194304]{0:T(1024)(128)(4,1)S(1)}, s32[]{:S(2)}) async-start(s8[4718592]{0:T(1024)(128)(4,1)} %bitcast.57), calls=%async_computation.1 | async-start | bytes 8388608
  92.6 2.9 %collective-permute-start.7 = (bf16[256,2304]{1,0:T(8,128)(2,1)S(1)}, bf16[256,2304]{1,0:T(8,128)(2,1)S(1)}, u32[]{:S(2)}, u32[]{:S(2)}) collective-permute-start(bf16[256,2304]{1,0:T(8,128)(2,1)S(1)} %shard_map.144), channel_id=1, source_target_pairs={{0,4},{4,0},{8,12},{12,8},{16,20},{20,16},{24,28},{28,24},{1,5},{5... | collective-permute-start | bytes 3538952 | tf_op jit(solution)/shard_map/ppermute | solution.py:19
  95.4 9.8 %copy-start.1 = (bf16[2304,256]{1,0:T(8,128)(2,1)S(1)}, bf16[2304,256]{1,0:T(8,128)(2,1)}, u32[]{:S(2)}) copy-start(bf16[2304,256]{1,0:T(8,128)(2,1)} %gate.1) | copy-start | bytes 3538948
  95.4 9.8 %copy-start.2 = (bf16[2304,256]{1,0:T(8,128)(2,1)S(1)}, bf16[2304,256]{1,0:T(8,128)(2,1)}, u32[]{:S(2)}) copy-start(bf16[2304,256]{1,0:T(8,128)(2,1)} %up.1) | copy-start | bytes 3538948
  95.4 9.8 %copy-start.3 = (bf16[256,2304]{1,0:T(8,128)(2,1)S(1)}, bf16[256,2304]{1,0:T(8,128)(2,1)}, u32[]{:S(2)}) copy-start(bf16[256,2304]{1,0:T(8,128)(2,1)} %down.5) | copy-start | bytes 3538948
  97.5 7.7 %collective-permute-start.11 = (bf16[32,2304]{1,0:T(8,128)(2,1)S(1)}, bf16[32,2304]{1,0:T(8,128)(2,1)S(1)}, u32[]{:S(2)}, u32[]{:S(2)}) collective-permute-start(bf16[32,2304]{1,0:T(8,128)(2,1)S(1)} %get-tuple-element.36), channel_id=1, source_target_pairs={{0,24},{4,28},{8,16},{12,20},{16,8},{20,12},{24,0},{28,4},{1,25},{... | collective-permute-start | bytes 442376 | tf_op jit(solution)/shard_map/ppermute | solution.py:19
  97.6 9.9 %collective-permute-start.13 = (bf16[32,2304]{1,0:T(8,128)(2,1)S(1)}, bf16[32,2304]{1,0:T(8,128)(2,1)S(1)}, u32[]{:S(2)}, u32[]{:S(2)}) collective-permute-start(bf16[32,2304]{1,0:T(8,128)(2,1)S(1)} %get-tuple-element.41), channel_id=1, source_target_pairs={{0,16},{4,20},{8,24},{12,28},{16,0},{20,4},{24,8},{28,12},{1,17},{... | collective-permute-start | bytes 442376 | tf_op jit(solution)/shard_map/ppermute | solution.py:19
  98.8 9.2 %collective-permute-start.12 = (bf16[32,2304]{1,0:T(8,128)(2,1)S(1)}, bf16[32,2304]{1,0:T(8,128)(2,1)S(1)}, u32[]{:S(2)}, u32[]{:S(2)}) collective-permute-start(bf16[32,2304]{1,0:T(8,128)(2,1)S(1)} %get-tuple-element.40), channel_id=1, source_target_pairs={{0,8},{4,12},{8,0},{12,4},{16,24},{20,28},{24,16},{28,20},{1,9},{5... | collective-permute-start | bytes 442376 | tf_op jit(solution)/shard_map/ppermute | solution.py:19
  101.0 10.5 %collective-permute-start.10 = (bf16[32,2304]{1,0:T(8,128)(2,1)S(1)}, bf16[32,2304]{1,0:T(8,128)(2,1)S(1)}, u32[]{:S(2)}, u32[]{:S(2)}) collective-permute-start(bf16[32,2304]{1,0:T(8,128)(2,1)S(1)} %get-tuple-element.35), channel_id=1, source_target_pairs={{0,24},{4,28},{8,16},{12,20},{16,8},{20,12},{24,0},{28,4},{1,25},{... | collective-permute-start | bytes 442376 | tf_op jit(solution)/shard_map/ppermute | solution.py:19
  101.7 11.6 %collective-permute-start.9 = (bf16[32,2304]{1,0:T(8,128)(2,1)S(1)}, bf16[32,2304]{1,0:T(8,128)(2,1)S(1)}, u32[]{:S(2)}, u32[]{:S(2)}) collective-permute-start(bf16[32,2304]{1,0:T(8,128)(2,1)S(1)} %get-tuple-element.34), channel_id=1, source_target_pairs={{0,16},{4,20},{8,24},{12,28},{16,0},{20,4},{24,8},{28,12},{1,17},{... | collective-permute-start | bytes 442376 | tf_op jit(solution)/shard_map/ppermute | solution.py:19
  105.2 8.8 %collective-permute-start.8 = (bf16[32,2304]{1,0:T(8,128)(2,1)S(1)}, bf16[32,2304]{1,0:T(8,128)(2,1)S(1)}, u32[]{:S(2)}, u32[]{:S(2)}) collective-permute-start(bf16[32,2304]{1,0:T(8,128)(2,1)S(1)} %get-tuple-element.33), channel_id=1, source_target_pairs={{0,8},{4,12},{8,0},{12,4},{16,24},{20,28},{24,16},{28,20},{1,9},{5... | collective-permute-start | bytes 442376 | tf_op jit(solution)/shard_map/ppermute | solution.py:19
  108.1 31.5 %copy-start.8 = (f32[512]{0:T(512)S(1)}, f32[512]{0:T(512)}, u32[]{:S(2)}) copy-start(f32[512]{0:T(512)} %param.23) | copy-start | bytes 6148
  108.2 5.8 %collective-permute-start.14 = (bf16[32,2304]{1,0:T(8,128)(2,1)S(1)}, bf16[32,2304]{1,0:T(8,128)(2,1)S(1)}, u32[]{:S(2)}, u32[]{:S(2)}) collective-permute-start(bf16[32,2304]{1,0:T(8,128)(2,1)S(1)} %add_convert_fusion.5), channel_id=1, source_target_pairs={{0,1},{1,0},{2,3},{3,2},{4,5},{5,4},{6,7},{7,6},{8,9},{9,8},{10,11... | collective-permute-start | bytes 442376 | tf_op jit(solution)/shard_map/ppermute | solution.py:19
  114.1 7.9 %collective-permute-start.15 = (bf16[2,16,2304]{2,1,0:T(8,128)(2,1)S(1)}, bf16[2,16,2304]{2,1,0:T(8,128)(2,1)S(1)}, u32[]{:S(2)}, u32[]{:S(2)}) collective-permute-start(bf16[2,16,2304]{2,1,0:T(8,128)(2,1)S(1)} %bitcast.108), channel_id=1, source_target_pairs={{0,2},{1,3},{2,0},{3,1},{4,6},{5,7},{6,4},{7,5},{8,10},{9,11},{10,... | collective-permute-start | bytes 442376 | tf_op jit(solution)/shard_map/ppermute | solution.py:19
  122.1 5.6 %collective-permute-start.16 = (bf16[32,2304]{1,0:T(8,128)(2,1)S(1)}, bf16[32,2304]{1,0:T(8,128)(2,1)S(1)}, u32[]{:S(2)}, u32[]{:S(2)}) collective-permute-start(bf16[32,2304]{1,0:T(8,128)(2,1)S(1)} %bitcast.103), channel_id=1, source_target_pairs={{0,1},{1,0},{2,3},{3,2},{4,5},{5,4},{6,7},{7,6},{8,9},{9,8},{10,11... | collective-permute-start | bytes 442376 | tf_op jit(solution)/shard_map/ppermute | solution.py:19
  122.1 9.3 %collective-permute-start.22 = (bf16[32,2304]{1,0:T(8,128)(2,1)S(1)}, bf16[32,2304]{1,0:T(8,128)(2,1)S(1)}, u32[]{:S(2)}, u32[]{:S(2)}) collective-permute-start(bf16[32,2304]{1,0:T(8,128)(2,1)S(1)} %bitcast.104), channel_id=1, source_target_pairs={{0,16},{4,20},{8,24},{12,28},{16,0},{20,4},{24,8},{28,12},{1,17},{... | collective-permute-start | bytes 442376 | tf_op jit(solution)/shard_map/ppermute | solution.py:19
  123.0 9.1 %collective-permute-start.21 = (bf16[32,2304]{1,0:T(8,128)(2,1)S(1)}, bf16[32,2304]{1,0:T(8,128)(2,1)S(1)}, u32[]{:S(2)}, u32[]{:S(2)}) collective-permute-start(bf16[32,2304]{1,0:T(8,128)(2,1)S(1)} %bitcast.105), channel_id=1, source_target_pairs={{0,8},{4,12},{8,0},{12,4},{16,24},{20,28},{24,16},{28,20},{1,9},{5... | collective-permute-start | bytes 442376 | tf_op jit(solution)/shard_map/ppermute | solution.py:19
  127.6 7.7 %collective-permute-start.23 = (bf16[32,2304]{1,0:T(8,128)(2,1)S(1)}, bf16[32,2304]{1,0:T(8,128)(2,1)S(1)}, u32[]{:S(2)}, u32[]{:S(2)}) collective-permute-start(bf16[32,2304]{1,0:T(8,128)(2,1)S(1)} %bitcast.106), channel_id=1, source_target_pairs={{0,24},{4,28},{8,16},{12,20},{16,8},{20,12},{24,0},{28,4},{1,25},{... | collective-permute-start | bytes 442376 | tf_op jit(solution)/shard_map/ppermute | solution.py:19
  128.5 11.2 %copy-start.7 = (bf16[2304,512]{1,0:T(8,128)(2,1)S(1)}, bf16[2304,512]{1,0:T(8,128)(2,1)}, u32[]{:S(2)}) copy-start(bf16[2304,512]{1,0:T(8,128)(2,1)} %param.22) | copy-start | bytes 7077892
  128.5 9.5 %collective-permute-start.19 = (bf16[32,2304]{1,0:T(8,128)(2,1)S(1)}, bf16[32,2304]{1,0:T(8,128)(2,1)S(1)}, u32[]{:S(2)}, u32[]{:S(2)}) collective-permute-start(bf16[32,2304]{1,0:T(8,128)(2,1)S(1)} %collective-permute-done.16), channel_id=1, source_target_pairs={{0,24},{4,28},{8,16},{12,20},{16,8},{20,12},{24,0},{28,4},{1,25},{... | collective-permute-start | bytes 442376 | tf_op jit(solution)/shard_map/ppermute | solution.py:19
  130.6 8.9 %collective-permute-start.18 = (bf16[32,2304]{1,0:T(8,128)(2,1)S(1)}, bf16[32,2304]{1,0:T(8,128)(2,1)S(1)}, u32[]{:S(2)}, u32[]{:S(2)}) collective-permute-start(bf16[32,2304]{1,0:T(8,128)(2,1)S(1)} %collective-permute-done.16), channel_id=1, source_target_pairs={{0,16},{4,20},{8,24},{12,28},{16,0},{20,4},{24,8},{28,12},{1,17},{... | collective-permute-start | bytes 442376 | tf_op jit(solution)/shard_map/ppermute | solution.py:19
  131.4 8.1 %collective-permute-start.17 = (bf16[32,2304]{1,0:T(8,128)(2,1)S(1)}, bf16[32,2304]{1,0:T(8,128)(2,1)S(1)}, u32[]{:S(2)}, u32[]{:S(2)}) collective-permute-start(bf16[32,2304]{1,0:T(8,128)(2,1)S(1)} %collective-permute-done.16), channel_id=1, source_target_pairs={{0,8},{4,12},{8,0},{12,4},{16,24},{20,28},{24,16},{28,20},{1,9},{5... | collective-permute-start | bytes 442376 | tf_op jit(solution)/shard_map/ppermute | solution.py:19
  135.5 6.8 %collective-permute-start.24 = (bf16[128,2304]{1,0:T(8,128)(2,1)S(1)}, bf16[128,2304]{1,0:T(8,128)(2,1)S(1)}, u32[]{:S(2)}, u32[]{:S(2)}) collective-permute-start(bf16[128,2304]{1,0:T(8,128)(2,1)S(1)} %bitcast.63), channel_id=1, source_target_pairs={{0,4},{4,0},{8,12},{12,8},{16,20},{20,16},{24,28},{28,24},{1,5},{5... | collective-permute-start | bytes 1769480 | tf_op jit(solution)/shard_map/ppermute | solution.py:19
  139.6 7.4 %collective-permute-start.20 = (bf16[128,2304]{1,0:T(8,128)(2,1)S(1)}, bf16[128,2304]{1,0:T(8,128)(2,1)S(1)}, u32[]{:S(2)}, u32[]{:S(2)}) collective-permute-start(bf16[128,2304]{1,0:T(8,128)(2,1)S(1)} %bitcast.61), channel_id=1, source_target_pairs={{0,4},{4,0},{8,12},{12,8},{16,20},{20,16},{24,28},{28,24},{1,5},{5... | collective-permute-start | bytes 1769480 | tf_op jit(solution)/shard_map/ppermute | solution.py:19
  140.7 2.2 %collective-permute-start.29 = (bf16[128,2304]{1,0:T(8,128)(2,1)S(1)}, bf16[128,2304]{1,0:T(8,128)(2,1)S(1)}, u32[]{:S(2)}, u32[]{:S(2)}) collective-permute-start(bf16[128,2304]{1,0:T(8,128)(2,1)S(1)} %convolution_convert_fusion), channel_id=1, source_target_pairs={{0,4},{4,0},{8,12},{12,8},{16,20},{20,16},{24,28},{28,24},{1,5},{5... | collective-permute-start | bytes 1769480 | tf_op jit(solution)/shard_map/ppermute | solution.py:19
  142.2 5.2 %collective-permute-start.25 = (bf16[128,2304]{1,0:T(8,128)(2,1)S(1)}, bf16[128,2304]{1,0:T(8,128)(2,1)S(1)}, u32[]{:S(2)}, u32[]{:S(2)}) collective-permute-start(bf16[128,2304]{1,0:T(8,128)(2,1)S(1)} %convolution_convert_fusion.1), channel_id=1, source_target_pairs={{0,4},{4,0},{8,12},{12,8},{16,20},{20,16},{24,28},{28,24},{1,5},{5... | collective-permute-start | bytes 1769480 | tf_op jit(solution)/shard_map/ppermute | solution.py:19
  143.4 8.5 %collective-permute-start.32 = (bf16[32,2304]{1,0:T(8,128)(2,1)S(1)}, bf16[32,2304]{1,0:T(8,128)(2,1)S(1)}, u32[]{:S(2)}, u32[]{:S(2)}) collective-permute-start(bf16[32,2304]{1,0:T(8,128)(2,1)S(1)} %get-tuple-element.50), channel_id=1, source_target_pairs={{0,24},{4,28},{8,16},{12,20},{16,8},{20,12},{24,0},{28,4},{1,25},{... | collective-permute-start | bytes 442376 | tf_op jit(solution)/shard_map/ppermute | solution.py:19
  145.3 8.9 %collective-permute-start.31 = (bf16[32,2304]{1,0:T(8,128)(2,1)S(1)}, bf16[32,2304]{1,0:T(8,128)(2,1)S(1)}, u32[]{:S(2)}, u32[]{:S(2)}) collective-permute-start(bf16[32,2304]{1,0:T(8,128)(2,1)S(1)} %get-tuple-element.51), channel_id=1, source_target_pairs={{0,16},{4,20},{8,24},{12,28},{16,0},{20,4},{24,8},{28,12},{1,17},{... | collective-permute-start | bytes 442376 | tf_op jit(solution)/shard_map/ppermute | solution.py:19
  146.7 7.5 %collective-permute-start.30 = (bf16[32,2304]{1,0:T(8,128)(2,1)S(1)}, bf16[32,2304]{1,0:T(8,128)(2,1)S(1)}, u32[]{:S(2)}, u32[]{:S(2)}) collective-permute-start(bf16[32,2304]{1,0:T(8,128)(2,1)S(1)} %get-tuple-element.49), channel_id=1, source_target_pairs={{0,8},{4,12},{8,0},{12,4},{16,24},{20,28},{24,16},{28,20},{1,9},{5... | collective-permute-start | bytes 442376 | tf_op jit(solution)/shard_map/ppermute | solution.py:19
  147.9 19.0 %copy-start.9 = (f32[2304]{0:T(1024)S(1)}, f32[2304]{0:T(1024)}, u32[]{:S(2)}) copy-start(f32[2304]{0:T(1024)} %param.25) | copy-start | bytes 27652
  148.0 9.4 %collective-permute-start.28 = (bf16[32,2304]{1,0:T(8,128)(2,1)S(1)}, bf16[32,2304]{1,0:T(8,128)(2,1)S(1)}, u32[]{:S(2)}, u32[]{:S(2)}) collective-permute-start(bf16[32,2304]{1,0:T(8,128)(2,1)S(1)} %get-tuple-element.47), channel_id=1, source_target_pairs={{0,24},{4,28},{8,16},{12,20},{16,8},{20,12},{24,0},{28,4},{1,25},{... | collective-permute-start | bytes 442376 | tf_op jit(solution)/shard_map/ppermute | solution.py:19
  149.9 10.1 %collective-permute-start.27 = (bf16[32,2304]{1,0:T(8,128)(2,1)S(1)}, bf16[32,2304]{1,0:T(8,128)(2,1)S(1)}, u32[]{:S(2)}, u32[]{:S(2)}) collective-permute-start(bf16[32,2304]{1,0:T(8,128)(2,1)S(1)} %get-tuple-element.48), channel_id=1, source_target_pairs={{0,16},{4,20},{8,24},{12,28},{16,0},{20,4},{24,8},{28,12},{1,17},{... | collective-permute-start | bytes 442376 | tf_op jit(solution)/shard_map/ppermute | solution.py:19
  151.9 8.1 %collective-permute-start.26 = (bf16[32,2304]{1,0:T(8,128)(2,1)S(1)}, bf16[32,2304]{1,0:T(8,128)(2,1)S(1)}, u32[]{:S(2)}, u32[]{:S(2)}) collective-permute-start(bf16[32,2304]{1,0:T(8,128)(2,1)S(1)} %get-tuple-element.46), channel_id=1, source_target_pairs={{0,8},{4,12},{8,0},{12,4},{16,24},{20,28},{24,16},{28,20},{1,9},{5... | collective-permute-start | bytes 442376 | tf_op jit(solution)/shard_map/ppermute | solution.py:19
  154.3 5.7 %collective-permute-start.33 = (bf16[32,2304]{1,0:T(8,128)(2,1)S(1)}, bf16[32,2304]{1,0:T(8,128)(2,1)S(1)}, u32[]{:S(2)}, u32[]{:S(2)}) collective-permute-start(bf16[32,2304]{1,0:T(8,128)(2,1)S(1)} %add_convert_fusion.2), channel_id=1, source_target_pairs={{0,1},{1,0},{2,3},{3,2},{4,5},{5,4},{6,7},{7,6},{8,9},{9,8},{10,11... | collective-permute-start | bytes 442376 | tf_op jit(solution)/shard_map/ppermute | solution.py:19
  160.2 6.8 %collective-permute-start.34 = (bf16[16,2304]{1,0:T(8,128)(2,1)S(1)}, bf16[16,2304]{1,0:T(8,128)(2,1)S(1)}, u32[]{:S(2)}, u32[]{:S(2)}) collective-permute-start(bf16[16,2304]{1,0:T(8,128)(2,1)S(1)} %fusion.9), channel_id=1, source_target_pairs={{0,2},{1,3},{2,0},{3,1},{4,6},{5,7},{6,4},{7,5},{8,10},{9,11},{10,... | collective-permute-start | bytes 221192 | tf_op jit(solution)/shard_map/ppermute | solution.py:19
  160.3 7.3 %copy-start.10 = (bf16[32,16,512]{2,1,0:T(8,128)(2,1)}, bf16[32,16,512]{2,1,0:T(8,128)(2,1)S(1)}, u32[]{:S(2)}) copy-start(bf16[32,16,512]{2,1,0:T(8,128)(2,1)S(1)} %constant_dynamic-update-slice_fusion) | copy-start | bytes 1572868

commit v11 on v10

--- a/solution.py
+++ b/solution.py
@@ -161,14 +161,16 @@
     )[0]
 
 
-def down_kernel(top, e, tile, pairs, flip, kind, scalars, hidden, down, table, *refs):
+def down_kernel(top, e, tile, feats, pairs, kind, scalars, hidden, down, table, *refs):
     count = 1 if kind is None else 2 * kind[0]
     more, outs = refs[:-count], refs[-count:]
     size = hidden.shape[0] // pairs
+    own = size // feats
     entries = []
     for p in range(pairs):
-        owner = 2 * jnp.bitwise_xor(scalars[2], p) + jnp.bitwise_xor(scalars[3], flip)
-        entries.append(full(table[pl.ds(pl.multiple_of(owner * size, size), size), :]))
+        for f in range(feats):
+            start = (jnp.bitwise_xor(scalars[2], f) * pairs + p) * own
+            entries.append(full(table[pl.ds(pl.multiple_of(start, own), own), :]))
     entries = jnp.concatenate(entries, axis=0)
     lane = lax.broadcasted_iota(jnp.int32, entries.shape, 1)
     expert = (scalars[0] * down.shape[0] + e).astype(jnp.float32)
@@ -183,7 +185,6 @@
         if kind is None:
             outs[0][:, cut] = half(value)
             continue
-        own = kind[1]
         for p in range(pairs):
             block = value[p * size : (p + 1) * size]
             block = block.reshape(size // own // 2, 2, own, tile)
@@ -192,7 +193,7 @@
             outs[pairs + p][:, cut] = half(jnp.where(scalars[1] == 0, high, low))
 
 
-def run_down(hidden, down, e, scalars, table, top, pairs, flip, more=(), kind=None):
+def run_down(hidden, down, e, scalars, table, top, feats, pairs, more=(), kind=None):
     rows, units = hidden.shape
     width = down.shape[2]
     tile = 256 if width % 256 == 0 else 128
@@ -200,7 +201,7 @@
     if kind is not None:
         outs = [((rows // kind[0] // 2, width), jnp.bfloat16)] * (2 * kind[0])
     return call(
-        functools.partial(down_kernel, top, e, tile, pairs, flip, kind),
+        functools.partial(down_kernel, top, e, tile, feats, pairs, kind),
         [scalars, hidden, down, table, *more],
         [SMEM_SPEC] + [VMEM_SPEC] * (3 + len(more)),
         outs,
@@ -235,16 +236,21 @@
     my_feat = lax.axis_index("feat")
     feat_bits = bits_of(feats)
     place = [(my_feat // bit) % 2 for bit in feat_bits]
-    my_expert = lax.axis_index("expert")
-    scalars = jnp.stack([me, place[0], my_expert // 2, my_expert % 2])
+    scalars = jnp.stack([me, place[0], my_feat])
     chunk_rows = pairs * feats // 2 * own
 
     table = run_pack(expert_ids, gate_weights)
-    table = lax.all_gather(table, ("expert", "feat"), axis=0, tiled=True)
-
-    near = [swap(tokens, "expert", 2 * p) for p in range(1, pairs)]
-    far = [swap(piece, "expert", 1) for piece in [tokens] + near]
-    mine, expert_gate, expert_up = run_load([tokens, expert_gate, expert_up])
+    table = [table] + [swap(table, "expert", 2 * p) for p in range(1, pairs)]
+    sent, table[1] = lax.optimization_barrier((tokens, table[1]))
+    table = jnp.concatenate(table, axis=0)
+    mine, table = lax.optimization_barrier((tokens, table))
+    for bit in feat_bits:
+        table = jnp.concatenate([table, swap(table, "feat", bit)], axis=0)
+    table_far = swap(table, "expert", 1)
+
+    near = [swap(sent, "expert", 2 * p) for p in range(1, pairs)]
+    far = [swap(piece, "expert", 1) for piece in [sent] + near]
+    mine, expert_gate, expert_up = run_load([mine, expert_gate, expert_up])
     near = [mine] + near
 
     hidden = [run_hidden(near, expert_gate, expert_up, e) for e in local_experts]
@@ -252,15 +258,15 @@
     arrived = None
     for e in local_experts:
         more = [] if arrived is None else [arrived]
-        arrived = run_down(hidden[e], expert_down, e, scalars, table, top, pairs, 0, more)[0]
+        arrived = run_down(hidden[e], expert_down, e, scalars, table, top, feats, pairs, more)[0]
     arrived = swap(arrived, "expert", 1)
     for e in local_experts:
         hidden = run_hidden(far, expert_gate, expert_up, e)
         if e < local_experts[-1]:
             more = [arrived]
-            arrived = run_down(hidden, expert_down, e, scalars, table, top, pairs, 1, more)[0]
+            arrived = run_down(hidden, expert_down, e, scalars, table_far, top, feats, pairs, more)[0]
     blocks = run_down(
-        hidden, expert_down, e, scalars, table, top, pairs, 1, [arrived], (pairs, own)
+        hidden, expert_down, e, scalars, table_far, top, feats, pairs, [arrived], (pairs, own)
     )
     blocks = [blocks[:pairs], blocks[pairs:]]
     blocks = [

time: 168 us -> 111 us (0.66)
  blocking collectives: 68.4 us -> 0 us
  starting transfers between devices: 26.1 us -> 45.8 us
  waiting for transfers between devices: 50.3 us -> 38.7 us
  local copies, waits for them, and re-layouts: 1.47 us -> 3.37 us
    all_gather x1 -> x0, blocking collectives: 68.4 us -> none  [shards(): table = lax.all_gather(table, ('expert', 'feat'), axis=0, tiled=True)]
    ppermute x35 -> x41, starting transfers between devices: 26.1 us -> 45.8 us  [swap(): lax.ppermute(value, axis, [(i, i ^ r) for i in range(lax.axis_size(axis))])]
    ppermute x35 -> x41, waiting for transfers between devices: 50.3 us -> 38.7 us  [swap(): lax.ppermute(value, axis, [(i, i ^ r) for i in range(lax.axis_size(axis))])]
    unnamed x57 -> x59, local copies, waits for them, and re-layouts: 1.38 us -> 3.27 us
  transfers between devices with their start and end apart: 35 -> 41, of which waited for: 19 -> 14; matrix products, arithmetic and copies ran while one was open for 3% -> 6% of each run, Pallas kernels for 6% -> 10%
where the time goes in v11:
time: 111 us
  starting transfers between devices  45.8 us (41%)
  waiting for transfers between devices  38.7 us (35%)
  Pallas kernels  14.7 us (13%)
  matrix products  5.52 us (5%)
  local copies, waits for them, and re-layouts  3.37 us (3%)
  other arithmetic  1.36 us (1%)
  between operations  1.29 us (1%)
    ppermute x41, starting transfers between devices, swap(): lax.ppermute(value, axis, [(i, i ^ r) for i in range(lax.axis_size(axis))])  45.8 us
    ppermute x41, waiting for transfers between devices, swap(): lax.ppermute(value, axis, [(i, i ^ r) for i in range(lax.axis_size(axis))])  38.7 us
    pallas_call x7, Pallas kernels, call(): pl.pallas_call(body, in_specs=specs, out_specs=[VMEM_SPEC] * len(outs), o...  14.7 us
    dot_general x8, matrix products, dot(): return jnp.dot(a, b, preferred_element_type=jnp.float32)  5.52 us
    unnamed x59, local copies, waits for them, and re-layouts  3.27 us
  transfers between devices with their start and end apart: 41, of which 14 were waited for; matrix products, arithmetic and copies ran while one was open for 6% of the time, Pallas kernels for 10%

profile of v11, /device:TPU:0, one launch (start us, length us, event | category | flops | bytes accessed | tf_op | source)
XLA Modules:
  0.0 110.8 jit_solution(11149290201008691066)
XLA Ops:
  0.7 0.8 copy-done.4
  1.5 0.7 copy-done.5
  2.3 2.9 %collective-permute-start = (bf16[16,128]{1,0:T(8,128)(2,1)S(1)}, bf16[16,128]{1,0:T(8,128)(2,1)S(1)}, u32[]{:S(2)}, u32[]{:S(2)}) collective-permute-start(bf16[16,128]{1,0:T(8,128)(2,1)S(1)} %shard_map.140), channel_id=1, source_target_pairs={{0,8},{4,12},{8,0},{12,4},{16,24},{20,28},{24,16},{28,20},{1,9},{5... | collective-permute-start | bytes 12296 | tf_op jit(solution)/shard_map/ppermute | solution.py:19
  5.3 1.5 %collective-permute-start.1 = (bf16[16,128]{1,0:T(8,128)(2,1)S(1)}, bf16[16,128]{1,0:T(8,128)(2,1)S(1)}, u32[]{:S(2)}, u32[]{:S(2)}) collective-permute-start(bf16[16,128]{1,0:T(8,128)(2,1)S(1)} %shard_map.140), channel_id=1, source_target_pairs={{0,16},{4,20},{8,24},{12,28},{16,0},{20,4},{24,8},{28,12},{1,17},{... | collective-permute-start | bytes 12296 | tf_op jit(solution)/shard_map/ppermute | solution.py:19
  6.9 2.0 %collective-permute-start.3 = (bf16[64,2304]{1,0:T(8,128)(2,1)}, bf16[64,2304]{1,0:T(8,128)(2,1)S(1)}, u32[]{:S(2)}, u32[]{:S(2)}) collective-permute-start(bf16[64,2304]{1,0:T(8,128)(2,1)} %refs_0_), channel_id=1, source_target_pairs={{0,8},{4,12},{8,0},{12,4},{16,24},{20,28},{24,16},{28,20},{1,9},{5... | collective-permute-start | bytes 884744 | tf_op jit(solution)/shard_map/ppermute | solution.py:19
  8.9 1.5 %collective-permute-start.4 = (bf16[64,2304]{1,0:T(8,128)(2,1)}, bf16[64,2304]{1,0:T(8,128)(2,1)S(1)}, u32[]{:S(2)}, u32[]{:S(2)}) collective-permute-start(bf16[64,2304]{1,0:T(8,128)(2,1)} %refs_0_), channel_id=1, source_target_pairs={{0,16},{4,20},{8,24},{12,28},{16,0},{20,4},{24,8},{28,12},{1,17},{... | collective-permute-start | bytes 884744 | tf_op jit(solution)/shard_map/ppermute | solution.py:19
  10.4 0.9 collective-permute-done.2
  11.4 1.6 %collective-permute-start.10 = (bf16[64,128]{1,0:T(8,128)(2,1)S(1)}, bf16[64,128]{1,0:T(8,128)(2,1)S(1)}, u32[]{:S(2)}, u32[]{:S(2)}) collective-permute-start(bf16[64,128]{1,0:T(8,128)(2,1)S(1)} %pad_maximum_fusion.3), channel_id=1, source_target_pairs={{0,1},{1,0},{2,3},{3,2},{4,5},{5,4},{6,7},{7,6},{8,9},{9,8},{10,11... | collective-permute-start | bytes 49160 | tf_op jit(solution)/shard_map/ppermute | solution.py:19
  13.0 1.0 copy-done.6
  13.9 3.9 %shard_map.141 = (bf16[64,2304]{1,0:T(8,128)(2,1)S(1)}, bf16[1,2304,1024]{2,1,0:T(8,128)(2,1)S(1)}, bf16[1,2304,1024]{2,1,0:T(8,128)(2,1)S(1)}) custom-call(bf16[64,2304]{1,0:T(8,128)(2,1)S(1)} %copy-done.6, bf16[1,2304,1024]{2,1,0:T(8,128)(2,1)} %refs_1_.1, bf16[1,2304,1024]{2,1,0:T(8,128)(2,1)} %refs_2_.1), custom_call_target="tpu_custom_call" | custom-call | flops 2676326400 | bytes 19464192 | tf_op jit(solution)/shard_map/pallas_call | solution.py:49
  17.9 2.7 %collective-permute-start.11 = (bf16[128,128]{1,0:T(8,128)(2,1)S(1)}, bf16[128,128]{1,0:T(8,128)(2,1)S(1)}, u32[]{:S(2)}, u32[]{:S(2)}) collective-permute-start(bf16[128,128]{1,0:T(8,128)(2,1)S(1)} %pad_maximum_fusion.2), channel_id=1, source_target_pairs={{0,2},{1,3},{2,0},{3,1},{4,6},{5,7},{6,4},{7,5},{8,10},{9,11},{10,... | collective-permute-start | bytes 98312 | tf_op jit(solution)/shard_map/ppermute | solution.py:19
  20.5 2.5 %collective-permute-done.4.refs_2_ = bf16[64,2304]{1,0:T(8,128)(2,1)S(1)} collective-permute-done((bf16[64,2304]{1,0:T(8,128)(2,1)}, bf16[64,2304]{1,0:T(8,128)(2,1)S(1)}, u32[]{:S(2)}, u32[]{:S(2)}) %collective-permute-start.4) | collective-permute-done | bytes 294944 | tf_op jit(solution)/shard_map/ppermute | solution.py:19
  23.6 2.7 %shard_map.142.hidden = bf16[256,1024]{1,0:T(8,128)(2,1)S(1)} custom-call(bf16[64,2304]{1,0:T(8,128)(2,1)S(1)} %get-tuple-element.30.refs_0_, bf16[64,2304]{1,0:T(8,128)(2,1)S(1)} %collective-permute-done.3.refs_1_, bf16[64,2304]{1,0:T(8,128)(2,1)S(1)} %collective-permute-done.4.refs_2_, bf16[64,2304]{1,0:T(8,128)(2,1)S(1)} %collective-permute-done.5.refs_3_, ...), custom_call_target="tpu_custom_call" | custom-call | flops 2415919104 | bytes 9437184 | tf_op jit(solution)/shard_map/pallas_call | solution.py:49
  26.4 1.9 %shard_map.144 = bf16[256,2304]{1,0:T(8,128)(2,1)S(1)} custom-call(s32[3]{0:T(128)S(1)} %pad_add_fusion.scalars, bf16[256,1024]{1,0:T(8,128)(2,1)S(1)} %shard_map.142.hidden, bf16[1,1024,2304]{2,1,0:T(8,128)(2,1)S(1)} %bitcast.57, bf16[256,128]{1,0:T(8,128)(2,1)S(1)} %constant_dynamic-update-slice_fusion.table), custom_call_target="tpu_custom_call" | custom-call | flops 1207959552 | bytes 4718592 | tf_op jit(solution)/shard_map/pallas_call | solution.py:49
  28.9 2.7 %shard_map.143.hidden = bf16[256,1024]{1,0:T(8,128)(2,1)S(1)} custom-call(bf16[64,2304]{1,0:T(8,128)(2,1)S(1)} %collective-permute-done.6.refs_0_.x, bf16[64,2304]{1,0:T(8,128)(2,1)S(1)} %collective-permute-done.7.refs_1_, bf16[64,2304]{1,0:T(8,128)(2,1)S(1)} %collective-permute-done.8.refs_2_, bf16[64,2304]{1,0:T(8,128)(2,1)S(1)} %collective-permute-done.9.refs_3_, ...), custom_call_target="tpu_custom_call" | custom-call | flops 2415919104 | bytes 9437184 | tf_op jit(solution)/shard_map/pallas_call | solution.py:49
  31.6 2.0 %shard_map.145 = (bf16[32,2304]{1,0:T(8,128)(2,1)S(1)}, bf16[32,2304]{1,0:T(8,128)(2,1)S(1)}, bf16[32,2304]{1,0:T(8,128)(2,1)S(1)}, bf16[32,2304]{1,0:T(8,128)(2...) custom-call(s32[3]{0:T(128)S(1)} %pad_add_fusion.scalars, ...), custom_call_target="tpu_custom_call" | custom-call | flops 1207959552 | bytes 4718592 | tf_op jit(solution)/shard_map/pallas_call | solution.py:49
  33.6 1.5 %collective-permute-start.17 = (bf16[32,2304]{1,0:T(8,128)(2,1)S(1)}, bf16[32,2304]{1,0:T(8,128)(2,1)S(1)}, u32[]{:S(2)}, u32[]{:S(2)}) collective-permute-start(bf16[32,2304]{1,0:T(8,128)(2,1)S(1)} %get-tuple-element.44), channel_id=1, source_target_pairs={{0,24},{4,28},{8,16},{12,20},{16,8},{20,12},{24,0},{28,4},{1,25},{... | collective-permute-start | bytes 442376 | tf_op jit(solution)/shard_map/ppermute | solution.py:19
  35.1 1.5 %collective-permute-start.18 = (bf16[32,2304]{1,0:T(8,128)(2,1)S(1)}, bf16[32,2304]{1,0:T(8,128)(2,1)S(1)}, u32[]{:S(2)}, u32[]{:S(2)}) collective-permute-start(bf16[32,2304]{1,0:T(8,128)(2,1)S(1)} %get-tuple-element.48), channel_id=1, source_target_pairs={{0,8},{4,12},{8,0},{12,4},{16,24},{20,28},{24,16},{28,20},{1,9},{5... | collective-permute-start | bytes 442376 | tf_op jit(solution)/shard_map/ppermute | solution.py:19
  37.2 0.8 collective-permute-start.14
  38.0 1.2 %collective-permute-start.15 = (bf16[32,2304]{1,0:T(8,128)(2,1)S(1)}, bf16[32,2304]{1,0:T(8,128)(2,1)S(1)}, u32[]{:S(2)}, u32[]{:S(2)}) collective-permute-start(bf16[32,2304]{1,0:T(8,128)(2,1)S(1)} %get-tuple-element.42), channel_id=1, source_target_pairs={{0,16},{4,20},{8,24},{12,28},{16,0},{20,4},{24,8},{28,12},{1,17},{... | collective-permute-start | bytes 442376 | tf_op jit(solution)/shard_map/ppermute | solution.py:19
  39.2 2.1 %collective-permute-done.17 = bf16[32,2304]{1,0:T(8,128)(2,1)S(1)} collective-permute-done((bf16[32,2304]{1,0:T(8,128)(2,1)S(1)}, bf16[32,2304]{1,0:T(8,128)(2,1)S(1)}, u32[]{:S(2)}, u32[]{:S(2)}) %collective-permute-start.17) | collective-permute-done | bytes 147488 | tf_op jit(solution)/shard_map/ppermute | solution.py:19
  41.3 1.4 %collective-permute-start.16 = (bf16[32,2304]{1,0:T(8,128)(2,1)S(1)}, bf16[32,2304]{1,0:T(8,128)(2,1)S(1)}, u32[]{:S(2)}, u32[]{:S(2)}) collective-permute-start(bf16[32,2304]{1,0:T(8,128)(2,1)S(1)} %get-tuple-element.43), channel_id=1, source_target_pairs={{0,24},{4,28},{8,16},{12,20},{16,8},{20,12},{24,0},{28,4},{1,25},{... | collective-permute-start | bytes 442376 | tf_op jit(solution)/shard_map/ppermute | solution.py:19
  42.7 1.4 %shard_map.146 = (f32[32,2304]{1,0:T(8,128)S(1)}, f32[32,2304]{1,0:T(8,128)S(1)}) custom-call(s32[3]{0:T(128)S(1)} %pad_add_fusion.scalars, bf16[64,2304]{1,0:T(8,128)(2,1)S(1)} %collective-permute-done.6.refs_0_.x, bf16[2304,256]{1,0:T(8,128)(2,1)S(1)} %copy-done.1, bf16[2304,256]{1,0:T(8,128)(2,1)S(1)} %copy-done.2, bf16[256,2304]{1,0:T(8,128)(2,1)S(1)} %copy-done.3), custom_call_target="tpu_custom_call" | custom-call | flops 226492416 | bytes 3538944 | tf_op jit(solution)/shard_map/pallas_call | solution.py:49
  44.6 1.7 %collective-permute-start.20 = (bf16[32,2304]{1,0:T(8,128)(2,1)S(1)}, bf16[32,2304]{1,0:T(8,128)(2,1)S(1)}, u32[]{:S(2)}, u32[]{:S(2)}) collective-permute-start(bf16[32,2304]{1,0:T(8,128)(2,1)S(1)} %add_convert_fusion.5), channel_id=1, source_target_pairs={{0,1},{1,0},{2,3},{3,2},{4,5},{5,4},{6,7},{7,6},{8,9},{9,8},{10,11... | collective-permute-start | bytes 442376 | tf_op jit(solution)/shard_map/ppermute | solution.py:19
  46.2 1.4 %collective-permute-done.14 = bf16[32,2304]{1,0:T(8,128)(2,1)S(1)} collective-permute-done((bf16[32,2304]{1,0:T(8,128)(2,1)S(1)}, bf16[32,2304]{1,0:T(8,128)(2,1)S(1)}, u32[]{:S(2)}, u32[]{:S(2)}) %collective-permute-start.14) | collective-permute-done | bytes 147488 | tf_op jit(solution)/shard_map/ppermute | solution.py:19
  47.6 2.3 %collective-permute-done.16 = bf16[32,2304]{1,0:T(8,128)(2,1)S(1)} collective-permute-done((bf16[32,2304]{1,0:T(8,128)(2,1)S(1)}, bf16[32,2304]{1,0:T(8,128)(2,1)S(1)}, u32[]{:S(2)}, u32[]{:S(2)}) %collective-permute-start.16) | collective-permute-done | bytes 147488 | tf_op jit(solution)/shard_map/ppermute | solution.py:19
  50.0 2.7 %collective-permute-start.21 = (bf16[2,16,2304]{2,1,0:T(8,128)(2,1)S(1)}, bf16[2,16,2304]{2,1,0:T(8,128)(2,1)S(1)}, u32[]{:S(2)}, u32[]{:S(2)}) collective-permute-start(bf16[2,16,2304]{2,1,0:T(8,128)(2,1)S(1)} %bitcast.107), channel_id=1, source_target_pairs={{0,2},{1,3},{2,0},{3,1},{4,6},{5,7},{6,4},{7,5},{8,10},{9,11},{10,... | collective-permute-start | bytes 442376 | tf_op jit(solution)/shard_map/ppermute | solution.py:19
  52.7 6.5 %collective-permute-done.21 = bf16[2,16,2304]{2,1,0:T(8,128)(2,1)S(1)} collective-permute-done((bf16[2,16,2304]{2,1,0:T(8,128)(2,1)S(1)}, bf16[2,16,2304]{2,1,0:T(8,128)(2,1)S(1)}, u32[]{:S(2)}, u32[]{:S(2)}) %collective-permute-start.21) | collective-permute-done | bytes 147488 | tf_op jit(solution)/shard_map/ppermute | solution.py:19
  59.2 0.7 collective-permute-start.22
  59.9 4.5 %collective-permute-done.22 = bf16[32,2304]{1,0:T(8,128)(2,1)S(1)} collective-permute-done((bf16[32,2304]{1,0:T(8,128)(2,1)S(1)}, bf16[32,2304]{1,0:T(8,128)(2,1)S(1)}, u32[]{:S(2)}, u32[]{:S(2)}) %collective-permute-start.22) | collective-permute-done | bytes 147488 | tf_op jit(solution)/shard_map/ppermute | solution.py:19
  64.4 1.4 %collective-permute-start.25 = (bf16[32,2304]{1,0:T(8,128)(2,1)S(1)}, bf16[32,2304]{1,0:T(8,128)(2,1)S(1)}, u32[]{:S(2)}, u32[]{:S(2)}) collective-permute-start(bf16[32,2304]{1,0:T(8,128)(2,1)S(1)} %collective-permute-done.22), channel_id=1, source_target_pairs={{0,24},{4,28},{8,16},{12,20},{16,8},{20,12},{24,0},{28,4},{1,25},{... | collective-permute-start | bytes 442376 | tf_op jit(solution)/shard_map/ppermute | solution.py:19
  65.9 1.5 %collective-permute-start.23 = (bf16[32,2304]{1,0:T(8,128)(2,1)S(1)}, bf16[32,2304]{1,0:T(8,128)(2,1)S(1)}, u32[]{:S(2)}, u32[]{:S(2)}) collective-permute-start(bf16[32,2304]{1,0:T(8,128)(2,1)S(1)} %collective-permute-done.22), channel_id=1, source_target_pairs={{0,8},{4,12},{8,0},{12,4},{16,24},{20,28},{24,16},{28,20},{1,9},{5... | collective-permute-start | bytes 442376 | tf_op jit(solution)/shard_map/ppermute | solution.py:19
  67.9 1.6 %collective-permute-start.27 = (bf16[32,2304]{1,0:T(8,128)(2,1)S(1)}, bf16[32,2304]{1,0:T(8,128)(2,1)S(1)}, u32[]{:S(2)}, u32[]{:S(2)}) collective-permute-start(bf16[32,2304]{1,0:T(8,128)(2,1)S(1)} %bitcast.103), channel_id=1, source_target_pairs={{0,8},{4,12},{8,0},{12,4},{16,24},{20,28},{24,16},{28,20},{1,9},{5... | collective-permute-start | bytes 442376 | tf_op jit(solution)/shard_map/ppermute | solution.py:19
  69.9 2.2 %collective-permute-done.25 = bf16[32,2304]{1,0:T(8,128)(2,1)S(1)} collective-permute-done((bf16[32,2304]{1,0:T(8,128)(2,1)S(1)}, bf16[32,2304]{1,0:T(8,128)(2,1)S(1)}, u32[]{:S(2)}, u32[]{:S(2)}) %collective-permute-start.25) | collective-permute-done | bytes 147488 | tf_op jit(solution)/shard_map/ppermute | solution.py:19
  72.1 1.5 %collective-permute-start.29 = (bf16[32,2304]{1,0:T(8,128)(2,1)S(1)}, bf16[32,2304]{1,0:T(8,128)(2,1)S(1)}, u32[]{:S(2)}, u32[]{:S(2)}) collective-permute-start(bf16[32,2304]{1,0:T(8,128)(2,1)S(1)} %bitcast.105), channel_id=1, source_target_pairs={{0,24},{4,28},{8,16},{12,20},{16,8},{20,12},{24,0},{28,4},{1,25},{... | collective-permute-start | bytes 442376 | tf_op jit(solution)/shard_map/ppermute | solution.py:19
  73.6 1.7 %collective-permute-done.23 = bf16[32,2304]{1,0:T(8,128)(2,1)S(1)} collective-permute-done((bf16[32,2304]{1,0:T(8,128)(2,1)S(1)}, bf16[32,2304]{1,0:T(8,128)(2,1)S(1)}, u32[]{:S(2)}, u32[]{:S(2)}) %collective-permute-start.23) | collective-permute-done | bytes 147488 | tf_op jit(solution)/shard_map/ppermute | solution.py:19
  75.5 2.1 %fusion.6 = bf16[128,512]{1,0:T(8,128)(2,1)S(1)} fusion(bf16[128,2304]{1,0:T(8,128)(2,1)S(1)} %bitcast.61, bf16[2304,512]{1,0:T(8,128)(2,1)} %param.22, f32[512]{0:T(512)S(1)} %copy-done.8), kind=kOutput, calls=%fused_computation.14 | convolution fusion | flops 302186496 | bytes 3082240 | tf_op jit(solution)/shard_map/dot_general | solution.py:23
  81.9 1.6 %collective-permute-start.32 = (bf16[32,2304]{1,0:T(8,128)(2,1)S(1)}, bf16[32,2304]{1,0:T(8,128)(2,1)S(1)}, u32[]{:S(2)}, u32[]{:S(2)}) collective-permute-start(bf16[32,2304]{1,0:T(8,128)(2,1)S(1)} %get-tuple-element.54), channel_id=1, source_target_pairs={{0,8},{4,12},{8,0},{12,4},{16,24},{20,28},{24,16},{28,20},{1,9},{5... | collective-permute-start | bytes 442376 | tf_op jit(solution)/shard_map/ppermute | solution.py:19
  85.1 1.4 %collective-permute-start.36 = (bf16[32,2304]{1,0:T(8,128)(2,1)S(1)}, bf16[32,2304]{1,0:T(8,128)(2,1)S(1)}, u32[]{:S(2)}, u32[]{:S(2)}) collective-permute-start(bf16[32,2304]{1,0:T(8,128)(2,1)S(1)} %get-tuple-element.57), channel_id=1, source_target_pairs={{0,8},{4,12},{8,0},{12,4},{16,24},{20,28},{24,16},{28,20},{1,9},{5... | collective-permute-start | bytes 442376 | tf_op jit(solution)/shard_map/ppermute | solution.py:19
  87.1 1.6 %collective-permute-start.38 = (bf16[32,2304]{1,0:T(8,128)(2,1)S(1)}, bf16[32,2304]{1,0:T(8,128)(2,1)S(1)}, u32[]{:S(2)}, u32[]{:S(2)}) collective-permute-start(bf16[32,2304]{1,0:T(8,128)(2,1)S(1)} %get-tuple-element.58), channel_id=1, source_target_pairs={{0,24},{4,28},{8,16},{12,20},{16,8},{20,12},{24,0},{28,4},{1,25},{... | collective-permute-start | bytes 442376 | tf_op jit(solution)/shard_map/ppermute | solution.py:19
  89.2 2.7 %collective-permute-done.36 = bf16[32,2304]{1,0:T(8,128)(2,1)S(1)} collective-permute-done((bf16[32,2304]{1,0:T(8,128)(2,1)S(1)}, bf16[32,2304]{1,0:T(8,128)(2,1)S(1)}, u32[]{:S(2)}, u32[]{:S(2)}) %collective-permute-start.36) | collective-permute-done | bytes 147488 | tf_op jit(solution)/shard_map/ppermute | solution.py:19
  91.9 1.4 %collective-permute-start.34 = (bf16[32,2304]{1,0:T(8,128)(2,1)S(1)}, bf16[32,2304]{1,0:T(8,128)(2,1)S(1)}, u32[]{:S(2)}, u32[]{:S(2)}) collective-permute-start(bf16[32,2304]{1,0:T(8,128)(2,1)S(1)} %get-tuple-element.55), channel_id=1, source_target_pairs={{0,24},{4,28},{8,16},{12,20},{16,8},{20,12},{24,0},{28,4},{1,25},{... | collective-permute-start | bytes 442376 | tf_op jit(solution)/shard_map/ppermute | solution.py:19
  93.3 5.1 %collective-permute-done.37 = bf16[32,2304]{1,0:T(8,128)(2,1)S(1)} collective-permute-done((bf16[32,2304]{1,0:T(8,128)(2,1)S(1)}, bf16[32,2304]{1,0:T(8,128)(2,1)S(1)}, u32[]{:S(2)}, u32[]{:S(2)}) %collective-permute-start.37) | collective-permute-done | bytes 147488 | tf_op jit(solution)/shard_map/ppermute | solution.py:19
  98.5 2.0 %collective-permute-start.39 = (bf16[32,2304]{1,0:T(8,128)(2,1)S(1)}, bf16[32,2304]{1,0:T(8,128)(2,1)S(1)}, u32[]{:S(2)}, u32[]{:S(2)}) collective-permute-start(bf16[32,2304]{1,0:T(8,128)(2,1)S(1)} %add_convert_fusion.2), channel_id=1, source_target_pairs={{0,1},{1,0},{2,3},{3,2},{4,5},{5,4},{6,7},{7,6},{8,9},{9,8},{10,11... | collective-permute-start | bytes 442376 | tf_op jit(solution)/shard_map/ppermute | solution.py:19
  100.5 4.0 %collective-permute-done.39 = bf16[32,2304]{1,0:T(8,128)(2,1)S(1)} collective-permute-done((bf16[32,2304]{1,0:T(8,128)(2,1)S(1)}, bf16[32,2304]{1,0:T(8,128)(2,1)S(1)}, u32[]{:S(2)}, u32[]{:S(2)}) %collective-permute-start.39) | collective-permute-done | bytes 147488 | tf_op jit(solution)/shard_map/ppermute | solution.py:19
  104.7 3.2 %collective-permute-start.40 = (bf16[16,2304]{1,0:T(8,128)(2,1)S(1)}, bf16[16,2304]{1,0:T(8,128)(2,1)S(1)}, u32[]{:S(2)}, u32[]{:S(2)}) collective-permute-start(bf16[16,2304]{1,0:T(8,128)(2,1)S(1)} %fusion.9), channel_id=1, source_target_pairs={{0,2},{1,3},{2,0},{3,1},{4,6},{5,7},{6,4},{7,5},{8,10},{9,11},{10,... | collective-permute-start | bytes 221192 | tf_op jit(solution)/shard_map/ppermute | solution.py:19
  107.8 2.3 %collective-permute-done.40 = bf16[16,2304]{1,0:T(8,128)(2,1)S(1)} collective-permute-done((bf16[16,2304]{1,0:T(8,128)(2,1)S(1)}, bf16[16,2304]{1,0:T(8,128)(2,1)S(1)}, u32[]{:S(2)}, u32[]{:S(2)}) %collective-permute-start.40) | collective-permute-done | bytes 73760 | tf_op jit(solution)/shard_map/ppermute | solution.py:19
  110.1 0.7 fusion.8
  (126 shorter events, 10.5 us)
Async XLA Ops:
  0.6 77.0 %copy-start = (bf16[512,2304]{1,0:T(8,128)(2,1)S(1)}, bf16[512,2304]{1,0:T(8,128)(2,1)}, u32[]{:S(2)}) copy-start(bf16[512,2304]{1,0:T(8,128)(2,1)} %param.24) | copy-start | bytes 7077892
  2.3 4.5 %collective-permute-start = (bf16[16,128]{1,0:T(8,128)(2,1)S(1)}, bf16[16,128]{1,0:T(8,128)(2,1)S(1)}, u32[]{:S(2)}, u32[]{:S(2)}) collective-permute-start(bf16[16,128]{1,0:T(8,128)(2,1)S(1)} %shard_map.140), channel_id=1, source_target_pairs={{0,8},{4,12},{8,0},{12,4},{16,24},{20,28},{24,16},{28,20},{1,9},{5... | collective-permute-start | bytes 12296 | tf_op jit(solution)/shard_map/ppermute | solution.py:19
  5.3 5.1 %collective-permute-start.1 = (bf16[16,128]{1,0:T(8,128)(2,1)S(1)}, bf16[16,128]{1,0:T(8,128)(2,1)S(1)}, u32[]{:S(2)}, u32[]{:S(2)}) collective-permute-start(bf16[16,128]{1,0:T(8,128)(2,1)S(1)} %shard_map.140), channel_id=1, source_target_pairs={{0,16},{4,20},{8,24},{12,28},{16,0},{20,4},{24,8},{28,12},{1,17},{... | collective-permute-start | bytes 12296 | tf_op jit(solution)/shard_map/ppermute | solution.py:19
  6.8 4.6 %collective-permute-start.2 = (bf16[16,128]{1,0:T(8,128)(2,1)S(1)}, bf16[16,128]{1,0:T(8,128)(2,1)S(1)}, u32[]{:S(2)}, u32[]{:S(2)}) collective-permute-start(bf16[16,128]{1,0:T(8,128)(2,1)S(1)} %shard_map.140), channel_id=1, source_target_pairs={{0,24},{4,28},{8,16},{12,20},{16,8},{20,12},{24,0},{28,4},{1,25},{... | collective-permute-start | bytes 12296 | tf_op jit(solution)/shard_map/ppermute | solution.py:19
  6.9 13.6 %collective-permute-start.3 = (bf16[64,2304]{1,0:T(8,128)(2,1)}, bf16[64,2304]{1,0:T(8,128)(2,1)S(1)}, u32[]{:S(2)}, u32[]{:S(2)}) collective-permute-start(bf16[64,2304]{1,0:T(8,128)(2,1)} %refs_0_), channel_id=1, source_target_pairs={{0,8},{4,12},{8,0},{12,4},{16,24},{20,28},{24,16},{28,20},{1,9},{5... | collective-permute-start | bytes 884744 | tf_op jit(solution)/shard_map/ppermute | solution.py:19
  8.9 14.2 %collective-permute-start.4 = (bf16[64,2304]{1,0:T(8,128)(2,1)}, bf16[64,2304]{1,0:T(8,128)(2,1)S(1)}, u32[]{:S(2)}, u32[]{:S(2)}) collective-permute-start(bf16[64,2304]{1,0:T(8,128)(2,1)} %refs_0_), channel_id=1, source_target_pairs={{0,16},{4,20},{8,24},{12,28},{16,0},{20,4},{24,8},{28,12},{1,17},{... | collective-permute-start | bytes 884744 | tf_op jit(solution)/shard_map/ppermute | solution.py:19
  10.4 12.7 %collective-permute-start.5 = (bf16[64,2304]{1,0:T(8,128)(2,1)}, bf16[64,2304]{1,0:T(8,128)(2,1)S(1)}, u32[]{:S(2)}, u32[]{:S(2)}) collective-permute-start(bf16[64,2304]{1,0:T(8,128)(2,1)} %refs_0_), channel_id=1, source_target_pairs={{0,24},{4,28},{8,16},{12,20},{16,8},{20,12},{24,0},{28,4},{1,25},{... | collective-permute-start | bytes 884744 | tf_op jit(solution)/shard_map/ppermute | solution.py:19
  10.4 15.9 %collective-permute-start.6 = (bf16[64,2304]{1,0:T(8,128)(2,1)}, bf16[64,2304]{1,0:T(8,128)(2,1)S(1)}, u32[]{:S(2)}, u32[]{:S(2)}) collective-permute-start(bf16[64,2304]{1,0:T(8,128)(2,1)} %refs_0_), channel_id=1, source_target_pairs={{0,4},{4,0},{8,12},{12,8},{16,20},{20,16},{24,28},{28,24},{1,5},{5... | collective-permute-start | bytes 884744 | tf_op jit(solution)/shard_map/ppermute | solution.py:19
  11.4 6.5 %collective-permute-start.10 = (bf16[64,128]{1,0:T(8,128)(2,1)S(1)}, bf16[64,128]{1,0:T(8,128)(2,1)S(1)}, u32[]{:S(2)}, u32[]{:S(2)}) collective-permute-start(bf16[64,128]{1,0:T(8,128)(2,1)S(1)} %pad_maximum_fusion.3), channel_id=1, source_target_pairs={{0,1},{1,0},{2,3},{3,2},{4,5},{5,4},{6,7},{7,6},{8,9},{9,8},{10,11... | collective-permute-start | bytes 49160 | tf_op jit(solution)/shard_map/ppermute | solution.py:19
  13.9 12.4 %slice-start = ((s8[4718592]{0:T(1024)(128)(4,1)}), s8[524288]{0:T(1024)(128)(4,1)S(1)}, s32[]{:S(2)}) async-start(s8[4718592]{0:T(1024)(128)(4,1)} %bitcast.56), calls=%async_computation | async-start | bytes 1048576
  17.9 5.7 %collective-permute-start.11 = (bf16[128,128]{1,0:T(8,128)(2,1)S(1)}, bf16[128,128]{1,0:T(8,128)(2,1)S(1)}, u32[]{:S(2)}, u32[]{:S(2)}) collective-permute-start(bf16[128,128]{1,0:T(8,128)(2,1)S(1)} %pad_maximum_fusion.2), channel_id=1, source_target_pairs={{0,2},{1,3},{2,0},{3,1},{4,6},{5,7},{6,4},{7,5},{8,10},{9,11},{10,... | collective-permute-start | bytes 98312 | tf_op jit(solution)/shard_map/ppermute | solution.py:19
  20.5 5.8 %collective-permute-start.7 = (bf16[64,2304]{1,0:T(8,128)(2,1)S(1)}, bf16[64,2304]{1,0:T(8,128)(2,1)S(1)}, u32[]{:S(2)}, u32[]{:S(2)}) collective-permute-start(bf16[64,2304]{1,0:T(8,128)(2,1)S(1)} %collective-permute-done.3.refs_1_), channel_id=1, source_target_pairs={{0,4},{4,0},{8,12},{12,8},{16,20},{20,16},{24,28},{28,24},{1,5},{5... | collective-permute-start | bytes 884744 | tf_op jit(solution)/shard_map/ppermute | solution.py:19
  23.1 3.2 %collective-permute-start.8 = (bf16[64,2304]{1,0:T(8,128)(2,1)S(1)}, bf16[64,2304]{1,0:T(8,128)(2,1)S(1)}, u32[]{:S(2)}, u32[]{:S(2)}) collective-permute-start(bf16[64,2304]{1,0:T(8,128)(2,1)S(1)} %collective-permute-done.4.refs_2_), channel_id=1, source_target_pairs={{0,4},{4,0},{8,12},{12,8},{16,20},{20,16},{24,28},{28,24},{1,5},{5... | collective-permute-start | bytes 884744 | tf_op jit(solution)/shard_map/ppermute | solution.py:19
  23.1 3.2 %collective-permute-start.9 = (bf16[64,2304]{1,0:T(8,128)(2,1)S(1)}, bf16[64,2304]{1,0:T(8,128)(2,1)S(1)}, u32[]{:S(2)}, u32[]{:S(2)}) collective-permute-start(bf16[64,2304]{1,0:T(8,128)(2,1)S(1)} %collective-permute-done.5.refs_3_), channel_id=1, source_target_pairs={{0,4},{4,0},{8,12},{12,8},{16,20},{20,16},{24,28},{28,24},{1,5},{5... | collective-permute-start | bytes 884744 | tf_op jit(solution)/shard_map/ppermute | solution.py:19
  28.3 3.3 %collective-permute-start.13 = (bf16[256,2304]{1,0:T(8,128)(2,1)S(1)}, bf16[256,2304]{1,0:T(8,128)(2,1)S(1)}, u32[]{:S(2)}, u32[]{:S(2)}) collective-permute-start(bf16[256,2304]{1,0:T(8,128)(2,1)S(1)} %shard_map.144), channel_id=1, source_target_pairs={{0,4},{4,0},{8,12},{12,8},{16,20},{20,16},{24,28},{28,24},{1,5},{5... | collective-permute-start | bytes 3538952 | tf_op jit(solution)/shard_map/ppermute | solution.py:19
  28.4 3.2 %collective-permute-start.12 = (bf16[256,128]{1,0:T(8,128)(2,1)S(1)}, bf16[256,128]{1,0:T(8,128)(2,1)S(1)}, u32[]{:S(2)}, u32[]{:S(2)}) collective-permute-start(bf16[256,128]{1,0:T(8,128)(2,1)S(1)} %constant_dynamic-update-slice_fusion.table), channel_id=1, source_target_pairs={{0,4},{4,0},{8,12},{12,8},{16,20},{20,16},{24,28},{28,24},{1,5},{5... | collective-permute-start | bytes 196616 | tf_op jit(solution)/shard_map/ppermute | solution.py:19
  31.5 11.2 %copy-start.1 = (bf16[2304,256]{1,0:T(8,128)(2,1)S(1)}, bf16[2304,256]{1,0:T(8,128)(2,1)}, u32[]{:S(2)}) copy-start(bf16[2304,256]{1,0:T(8,128)(2,1)} %gate.1) | copy-start | bytes 3538948
  31.6 11.2 %copy-start.2 = (bf16[2304,256]{1,0:T(8,128)(2,1)S(1)}, bf16[2304,256]{1,0:T(8,128)(2,1)}, u32[]{:S(2)}) copy-start(bf16[2304,256]{1,0:T(8,128)(2,1)} %up.1) | copy-start | bytes 3538948
  31.6 11.2 %copy-start.3 = (bf16[256,2304]{1,0:T(8,128)(2,1)S(1)}, bf16[256,2304]{1,0:T(8,128)(2,1)}, u32[]{:S(2)}) copy-start(bf16[256,2304]{1,0:T(8,128)(2,1)} %down.5) | copy-start | bytes 3538948
  33.6 7.7 %collective-permute-start.17 = (bf16[32,2304]{1,0:T(8,128)(2,1)S(1)}, bf16[32,2304]{1,0:T(8,128)(2,1)S(1)}, u32[]{:S(2)}, u32[]{:S(2)}) collective-permute-start(bf16[32,2304]{1,0:T(8,128)(2,1)S(1)} %get-tuple-element.44), channel_id=1, source_target_pairs={{0,24},{4,28},{8,16},{12,20},{16,8},{20,12},{24,0},{28,4},{1,25},{... | collective-permute-start | bytes 442376 | tf_op jit(solution)/shard_map/ppermute | solution.py:19
  35.1 9.4 %collective-permute-start.18 = (bf16[32,2304]{1,0:T(8,128)(2,1)S(1)}, bf16[32,2304]{1,0:T(8,128)(2,1)S(1)}, u32[]{:S(2)}, u32[]{:S(2)}) collective-permute-start(bf16[32,2304]{1,0:T(8,128)(2,1)S(1)} %get-tuple-element.48), channel_id=1, source_target_pairs={{0,8},{4,12},{8,0},{12,4},{16,24},{20,28},{24,16},{28,20},{1,9},{5... | collective-permute-start | bytes 442376 | tf_op jit(solution)/shard_map/ppermute | solution.py:19
  36.6 7.9 %collective-permute-start.19 = (bf16[32,2304]{1,0:T(8,128)(2,1)S(1)}, bf16[32,2304]{1,0:T(8,128)(2,1)S(1)}, u32[]{:S(2)}, u32[]{:S(2)}) collective-permute-start(bf16[32,2304]{1,0:T(8,128)(2,1)S(1)} %get-tuple-element.49), channel_id=1, source_target_pairs={{0,16},{4,20},{8,24},{12,28},{16,0},{20,4},{24,8},{28,12},{1,17},{... | collective-permute-start | bytes 442376 | tf_op jit(solution)/shard_map/ppermute | solution.py:19
  37.2 10.5 %collective-permute-start.14 = (bf16[32,2304]{1,0:T(8,128)(2,1)S(1)}, bf16[32,2304]{1,0:T(8,128)(2,1)S(1)}, u32[]{:S(2)}, u32[]{:S(2)}) collective-permute-start(bf16[32,2304]{1,0:T(8,128)(2,1)S(1)} %get-tuple-element.41), channel_id=1, source_target_pairs={{0,8},{4,12},{8,0},{12,4},{16,24},{20,28},{24,16},{28,20},{1,9},{5... | collective-permute-start | bytes 442376 | tf_op jit(solution)/shard_map/ppermute | solution.py:19
  38.0 9.6 %collective-permute-start.15 = (bf16[32,2304]{1,0:T(8,128)(2,1)S(1)}, bf16[32,2304]{1,0:T(8,128)(2,1)S(1)}, u32[]{:S(2)}, u32[]{:S(2)}) collective-permute-start(bf16[32,2304]{1,0:T(8,128)(2,1)S(1)} %get-tuple-element.42), channel_id=1, source_target_pairs={{0,16},{4,20},{8,24},{12,28},{16,0},{20,4},{24,8},{28,12},{1,17},{... | collective-permute-start | bytes 442376 | tf_op jit(solution)/shard_map/ppermute | solution.py:19
  41.3 8.6 %collective-permute-start.16 = (bf16[32,2304]{1,0:T(8,128)(2,1)S(1)}, bf16[32,2304]{1,0:T(8,128)(2,1)S(1)}, u32[]{:S(2)}, u32[]{:S(2)}) collective-permute-start(bf16[32,2304]{1,0:T(8,128)(2,1)S(1)} %get-tuple-element.43), channel_id=1, source_target_pairs={{0,24},{4,28},{8,16},{12,20},{16,8},{20,12},{24,0},{28,4},{1,25},{... | collective-permute-start | bytes 442376 | tf_op jit(solution)/shard_map/ppermute | solution.py:19
  44.1 31.3 %copy-start.8 = (f32[512]{0:T(512)S(1)}, f32[512]{0:T(512)}, u32[]{:S(2)}) copy-start(f32[512]{0:T(512)} %param.23) | copy-start | bytes 6148
  44.6 5.3 %collective-permute-start.20 = (bf16[32,2304]{1,0:T(8,128)(2,1)S(1)}, bf16[32,2304]{1,0:T(8,128)(2,1)S(1)}, u32[]{:S(2)}, u32[]{:S(2)}) collective-permute-start(bf16[32,2304]{1,0:T(8,128)(2,1)S(1)} %add_convert_fusion.5), channel_id=1, source_target_pairs={{0,1},{1,0},{2,3},{3,2},{4,5},{5,4},{6,7},{7,6},{8,9},{9,8},{10,11... | collective-permute-start | bytes 442376 | tf_op jit(solution)/shard_map/ppermute | solution.py:19
  50.0 9.1 %collective-permute-start.21 = (bf16[2,16,2304]{2,1,0:T(8,128)(2,1)S(1)}, bf16[2,16,2304]{2,1,0:T(8,128)(2,1)S(1)}, u32[]{:S(2)}, u32[]{:S(2)}) collective-permute-start(bf16[2,16,2304]{2,1,0:T(8,128)(2,1)S(1)} %bitcast.107), channel_id=1, source_target_pairs={{0,2},{1,3},{2,0},{3,1},{4,6},{5,7},{6,4},{7,5},{8,10},{9,11},{10,... | collective-permute-start | bytes 442376 | tf_op jit(solution)/shard_map/ppermute | solution.py:19
  59.2 5.2 %collective-permute-start.22 = (bf16[32,2304]{1,0:T(8,128)(2,1)S(1)}, bf16[32,2304]{1,0:T(8,128)(2,1)S(1)}, u32[]{:S(2)}, u32[]{:S(2)}) collective-permute-start(bf16[32,2304]{1,0:T(8,128)(2,1)S(1)} %bitcast.102), channel_id=1, source_target_pairs={{0,1},{1,0},{2,3},{3,2},{4,5},{5,4},{6,7},{7,6},{8,9},{9,8},{10,11... | collective-permute-start | bytes 442376 | tf_op jit(solution)/shard_map/ppermute | solution.py:19
  64.4 7.7 %collective-permute-start.25 = (bf16[32,2304]{1,0:T(8,128)(2,1)S(1)}, bf16[32,2304]{1,0:T(8,128)(2,1)S(1)}, u32[]{:S(2)}, u32[]{:S(2)}) collective-permute-start(bf16[32,2304]{1,0:T(8,128)(2,1)S(1)} %collective-permute-done.22), channel_id=1, source_target_pairs={{0,24},{4,28},{8,16},{12,20},{16,8},{20,12},{24,0},{28,4},{1,25},{... | collective-permute-start | bytes 442376 | tf_op jit(solution)/shard_map/ppermute | solution.py:19
  65.9 9.4 %collective-permute-start.23 = (bf16[32,2304]{1,0:T(8,128)(2,1)S(1)}, bf16[32,2304]{1,0:T(8,128)(2,1)S(1)}, u32[]{:S(2)}, u32[]{:S(2)}) collective-permute-start(bf16[32,2304]{1,0:T(8,128)(2,1)S(1)} %collective-permute-done.22), channel_id=1, source_target_pairs={{0,8},{4,12},{8,0},{12,4},{16,24},{20,28},{24,16},{28,20},{1,9},{5... | collective-permute-start | bytes 442376 | tf_op jit(solution)/shard_map/ppermute | solution.py:19
  67.4 7.9 %collective-permute-start.24 = (bf16[32,2304]{1,0:T(8,128)(2,1)S(1)}, bf16[32,2304]{1,0:T(8,128)(2,1)S(1)}, u32[]{:S(2)}, u32[]{:S(2)}) collective-permute-start(bf16[32,2304]{1,0:T(8,128)(2,1)S(1)} %collective-permute-done.22), channel_id=1, source_target_pairs={{0,16},{4,20},{8,24},{12,28},{16,0},{20,4},{24,8},{28,12},{1,17},{... | collective-permute-start | bytes 442376 | tf_op jit(solution)/shard_map/ppermute | solution.py:19
  67.9 10.8 %collective-permute-start.27 = (bf16[32,2304]{1,0:T(8,128)(2,1)S(1)}, bf16[32,2304]{1,0:T(8,128)(2,1)S(1)}, u32[]{:S(2)}, u32[]{:S(2)}) collective-permute-start(bf16[32,2304]{1,0:T(8,128)(2,1)S(1)} %bitcast.103), channel_id=1, source_target_pairs={{0,8},{4,12},{8,0},{12,4},{16,24},{20,28},{24,16},{28,20},{1,9},{5... | collective-permute-start | bytes 442376 | tf_op jit(solution)/shard_map/ppermute | solution.py:19
  69.5 9.2 %collective-permute-start.28 = (bf16[32,2304]{1,0:T(8,128)(2,1)S(1)}, bf16[32,2304]{1,0:T(8,128)(2,1)S(1)}, u32[]{:S(2)}, u32[]{:S(2)}) collective-permute-start(bf16[32,2304]{1,0:T(8,128)(2,1)S(1)} %bitcast.104), channel_id=1, source_target_pairs={{0,16},{4,20},{8,24},{12,28},{16,0},{20,4},{24,8},{28,12},{1,17},{... | collective-permute-start | bytes 442376 | tf_op jit(solution)/shard_map/ppermute | solution.py:19
  72.1 6.6 %collective-permute-start.29 = (bf16[32,2304]{1,0:T(8,128)(2,1)S(1)}, bf16[32,2304]{1,0:T(8,128)(2,1)S(1)}, u32[]{:S(2)}, u32[]{:S(2)}) collective-permute-start(bf16[32,2304]{1,0:T(8,128)(2,1)S(1)} %bitcast.105), channel_id=1, source_target_pairs={{0,24},{4,28},{8,16},{12,20},{16,8},{20,12},{24,0},{28,4},{1,25},{... | collective-permute-start | bytes 442376 | tf_op jit(solution)/shard_map/ppermute | solution.py:19
  75.4 5.4 %collective-permute-start.26 = (bf16[128,2304]{1,0:T(8,128)(2,1)S(1)}, bf16[128,2304]{1,0:T(8,128)(2,1)S(1)}, u32[]{:S(2)}, u32[]{:S(2)}) collective-permute-start(bf16[128,2304]{1,0:T(8,128)(2,1)S(1)} %bitcast.60), channel_id=1, source_target_pairs={{0,4},{4,0},{8,12},{12,8},{16,20},{20,16},{24,28},{28,24},{1,5},{5... | collective-permute-start | bytes 1769480 | tf_op jit(solution)/shard_map/ppermute | solution.py:19
  78.1 3.2 %collective-permute-start.31 = (bf16[128,2304]{1,0:T(8,128)(2,1)S(1)}, bf16[128,2304]{1,0:T(8,128)(2,1)S(1)}, u32[]{:S(2)}, u32[]{:S(2)}) collective-permute-start(bf16[128,2304]{1,0:T(8,128)(2,1)S(1)} %convolution_convert_fusion.1), channel_id=1, source_target_pairs={{0,4},{4,0},{8,12},{12,8},{16,20},{20,16},{24,28},{28,24},{1,5},{5... | collective-permute-start | bytes 1769480 | tf_op jit(solution)/shard_map/ppermute | solution.py:19
  78.8 5.3 %collective-permute-start.30 = (bf16[128,2304]{1,0:T(8,128)(2,1)S(1)}, bf16[128,2304]{1,0:T(8,128)(2,1)S(1)}, u32[]{:S(2)}, u32[]{:S(2)}) collective-permute-start(bf16[128,2304]{1,0:T(8,128)(2,1)S(1)} %bitcast.62), channel_id=1, source_target_pairs={{0,4},{4,0},{8,12},{12,8},{16,20},{20,16},{24,28},{28,24},{1,5},{5... | collective-permute-start | bytes 1769480 | tf_op jit(solution)/shard_map/ppermute | solution.py:19
  80.3 4.2 %collective-permute-start.35 = (bf16[128,2304]{1,0:T(8,128)(2,1)S(1)}, bf16[128,2304]{1,0:T(8,128)(2,1)S(1)}, u32[]{:S(2)}, u32[]{:S(2)}) collective-permute-start(bf16[128,2304]{1,0:T(8,128)(2,1)S(1)} %convolution_convert_fusion), channel_id=1, source_target_pairs={{0,4},{4,0},{8,12},{12,8},{16,20},{20,16},{24,28},{28,24},{1,5},{5... | collective-permute-start | bytes 1769480 | tf_op jit(solution)/shard_map/ppermute | solution.py:19
  81.9 18.7 %collective-permute-start.32 = (bf16[32,2304]{1,0:T(8,128)(2,1)S(1)}, bf16[32,2304]{1,0:T(8,128)(2,1)S(1)}, u32[]{:S(2)}, u32[]{:S(2)}) collective-permute-start(bf16[32,2304]{1,0:T(8,128)(2,1)S(1)} %get-tuple-element.54), channel_id=1, source_target_pairs={{0,8},{4,12},{8,0},{12,4},{16,24},{20,28},{24,16},{28,20},{1,9},{5... | collective-permute-start | bytes 442376 | tf_op jit(solution)/shard_map/ppermute | solution.py:19
  83.5 17.1 %collective-permute-start.33 = (bf16[32,2304]{1,0:T(8,128)(2,1)S(1)}, bf16[32,2304]{1,0:T(8,128)(2,1)S(1)}, u32[]{:S(2)}, u32[]{:S(2)}) collective-permute-start(bf16[32,2304]{1,0:T(8,128)(2,1)S(1)} %get-tuple-element.56), channel_id=1, source_target_pairs={{0,16},{4,20},{8,24},{12,28},{16,0},{20,4},{24,8},{28,12},{1,17},{... | collective-permute-start | bytes 442376 | tf_op jit(solution)/shard_map/ppermute | solution.py:19
  85.0 25.1 %copy-start.9 = (f32[2304]{0:T(1024)S(1)}, f32[2304]{0:T(1024)}, u32[]{:S(2)}) copy-start(f32[2304]{0:T(1024)} %param.25) | copy-start | bytes 27652
  85.1 6.9 %collective-permute-start.36 = (bf16[32,2304]{1,0:T(8,128)(2,1)S(1)}, bf16[32,2304]{1,0:T(8,128)(2,1)S(1)}, u32[]{:S(2)}, u32[]{:S(2)}) collective-permute-start(bf16[32,2304]{1,0:T(8,128)(2,1)S(1)} %get-tuple-element.57), channel_id=1, source_target_pairs={{0,8},{4,12},{8,0},{12,4},{16,24},{20,28},{24,16},{28,20},{1,9},{5... | collective-permute-start | bytes 442376 | tf_op jit(solution)/shard_map/ppermute | solution.py:19
  86.5 11.9 %collective-permute-start.37 = (bf16[32,2304]{1,0:T(8,128)(2,1)S(1)}, bf16[32,2304]{1,0:T(8,128)(2,1)S(1)}, u32[]{:S(2)}, u32[]{:S(2)}) collective-permute-start(bf16[32,2304]{1,0:T(8,128)(2,1)S(1)} %get-tuple-element.59), channel_id=1, source_target_pairs={{0,16},{4,20},{8,24},{12,28},{16,0},{20,4},{24,8},{28,12},{1,17},{... | collective-permute-start | bytes 442376 | tf_op jit(solution)/shard_map/ppermute | solution.py:19
  87.1 11.4 %collective-permute-start.38 = (bf16[32,2304]{1,0:T(8,128)(2,1)S(1)}, bf16[32,2304]{1,0:T(8,128)(2,1)S(1)}, u32[]{:S(2)}, u32[]{:S(2)}) collective-permute-start(bf16[32,2304]{1,0:T(8,128)(2,1)S(1)} %get-tuple-element.58), channel_id=1, source_target_pairs={{0,24},{4,28},{8,16},{12,20},{16,8},{20,12},{24,0},{28,4},{1,25},{... | collective-permute-start | bytes 442376 | tf_op jit(solution)/shard_map/ppermute | solution.py:19
  91.9 8.6 %collective-permute-start.34 = (bf16[32,2304]{1,0:T(8,128)(2,1)S(1)}, bf16[32,2304]{1,0:T(8,128)(2,1)S(1)}, u32[]{:S(2)}, u32[]{:S(2)}) collective-permute-start(bf16[32,2304]{1,0:T(8,128)(2,1)S(1)} %get-tuple-element.55), channel_id=1, source_target_pairs={{0,24},{4,28},{8,16},{12,20},{16,8},{20,12},{24,0},{28,4},{1,25},{... | collective-permute-start | bytes 442376 | tf_op jit(solution)/shard_map/ppermute | solution.py:19
  98.5 6.0 %collective-permute-start.39 = (bf16[32,2304]{1,0:T(8,128)(2,1)S(1)}, bf16[32,2304]{1,0:T(8,128)(2,1)S(1)}, u32[]{:S(2)}, u32[]{:S(2)}) collective-permute-start(bf16[32,2304]{1,0:T(8,128)(2,1)S(1)} %add_convert_fusion.2), channel_id=1, source_target_pairs={{0,1},{1,0},{2,3},{3,2},{4,5},{5,4},{6,7},{7,6},{8,9},{9,8},{10,11... | collective-permute-start | bytes 442376 | tf_op jit(solution)/shard_map/ppermute | solution.py:19
  104.7 5.5 %collective-permute-start.40 = (bf16[16,2304]{1,0:T(8,128)(2,1)S(1)}, bf16[16,2304]{1,0:T(8,128)(2,1)S(1)}, u32[]{:S(2)}, u32[]{:S(2)}) collective-permute-start(bf16[16,2304]{1,0:T(8,128)(2,1)S(1)} %fusion.9), channel_id=1, source_target_pairs={{0,2},{1,3},{2,0},{3,1},{4,6},{5,7},{6,4},{7,5},{8,10},{9,11},{10,... | collective-permute-start | bytes 221192 | tf_op jit(solution)/shard_map/ppermute | solution.py:19
  (6 other events, 9.9 us)

commit v12 on v11

--- a/solution.py
+++ b/solution.py
@@ -296,16 +296,17 @@
     def encode(x):
         return half(jax.nn.relu(dot(x, encoder) + encoder_bias[None, :]))
 
-    features, blocks = [None, None], [None, None]
+    features, blocks, zero = [None, None], [None, None], 0.0
     for chunk in (1, 0):
         near = jnp.stack(sides[chunk]).reshape(chunk_rows, width)
         far = swap(near, "expert", 1)
         features_near = encode(near)
         decoded = swap(half(dot(features_near, decoder)), "expert", 1)
         features_far = encode(far)
-        total = half(dot(features_far, decoder) + full(decoded))
+        total = half(dot(features_far, decoder) + full(decoded) + zero)
         total = total.reshape(pairs, feats // 2 * own, width)
         blocks[chunk] = [total[0]] + [swap(total[p], "expert", 2 * p) for p in range(1, pairs)]
+        zero = 0.0 * full(blocks[chunk][1][0, 0])
         both = jnp.stack([features_far, features_near])
         features[chunk] = both.reshape(2, pairs, feats // 2, 1, own, -1)
     arrived = swap(half(sum(full(block) for block in blocks[1])), "feat", feat_bits[0])

time: 111 us -> 105 us (0.946)
  waiting for transfers between devices: 38.7 us -> 31 us
    ppermute x41, waiting for transfers between devices: 38.7 us -> 31 us  [swap(): lax.ppermute(value, axis, [(i, i ^ r) for i in range(lax.axis_size(axis))])]
  transfers between devices with their start and end apart: 41 -> 41, of which waited for: 14 -> 16; matrix products, arithmetic and copies ran while one was open for 6% -> 7% of each run, Pallas kernels for 10% -> 10%
where the time goes in v12:
time: 105 us; the launch traced here: 104 us
  starting transfers between devices  46.3 us (44%)
  waiting for transfers between devices  31 us (30%)
  Pallas kernels  14.7 us (14%)
  matrix products  5.53 us (5%)
  local copies, waits for them, and re-layouts  3.46 us (3%)
  between operations  1.95 us (2%)
  other arithmetic  1.36 us (1%)
    ppermute x41, starting transfers between devices, swap(): lax.ppermute(value, axis, [(i, i ^ r) for i in range(lax.axis_size(axis))])  46.3 us
    ppermute x41, waiting for transfers between devices, swap(): lax.ppermute(value, axis, [(i, i ^ r) for i in range(lax.axis_size(axis))])  31 us
    pallas_call x7, Pallas kernels, call(): pl.pallas_call(body, in_specs=specs, out_specs=[VMEM_SPEC] * len(outs), o...  14.7 us
    dot_general x8, matrix products, dot(): return jnp.dot(a, b, preferred_element_type=jnp.float32)  5.53 us
    unnamed x59, local copies, waits for them, and re-layouts  2.86 us
  transfers between devices with their start and end apart: 41, of which 16 were waited for; matrix products, arithmetic and copies ran while one was open for 7% of the time, Pallas kernels for 10%

profile of v12, /device:TPU:0, one launch (start us, length us, event | category | flops | bytes accessed | tf_op | source)
XLA Modules:
  0.0 104.3 jit_solution(1963288695478954426)
XLA Ops:
  0.7 0.8 copy-done.4
  1.5 0.7 copy-done.5
  2.3 2.9 %collective-permute-start = (bf16[16,128]{1,0:T(8,128)(2,1)S(1)}, bf16[16,128]{1,0:T(8,128)(2,1)S(1)}, u32[]{:S(2)}, u32[]{:S(2)}) collective-permute-start(bf16[16,128]{1,0:T(8,128)(2,1)S(1)} %shard_map.140), channel_id=1, source_target_pairs={{0,8},{4,12},{8,0},{12,4},{16,24},{20,28},{24,16},{28,20},{1,9},{5... | collective-permute-start | bytes 12296 | tf_op jit(solution)/shard_map/ppermute | solution.py:19
  5.3 1.5 %collective-permute-start.1 = (bf16[16,128]{1,0:T(8,128)(2,1)S(1)}, bf16[16,128]{1,0:T(8,128)(2,1)S(1)}, u32[]{:S(2)}, u32[]{:S(2)}) collective-permute-start(bf16[16,128]{1,0:T(8,128)(2,1)S(1)} %shard_map.140), channel_id=1, source_target_pairs={{0,16},{4,20},{8,24},{12,28},{16,0},{20,4},{24,8},{28,12},{1,17},{... | collective-permute-start | bytes 12296 | tf_op jit(solution)/shard_map/ppermute | solution.py:19
  6.9 2.0 %collective-permute-start.3 = (bf16[64,2304]{1,0:T(8,128)(2,1)}, bf16[64,2304]{1,0:T(8,128)(2,1)S(1)}, u32[]{:S(2)}, u32[]{:S(2)}) collective-permute-start(bf16[64,2304]{1,0:T(8,128)(2,1)} %refs_0_), channel_id=1, source_target_pairs={{0,8},{4,12},{8,0},{12,4},{16,24},{20,28},{24,16},{28,20},{1,9},{5... | collective-permute-start | bytes 884744 | tf_op jit(solution)/shard_map/ppermute | solution.py:19
  8.9 1.5 %collective-permute-start.4 = (bf16[64,2304]{1,0:T(8,128)(2,1)}, bf16[64,2304]{1,0:T(8,128)(2,1)S(1)}, u32[]{:S(2)}, u32[]{:S(2)}) collective-permute-start(bf16[64,2304]{1,0:T(8,128)(2,1)} %refs_0_), channel_id=1, source_target_pairs={{0,16},{4,20},{8,24},{12,28},{16,0},{20,4},{24,8},{28,12},{1,17},{... | collective-permute-start | bytes 884744 | tf_op jit(solution)/shard_map/ppermute | solution.py:19
  10.4 0.9 collective-permute-done.2
  11.4 1.6 %collective-permute-start.10 = (bf16[64,128]{1,0:T(8,128)(2,1)S(1)}, bf16[64,128]{1,0:T(8,128)(2,1)S(1)}, u32[]{:S(2)}, u32[]{:S(2)}) collective-permute-start(bf16[64,128]{1,0:T(8,128)(2,1)S(1)} %pad_maximum_fusion.3), channel_id=1, source_target_pairs={{0,1},{1,0},{2,3},{3,2},{4,5},{5,4},{6,7},{7,6},{8,9},{9,8},{10,11... | collective-permute-start | bytes 49160 | tf_op jit(solution)/shard_map/ppermute | solution.py:19
  13.0 1.0 copy-done.6
  13.9 3.9 %shard_map.141 = (bf16[64,2304]{1,0:T(8,128)(2,1)S(1)}, bf16[1,2304,1024]{2,1,0:T(8,128)(2,1)S(1)}, bf16[1,2304,1024]{2,1,0:T(8,128)(2,1)S(1)}) custom-call(bf16[64,2304]{1,0:T(8,128)(2,1)S(1)} %copy-done.6, bf16[1,2304,1024]{2,1,0:T(8,128)(2,1)} %refs_1_.1, bf16[1,2304,1024]{2,1,0:T(8,128)(2,1)} %refs_2_.1), custom_call_target="tpu_custom_call" | custom-call | flops 2676326400 | bytes 19464192 | tf_op jit(solution)/shard_map/pallas_call | solution.py:49
  17.9 2.7 %collective-permute-start.11 = (bf16[128,128]{1,0:T(8,128)(2,1)S(1)}, bf16[128,128]{1,0:T(8,128)(2,1)S(1)}, u32[]{:S(2)}, u32[]{:S(2)}) collective-permute-start(bf16[128,128]{1,0:T(8,128)(2,1)S(1)} %pad_maximum_fusion.2), channel_id=1, source_target_pairs={{0,2},{1,3},{2,0},{3,1},{4,6},{5,7},{6,4},{7,5},{8,10},{9,11},{10,... | collective-permute-start | bytes 98312 | tf_op jit(solution)/shard_map/ppermute | solution.py:19
  20.5 2.5 %collective-permute-done.4.refs_2_ = bf16[64,2304]{1,0:T(8,128)(2,1)S(1)} collective-permute-done((bf16[64,2304]{1,0:T(8,128)(2,1)}, bf16[64,2304]{1,0:T(8,128)(2,1)S(1)}, u32[]{:S(2)}, u32[]{:S(2)}) %collective-permute-start.4) | collective-permute-done | bytes 294944 | tf_op jit(solution)/shard_map/ppermute | solution.py:19
  23.6 2.7 %shard_map.142.hidden = bf16[256,1024]{1,0:T(8,128)(2,1)S(1)} custom-call(bf16[64,2304]{1,0:T(8,128)(2,1)S(1)} %get-tuple-element.30.refs_0_, bf16[64,2304]{1,0:T(8,128)(2,1)S(1)} %collective-permute-done.3.refs_1_, bf16[64,2304]{1,0:T(8,128)(2,1)S(1)} %collective-permute-done.4.refs_2_, bf16[64,2304]{1,0:T(8,128)(2,1)S(1)} %collective-permute-done.5.refs_3_, ...), custom_call_target="tpu_custom_call" | custom-call | flops 2415919104 | bytes 9437184 | tf_op jit(solution)/shard_map/pallas_call | solution.py:49
  26.4 1.9 %shard_map.144 = bf16[256,2304]{1,0:T(8,128)(2,1)S(1)} custom-call(s32[3]{0:T(128)S(1)} %pad_add_fusion.scalars, bf16[256,1024]{1,0:T(8,128)(2,1)S(1)} %shard_map.142.hidden, bf16[1,1024,2304]{2,1,0:T(8,128)(2,1)S(1)} %bitcast.58, bf16[256,128]{1,0:T(8,128)(2,1)S(1)} %constant_dynamic-update-slice_fusion.table), custom_call_target="tpu_custom_call" | custom-call | flops 1207959552 | bytes 4718592 | tf_op jit(solution)/shard_map/pallas_call | solution.py:49
  28.9 2.7 %shard_map.143.hidden = bf16[256,1024]{1,0:T(8,128)(2,1)S(1)} custom-call(bf16[64,2304]{1,0:T(8,128)(2,1)S(1)} %collective-permute-done.6.refs_0_.x, bf16[64,2304]{1,0:T(8,128)(2,1)S(1)} %collective-permute-done.7.refs_1_, bf16[64,2304]{1,0:T(8,128)(2,1)S(1)} %collective-permute-done.8.refs_2_, bf16[64,2304]{1,0:T(8,128)(2,1)S(1)} %collective-permute-done.9.refs_3_, ...), custom_call_target="tpu_custom_call" | custom-call | flops 2415919104 | bytes 9437184 | tf_op jit(solution)/shard_map/pallas_call | solution.py:49
  31.6 2.0 %shard_map.145 = (bf16[32,2304]{1,0:T(8,128)(2,1)S(1)}, bf16[32,2304]{1,0:T(8,128)(2,1)S(1)}, bf16[32,2304]{1,0:T(8,128)(2,1)S(1)}, bf16[32,2304]{1,0:T(8,128)(2...) custom-call(s32[3]{0:T(128)S(1)} %pad_add_fusion.scalars, ...), custom_call_target="tpu_custom_call" | custom-call | flops 1207959552 | bytes 4718592 | tf_op jit(solution)/shard_map/pallas_call | solution.py:49
  33.6 1.5 %collective-permute-start.17 = (bf16[32,2304]{1,0:T(8,128)(2,1)S(1)}, bf16[32,2304]{1,0:T(8,128)(2,1)S(1)}, u32[]{:S(2)}, u32[]{:S(2)}) collective-permute-start(bf16[32,2304]{1,0:T(8,128)(2,1)S(1)} %get-tuple-element.44), channel_id=1, source_target_pairs={{0,24},{4,28},{8,16},{12,20},{16,8},{20,12},{24,0},{28,4},{1,25},{... | collective-permute-start | bytes 442376 | tf_op jit(solution)/shard_map/ppermute | solution.py:19
  35.1 1.5 %collective-permute-start.18 = (bf16[32,2304]{1,0:T(8,128)(2,1)S(1)}, bf16[32,2304]{1,0:T(8,128)(2,1)S(1)}, u32[]{:S(2)}, u32[]{:S(2)}) collective-permute-start(bf16[32,2304]{1,0:T(8,128)(2,1)S(1)} %get-tuple-element.48), channel_id=1, source_target_pairs={{0,8},{4,12},{8,0},{12,4},{16,24},{20,28},{24,16},{28,20},{1,9},{5... | collective-permute-start | bytes 442376 | tf_op jit(solution)/shard_map/ppermute | solution.py:19
  37.2 0.8 collective-permute-start.14
  38.0 1.2 %collective-permute-start.15 = (bf16[32,2304]{1,0:T(8,128)(2,1)S(1)}, bf16[32,2304]{1,0:T(8,128)(2,1)S(1)}, u32[]{:S(2)}, u32[]{:S(2)}) collective-permute-start(bf16[32,2304]{1,0:T(8,128)(2,1)S(1)} %get-tuple-element.42), channel_id=1, source_target_pairs={{0,16},{4,20},{8,24},{12,28},{16,0},{20,4},{24,8},{28,12},{1,17},{... | collective-permute-start | bytes 442376 | tf_op jit(solution)/shard_map/ppermute | solution.py:19
  39.2 2.1 %collective-permute-done.17 = bf16[32,2304]{1,0:T(8,128)(2,1)S(1)} collective-permute-done((bf16[32,2304]{1,0:T(8,128)(2,1)S(1)}, bf16[32,2304]{1,0:T(8,128)(2,1)S(1)}, u32[]{:S(2)}, u32[]{:S(2)}) %collective-permute-start.17) | collective-permute-done | bytes 147488 | tf_op jit(solution)/shard_map/ppermute | solution.py:19
  41.3 1.4 %collective-permute-start.16 = (bf16[32,2304]{1,0:T(8,128)(2,1)S(1)}, bf16[32,2304]{1,0:T(8,128)(2,1)S(1)}, u32[]{:S(2)}, u32[]{:S(2)}) collective-permute-start(bf16[32,2304]{1,0:T(8,128)(2,1)S(1)} %get-tuple-element.43), channel_id=1, source_target_pairs={{0,24},{4,28},{8,16},{12,20},{16,8},{20,12},{24,0},{28,4},{1,25},{... | collective-permute-start | bytes 442376 | tf_op jit(solution)/shard_map/ppermute | solution.py:19
  42.7 1.4 %shard_map.146 = (f32[32,2304]{1,0:T(8,128)S(1)}, f32[32,2304]{1,0:T(8,128)S(1)}) custom-call(s32[3]{0:T(128)S(1)} %pad_add_fusion.scalars, bf16[64,2304]{1,0:T(8,128)(2,1)S(1)} %collective-permute-done.6.refs_0_.x, bf16[2304,256]{1,0:T(8,128)(2,1)S(1)} %copy-done.1, bf16[2304,256]{1,0:T(8,128)(2,1)S(1)} %copy-done.2, bf16[256,2304]{1,0:T(8,128)(2,1)S(1)} %copy-done.3), custom_call_target="tpu_custom_call" | custom-call | flops 226492416 | bytes 3538944 | tf_op jit(solution)/shard_map/pallas_call | solution.py:49
  44.6 1.7 %collective-permute-start.20 = (bf16[32,2304]{1,0:T(8,128)(2,1)S(1)}, bf16[32,2304]{1,0:T(8,128)(2,1)S(1)}, u32[]{:S(2)}, u32[]{:S(2)}) collective-permute-start(bf16[32,2304]{1,0:T(8,128)(2,1)S(1)} %add_convert_fusion.5), channel_id=1, source_target_pairs={{0,1},{1,0},{2,3},{3,2},{4,5},{5,4},{6,7},{7,6},{8,9},{9,8},{10,11... | collective-permute-start | bytes 442376 | tf_op jit(solution)/shard_map/ppermute | solution.py:19
  46.2 1.4 %collective-permute-done.14 = bf16[32,2304]{1,0:T(8,128)(2,1)S(1)} collective-permute-done((bf16[32,2304]{1,0:T(8,128)(2,1)S(1)}, bf16[32,2304]{1,0:T(8,128)(2,1)S(1)}, u32[]{:S(2)}, u32[]{:S(2)}) %collective-permute-start.14) | collective-permute-done | bytes 147488 | tf_op jit(solution)/shard_map/ppermute | solution.py:19
  47.6 2.3 %collective-permute-done.16 = bf16[32,2304]{1,0:T(8,128)(2,1)S(1)} collective-permute-done((bf16[32,2304]{1,0:T(8,128)(2,1)S(1)}, bf16[32,2304]{1,0:T(8,128)(2,1)S(1)}, u32[]{:S(2)}, u32[]{:S(2)}) %collective-permute-start.16) | collective-permute-done | bytes 147488 | tf_op jit(solution)/shard_map/ppermute | solution.py:19
  50.0 2.7 %collective-permute-start.21 = (bf16[2,16,2304]{2,1,0:T(8,128)(2,1)S(1)}, bf16[2,16,2304]{2,1,0:T(8,128)(2,1)S(1)}, u32[]{:S(2)}, u32[]{:S(2)}) collective-permute-start(bf16[2,16,2304]{2,1,0:T(8,128)(2,1)S(1)} %bitcast.108), channel_id=1, source_target_pairs={{0,2},{1,3},{2,0},{3,1},{4,6},{5,7},{6,4},{7,5},{8,10},{9,11},{10,... | collective-permute-start | bytes 442376 | tf_op jit(solution)/shard_map/ppermute | solution.py:19
  52.7 6.5 %collective-permute-done.21 = bf16[2,16,2304]{2,1,0:T(8,128)(2,1)S(1)} collective-permute-done((bf16[2,16,2304]{2,1,0:T(8,128)(2,1)S(1)}, bf16[2,16,2304]{2,1,0:T(8,128)(2,1)S(1)}, u32[]{:S(2)}, u32[]{:S(2)}) %collective-permute-start.21) | collective-permute-done | bytes 147488 | tf_op jit(solution)/shard_map/ppermute | solution.py:19
  59.2 0.7 collective-permute-start.22
  59.9 1.6 %collective-permute-start.27 = (bf16[32,2304]{1,0:T(8,128)(2,1)S(1)}, bf16[32,2304]{1,0:T(8,128)(2,1)S(1)}, u32[]{:S(2)}, u32[]{:S(2)}) collective-permute-start(bf16[32,2304]{1,0:T(8,128)(2,1)S(1)} %bitcast.104), channel_id=1, source_target_pairs={{0,8},{4,12},{8,0},{12,4},{16,24},{20,28},{24,16},{28,20},{1,9},{5... | collective-permute-start | bytes 442376 | tf_op jit(solution)/shard_map/ppermute | solution.py:19
  62.0 2.4 %collective-permute-done.22 = bf16[32,2304]{1,0:T(8,128)(2,1)S(1)} collective-permute-done((bf16[32,2304]{1,0:T(8,128)(2,1)S(1)}, bf16[32,2304]{1,0:T(8,128)(2,1)S(1)}, u32[]{:S(2)}, u32[]{:S(2)}) %collective-permute-start.22) | collective-permute-done | bytes 147488 | tf_op jit(solution)/shard_map/ppermute | solution.py:19
  64.4 1.4 %collective-permute-start.29 = (bf16[32,2304]{1,0:T(8,128)(2,1)S(1)}, bf16[32,2304]{1,0:T(8,128)(2,1)S(1)}, u32[]{:S(2)}, u32[]{:S(2)}) collective-permute-start(bf16[32,2304]{1,0:T(8,128)(2,1)S(1)} %bitcast.106), channel_id=1, source_target_pairs={{0,24},{4,28},{8,16},{12,20},{16,8},{20,12},{24,0},{28,4},{1,25},{... | collective-permute-start | bytes 442376 | tf_op jit(solution)/shard_map/ppermute | solution.py:19
  65.9 1.5 %collective-permute-start.25 = (bf16[32,2304]{1,0:T(8,128)(2,1)S(1)}, bf16[32,2304]{1,0:T(8,128)(2,1)S(1)}, u32[]{:S(2)}, u32[]{:S(2)}) collective-permute-start(bf16[32,2304]{1,0:T(8,128)(2,1)S(1)} %collective-permute-done.22), channel_id=1, source_target_pairs={{0,24},{4,28},{8,16},{12,20},{16,8},{20,12},{24,0},{28,4},{1,25},{... | collective-permute-start | bytes 442376 | tf_op jit(solution)/shard_map/ppermute | solution.py:19
  67.3 1.6 %collective-permute-start.23 = (bf16[32,2304]{1,0:T(8,128)(2,1)S(1)}, bf16[32,2304]{1,0:T(8,128)(2,1)S(1)}, u32[]{:S(2)}, u32[]{:S(2)}) collective-permute-start(bf16[32,2304]{1,0:T(8,128)(2,1)S(1)} %collective-permute-done.22), channel_id=1, source_target_pairs={{0,8},{4,12},{8,0},{12,4},{16,24},{20,28},{24,16},{28,20},{1,9},{5... | collective-permute-start | bytes 442376 | tf_op jit(solution)/shard_map/ppermute | solution.py:19
  69.4 1.9 %collective-permute-done.28 = bf16[32,2304]{1,0:T(8,128)(2,1)S(1)} collective-permute-done((bf16[32,2304]{1,0:T(8,128)(2,1)S(1)}, bf16[32,2304]{1,0:T(8,128)(2,1)S(1)}, u32[]{:S(2)}, u32[]{:S(2)}) %collective-permute-start.28) | collective-permute-done | bytes 147488 | tf_op jit(solution)/shard_map/ppermute | solution.py:19
  71.3 0.8 collective-permute-done.29
  72.3 2.1 %fusion.4 = bf16[128,512]{1,0:T(8,128)(2,1)S(1)} fusion(bf16[128,2304]{1,0:T(8,128)(2,1)S(1)} %bitcast.64, bf16[2304,512]{1,0:T(8,128)(2,1)} %param.22, f32[512]{0:T(512)S(1)} %copy-done.8), kind=kOutput, calls=%fused_computation.12 | convolution fusion | flops 302186496 | bytes 3082240 | tf_op jit(solution)/shard_map/dot_general | solution.py:23
  75.5 0.7 collective-permute-done.24
  78.9 1.4 %collective-permute-start.33 = (bf16[32,2304]{1,0:T(8,128)(2,1)S(1)}, bf16[32,2304]{1,0:T(8,128)(2,1)S(1)}, u32[]{:S(2)}, u32[]{:S(2)}) collective-permute-start(bf16[32,2304]{1,0:T(8,128)(2,1)S(1)} %get-tuple-element.57), channel_id=1, source_target_pairs={{0,8},{4,12},{8,0},{12,4},{16,24},{20,28},{24,16},{28,20},{1,9},{5... | collective-permute-start | bytes 442376 | tf_op jit(solution)/shard_map/ppermute | solution.py:19
  80.9 1.6 %collective-permute-start.38 = (bf16[32,2304]{1,0:T(8,128)(2,1)S(1)}, bf16[32,2304]{1,0:T(8,128)(2,1)S(1)}, u32[]{:S(2)}, u32[]{:S(2)}) collective-permute-start(bf16[32,2304]{1,0:T(8,128)(2,1)S(1)} %get-tuple-element.58), channel_id=1, source_target_pairs={{0,24},{4,28},{8,16},{12,20},{16,8},{20,12},{24,0},{28,4},{1,25},{... | collective-permute-start | bytes 442376 | tf_op jit(solution)/shard_map/ppermute | solution.py:19
  83.6 2.1 %collective-permute-done.33 = bf16[32,2304]{1,0:T(8,128)(2,1)S(1)} collective-permute-done((bf16[32,2304]{1,0:T(8,128)(2,1)S(1)}, bf16[32,2304]{1,0:T(8,128)(2,1)S(1)}, u32[]{:S(2)}, u32[]{:S(2)}) %collective-permute-start.33) | collective-permute-done | bytes 147488 | tf_op jit(solution)/shard_map/ppermute | solution.py:19
  87.4 1.4 %collective-permute-start.34 = (bf16[32,2304]{1,0:T(8,128)(2,1)S(1)}, bf16[32,2304]{1,0:T(8,128)(2,1)S(1)}, u32[]{:S(2)}, u32[]{:S(2)}) collective-permute-start(bf16[32,2304]{1,0:T(8,128)(2,1)S(1)} %get-tuple-element.54), channel_id=1, source_target_pairs={{0,8},{4,12},{8,0},{12,4},{16,24},{20,28},{24,16},{28,20},{1,9},{5... | collective-permute-start | bytes 442376 | tf_op jit(solution)/shard_map/ppermute | solution.py:19
  89.4 1.6 %collective-permute-start.36 = (bf16[32,2304]{1,0:T(8,128)(2,1)S(1)}, bf16[32,2304]{1,0:T(8,128)(2,1)S(1)}, u32[]{:S(2)}, u32[]{:S(2)}) collective-permute-start(bf16[32,2304]{1,0:T(8,128)(2,1)S(1)} %get-tuple-element.55), channel_id=1, source_target_pairs={{0,24},{4,28},{8,16},{12,20},{16,8},{20,12},{24,0},{28,4},{1,25},{... | collective-permute-start | bytes 442376 | tf_op jit(solution)/shard_map/ppermute | solution.py:19
  91.0 1.5 %collective-permute-start.39 = (bf16[32,2304]{1,0:T(8,128)(2,1)S(1)}, bf16[32,2304]{1,0:T(8,128)(2,1)S(1)}, u32[]{:S(2)}, u32[]{:S(2)}) collective-permute-start(bf16[32,2304]{1,0:T(8,128)(2,1)S(1)} %add_convert_fusion.2), channel_id=1, source_target_pairs={{0,1},{1,0},{2,3},{3,2},{4,5},{5,4},{6,7},{7,6},{8,9},{9,8},{10,11... | collective-permute-start | bytes 442376 | tf_op jit(solution)/shard_map/ppermute | solution.py:19
  92.5 1.2 %collective-permute-done.34 = bf16[32,2304]{1,0:T(8,128)(2,1)S(1)} collective-permute-done((bf16[32,2304]{1,0:T(8,128)(2,1)S(1)}, bf16[32,2304]{1,0:T(8,128)(2,1)S(1)}, u32[]{:S(2)}, u32[]{:S(2)}) %collective-permute-start.34) | collective-permute-done | bytes 147488 | tf_op jit(solution)/shard_map/ppermute | solution.py:19
  93.7 2.0 %collective-permute-done.35 = bf16[32,2304]{1,0:T(8,128)(2,1)S(1)} collective-permute-done((bf16[32,2304]{1,0:T(8,128)(2,1)S(1)}, bf16[32,2304]{1,0:T(8,128)(2,1)S(1)}, u32[]{:S(2)}, u32[]{:S(2)}) %collective-permute-start.35) | collective-permute-done | bytes 147488 | tf_op jit(solution)/shard_map/ppermute | solution.py:19
  96.4 4.1 %collective-permute-start.40 = (bf16[16,2304]{1,0:T(8,128)(2,1)S(1)}, bf16[16,2304]{1,0:T(8,128)(2,1)S(1)}, u32[]{:S(2)}, u32[]{:S(2)}) collective-permute-start(bf16[16,2304]{1,0:T(8,128)(2,1)S(1)} %fusion.9), channel_id=1, source_target_pairs={{0,2},{1,3},{2,0},{3,1},{4,6},{5,7},{6,4},{7,5},{8,10},{9,11},{10,... | collective-permute-start | bytes 221192 | tf_op jit(solution)/shard_map/ppermute | solution.py:19
  100.5 3.1 %collective-permute-done.40 = bf16[16,2304]{1,0:T(8,128)(2,1)S(1)} collective-permute-done((bf16[16,2304]{1,0:T(8,128)(2,1)S(1)}, bf16[16,2304]{1,0:T(8,128)(2,1)S(1)}, u32[]{:S(2)}, u32[]{:S(2)}) %collective-permute-start.40) | collective-permute-done | bytes 73760 | tf_op jit(solution)/shard_map/ppermute | solution.py:19
  (127 shorter events, 11.7 us)
Async XLA Ops:
  0.6 73.8 %copy-start = (bf16[512,2304]{1,0:T(8,128)(2,1)S(1)}, bf16[512,2304]{1,0:T(8,128)(2,1)}, u32[]{:S(2)}) copy-start(bf16[512,2304]{1,0:T(8,128)(2,1)} %param.24) | copy-start | bytes 7077892
  2.3 4.5 %collective-permute-start = (bf16[16,128]{1,0:T(8,128)(2,1)S(1)}, bf16[16,128]{1,0:T(8,128)(2,1)S(1)}, u32[]{:S(2)}, u32[]{:S(2)}) collective-permute-start(bf16[16,128]{1,0:T(8,128)(2,1)S(1)} %shard_map.140), channel_id=1, source_target_pairs={{0,8},{4,12},{8,0},{12,4},{16,24},{20,28},{24,16},{28,20},{1,9},{5... | collective-permute-start | bytes 12296 | tf_op jit(solution)/shard_map/ppermute | solution.py:19
  5.3 5.1 %collective-permute-start.1 = (bf16[16,128]{1,0:T(8,128)(2,1)S(1)}, bf16[16,128]{1,0:T(8,128)(2,1)S(1)}, u32[]{:S(2)}, u32[]{:S(2)}) collective-permute-start(bf16[16,128]{1,0:T(8,128)(2,1)S(1)} %shard_map.140), channel_id=1, source_target_pairs={{0,16},{4,20},{8,24},{12,28},{16,0},{20,4},{24,8},{28,12},{1,17},{... | collective-permute-start | bytes 12296 | tf_op jit(solution)/shard_map/ppermute | solution.py:19
  6.8 4.6 %collective-permute-start.2 = (bf16[16,128]{1,0:T(8,128)(2,1)S(1)}, bf16[16,128]{1,0:T(8,128)(2,1)S(1)}, u32[]{:S(2)}, u32[]{:S(2)}) collective-permute-start(bf16[16,128]{1,0:T(8,128)(2,1)S(1)} %shard_map.140), channel_id=1, source_target_pairs={{0,24},{4,28},{8,16},{12,20},{16,8},{20,12},{24,0},{28,4},{1,25},{... | collective-permute-start | bytes 12296 | tf_op jit(solution)/shard_map/ppermute | solution.py:19
  6.9 13.6 %collective-permute-start.3 = (bf16[64,2304]{1,0:T(8,128)(2,1)}, bf16[64,2304]{1,0:T(8,128)(2,1)S(1)}, u32[]{:S(2)}, u32[]{:S(2)}) collective-permute-start(bf16[64,2304]{1,0:T(8,128)(2,1)} %refs_0_), channel_id=1, source_target_pairs={{0,8},{4,12},{8,0},{12,4},{16,24},{20,28},{24,16},{28,20},{1,9},{5... | collective-permute-start | bytes 884744 | tf_op jit(solution)/shard_map/ppermute | solution.py:19
  8.9 14.2 %collective-permute-start.4 = (bf16[64,2304]{1,0:T(8,128)(2,1)}, bf16[64,2304]{1,0:T(8,128)(2,1)S(1)}, u32[]{:S(2)}, u32[]{:S(2)}) collective-permute-start(bf16[64,2304]{1,0:T(8,128)(2,1)} %refs_0_), channel_id=1, source_target_pairs={{0,16},{4,20},{8,24},{12,28},{16,0},{20,4},{24,8},{28,12},{1,17},{... | collective-permute-start | bytes 884744 | tf_op jit(solution)/shard_map/ppermute | solution.py:19
  10.4 12.7 %collective-permute-start.5 = (bf16[64,2304]{1,0:T(8,128)(2,1)}, bf16[64,2304]{1,0:T(8,128)(2,1)S(1)}, u32[]{:S(2)}, u32[]{:S(2)}) collective-permute-start(bf16[64,2304]{1,0:T(8,128)(2,1)} %refs_0_), channel_id=1, source_target_pairs={{0,24},{4,28},{8,16},{12,20},{16,8},{20,12},{24,0},{28,4},{1,25},{... | collective-permute-start | bytes 884744 | tf_op jit(solution)/shard_map/ppermute | solution.py:19
  10.4 15.9 %collective-permute-start.6 = (bf16[64,2304]{1,0:T(8,128)(2,1)}, bf16[64,2304]{1,0:T(8,128)(2,1)S(1)}, u32[]{:S(2)}, u32[]{:S(2)}) collective-permute-start(bf16[64,2304]{1,0:T(8,128)(2,1)} %refs_0_), channel_id=1, source_target_pairs={{0,4},{4,0},{8,12},{12,8},{16,20},{20,16},{24,28},{28,24},{1,5},{5... | collective-permute-start | bytes 884744 | tf_op jit(solution)/shard_map/ppermute | solution.py:19
  11.4 6.5 %collective-permute-start.10 = (bf16[64,128]{1,0:T(8,128)(2,1)S(1)}, bf16[64,128]{1,0:T(8,128)(2,1)S(1)}, u32[]{:S(2)}, u32[]{:S(2)}) collective-permute-start(bf16[64,128]{1,0:T(8,128)(2,1)S(1)} %pad_maximum_fusion.3), channel_id=1, source_target_pairs={{0,1},{1,0},{2,3},{3,2},{4,5},{5,4},{6,7},{7,6},{8,9},{9,8},{10,11... | collective-permute-start | bytes 49160 | tf_op jit(solution)/shard_map/ppermute | solution.py:19
  13.9 12.4 %slice-start = ((s8[4718592]{0:T(1024)(128)(4,1)}), s8[524288]{0:T(1024)(128)(4,1)S(1)}, s32[]{:S(2)}) async-start(s8[4718592]{0:T(1024)(128)(4,1)} %bitcast.57), calls=%async_computation | async-start | bytes 1048576
  17.9 5.7 %collective-permute-start.11 = (bf16[128,128]{1,0:T(8,128)(2,1)S(1)}, bf16[128,128]{1,0:T(8,128)(2,1)S(1)}, u32[]{:S(2)}, u32[]{:S(2)}) collective-permute-start(bf16[128,128]{1,0:T(8,128)(2,1)S(1)} %pad_maximum_fusion.2), channel_id=1, source_target_pairs={{0,2},{1,3},{2,0},{3,1},{4,6},{5,7},{6,4},{7,5},{8,10},{9,11},{10,... | collective-permute-start | bytes 98312 | tf_op jit(solution)/shard_map/ppermute | solution.py:19
  20.5 5.8 %collective-permute-start.7 = (bf16[64,2304]{1,0:T(8,128)(2,1)S(1)}, bf16[64,2304]{1,0:T(8,128)(2,1)S(1)}, u32[]{:S(2)}, u32[]{:S(2)}) collective-permute-start(bf16[64,2304]{1,0:T(8,128)(2,1)S(1)} %collective-permute-done.3.refs_1_), channel_id=1, source_target_pairs={{0,4},{4,0},{8,12},{12,8},{16,20},{20,16},{24,28},{28,24},{1,5},{5... | collective-permute-start | bytes 884744 | tf_op jit(solution)/shard_map/ppermute | solution.py:19
  23.1 3.2 %collective-permute-start.8 = (bf16[64,2304]{1,0:T(8,128)(2,1)S(1)}, bf16[64,2304]{1,0:T(8,128)(2,1)S(1)}, u32[]{:S(2)}, u32[]{:S(2)}) collective-permute-start(bf16[64,2304]{1,0:T(8,128)(2,1)S(1)} %collective-permute-done.4.refs_2_), channel_id=1, source_target_pairs={{0,4},{4,0},{8,12},{12,8},{16,20},{20,16},{24,28},{28,24},{1,5},{5... | collective-permute-start | bytes 884744 | tf_op jit(solution)/shard_map/ppermute | solution.py:19
  23.1 3.2 %collective-permute-start.9 = (bf16[64,2304]{1,0:T(8,128)(2,1)S(1)}, bf16[64,2304]{1,0:T(8,128)(2,1)S(1)}, u32[]{:S(2)}, u32[]{:S(2)}) collective-permute-start(bf16[64,2304]{1,0:T(8,128)(2,1)S(1)} %collective-permute-done.5.refs_3_), channel_id=1, source_target_pairs={{0,4},{4,0},{8,12},{12,8},{16,20},{20,16},{24,28},{28,24},{1,5},{5... | collective-permute-start | bytes 884744 | tf_op jit(solution)/shard_map/ppermute | solution.py:19
  28.3 3.3 %collective-permute-start.13 = (bf16[256,2304]{1,0:T(8,128)(2,1)S(1)}, bf16[256,2304]{1,0:T(8,128)(2,1)S(1)}, u32[]{:S(2)}, u32[]{:S(2)}) collective-permute-start(bf16[256,2304]{1,0:T(8,128)(2,1)S(1)} %shard_map.144), channel_id=1, source_target_pairs={{0,4},{4,0},{8,12},{12,8},{16,20},{20,16},{24,28},{28,24},{1,5},{5... | collective-permute-start | bytes 3538952 | tf_op jit(solution)/shard_map/ppermute | solution.py:19
  28.4 3.2 %collective-permute-start.12 = (bf16[256,128]{1,0:T(8,128)(2,1)S(1)}, bf16[256,128]{1,0:T(8,128)(2,1)S(1)}, u32[]{:S(2)}, u32[]{:S(2)}) collective-permute-start(bf16[256,128]{1,0:T(8,128)(2,1)S(1)} %constant_dynamic-update-slice_fusion.table), channel_id=1, source_target_pairs={{0,4},{4,0},{8,12},{12,8},{16,20},{20,16},{24,28},{28,24},{1,5},{5... | collective-permute-start | bytes 196616 | tf_op jit(solution)/shard_map/ppermute | solution.py:19
  31.5 11.2 %copy-start.1 = (bf16[2304,256]{1,0:T(8,128)(2,1)S(1)}, bf16[2304,256]{1,0:T(8,128)(2,1)}, u32[]{:S(2)}) copy-start(bf16[2304,256]{1,0:T(8,128)(2,1)} %gate.1) | copy-start | bytes 3538948
  31.6 11.2 %copy-start.2 = (bf16[2304,256]{1,0:T(8,128)(2,1)S(1)}, bf16[2304,256]{1,0:T(8,128)(2,1)}, u32[]{:S(2)}) copy-start(bf16[2304,256]{1,0:T(8,128)(2,1)} %up.1) | copy-start | bytes 3538948
  31.6 11.2 %copy-start.3 = (bf16[256,2304]{1,0:T(8,128)(2,1)S(1)}, bf16[256,2304]{1,0:T(8,128)(2,1)}, u32[]{:S(2)}) copy-start(bf16[256,2304]{1,0:T(8,128)(2,1)} %down.5) | copy-start | bytes 3538948
  33.6 7.7 %collective-permute-start.17 = (bf16[32,2304]{1,0:T(8,128)(2,1)S(1)}, bf16[32,2304]{1,0:T(8,128)(2,1)S(1)}, u32[]{:S(2)}, u32[]{:S(2)}) collective-permute-start(bf16[32,2304]{1,0:T(8,128)(2,1)S(1)} %get-tuple-element.44), channel_id=1, source_target_pairs={{0,24},{4,28},{8,16},{12,20},{16,8},{20,12},{24,0},{28,4},{1,25},{... | collective-permute-start | bytes 442376 | tf_op jit(solution)/shard_map/ppermute | solution.py:19
  35.1 9.4 %collective-permute-start.18 = (bf16[32,2304]{1,0:T(8,128)(2,1)S(1)}, bf16[32,2304]{1,0:T(8,128)(2,1)S(1)}, u32[]{:S(2)}, u32[]{:S(2)}) collective-permute-start(bf16[32,2304]{1,0:T(8,128)(2,1)S(1)} %get-tuple-element.48), channel_id=1, source_target_pairs={{0,8},{4,12},{8,0},{12,4},{16,24},{20,28},{24,16},{28,20},{1,9},{5... | collective-permute-start | bytes 442376 | tf_op jit(solution)/shard_map/ppermute | solution.py:19
  36.6 7.9 %collective-permute-start.19 = (bf16[32,2304]{1,0:T(8,128)(2,1)S(1)}, bf16[32,2304]{1,0:T(8,128)(2,1)S(1)}, u32[]{:S(2)}, u32[]{:S(2)}) collective-permute-start(bf16[32,2304]{1,0:T(8,128)(2,1)S(1)} %get-tuple-element.49), channel_id=1, source_target_pairs={{0,16},{4,20},{8,24},{12,28},{16,0},{20,4},{24,8},{28,12},{1,17},{... | collective-permute-start | bytes 442376 | tf_op jit(solution)/shard_map/ppermute | solution.py:19
  37.2 10.5 %collective-permute-start.14 = (bf16[32,2304]{1,0:T(8,128)(2,1)S(1)}, bf16[32,2304]{1,0:T(8,128)(2,1)S(1)}, u32[]{:S(2)}, u32[]{:S(2)}) collective-permute-start(bf16[32,2304]{1,0:T(8,128)(2,1)S(1)} %get-tuple-element.41), channel_id=1, source_target_pairs={{0,8},{4,12},{8,0},{12,4},{16,24},{20,28},{24,16},{28,20},{1,9},{5... | collective-permute-start | bytes 442376 | tf_op jit(solution)/shard_map/ppermute | solution.py:19
  38.0 9.6 %collective-permute-start.15 = (bf16[32,2304]{1,0:T(8,128)(2,1)S(1)}, bf16[32,2304]{1,0:T(8,128)(2,1)S(1)}, u32[]{:S(2)}, u32[]{:S(2)}) collective-permute-start(bf16[32,2304]{1,0:T(8,128)(2,1)S(1)} %get-tuple-element.42), channel_id=1, source_target_pairs={{0,16},{4,20},{8,24},{12,28},{16,0},{20,4},{24,8},{28,12},{1,17},{... | collective-permute-start | bytes 442376 | tf_op jit(solution)/shard_map/ppermute | solution.py:19
  41.3 8.6 %collective-permute-start.16 = (bf16[32,2304]{1,0:T(8,128)(2,1)S(1)}, bf16[32,2304]{1,0:T(8,128)(2,1)S(1)}, u32[]{:S(2)}, u32[]{:S(2)}) collective-permute-start(bf16[32,2304]{1,0:T(8,128)(2,1)S(1)} %get-tuple-element.43), channel_id=1, source_target_pairs={{0,24},{4,28},{8,16},{12,20},{16,8},{20,12},{24,0},{28,4},{1,25},{... | collective-permute-start | bytes 442376 | tf_op jit(solution)/shard_map/ppermute | solution.py:19
  44.1 28.1 %copy-start.8 = (f32[512]{0:T(512)S(1)}, f32[512]{0:T(512)}, u32[]{:S(2)}) copy-start(f32[512]{0:T(512)} %param.23) | copy-start | bytes 6148
  44.6 5.3 %collective-permute-start.20 = (bf16[32,2304]{1,0:T(8,128)(2,1)S(1)}, bf16[32,2304]{1,0:T(8,128)(2,1)S(1)}, u32[]{:S(2)}, u32[]{:S(2)}) collective-permute-start(bf16[32,2304]{1,0:T(8,128)(2,1)S(1)} %add_convert_fusion.5), channel_id=1, source_target_pairs={{0,1},{1,0},{2,3},{3,2},{4,5},{5,4},{6,7},{7,6},{8,9},{9,8},{10,11... | collective-permute-start | bytes 442376 | tf_op jit(solution)/shard_map/ppermute | solution.py:19
  50.0 9.1 %collective-permute-start.21 = (bf16[2,16,2304]{2,1,0:T(8,128)(2,1)S(1)}, bf16[2,16,2304]{2,1,0:T(8,128)(2,1)S(1)}, u32[]{:S(2)}, u32[]{:S(2)}) collective-permute-start(bf16[2,16,2304]{2,1,0:T(8,128)(2,1)S(1)} %bitcast.108), channel_id=1, source_target_pairs={{0,2},{1,3},{2,0},{3,1},{4,6},{5,7},{6,4},{7,5},{8,10},{9,11},{10,... | collective-permute-start | bytes 442376 | tf_op jit(solution)/shard_map/ppermute | solution.py:19
  59.2 5.2 %collective-permute-start.22 = (bf16[32,2304]{1,0:T(8,128)(2,1)S(1)}, bf16[32,2304]{1,0:T(8,128)(2,1)S(1)}, u32[]{:S(2)}, u32[]{:S(2)}) collective-permute-start(bf16[32,2304]{1,0:T(8,128)(2,1)S(1)} %bitcast.103), channel_id=1, source_target_pairs={{0,1},{1,0},{2,3},{3,2},{4,5},{5,4},{6,7},{7,6},{8,9},{9,8},{10,11... | collective-permute-start | bytes 442376 | tf_op jit(solution)/shard_map/ppermute | solution.py:19
  59.9 9.0 %collective-permute-start.27 = (bf16[32,2304]{1,0:T(8,128)(2,1)S(1)}, bf16[32,2304]{1,0:T(8,128)(2,1)S(1)}, u32[]{:S(2)}, u32[]{:S(2)}) collective-permute-start(bf16[32,2304]{1,0:T(8,128)(2,1)S(1)} %bitcast.104), channel_id=1, source_target_pairs={{0,8},{4,12},{8,0},{12,4},{16,24},{20,28},{24,16},{28,20},{1,9},{5... | collective-permute-start | bytes 442376 | tf_op jit(solution)/shard_map/ppermute | solution.py:19
  61.5 9.8 %collective-permute-start.28 = (bf16[32,2304]{1,0:T(8,128)(2,1)S(1)}, bf16[32,2304]{1,0:T(8,128)(2,1)S(1)}, u32[]{:S(2)}, u32[]{:S(2)}) collective-permute-start(bf16[32,2304]{1,0:T(8,128)(2,1)S(1)} %bitcast.105), channel_id=1, source_target_pairs={{0,16},{4,20},{8,24},{12,28},{16,0},{20,4},{24,8},{28,12},{1,17},{... | collective-permute-start | bytes 442376 | tf_op jit(solution)/shard_map/ppermute | solution.py:19
  64.4 7.7 %collective-permute-start.29 = (bf16[32,2304]{1,0:T(8,128)(2,1)S(1)}, bf16[32,2304]{1,0:T(8,128)(2,1)S(1)}, u32[]{:S(2)}, u32[]{:S(2)}) collective-permute-start(bf16[32,2304]{1,0:T(8,128)(2,1)S(1)} %bitcast.106), channel_id=1, source_target_pairs={{0,24},{4,28},{8,16},{12,20},{16,8},{20,12},{24,0},{28,4},{1,25},{... | collective-permute-start | bytes 442376 | tf_op jit(solution)/shard_map/ppermute | solution.py:19
  65.9 9.6 %collective-permute-start.25 = (bf16[32,2304]{1,0:T(8,128)(2,1)S(1)}, bf16[32,2304]{1,0:T(8,128)(2,1)S(1)}, u32[]{:S(2)}, u32[]{:S(2)}) collective-permute-start(bf16[32,2304]{1,0:T(8,128)(2,1)S(1)} %collective-permute-done.22), channel_id=1, source_target_pairs={{0,24},{4,28},{8,16},{12,20},{16,8},{20,12},{24,0},{28,4},{1,25},{... | collective-permute-start | bytes 442376 | tf_op jit(solution)/shard_map/ppermute | solution.py:19
  67.3 8.2 %collective-permute-start.23 = (bf16[32,2304]{1,0:T(8,128)(2,1)S(1)}, bf16[32,2304]{1,0:T(8,128)(2,1)S(1)}, u32[]{:S(2)}, u32[]{:S(2)}) collective-permute-start(bf16[32,2304]{1,0:T(8,128)(2,1)S(1)} %collective-permute-done.22), channel_id=1, source_target_pairs={{0,8},{4,12},{8,0},{12,4},{16,24},{20,28},{24,16},{28,20},{1,9},{5... | collective-permute-start | bytes 442376 | tf_op jit(solution)/shard_map/ppermute | solution.py:19
  68.9 7.3 %collective-permute-start.24 = (bf16[32,2304]{1,0:T(8,128)(2,1)S(1)}, bf16[32,2304]{1,0:T(8,128)(2,1)S(1)}, u32[]{:S(2)}, u32[]{:S(2)}) collective-permute-start(bf16[32,2304]{1,0:T(8,128)(2,1)S(1)} %collective-permute-done.22), channel_id=1, source_target_pairs={{0,16},{4,20},{8,24},{12,28},{16,0},{20,4},{24,8},{28,12},{1,17},{... | collective-permute-start | bytes 442376 | tf_op jit(solution)/shard_map/ppermute | solution.py:19
  72.2 5.7 %collective-permute-start.30 = (bf16[128,2304]{1,0:T(8,128)(2,1)S(1)}, bf16[128,2304]{1,0:T(8,128)(2,1)S(1)}, u32[]{:S(2)}, u32[]{:S(2)}) collective-permute-start(bf16[128,2304]{1,0:T(8,128)(2,1)S(1)} %bitcast.63), channel_id=1, source_target_pairs={{0,4},{4,0},{8,12},{12,8},{16,20},{20,16},{24,28},{28,24},{1,5},{5... | collective-permute-start | bytes 1769480 | tf_op jit(solution)/shard_map/ppermute | solution.py:19
  74.9 3.5 %collective-permute-start.32 = (bf16[128,2304]{1,0:T(8,128)(2,1)S(1)}, bf16[128,2304]{1,0:T(8,128)(2,1)S(1)}, u32[]{:S(2)}, u32[]{:S(2)}) collective-permute-start(bf16[128,2304]{1,0:T(8,128)(2,1)S(1)} %convolution_convert_fusion), channel_id=1, source_target_pairs={{0,4},{4,0},{8,12},{12,8},{16,20},{20,16},{24,28},{28,24},{1,5},{5... | collective-permute-start | bytes 1769480 | tf_op jit(solution)/shard_map/ppermute | solution.py:19
  76.3 6.2 %collective-permute-start.26 = (bf16[128,2304]{1,0:T(8,128)(2,1)S(1)}, bf16[128,2304]{1,0:T(8,128)(2,1)S(1)}, u32[]{:S(2)}, u32[]{:S(2)}) collective-permute-start(bf16[128,2304]{1,0:T(8,128)(2,1)S(1)} %bitcast.61), channel_id=1, source_target_pairs={{0,4},{4,0},{8,12},{12,8},{16,20},{20,16},{24,28},{28,24},{1,5},{5... | collective-permute-start | bytes 1769480 | tf_op jit(solution)/shard_map/ppermute | solution.py:19
  77.4 9.5 %collective-permute-start.31 = (bf16[128,2304]{1,0:T(8,128)(2,1)S(1)}, bf16[128,2304]{1,0:T(8,128)(2,1)S(1)}, u32[]{:S(2)}, u32[]{:S(2)}) collective-permute-start(bf16[128,2304]{1,0:T(8,128)(2,1)S(1)} %convolution_convert_fusion.1), channel_id=1, source_target_pairs={{0,4},{4,0},{8,12},{12,8},{16,20},{20,16},{24,28},{28,24},{1,5},{5... | collective-permute-start | bytes 1769480 | tf_op jit(solution)/shard_map/ppermute | solution.py:19
  78.9 6.7 %collective-permute-start.33 = (bf16[32,2304]{1,0:T(8,128)(2,1)S(1)}, bf16[32,2304]{1,0:T(8,128)(2,1)S(1)}, u32[]{:S(2)}, u32[]{:S(2)}) collective-permute-start(bf16[32,2304]{1,0:T(8,128)(2,1)S(1)} %get-tuple-element.57), channel_id=1, source_target_pairs={{0,8},{4,12},{8,0},{12,4},{16,24},{20,28},{24,16},{28,20},{1,9},{5... | collective-permute-start | bytes 442376 | tf_op jit(solution)/shard_map/ppermute | solution.py:19
  80.3 10.6 %collective-permute-start.37 = (bf16[32,2304]{1,0:T(8,128)(2,1)S(1)}, bf16[32,2304]{1,0:T(8,128)(2,1)S(1)}, u32[]{:S(2)}, u32[]{:S(2)}) collective-permute-start(bf16[32,2304]{1,0:T(8,128)(2,1)S(1)} %get-tuple-element.59), channel_id=1, source_target_pairs={{0,16},{4,20},{8,24},{12,28},{16,0},{20,4},{24,8},{28,12},{1,17},{... | collective-permute-start | bytes 442376 | tf_op jit(solution)/shard_map/ppermute | solution.py:19
  80.9 10.0 %collective-permute-start.38 = (bf16[32,2304]{1,0:T(8,128)(2,1)S(1)}, bf16[32,2304]{1,0:T(8,128)(2,1)S(1)}, u32[]{:S(2)}, u32[]{:S(2)}) collective-permute-start(bf16[32,2304]{1,0:T(8,128)(2,1)S(1)} %get-tuple-element.58), channel_id=1, source_target_pairs={{0,24},{4,28},{8,16},{12,20},{16,8},{20,12},{24,0},{28,4},{1,25},{... | collective-permute-start | bytes 442376 | tf_op jit(solution)/shard_map/ppermute | solution.py:19
  87.3 16.3 %copy-start.9 = (f32[2304]{0:T(1024)S(1)}, f32[2304]{0:T(1024)}, u32[]{:S(2)}) copy-start(f32[2304]{0:T(1024)} %param.25) | copy-start | bytes 27652
  87.4 6.3 %collective-permute-start.34 = (bf16[32,2304]{1,0:T(8,128)(2,1)S(1)}, bf16[32,2304]{1,0:T(8,128)(2,1)S(1)}, u32[]{:S(2)}, u32[]{:S(2)}) collective-permute-start(bf16[32,2304]{1,0:T(8,128)(2,1)S(1)} %get-tuple-element.54), channel_id=1, source_target_pairs={{0,8},{4,12},{8,0},{12,4},{16,24},{20,28},{24,16},{28,20},{1,9},{5... | collective-permute-start | bytes 442376 | tf_op jit(solution)/shard_map/ppermute | solution.py:19
  88.8 6.9 %collective-permute-start.35 = (bf16[32,2304]{1,0:T(8,128)(2,1)S(1)}, bf16[32,2304]{1,0:T(8,128)(2,1)S(1)}, u32[]{:S(2)}, u32[]{:S(2)}) collective-permute-start(bf16[32,2304]{1,0:T(8,128)(2,1)S(1)} %get-tuple-element.56), channel_id=1, source_target_pairs={{0,16},{4,20},{8,24},{12,28},{16,0},{20,4},{24,8},{28,12},{1,17},{... | collective-permute-start | bytes 442376 | tf_op jit(solution)/shard_map/ppermute | solution.py:19
  89.4 6.3 %collective-permute-start.36 = (bf16[32,2304]{1,0:T(8,128)(2,1)S(1)}, bf16[32,2304]{1,0:T(8,128)(2,1)S(1)}, u32[]{:S(2)}, u32[]{:S(2)}) collective-permute-start(bf16[32,2304]{1,0:T(8,128)(2,1)S(1)} %get-tuple-element.55), channel_id=1, source_target_pairs={{0,24},{4,28},{8,16},{12,20},{16,8},{20,12},{24,0},{28,4},{1,25},{... | collective-permute-start | bytes 442376 | tf_op jit(solution)/shard_map/ppermute | solution.py:19
  91.0 5.2 %collective-permute-start.39 = (bf16[32,2304]{1,0:T(8,128)(2,1)S(1)}, bf16[32,2304]{1,0:T(8,128)(2,1)S(1)}, u32[]{:S(2)}, u32[]{:S(2)}) collective-permute-start(bf16[32,2304]{1,0:T(8,128)(2,1)S(1)} %add_convert_fusion.2), channel_id=1, source_target_pairs={{0,1},{1,0},{2,3},{3,2},{4,5},{5,4},{6,7},{7,6},{8,9},{9,8},{10,11... | collective-permute-start | bytes 442376 | tf_op jit(solution)/shard_map/ppermute | solution.py:19
  96.4 7.2 %collective-permute-start.40 = (bf16[16,2304]{1,0:T(8,128)(2,1)S(1)}, bf16[16,2304]{1,0:T(8,128)(2,1)S(1)}, u32[]{:S(2)}, u32[]{:S(2)}) collective-permute-start(bf16[16,2304]{1,0:T(8,128)(2,1)S(1)} %fusion.9), channel_id=1, source_target_pairs={{0,2},{1,3},{2,0},{3,1},{4,6},{5,7},{6,4},{7,5},{8,10},{9,11},{10,... | collective-permute-start | bytes 221192 | tf_op jit(solution)/shard_map/ppermute | solution.py:19
  (6 other events, 11.0 us)

commit v13 on v12

--- a/solution.py
+++ b/solution.py
@@ -112,7 +112,9 @@
     )
 
 
-def shared_kernel(own, scalars, x, gate, up, down, kept, sent):
+def shared_kernel(own, scalars, x, gate, up, down, extra, kept, sent, extra_out, sem):
+    copy = pltpu.make_async_copy(extra, extra_out, sem)
+    copy.start()
     hidden = half(silu(dot(x[...], gate[...])) * dot(x[...], up[...]))
     rows, width = x.shape
     for j in range(0, width, 256):
@@ -121,16 +123,17 @@
         low, high = [value[:, i].reshape(rows // 2, -1) for i in range(2)]
         kept[:, cut] = jnp.where(scalars[1] == 0, low, high)
         sent[:, cut] = jnp.where(scalars[1] == 0, high, low)
-
-
-def run_shared(scalars, x, weights, own):
+    copy.wait()
+
+
+def run_shared(scalars, x, weights, extra, own):
     rows, width = x.shape
     return call(
         functools.partial(shared_kernel, own),
-        [scalars, x, *weights],
-        [SMEM_SPEC] + [VMEM_SPEC] * 4,
-        [((rows // 2, width), jnp.float32)] * 2,
-        [],
+        [scalars, x, *weights, extra],
+        [SMEM_SPEC] + [VMEM_SPEC] * 4 + [HBM_SPEC],
+        [((rows // 2, width), jnp.float32)] * 2 + [(extra.shape, extra.dtype)],
+        [pltpu.SemaphoreType.DMA],
         6,
         (6 * rows * weights[0].size, 6 * weights[0].size),
     )
@@ -273,7 +276,10 @@
         [mine[0]] + [swap(mine[p], "expert", 2 * p) for p in range(1, pairs)] for mine in blocks
     ]
     scalars, blocks[0][-1] = lax.optimization_barrier((scalars, blocks[0][-1]))
-    shared_out = run_shared(scalars, far[0], [shared_gate, shared_up, shared_down], own)
+    shared_out = run_shared(
+        scalars, far[0], [shared_gate, shared_up, shared_down], encoder, own
+    )
+    encoder = shared_out[2]
     totals = [sum(full(part) for part in blocks[i] + [shared_out[i]]) for i in range(2)]
 
     total = totals[1] + full(swap(half(totals[0]), "feat", feat_bits[0]))

time: 105 us -> 103 us (0.981)
  waiting for transfers between devices: 31 us -> 28.8 us
  local copies, waits for them, and re-layouts: 3.46 us -> 5.19 us
  starting transfers between devices: 46.3 us -> 45 us
    ppermute x41, waiting for transfers between devices: 31 us -> 28.8 us  [swap(): lax.ppermute(value, axis, [(i, i ^ r) for i in range(lax.axis_size(axis))])]
    unnamed x59 -> x63, local copies, waits for them, and re-layouts: 2.86 us -> 4.58 us
    ppermute x41, starting transfers between devices: 46.3 us -> 45 us  [swap(): lax.ppermute(value, axis, [(i, i ^ r) for i in range(lax.axis_size(axis))])]
  transfers between devices with their start and end apart: 41 -> 41, of which waited for: 16 -> 16; matrix products, arithmetic and copies ran while one was open for 7% -> 7% of each run, Pallas kernels for 10% -> 11%
where the time goes in v13:
time: 103 us
  starting transfers between devices  45 us (44%)
  waiting for transfers between devices  28.8 us (28%)
  Pallas kernels  15.1 us (15%)
  matrix products  5.51 us (5%)
  local copies, waits for them, and re-layouts  5.19 us (5%)
  between operations  1.96 us (2%)
  other arithmetic  1.38 us (1%)
    ppermute x41, starting transfers between devices, swap(): lax.ppermute(value, axis, [(i, i ^ r) for i in range(lax.axis_size(axis))])  45 us
    ppermute x41, waiting for transfers between devices, swap(): lax.ppermute(value, axis, [(i, i ^ r) for i in range(lax.axis_size(axis))])  28.8 us
    pallas_call x7, Pallas kernels, call(): pl.pallas_call(body, in_specs=specs, out_specs=[VMEM_SPEC] * len(outs), o...  15.1 us
    dot_general x8, matrix products, dot(): return jnp.dot(a, b, preferred_element_type=jnp.float32)  5.51 us
    unnamed x63, local copies, waits for them, and re-layouts  4.58 us
  transfers between devices with their start and end apart: 41, of which 16 were waited for; matrix products, arithmetic and copies ran while one was open for 7% of the time, Pallas kernels for 11%

profile of v13, /device:TPU:0, one launch (start us, length us, event | category | flops | bytes accessed | tf_op | source)
XLA Modules:
  0.0 103.0 jit_solution(16386070522826155469)
XLA Ops:
  0.7 0.8 copy-done.7
  1.5 0.7 copy-done.8
  2.3 2.9 %collective-permute-start = (bf16[16,128]{1,0:T(8,128)(2,1)S(1)}, bf16[16,128]{1,0:T(8,128)(2,1)S(1)}, u32[]{:S(2)}, u32[]{:S(2)}) collective-permute-start(bf16[16,128]{1,0:T(8,128)(2,1)S(1)} %shard_map.140), channel_id=1, source_target_pairs={{0,8},{4,12},{8,0},{12,4},{16,24},{20,28},{24,16},{28,20},{1,9},{5... | collective-permute-start | bytes 12296 | tf_op jit(solution)/shard_map/ppermute | solution.py:19
  5.3 1.5 %collective-permute-start.1 = (bf16[16,128]{1,0:T(8,128)(2,1)S(1)}, bf16[16,128]{1,0:T(8,128)(2,1)S(1)}, u32[]{:S(2)}, u32[]{:S(2)}) collective-permute-start(bf16[16,128]{1,0:T(8,128)(2,1)S(1)} %shard_map.140), channel_id=1, source_target_pairs={{0,16},{4,20},{8,24},{12,28},{16,0},{20,4},{24,8},{28,12},{1,17},{... | collective-permute-start | bytes 12296 | tf_op jit(solution)/shard_map/ppermute | solution.py:19
  6.9 2.0 %collective-permute-start.3 = (bf16[64,2304]{1,0:T(8,128)(2,1)}, bf16[64,2304]{1,0:T(8,128)(2,1)S(1)}, u32[]{:S(2)}, u32[]{:S(2)}) collective-permute-start(bf16[64,2304]{1,0:T(8,128)(2,1)} %refs_0_), channel_id=1, source_target_pairs={{0,8},{4,12},{8,0},{12,4},{16,24},{20,28},{24,16},{28,20},{1,9},{5... | collective-permute-start | bytes 884744 | tf_op jit(solution)/shard_map/ppermute | solution.py:19
  8.9 1.5 %collective-permute-start.4 = (bf16[64,2304]{1,0:T(8,128)(2,1)}, bf16[64,2304]{1,0:T(8,128)(2,1)S(1)}, u32[]{:S(2)}, u32[]{:S(2)}) collective-permute-start(bf16[64,2304]{1,0:T(8,128)(2,1)} %refs_0_), channel_id=1, source_target_pairs={{0,16},{4,20},{8,24},{12,28},{16,0},{20,4},{24,8},{28,12},{1,17},{... | collective-permute-start | bytes 884744 | tf_op jit(solution)/shard_map/ppermute | solution.py:19
  10.4 0.9 collective-permute-done.2
  11.4 1.6 %collective-permute-start.10 = (bf16[64,128]{1,0:T(8,128)(2,1)S(1)}, bf16[64,128]{1,0:T(8,128)(2,1)S(1)}, u32[]{:S(2)}, u32[]{:S(2)}) collective-permute-start(bf16[64,128]{1,0:T(8,128)(2,1)S(1)} %pad_maximum_fusion.3), channel_id=1, source_target_pairs={{0,1},{1,0},{2,3},{3,2},{4,5},{5,4},{6,7},{7,6},{8,9},{9,8},{10,11... | collective-permute-start | bytes 49160 | tf_op jit(solution)/shard_map/ppermute | solution.py:19
  13.0 1.0 copy-done.9
  13.9 3.9 %shard_map.141 = (bf16[64,2304]{1,0:T(8,128)(2,1)S(1)}, bf16[1,2304,1024]{2,1,0:T(8,128)(2,1)S(1)}, bf16[1,2304,1024]{2,1,0:T(8,128)(2,1)S(1)}) custom-call(bf16[64,2304]{1,0:T(8,128)(2,1)S(1)} %copy-done.9, bf16[1,2304,1024]{2,1,0:T(8,128)(2,1)} %refs_1_.1, bf16[1,2304,1024]{2,1,0:T(8,128)(2,1)} %refs_2_.1), custom_call_target="tpu_custom_call" | custom-call | flops 2676326400 | bytes 19464192 | tf_op jit(solution)/shard_map/pallas_call | solution.py:49
  17.9 2.7 %collective-permute-start.11 = (bf16[128,128]{1,0:T(8,128)(2,1)S(1)}, bf16[128,128]{1,0:T(8,128)(2,1)S(1)}, u32[]{:S(2)}, u32[]{:S(2)}) collective-permute-start(bf16[128,128]{1,0:T(8,128)(2,1)S(1)} %pad_maximum_fusion.2), channel_id=1, source_target_pairs={{0,2},{1,3},{2,0},{3,1},{4,6},{5,7},{6,4},{7,5},{8,10},{9,11},{10,... | collective-permute-start | bytes 98312 | tf_op jit(solution)/shard_map/ppermute | solution.py:19
  20.5 2.5 %collective-permute-done.4.refs_2_ = bf16[64,2304]{1,0:T(8,128)(2,1)S(1)} collective-permute-done((bf16[64,2304]{1,0:T(8,128)(2,1)}, bf16[64,2304]{1,0:T(8,128)(2,1)S(1)}, u32[]{:S(2)}, u32[]{:S(2)}) %collective-permute-start.4) | collective-permute-done | bytes 294944 | tf_op jit(solution)/shard_map/ppermute | solution.py:19
  23.6 2.7 %shard_map.142.hidden = bf16[256,1024]{1,0:T(8,128)(2,1)S(1)} custom-call(bf16[64,2304]{1,0:T(8,128)(2,1)S(1)} %get-tuple-element.31.refs_0_, bf16[64,2304]{1,0:T(8,128)(2,1)S(1)} %collective-permute-done.3.refs_1_, bf16[64,2304]{1,0:T(8,128)(2,1)S(1)} %collective-permute-done.4.refs_2_, bf16[64,2304]{1,0:T(8,128)(2,1)S(1)} %collective-permute-done.5.refs_3_, ...), custom_call_target="tpu_custom_call" | custom-call | flops 2415919104 | bytes 9437184 | tf_op jit(solution)/shard_map/pallas_call | solution.py:49
  26.4 1.9 %shard_map.144 = bf16[256,2304]{1,0:T(8,128)(2,1)S(1)} custom-call(s32[3]{0:T(128)S(1)} %pad_add_fusion.scalars, bf16[256,1024]{1,0:T(8,128)(2,1)S(1)} %shard_map.142.hidden, bf16[1,1024,2304]{2,1,0:T(8,128)(2,1)S(1)} %bitcast.58, bf16[256,128]{1,0:T(8,128)(2,1)S(1)} %constant_dynamic-update-slice_fusion.table), custom_call_target="tpu_custom_call" | custom-call | flops 1207959552 | bytes 4718592 | tf_op jit(solution)/shard_map/pallas_call | solution.py:49
  28.9 2.7 %shard_map.143.hidden = bf16[256,1024]{1,0:T(8,128)(2,1)S(1)} custom-call(bf16[64,2304]{1,0:T(8,128)(2,1)S(1)} %collective-permute-done.6.refs_0_.x, bf16[64,2304]{1,0:T(8,128)(2,1)S(1)} %collective-permute-done.7.refs_1_, bf16[64,2304]{1,0:T(8,128)(2,1)S(1)} %collective-permute-done.8.refs_2_, bf16[64,2304]{1,0:T(8,128)(2,1)S(1)} %collective-permute-done.9.refs_3_, ...), custom_call_target="tpu_custom_call" | custom-call | flops 2415919104 | bytes 9437184 | tf_op jit(solution)/shard_map/pallas_call | solution.py:49
  31.6 2.0 %shard_map.145 = (bf16[32,2304]{1,0:T(8,128)(2,1)S(1)}, bf16[32,2304]{1,0:T(8,128)(2,1)S(1)}, bf16[32,2304]{1,0:T(8,128)(2,1)S(1)}, bf16[32,2304]{1,0:T(8,128)(2...) custom-call(s32[3]{0:T(128)S(1)} %pad_add_fusion.scalars, ...), custom_call_target="tpu_custom_call" | custom-call | flops 1207959552 | bytes 4718592 | tf_op jit(solution)/shard_map/pallas_call | solution.py:49
  33.6 1.5 %collective-permute-start.17 = (bf16[32,2304]{1,0:T(8,128)(2,1)S(1)}, bf16[32,2304]{1,0:T(8,128)(2,1)S(1)}, u32[]{:S(2)}, u32[]{:S(2)}) collective-permute-start(bf16[32,2304]{1,0:T(8,128)(2,1)S(1)} %get-tuple-element.45), channel_id=1, source_target_pairs={{0,24},{4,28},{8,16},{12,20},{16,8},{20,12},{24,0},{28,4},{1,25},{... | collective-permute-start | bytes 442376 | tf_op jit(solution)/shard_map/ppermute | solution.py:19
  35.1 1.5 %collective-permute-start.18 = (bf16[32,2304]{1,0:T(8,128)(2,1)S(1)}, bf16[32,2304]{1,0:T(8,128)(2,1)S(1)}, u32[]{:S(2)}, u32[]{:S(2)}) collective-permute-start(bf16[32,2304]{1,0:T(8,128)(2,1)S(1)} %get-tuple-element.49), channel_id=1, source_target_pairs={{0,8},{4,12},{8,0},{12,4},{16,24},{20,28},{24,16},{28,20},{1,9},{5... | collective-permute-start | bytes 442376 | tf_op jit(solution)/shard_map/ppermute | solution.py:19
  37.2 0.8 collective-permute-start.14
  38.0 1.2 %collective-permute-start.15 = (bf16[32,2304]{1,0:T(8,128)(2,1)S(1)}, bf16[32,2304]{1,0:T(8,128)(2,1)S(1)}, u32[]{:S(2)}, u32[]{:S(2)}) collective-permute-start(bf16[32,2304]{1,0:T(8,128)(2,1)S(1)} %get-tuple-element.43), channel_id=1, source_target_pairs={{0,16},{4,20},{8,24},{12,28},{16,0},{20,4},{24,8},{28,12},{1,17},{... | collective-permute-start | bytes 442376 | tf_op jit(solution)/shard_map/ppermute | solution.py:19
  39.2 2.1 %collective-permute-done.17 = bf16[32,2304]{1,0:T(8,128)(2,1)S(1)} collective-permute-done((bf16[32,2304]{1,0:T(8,128)(2,1)S(1)}, bf16[32,2304]{1,0:T(8,128)(2,1)S(1)}, u32[]{:S(2)}, u32[]{:S(2)}) %collective-permute-start.17) | collective-permute-done | bytes 147488 | tf_op jit(solution)/shard_map/ppermute | solution.py:19
  41.3 1.4 %collective-permute-start.16 = (bf16[32,2304]{1,0:T(8,128)(2,1)S(1)}, bf16[32,2304]{1,0:T(8,128)(2,1)S(1)}, u32[]{:S(2)}, u32[]{:S(2)}) collective-permute-start(bf16[32,2304]{1,0:T(8,128)(2,1)S(1)} %get-tuple-element.44), channel_id=1, source_target_pairs={{0,24},{4,28},{8,16},{12,20},{16,8},{20,12},{24,0},{28,4},{1,25},{... | collective-permute-start | bytes 442376 | tf_op jit(solution)/shard_map/ppermute | solution.py:19
  42.8 1.8 %shard_map.146 = (f32[32,2304]{1,0:T(8,128)S(1)}, f32[32,2304]{1,0:T(8,128)S(1)}, bf16[2304,512]{1,0:T(8,128)(2,1)S(1)}) custom-call(s32[3]{0:T(128)S(1)} %pad_add_fusion.scalars, bf16[64,2304]{1,0:T(8,128)(2,1)S(1)} %collective-permute-done.6.refs_0_.x, bf16[2304,256]{1,0:T(8,128)(2,1)S(1)} %copy-done.4, bf16[2304,256]{1,0:T(8,128)(2,1)S(1)} %copy-done.5, ...), custom_call_target="tpu_custom_call" | custom-call | flops 226492416 | bytes 3538944 | tf_op jit(solution)/shard_map/pallas_call | solution.py:49
  44.5 1.4 %copy-done.1 = bf16[2304,512]{1,0:T(8,128)(2,1)} copy-done((bf16[2304,512]{1,0:T(8,128)(2,1)}, bf16[2304,512]{1,0:T(8,128)(2,1)S(1)}, u32[]{:S(2)}) %copy-start.1) | copy-done | bytes 2359320
  46.0 1.6 %collective-permute-start.20 = (bf16[32,2304]{1,0:T(8,128)(2,1)S(1)}, bf16[32,2304]{1,0:T(8,128)(2,1)S(1)}, u32[]{:S(2)}, u32[]{:S(2)}) collective-permute-start(bf16[32,2304]{1,0:T(8,128)(2,1)S(1)} %add_convert_fusion.5), channel_id=1, source_target_pairs={{0,1},{1,0},{2,3},{3,2},{4,5},{5,4},{6,7},{7,6},{8,9},{9,8},{10,11... | collective-permute-start | bytes 442376 | tf_op jit(solution)/shard_map/ppermute | solution.py:19
  47.7 2.2 %collective-permute-done.16 = bf16[32,2304]{1,0:T(8,128)(2,1)S(1)} collective-permute-done((bf16[32,2304]{1,0:T(8,128)(2,1)S(1)}, bf16[32,2304]{1,0:T(8,128)(2,1)S(1)}, u32[]{:S(2)}, u32[]{:S(2)}) %collective-permute-start.16) | collective-permute-done | bytes 147488 | tf_op jit(solution)/shard_map/ppermute | solution.py:19
  49.9 1.3 %collective-permute-done.20 = bf16[32,2304]{1,0:T(8,128)(2,1)S(1)} collective-permute-done((bf16[32,2304]{1,0:T(8,128)(2,1)S(1)}, bf16[32,2304]{1,0:T(8,128)(2,1)S(1)}, u32[]{:S(2)}, u32[]{:S(2)}) %collective-permute-start.20) | collective-permute-done | bytes 147488 | tf_op jit(solution)/shard_map/ppermute | solution.py:19
  51.4 2.7 %collective-permute-start.21 = (bf16[2,16,2304]{2,1,0:T(8,128)(2,1)S(1)}, bf16[2,16,2304]{2,1,0:T(8,128)(2,1)S(1)}, u32[]{:S(2)}, u32[]{:S(2)}) collective-permute-start(bf16[2,16,2304]{2,1,0:T(8,128)(2,1)S(1)} %bitcast.108), channel_id=1, source_target_pairs={{0,2},{1,3},{2,0},{3,1},{4,6},{5,7},{6,4},{7,5},{8,10},{9,11},{10,... | collective-permute-start | bytes 442376 | tf_op jit(solution)/shard_map/ppermute | solution.py:19
  54.0 5.2 %collective-permute-done.21 = bf16[2,16,2304]{2,1,0:T(8,128)(2,1)S(1)} collective-permute-done((bf16[2,16,2304]{2,1,0:T(8,128)(2,1)S(1)}, bf16[2,16,2304]{2,1,0:T(8,128)(2,1)S(1)}, u32[]{:S(2)}, u32[]{:S(2)}) %collective-permute-start.21) | collective-permute-done | bytes 147488 | tf_op jit(solution)/shard_map/ppermute | solution.py:19
  59.2 0.7 collective-permute-start.22
  59.9 1.6 %collective-permute-start.27 = (bf16[32,2304]{1,0:T(8,128)(2,1)S(1)}, bf16[32,2304]{1,0:T(8,128)(2,1)S(1)}, u32[]{:S(2)}, u32[]{:S(2)}) collective-permute-start(bf16[32,2304]{1,0:T(8,128)(2,1)S(1)} %bitcast.104), channel_id=1, source_target_pairs={{0,8},{4,12},{8,0},{12,4},{16,24},{20,28},{24,16},{28,20},{1,9},{5... | collective-permute-start | bytes 442376 | tf_op jit(solution)/shard_map/ppermute | solution.py:19
  61.9 2.5 %collective-permute-done.22 = bf16[32,2304]{1,0:T(8,128)(2,1)S(1)} collective-permute-done((bf16[32,2304]{1,0:T(8,128)(2,1)S(1)}, bf16[32,2304]{1,0:T(8,128)(2,1)S(1)}, u32[]{:S(2)}, u32[]{:S(2)}) %collective-permute-start.22) | collective-permute-done | bytes 147488 | tf_op jit(solution)/shard_map/ppermute | solution.py:19
  64.4 1.5 %collective-permute-start.29 = (bf16[32,2304]{1,0:T(8,128)(2,1)S(1)}, bf16[32,2304]{1,0:T(8,128)(2,1)S(1)}, u32[]{:S(2)}, u32[]{:S(2)}) collective-permute-start(bf16[32,2304]{1,0:T(8,128)(2,1)S(1)} %bitcast.106), channel_id=1, source_target_pairs={{0,24},{4,28},{8,16},{12,20},{16,8},{20,12},{24,0},{28,4},{1,25},{... | collective-permute-start | bytes 442376 | tf_op jit(solution)/shard_map/ppermute | solution.py:19
  65.9 1.4 %collective-permute-start.25 = (bf16[32,2304]{1,0:T(8,128)(2,1)S(1)}, bf16[32,2304]{1,0:T(8,128)(2,1)S(1)}, u32[]{:S(2)}, u32[]{:S(2)}) collective-permute-start(bf16[32,2304]{1,0:T(8,128)(2,1)S(1)} %collective-permute-done.22), channel_id=1, source_target_pairs={{0,24},{4,28},{8,16},{12,20},{16,8},{20,12},{24,0},{28,4},{1,25},{... | collective-permute-start | bytes 442376 | tf_op jit(solution)/shard_map/ppermute | solution.py:19
  67.4 1.6 %collective-permute-start.23 = (bf16[32,2304]{1,0:T(8,128)(2,1)S(1)}, bf16[32,2304]{1,0:T(8,128)(2,1)S(1)}, u32[]{:S(2)}, u32[]{:S(2)}) collective-permute-start(bf16[32,2304]{1,0:T(8,128)(2,1)S(1)} %collective-permute-done.22), channel_id=1, source_target_pairs={{0,8},{4,12},{8,0},{12,4},{16,24},{20,28},{24,16},{28,20},{1,9},{5... | collective-permute-start | bytes 442376 | tf_op jit(solution)/shard_map/ppermute | solution.py:19
  69.4 0.9 collective-permute-done.28
  70.3 1.7 %collective-permute-done.29 = bf16[32,2304]{1,0:T(8,128)(2,1)S(1)} collective-permute-done((bf16[32,2304]{1,0:T(8,128)(2,1)S(1)}, bf16[32,2304]{1,0:T(8,128)(2,1)S(1)}, u32[]{:S(2)}, u32[]{:S(2)}) %collective-permute-start.29) | collective-permute-done | bytes 147488 | tf_op jit(solution)/shard_map/ppermute | solution.py:19
  72.2 2.1 %fusion.4 = bf16[128,512]{1,0:T(8,128)(2,1)S(1)} fusion(bf16[128,2304]{1,0:T(8,128)(2,1)S(1)} %bitcast.64, bf16[2304,512]{1,0:T(8,128)(2,1)} %copy-done.1, f32[512]{0:T(512)S(1)} %copy-done.10), kind=kOutput, calls=%fused_computation.12 | convolution fusion | flops 302186496 | bytes 3082240 | tf_op jit(solution)/shard_map/dot_general | solution.py:23
  78.6 1.3 %collective-permute-start.33 = (bf16[32,2304]{1,0:T(8,128)(2,1)S(1)}, bf16[32,2304]{1,0:T(8,128)(2,1)S(1)}, u32[]{:S(2)}, u32[]{:S(2)}) collective-permute-start(bf16[32,2304]{1,0:T(8,128)(2,1)S(1)} %get-tuple-element.59), channel_id=1, source_target_pairs={{0,8},{4,12},{8,0},{12,4},{16,24},{20,28},{24,16},{28,20},{1,9},{5... | collective-permute-start | bytes 442376 | tf_op jit(solution)/shard_map/ppermute | solution.py:19
  80.5 1.6 %collective-permute-start.38 = (bf16[32,2304]{1,0:T(8,128)(2,1)S(1)}, bf16[32,2304]{1,0:T(8,128)(2,1)S(1)}, u32[]{:S(2)}, u32[]{:S(2)}) collective-permute-start(bf16[32,2304]{1,0:T(8,128)(2,1)S(1)} %get-tuple-element.60), channel_id=1, source_target_pairs={{0,24},{4,28},{8,16},{12,20},{16,8},{20,12},{24,0},{28,4},{1,25},{... | collective-permute-start | bytes 442376 | tf_op jit(solution)/shard_map/ppermute | solution.py:19
  83.2 2.1 %collective-permute-done.33 = bf16[32,2304]{1,0:T(8,128)(2,1)S(1)} collective-permute-done((bf16[32,2304]{1,0:T(8,128)(2,1)S(1)}, bf16[32,2304]{1,0:T(8,128)(2,1)S(1)}, u32[]{:S(2)}, u32[]{:S(2)}) %collective-permute-start.33) | collective-permute-done | bytes 147488 | tf_op jit(solution)/shard_map/ppermute | solution.py:19
  87.1 1.3 %collective-permute-start.34 = (bf16[32,2304]{1,0:T(8,128)(2,1)S(1)}, bf16[32,2304]{1,0:T(8,128)(2,1)S(1)}, u32[]{:S(2)}, u32[]{:S(2)}) collective-permute-start(bf16[32,2304]{1,0:T(8,128)(2,1)S(1)} %get-tuple-element.56), channel_id=1, source_target_pairs={{0,8},{4,12},{8,0},{12,4},{16,24},{20,28},{24,16},{28,20},{1,9},{5... | collective-permute-start | bytes 442376 | tf_op jit(solution)/shard_map/ppermute | solution.py:19
  88.7 1.9 %collective-permute-start.36 = (bf16[32,2304]{1,0:T(8,128)(2,1)S(1)}, bf16[32,2304]{1,0:T(8,128)(2,1)S(1)}, u32[]{:S(2)}, u32[]{:S(2)}) collective-permute-start(bf16[32,2304]{1,0:T(8,128)(2,1)S(1)} %get-tuple-element.57), channel_id=1, source_target_pairs={{0,24},{4,28},{8,16},{12,20},{16,8},{20,12},{24,0},{28,4},{1,25},{... | collective-permute-start | bytes 442376 | tf_op jit(solution)/shard_map/ppermute | solution.py:19
  91.3 1.9 %collective-permute-done.34 = bf16[32,2304]{1,0:T(8,128)(2,1)S(1)} collective-permute-done((bf16[32,2304]{1,0:T(8,128)(2,1)S(1)}, bf16[32,2304]{1,0:T(8,128)(2,1)S(1)}, u32[]{:S(2)}, u32[]{:S(2)}) %collective-permute-start.34) | collective-permute-done | bytes 147488 | tf_op jit(solution)/shard_map/ppermute | solution.py:19
  93.8 1.6 %collective-permute-done.36 = bf16[32,2304]{1,0:T(8,128)(2,1)S(1)} collective-permute-done((bf16[32,2304]{1,0:T(8,128)(2,1)S(1)}, bf16[32,2304]{1,0:T(8,128)(2,1)S(1)}, u32[]{:S(2)}, u32[]{:S(2)}) %collective-permute-start.36) | collective-permute-done | bytes 147488 | tf_op jit(solution)/shard_map/ppermute | solution.py:19
  96.0 3.8 %collective-permute-start.40 = (bf16[16,2304]{1,0:T(8,128)(2,1)S(1)}, bf16[16,2304]{1,0:T(8,128)(2,1)S(1)}, u32[]{:S(2)}, u32[]{:S(2)}) collective-permute-start(bf16[16,2304]{1,0:T(8,128)(2,1)S(1)} %fusion.9), channel_id=1, source_target_pairs={{0,2},{1,3},{2,0},{3,1},{4,6},{5,7},{6,4},{7,5},{8,10},{9,11},{10,... | collective-permute-start | bytes 221192 | tf_op jit(solution)/shard_map/ppermute | solution.py:19
  99.8 2.5 %collective-permute-done.40 = bf16[16,2304]{1,0:T(8,128)(2,1)S(1)} collective-permute-done((bf16[16,2304]{1,0:T(8,128)(2,1)S(1)}, bf16[16,2304]{1,0:T(8,128)(2,1)S(1)}, u32[]{:S(2)}, u32[]{:S(2)}) %collective-permute-start.40) | collective-permute-done | bytes 73760 | tf_op jit(solution)/shard_map/ppermute | solution.py:19
  102.3 0.7 fusion.8
  (131 shorter events, 12.2 us)
Async XLA Ops:
  0.6 73.7 %copy-start = (bf16[512,2304]{1,0:T(8,128)(2,1)S(1)}, bf16[512,2304]{1,0:T(8,128)(2,1)}, u32[]{:S(2)}) copy-start(bf16[512,2304]{1,0:T(8,128)(2,1)} %param.24) | copy-start | bytes 7077892
  2.3 4.5 %collective-permute-start = (bf16[16,128]{1,0:T(8,128)(2,1)S(1)}, bf16[16,128]{1,0:T(8,128)(2,1)S(1)}, u32[]{:S(2)}, u32[]{:S(2)}) collective-permute-start(bf16[16,128]{1,0:T(8,128)(2,1)S(1)} %shard_map.140), channel_id=1, source_target_pairs={{0,8},{4,12},{8,0},{12,4},{16,24},{20,28},{24,16},{28,20},{1,9},{5... | collective-permute-start | bytes 12296 | tf_op jit(solution)/shard_map/ppermute | solution.py:19
  5.3 5.1 %collective-permute-start.1 = (bf16[16,128]{1,0:T(8,128)(2,1)S(1)}, bf16[16,128]{1,0:T(8,128)(2,1)S(1)}, u32[]{:S(2)}, u32[]{:S(2)}) collective-permute-start(bf16[16,128]{1,0:T(8,128)(2,1)S(1)} %shard_map.140), channel_id=1, source_target_pairs={{0,16},{4,20},{8,24},{12,28},{16,0},{20,4},{24,8},{28,12},{1,17},{... | collective-permute-start | bytes 12296 | tf_op jit(solution)/shard_map/ppermute | solution.py:19
  6.8 4.6 %collective-permute-start.2 = (bf16[16,128]{1,0:T(8,128)(2,1)S(1)}, bf16[16,128]{1,0:T(8,128)(2,1)S(1)}, u32[]{:S(2)}, u32[]{:S(2)}) collective-permute-start(bf16[16,128]{1,0:T(8,128)(2,1)S(1)} %shard_map.140), channel_id=1, source_target_pairs={{0,24},{4,28},{8,16},{12,20},{16,8},{20,12},{24,0},{28,4},{1,25},{... | collective-permute-start | bytes 12296 | tf_op jit(solution)/shard_map/ppermute | solution.py:19
  6.9 13.6 %collective-permute-start.3 = (bf16[64,2304]{1,0:T(8,128)(2,1)}, bf16[64,2304]{1,0:T(8,128)(2,1)S(1)}, u32[]{:S(2)}, u32[]{:S(2)}) collective-permute-start(bf16[64,2304]{1,0:T(8,128)(2,1)} %refs_0_), channel_id=1, source_target_pairs={{0,8},{4,12},{8,0},{12,4},{16,24},{20,28},{24,16},{28,20},{1,9},{5... | collective-permute-start | bytes 884744 | tf_op jit(solution)/shard_map/ppermute | solution.py:19
  8.9 14.2 %collective-permute-start.4 = (bf16[64,2304]{1,0:T(8,128)(2,1)}, bf16[64,2304]{1,0:T(8,128)(2,1)S(1)}, u32[]{:S(2)}, u32[]{:S(2)}) collective-permute-start(bf16[64,2304]{1,0:T(8,128)(2,1)} %refs_0_), channel_id=1, source_target_pairs={{0,16},{4,20},{8,24},{12,28},{16,0},{20,4},{24,8},{28,12},{1,17},{... | collective-permute-start | bytes 884744 | tf_op jit(solution)/shard_map/ppermute | solution.py:19
  10.4 12.7 %collective-permute-start.5 = (bf16[64,2304]{1,0:T(8,128)(2,1)}, bf16[64,2304]{1,0:T(8,128)(2,1)S(1)}, u32[]{:S(2)}, u32[]{:S(2)}) collective-permute-start(bf16[64,2304]{1,0:T(8,128)(2,1)} %refs_0_), channel_id=1, source_target_pairs={{0,24},{4,28},{8,16},{12,20},{16,8},{20,12},{24,0},{28,4},{1,25},{... | collective-permute-start | bytes 884744 | tf_op jit(solution)/shard_map/ppermute | solution.py:19
  10.4 15.9 %collective-permute-start.6 = (bf16[64,2304]{1,0:T(8,128)(2,1)}, bf16[64,2304]{1,0:T(8,128)(2,1)S(1)}, u32[]{:S(2)}, u32[]{:S(2)}) collective-permute-start(bf16[64,2304]{1,0:T(8,128)(2,1)} %refs_0_), channel_id=1, source_target_pairs={{0,4},{4,0},{8,12},{12,8},{16,20},{20,16},{24,28},{28,24},{1,5},{5... | collective-permute-start | bytes 884744 | tf_op jit(solution)/shard_map/ppermute | solution.py:19
  11.4 6.5 %collective-permute-start.10 = (bf16[64,128]{1,0:T(8,128)(2,1)S(1)}, bf16[64,128]{1,0:T(8,128)(2,1)S(1)}, u32[]{:S(2)}, u32[]{:S(2)}) collective-permute-start(bf16[64,128]{1,0:T(8,128)(2,1)S(1)} %pad_maximum_fusion.3), channel_id=1, source_target_pairs={{0,1},{1,0},{2,3},{3,2},{4,5},{5,4},{6,7},{7,6},{8,9},{9,8},{10,11... | collective-permute-start | bytes 49160 | tf_op jit(solution)/shard_map/ppermute | solution.py:19
  13.9 12.4 %slice-start = ((s8[4718592]{0:T(1024)(128)(4,1)}), s8[524288]{0:T(1024)(128)(4,1)S(1)}, s32[]{:S(2)}) async-start(s8[4718592]{0:T(1024)(128)(4,1)} %bitcast.57), calls=%async_computation | async-start | bytes 1048576
  17.9 5.7 %collective-permute-start.11 = (bf16[128,128]{1,0:T(8,128)(2,1)S(1)}, bf16[128,128]{1,0:T(8,128)(2,1)S(1)}, u32[]{:S(2)}, u32[]{:S(2)}) collective-permute-start(bf16[128,128]{1,0:T(8,128)(2,1)S(1)} %pad_maximum_fusion.2), channel_id=1, source_target_pairs={{0,2},{1,3},{2,0},{3,1},{4,6},{5,7},{6,4},{7,5},{8,10},{9,11},{10,... | collective-permute-start | bytes 98312 | tf_op jit(solution)/shard_map/ppermute | solution.py:19
  20.5 5.8 %collective-permute-start.7 = (bf16[64,2304]{1,0:T(8,128)(2,1)S(1)}, bf16[64,2304]{1,0:T(8,128)(2,1)S(1)}, u32[]{:S(2)}, u32[]{:S(2)}) collective-permute-start(bf16[64,2304]{1,0:T(8,128)(2,1)S(1)} %collective-permute-done.3.refs_1_), channel_id=1, source_target_pairs={{0,4},{4,0},{8,12},{12,8},{16,20},{20,16},{24,28},{28,24},{1,5},{5... | collective-permute-start | bytes 884744 | tf_op jit(solution)/shard_map/ppermute | solution.py:19
  23.1 3.2 %collective-permute-start.8 = (bf16[64,2304]{1,0:T(8,128)(2,1)S(1)}, bf16[64,2304]{1,0:T(8,128)(2,1)S(1)}, u32[]{:S(2)}, u32[]{:S(2)}) collective-permute-start(bf16[64,2304]{1,0:T(8,128)(2,1)S(1)} %collective-permute-done.4.refs_2_), channel_id=1, source_target_pairs={{0,4},{4,0},{8,12},{12,8},{16,20},{20,16},{24,28},{28,24},{1,5},{5... | collective-permute-start | bytes 884744 | tf_op jit(solution)/shard_map/ppermute | solution.py:19
  23.1 3.2 %collective-permute-start.9 = (bf16[64,2304]{1,0:T(8,128)(2,1)S(1)}, bf16[64,2304]{1,0:T(8,128)(2,1)S(1)}, u32[]{:S(2)}, u32[]{:S(2)}) collective-permute-start(bf16[64,2304]{1,0:T(8,128)(2,1)S(1)} %collective-permute-done.5.refs_3_), channel_id=1, source_target_pairs={{0,4},{4,0},{8,12},{12,8},{16,20},{20,16},{24,28},{28,24},{1,5},{5... | collective-permute-start | bytes 884744 | tf_op jit(solution)/shard_map/ppermute | solution.py:19
  28.3 3.3 %collective-permute-start.13 = (bf16[256,2304]{1,0:T(8,128)(2,1)S(1)}, bf16[256,2304]{1,0:T(8,128)(2,1)S(1)}, u32[]{:S(2)}, u32[]{:S(2)}) collective-permute-start(bf16[256,2304]{1,0:T(8,128)(2,1)S(1)} %shard_map.144), channel_id=1, source_target_pairs={{0,4},{4,0},{8,12},{12,8},{16,20},{20,16},{24,28},{28,24},{1,5},{5... | collective-permute-start | bytes 3538952 | tf_op jit(solution)/shard_map/ppermute | solution.py:19
  28.4 3.2 %collective-permute-start.12 = (bf16[256,128]{1,0:T(8,128)(2,1)S(1)}, bf16[256,128]{1,0:T(8,128)(2,1)S(1)}, u32[]{:S(2)}, u32[]{:S(2)}) collective-permute-start(bf16[256,128]{1,0:T(8,128)(2,1)S(1)} %constant_dynamic-update-slice_fusion.table), channel_id=1, source_target_pairs={{0,4},{4,0},{8,12},{12,8},{16,20},{20,16},{24,28},{28,24},{1,5},{5... | collective-permute-start | bytes 196616 | tf_op jit(solution)/shard_map/ppermute | solution.py:19
  31.6 11.2 %copy-start.3 = (bf16[2304,512]{1,0:T(8,128)(2,1)S(1)}, bf16[2304,512]{1,0:T(8,128)(2,1)}, u32[]{:S(2)}) copy-start(bf16[2304,512]{1,0:T(8,128)(2,1)} %extra.1) | copy-start | bytes 7077892
  31.6 11.2 %copy-start.4 = (bf16[2304,256]{1,0:T(8,128)(2,1)S(1)}, bf16[2304,256]{1,0:T(8,128)(2,1)}, u32[]{:S(2)}) copy-start(bf16[2304,256]{1,0:T(8,128)(2,1)} %gate.1) | copy-start | bytes 3538948
  31.6 11.2 %copy-start.5 = (bf16[2304,256]{1,0:T(8,128)(2,1)S(1)}, bf16[2304,256]{1,0:T(8,128)(2,1)}, u32[]{:S(2)}) copy-start(bf16[2304,256]{1,0:T(8,128)(2,1)} %up.1) | copy-start | bytes 3538948
  33.6 7.7 %collective-permute-start.17 = (bf16[32,2304]{1,0:T(8,128)(2,1)S(1)}, bf16[32,2304]{1,0:T(8,128)(2,1)S(1)}, u32[]{:S(2)}, u32[]{:S(2)}) collective-permute-start(bf16[32,2304]{1,0:T(8,128)(2,1)S(1)} %get-tuple-element.45), channel_id=1, source_target_pairs={{0,24},{4,28},{8,16},{12,20},{16,8},{20,12},{24,0},{28,4},{1,25},{... | collective-permute-start | bytes 442376 | tf_op jit(solution)/shard_map/ppermute | solution.py:19
  35.1 10.8 %collective-permute-start.18 = (bf16[32,2304]{1,0:T(8,128)(2,1)S(1)}, bf16[32,2304]{1,0:T(8,128)(2,1)S(1)}, u32[]{:S(2)}, u32[]{:S(2)}) collective-permute-start(bf16[32,2304]{1,0:T(8,128)(2,1)S(1)} %get-tuple-element.49), channel_id=1, source_target_pairs={{0,8},{4,12},{8,0},{12,4},{16,24},{20,28},{24,16},{28,20},{1,9},{5... | collective-permute-start | bytes 442376 | tf_op jit(solution)/shard_map/ppermute | solution.py:19
  36.6 9.3 %collective-permute-start.19 = (bf16[32,2304]{1,0:T(8,128)(2,1)S(1)}, bf16[32,2304]{1,0:T(8,128)(2,1)S(1)}, u32[]{:S(2)}, u32[]{:S(2)}) collective-permute-start(bf16[32,2304]{1,0:T(8,128)(2,1)S(1)} %get-tuple-element.50), channel_id=1, source_target_pairs={{0,16},{4,20},{8,24},{12,28},{16,0},{20,4},{24,8},{28,12},{1,17},{... | collective-permute-start | bytes 442376 | tf_op jit(solution)/shard_map/ppermute | solution.py:19
  37.2 10.5 %collective-permute-start.14 = (bf16[32,2304]{1,0:T(8,128)(2,1)S(1)}, bf16[32,2304]{1,0:T(8,128)(2,1)S(1)}, u32[]{:S(2)}, u32[]{:S(2)}) collective-permute-start(bf16[32,2304]{1,0:T(8,128)(2,1)S(1)} %get-tuple-element.42), channel_id=1, source_target_pairs={{0,8},{4,12},{8,0},{12,4},{16,24},{20,28},{24,16},{28,20},{1,9},{5... | collective-permute-start | bytes 442376 | tf_op jit(solution)/shard_map/ppermute | solution.py:19
  38.0 9.7 %collective-permute-start.15 = (bf16[32,2304]{1,0:T(8,128)(2,1)S(1)}, bf16[32,2304]{1,0:T(8,128)(2,1)S(1)}, u32[]{:S(2)}, u32[]{:S(2)}) collective-permute-start(bf16[32,2304]{1,0:T(8,128)(2,1)S(1)} %get-tuple-element.43), channel_id=1, source_target_pairs={{0,16},{4,20},{8,24},{12,28},{16,0},{20,4},{24,8},{28,12},{1,17},{... | collective-permute-start | bytes 442376 | tf_op jit(solution)/shard_map/ppermute | solution.py:19
  41.3 8.6 %collective-permute-start.16 = (bf16[32,2304]{1,0:T(8,128)(2,1)S(1)}, bf16[32,2304]{1,0:T(8,128)(2,1)S(1)}, u32[]{:S(2)}, u32[]{:S(2)}) collective-permute-start(bf16[32,2304]{1,0:T(8,128)(2,1)S(1)} %get-tuple-element.44), channel_id=1, source_target_pairs={{0,24},{4,28},{8,16},{12,20},{16,8},{20,12},{24,0},{28,4},{1,25},{... | collective-permute-start | bytes 442376 | tf_op jit(solution)/shard_map/ppermute | solution.py:19
  45.9 26.3 %copy-start.10 = (f32[512]{0:T(512)S(1)}, f32[512]{0:T(512)}, u32[]{:S(2)}) copy-start(f32[512]{0:T(512)} %param.23) | copy-start | bytes 6148
  46.0 5.2 %collective-permute-start.20 = (bf16[32,2304]{1,0:T(8,128)(2,1)S(1)}, bf16[32,2304]{1,0:T(8,128)(2,1)S(1)}, u32[]{:S(2)}, u32[]{:S(2)}) collective-permute-start(bf16[32,2304]{1,0:T(8,128)(2,1)S(1)} %add_convert_fusion.5), channel_id=1, source_target_pairs={{0,1},{1,0},{2,3},{3,2},{4,5},{5,4},{6,7},{7,6},{8,9},{9,8},{10,11... | collective-permute-start | bytes 442376 | tf_op jit(solution)/shard_map/ppermute | solution.py:19
  51.4 7.8 %collective-permute-start.21 = (bf16[2,16,2304]{2,1,0:T(8,128)(2,1)S(1)}, bf16[2,16,2304]{2,1,0:T(8,128)(2,1)S(1)}, u32[]{:S(2)}, u32[]{:S(2)}) collective-permute-start(bf16[2,16,2304]{2,1,0:T(8,128)(2,1)S(1)} %bitcast.108), channel_id=1, source_target_pairs={{0,2},{1,3},{2,0},{3,1},{4,6},{5,7},{6,4},{7,5},{8,10},{9,11},{10,... | collective-permute-start | bytes 442376 | tf_op jit(solution)/shard_map/ppermute | solution.py:19
  59.2 5.2 %collective-permute-start.22 = (bf16[32,2304]{1,0:T(8,128)(2,1)S(1)}, bf16[32,2304]{1,0:T(8,128)(2,1)S(1)}, u32[]{:S(2)}, u32[]{:S(2)}) collective-permute-start(bf16[32,2304]{1,0:T(8,128)(2,1)S(1)} %bitcast.103), channel_id=1, source_target_pairs={{0,1},{1,0},{2,3},{3,2},{4,5},{5,4},{6,7},{7,6},{8,9},{9,8},{10,11... | collective-permute-start | bytes 442376 | tf_op jit(solution)/shard_map/ppermute | solution.py:19
  59.9 9.1 %collective-permute-start.27 = (bf16[32,2304]{1,0:T(8,128)(2,1)S(1)}, bf16[32,2304]{1,0:T(8,128)(2,1)S(1)}, u32[]{:S(2)}, u32[]{:S(2)}) collective-permute-start(bf16[32,2304]{1,0:T(8,128)(2,1)S(1)} %bitcast.104), channel_id=1, source_target_pairs={{0,8},{4,12},{8,0},{12,4},{16,24},{20,28},{24,16},{28,20},{1,9},{5... | collective-permute-start | bytes 442376 | tf_op jit(solution)/shard_map/ppermute | solution.py:19
  61.6 8.8 %collective-permute-start.28 = (bf16[32,2304]{1,0:T(8,128)(2,1)S(1)}, bf16[32,2304]{1,0:T(8,128)(2,1)S(1)}, u32[]{:S(2)}, u32[]{:S(2)}) collective-permute-start(bf16[32,2304]{1,0:T(8,128)(2,1)S(1)} %bitcast.105), channel_id=1, source_target_pairs={{0,16},{4,20},{8,24},{12,28},{16,0},{20,4},{24,8},{28,12},{1,17},{... | collective-permute-start | bytes 442376 | tf_op jit(solution)/shard_map/ppermute | solution.py:19
  64.4 7.6 %collective-permute-start.29 = (bf16[32,2304]{1,0:T(8,128)(2,1)S(1)}, bf16[32,2304]{1,0:T(8,128)(2,1)S(1)}, u32[]{:S(2)}, u32[]{:S(2)}) collective-permute-start(bf16[32,2304]{1,0:T(8,128)(2,1)S(1)} %bitcast.106), channel_id=1, source_target_pairs={{0,24},{4,28},{8,16},{12,20},{16,8},{20,12},{24,0},{28,4},{1,25},{... | collective-permute-start | bytes 442376 | tf_op jit(solution)/shard_map/ppermute | solution.py:19
  65.9 9.4 %collective-permute-start.25 = (bf16[32,2304]{1,0:T(8,128)(2,1)S(1)}, bf16[32,2304]{1,0:T(8,128)(2,1)S(1)}, u32[]{:S(2)}, u32[]{:S(2)}) collective-permute-start(bf16[32,2304]{1,0:T(8,128)(2,1)S(1)} %collective-permute-done.22), channel_id=1, source_target_pairs={{0,24},{4,28},{8,16},{12,20},{16,8},{20,12},{24,0},{28,4},{1,25},{... | collective-permute-start | bytes 442376 | tf_op jit(solution)/shard_map/ppermute | solution.py:19
  67.4 8.0 %collective-permute-start.23 = (bf16[32,2304]{1,0:T(8,128)(2,1)S(1)}, bf16[32,2304]{1,0:T(8,128)(2,1)S(1)}, u32[]{:S(2)}, u32[]{:S(2)}) collective-permute-start(bf16[32,2304]{1,0:T(8,128)(2,1)S(1)} %collective-permute-done.22), channel_id=1, source_target_pairs={{0,8},{4,12},{8,0},{12,4},{16,24},{20,28},{24,16},{28,20},{1,9},{5... | collective-permute-start | bytes 442376 | tf_op jit(solution)/shard_map/ppermute | solution.py:19
  69.0 6.5 %collective-permute-start.24 = (bf16[32,2304]{1,0:T(8,128)(2,1)S(1)}, bf16[32,2304]{1,0:T(8,128)(2,1)S(1)}, u32[]{:S(2)}, u32[]{:S(2)}) collective-permute-start(bf16[32,2304]{1,0:T(8,128)(2,1)S(1)} %collective-permute-done.22), channel_id=1, source_target_pairs={{0,16},{4,20},{8,24},{12,28},{16,0},{20,4},{24,8},{28,12},{1,17},{... | collective-permute-start | bytes 442376 | tf_op jit(solution)/shard_map/ppermute | solution.py:19
  72.1 5.4 %collective-permute-start.30 = (bf16[128,2304]{1,0:T(8,128)(2,1)S(1)}, bf16[128,2304]{1,0:T(8,128)(2,1)S(1)}, u32[]{:S(2)}, u32[]{:S(2)}) collective-permute-start(bf16[128,2304]{1,0:T(8,128)(2,1)S(1)} %bitcast.63), channel_id=1, source_target_pairs={{0,4},{4,0},{8,12},{12,8},{16,20},{20,16},{24,28},{28,24},{1,5},{5... | collective-permute-start | bytes 1769480 | tf_op jit(solution)/shard_map/ppermute | solution.py:19
  74.8 3.2 %collective-permute-start.32 = (bf16[128,2304]{1,0:T(8,128)(2,1)S(1)}, bf16[128,2304]{1,0:T(8,128)(2,1)S(1)}, u32[]{:S(2)}, u32[]{:S(2)}) collective-permute-start(bf16[128,2304]{1,0:T(8,128)(2,1)S(1)} %convolution_convert_fusion), channel_id=1, source_target_pairs={{0,4},{4,0},{8,12},{12,8},{16,20},{20,16},{24,28},{28,24},{1,5},{5... | collective-permute-start | bytes 1769480 | tf_op jit(solution)/shard_map/ppermute | solution.py:19
  75.6 6.5 %collective-permute-start.26 = (bf16[128,2304]{1,0:T(8,128)(2,1)S(1)}, bf16[128,2304]{1,0:T(8,128)(2,1)S(1)}, u32[]{:S(2)}, u32[]{:S(2)}) collective-permute-start(bf16[128,2304]{1,0:T(8,128)(2,1)S(1)} %bitcast.61), channel_id=1, source_target_pairs={{0,4},{4,0},{8,12},{12,8},{16,20},{20,16},{24,28},{28,24},{1,5},{5... | collective-permute-start | bytes 1769480 | tf_op jit(solution)/shard_map/ppermute | solution.py:19
  77.0 9.5 %collective-permute-start.31 = (bf16[128,2304]{1,0:T(8,128)(2,1)S(1)}, bf16[128,2304]{1,0:T(8,128)(2,1)S(1)}, u32[]{:S(2)}, u32[]{:S(2)}) collective-permute-start(bf16[128,2304]{1,0:T(8,128)(2,1)S(1)} %convolution_convert_fusion.1), channel_id=1, source_target_pairs={{0,4},{4,0},{8,12},{12,8},{16,20},{20,16},{24,28},{28,24},{1,5},{5... | collective-permute-start | bytes 1769480 | tf_op jit(solution)/shard_map/ppermute | solution.py:19
  78.6 6.8 %collective-permute-start.33 = (bf16[32,2304]{1,0:T(8,128)(2,1)S(1)}, bf16[32,2304]{1,0:T(8,128)(2,1)S(1)}, u32[]{:S(2)}, u32[]{:S(2)}) collective-permute-start(bf16[32,2304]{1,0:T(8,128)(2,1)S(1)} %get-tuple-element.59), channel_id=1, source_target_pairs={{0,8},{4,12},{8,0},{12,4},{16,24},{20,28},{24,16},{28,20},{1,9},{5... | collective-permute-start | bytes 442376 | tf_op jit(solution)/shard_map/ppermute | solution.py:19
  79.8 10.8 %collective-permute-start.37 = (bf16[32,2304]{1,0:T(8,128)(2,1)S(1)}, bf16[32,2304]{1,0:T(8,128)(2,1)S(1)}, u32[]{:S(2)}, u32[]{:S(2)}) collective-permute-start(bf16[32,2304]{1,0:T(8,128)(2,1)S(1)} %get-tuple-element.61), channel_id=1, source_target_pairs={{0,16},{4,20},{8,24},{12,28},{16,0},{20,4},{24,8},{28,12},{1,17},{... | collective-permute-start | bytes 442376 | tf_op jit(solution)/shard_map/ppermute | solution.py:19
  80.5 10.1 %collective-permute-start.38 = (bf16[32,2304]{1,0:T(8,128)(2,1)S(1)}, bf16[32,2304]{1,0:T(8,128)(2,1)S(1)}, u32[]{:S(2)}, u32[]{:S(2)}) collective-permute-start(bf16[32,2304]{1,0:T(8,128)(2,1)S(1)} %get-tuple-element.60), channel_id=1, source_target_pairs={{0,24},{4,28},{8,16},{12,20},{16,8},{20,12},{24,0},{28,4},{1,25},{... | collective-permute-start | bytes 442376 | tf_op jit(solution)/shard_map/ppermute | solution.py:19
  87.0 15.3 %copy-start.11 = (f32[2304]{0:T(1024)S(1)}, f32[2304]{0:T(1024)}, u32[]{:S(2)}) copy-start(f32[2304]{0:T(1024)} %param.25) | copy-start | bytes 27652
  87.1 6.2 %collective-permute-start.34 = (bf16[32,2304]{1,0:T(8,128)(2,1)S(1)}, bf16[32,2304]{1,0:T(8,128)(2,1)S(1)}, u32[]{:S(2)}, u32[]{:S(2)}) collective-permute-start(bf16[32,2304]{1,0:T(8,128)(2,1)S(1)} %get-tuple-element.56), channel_id=1, source_target_pairs={{0,8},{4,12},{8,0},{12,4},{16,24},{20,28},{24,16},{28,20},{1,9},{5... | collective-permute-start | bytes 442376 | tf_op jit(solution)/shard_map/ppermute | solution.py:19
  88.3 5.5 %collective-permute-start.35 = (bf16[32,2304]{1,0:T(8,128)(2,1)S(1)}, bf16[32,2304]{1,0:T(8,128)(2,1)S(1)}, u32[]{:S(2)}, u32[]{:S(2)}) collective-permute-start(bf16[32,2304]{1,0:T(8,128)(2,1)S(1)} %get-tuple-element.58), channel_id=1, source_target_pairs={{0,16},{4,20},{8,24},{12,28},{16,0},{20,4},{24,8},{28,12},{1,17},{... | collective-permute-start | bytes 442376 | tf_op jit(solution)/shard_map/ppermute | solution.py:19
  88.7 6.6 %collective-permute-start.36 = (bf16[32,2304]{1,0:T(8,128)(2,1)S(1)}, bf16[32,2304]{1,0:T(8,128)(2,1)S(1)}, u32[]{:S(2)}, u32[]{:S(2)}) collective-permute-start(bf16[32,2304]{1,0:T(8,128)(2,1)S(1)} %get-tuple-element.57), channel_id=1, source_target_pairs={{0,24},{4,28},{8,16},{12,20},{16,8},{20,12},{24,0},{28,4},{1,25},{... | collective-permute-start | bytes 442376 | tf_op jit(solution)/shard_map/ppermute | solution.py:19
  90.7 5.2 %collective-permute-start.39 = (bf16[32,2304]{1,0:T(8,128)(2,1)S(1)}, bf16[32,2304]{1,0:T(8,128)(2,1)S(1)}, u32[]{:S(2)}, u32[]{:S(2)}) collective-permute-start(bf16[32,2304]{1,0:T(8,128)(2,1)S(1)} %add_convert_fusion.2), channel_id=1, source_target_pairs={{0,1},{1,0},{2,3},{3,2},{4,5},{5,4},{6,7},{7,6},{8,9},{9,8},{10,11... | collective-permute-start | bytes 442376 | tf_op jit(solution)/shard_map/ppermute | solution.py:19
  96.0 6.3 %collective-permute-start.40 = (bf16[16,2304]{1,0:T(8,128)(2,1)S(1)}, bf16[16,2304]{1,0:T(8,128)(2,1)S(1)}, u32[]{:S(2)}, u32[]{:S(2)}) collective-permute-start(bf16[16,2304]{1,0:T(8,128)(2,1)S(1)} %fusion.9), channel_id=1, source_target_pairs={{0,2},{1,3},{2,0},{3,1},{4,6},{5,7},{6,4},{7,5},{8,10},{9,11},{10,... | collective-permute-start | bytes 221192 | tf_op jit(solution)/shard_map/ppermute | solution.py:19
  (8 other events, 22.6 us)

commit v14 on v12

--- a/solution.py
+++ b/solution.py
@@ -161,47 +161,53 @@
     )[0]
 
 
-def down_kernel(top, e, tile, feats, pairs, kind, scalars, hidden, down, table, *refs):
-    count = 1 if kind is None else 2 * kind[0]
+def down_kernel(top, e, tile, feats, pairs, chunk, scalars, hidden, down, table, *refs):
+    count = 1 if chunk is None else pairs
     more, outs = refs[:-count], refs[-count:]
-    size = hidden.shape[0] // pairs
-    own = size // feats
+    own = hidden.shape[0] // pairs // feats
+    if chunk is None:
+        blocks = [(p, f) for p in range(pairs) for f in range(feats)]
+    else:
+        side = jnp.bitwise_xor(scalars[1], chunk)
+        blocks = [(p, 2 * f + side) for p in range(pairs) for f in range(feats // 2)]
+
+    def rows_of(ref):
+        if chunk is None:
+            return ref[...]
+        starts = [pl.multiple_of((p * feats + f) * own, own) for p, f in blocks]
+        return jnp.concatenate([ref[pl.ds(start, own), :] for start in starts], axis=0)
+
     entries = []
-    for p in range(pairs):
-        for f in range(feats):
-            start = (jnp.bitwise_xor(scalars[2], f) * pairs + p) * own
-            entries.append(full(table[pl.ds(pl.multiple_of(start, own), own), :]))
+    for p, f in blocks:
+        start = (jnp.bitwise_xor(scalars[2], f) * pairs + p) * own
+        entries.append(full(table[pl.ds(pl.multiple_of(start, own), own), :]))
     entries = jnp.concatenate(entries, axis=0)
     lane = lax.broadcasted_iota(jnp.int32, entries.shape, 1)
     expert = (scalars[0] * down.shape[0] + e).astype(jnp.float32)
     chosen = jnp.where((entries == expert) & (lane < top), 1.0, 0.0)
     chosen = pltpu.roll(chosen, top, 1) + pltpu.roll(chosen, 2 * top, 1)
     scale = jnp.sum(chosen * entries, axis=1, keepdims=True)
+    rows = rows_of(hidden)
+    arrived = rows_of(more[0]) if more else None
+    size = outs[0].shape[0]
     for j in range(0, down.shape[2], tile):
         cut = slice(j, j + tile)
-        value = dot(hidden[...], down[e, :, cut]) * scale
+        value = dot(rows, down[e, :, cut]) * scale
         if more:
-            value += full(more[0][:, cut])
-        if kind is None:
-            outs[0][:, cut] = half(value)
-            continue
-        for p in range(pairs):
-            block = value[p * size : (p + 1) * size]
-            block = block.reshape(size // own // 2, 2, own, tile)
-            low, high = block[:, 0].reshape(-1, tile), block[:, 1].reshape(-1, tile)
-            outs[p][:, cut] = half(jnp.where(scalars[1] == 0, low, high))
-            outs[pairs + p][:, cut] = half(jnp.where(scalars[1] == 0, high, low))
-
-
-def run_down(hidden, down, e, scalars, table, top, feats, pairs, more=(), kind=None):
+            value += full(arrived[:, cut])
+        for p, out in enumerate(outs):
+            out[:, cut] = half(value[p * size : (p + 1) * size])
+
+
+def run_down(hidden, down, e, scalars, table, top, feats, pairs, more=(), chunk=None):
     rows, units = hidden.shape
     width = down.shape[2]
     tile = 256 if width % 256 == 0 else 128
     outs = [((rows, width), jnp.bfloat16)]
-    if kind is not None:
-        outs = [((rows // kind[0] // 2, width), jnp.bfloat16)] * (2 * kind[0])
-    return call(
-        functools.partial(down_kernel, top, e, tile, feats, pairs, kind),
+    if chunk is not None:
+        outs = [((rows // pairs // 2, width), jnp.bfloat16)] * pairs
+    return call(
+        functools.partial(down_kernel, top, e, tile, feats, pairs, chunk),
         [scalars, hidden, down, table, *more],
         [SMEM_SPEC] + [VMEM_SPEC] * (3 + len(more)),
         outs,
@@ -265,10 +271,11 @@
         if e < local_experts[-1]:
             more = [arrived]
             arrived = run_down(hidden, expert_down, e, scalars, table_far, top, feats, pairs, more)[0]
-    blocks = run_down(
-        hidden, expert_down, e, scalars, table_far, top, feats, pairs, [arrived], (pairs, own)
-    )
-    blocks = [blocks[:pairs], blocks[pairs:]]
+    more = [arrived]
+    blocks = [
+        run_down(hidden, expert_down, e, scalars, table_far, top, feats, pairs, more, chunk)
+        for chunk in range(2)
+    ]
     blocks = [
         [mine[0]] + [swap(mine[p], "expert", 2 * p) for p in range(1, pairs)] for mine in blocks
     ]
@@ -306,7 +313,7 @@
         total = half(dot(features_far, decoder) + full(decoded) + zero)
         total = total.reshape(pairs, feats // 2 * own, width)
         blocks[chunk] = [total[0]] + [swap(total[p], "expert", 2 * p) for p in range(1, pairs)]
-        zero = 0.0 * full(blocks[chunk][1][0, 0])
+        zero = 0.0 * full(blocks[chunk][1][:1])
         both = jnp.stack([features_far, features_near])
         features[chunk] = both.reshape(2, pairs, feats // 2, 1, own, -1)
     arrived = swap(half(sum(full(block) for block in blocks[1])), "feat", feat_bits[0])

time: 105 us -> 102 us (0.971)
  waiting for transfers between devices: 31 us -> 29.1 us
    ppermute x41, waiting for transfers between devices: 31 us -> 29.1 us  [swap(): lax.ppermute(value, axis, [(i, i ^ r) for i in range(lax.axis_size(axis))])]
    pallas_call x7 -> x8, Pallas kernels: 14.7 us -> 15.5 us  [call(): pl.pallas_call(body, in_specs=specs, out_specs=[VMEM_SPEC] * len(outs), o...]
  transfers between devices with their start and end apart: 41 -> 41, of which waited for: 16 -> 15; matrix products, arithmetic and copies ran while one was open for 7% -> 6% of each run, Pallas kernels for 10% -> 12%
where the time goes in v14:
time: 102 us
  starting transfers between devices  46.1 us (45%)
  waiting for transfers between devices  29.1 us (29%)
  Pallas kernels  15.5 us (15%)
  matrix products  5.53 us (5%)
  local copies, waits for them, and re-layouts  2.94 us (3%)
  other arithmetic  1.39 us (1%)
  between operations  1.28 us (1%)
    ppermute x41, starting transfers between devices, swap(): lax.ppermute(value, axis, [(i, i ^ r) for i in range(lax.axis_size(axis))])  46.1 us
    ppermute x41, waiting for transfers between devices, swap(): lax.ppermute(value, axis, [(i, i ^ r) for i in range(lax.axis_size(axis))])  29.1 us
    pallas_call x8, Pallas kernels, call(): pl.pallas_call(body, in_specs=specs, out_specs=[VMEM_SPEC] * len(outs), o...  15.5 us
    dot_general x8, matrix products, dot(): return jnp.dot(a, b, preferred_element_type=jnp.float32)  5.53 us
    unnamed x59, local copies, waits for them, and re-layouts  2.85 us
  transfers between devices with their start and end apart: 41, of which 15 were waited for; matrix products, arithmetic and copies ran while one was open for 6% of the time, Pallas kernels for 12%

profile of v14, /device:TPU:0, one launch (start us, length us, event | category | flops | bytes accessed | tf_op | source)
XLA Modules:
  0.0 101.7 jit_solution(4631048183559215037)
XLA Ops:
  0.7 0.8 copy-done.4
  1.5 0.7 copy-done.5
  2.3 2.9 %collective-permute-start = (bf16[16,128]{1,0:T(8,128)(2,1)S(1)}, bf16[16,128]{1,0:T(8,128)(2,1)S(1)}, u32[]{:S(2)}, u32[]{:S(2)}) collective-permute-start(bf16[16,128]{1,0:T(8,128)(2,1)S(1)} %shard_map.140), channel_id=1, source_target_pairs={{0,8},{4,12},{8,0},{12,4},{16,24},{20,28},{24,16},{28,20},{1,9},{5... | collective-permute-start | bytes 12296 | tf_op jit(solution)/shard_map/ppermute | solution.py:19
  5.3 1.5 %collective-permute-start.1 = (bf16[16,128]{1,0:T(8,128)(2,1)S(1)}, bf16[16,128]{1,0:T(8,128)(2,1)S(1)}, u32[]{:S(2)}, u32[]{:S(2)}) collective-permute-start(bf16[16,128]{1,0:T(8,128)(2,1)S(1)} %shard_map.140), channel_id=1, source_target_pairs={{0,16},{4,20},{8,24},{12,28},{16,0},{20,4},{24,8},{28,12},{1,17},{... | collective-permute-start | bytes 12296 | tf_op jit(solution)/shard_map/ppermute | solution.py:19
  6.9 2.0 %collective-permute-start.3 = (bf16[64,2304]{1,0:T(8,128)(2,1)}, bf16[64,2304]{1,0:T(8,128)(2,1)S(1)}, u32[]{:S(2)}, u32[]{:S(2)}) collective-permute-start(bf16[64,2304]{1,0:T(8,128)(2,1)} %refs_0_), channel_id=1, source_target_pairs={{0,8},{4,12},{8,0},{12,4},{16,24},{20,28},{24,16},{28,20},{1,9},{5... | collective-permute-start | bytes 884744 | tf_op jit(solution)/shard_map/ppermute | solution.py:19
  8.9 1.5 %collective-permute-start.4 = (bf16[64,2304]{1,0:T(8,128)(2,1)}, bf16[64,2304]{1,0:T(8,128)(2,1)S(1)}, u32[]{:S(2)}, u32[]{:S(2)}) collective-permute-start(bf16[64,2304]{1,0:T(8,128)(2,1)} %refs_0_), channel_id=1, source_target_pairs={{0,16},{4,20},{8,24},{12,28},{16,0},{20,4},{24,8},{28,12},{1,17},{... | collective-permute-start | bytes 884744 | tf_op jit(solution)/shard_map/ppermute | solution.py:19
  10.4 0.9 collective-permute-done.2
  11.4 1.6 %collective-permute-start.10 = (bf16[64,128]{1,0:T(8,128)(2,1)S(1)}, bf16[64,128]{1,0:T(8,128)(2,1)S(1)}, u32[]{:S(2)}, u32[]{:S(2)}) collective-permute-start(bf16[64,128]{1,0:T(8,128)(2,1)S(1)} %pad_maximum_fusion.3), channel_id=1, source_target_pairs={{0,1},{1,0},{2,3},{3,2},{4,5},{5,4},{6,7},{7,6},{8,9},{9,8},{10,11... | collective-permute-start | bytes 49160 | tf_op jit(solution)/shard_map/ppermute | solution.py:19
  13.0 1.0 copy-done.6
  13.9 3.9 %shard_map.141 = (bf16[64,2304]{1,0:T(8,128)(2,1)S(1)}, bf16[1,2304,1024]{2,1,0:T(8,128)(2,1)S(1)}, bf16[1,2304,1024]{2,1,0:T(8,128)(2,1)S(1)}) custom-call(bf16[64,2304]{1,0:T(8,128)(2,1)S(1)} %copy-done.6, bf16[1,2304,1024]{2,1,0:T(8,128)(2,1)} %refs_1_.1, bf16[1,2304,1024]{2,1,0:T(8,128)(2,1)} %refs_2_.1), custom_call_target="tpu_custom_call" | custom-call | flops 2676326400 | bytes 19464192 | tf_op jit(solution)/shard_map/pallas_call | solution.py:49
  17.9 2.7 %collective-permute-start.11 = (bf16[128,128]{1,0:T(8,128)(2,1)S(1)}, bf16[128,128]{1,0:T(8,128)(2,1)S(1)}, u32[]{:S(2)}, u32[]{:S(2)}) collective-permute-start(bf16[128,128]{1,0:T(8,128)(2,1)S(1)} %pad_maximum_fusion.2), channel_id=1, source_target_pairs={{0,2},{1,3},{2,0},{3,1},{4,6},{5,7},{6,4},{7,5},{8,10},{9,11},{10,... | collective-permute-start | bytes 98312 | tf_op jit(solution)/shard_map/ppermute | solution.py:19
  20.5 2.5 %collective-permute-done.4.refs_2_ = bf16[64,2304]{1,0:T(8,128)(2,1)S(1)} collective-permute-done((bf16[64,2304]{1,0:T(8,128)(2,1)}, bf16[64,2304]{1,0:T(8,128)(2,1)S(1)}, u32[]{:S(2)}, u32[]{:S(2)}) %collective-permute-start.4) | collective-permute-done | bytes 294944 | tf_op jit(solution)/shard_map/ppermute | solution.py:19
  23.6 2.7 %shard_map.142.hidden = bf16[256,1024]{1,0:T(8,128)(2,1)S(1)} custom-call(bf16[64,2304]{1,0:T(8,128)(2,1)S(1)} %get-tuple-element.30.refs_0_, bf16[64,2304]{1,0:T(8,128)(2,1)S(1)} %collective-permute-done.3.refs_1_, bf16[64,2304]{1,0:T(8,128)(2,1)S(1)} %collective-permute-done.4.refs_2_, bf16[64,2304]{1,0:T(8,128)(2,1)S(1)} %collective-permute-done.5.refs_3_, ...), custom_call_target="tpu_custom_call" | custom-call | flops 2415919104 | bytes 9437184 | tf_op jit(solution)/shard_map/pallas_call | solution.py:49
  26.4 2.0 %shard_map.144 = bf16[256,2304]{1,0:T(8,128)(2,1)S(1)} custom-call(s32[3]{0:T(128)S(1)} %pad_add_fusion.scalars, bf16[256,1024]{1,0:T(8,128)(2,1)S(1)} %shard_map.142.hidden, bf16[1,1024,2304]{2,1,0:T(8,128)(2,1)S(1)} %bitcast.57, bf16[256,128]{1,0:T(8,128)(2,1)S(1)} %constant_dynamic-update-slice_fusion.table), custom_call_target="tpu_custom_call" | custom-call | flops 1207959552 | bytes 4718592 | tf_op jit(solution)/shard_map/pallas_call | solution.py:49
  28.9 2.7 %shard_map.143.hidden = bf16[256,1024]{1,0:T(8,128)(2,1)S(1)} custom-call(bf16[64,2304]{1,0:T(8,128)(2,1)S(1)} %collective-permute-done.6.refs_0_.x, bf16[64,2304]{1,0:T(8,128)(2,1)S(1)} %collective-permute-done.7.refs_1_, bf16[64,2304]{1,0:T(8,128)(2,1)S(1)} %collective-permute-done.8.refs_2_, bf16[64,2304]{1,0:T(8,128)(2,1)S(1)} %collective-permute-done.9.refs_3_, ...), custom_call_target="tpu_custom_call" | custom-call | flops 2415919104 | bytes 9437184 | tf_op jit(solution)/shard_map/pallas_call | solution.py:49
  31.6 1.3 %shard_map.146 = (bf16[32,2304]{1,0:T(8,128)(2,1)S(1)}, bf16[32,2304]{1,0:T(8,128)(2,1)S(1)}, bf16[32,2304]{1,0:T(8,128)(2,1)S(1)}, bf16[32,2304]{1,0:T(8,128)(2,1)S(1)}) custom-call(s32[3]{0:T(128)S(1)} %pad_add_fusion.scalars, bf16[256,1024]{1,0:T(8,128)(2,1)S(1)} %shard_map.143.hidden, bf16[1,1024,2304]{2,1,0:T(8,128)(2,1)S(1)} %bitcast.57, ...), custom_call_target="tpu_custom_call" | custom-call | flops 1207959552 | bytes 4718592 | tf_op jit(solution)/shard_map/pallas_call | solution.py:49
  33.0 1.5 %collective-permute-start.17 = (bf16[32,2304]{1,0:T(8,128)(2,1)S(1)}, bf16[32,2304]{1,0:T(8,128)(2,1)S(1)}, u32[]{:S(2)}, u32[]{:S(2)}) collective-permute-start(bf16[32,2304]{1,0:T(8,128)(2,1)S(1)} %get-tuple-element.44), channel_id=1, source_target_pairs={{0,24},{4,28},{8,16},{12,20},{16,8},{20,12},{24,0},{28,4},{1,25},{... | collective-permute-start | bytes 442376 | tf_op jit(solution)/shard_map/ppermute | solution.py:19
  34.5 1.5 %collective-permute-start.18 = (bf16[32,2304]{1,0:T(8,128)(2,1)S(1)}, bf16[32,2304]{1,0:T(8,128)(2,1)S(1)}, u32[]{:S(2)}, u32[]{:S(2)}) collective-permute-start(bf16[32,2304]{1,0:T(8,128)(2,1)S(1)} %get-tuple-element.48), channel_id=1, source_target_pairs={{0,8},{4,12},{8,0},{12,4},{16,24},{20,28},{24,16},{28,20},{1,9},{5... | collective-permute-start | bytes 442376 | tf_op jit(solution)/shard_map/ppermute | solution.py:19
  36.5 1.4 %shard_map.145 = (bf16[32,2304]{1,0:T(8,128)(2,1)S(1)}, bf16[32,2304]{1,0:T(8,128)(2,1)S(1)}, bf16[32,2304]{1,0:T(8,128)(2,1)S(1)}, bf16[32,2304]{1,0:T(8,128)(2,1)S(1)}) custom-call(s32[3]{0:T(128)S(1)} %pad_add_fusion.scalars, bf16[256,1024]{1,0:T(8,128)(2,1)S(1)} %shard_map.143.hidden, bf16[1,1024,2304]{2,1,0:T(8,128)(2,1)S(1)} %bitcast.57, ...), custom_call_target="tpu_custom_call" | custom-call | flops 1207959552 | bytes 4718592 | tf_op jit(solution)/shard_map/pallas_call | solution.py:49
  37.9 0.9 collective-permute-start.14
  38.8 1.2 %collective-permute-start.15 = (bf16[32,2304]{1,0:T(8,128)(2,1)S(1)}, bf16[32,2304]{1,0:T(8,128)(2,1)S(1)}, u32[]{:S(2)}, u32[]{:S(2)}) collective-permute-start(bf16[32,2304]{1,0:T(8,128)(2,1)S(1)} %get-tuple-element.42), channel_id=1, source_target_pairs={{0,16},{4,20},{8,24},{12,28},{16,0},{20,4},{24,8},{28,12},{1,17},{... | collective-permute-start | bytes 442376 | tf_op jit(solution)/shard_map/ppermute | solution.py:19
  39.9 0.7 collective-permute-done.17
  40.6 1.4 %collective-permute-start.16 = (bf16[32,2304]{1,0:T(8,128)(2,1)S(1)}, bf16[32,2304]{1,0:T(8,128)(2,1)S(1)}, u32[]{:S(2)}, u32[]{:S(2)}) collective-permute-start(bf16[32,2304]{1,0:T(8,128)(2,1)S(1)} %get-tuple-element.43), channel_id=1, source_target_pairs={{0,24},{4,28},{8,16},{12,20},{16,8},{20,12},{24,0},{28,4},{1,25},{... | collective-permute-start | bytes 442376 | tf_op jit(solution)/shard_map/ppermute | solution.py:19
  42.1 1.4 %shard_map.147 = (f32[32,2304]{1,0:T(8,128)S(1)}, f32[32,2304]{1,0:T(8,128)S(1)}) custom-call(s32[3]{0:T(128)S(1)} %pad_add_fusion.scalars, bf16[64,2304]{1,0:T(8,128)(2,1)S(1)} %collective-permute-done.6.refs_0_.x, bf16[2304,256]{1,0:T(8,128)(2,1)S(1)} %copy-done.1, bf16[2304,256]{1,0:T(8,128)(2,1)S(1)} %copy-done.2, bf16[256,2304]{1,0:T(8,128)(2,1)S(1)} %copy-done.3), custom_call_target="tpu_custom_call" | custom-call | flops 226492416 | bytes 3538944 | tf_op jit(solution)/shard_map/pallas_call | solution.py:49
  43.9 1.7 %collective-permute-start.20 = (bf16[32,2304]{1,0:T(8,128)(2,1)S(1)}, bf16[32,2304]{1,0:T(8,128)(2,1)S(1)}, u32[]{:S(2)}, u32[]{:S(2)}) collective-permute-start(bf16[32,2304]{1,0:T(8,128)(2,1)S(1)} %add_convert_fusion.5), channel_id=1, source_target_pairs={{0,1},{1,0},{2,3},{3,2},{4,5},{5,4},{6,7},{7,6},{8,9},{9,8},{10,11... | collective-permute-start | bytes 442376 | tf_op jit(solution)/shard_map/ppermute | solution.py:19
  45.6 1.4 %collective-permute-done.14 = bf16[32,2304]{1,0:T(8,128)(2,1)S(1)} collective-permute-done((bf16[32,2304]{1,0:T(8,128)(2,1)S(1)}, bf16[32,2304]{1,0:T(8,128)(2,1)S(1)}, u32[]{:S(2)}, u32[]{:S(2)}) %collective-permute-start.14) | collective-permute-done | bytes 147488 | tf_op jit(solution)/shard_map/ppermute | solution.py:19
  47.0 2.2 %collective-permute-done.16 = bf16[32,2304]{1,0:T(8,128)(2,1)S(1)} collective-permute-done((bf16[32,2304]{1,0:T(8,128)(2,1)S(1)}, bf16[32,2304]{1,0:T(8,128)(2,1)S(1)}, u32[]{:S(2)}, u32[]{:S(2)}) %collective-permute-start.16) | collective-permute-done | bytes 147488 | tf_op jit(solution)/shard_map/ppermute | solution.py:19
  49.4 2.7 %collective-permute-start.21 = (bf16[2,16,2304]{2,1,0:T(8,128)(2,1)S(1)}, bf16[2,16,2304]{2,1,0:T(8,128)(2,1)S(1)}, u32[]{:S(2)}, u32[]{:S(2)}) collective-permute-start(bf16[2,16,2304]{2,1,0:T(8,128)(2,1)S(1)} %bitcast.107), channel_id=1, source_target_pairs={{0,2},{1,3},{2,0},{3,1},{4,6},{5,7},{6,4},{7,5},{8,10},{9,11},{10,... | collective-permute-start | bytes 442376 | tf_op jit(solution)/shard_map/ppermute | solution.py:19
  52.0 6.5 %collective-permute-done.21 = bf16[2,16,2304]{2,1,0:T(8,128)(2,1)S(1)} collective-permute-done((bf16[2,16,2304]{2,1,0:T(8,128)(2,1)S(1)}, bf16[2,16,2304]{2,1,0:T(8,128)(2,1)S(1)}, u32[]{:S(2)}, u32[]{:S(2)}) %collective-permute-start.21) | collective-permute-done | bytes 147488 | tf_op jit(solution)/shard_map/ppermute | solution.py:19
  58.5 0.7 collective-permute-start.22
  59.2 1.6 %collective-permute-start.27 = (bf16[32,2304]{1,0:T(8,128)(2,1)S(1)}, bf16[32,2304]{1,0:T(8,128)(2,1)S(1)}, u32[]{:S(2)}, u32[]{:S(2)}) collective-permute-start(bf16[32,2304]{1,0:T(8,128)(2,1)S(1)} %bitcast.103), channel_id=1, source_target_pairs={{0,8},{4,12},{8,0},{12,4},{16,24},{20,28},{24,16},{28,20},{1,9},{5... | collective-permute-start | bytes 442376 | tf_op jit(solution)/shard_map/ppermute | solution.py:19
  61.3 2.5 %collective-permute-done.22 = bf16[32,2304]{1,0:T(8,128)(2,1)S(1)} collective-permute-done((bf16[32,2304]{1,0:T(8,128)(2,1)S(1)}, bf16[32,2304]{1,0:T(8,128)(2,1)S(1)}, u32[]{:S(2)}, u32[]{:S(2)}) %collective-permute-start.22) | collective-permute-done | bytes 147488 | tf_op jit(solution)/shard_map/ppermute | solution.py:19
  63.7 1.5 %collective-permute-start.29 = (bf16[32,2304]{1,0:T(8,128)(2,1)S(1)}, bf16[32,2304]{1,0:T(8,128)(2,1)S(1)}, u32[]{:S(2)}, u32[]{:S(2)}) collective-permute-start(bf16[32,2304]{1,0:T(8,128)(2,1)S(1)} %bitcast.105), channel_id=1, source_target_pairs={{0,24},{4,28},{8,16},{12,20},{16,8},{20,12},{24,0},{28,4},{1,25},{... | collective-permute-start | bytes 442376 | tf_op jit(solution)/shard_map/ppermute | solution.py:19
  65.2 1.4 %collective-permute-start.25 = (bf16[32,2304]{1,0:T(8,128)(2,1)S(1)}, bf16[32,2304]{1,0:T(8,128)(2,1)S(1)}, u32[]{:S(2)}, u32[]{:S(2)}) collective-permute-start(bf16[32,2304]{1,0:T(8,128)(2,1)S(1)} %collective-permute-done.22), channel_id=1, source_target_pairs={{0,24},{4,28},{8,16},{12,20},{16,8},{20,12},{24,0},{28,4},{1,25},{... | collective-permute-start | bytes 442376 | tf_op jit(solution)/shard_map/ppermute | solution.py:19
  66.6 1.6 %collective-permute-start.23 = (bf16[32,2304]{1,0:T(8,128)(2,1)S(1)}, bf16[32,2304]{1,0:T(8,128)(2,1)S(1)}, u32[]{:S(2)}, u32[]{:S(2)}) collective-permute-start(bf16[32,2304]{1,0:T(8,128)(2,1)S(1)} %collective-permute-done.22), channel_id=1, source_target_pairs={{0,8},{4,12},{8,0},{12,4},{16,24},{20,28},{24,16},{28,20},{1,9},{5... | collective-permute-start | bytes 442376 | tf_op jit(solution)/shard_map/ppermute | solution.py:19
  68.7 2.1 %collective-permute-done.28 = bf16[32,2304]{1,0:T(8,128)(2,1)S(1)} collective-permute-done((bf16[32,2304]{1,0:T(8,128)(2,1)S(1)}, bf16[32,2304]{1,0:T(8,128)(2,1)S(1)}, u32[]{:S(2)}, u32[]{:S(2)}) %collective-permute-start.28) | collective-permute-done | bytes 147488 | tf_op jit(solution)/shard_map/ppermute | solution.py:19
  71.6 2.1 %fusion.4 = bf16[128,512]{1,0:T(8,128)(2,1)S(1)} fusion(bf16[128,2304]{1,0:T(8,128)(2,1)S(1)} %bitcast.63, bf16[2304,512]{1,0:T(8,128)(2,1)} %param.22, f32[512]{0:T(512)S(1)} %copy-done.8), kind=kOutput, calls=%fused_computation.12 | convolution fusion | flops 302186496 | bytes 3082240 | tf_op jit(solution)/shard_map/dot_general | solution.py:23
  74.8 0.8 collective-permute-done.24
  78.3 1.4 %collective-permute-start.33 = (bf16[32,2304]{1,0:T(8,128)(2,1)S(1)}, bf16[32,2304]{1,0:T(8,128)(2,1)S(1)}, u32[]{:S(2)}, u32[]{:S(2)}) collective-permute-start(bf16[32,2304]{1,0:T(8,128)(2,1)S(1)} %get-tuple-element.57), channel_id=1, source_target_pairs={{0,8},{4,12},{8,0},{12,4},{16,24},{20,28},{24,16},{28,20},{1,9},{5... | collective-permute-start | bytes 442376 | tf_op jit(solution)/shard_map/ppermute | solution.py:19
  80.2 1.6 %collective-permute-start.38 = (bf16[32,2304]{1,0:T(8,128)(2,1)S(1)}, bf16[32,2304]{1,0:T(8,128)(2,1)S(1)}, u32[]{:S(2)}, u32[]{:S(2)}) collective-permute-start(bf16[32,2304]{1,0:T(8,128)(2,1)S(1)} %get-tuple-element.58), channel_id=1, source_target_pairs={{0,24},{4,28},{8,16},{12,20},{16,8},{20,12},{24,0},{28,4},{1,25},{... | collective-permute-start | bytes 442376 | tf_op jit(solution)/shard_map/ppermute | solution.py:19
  82.9 2.1 %collective-permute-done.33 = bf16[32,2304]{1,0:T(8,128)(2,1)S(1)} collective-permute-done((bf16[32,2304]{1,0:T(8,128)(2,1)S(1)}, bf16[32,2304]{1,0:T(8,128)(2,1)S(1)}, u32[]{:S(2)}, u32[]{:S(2)}) %collective-permute-start.33) | collective-permute-done | bytes 147488 | tf_op jit(solution)/shard_map/ppermute | solution.py:19
  85.6 1.5 %collective-permute-start.34 = (bf16[32,2304]{1,0:T(8,128)(2,1)S(1)}, bf16[32,2304]{1,0:T(8,128)(2,1)S(1)}, u32[]{:S(2)}, u32[]{:S(2)}) collective-permute-start(bf16[32,2304]{1,0:T(8,128)(2,1)S(1)} %get-tuple-element.54), channel_id=1, source_target_pairs={{0,8},{4,12},{8,0},{12,4},{16,24},{20,28},{24,16},{28,20},{1,9},{5... | collective-permute-start | bytes 442376 | tf_op jit(solution)/shard_map/ppermute | solution.py:19
  87.5 1.6 %collective-permute-start.36 = (bf16[32,2304]{1,0:T(8,128)(2,1)S(1)}, bf16[32,2304]{1,0:T(8,128)(2,1)S(1)}, u32[]{:S(2)}, u32[]{:S(2)}) collective-permute-start(bf16[32,2304]{1,0:T(8,128)(2,1)S(1)} %get-tuple-element.55), channel_id=1, source_target_pairs={{0,24},{4,28},{8,16},{12,20},{16,8},{20,12},{24,0},{28,4},{1,25},{... | collective-permute-start | bytes 442376 | tf_op jit(solution)/shard_map/ppermute | solution.py:19
  89.2 1.4 %collective-permute-start.39 = (bf16[32,2304]{1,0:T(8,128)(2,1)S(1)}, bf16[32,2304]{1,0:T(8,128)(2,1)S(1)}, u32[]{:S(2)}, u32[]{:S(2)}) collective-permute-start(bf16[32,2304]{1,0:T(8,128)(2,1)S(1)} %add_convert_fusion.2), channel_id=1, source_target_pairs={{0,1},{1,0},{2,3},{3,2},{4,5},{5,4},{6,7},{7,6},{8,9},{9,8},{10,11... | collective-permute-start | bytes 442376 | tf_op jit(solution)/shard_map/ppermute | solution.py:19
  90.6 1.4 %collective-permute-done.34 = bf16[32,2304]{1,0:T(8,128)(2,1)S(1)} collective-permute-done((bf16[32,2304]{1,0:T(8,128)(2,1)S(1)}, bf16[32,2304]{1,0:T(8,128)(2,1)S(1)}, u32[]{:S(2)}, u32[]{:S(2)}) %collective-permute-start.34) | collective-permute-done | bytes 147488 | tf_op jit(solution)/shard_map/ppermute | solution.py:19
  92.1 2.6 %collective-permute-done.35 = bf16[32,2304]{1,0:T(8,128)(2,1)S(1)} collective-permute-done((bf16[32,2304]{1,0:T(8,128)(2,1)S(1)}, bf16[32,2304]{1,0:T(8,128)(2,1)S(1)}, u32[]{:S(2)}, u32[]{:S(2)}) %collective-permute-start.35) | collective-permute-done | bytes 147488 | tf_op jit(solution)/shard_map/ppermute | solution.py:19
  94.8 3.9 %collective-permute-start.40 = (bf16[16,2304]{1,0:T(8,128)(2,1)S(1)}, bf16[16,2304]{1,0:T(8,128)(2,1)S(1)}, u32[]{:S(2)}, u32[]{:S(2)}) collective-permute-start(bf16[16,2304]{1,0:T(8,128)(2,1)S(1)} %fusion.9), channel_id=1, source_target_pairs={{0,2},{1,3},{2,0},{3,1},{4,6},{5,7},{6,4},{7,5},{8,10},{9,11},{10,... | collective-permute-start | bytes 221192 | tf_op jit(solution)/shard_map/ppermute | solution.py:19
  98.7 2.3 %collective-permute-done.40 = bf16[16,2304]{1,0:T(8,128)(2,1)S(1)} collective-permute-done((bf16[16,2304]{1,0:T(8,128)(2,1)S(1)}, bf16[16,2304]{1,0:T(8,128)(2,1)S(1)}, u32[]{:S(2)}, u32[]{:S(2)}) %collective-permute-start.40) | collective-permute-done | bytes 73760 | tf_op jit(solution)/shard_map/ppermute | solution.py:19
  (128 shorter events, 11.1 us)
Async XLA Ops:
  0.6 73.1 %copy-start = (bf16[512,2304]{1,0:T(8,128)(2,1)S(1)}, bf16[512,2304]{1,0:T(8,128)(2,1)}, u32[]{:S(2)}) copy-start(bf16[512,2304]{1,0:T(8,128)(2,1)} %param.24) | copy-start | bytes 7077892
  2.3 4.5 %collective-permute-start = (bf16[16,128]{1,0:T(8,128)(2,1)S(1)}, bf16[16,128]{1,0:T(8,128)(2,1)S(1)}, u32[]{:S(2)}, u32[]{:S(2)}) collective-permute-start(bf16[16,128]{1,0:T(8,128)(2,1)S(1)} %shard_map.140), channel_id=1, source_target_pairs={{0,8},{4,12},{8,0},{12,4},{16,24},{20,28},{24,16},{28,20},{1,9},{5... | collective-permute-start | bytes 12296 | tf_op jit(solution)/shard_map/ppermute | solution.py:19
  5.3 5.1 %collective-permute-start.1 = (bf16[16,128]{1,0:T(8,128)(2,1)S(1)}, bf16[16,128]{1,0:T(8,128)(2,1)S(1)}, u32[]{:S(2)}, u32[]{:S(2)}) collective-permute-start(bf16[16,128]{1,0:T(8,128)(2,1)S(1)} %shard_map.140), channel_id=1, source_target_pairs={{0,16},{4,20},{8,24},{12,28},{16,0},{20,4},{24,8},{28,12},{1,17},{... | collective-permute-start | bytes 12296 | tf_op jit(solution)/shard_map/ppermute | solution.py:19
  6.8 4.6 %collective-permute-start.2 = (bf16[16,128]{1,0:T(8,128)(2,1)S(1)}, bf16[16,128]{1,0:T(8,128)(2,1)S(1)}, u32[]{:S(2)}, u32[]{:S(2)}) collective-permute-start(bf16[16,128]{1,0:T(8,128)(2,1)S(1)} %shard_map.140), channel_id=1, source_target_pairs={{0,24},{4,28},{8,16},{12,20},{16,8},{20,12},{24,0},{28,4},{1,25},{... | collective-permute-start | bytes 12296 | tf_op jit(solution)/shard_map/ppermute | solution.py:19
  6.9 13.6 %collective-permute-start.3 = (bf16[64,2304]{1,0:T(8,128)(2,1)}, bf16[64,2304]{1,0:T(8,128)(2,1)S(1)}, u32[]{:S(2)}, u32[]{:S(2)}) collective-permute-start(bf16[64,2304]{1,0:T(8,128)(2,1)} %refs_0_), channel_id=1, source_target_pairs={{0,8},{4,12},{8,0},{12,4},{16,24},{20,28},{24,16},{28,20},{1,9},{5... | collective-permute-start | bytes 884744 | tf_op jit(solution)/shard_map/ppermute | solution.py:19
  8.9 14.2 %collective-permute-start.4 = (bf16[64,2304]{1,0:T(8,128)(2,1)}, bf16[64,2304]{1,0:T(8,128)(2,1)S(1)}, u32[]{:S(2)}, u32[]{:S(2)}) collective-permute-start(bf16[64,2304]{1,0:T(8,128)(2,1)} %refs_0_), channel_id=1, source_target_pairs={{0,16},{4,20},{8,24},{12,28},{16,0},{20,4},{24,8},{28,12},{1,17},{... | collective-permute-start | bytes 884744 | tf_op jit(solution)/shard_map/ppermute | solution.py:19
  10.4 12.7 %collective-permute-start.5 = (bf16[64,2304]{1,0:T(8,128)(2,1)}, bf16[64,2304]{1,0:T(8,128)(2,1)S(1)}, u32[]{:S(2)}, u32[]{:S(2)}) collective-permute-start(bf16[64,2304]{1,0:T(8,128)(2,1)} %refs_0_), channel_id=1, source_target_pairs={{0,24},{4,28},{8,16},{12,20},{16,8},{20,12},{24,0},{28,4},{1,25},{... | collective-permute-start | bytes 884744 | tf_op jit(solution)/shard_map/ppermute | solution.py:19
  10.4 15.9 %collective-permute-start.6 = (bf16[64,2304]{1,0:T(8,128)(2,1)}, bf16[64,2304]{1,0:T(8,128)(2,1)S(1)}, u32[]{:S(2)}, u32[]{:S(2)}) collective-permute-start(bf16[64,2304]{1,0:T(8,128)(2,1)} %refs_0_), channel_id=1, source_target_pairs={{0,4},{4,0},{8,12},{12,8},{16,20},{20,16},{24,28},{28,24},{1,5},{5... | collective-permute-start | bytes 884744 | tf_op jit(solution)/shard_map/ppermute | solution.py:19
  11.4 6.5 %collective-permute-start.10 = (bf16[64,128]{1,0:T(8,128)(2,1)S(1)}, bf16[64,128]{1,0:T(8,128)(2,1)S(1)}, u32[]{:S(2)}, u32[]{:S(2)}) collective-permute-start(bf16[64,128]{1,0:T(8,128)(2,1)S(1)} %pad_maximum_fusion.3), channel_id=1, source_target_pairs={{0,1},{1,0},{2,3},{3,2},{4,5},{5,4},{6,7},{7,6},{8,9},{9,8},{10,11... | collective-permute-start | bytes 49160 | tf_op jit(solution)/shard_map/ppermute | solution.py:19
  13.9 12.4 %slice-start = ((s8[4718592]{0:T(1024)(128)(4,1)}), s8[524288]{0:T(1024)(128)(4,1)S(1)}, s32[]{:S(2)}) async-start(s8[4718592]{0:T(1024)(128)(4,1)} %bitcast.56), calls=%async_computation | async-start | bytes 1048576
  17.9 5.7 %collective-permute-start.11 = (bf16[128,128]{1,0:T(8,128)(2,1)S(1)}, bf16[128,128]{1,0:T(8,128)(2,1)S(1)}, u32[]{:S(2)}, u32[]{:S(2)}) collective-permute-start(bf16[128,128]{1,0:T(8,128)(2,1)S(1)} %pad_maximum_fusion.2), channel_id=1, source_target_pairs={{0,2},{1,3},{2,0},{3,1},{4,6},{5,7},{6,4},{7,5},{8,10},{9,11},{10,... | collective-permute-start | bytes 98312 | tf_op jit(solution)/shard_map/ppermute | solution.py:19
  20.5 5.8 %collective-permute-start.7 = (bf16[64,2304]{1,0:T(8,128)(2,1)S(1)}, bf16[64,2304]{1,0:T(8,128)(2,1)S(1)}, u32[]{:S(2)}, u32[]{:S(2)}) collective-permute-start(bf16[64,2304]{1,0:T(8,128)(2,1)S(1)} %collective-permute-done.3.refs_1_), channel_id=1, source_target_pairs={{0,4},{4,0},{8,12},{12,8},{16,20},{20,16},{24,28},{28,24},{1,5},{5... | collective-permute-start | bytes 884744 | tf_op jit(solution)/shard_map/ppermute | solution.py:19
  23.1 3.2 %collective-permute-start.8 = (bf16[64,2304]{1,0:T(8,128)(2,1)S(1)}, bf16[64,2304]{1,0:T(8,128)(2,1)S(1)}, u32[]{:S(2)}, u32[]{:S(2)}) collective-permute-start(bf16[64,2304]{1,0:T(8,128)(2,1)S(1)} %collective-permute-done.4.refs_2_), channel_id=1, source_target_pairs={{0,4},{4,0},{8,12},{12,8},{16,20},{20,16},{24,28},{28,24},{1,5},{5... | collective-permute-start | bytes 884744 | tf_op jit(solution)/shard_map/ppermute | solution.py:19
  23.1 3.2 %collective-permute-start.9 = (bf16[64,2304]{1,0:T(8,128)(2,1)S(1)}, bf16[64,2304]{1,0:T(8,128)(2,1)S(1)}, u32[]{:S(2)}, u32[]{:S(2)}) collective-permute-start(bf16[64,2304]{1,0:T(8,128)(2,1)S(1)} %collective-permute-done.5.refs_3_), channel_id=1, source_target_pairs={{0,4},{4,0},{8,12},{12,8},{16,20},{20,16},{24,28},{28,24},{1,5},{5... | collective-permute-start | bytes 884744 | tf_op jit(solution)/shard_map/ppermute | solution.py:19
  28.3 3.3 %collective-permute-start.13 = (bf16[256,2304]{1,0:T(8,128)(2,1)S(1)}, bf16[256,2304]{1,0:T(8,128)(2,1)S(1)}, u32[]{:S(2)}, u32[]{:S(2)}) collective-permute-start(bf16[256,2304]{1,0:T(8,128)(2,1)S(1)} %shard_map.144), channel_id=1, source_target_pairs={{0,4},{4,0},{8,12},{12,8},{16,20},{20,16},{24,28},{28,24},{1,5},{5... | collective-permute-start | bytes 3538952 | tf_op jit(solution)/shard_map/ppermute | solution.py:19
  28.4 3.2 %collective-permute-start.12 = (bf16[256,128]{1,0:T(8,128)(2,1)S(1)}, bf16[256,128]{1,0:T(8,128)(2,1)S(1)}, u32[]{:S(2)}, u32[]{:S(2)}) collective-permute-start(bf16[256,128]{1,0:T(8,128)(2,1)S(1)} %constant_dynamic-update-slice_fusion.table), channel_id=1, source_target_pairs={{0,4},{4,0},{8,12},{12,8},{16,20},{20,16},{24,28},{28,24},{1,5},{5... | collective-permute-start | bytes 196616 | tf_op jit(solution)/shard_map/ppermute | solution.py:19
  33.0 7.7 %collective-permute-start.17 = (bf16[32,2304]{1,0:T(8,128)(2,1)S(1)}, bf16[32,2304]{1,0:T(8,128)(2,1)S(1)}, u32[]{:S(2)}, u32[]{:S(2)}) collective-permute-start(bf16[32,2304]{1,0:T(8,128)(2,1)S(1)} %get-tuple-element.44), channel_id=1, source_target_pairs={{0,24},{4,28},{8,16},{12,20},{16,8},{20,12},{24,0},{28,4},{1,25},{... | collective-permute-start | bytes 442376 | tf_op jit(solution)/shard_map/ppermute | solution.py:19
  34.5 9.4 %collective-permute-start.18 = (bf16[32,2304]{1,0:T(8,128)(2,1)S(1)}, bf16[32,2304]{1,0:T(8,128)(2,1)S(1)}, u32[]{:S(2)}, u32[]{:S(2)}) collective-permute-start(bf16[32,2304]{1,0:T(8,128)(2,1)S(1)} %get-tuple-element.48), channel_id=1, source_target_pairs={{0,8},{4,12},{8,0},{12,4},{16,24},{20,28},{24,16},{28,20},{1,9},{5... | collective-permute-start | bytes 442376 | tf_op jit(solution)/shard_map/ppermute | solution.py:19
  36.0 6.1 %copy-start.1 = (bf16[2304,256]{1,0:T(8,128)(2,1)S(1)}, bf16[2304,256]{1,0:T(8,128)(2,1)}, u32[]{:S(2)}) copy-start(bf16[2304,256]{1,0:T(8,128)(2,1)} %gate.1) | copy-start | bytes 3538948
  36.0 6.1 %copy-start.2 = (bf16[2304,256]{1,0:T(8,128)(2,1)S(1)}, bf16[2304,256]{1,0:T(8,128)(2,1)}, u32[]{:S(2)}) copy-start(bf16[2304,256]{1,0:T(8,128)(2,1)} %up.1) | copy-start | bytes 3538948
  36.0 6.1 %copy-start.3 = (bf16[256,2304]{1,0:T(8,128)(2,1)S(1)}, bf16[256,2304]{1,0:T(8,128)(2,1)}, u32[]{:S(2)}) copy-start(bf16[256,2304]{1,0:T(8,128)(2,1)} %down.7) | copy-start | bytes 3538948
  36.0 7.9 %collective-permute-start.19 = (bf16[32,2304]{1,0:T(8,128)(2,1)S(1)}, bf16[32,2304]{1,0:T(8,128)(2,1)S(1)}, u32[]{:S(2)}, u32[]{:S(2)}) collective-permute-start(bf16[32,2304]{1,0:T(8,128)(2,1)S(1)} %get-tuple-element.49), channel_id=1, source_target_pairs={{0,16},{4,20},{8,24},{12,28},{16,0},{20,4},{24,8},{28,12},{1,17},{... | collective-permute-start | bytes 442376 | tf_op jit(solution)/shard_map/ppermute | solution.py:19
  37.9 9.1 %collective-permute-start.14 = (bf16[32,2304]{1,0:T(8,128)(2,1)S(1)}, bf16[32,2304]{1,0:T(8,128)(2,1)S(1)}, u32[]{:S(2)}, u32[]{:S(2)}) collective-permute-start(bf16[32,2304]{1,0:T(8,128)(2,1)S(1)} %get-tuple-element.41), channel_id=1, source_target_pairs={{0,8},{4,12},{8,0},{12,4},{16,24},{20,28},{24,16},{28,20},{1,9},{5... | collective-permute-start | bytes 442376 | tf_op jit(solution)/shard_map/ppermute | solution.py:19
  38.8 8.2 %collective-permute-start.15 = (bf16[32,2304]{1,0:T(8,128)(2,1)S(1)}, bf16[32,2304]{1,0:T(8,128)(2,1)S(1)}, u32[]{:S(2)}, u32[]{:S(2)}) collective-permute-start(bf16[32,2304]{1,0:T(8,128)(2,1)S(1)} %get-tuple-element.42), channel_id=1, source_target_pairs={{0,16},{4,20},{8,24},{12,28},{16,0},{20,4},{24,8},{28,12},{1,17},{... | collective-permute-start | bytes 442376 | tf_op jit(solution)/shard_map/ppermute | solution.py:19
  40.6 8.6 %collective-permute-start.16 = (bf16[32,2304]{1,0:T(8,128)(2,1)S(1)}, bf16[32,2304]{1,0:T(8,128)(2,1)S(1)}, u32[]{:S(2)}, u32[]{:S(2)}) collective-permute-start(bf16[32,2304]{1,0:T(8,128)(2,1)S(1)} %get-tuple-element.43), channel_id=1, source_target_pairs={{0,24},{4,28},{8,16},{12,20},{16,8},{20,12},{24,0},{28,4},{1,25},{... | collective-permute-start | bytes 442376 | tf_op jit(solution)/shard_map/ppermute | solution.py:19
  43.5 28.1 %copy-start.8 = (f32[512]{0:T(512)S(1)}, f32[512]{0:T(512)}, u32[]{:S(2)}) copy-start(f32[512]{0:T(512)} %param.23) | copy-start | bytes 6148
  43.9 5.3 %collective-permute-start.20 = (bf16[32,2304]{1,0:T(8,128)(2,1)S(1)}, bf16[32,2304]{1,0:T(8,128)(2,1)S(1)}, u32[]{:S(2)}, u32[]{:S(2)}) collective-permute-start(bf16[32,2304]{1,0:T(8,128)(2,1)S(1)} %add_convert_fusion.5), channel_id=1, source_target_pairs={{0,1},{1,0},{2,3},{3,2},{4,5},{5,4},{6,7},{7,6},{8,9},{9,8},{10,11... | collective-permute-start | bytes 442376 | tf_op jit(solution)/shard_map/ppermute | solution.py:19
  49.4 9.1 %collective-permute-start.21 = (bf16[2,16,2304]{2,1,0:T(8,128)(2,1)S(1)}, bf16[2,16,2304]{2,1,0:T(8,128)(2,1)S(1)}, u32[]{:S(2)}, u32[]{:S(2)}) collective-permute-start(bf16[2,16,2304]{2,1,0:T(8,128)(2,1)S(1)} %bitcast.107), channel_id=1, source_target_pairs={{0,2},{1,3},{2,0},{3,1},{4,6},{5,7},{6,4},{7,5},{8,10},{9,11},{10,... | collective-permute-start | bytes 442376 | tf_op jit(solution)/shard_map/ppermute | solution.py:19
  58.5 5.2 %collective-permute-start.22 = (bf16[32,2304]{1,0:T(8,128)(2,1)S(1)}, bf16[32,2304]{1,0:T(8,128)(2,1)S(1)}, u32[]{:S(2)}, u32[]{:S(2)}) collective-permute-start(bf16[32,2304]{1,0:T(8,128)(2,1)S(1)} %bitcast.102), channel_id=1, source_target_pairs={{0,1},{1,0},{2,3},{3,2},{4,5},{5,4},{6,7},{7,6},{8,9},{9,8},{10,11... | collective-permute-start | bytes 442376 | tf_op jit(solution)/shard_map/ppermute | solution.py:19
  59.2 9.0 %collective-permute-start.27 = (bf16[32,2304]{1,0:T(8,128)(2,1)S(1)}, bf16[32,2304]{1,0:T(8,128)(2,1)S(1)}, u32[]{:S(2)}, u32[]{:S(2)}) collective-permute-start(bf16[32,2304]{1,0:T(8,128)(2,1)S(1)} %bitcast.103), channel_id=1, source_target_pairs={{0,8},{4,12},{8,0},{12,4},{16,24},{20,28},{24,16},{28,20},{1,9},{5... | collective-permute-start | bytes 442376 | tf_op jit(solution)/shard_map/ppermute | solution.py:19
  60.9 9.9 %collective-permute-start.28 = (bf16[32,2304]{1,0:T(8,128)(2,1)S(1)}, bf16[32,2304]{1,0:T(8,128)(2,1)S(1)}, u32[]{:S(2)}, u32[]{:S(2)}) collective-permute-start(bf16[32,2304]{1,0:T(8,128)(2,1)S(1)} %bitcast.104), channel_id=1, source_target_pairs={{0,16},{4,20},{8,24},{12,28},{16,0},{20,4},{24,8},{28,12},{1,17},{... | collective-permute-start | bytes 442376 | tf_op jit(solution)/shard_map/ppermute | solution.py:19
  63.7 7.7 %collective-permute-start.29 = (bf16[32,2304]{1,0:T(8,128)(2,1)S(1)}, bf16[32,2304]{1,0:T(8,128)(2,1)S(1)}, u32[]{:S(2)}, u32[]{:S(2)}) collective-permute-start(bf16[32,2304]{1,0:T(8,128)(2,1)S(1)} %bitcast.105), channel_id=1, source_target_pairs={{0,24},{4,28},{8,16},{12,20},{16,8},{20,12},{24,0},{28,4},{1,25},{... | collective-permute-start | bytes 442376 | tf_op jit(solution)/shard_map/ppermute | solution.py:19
  65.2 9.6 %collective-permute-start.25 = (bf16[32,2304]{1,0:T(8,128)(2,1)S(1)}, bf16[32,2304]{1,0:T(8,128)(2,1)S(1)}, u32[]{:S(2)}, u32[]{:S(2)}) collective-permute-start(bf16[32,2304]{1,0:T(8,128)(2,1)S(1)} %collective-permute-done.22), channel_id=1, source_target_pairs={{0,24},{4,28},{8,16},{12,20},{16,8},{20,12},{24,0},{28,4},{1,25},{... | collective-permute-start | bytes 442376 | tf_op jit(solution)/shard_map/ppermute | solution.py:19
  66.6 8.2 %collective-permute-start.23 = (bf16[32,2304]{1,0:T(8,128)(2,1)S(1)}, bf16[32,2304]{1,0:T(8,128)(2,1)S(1)}, u32[]{:S(2)}, u32[]{:S(2)}) collective-permute-start(bf16[32,2304]{1,0:T(8,128)(2,1)S(1)} %collective-permute-done.22), channel_id=1, source_target_pairs={{0,8},{4,12},{8,0},{12,4},{16,24},{20,28},{24,16},{28,20},{1,9},{5... | collective-permute-start | bytes 442376 | tf_op jit(solution)/shard_map/ppermute | solution.py:19
  68.3 7.3 %collective-permute-start.24 = (bf16[32,2304]{1,0:T(8,128)(2,1)S(1)}, bf16[32,2304]{1,0:T(8,128)(2,1)S(1)}, u32[]{:S(2)}, u32[]{:S(2)}) collective-permute-start(bf16[32,2304]{1,0:T(8,128)(2,1)S(1)} %collective-permute-done.22), channel_id=1, source_target_pairs={{0,16},{4,20},{8,24},{12,28},{16,0},{20,4},{24,8},{28,12},{1,17},{... | collective-permute-start | bytes 442376 | tf_op jit(solution)/shard_map/ppermute | solution.py:19
  71.5 5.8 %collective-permute-start.30 = (bf16[128,2304]{1,0:T(8,128)(2,1)S(1)}, bf16[128,2304]{1,0:T(8,128)(2,1)S(1)}, u32[]{:S(2)}, u32[]{:S(2)}) collective-permute-start(bf16[128,2304]{1,0:T(8,128)(2,1)S(1)} %bitcast.62), channel_id=1, source_target_pairs={{0,4},{4,0},{8,12},{12,8},{16,20},{20,16},{24,28},{28,24},{1,5},{5... | collective-permute-start | bytes 1769480 | tf_op jit(solution)/shard_map/ppermute | solution.py:19
  74.2 3.5 %collective-permute-start.32 = (bf16[128,2304]{1,0:T(8,128)(2,1)S(1)}, bf16[128,2304]{1,0:T(8,128)(2,1)S(1)}, u32[]{:S(2)}, u32[]{:S(2)}) collective-permute-start(bf16[128,2304]{1,0:T(8,128)(2,1)S(1)} %convolution_convert_fusion), channel_id=1, source_target_pairs={{0,4},{4,0},{8,12},{12,8},{16,20},{20,16},{24,28},{28,24},{1,5},{5... | collective-permute-start | bytes 1769480 | tf_op jit(solution)/shard_map/ppermute | solution.py:19
  75.6 6.2 %collective-permute-start.26 = (bf16[128,2304]{1,0:T(8,128)(2,1)S(1)}, bf16[128,2304]{1,0:T(8,128)(2,1)S(1)}, u32[]{:S(2)}, u32[]{:S(2)}) collective-permute-start(bf16[128,2304]{1,0:T(8,128)(2,1)S(1)} %bitcast.60), channel_id=1, source_target_pairs={{0,4},{4,0},{8,12},{12,8},{16,20},{20,16},{24,28},{28,24},{1,5},{5... | collective-permute-start | bytes 1769480 | tf_op jit(solution)/shard_map/ppermute | solution.py:19
  76.7 8.3 %collective-permute-start.31 = (bf16[128,2304]{1,0:T(8,128)(2,1)S(1)}, bf16[128,2304]{1,0:T(8,128)(2,1)S(1)}, u32[]{:S(2)}, u32[]{:S(2)}) collective-permute-start(bf16[128,2304]{1,0:T(8,128)(2,1)S(1)} %convolution_convert_fusion.1), channel_id=1, source_target_pairs={{0,4},{4,0},{8,12},{12,8},{16,20},{20,16},{24,28},{28,24},{1,5},{5... | collective-permute-start | bytes 1769480 | tf_op jit(solution)/shard_map/ppermute | solution.py:19
  78.3 6.7 %collective-permute-start.33 = (bf16[32,2304]{1,0:T(8,128)(2,1)S(1)}, bf16[32,2304]{1,0:T(8,128)(2,1)S(1)}, u32[]{:S(2)}, u32[]{:S(2)}) collective-permute-start(bf16[32,2304]{1,0:T(8,128)(2,1)S(1)} %get-tuple-element.57), channel_id=1, source_target_pairs={{0,8},{4,12},{8,0},{12,4},{16,24},{20,28},{24,16},{28,20},{1,9},{5... | collective-permute-start | bytes 442376 | tf_op jit(solution)/shard_map/ppermute | solution.py:19
  79.7 9.4 %collective-permute-start.37 = (bf16[32,2304]{1,0:T(8,128)(2,1)S(1)}, bf16[32,2304]{1,0:T(8,128)(2,1)S(1)}, u32[]{:S(2)}, u32[]{:S(2)}) collective-permute-start(bf16[32,2304]{1,0:T(8,128)(2,1)S(1)} %get-tuple-element.59), channel_id=1, source_target_pairs={{0,16},{4,20},{8,24},{12,28},{16,0},{20,4},{24,8},{28,12},{1,17},{... | collective-permute-start | bytes 442376 | tf_op jit(solution)/shard_map/ppermute | solution.py:19
  80.2 8.9 %collective-permute-start.38 = (bf16[32,2304]{1,0:T(8,128)(2,1)S(1)}, bf16[32,2304]{1,0:T(8,128)(2,1)S(1)}, u32[]{:S(2)}, u32[]{:S(2)}) collective-permute-start(bf16[32,2304]{1,0:T(8,128)(2,1)S(1)} %get-tuple-element.58), channel_id=1, source_target_pairs={{0,24},{4,28},{8,16},{12,20},{16,8},{20,12},{24,0},{28,4},{1,25},{... | collective-permute-start | bytes 442376 | tf_op jit(solution)/shard_map/ppermute | solution.py:19
  85.5 15.5 %copy-start.9 = (f32[2304]{0:T(1024)S(1)}, f32[2304]{0:T(1024)}, u32[]{:S(2)}) copy-start(f32[2304]{0:T(1024)} %param.25) | copy-start | bytes 27652
  85.6 6.5 %collective-permute-start.34 = (bf16[32,2304]{1,0:T(8,128)(2,1)S(1)}, bf16[32,2304]{1,0:T(8,128)(2,1)S(1)}, u32[]{:S(2)}, u32[]{:S(2)}) collective-permute-start(bf16[32,2304]{1,0:T(8,128)(2,1)S(1)} %get-tuple-element.54), channel_id=1, source_target_pairs={{0,8},{4,12},{8,0},{12,4},{16,24},{20,28},{24,16},{28,20},{1,9},{5... | collective-permute-start | bytes 442376 | tf_op jit(solution)/shard_map/ppermute | solution.py:19
  87.1 7.6 %collective-permute-start.35 = (bf16[32,2304]{1,0:T(8,128)(2,1)S(1)}, bf16[32,2304]{1,0:T(8,128)(2,1)S(1)}, u32[]{:S(2)}, u32[]{:S(2)}) collective-permute-start(bf16[32,2304]{1,0:T(8,128)(2,1)S(1)} %get-tuple-element.56), channel_id=1, source_target_pairs={{0,16},{4,20},{8,24},{12,28},{16,0},{20,4},{24,8},{28,12},{1,17},{... | collective-permute-start | bytes 442376 | tf_op jit(solution)/shard_map/ppermute | solution.py:19
  87.5 7.2 %collective-permute-start.36 = (bf16[32,2304]{1,0:T(8,128)(2,1)S(1)}, bf16[32,2304]{1,0:T(8,128)(2,1)S(1)}, u32[]{:S(2)}, u32[]{:S(2)}) collective-permute-start(bf16[32,2304]{1,0:T(8,128)(2,1)S(1)} %get-tuple-element.55), channel_id=1, source_target_pairs={{0,24},{4,28},{8,16},{12,20},{16,8},{20,12},{24,0},{28,4},{1,25},{... | collective-permute-start | bytes 442376 | tf_op jit(solution)/shard_map/ppermute | solution.py:19
  89.2 5.5 %collective-permute-start.39 = (bf16[32,2304]{1,0:T(8,128)(2,1)S(1)}, bf16[32,2304]{1,0:T(8,128)(2,1)S(1)}, u32[]{:S(2)}, u32[]{:S(2)}) collective-permute-start(bf16[32,2304]{1,0:T(8,128)(2,1)S(1)} %add_convert_fusion.2), channel_id=1, source_target_pairs={{0,1},{1,0},{2,3},{3,2},{4,5},{5,4},{6,7},{7,6},{8,9},{9,8},{10,11... | collective-permute-start | bytes 442376 | tf_op jit(solution)/shard_map/ppermute | solution.py:19
  94.8 6.2 %collective-permute-start.40 = (bf16[16,2304]{1,0:T(8,128)(2,1)S(1)}, bf16[16,2304]{1,0:T(8,128)(2,1)S(1)}, u32[]{:S(2)}, u32[]{:S(2)}) collective-permute-start(bf16[16,2304]{1,0:T(8,128)(2,1)S(1)} %fusion.9), channel_id=1, source_target_pairs={{0,2},{1,3},{2,0},{3,1},{4,6},{5,7},{6,4},{7,5},{8,10},{9,11},{10,... | collective-permute-start | bytes 221192 | tf_op jit(solution)/shard_map/ppermute | solution.py:19
  (6 other events, 10.2 us)

commit v15 on v14

--- a/solution.py
+++ b/solution.py
@@ -64,14 +64,15 @@
     return copies
 
 
-def pack_kernel(ids, weights, out):
-    top, own = ids.shape
+def pack_kernel(both, out):
+    top, own = both.shape[0] // 2, both.shape[1]
+    ids, weights = both[:top], both[top:]
     lane = lax.broadcasted_iota(jnp.int32, (top, LANES), 1)
     row = lax.broadcasted_iota(jnp.int32, (top, LANES), 0)
-    high = half(weights[...])
-    low = half(weights[...] - full(high))
+    high = half(weights)
+    low = half(weights - full(high))
     values = jnp.zeros((own, LANES), jnp.float32)
-    for i, part in enumerate([half(full(ids[...])), high, low]):
+    for i, part in enumerate([half(ids), high, low]):
         places = half(jnp.where(lane == row + i * top, 1.0, 0.0))
         values += lax.dot_general(
             part, places, (((0,), (0,)), ((), ())), preferred_element_type=jnp.float32
@@ -81,10 +82,12 @@
 
 def run_pack(expert_ids, gate_weights):
     own, top = expert_ids.shape
+    ids = jnp.pad(expert_ids.T, ((0, top), (0, 0)))
+    weights = jnp.pad(gate_weights.T, ((top, 0), (0, 0)))
     return call(
         pack_kernel,
-        [expert_ids.T, gate_weights.T],
-        [VMEM_SPEC] * 2,
+        [full(ids) + weights],
+        [VMEM_SPEC],
         [((own, LANES), jnp.bfloat16)],
         [],
         2,

time: 102 us -> 101 us (level)
  local copies, waits for them, and re-layouts: 2.94 us -> 1.43 us
    unnamed x59 -> x55, local copies, waits for them, and re-layouts: 2.85 us -> 1.34 us
where the time goes in v15:
time: 101 us
  starting transfers between devices  46.1 us (46%)
  waiting for transfers between devices  29.1 us (29%)
  Pallas kernels  15.5 us (15%)
  matrix products  5.52 us (5%)
  other arithmetic  2.25 us (2%)
  local copies, waits for them, and re-layouts  1.43 us (1%)
  between operations  1.27 us (1%)
    ppermute x41, starting transfers between devices, swap(): lax.ppermute(value, axis, [(i, i ^ r) for i in range(lax.axis_size(axis))])  46.1 us
    ppermute x41, waiting for transfers between devices, swap(): lax.ppermute(value, axis, [(i, i ^ r) for i in range(lax.axis_size(axis))])  29.1 us
    pallas_call x8, Pallas kernels, call(): pl.pallas_call(body, in_specs=specs, out_specs=[VMEM_SPEC] * len(outs), o...  15.5 us
    dot_general x8, matrix products, dot(): return jnp.dot(a, b, preferred_element_type=jnp.float32)  5.52 us
  transfers between devices with their start and end apart: 41, of which 15 were waited for; matrix products, arithmetic and copies ran while one was open for 6% of the time, Pallas kernels for 12%

profile of v15, /device:TPU:0, one launch (start us, length us, event | category | flops | bytes accessed | tf_op | source)
XLA Modules:
  0.0 101.0 jit_solution(7759271183565128241)
XLA Ops:
  0.6 0.9 pad_add_fusion.both
  1.7 2.9 %collective-permute-start = (bf16[16,128]{1,0:T(8,128)(2,1)S(1)}, bf16[16,128]{1,0:T(8,128)(2,1)S(1)}, u32[]{:S(2)}, u32[]{:S(2)}) collective-permute-start(bf16[16,128]{1,0:T(8,128)(2,1)S(1)} %shard_map.140), channel_id=1, source_target_pairs={{0,8},{4,12},{8,0},{12,4},{16,24},{20,28},{24,16},{28,20},{1,9},{5... | collective-permute-start | bytes 12296 | tf_op jit(solution)/shard_map/ppermute | solution.py:19
  4.6 1.5 %collective-permute-start.1 = (bf16[16,128]{1,0:T(8,128)(2,1)S(1)}, bf16[16,128]{1,0:T(8,128)(2,1)S(1)}, u32[]{:S(2)}, u32[]{:S(2)}) collective-permute-start(bf16[16,128]{1,0:T(8,128)(2,1)S(1)} %shard_map.140), channel_id=1, source_target_pairs={{0,16},{4,20},{8,24},{12,28},{16,0},{20,4},{24,8},{28,12},{1,17},{... | collective-permute-start | bytes 12296 | tf_op jit(solution)/shard_map/ppermute | solution.py:19
  6.2 2.0 %collective-permute-start.3 = (bf16[64,2304]{1,0:T(8,128)(2,1)}, bf16[64,2304]{1,0:T(8,128)(2,1)S(1)}, u32[]{:S(2)}, u32[]{:S(2)}) collective-permute-start(bf16[64,2304]{1,0:T(8,128)(2,1)} %refs_0_), channel_id=1, source_target_pairs={{0,8},{4,12},{8,0},{12,4},{16,24},{20,28},{24,16},{28,20},{1,9},{5... | collective-permute-start | bytes 884744 | tf_op jit(solution)/shard_map/ppermute | solution.py:19
  8.2 1.5 %collective-permute-start.4 = (bf16[64,2304]{1,0:T(8,128)(2,1)}, bf16[64,2304]{1,0:T(8,128)(2,1)S(1)}, u32[]{:S(2)}, u32[]{:S(2)}) collective-permute-start(bf16[64,2304]{1,0:T(8,128)(2,1)} %refs_0_), channel_id=1, source_target_pairs={{0,16},{4,20},{8,24},{12,28},{16,0},{20,4},{24,8},{28,12},{1,17},{... | collective-permute-start | bytes 884744 | tf_op jit(solution)/shard_map/ppermute | solution.py:19
  9.8 0.9 collective-permute-done.2
  10.7 1.6 %collective-permute-start.10 = (bf16[64,128]{1,0:T(8,128)(2,1)S(1)}, bf16[64,128]{1,0:T(8,128)(2,1)S(1)}, u32[]{:S(2)}, u32[]{:S(2)}) collective-permute-start(bf16[64,128]{1,0:T(8,128)(2,1)S(1)} %pad_maximum_fusion.3), channel_id=1, source_target_pairs={{0,1},{1,0},{2,3},{3,2},{4,5},{5,4},{6,7},{7,6},{8,9},{9,8},{10,11... | collective-permute-start | bytes 49160 | tf_op jit(solution)/shard_map/ppermute | solution.py:19
  12.3 1.0 copy-done.4
  13.3 3.9 %shard_map.141 = (bf16[64,2304]{1,0:T(8,128)(2,1)S(1)}, bf16[1,2304,1024]{2,1,0:T(8,128)(2,1)S(1)}, bf16[1,2304,1024]{2,1,0:T(8,128)(2,1)S(1)}) custom-call(bf16[64,2304]{1,0:T(8,128)(2,1)S(1)} %copy-done.4, bf16[1,2304,1024]{2,1,0:T(8,128)(2,1)} %refs_1_.1, bf16[1,2304,1024]{2,1,0:T(8,128)(2,1)} %refs_2_.1), custom_call_target="tpu_custom_call" | custom-call | flops 2676326400 | bytes 19464192 | tf_op jit(solution)/shard_map/pallas_call | solution.py:49
  17.2 2.7 %collective-permute-start.11 = (bf16[128,128]{1,0:T(8,128)(2,1)S(1)}, bf16[128,128]{1,0:T(8,128)(2,1)S(1)}, u32[]{:S(2)}, u32[]{:S(2)}) collective-permute-start(bf16[128,128]{1,0:T(8,128)(2,1)S(1)} %pad_maximum_fusion.2), channel_id=1, source_target_pairs={{0,2},{1,3},{2,0},{3,1},{4,6},{5,7},{6,4},{7,5},{8,10},{9,11},{10,... | collective-permute-start | bytes 98312 | tf_op jit(solution)/shard_map/ppermute | solution.py:19
  19.9 2.5 %collective-permute-done.4.refs_2_ = bf16[64,2304]{1,0:T(8,128)(2,1)S(1)} collective-permute-done((bf16[64,2304]{1,0:T(8,128)(2,1)}, bf16[64,2304]{1,0:T(8,128)(2,1)S(1)}, u32[]{:S(2)}, u32[]{:S(2)}) %collective-permute-start.4) | collective-permute-done | bytes 294944 | tf_op jit(solution)/shard_map/ppermute | solution.py:19
  22.9 2.7 %shard_map.142.hidden = bf16[256,1024]{1,0:T(8,128)(2,1)S(1)} custom-call(bf16[64,2304]{1,0:T(8,128)(2,1)S(1)} %get-tuple-element.30.refs_0_, bf16[64,2304]{1,0:T(8,128)(2,1)S(1)} %collective-permute-done.3.refs_1_, bf16[64,2304]{1,0:T(8,128)(2,1)S(1)} %collective-permute-done.4.refs_2_, bf16[64,2304]{1,0:T(8,128)(2,1)S(1)} %collective-permute-done.5.refs_3_, ...), custom_call_target="tpu_custom_call" | custom-call | flops 2415919104 | bytes 9437184 | tf_op jit(solution)/shard_map/pallas_call | solution.py:49
  25.7 2.0 %shard_map.144 = bf16[256,2304]{1,0:T(8,128)(2,1)S(1)} custom-call(s32[3]{0:T(128)S(1)} %pad_add_fusion.1.scalars, bf16[256,1024]{1,0:T(8,128)(2,1)S(1)} %shard_map.142.hidden, bf16[1,1024,2304]{2,1,0:T(8,128)(2,1)S(1)} %bitcast.57, bf16[256,128]{1,0:T(8,128)(2,1)S(1)} %constant_dynamic-update-slice_fusion.table), custom_call_target="tpu_custom_call" | custom-call | flops 1207959552 | bytes 4718592 | tf_op jit(solution)/shard_map/pallas_call | solution.py:49
  28.2 2.7 %shard_map.143.hidden = bf16[256,1024]{1,0:T(8,128)(2,1)S(1)} custom-call(bf16[64,2304]{1,0:T(8,128)(2,1)S(1)} %collective-permute-done.6.refs_0_.x, bf16[64,2304]{1,0:T(8,128)(2,1)S(1)} %collective-permute-done.7.refs_1_, bf16[64,2304]{1,0:T(8,128)(2,1)S(1)} %collective-permute-done.8.refs_2_, bf16[64,2304]{1,0:T(8,128)(2,1)S(1)} %collective-permute-done.9.refs_3_, ...), custom_call_target="tpu_custom_call" | custom-call | flops 2415919104 | bytes 9437184 | tf_op jit(solution)/shard_map/pallas_call | solution.py:49
  30.9 1.3 %shard_map.146 = (bf16[32,2304]{1,0:T(8,128)(2,1)S(1)}, bf16[32,2304]{1,0:T(8,128)(2,1)S(1)}, bf16[32,2304]{1,0:T(8,128)(2,1)S(1)}, bf16[32,2304]{1,0:T(8,128)(2,1)S(1)}) custom-call(s32[3]{0:T(128)S(1)} %pad_add_fusion.1.scalars, bf16[256,1024]{1,0:T(8,128)(2,1)S(1)} %shard_map.143.hidden, bf16[1,1024,2304]{2,1,0:T(8,128)(2,1)S(1)} %bitcast.57, ...), custom_call_target="tpu_custom_call" | custom-call | flops 1207959552 | bytes 4718592 | tf_op jit(solution)/shard_map/pallas_call | solution.py:49
  32.3 1.5 %collective-permute-start.17 = (bf16[32,2304]{1,0:T(8,128)(2,1)S(1)}, bf16[32,2304]{1,0:T(8,128)(2,1)S(1)}, u32[]{:S(2)}, u32[]{:S(2)}) collective-permute-start(bf16[32,2304]{1,0:T(8,128)(2,1)S(1)} %get-tuple-element.44), channel_id=1, source_target_pairs={{0,24},{4,28},{8,16},{12,20},{16,8},{20,12},{24,0},{28,4},{1,25},{... | collective-permute-start | bytes 442376 | tf_op jit(solution)/shard_map/ppermute | solution.py:19
  33.8 1.5 %collective-permute-start.18 = (bf16[32,2304]{1,0:T(8,128)(2,1)S(1)}, bf16[32,2304]{1,0:T(8,128)(2,1)S(1)}, u32[]{:S(2)}, u32[]{:S(2)}) collective-permute-start(bf16[32,2304]{1,0:T(8,128)(2,1)S(1)} %get-tuple-element.48), channel_id=1, source_target_pairs={{0,8},{4,12},{8,0},{12,4},{16,24},{20,28},{24,16},{28,20},{1,9},{5... | collective-permute-start | bytes 442376 | tf_op jit(solution)/shard_map/ppermute | solution.py:19
  35.9 1.4 %shard_map.145 = (bf16[32,2304]{1,0:T(8,128)(2,1)S(1)}, bf16[32,2304]{1,0:T(8,128)(2,1)S(1)}, bf16[32,2304]{1,0:T(8,128)(2,1)S(1)}, bf16[32,2304]{1,0:T(8,128)(2,1)S(1)}) custom-call(s32[3]{0:T(128)S(1)} %pad_add_fusion.1.scalars, bf16[256,1024]{1,0:T(8,128)(2,1)S(1)} %shard_map.143.hidden, bf16[1,1024,2304]{2,1,0:T(8,128)(2,1)S(1)} %bitcast.57, ...), custom_call_target="tpu_custom_call" | custom-call | flops 1207959552 | bytes 4718592 | tf_op jit(solution)/shard_map/pallas_call | solution.py:49
  37.2 0.9 collective-permute-start.14
  38.1 1.2 %collective-permute-start.15 = (bf16[32,2304]{1,0:T(8,128)(2,1)S(1)}, bf16[32,2304]{1,0:T(8,128)(2,1)S(1)}, u32[]{:S(2)}, u32[]{:S(2)}) collective-permute-start(bf16[32,2304]{1,0:T(8,128)(2,1)S(1)} %get-tuple-element.42), channel_id=1, source_target_pairs={{0,16},{4,20},{8,24},{12,28},{16,0},{20,4},{24,8},{28,12},{1,17},{... | collective-permute-start | bytes 442376 | tf_op jit(solution)/shard_map/ppermute | solution.py:19
  39.3 0.7 collective-permute-done.17
  40.0 1.4 %collective-permute-start.16 = (bf16[32,2304]{1,0:T(8,128)(2,1)S(1)}, bf16[32,2304]{1,0:T(8,128)(2,1)S(1)}, u32[]{:S(2)}, u32[]{:S(2)}) collective-permute-start(bf16[32,2304]{1,0:T(8,128)(2,1)S(1)} %get-tuple-element.43), channel_id=1, source_target_pairs={{0,24},{4,28},{8,16},{12,20},{16,8},{20,12},{24,0},{28,4},{1,25},{... | collective-permute-start | bytes 442376 | tf_op jit(solution)/shard_map/ppermute | solution.py:19
  41.4 1.4 %shard_map.147 = (f32[32,2304]{1,0:T(8,128)S(1)}, f32[32,2304]{1,0:T(8,128)S(1)}) custom-call(s32[3]{0:T(128)S(1)} %pad_add_fusion.1.scalars, bf16[64,2304]{1,0:T(8,128)(2,1)S(1)} %collective-permute-done.6.refs_0_.x, bf16[2304,256]{1,0:T(8,128)(2,1)S(1)} %copy-done.1, bf16[2304,256]{1,0:T(8,128)(2,1)S(1)} %copy-done.2, bf16[256,2304]{1,0:T(8,128)(2,1)S(1)} %copy-done.3), custom_call_target="tpu_custom_call" | custom-call | flops 226492416 | bytes 3538944 | tf_op jit(solution)/shard_map/pallas_call | solution.py:49
  43.3 1.6 %collective-permute-start.20 = (bf16[32,2304]{1,0:T(8,128)(2,1)S(1)}, bf16[32,2304]{1,0:T(8,128)(2,1)S(1)}, u32[]{:S(2)}, u32[]{:S(2)}) collective-permute-start(bf16[32,2304]{1,0:T(8,128)(2,1)S(1)} %add_convert_fusion.5), channel_id=1, source_target_pairs={{0,1},{1,0},{2,3},{3,2},{4,5},{5,4},{6,7},{7,6},{8,9},{9,8},{10,11... | collective-permute-start | bytes 442376 | tf_op jit(solution)/shard_map/ppermute | solution.py:19
  44.9 1.4 %collective-permute-done.14 = bf16[32,2304]{1,0:T(8,128)(2,1)S(1)} collective-permute-done((bf16[32,2304]{1,0:T(8,128)(2,1)S(1)}, bf16[32,2304]{1,0:T(8,128)(2,1)S(1)}, u32[]{:S(2)}, u32[]{:S(2)}) %collective-permute-start.14) | collective-permute-done | bytes 147488 | tf_op jit(solution)/shard_map/ppermute | solution.py:19
  46.3 2.2 %collective-permute-done.16 = bf16[32,2304]{1,0:T(8,128)(2,1)S(1)} collective-permute-done((bf16[32,2304]{1,0:T(8,128)(2,1)S(1)}, bf16[32,2304]{1,0:T(8,128)(2,1)S(1)}, u32[]{:S(2)}, u32[]{:S(2)}) %collective-permute-start.16) | collective-permute-done | bytes 147488 | tf_op jit(solution)/shard_map/ppermute | solution.py:19
  48.7 2.7 %collective-permute-start.21 = (bf16[2,16,2304]{2,1,0:T(8,128)(2,1)S(1)}, bf16[2,16,2304]{2,1,0:T(8,128)(2,1)S(1)}, u32[]{:S(2)}, u32[]{:S(2)}) collective-permute-start(bf16[2,16,2304]{2,1,0:T(8,128)(2,1)S(1)} %bitcast.105), channel_id=1, source_target_pairs={{0,2},{1,3},{2,0},{3,1},{4,6},{5,7},{6,4},{7,5},{8,10},{9,11},{10,... | collective-permute-start | bytes 442376 | tf_op jit(solution)/shard_map/ppermute | solution.py:19
  51.4 6.4 %collective-permute-done.21 = bf16[2,16,2304]{2,1,0:T(8,128)(2,1)S(1)} collective-permute-done((bf16[2,16,2304]{2,1,0:T(8,128)(2,1)S(1)}, bf16[2,16,2304]{2,1,0:T(8,128)(2,1)S(1)}, u32[]{:S(2)}, u32[]{:S(2)}) %collective-permute-start.21) | collective-permute-done | bytes 147488 | tf_op jit(solution)/shard_map/ppermute | solution.py:19
  57.8 0.8 collective-permute-start.22
  58.6 1.6 %collective-permute-start.27 = (bf16[32,2304]{1,0:T(8,128)(2,1)S(1)}, bf16[32,2304]{1,0:T(8,128)(2,1)S(1)}, u32[]{:S(2)}, u32[]{:S(2)}) collective-permute-start(bf16[32,2304]{1,0:T(8,128)(2,1)S(1)} %bitcast.101), channel_id=1, source_target_pairs={{0,8},{4,12},{8,0},{12,4},{16,24},{20,28},{24,16},{28,20},{1,9},{5... | collective-permute-start | bytes 442376 | tf_op jit(solution)/shard_map/ppermute | solution.py:19
  60.6 2.5 %collective-permute-done.22 = bf16[32,2304]{1,0:T(8,128)(2,1)S(1)} collective-permute-done((bf16[32,2304]{1,0:T(8,128)(2,1)S(1)}, bf16[32,2304]{1,0:T(8,128)(2,1)S(1)}, u32[]{:S(2)}, u32[]{:S(2)}) %collective-permute-start.22) | collective-permute-done | bytes 147488 | tf_op jit(solution)/shard_map/ppermute | solution.py:19
  63.0 1.4 %collective-permute-start.29 = (bf16[32,2304]{1,0:T(8,128)(2,1)S(1)}, bf16[32,2304]{1,0:T(8,128)(2,1)S(1)}, u32[]{:S(2)}, u32[]{:S(2)}) collective-permute-start(bf16[32,2304]{1,0:T(8,128)(2,1)S(1)} %bitcast.103), channel_id=1, source_target_pairs={{0,24},{4,28},{8,16},{12,20},{16,8},{20,12},{24,0},{28,4},{1,25},{... | collective-permute-start | bytes 442376 | tf_op jit(solution)/shard_map/ppermute | solution.py:19
  64.5 1.5 %collective-permute-start.25 = (bf16[32,2304]{1,0:T(8,128)(2,1)S(1)}, bf16[32,2304]{1,0:T(8,128)(2,1)S(1)}, u32[]{:S(2)}, u32[]{:S(2)}) collective-permute-start(bf16[32,2304]{1,0:T(8,128)(2,1)S(1)} %collective-permute-done.22), channel_id=1, source_target_pairs={{0,24},{4,28},{8,16},{12,20},{16,8},{20,12},{24,0},{28,4},{1,25},{... | collective-permute-start | bytes 442376 | tf_op jit(solution)/shard_map/ppermute | solution.py:19
  66.0 1.6 %collective-permute-start.23 = (bf16[32,2304]{1,0:T(8,128)(2,1)S(1)}, bf16[32,2304]{1,0:T(8,128)(2,1)S(1)}, u32[]{:S(2)}, u32[]{:S(2)}) collective-permute-start(bf16[32,2304]{1,0:T(8,128)(2,1)S(1)} %collective-permute-done.22), channel_id=1, source_target_pairs={{0,8},{4,12},{8,0},{12,4},{16,24},{20,28},{24,16},{28,20},{1,9},{5... | collective-permute-start | bytes 442376 | tf_op jit(solution)/shard_map/ppermute | solution.py:19
  68.0 2.1 %collective-permute-done.28 = bf16[32,2304]{1,0:T(8,128)(2,1)S(1)} collective-permute-done((bf16[32,2304]{1,0:T(8,128)(2,1)S(1)}, bf16[32,2304]{1,0:T(8,128)(2,1)S(1)}, u32[]{:S(2)}, u32[]{:S(2)}) %collective-permute-start.28) | collective-permute-done | bytes 147488 | tf_op jit(solution)/shard_map/ppermute | solution.py:19
  70.9 2.1 %fusion.4 = bf16[128,512]{1,0:T(8,128)(2,1)S(1)} fusion(bf16[128,2304]{1,0:T(8,128)(2,1)S(1)} %bitcast.61, bf16[2304,512]{1,0:T(8,128)(2,1)} %param.22, f32[512]{0:T(512)S(1)} %copy-done.6), kind=kOutput, calls=%fused_computation.12 | convolution fusion | flops 302186496 | bytes 3082240 | tf_op jit(solution)/shard_map/dot_general | solution.py:23
  74.1 0.8 collective-permute-done.24
  77.6 1.4 %collective-permute-start.33 = (bf16[32,2304]{1,0:T(8,128)(2,1)S(1)}, bf16[32,2304]{1,0:T(8,128)(2,1)S(1)}, u32[]{:S(2)}, u32[]{:S(2)}) collective-permute-start(bf16[32,2304]{1,0:T(8,128)(2,1)S(1)} %get-tuple-element.57), channel_id=1, source_target_pairs={{0,8},{4,12},{8,0},{12,4},{16,24},{20,28},{24,16},{28,20},{1,9},{5... | collective-permute-start | bytes 442376 | tf_op jit(solution)/shard_map/ppermute | solution.py:19
  79.5 1.6 %collective-permute-start.38 = (bf16[32,2304]{1,0:T(8,128)(2,1)S(1)}, bf16[32,2304]{1,0:T(8,128)(2,1)S(1)}, u32[]{:S(2)}, u32[]{:S(2)}) collective-permute-start(bf16[32,2304]{1,0:T(8,128)(2,1)S(1)} %get-tuple-element.58), channel_id=1, source_target_pairs={{0,24},{4,28},{8,16},{12,20},{16,8},{20,12},{24,0},{28,4},{1,25},{... | collective-permute-start | bytes 442376 | tf_op jit(solution)/shard_map/ppermute | solution.py:19
  82.2 2.1 %collective-permute-done.33 = bf16[32,2304]{1,0:T(8,128)(2,1)S(1)} collective-permute-done((bf16[32,2304]{1,0:T(8,128)(2,1)S(1)}, bf16[32,2304]{1,0:T(8,128)(2,1)S(1)}, u32[]{:S(2)}, u32[]{:S(2)}) %collective-permute-start.33) | collective-permute-done | bytes 147488 | tf_op jit(solution)/shard_map/ppermute | solution.py:19
  84.9 1.4 %collective-permute-start.34 = (bf16[32,2304]{1,0:T(8,128)(2,1)S(1)}, bf16[32,2304]{1,0:T(8,128)(2,1)S(1)}, u32[]{:S(2)}, u32[]{:S(2)}) collective-permute-start(bf16[32,2304]{1,0:T(8,128)(2,1)S(1)} %get-tuple-element.54), channel_id=1, source_target_pairs={{0,8},{4,12},{8,0},{12,4},{16,24},{20,28},{24,16},{28,20},{1,9},{5... | collective-permute-start | bytes 442376 | tf_op jit(solution)/shard_map/ppermute | solution.py:19
  86.9 1.6 %collective-permute-start.36 = (bf16[32,2304]{1,0:T(8,128)(2,1)S(1)}, bf16[32,2304]{1,0:T(8,128)(2,1)S(1)}, u32[]{:S(2)}, u32[]{:S(2)}) collective-permute-start(bf16[32,2304]{1,0:T(8,128)(2,1)S(1)} %get-tuple-element.55), channel_id=1, source_target_pairs={{0,24},{4,28},{8,16},{12,20},{16,8},{20,12},{24,0},{28,4},{1,25},{... | collective-permute-start | bytes 442376 | tf_op jit(solution)/shard_map/ppermute | solution.py:19
  88.6 1.4 %collective-permute-start.39 = (bf16[32,2304]{1,0:T(8,128)(2,1)S(1)}, bf16[32,2304]{1,0:T(8,128)(2,1)S(1)}, u32[]{:S(2)}, u32[]{:S(2)}) collective-permute-start(bf16[32,2304]{1,0:T(8,128)(2,1)S(1)} %add_convert_fusion.2), channel_id=1, source_target_pairs={{0,1},{1,0},{2,3},{3,2},{4,5},{5,4},{6,7},{7,6},{8,9},{9,8},{10,11... | collective-permute-start | bytes 442376 | tf_op jit(solution)/shard_map/ppermute | solution.py:19
  90.0 1.4 %collective-permute-done.34 = bf16[32,2304]{1,0:T(8,128)(2,1)S(1)} collective-permute-done((bf16[32,2304]{1,0:T(8,128)(2,1)S(1)}, bf16[32,2304]{1,0:T(8,128)(2,1)S(1)}, u32[]{:S(2)}, u32[]{:S(2)}) %collective-permute-start.34) | collective-permute-done | bytes 147488 | tf_op jit(solution)/shard_map/ppermute | solution.py:19
  91.4 2.6 %collective-permute-done.35 = bf16[32,2304]{1,0:T(8,128)(2,1)S(1)} collective-permute-done((bf16[32,2304]{1,0:T(8,128)(2,1)S(1)}, bf16[32,2304]{1,0:T(8,128)(2,1)S(1)}, u32[]{:S(2)}, u32[]{:S(2)}) %collective-permute-start.35) | collective-permute-done | bytes 147488 | tf_op jit(solution)/shard_map/ppermute | solution.py:19
  94.1 3.9 %collective-permute-start.40 = (bf16[16,2304]{1,0:T(8,128)(2,1)S(1)}, bf16[16,2304]{1,0:T(8,128)(2,1)S(1)}, u32[]{:S(2)}, u32[]{:S(2)}) collective-permute-start(bf16[16,2304]{1,0:T(8,128)(2,1)S(1)} %fusion.9), channel_id=1, source_target_pairs={{0,2},{1,3},{2,0},{3,1},{4,6},{5,7},{6,4},{7,5},{8,10},{9,11},{10,... | collective-permute-start | bytes 221192 | tf_op jit(solution)/shard_map/ppermute | solution.py:19
  98.0 2.3 %collective-permute-done.40 = bf16[16,2304]{1,0:T(8,128)(2,1)S(1)} collective-permute-done((bf16[16,2304]{1,0:T(8,128)(2,1)S(1)}, bf16[16,2304]{1,0:T(8,128)(2,1)S(1)}, u32[]{:S(2)}, u32[]{:S(2)}) %collective-permute-start.40) | collective-permute-done | bytes 73760 | tf_op jit(solution)/shard_map/ppermute | solution.py:19
  100.4 0.7 fusion.8
  (125 shorter events, 10.5 us)
Async XLA Ops:
  0.6 72.4 %copy-start = (bf16[512,2304]{1,0:T(8,128)(2,1)S(1)}, bf16[512,2304]{1,0:T(8,128)(2,1)}, u32[]{:S(2)}) copy-start(bf16[512,2304]{1,0:T(8,128)(2,1)} %param.24) | copy-start | bytes 7077892
  1.7 4.5 %collective-permute-start = (bf16[16,128]{1,0:T(8,128)(2,1)S(1)}, bf16[16,128]{1,0:T(8,128)(2,1)S(1)}, u32[]{:S(2)}, u32[]{:S(2)}) collective-permute-start(bf16[16,128]{1,0:T(8,128)(2,1)S(1)} %shard_map.140), channel_id=1, source_target_pairs={{0,8},{4,12},{8,0},{12,4},{16,24},{20,28},{24,16},{28,20},{1,9},{5... | collective-permute-start | bytes 12296 | tf_op jit(solution)/shard_map/ppermute | solution.py:19
  4.6 5.1 %collective-permute-start.1 = (bf16[16,128]{1,0:T(8,128)(2,1)S(1)}, bf16[16,128]{1,0:T(8,128)(2,1)S(1)}, u32[]{:S(2)}, u32[]{:S(2)}) collective-permute-start(bf16[16,128]{1,0:T(8,128)(2,1)S(1)} %shard_map.140), channel_id=1, source_target_pairs={{0,16},{4,20},{8,24},{12,28},{16,0},{20,4},{24,8},{28,12},{1,17},{... | collective-permute-start | bytes 12296 | tf_op jit(solution)/shard_map/ppermute | solution.py:19
  6.1 4.6 %collective-permute-start.2 = (bf16[16,128]{1,0:T(8,128)(2,1)S(1)}, bf16[16,128]{1,0:T(8,128)(2,1)S(1)}, u32[]{:S(2)}, u32[]{:S(2)}) collective-permute-start(bf16[16,128]{1,0:T(8,128)(2,1)S(1)} %shard_map.140), channel_id=1, source_target_pairs={{0,24},{4,28},{8,16},{12,20},{16,8},{20,12},{24,0},{28,4},{1,25},{... | collective-permute-start | bytes 12296 | tf_op jit(solution)/shard_map/ppermute | solution.py:19
  6.2 13.6 %collective-permute-start.3 = (bf16[64,2304]{1,0:T(8,128)(2,1)}, bf16[64,2304]{1,0:T(8,128)(2,1)S(1)}, u32[]{:S(2)}, u32[]{:S(2)}) collective-permute-start(bf16[64,2304]{1,0:T(8,128)(2,1)} %refs_0_), channel_id=1, source_target_pairs={{0,8},{4,12},{8,0},{12,4},{16,24},{20,28},{24,16},{28,20},{1,9},{5... | collective-permute-start | bytes 884744 | tf_op jit(solution)/shard_map/ppermute | solution.py:19
  8.2 14.2 %collective-permute-start.4 = (bf16[64,2304]{1,0:T(8,128)(2,1)}, bf16[64,2304]{1,0:T(8,128)(2,1)S(1)}, u32[]{:S(2)}, u32[]{:S(2)}) collective-permute-start(bf16[64,2304]{1,0:T(8,128)(2,1)} %refs_0_), channel_id=1, source_target_pairs={{0,16},{4,20},{8,24},{12,28},{16,0},{20,4},{24,8},{28,12},{1,17},{... | collective-permute-start | bytes 884744 | tf_op jit(solution)/shard_map/ppermute | solution.py:19
  9.8 12.7 %collective-permute-start.5 = (bf16[64,2304]{1,0:T(8,128)(2,1)}, bf16[64,2304]{1,0:T(8,128)(2,1)S(1)}, u32[]{:S(2)}, u32[]{:S(2)}) collective-permute-start(bf16[64,2304]{1,0:T(8,128)(2,1)} %refs_0_), channel_id=1, source_target_pairs={{0,24},{4,28},{8,16},{12,20},{16,8},{20,12},{24,0},{28,4},{1,25},{... | collective-permute-start | bytes 884744 | tf_op jit(solution)/shard_map/ppermute | solution.py:19
  9.8 15.9 %collective-permute-start.6 = (bf16[64,2304]{1,0:T(8,128)(2,1)}, bf16[64,2304]{1,0:T(8,128)(2,1)S(1)}, u32[]{:S(2)}, u32[]{:S(2)}) collective-permute-start(bf16[64,2304]{1,0:T(8,128)(2,1)} %refs_0_), channel_id=1, source_target_pairs={{0,4},{4,0},{8,12},{12,8},{16,20},{20,16},{24,28},{28,24},{1,5},{5... | collective-permute-start | bytes 884744 | tf_op jit(solution)/shard_map/ppermute | solution.py:19
  10.7 6.5 %collective-permute-start.10 = (bf16[64,128]{1,0:T(8,128)(2,1)S(1)}, bf16[64,128]{1,0:T(8,128)(2,1)S(1)}, u32[]{:S(2)}, u32[]{:S(2)}) collective-permute-start(bf16[64,128]{1,0:T(8,128)(2,1)S(1)} %pad_maximum_fusion.3), channel_id=1, source_target_pairs={{0,1},{1,0},{2,3},{3,2},{4,5},{5,4},{6,7},{7,6},{8,9},{9,8},{10,11... | collective-permute-start | bytes 49160 | tf_op jit(solution)/shard_map/ppermute | solution.py:19
  13.3 12.4 %slice-start = ((s8[4718592]{0:T(1024)(128)(4,1)}), s8[524288]{0:T(1024)(128)(4,1)S(1)}, s32[]{:S(2)}) async-start(s8[4718592]{0:T(1024)(128)(4,1)} %bitcast.56), calls=%async_computation | async-start | bytes 1048576
  17.2 5.7 %collective-permute-start.11 = (bf16[128,128]{1,0:T(8,128)(2,1)S(1)}, bf16[128,128]{1,0:T(8,128)(2,1)S(1)}, u32[]{:S(2)}, u32[]{:S(2)}) collective-permute-start(bf16[128,128]{1,0:T(8,128)(2,1)S(1)} %pad_maximum_fusion.2), channel_id=1, source_target_pairs={{0,2},{1,3},{2,0},{3,1},{4,6},{5,7},{6,4},{7,5},{8,10},{9,11},{10,... | collective-permute-start | bytes 98312 | tf_op jit(solution)/shard_map/ppermute | solution.py:19
  19.9 5.8 %collective-permute-start.7 = (bf16[64,2304]{1,0:T(8,128)(2,1)S(1)}, bf16[64,2304]{1,0:T(8,128)(2,1)S(1)}, u32[]{:S(2)}, u32[]{:S(2)}) collective-permute-start(bf16[64,2304]{1,0:T(8,128)(2,1)S(1)} %collective-permute-done.3.refs_1_), channel_id=1, source_target_pairs={{0,4},{4,0},{8,12},{12,8},{16,20},{20,16},{24,28},{28,24},{1,5},{5... | collective-permute-start | bytes 884744 | tf_op jit(solution)/shard_map/ppermute | solution.py:19
  22.4 3.2 %collective-permute-start.8 = (bf16[64,2304]{1,0:T(8,128)(2,1)S(1)}, bf16[64,2304]{1,0:T(8,128)(2,1)S(1)}, u32[]{:S(2)}, u32[]{:S(2)}) collective-permute-start(bf16[64,2304]{1,0:T(8,128)(2,1)S(1)} %collective-permute-done.4.refs_2_), channel_id=1, source_target_pairs={{0,4},{4,0},{8,12},{12,8},{16,20},{20,16},{24,28},{28,24},{1,5},{5... | collective-permute-start | bytes 884744 | tf_op jit(solution)/shard_map/ppermute | solution.py:19
  22.4 3.2 %collective-permute-start.9 = (bf16[64,2304]{1,0:T(8,128)(2,1)S(1)}, bf16[64,2304]{1,0:T(8,128)(2,1)S(1)}, u32[]{:S(2)}, u32[]{:S(2)}) collective-permute-start(bf16[64,2304]{1,0:T(8,128)(2,1)S(1)} %collective-permute-done.5.refs_3_), channel_id=1, source_target_pairs={{0,4},{4,0},{8,12},{12,8},{16,20},{20,16},{24,28},{28,24},{1,5},{5... | collective-permute-start | bytes 884744 | tf_op jit(solution)/shard_map/ppermute | solution.py:19
  27.7 3.3 %collective-permute-start.13 = (bf16[256,2304]{1,0:T(8,128)(2,1)S(1)}, bf16[256,2304]{1,0:T(8,128)(2,1)S(1)}, u32[]{:S(2)}, u32[]{:S(2)}) collective-permute-start(bf16[256,2304]{1,0:T(8,128)(2,1)S(1)} %shard_map.144), channel_id=1, source_target_pairs={{0,4},{4,0},{8,12},{12,8},{16,20},{20,16},{24,28},{28,24},{1,5},{5... | collective-permute-start | bytes 3538952 | tf_op jit(solution)/shard_map/ppermute | solution.py:19
  27.8 3.2 %collective-permute-start.12 = (bf16[256,128]{1,0:T(8,128)(2,1)S(1)}, bf16[256,128]{1,0:T(8,128)(2,1)S(1)}, u32[]{:S(2)}, u32[]{:S(2)}) collective-permute-start(bf16[256,128]{1,0:T(8,128)(2,1)S(1)} %constant_dynamic-update-slice_fusion.table), channel_id=1, source_target_pairs={{0,4},{4,0},{8,12},{12,8},{16,20},{20,16},{24,28},{28,24},{1,5},{5... | collective-permute-start | bytes 196616 | tf_op jit(solution)/shard_map/ppermute | solution.py:19
  32.3 7.7 %collective-permute-start.17 = (bf16[32,2304]{1,0:T(8,128)(2,1)S(1)}, bf16[32,2304]{1,0:T(8,128)(2,1)S(1)}, u32[]{:S(2)}, u32[]{:S(2)}) collective-permute-start(bf16[32,2304]{1,0:T(8,128)(2,1)S(1)} %get-tuple-element.44), channel_id=1, source_target_pairs={{0,24},{4,28},{8,16},{12,20},{16,8},{20,12},{24,0},{28,4},{1,25},{... | collective-permute-start | bytes 442376 | tf_op jit(solution)/shard_map/ppermute | solution.py:19
  33.8 9.4 %collective-permute-start.18 = (bf16[32,2304]{1,0:T(8,128)(2,1)S(1)}, bf16[32,2304]{1,0:T(8,128)(2,1)S(1)}, u32[]{:S(2)}, u32[]{:S(2)}) collective-permute-start(bf16[32,2304]{1,0:T(8,128)(2,1)S(1)} %get-tuple-element.48), channel_id=1, source_target_pairs={{0,8},{4,12},{8,0},{12,4},{16,24},{20,28},{24,16},{28,20},{1,9},{5... | collective-permute-start | bytes 442376 | tf_op jit(solution)/shard_map/ppermute | solution.py:19
  35.3 6.1 %copy-start.1 = (bf16[2304,256]{1,0:T(8,128)(2,1)S(1)}, bf16[2304,256]{1,0:T(8,128)(2,1)}, u32[]{:S(2)}) copy-start(bf16[2304,256]{1,0:T(8,128)(2,1)} %gate.1) | copy-start | bytes 3538948
  35.3 6.1 %copy-start.2 = (bf16[2304,256]{1,0:T(8,128)(2,1)S(1)}, bf16[2304,256]{1,0:T(8,128)(2,1)}, u32[]{:S(2)}) copy-start(bf16[2304,256]{1,0:T(8,128)(2,1)} %up.1) | copy-start | bytes 3538948
  35.3 6.1 %copy-start.3 = (bf16[256,2304]{1,0:T(8,128)(2,1)S(1)}, bf16[256,2304]{1,0:T(8,128)(2,1)}, u32[]{:S(2)}) copy-start(bf16[256,2304]{1,0:T(8,128)(2,1)} %down.7) | copy-start | bytes 3538948
  35.3 7.9 %collective-permute-start.19 = (bf16[32,2304]{1,0:T(8,128)(2,1)S(1)}, bf16[32,2304]{1,0:T(8,128)(2,1)S(1)}, u32[]{:S(2)}, u32[]{:S(2)}) collective-permute-start(bf16[32,2304]{1,0:T(8,128)(2,1)S(1)} %get-tuple-element.49), channel_id=1, source_target_pairs={{0,16},{4,20},{8,24},{12,28},{16,0},{20,4},{24,8},{28,12},{1,17},{... | collective-permute-start | bytes 442376 | tf_op jit(solution)/shard_map/ppermute | solution.py:19
  37.2 9.1 %collective-permute-start.14 = (bf16[32,2304]{1,0:T(8,128)(2,1)S(1)}, bf16[32,2304]{1,0:T(8,128)(2,1)S(1)}, u32[]{:S(2)}, u32[]{:S(2)}) collective-permute-start(bf16[32,2304]{1,0:T(8,128)(2,1)S(1)} %get-tuple-element.41), channel_id=1, source_target_pairs={{0,8},{4,12},{8,0},{12,4},{16,24},{20,28},{24,16},{28,20},{1,9},{5... | collective-permute-start | bytes 442376 | tf_op jit(solution)/shard_map/ppermute | solution.py:19
  38.1 8.2 %collective-permute-start.15 = (bf16[32,2304]{1,0:T(8,128)(2,1)S(1)}, bf16[32,2304]{1,0:T(8,128)(2,1)S(1)}, u32[]{:S(2)}, u32[]{:S(2)}) collective-permute-start(bf16[32,2304]{1,0:T(8,128)(2,1)S(1)} %get-tuple-element.42), channel_id=1, source_target_pairs={{0,16},{4,20},{8,24},{12,28},{16,0},{20,4},{24,8},{28,12},{1,17},{... | collective-permute-start | bytes 442376 | tf_op jit(solution)/shard_map/ppermute | solution.py:19
  40.0 8.6 %collective-permute-start.16 = (bf16[32,2304]{1,0:T(8,128)(2,1)S(1)}, bf16[32,2304]{1,0:T(8,128)(2,1)S(1)}, u32[]{:S(2)}, u32[]{:S(2)}) collective-permute-start(bf16[32,2304]{1,0:T(8,128)(2,1)S(1)} %get-tuple-element.43), channel_id=1, source_target_pairs={{0,24},{4,28},{8,16},{12,20},{16,8},{20,12},{24,0},{28,4},{1,25},{... | collective-permute-start | bytes 442376 | tf_op jit(solution)/shard_map/ppermute | solution.py:19
  42.8 28.1 %copy-start.6 = (f32[512]{0:T(512)S(1)}, f32[512]{0:T(512)}, u32[]{:S(2)}) copy-start(f32[512]{0:T(512)} %param.23) | copy-start | bytes 6148
  43.3 5.3 %collective-permute-start.20 = (bf16[32,2304]{1,0:T(8,128)(2,1)S(1)}, bf16[32,2304]{1,0:T(8,128)(2,1)S(1)}, u32[]{:S(2)}, u32[]{:S(2)}) collective-permute-start(bf16[32,2304]{1,0:T(8,128)(2,1)S(1)} %add_convert_fusion.5), channel_id=1, source_target_pairs={{0,1},{1,0},{2,3},{3,2},{4,5},{5,4},{6,7},{7,6},{8,9},{9,8},{10,11... | collective-permute-start | bytes 442376 | tf_op jit(solution)/shard_map/ppermute | solution.py:19
  48.7 9.1 %collective-permute-start.21 = (bf16[2,16,2304]{2,1,0:T(8,128)(2,1)S(1)}, bf16[2,16,2304]{2,1,0:T(8,128)(2,1)S(1)}, u32[]{:S(2)}, u32[]{:S(2)}) collective-permute-start(bf16[2,16,2304]{2,1,0:T(8,128)(2,1)S(1)} %bitcast.105), channel_id=1, source_target_pairs={{0,2},{1,3},{2,0},{3,1},{4,6},{5,7},{6,4},{7,5},{8,10},{9,11},{10,... | collective-permute-start | bytes 442376 | tf_op jit(solution)/shard_map/ppermute | solution.py:19
  57.8 5.2 %collective-permute-start.22 = (bf16[32,2304]{1,0:T(8,128)(2,1)S(1)}, bf16[32,2304]{1,0:T(8,128)(2,1)S(1)}, u32[]{:S(2)}, u32[]{:S(2)}) collective-permute-start(bf16[32,2304]{1,0:T(8,128)(2,1)S(1)} %bitcast.100), channel_id=1, source_target_pairs={{0,1},{1,0},{2,3},{3,2},{4,5},{5,4},{6,7},{7,6},{8,9},{9,8},{10,11... | collective-permute-start | bytes 442376 | tf_op jit(solution)/shard_map/ppermute | solution.py:19
  58.6 9.0 %collective-permute-start.27 = (bf16[32,2304]{1,0:T(8,128)(2,1)S(1)}, bf16[32,2304]{1,0:T(8,128)(2,1)S(1)}, u32[]{:S(2)}, u32[]{:S(2)}) collective-permute-start(bf16[32,2304]{1,0:T(8,128)(2,1)S(1)} %bitcast.101), channel_id=1, source_target_pairs={{0,8},{4,12},{8,0},{12,4},{16,24},{20,28},{24,16},{28,20},{1,9},{5... | collective-permute-start | bytes 442376 | tf_op jit(solution)/shard_map/ppermute | solution.py:19
  60.2 9.9 %collective-permute-start.28 = (bf16[32,2304]{1,0:T(8,128)(2,1)S(1)}, bf16[32,2304]{1,0:T(8,128)(2,1)S(1)}, u32[]{:S(2)}, u32[]{:S(2)}) collective-permute-start(bf16[32,2304]{1,0:T(8,128)(2,1)S(1)} %bitcast.102), channel_id=1, source_target_pairs={{0,16},{4,20},{8,24},{12,28},{16,0},{20,4},{24,8},{28,12},{1,17},{... | collective-permute-start | bytes 442376 | tf_op jit(solution)/shard_map/ppermute | solution.py:19
  63.0 7.7 %collective-permute-start.29 = (bf16[32,2304]{1,0:T(8,128)(2,1)S(1)}, bf16[32,2304]{1,0:T(8,128)(2,1)S(1)}, u32[]{:S(2)}, u32[]{:S(2)}) collective-permute-start(bf16[32,2304]{1,0:T(8,128)(2,1)S(1)} %bitcast.103), channel_id=1, source_target_pairs={{0,24},{4,28},{8,16},{12,20},{16,8},{20,12},{24,0},{28,4},{1,25},{... | collective-permute-start | bytes 442376 | tf_op jit(solution)/shard_map/ppermute | solution.py:19
  64.5 9.6 %collective-permute-start.25 = (bf16[32,2304]{1,0:T(8,128)(2,1)S(1)}, bf16[32,2304]{1,0:T(8,128)(2,1)S(1)}, u32[]{:S(2)}, u32[]{:S(2)}) collective-permute-start(bf16[32,2304]{1,0:T(8,128)(2,1)S(1)} %collective-permute-done.22), channel_id=1, source_target_pairs={{0,24},{4,28},{8,16},{12,20},{16,8},{20,12},{24,0},{28,4},{1,25},{... | collective-permute-start | bytes 442376 | tf_op jit(solution)/shard_map/ppermute | solution.py:19
  66.0 8.2 %collective-permute-start.23 = (bf16[32,2304]{1,0:T(8,128)(2,1)S(1)}, bf16[32,2304]{1,0:T(8,128)(2,1)S(1)}, u32[]{:S(2)}, u32[]{:S(2)}) collective-permute-start(bf16[32,2304]{1,0:T(8,128)(2,1)S(1)} %collective-permute-done.22), channel_id=1, source_target_pairs={{0,8},{4,12},{8,0},{12,4},{16,24},{20,28},{24,16},{28,20},{1,9},{5... | collective-permute-start | bytes 442376 | tf_op jit(solution)/shard_map/ppermute | solution.py:19
  67.6 7.3 %collective-permute-start.24 = (bf16[32,2304]{1,0:T(8,128)(2,1)S(1)}, bf16[32,2304]{1,0:T(8,128)(2,1)S(1)}, u32[]{:S(2)}, u32[]{:S(2)}) collective-permute-start(bf16[32,2304]{1,0:T(8,128)(2,1)S(1)} %collective-permute-done.22), channel_id=1, source_target_pairs={{0,16},{4,20},{8,24},{12,28},{16,0},{20,4},{24,8},{28,12},{1,17},{... | collective-permute-start | bytes 442376 | tf_op jit(solution)/shard_map/ppermute | solution.py:19
  70.8 5.8 %collective-permute-start.30 = (bf16[128,2304]{1,0:T(8,128)(2,1)S(1)}, bf16[128,2304]{1,0:T(8,128)(2,1)S(1)}, u32[]{:S(2)}, u32[]{:S(2)}) collective-permute-start(bf16[128,2304]{1,0:T(8,128)(2,1)S(1)} %bitcast.60), channel_id=1, source_target_pairs={{0,4},{4,0},{8,12},{12,8},{16,20},{20,16},{24,28},{28,24},{1,5},{5... | collective-permute-start | bytes 1769480 | tf_op jit(solution)/shard_map/ppermute | solution.py:19
  73.6 3.5 %collective-permute-start.32 = (bf16[128,2304]{1,0:T(8,128)(2,1)S(1)}, bf16[128,2304]{1,0:T(8,128)(2,1)S(1)}, u32[]{:S(2)}, u32[]{:S(2)}) collective-permute-start(bf16[128,2304]{1,0:T(8,128)(2,1)S(1)} %convolution_convert_fusion), channel_id=1, source_target_pairs={{0,4},{4,0},{8,12},{12,8},{16,20},{20,16},{24,28},{28,24},{1,5},{5... | collective-permute-start | bytes 1769480 | tf_op jit(solution)/shard_map/ppermute | solution.py:19
  75.0 6.2 %collective-permute-start.26 = (bf16[128,2304]{1,0:T(8,128)(2,1)S(1)}, bf16[128,2304]{1,0:T(8,128)(2,1)S(1)}, u32[]{:S(2)}, u32[]{:S(2)}) collective-permute-start(bf16[128,2304]{1,0:T(8,128)(2,1)S(1)} %bitcast.58), channel_id=1, source_target_pairs={{0,4},{4,0},{8,12},{12,8},{16,20},{20,16},{24,28},{28,24},{1,5},{5... | collective-permute-start | bytes 1769480 | tf_op jit(solution)/shard_map/ppermute | solution.py:19
  76.0 8.3 %collective-permute-start.31 = (bf16[128,2304]{1,0:T(8,128)(2,1)S(1)}, bf16[128,2304]{1,0:T(8,128)(2,1)S(1)}, u32[]{:S(2)}, u32[]{:S(2)}) collective-permute-start(bf16[128,2304]{1,0:T(8,128)(2,1)S(1)} %convolution_convert_fusion.1), channel_id=1, source_target_pairs={{0,4},{4,0},{8,12},{12,8},{16,20},{20,16},{24,28},{28,24},{1,5},{5... | collective-permute-start | bytes 1769480 | tf_op jit(solution)/shard_map/ppermute | solution.py:19
  77.6 6.7 %collective-permute-start.33 = (bf16[32,2304]{1,0:T(8,128)(2,1)S(1)}, bf16[32,2304]{1,0:T(8,128)(2,1)S(1)}, u32[]{:S(2)}, u32[]{:S(2)}) collective-permute-start(bf16[32,2304]{1,0:T(8,128)(2,1)S(1)} %get-tuple-element.57), channel_id=1, source_target_pairs={{0,8},{4,12},{8,0},{12,4},{16,24},{20,28},{24,16},{28,20},{1,9},{5... | collective-permute-start | bytes 442376 | tf_op jit(solution)/shard_map/ppermute | solution.py:19
  79.0 9.5 %collective-permute-start.37 = (bf16[32,2304]{1,0:T(8,128)(2,1)S(1)}, bf16[32,2304]{1,0:T(8,128)(2,1)S(1)}, u32[]{:S(2)}, u32[]{:S(2)}) collective-permute-start(bf16[32,2304]{1,0:T(8,128)(2,1)S(1)} %get-tuple-element.59), channel_id=1, source_target_pairs={{0,16},{4,20},{8,24},{12,28},{16,0},{20,4},{24,8},{28,12},{1,17},{... | collective-permute-start | bytes 442376 | tf_op jit(solution)/shard_map/ppermute | solution.py:19
  79.5 8.9 %collective-permute-start.38 = (bf16[32,2304]{1,0:T(8,128)(2,1)S(1)}, bf16[32,2304]{1,0:T(8,128)(2,1)S(1)}, u32[]{:S(2)}, u32[]{:S(2)}) collective-permute-start(bf16[32,2304]{1,0:T(8,128)(2,1)S(1)} %get-tuple-element.58), channel_id=1, source_target_pairs={{0,24},{4,28},{8,16},{12,20},{16,8},{20,12},{24,0},{28,4},{1,25},{... | collective-permute-start | bytes 442376 | tf_op jit(solution)/shard_map/ppermute | solution.py:19
  84.9 15.5 %copy-start.7 = (f32[2304]{0:T(1024)S(1)}, f32[2304]{0:T(1024)}, u32[]{:S(2)}) copy-start(f32[2304]{0:T(1024)} %param.25) | copy-start | bytes 27652
  84.9 6.5 %collective-permute-start.34 = (bf16[32,2304]{1,0:T(8,128)(2,1)S(1)}, bf16[32,2304]{1,0:T(8,128)(2,1)S(1)}, u32[]{:S(2)}, u32[]{:S(2)}) collective-permute-start(bf16[32,2304]{1,0:T(8,128)(2,1)S(1)} %get-tuple-element.54), channel_id=1, source_target_pairs={{0,8},{4,12},{8,0},{12,4},{16,24},{20,28},{24,16},{28,20},{1,9},{5... | collective-permute-start | bytes 442376 | tf_op jit(solution)/shard_map/ppermute | solution.py:19
  86.4 7.6 %collective-permute-start.35 = (bf16[32,2304]{1,0:T(8,128)(2,1)S(1)}, bf16[32,2304]{1,0:T(8,128)(2,1)S(1)}, u32[]{:S(2)}, u32[]{:S(2)}) collective-permute-start(bf16[32,2304]{1,0:T(8,128)(2,1)S(1)} %get-tuple-element.56), channel_id=1, source_target_pairs={{0,16},{4,20},{8,24},{12,28},{16,0},{20,4},{24,8},{28,12},{1,17},{... | collective-permute-start | bytes 442376 | tf_op jit(solution)/shard_map/ppermute | solution.py:19
  86.9 7.1 %collective-permute-start.36 = (bf16[32,2304]{1,0:T(8,128)(2,1)S(1)}, bf16[32,2304]{1,0:T(8,128)(2,1)S(1)}, u32[]{:S(2)}, u32[]{:S(2)}) collective-permute-start(bf16[32,2304]{1,0:T(8,128)(2,1)S(1)} %get-tuple-element.55), channel_id=1, source_target_pairs={{0,24},{4,28},{8,16},{12,20},{16,8},{20,12},{24,0},{28,4},{1,25},{... | collective-permute-start | bytes 442376 | tf_op jit(solution)/shard_map/ppermute | solution.py:19
  88.6 5.4 %collective-permute-start.39 = (bf16[32,2304]{1,0:T(8,128)(2,1)S(1)}, bf16[32,2304]{1,0:T(8,128)(2,1)S(1)}, u32[]{:S(2)}, u32[]{:S(2)}) collective-permute-start(bf16[32,2304]{1,0:T(8,128)(2,1)S(1)} %add_convert_fusion.2), channel_id=1, source_target_pairs={{0,1},{1,0},{2,3},{3,2},{4,5},{5,4},{6,7},{7,6},{8,9},{9,8},{10,11... | collective-permute-start | bytes 442376 | tf_op jit(solution)/shard_map/ppermute | solution.py:19
  94.1 6.2 %collective-permute-start.40 = (bf16[16,2304]{1,0:T(8,128)(2,1)S(1)}, bf16[16,2304]{1,0:T(8,128)(2,1)S(1)}, u32[]{:S(2)}, u32[]{:S(2)}) collective-permute-start(bf16[16,2304]{1,0:T(8,128)(2,1)S(1)} %fusion.9), channel_id=1, source_target_pairs={{0,2},{1,3},{2,0},{3,1},{4,6},{5,7},{6,4},{7,5},{8,10},{9,11},{10,... | collective-permute-start | bytes 221192 | tf_op jit(solution)/shard_map/ppermute | solution.py:19
  (4 other events, 8.7 us)

commit v16 on v15

--- a/solution.py
+++ b/solution.py
@@ -154,7 +154,7 @@
     count, (size, width) = len(pieces), pieces[0].shape
     units = gate.shape[2]
     return call(
-        functools.partial(hidden_kernel, count, e, min(256, units)),
+        functools.partial(hidden_kernel, count, e, min(512, units)),
         [*pieces, gate, up],
         [VMEM_SPEC] * (count + 2),
         [((count * size, units), jnp.bfloat16)],
@@ -205,7 +205,7 @@
 def run_down(hidden, down, e, scalars, table, top, feats, pairs, more=(), chunk=None):
     rows, units = hidden.shape
     width = down.shape[2]
-    tile = 256 if width % 256 == 0 else 128
+    tile = max(t for t in range(128, 769, 128) if width % t == 0)
     outs = [((rows, width), jnp.bfloat16)]
     if chunk is not None:
         outs = [((rows // pairs // 2, width), jnp.bfloat16)] * pairs

time: 101 us -> 101 us (level)
  no operation moved by 1% of the time
where the time goes in v16:
time: 101 us
  starting transfers between devices  46 us (46%)
  waiting for transfers between devices  29.1 us (29%)
  Pallas kernels  15.4 us (15%)
  matrix products  5.52 us (5%)
  other arithmetic  2.25 us (2%)
  local copies, waits for them, and re-layouts  1.43 us (1%)
  between operations  1.27 us (1%)
    ppermute x41, starting transfers between devices, swap(): lax.ppermute(value, axis, [(i, i ^ r) for i in range(lax.axis_size(axis))])  46 us
    ppermute x41, waiting for transfers between devices, swap(): lax.ppermute(value, axis, [(i, i ^ r) for i in range(lax.axis_size(axis))])  29.1 us
    pallas_call x8, Pallas kernels, call(): pl.pallas_call(body, in_specs=specs, out_specs=[VMEM_SPEC] * len(outs), o...  15.4 us
    dot_general x8, matrix products, dot(): return jnp.dot(a, b, preferred_element_type=jnp.float32)  5.52 us
  transfers between devices with their start and end apart: 41, of which 15 were waited for; matrix products, arithmetic and copies ran while one was open for 6% of the time, Pallas kernels for 12%

profile of v16, /device:TPU:0, one launch (start us, length us, event | category | flops | bytes accessed | tf_op | source)
XLA Modules:
  0.0 101.0 jit_solution(1725373036913822764)
XLA Ops:
  0.6 0.9 pad_add_fusion.both
  1.7 2.9 %collective-permute-start = (bf16[16,128]{1,0:T(8,128)(2,1)S(1)}, bf16[16,128]{1,0:T(8,128)(2,1)S(1)}, u32[]{:S(2)}, u32[]{:S(2)}) collective-permute-start(bf16[16,128]{1,0:T(8,128)(2,1)S(1)} %shard_map.140), channel_id=1, source_target_pairs={{0,8},{4,12},{8,0},{12,4},{16,24},{20,28},{24,16},{28,20},{1,9},{5... | collective-permute-start | bytes 12296 | tf_op jit(solution)/shard_map/ppermute | solution.py:19
  4.6 1.5 %collective-permute-start.1 = (bf16[16,128]{1,0:T(8,128)(2,1)S(1)}, bf16[16,128]{1,0:T(8,128)(2,1)S(1)}, u32[]{:S(2)}, u32[]{:S(2)}) collective-permute-start(bf16[16,128]{1,0:T(8,128)(2,1)S(1)} %shard_map.140), channel_id=1, source_target_pairs={{0,16},{4,20},{8,24},{12,28},{16,0},{20,4},{24,8},{28,12},{1,17},{... | collective-permute-start | bytes 12296 | tf_op jit(solution)/shard_map/ppermute | solution.py:19
  6.2 2.0 %collective-permute-start.3 = (bf16[64,2304]{1,0:T(8,128)(2,1)}, bf16[64,2304]{1,0:T(8,128)(2,1)S(1)}, u32[]{:S(2)}, u32[]{:S(2)}) collective-permute-start(bf16[64,2304]{1,0:T(8,128)(2,1)} %refs_0_), channel_id=1, source_target_pairs={{0,8},{4,12},{8,0},{12,4},{16,24},{20,28},{24,16},{28,20},{1,9},{5... | collective-permute-start | bytes 884744 | tf_op jit(solution)/shard_map/ppermute | solution.py:19
  8.2 1.5 %collective-permute-start.4 = (bf16[64,2304]{1,0:T(8,128)(2,1)}, bf16[64,2304]{1,0:T(8,128)(2,1)S(1)}, u32[]{:S(2)}, u32[]{:S(2)}) collective-permute-start(bf16[64,2304]{1,0:T(8,128)(2,1)} %refs_0_), channel_id=1, source_target_pairs={{0,16},{4,20},{8,24},{12,28},{16,0},{20,4},{24,8},{28,12},{1,17},{... | collective-permute-start | bytes 884744 | tf_op jit(solution)/shard_map/ppermute | solution.py:19
  9.8 0.9 collective-permute-done.2
  10.7 1.6 %collective-permute-start.10 = (bf16[64,128]{1,0:T(8,128)(2,1)S(1)}, bf16[64,128]{1,0:T(8,128)(2,1)S(1)}, u32[]{:S(2)}, u32[]{:S(2)}) collective-permute-start(bf16[64,128]{1,0:T(8,128)(2,1)S(1)} %pad_maximum_fusion.3), channel_id=1, source_target_pairs={{0,1},{1,0},{2,3},{3,2},{4,5},{5,4},{6,7},{7,6},{8,9},{9,8},{10,11... | collective-permute-start | bytes 49160 | tf_op jit(solution)/shard_map/ppermute | solution.py:19
  12.3 1.0 copy-done.4
  13.3 3.9 %shard_map.141 = (bf16[64,2304]{1,0:T(8,128)(2,1)S(1)}, bf16[1,2304,1024]{2,1,0:T(8,128)(2,1)S(1)}, bf16[1,2304,1024]{2,1,0:T(8,128)(2,1)S(1)}) custom-call(bf16[64,2304]{1,0:T(8,128)(2,1)S(1)} %copy-done.4, bf16[1,2304,1024]{2,1,0:T(8,128)(2,1)} %refs_1_.1, bf16[1,2304,1024]{2,1,0:T(8,128)(2,1)} %refs_2_.1), custom_call_target="tpu_custom_call" | custom-call | flops 2676326400 | bytes 19464192 | tf_op jit(solution)/shard_map/pallas_call | solution.py:49
  17.2 2.7 %collective-permute-start.11 = (bf16[128,128]{1,0:T(8,128)(2,1)S(1)}, bf16[128,128]{1,0:T(8,128)(2,1)S(1)}, u32[]{:S(2)}, u32[]{:S(2)}) collective-permute-start(bf16[128,128]{1,0:T(8,128)(2,1)S(1)} %pad_maximum_fusion.2), channel_id=1, source_target_pairs={{0,2},{1,3},{2,0},{3,1},{4,6},{5,7},{6,4},{7,5},{8,10},{9,11},{10,... | collective-permute-start | bytes 98312 | tf_op jit(solution)/shard_map/ppermute | solution.py:19
  19.9 2.5 %collective-permute-done.4.refs_2_ = bf16[64,2304]{1,0:T(8,128)(2,1)S(1)} collective-permute-done((bf16[64,2304]{1,0:T(8,128)(2,1)}, bf16[64,2304]{1,0:T(8,128)(2,1)S(1)}, u32[]{:S(2)}, u32[]{:S(2)}) %collective-permute-start.4) | collective-permute-done | bytes 294944 | tf_op jit(solution)/shard_map/ppermute | solution.py:19
  22.9 2.6 %shard_map.142.hidden = bf16[256,1024]{1,0:T(8,128)(2,1)S(1)} custom-call(bf16[64,2304]{1,0:T(8,128)(2,1)S(1)} %get-tuple-element.30.refs_0_, bf16[64,2304]{1,0:T(8,128)(2,1)S(1)} %collective-permute-done.3.refs_1_, bf16[64,2304]{1,0:T(8,128)(2,1)S(1)} %collective-permute-done.4.refs_2_, bf16[64,2304]{1,0:T(8,128)(2,1)S(1)} %collective-permute-done.5.refs_3_, ...), custom_call_target="tpu_custom_call" | custom-call | flops 2415919104 | bytes 9437184 | tf_op jit(solution)/shard_map/pallas_call | solution.py:49
  25.7 2.0 %shard_map.144 = bf16[256,2304]{1,0:T(8,128)(2,1)S(1)} custom-call(s32[3]{0:T(128)S(1)} %pad_add_fusion.1.scalars, bf16[256,1024]{1,0:T(8,128)(2,1)S(1)} %shard_map.142.hidden, bf16[1,1024,2304]{2,1,0:T(8,128)(2,1)S(1)} %bitcast.57, bf16[256,128]{1,0:T(8,128)(2,1)S(1)} %constant_dynamic-update-slice_fusion.table), custom_call_target="tpu_custom_call" | custom-call | flops 1207959552 | bytes 4718592 | tf_op jit(solution)/shard_map/pallas_call | solution.py:49
  28.2 2.6 %shard_map.143.hidden = bf16[256,1024]{1,0:T(8,128)(2,1)S(1)} custom-call(bf16[64,2304]{1,0:T(8,128)(2,1)S(1)} %collective-permute-done.6.refs_0_.x, bf16[64,2304]{1,0:T(8,128)(2,1)S(1)} %collective-permute-done.7.refs_1_, bf16[64,2304]{1,0:T(8,128)(2,1)S(1)} %collective-permute-done.8.refs_2_, bf16[64,2304]{1,0:T(8,128)(2,1)S(1)} %collective-permute-done.9.refs_3_, ...), custom_call_target="tpu_custom_call" | custom-call | flops 2415919104 | bytes 9437184 | tf_op jit(solution)/shard_map/pallas_call | solution.py:49
  30.9 1.3 %shard_map.146 = (bf16[32,2304]{1,0:T(8,128)(2,1)S(1)}, bf16[32,2304]{1,0:T(8,128)(2,1)S(1)}, bf16[32,2304]{1,0:T(8,128)(2,1)S(1)}, bf16[32,2304]{1,0:T(8,128)(2,1)S(1)}) custom-call(s32[3]{0:T(128)S(1)} %pad_add_fusion.1.scalars, bf16[256,1024]{1,0:T(8,128)(2,1)S(1)} %shard_map.143.hidden, bf16[1,1024,2304]{2,1,0:T(8,128)(2,1)S(1)} %bitcast.57, ...), custom_call_target="tpu_custom_call" | custom-call | flops 1207959552 | bytes 4718592 | tf_op jit(solution)/shard_map/pallas_call | solution.py:49
  32.2 1.5 %collective-permute-start.17 = (bf16[32,2304]{1,0:T(8,128)(2,1)S(1)}, bf16[32,2304]{1,0:T(8,128)(2,1)S(1)}, u32[]{:S(2)}, u32[]{:S(2)}) collective-permute-start(bf16[32,2304]{1,0:T(8,128)(2,1)S(1)} %get-tuple-element.44), channel_id=1, source_target_pairs={{0,24},{4,28},{8,16},{12,20},{16,8},{20,12},{24,0},{28,4},{1,25},{... | collective-permute-start | bytes 442376 | tf_op jit(solution)/shard_map/ppermute | solution.py:19
  33.7 1.5 %collective-permute-start.18 = (bf16[32,2304]{1,0:T(8,128)(2,1)S(1)}, bf16[32,2304]{1,0:T(8,128)(2,1)S(1)}, u32[]{:S(2)}, u32[]{:S(2)}) collective-permute-start(bf16[32,2304]{1,0:T(8,128)(2,1)S(1)} %get-tuple-element.48), channel_id=1, source_target_pairs={{0,8},{4,12},{8,0},{12,4},{16,24},{20,28},{24,16},{28,20},{1,9},{5... | collective-permute-start | bytes 442376 | tf_op jit(solution)/shard_map/ppermute | solution.py:19
  35.8 1.4 %shard_map.145 = (bf16[32,2304]{1,0:T(8,128)(2,1)S(1)}, bf16[32,2304]{1,0:T(8,128)(2,1)S(1)}, bf16[32,2304]{1,0:T(8,128)(2,1)S(1)}, bf16[32,2304]{1,0:T(8,128)(2,1)S(1)}) custom-call(s32[3]{0:T(128)S(1)} %pad_add_fusion.1.scalars, bf16[256,1024]{1,0:T(8,128)(2,1)S(1)} %shard_map.143.hidden, bf16[1,1024,2304]{2,1,0:T(8,128)(2,1)S(1)} %bitcast.57, ...), custom_call_target="tpu_custom_call" | custom-call | flops 1207959552 | bytes 4718592 | tf_op jit(solution)/shard_map/pallas_call | solution.py:49
  37.1 0.9 collective-permute-start.14
  38.0 1.2 %collective-permute-start.15 = (bf16[32,2304]{1,0:T(8,128)(2,1)S(1)}, bf16[32,2304]{1,0:T(8,128)(2,1)S(1)}, u32[]{:S(2)}, u32[]{:S(2)}) collective-permute-start(bf16[32,2304]{1,0:T(8,128)(2,1)S(1)} %get-tuple-element.42), channel_id=1, source_target_pairs={{0,16},{4,20},{8,24},{12,28},{16,0},{20,4},{24,8},{28,12},{1,17},{... | collective-permute-start | bytes 442376 | tf_op jit(solution)/shard_map/ppermute | solution.py:19
  39.2 0.7 collective-permute-done.17
  39.9 1.4 %collective-permute-start.16 = (bf16[32,2304]{1,0:T(8,128)(2,1)S(1)}, bf16[32,2304]{1,0:T(8,128)(2,1)S(1)}, u32[]{:S(2)}, u32[]{:S(2)}) collective-permute-start(bf16[32,2304]{1,0:T(8,128)(2,1)S(1)} %get-tuple-element.43), channel_id=1, source_target_pairs={{0,24},{4,28},{8,16},{12,20},{16,8},{20,12},{24,0},{28,4},{1,25},{... | collective-permute-start | bytes 442376 | tf_op jit(solution)/shard_map/ppermute | solution.py:19
  41.3 1.4 %shard_map.147 = (f32[32,2304]{1,0:T(8,128)S(1)}, f32[32,2304]{1,0:T(8,128)S(1)}) custom-call(s32[3]{0:T(128)S(1)} %pad_add_fusion.1.scalars, bf16[64,2304]{1,0:T(8,128)(2,1)S(1)} %collective-permute-done.6.refs_0_.x, bf16[2304,256]{1,0:T(8,128)(2,1)S(1)} %copy-done.1, bf16[2304,256]{1,0:T(8,128)(2,1)S(1)} %copy-done.2, bf16[256,2304]{1,0:T(8,128)(2,1)S(1)} %copy-done.3), custom_call_target="tpu_custom_call" | custom-call | flops 226492416 | bytes 3538944 | tf_op jit(solution)/shard_map/pallas_call | solution.py:49
  43.2 1.7 %collective-permute-start.20 = (bf16[32,2304]{1,0:T(8,128)(2,1)S(1)}, bf16[32,2304]{1,0:T(8,128)(2,1)S(1)}, u32[]{:S(2)}, u32[]{:S(2)}) collective-permute-start(bf16[32,2304]{1,0:T(8,128)(2,1)S(1)} %add_convert_fusion.5), channel_id=1, source_target_pairs={{0,1},{1,0},{2,3},{3,2},{4,5},{5,4},{6,7},{7,6},{8,9},{9,8},{10,11... | collective-permute-start | bytes 442376 | tf_op jit(solution)/shard_map/ppermute | solution.py:19
  44.8 1.4 %collective-permute-done.14 = bf16[32,2304]{1,0:T(8,128)(2,1)S(1)} collective-permute-done((bf16[32,2304]{1,0:T(8,128)(2,1)S(1)}, bf16[32,2304]{1,0:T(8,128)(2,1)S(1)}, u32[]{:S(2)}, u32[]{:S(2)}) %collective-permute-start.14) | collective-permute-done | bytes 147488 | tf_op jit(solution)/shard_map/ppermute | solution.py:19
  46.2 2.2 %collective-permute-done.16 = bf16[32,2304]{1,0:T(8,128)(2,1)S(1)} collective-permute-done((bf16[32,2304]{1,0:T(8,128)(2,1)S(1)}, bf16[32,2304]{1,0:T(8,128)(2,1)S(1)}, u32[]{:S(2)}, u32[]{:S(2)}) %collective-permute-start.16) | collective-permute-done | bytes 147488 | tf_op jit(solution)/shard_map/ppermute | solution.py:19
  48.6 2.7 %collective-permute-start.21 = (bf16[2,16,2304]{2,1,0:T(8,128)(2,1)S(1)}, bf16[2,16,2304]{2,1,0:T(8,128)(2,1)S(1)}, u32[]{:S(2)}, u32[]{:S(2)}) collective-permute-start(bf16[2,16,2304]{2,1,0:T(8,128)(2,1)S(1)} %bitcast.105), channel_id=1, source_target_pairs={{0,2},{1,3},{2,0},{3,1},{4,6},{5,7},{6,4},{7,5},{8,10},{9,11},{10,... | collective-permute-start | bytes 442376 | tf_op jit(solution)/shard_map/ppermute | solution.py:19
  51.3 6.5 %collective-permute-done.21 = bf16[2,16,2304]{2,1,0:T(8,128)(2,1)S(1)} collective-permute-done((bf16[2,16,2304]{2,1,0:T(8,128)(2,1)S(1)}, bf16[2,16,2304]{2,1,0:T(8,128)(2,1)S(1)}, u32[]{:S(2)}, u32[]{:S(2)}) %collective-permute-start.21) | collective-permute-done | bytes 147488 | tf_op jit(solution)/shard_map/ppermute | solution.py:19
  57.8 0.7 collective-permute-start.22
  58.5 1.6 %collective-permute-start.27 = (bf16[32,2304]{1,0:T(8,128)(2,1)S(1)}, bf16[32,2304]{1,0:T(8,128)(2,1)S(1)}, u32[]{:S(2)}, u32[]{:S(2)}) collective-permute-start(bf16[32,2304]{1,0:T(8,128)(2,1)S(1)} %bitcast.101), channel_id=1, source_target_pairs={{0,8},{4,12},{8,0},{12,4},{16,24},{20,28},{24,16},{28,20},{1,9},{5... | collective-permute-start | bytes 442376 | tf_op jit(solution)/shard_map/ppermute | solution.py:19
  60.5 2.5 %collective-permute-done.22 = bf16[32,2304]{1,0:T(8,128)(2,1)S(1)} collective-permute-done((bf16[32,2304]{1,0:T(8,128)(2,1)S(1)}, bf16[32,2304]{1,0:T(8,128)(2,1)S(1)}, u32[]{:S(2)}, u32[]{:S(2)}) %collective-permute-start.22) | collective-permute-done | bytes 147488 | tf_op jit(solution)/shard_map/ppermute | solution.py:19
  63.0 1.4 %collective-permute-start.29 = (bf16[32,2304]{1,0:T(8,128)(2,1)S(1)}, bf16[32,2304]{1,0:T(8,128)(2,1)S(1)}, u32[]{:S(2)}, u32[]{:S(2)}) collective-permute-start(bf16[32,2304]{1,0:T(8,128)(2,1)S(1)} %bitcast.103), channel_id=1, source_target_pairs={{0,24},{4,28},{8,16},{12,20},{16,8},{20,12},{24,0},{28,4},{1,25},{... | collective-permute-start | bytes 442376 | tf_op jit(solution)/shard_map/ppermute | solution.py:19
  64.4 1.5 %collective-permute-start.25 = (bf16[32,2304]{1,0:T(8,128)(2,1)S(1)}, bf16[32,2304]{1,0:T(8,128)(2,1)S(1)}, u32[]{:S(2)}, u32[]{:S(2)}) collective-permute-start(bf16[32,2304]{1,0:T(8,128)(2,1)S(1)} %collective-permute-done.22), channel_id=1, source_target_pairs={{0,24},{4,28},{8,16},{12,20},{16,8},{20,12},{24,0},{28,4},{1,25},{... | collective-permute-start | bytes 442376 | tf_op jit(solution)/shard_map/ppermute | solution.py:19
  65.9 1.6 %collective-permute-start.23 = (bf16[32,2304]{1,0:T(8,128)(2,1)S(1)}, bf16[32,2304]{1,0:T(8,128)(2,1)S(1)}, u32[]{:S(2)}, u32[]{:S(2)}) collective-permute-start(bf16[32,2304]{1,0:T(8,128)(2,1)S(1)} %collective-permute-done.22), channel_id=1, source_target_pairs={{0,8},{4,12},{8,0},{12,4},{16,24},{20,28},{24,16},{28,20},{1,9},{5... | collective-permute-start | bytes 442376 | tf_op jit(solution)/shard_map/ppermute | solution.py:19
  67.9 2.1 %collective-permute-done.28 = bf16[32,2304]{1,0:T(8,128)(2,1)S(1)} collective-permute-done((bf16[32,2304]{1,0:T(8,128)(2,1)S(1)}, bf16[32,2304]{1,0:T(8,128)(2,1)S(1)}, u32[]{:S(2)}, u32[]{:S(2)}) %collective-permute-start.28) | collective-permute-done | bytes 147488 | tf_op jit(solution)/shard_map/ppermute | solution.py:19
  70.8 2.1 %fusion.4 = bf16[128,512]{1,0:T(8,128)(2,1)S(1)} fusion(bf16[128,2304]{1,0:T(8,128)(2,1)S(1)} %bitcast.61, bf16[2304,512]{1,0:T(8,128)(2,1)} %param.22, f32[512]{0:T(512)S(1)} %copy-done.6), kind=kOutput, calls=%fused_computation.12 | convolution fusion | flops 302186496 | bytes 3082240 | tf_op jit(solution)/shard_map/dot_general | solution.py:23
  74.0 0.8 collective-permute-done.24
  77.5 1.4 %collective-permute-start.33 = (bf16[32,2304]{1,0:T(8,128)(2,1)S(1)}, bf16[32,2304]{1,0:T(8,128)(2,1)S(1)}, u32[]{:S(2)}, u32[]{:S(2)}) collective-permute-start(bf16[32,2304]{1,0:T(8,128)(2,1)S(1)} %get-tuple-element.57), channel_id=1, source_target_pairs={{0,8},{4,12},{8,0},{12,4},{16,24},{20,28},{24,16},{28,20},{1,9},{5... | collective-permute-start | bytes 442376 | tf_op jit(solution)/shard_map/ppermute | solution.py:19
  79.5 1.6 %collective-permute-start.38 = (bf16[32,2304]{1,0:T(8,128)(2,1)S(1)}, bf16[32,2304]{1,0:T(8,128)(2,1)S(1)}, u32[]{:S(2)}, u32[]{:S(2)}) collective-permute-start(bf16[32,2304]{1,0:T(8,128)(2,1)S(1)} %get-tuple-element.58), channel_id=1, source_target_pairs={{0,24},{4,28},{8,16},{12,20},{16,8},{20,12},{24,0},{28,4},{1,25},{... | collective-permute-start | bytes 442376 | tf_op jit(solution)/shard_map/ppermute | solution.py:19
  82.2 2.1 %collective-permute-done.33 = bf16[32,2304]{1,0:T(8,128)(2,1)S(1)} collective-permute-done((bf16[32,2304]{1,0:T(8,128)(2,1)S(1)}, bf16[32,2304]{1,0:T(8,128)(2,1)S(1)}, u32[]{:S(2)}, u32[]{:S(2)}) %collective-permute-start.33) | collective-permute-done | bytes 147488 | tf_op jit(solution)/shard_map/ppermute | solution.py:19
  84.9 1.4 %collective-permute-start.34 = (bf16[32,2304]{1,0:T(8,128)(2,1)S(1)}, bf16[32,2304]{1,0:T(8,128)(2,1)S(1)}, u32[]{:S(2)}, u32[]{:S(2)}) collective-permute-start(bf16[32,2304]{1,0:T(8,128)(2,1)S(1)} %get-tuple-element.54), channel_id=1, source_target_pairs={{0,8},{4,12},{8,0},{12,4},{16,24},{20,28},{24,16},{28,20},{1,9},{5... | collective-permute-start | bytes 442376 | tf_op jit(solution)/shard_map/ppermute | solution.py:19
  86.8 1.7 %collective-permute-start.36 = (bf16[32,2304]{1,0:T(8,128)(2,1)S(1)}, bf16[32,2304]{1,0:T(8,128)(2,1)S(1)}, u32[]{:S(2)}, u32[]{:S(2)}) collective-permute-start(bf16[32,2304]{1,0:T(8,128)(2,1)S(1)} %get-tuple-element.55), channel_id=1, source_target_pairs={{0,24},{4,28},{8,16},{12,20},{16,8},{20,12},{24,0},{28,4},{1,25},{... | collective-permute-start | bytes 442376 | tf_op jit(solution)/shard_map/ppermute | solution.py:19
  88.5 1.4 %collective-permute-start.39 = (bf16[32,2304]{1,0:T(8,128)(2,1)S(1)}, bf16[32,2304]{1,0:T(8,128)(2,1)S(1)}, u32[]{:S(2)}, u32[]{:S(2)}) collective-permute-start(bf16[32,2304]{1,0:T(8,128)(2,1)S(1)} %add_convert_fusion.2), channel_id=1, source_target_pairs={{0,1},{1,0},{2,3},{3,2},{4,5},{5,4},{6,7},{7,6},{8,9},{9,8},{10,11... | collective-permute-start | bytes 442376 | tf_op jit(solution)/shard_map/ppermute | solution.py:19
  89.9 1.4 %collective-permute-done.34 = bf16[32,2304]{1,0:T(8,128)(2,1)S(1)} collective-permute-done((bf16[32,2304]{1,0:T(8,128)(2,1)S(1)}, bf16[32,2304]{1,0:T(8,128)(2,1)S(1)}, u32[]{:S(2)}, u32[]{:S(2)}) %collective-permute-start.34) | collective-permute-done | bytes 147488 | tf_op jit(solution)/shard_map/ppermute | solution.py:19
  91.3 2.6 %collective-permute-done.35 = bf16[32,2304]{1,0:T(8,128)(2,1)S(1)} collective-permute-done((bf16[32,2304]{1,0:T(8,128)(2,1)S(1)}, bf16[32,2304]{1,0:T(8,128)(2,1)S(1)}, u32[]{:S(2)}, u32[]{:S(2)}) %collective-permute-start.35) | collective-permute-done | bytes 147488 | tf_op jit(solution)/shard_map/ppermute | solution.py:19
  94.0 3.9 %collective-permute-start.40 = (bf16[16,2304]{1,0:T(8,128)(2,1)S(1)}, bf16[16,2304]{1,0:T(8,128)(2,1)S(1)}, u32[]{:S(2)}, u32[]{:S(2)}) collective-permute-start(bf16[16,2304]{1,0:T(8,128)(2,1)S(1)} %fusion.9), channel_id=1, source_target_pairs={{0,2},{1,3},{2,0},{3,1},{4,6},{5,7},{6,4},{7,5},{8,10},{9,11},{10,... | collective-permute-start | bytes 221192 | tf_op jit(solution)/shard_map/ppermute | solution.py:19
  98.0 2.3 %collective-permute-done.40 = bf16[16,2304]{1,0:T(8,128)(2,1)S(1)} collective-permute-done((bf16[16,2304]{1,0:T(8,128)(2,1)S(1)}, bf16[16,2304]{1,0:T(8,128)(2,1)S(1)}, u32[]{:S(2)}, u32[]{:S(2)}) %collective-permute-start.40) | collective-permute-done | bytes 73760 | tf_op jit(solution)/shard_map/ppermute | solution.py:19
  100.3 0.7 fusion.8
  (125 shorter events, 10.4 us)
Async XLA Ops:
  0.6 72.3 %copy-start = (bf16[512,2304]{1,0:T(8,128)(2,1)S(1)}, bf16[512,2304]{1,0:T(8,128)(2,1)}, u32[]{:S(2)}) copy-start(bf16[512,2304]{1,0:T(8,128)(2,1)} %param.24) | copy-start | bytes 7077892
  1.7 4.5 %collective-permute-start = (bf16[16,128]{1,0:T(8,128)(2,1)S(1)}, bf16[16,128]{1,0:T(8,128)(2,1)S(1)}, u32[]{:S(2)}, u32[]{:S(2)}) collective-permute-start(bf16[16,128]{1,0:T(8,128)(2,1)S(1)} %shard_map.140), channel_id=1, source_target_pairs={{0,8},{4,12},{8,0},{12,4},{16,24},{20,28},{24,16},{28,20},{1,9},{5... | collective-permute-start | bytes 12296 | tf_op jit(solution)/shard_map/ppermute | solution.py:19
  4.6 5.1 %collective-permute-start.1 = (bf16[16,128]{1,0:T(8,128)(2,1)S(1)}, bf16[16,128]{1,0:T(8,128)(2,1)S(1)}, u32[]{:S(2)}, u32[]{:S(2)}) collective-permute-start(bf16[16,128]{1,0:T(8,128)(2,1)S(1)} %shard_map.140), channel_id=1, source_target_pairs={{0,16},{4,20},{8,24},{12,28},{16,0},{20,4},{24,8},{28,12},{1,17},{... | collective-permute-start | bytes 12296 | tf_op jit(solution)/shard_map/ppermute | solution.py:19
  6.1 4.6 %collective-permute-start.2 = (bf16[16,128]{1,0:T(8,128)(2,1)S(1)}, bf16[16,128]{1,0:T(8,128)(2,1)S(1)}, u32[]{:S(2)}, u32[]{:S(2)}) collective-permute-start(bf16[16,128]{1,0:T(8,128)(2,1)S(1)} %shard_map.140), channel_id=1, source_target_pairs={{0,24},{4,28},{8,16},{12,20},{16,8},{20,12},{24,0},{28,4},{1,25},{... | collective-permute-start | bytes 12296 | tf_op jit(solution)/shard_map/ppermute | solution.py:19
  6.2 13.6 %collective-permute-start.3 = (bf16[64,2304]{1,0:T(8,128)(2,1)}, bf16[64,2304]{1,0:T(8,128)(2,1)S(1)}, u32[]{:S(2)}, u32[]{:S(2)}) collective-permute-start(bf16[64,2304]{1,0:T(8,128)(2,1)} %refs_0_), channel_id=1, source_target_pairs={{0,8},{4,12},{8,0},{12,4},{16,24},{20,28},{24,16},{28,20},{1,9},{5... | collective-permute-start | bytes 884744 | tf_op jit(solution)/shard_map/ppermute | solution.py:19
  8.2 14.2 %collective-permute-start.4 = (bf16[64,2304]{1,0:T(8,128)(2,1)}, bf16[64,2304]{1,0:T(8,128)(2,1)S(1)}, u32[]{:S(2)}, u32[]{:S(2)}) collective-permute-start(bf16[64,2304]{1,0:T(8,128)(2,1)} %refs_0_), channel_id=1, source_target_pairs={{0,16},{4,20},{8,24},{12,28},{16,0},{20,4},{24,8},{28,12},{1,17},{... | collective-permute-start | bytes 884744 | tf_op jit(solution)/shard_map/ppermute | solution.py:19
  9.8 12.7 %collective-permute-start.5 = (bf16[64,2304]{1,0:T(8,128)(2,1)}, bf16[64,2304]{1,0:T(8,128)(2,1)S(1)}, u32[]{:S(2)}, u32[]{:S(2)}) collective-permute-start(bf16[64,2304]{1,0:T(8,128)(2,1)} %refs_0_), channel_id=1, source_target_pairs={{0,24},{4,28},{8,16},{12,20},{16,8},{20,12},{24,0},{28,4},{1,25},{... | collective-permute-start | bytes 884744 | tf_op jit(solution)/shard_map/ppermute | solution.py:19
  9.8 15.8 %collective-permute-start.6 = (bf16[64,2304]{1,0:T(8,128)(2,1)}, bf16[64,2304]{1,0:T(8,128)(2,1)S(1)}, u32[]{:S(2)}, u32[]{:S(2)}) collective-permute-start(bf16[64,2304]{1,0:T(8,128)(2,1)} %refs_0_), channel_id=1, source_target_pairs={{0,4},{4,0},{8,12},{12,8},{16,20},{20,16},{24,28},{28,24},{1,5},{5... | collective-permute-start | bytes 884744 | tf_op jit(solution)/shard_map/ppermute | solution.py:19
  10.7 6.5 %collective-permute-start.10 = (bf16[64,128]{1,0:T(8,128)(2,1)S(1)}, bf16[64,128]{1,0:T(8,128)(2,1)S(1)}, u32[]{:S(2)}, u32[]{:S(2)}) collective-permute-start(bf16[64,128]{1,0:T(8,128)(2,1)S(1)} %pad_maximum_fusion.3), channel_id=1, source_target_pairs={{0,1},{1,0},{2,3},{3,2},{4,5},{5,4},{6,7},{7,6},{8,9},{9,8},{10,11... | collective-permute-start | bytes 49160 | tf_op jit(solution)/shard_map/ppermute | solution.py:19
  13.3 12.4 %slice-start = ((s8[4718592]{0:T(1024)(128)(4,1)}), s8[524288]{0:T(1024)(128)(4,1)S(1)}, s32[]{:S(2)}) async-start(s8[4718592]{0:T(1024)(128)(4,1)} %bitcast.56), calls=%async_computation | async-start | bytes 1048576
  17.2 5.7 %collective-permute-start.11 = (bf16[128,128]{1,0:T(8,128)(2,1)S(1)}, bf16[128,128]{1,0:T(8,128)(2,1)S(1)}, u32[]{:S(2)}, u32[]{:S(2)}) collective-permute-start(bf16[128,128]{1,0:T(8,128)(2,1)S(1)} %pad_maximum_fusion.2), channel_id=1, source_target_pairs={{0,2},{1,3},{2,0},{3,1},{4,6},{5,7},{6,4},{7,5},{8,10},{9,11},{10,... | collective-permute-start | bytes 98312 | tf_op jit(solution)/shard_map/ppermute | solution.py:19
  19.9 5.7 %collective-permute-start.7 = (bf16[64,2304]{1,0:T(8,128)(2,1)S(1)}, bf16[64,2304]{1,0:T(8,128)(2,1)S(1)}, u32[]{:S(2)}, u32[]{:S(2)}) collective-permute-start(bf16[64,2304]{1,0:T(8,128)(2,1)S(1)} %collective-permute-done.3.refs_1_), channel_id=1, source_target_pairs={{0,4},{4,0},{8,12},{12,8},{16,20},{20,16},{24,28},{28,24},{1,5},{5... | collective-permute-start | bytes 884744 | tf_op jit(solution)/shard_map/ppermute | solution.py:19
  22.4 3.2 %collective-permute-start.8 = (bf16[64,2304]{1,0:T(8,128)(2,1)S(1)}, bf16[64,2304]{1,0:T(8,128)(2,1)S(1)}, u32[]{:S(2)}, u32[]{:S(2)}) collective-permute-start(bf16[64,2304]{1,0:T(8,128)(2,1)S(1)} %collective-permute-done.4.refs_2_), channel_id=1, source_target_pairs={{0,4},{4,0},{8,12},{12,8},{16,20},{20,16},{24,28},{28,24},{1,5},{5... | collective-permute-start | bytes 884744 | tf_op jit(solution)/shard_map/ppermute | solution.py:19
  22.4 3.2 %collective-permute-start.9 = (bf16[64,2304]{1,0:T(8,128)(2,1)S(1)}, bf16[64,2304]{1,0:T(8,128)(2,1)S(1)}, u32[]{:S(2)}, u32[]{:S(2)}) collective-permute-start(bf16[64,2304]{1,0:T(8,128)(2,1)S(1)} %collective-permute-done.5.refs_3_), channel_id=1, source_target_pairs={{0,4},{4,0},{8,12},{12,8},{16,20},{20,16},{24,28},{28,24},{1,5},{5... | collective-permute-start | bytes 884744 | tf_op jit(solution)/shard_map/ppermute | solution.py:19
  27.6 3.2 %collective-permute-start.13 = (bf16[256,2304]{1,0:T(8,128)(2,1)S(1)}, bf16[256,2304]{1,0:T(8,128)(2,1)S(1)}, u32[]{:S(2)}, u32[]{:S(2)}) collective-permute-start(bf16[256,2304]{1,0:T(8,128)(2,1)S(1)} %shard_map.144), channel_id=1, source_target_pairs={{0,4},{4,0},{8,12},{12,8},{16,20},{20,16},{24,28},{28,24},{1,5},{5... | collective-permute-start | bytes 3538952 | tf_op jit(solution)/shard_map/ppermute | solution.py:19
  27.7 3.1 %collective-permute-start.12 = (bf16[256,128]{1,0:T(8,128)(2,1)S(1)}, bf16[256,128]{1,0:T(8,128)(2,1)S(1)}, u32[]{:S(2)}, u32[]{:S(2)}) collective-permute-start(bf16[256,128]{1,0:T(8,128)(2,1)S(1)} %constant_dynamic-update-slice_fusion.table), channel_id=1, source_target_pairs={{0,4},{4,0},{8,12},{12,8},{16,20},{20,16},{24,28},{28,24},{1,5},{5... | collective-permute-start | bytes 196616 | tf_op jit(solution)/shard_map/ppermute | solution.py:19
  32.2 7.7 %collective-permute-start.17 = (bf16[32,2304]{1,0:T(8,128)(2,1)S(1)}, bf16[32,2304]{1,0:T(8,128)(2,1)S(1)}, u32[]{:S(2)}, u32[]{:S(2)}) collective-permute-start(bf16[32,2304]{1,0:T(8,128)(2,1)S(1)} %get-tuple-element.44), channel_id=1, source_target_pairs={{0,24},{4,28},{8,16},{12,20},{16,8},{20,12},{24,0},{28,4},{1,25},{... | collective-permute-start | bytes 442376 | tf_op jit(solution)/shard_map/ppermute | solution.py:19
  33.7 9.4 %collective-permute-start.18 = (bf16[32,2304]{1,0:T(8,128)(2,1)S(1)}, bf16[32,2304]{1,0:T(8,128)(2,1)S(1)}, u32[]{:S(2)}, u32[]{:S(2)}) collective-permute-start(bf16[32,2304]{1,0:T(8,128)(2,1)S(1)} %get-tuple-element.48), channel_id=1, source_target_pairs={{0,8},{4,12},{8,0},{12,4},{16,24},{20,28},{24,16},{28,20},{1,9},{5... | collective-permute-start | bytes 442376 | tf_op jit(solution)/shard_map/ppermute | solution.py:19
  35.2 6.1 %copy-start.1 = (bf16[2304,256]{1,0:T(8,128)(2,1)S(1)}, bf16[2304,256]{1,0:T(8,128)(2,1)}, u32[]{:S(2)}) copy-start(bf16[2304,256]{1,0:T(8,128)(2,1)} %gate.1) | copy-start | bytes 3538948
  35.2 6.1 %copy-start.2 = (bf16[2304,256]{1,0:T(8,128)(2,1)S(1)}, bf16[2304,256]{1,0:T(8,128)(2,1)}, u32[]{:S(2)}) copy-start(bf16[2304,256]{1,0:T(8,128)(2,1)} %up.1) | copy-start | bytes 3538948
  35.2 6.1 %copy-start.3 = (bf16[256,2304]{1,0:T(8,128)(2,1)S(1)}, bf16[256,2304]{1,0:T(8,128)(2,1)}, u32[]{:S(2)}) copy-start(bf16[256,2304]{1,0:T(8,128)(2,1)} %down.7) | copy-start | bytes 3538948
  35.2 7.9 %collective-permute-start.19 = (bf16[32,2304]{1,0:T(8,128)(2,1)S(1)}, bf16[32,2304]{1,0:T(8,128)(2,1)S(1)}, u32[]{:S(2)}, u32[]{:S(2)}) collective-permute-start(bf16[32,2304]{1,0:T(8,128)(2,1)S(1)} %get-tuple-element.49), channel_id=1, source_target_pairs={{0,16},{4,20},{8,24},{12,28},{16,0},{20,4},{24,8},{28,12},{1,17},{... | collective-permute-start | bytes 442376 | tf_op jit(solution)/shard_map/ppermute | solution.py:19
  37.1 9.1 %collective-permute-start.14 = (bf16[32,2304]{1,0:T(8,128)(2,1)S(1)}, bf16[32,2304]{1,0:T(8,128)(2,1)S(1)}, u32[]{:S(2)}, u32[]{:S(2)}) collective-permute-start(bf16[32,2304]{1,0:T(8,128)(2,1)S(1)} %get-tuple-element.41), channel_id=1, source_target_pairs={{0,8},{4,12},{8,0},{12,4},{16,24},{20,28},{24,16},{28,20},{1,9},{5... | collective-permute-start | bytes 442376 | tf_op jit(solution)/shard_map/ppermute | solution.py:19
  38.0 8.2 %collective-permute-start.15 = (bf16[32,2304]{1,0:T(8,128)(2,1)S(1)}, bf16[32,2304]{1,0:T(8,128)(2,1)S(1)}, u32[]{:S(2)}, u32[]{:S(2)}) collective-permute-start(bf16[32,2304]{1,0:T(8,128)(2,1)S(1)} %get-tuple-element.42), channel_id=1, source_target_pairs={{0,16},{4,20},{8,24},{12,28},{16,0},{20,4},{24,8},{28,12},{1,17},{... | collective-permute-start | bytes 442376 | tf_op jit(solution)/shard_map/ppermute | solution.py:19
  39.9 8.6 %collective-permute-start.16 = (bf16[32,2304]{1,0:T(8,128)(2,1)S(1)}, bf16[32,2304]{1,0:T(8,128)(2,1)S(1)}, u32[]{:S(2)}, u32[]{:S(2)}) collective-permute-start(bf16[32,2304]{1,0:T(8,128)(2,1)S(1)} %get-tuple-element.43), channel_id=1, source_target_pairs={{0,24},{4,28},{8,16},{12,20},{16,8},{20,12},{24,0},{28,4},{1,25},{... | collective-permute-start | bytes 442376 | tf_op jit(solution)/shard_map/ppermute | solution.py:19
  42.7 28.1 %copy-start.6 = (f32[512]{0:T(512)S(1)}, f32[512]{0:T(512)}, u32[]{:S(2)}) copy-start(f32[512]{0:T(512)} %param.23) | copy-start | bytes 6148
  43.2 5.3 %collective-permute-start.20 = (bf16[32,2304]{1,0:T(8,128)(2,1)S(1)}, bf16[32,2304]{1,0:T(8,128)(2,1)S(1)}, u32[]{:S(2)}, u32[]{:S(2)}) collective-permute-start(bf16[32,2304]{1,0:T(8,128)(2,1)S(1)} %add_convert_fusion.5), channel_id=1, source_target_pairs={{0,1},{1,0},{2,3},{3,2},{4,5},{5,4},{6,7},{7,6},{8,9},{9,8},{10,11... | collective-permute-start | bytes 442376 | tf_op jit(solution)/shard_map/ppermute | solution.py:19
  48.6 9.1 %collective-permute-start.21 = (bf16[2,16,2304]{2,1,0:T(8,128)(2,1)S(1)}, bf16[2,16,2304]{2,1,0:T(8,128)(2,1)S(1)}, u32[]{:S(2)}, u32[]{:S(2)}) collective-permute-start(bf16[2,16,2304]{2,1,0:T(8,128)(2,1)S(1)} %bitcast.105), channel_id=1, source_target_pairs={{0,2},{1,3},{2,0},{3,1},{4,6},{5,7},{6,4},{7,5},{8,10},{9,11},{10,... | collective-permute-start | bytes 442376 | tf_op jit(solution)/shard_map/ppermute | solution.py:19
  57.8 5.2 %collective-permute-start.22 = (bf16[32,2304]{1,0:T(8,128)(2,1)S(1)}, bf16[32,2304]{1,0:T(8,128)(2,1)S(1)}, u32[]{:S(2)}, u32[]{:S(2)}) collective-permute-start(bf16[32,2304]{1,0:T(8,128)(2,1)S(1)} %bitcast.100), channel_id=1, source_target_pairs={{0,1},{1,0},{2,3},{3,2},{4,5},{5,4},{6,7},{7,6},{8,9},{9,8},{10,11... | collective-permute-start | bytes 442376 | tf_op jit(solution)/shard_map/ppermute | solution.py:19
  58.5 9.0 %collective-permute-start.27 = (bf16[32,2304]{1,0:T(8,128)(2,1)S(1)}, bf16[32,2304]{1,0:T(8,128)(2,1)S(1)}, u32[]{:S(2)}, u32[]{:S(2)}) collective-permute-start(bf16[32,2304]{1,0:T(8,128)(2,1)S(1)} %bitcast.101), channel_id=1, source_target_pairs={{0,8},{4,12},{8,0},{12,4},{16,24},{20,28},{24,16},{28,20},{1,9},{5... | collective-permute-start | bytes 442376 | tf_op jit(solution)/shard_map/ppermute | solution.py:19
  60.1 9.9 %collective-permute-start.28 = (bf16[32,2304]{1,0:T(8,128)(2,1)S(1)}, bf16[32,2304]{1,0:T(8,128)(2,1)S(1)}, u32[]{:S(2)}, u32[]{:S(2)}) collective-permute-start(bf16[32,2304]{1,0:T(8,128)(2,1)S(1)} %bitcast.102), channel_id=1, source_target_pairs={{0,16},{4,20},{8,24},{12,28},{16,0},{20,4},{24,8},{28,12},{1,17},{... | collective-permute-start | bytes 442376 | tf_op jit(solution)/shard_map/ppermute | solution.py:19
  63.0 7.7 %collective-permute-start.29 = (bf16[32,2304]{1,0:T(8,128)(2,1)S(1)}, bf16[32,2304]{1,0:T(8,128)(2,1)S(1)}, u32[]{:S(2)}, u32[]{:S(2)}) collective-permute-start(bf16[32,2304]{1,0:T(8,128)(2,1)S(1)} %bitcast.103), channel_id=1, source_target_pairs={{0,24},{4,28},{8,16},{12,20},{16,8},{20,12},{24,0},{28,4},{1,25},{... | collective-permute-start | bytes 442376 | tf_op jit(solution)/shard_map/ppermute | solution.py:19
  64.4 9.6 %collective-permute-start.25 = (bf16[32,2304]{1,0:T(8,128)(2,1)S(1)}, bf16[32,2304]{1,0:T(8,128)(2,1)S(1)}, u32[]{:S(2)}, u32[]{:S(2)}) collective-permute-start(bf16[32,2304]{1,0:T(8,128)(2,1)S(1)} %collective-permute-done.22), channel_id=1, source_target_pairs={{0,24},{4,28},{8,16},{12,20},{16,8},{20,12},{24,0},{28,4},{1,25},{... | collective-permute-start | bytes 442376 | tf_op jit(solution)/shard_map/ppermute | solution.py:19
  65.9 8.1 %collective-permute-start.23 = (bf16[32,2304]{1,0:T(8,128)(2,1)S(1)}, bf16[32,2304]{1,0:T(8,128)(2,1)S(1)}, u32[]{:S(2)}, u32[]{:S(2)}) collective-permute-start(bf16[32,2304]{1,0:T(8,128)(2,1)S(1)} %collective-permute-done.22), channel_id=1, source_target_pairs={{0,8},{4,12},{8,0},{12,4},{16,24},{20,28},{24,16},{28,20},{1,9},{5... | collective-permute-start | bytes 442376 | tf_op jit(solution)/shard_map/ppermute | solution.py:19
  67.5 7.3 %collective-permute-start.24 = (bf16[32,2304]{1,0:T(8,128)(2,1)S(1)}, bf16[32,2304]{1,0:T(8,128)(2,1)S(1)}, u32[]{:S(2)}, u32[]{:S(2)}) collective-permute-start(bf16[32,2304]{1,0:T(8,128)(2,1)S(1)} %collective-permute-done.22), channel_id=1, source_target_pairs={{0,16},{4,20},{8,24},{12,28},{16,0},{20,4},{24,8},{28,12},{1,17},{... | collective-permute-start | bytes 442376 | tf_op jit(solution)/shard_map/ppermute | solution.py:19
  70.7 5.8 %collective-permute-start.30 = (bf16[128,2304]{1,0:T(8,128)(2,1)S(1)}, bf16[128,2304]{1,0:T(8,128)(2,1)S(1)}, u32[]{:S(2)}, u32[]{:S(2)}) collective-permute-start(bf16[128,2304]{1,0:T(8,128)(2,1)S(1)} %bitcast.60), channel_id=1, source_target_pairs={{0,4},{4,0},{8,12},{12,8},{16,20},{20,16},{24,28},{28,24},{1,5},{5... | collective-permute-start | bytes 1769480 | tf_op jit(solution)/shard_map/ppermute | solution.py:19
  73.5 3.5 %collective-permute-start.32 = (bf16[128,2304]{1,0:T(8,128)(2,1)S(1)}, bf16[128,2304]{1,0:T(8,128)(2,1)S(1)}, u32[]{:S(2)}, u32[]{:S(2)}) collective-permute-start(bf16[128,2304]{1,0:T(8,128)(2,1)S(1)} %convolution_convert_fusion), channel_id=1, source_target_pairs={{0,4},{4,0},{8,12},{12,8},{16,20},{20,16},{24,28},{28,24},{1,5},{5... | collective-permute-start | bytes 1769480 | tf_op jit(solution)/shard_map/ppermute | solution.py:19
  74.9 6.2 %collective-permute-start.26 = (bf16[128,2304]{1,0:T(8,128)(2,1)S(1)}, bf16[128,2304]{1,0:T(8,128)(2,1)S(1)}, u32[]{:S(2)}, u32[]{:S(2)}) collective-permute-start(bf16[128,2304]{1,0:T(8,128)(2,1)S(1)} %bitcast.58), channel_id=1, source_target_pairs={{0,4},{4,0},{8,12},{12,8},{16,20},{20,16},{24,28},{28,24},{1,5},{5... | collective-permute-start | bytes 1769480 | tf_op jit(solution)/shard_map/ppermute | solution.py:19
  76.0 8.3 %collective-permute-start.31 = (bf16[128,2304]{1,0:T(8,128)(2,1)S(1)}, bf16[128,2304]{1,0:T(8,128)(2,1)S(1)}, u32[]{:S(2)}, u32[]{:S(2)}) collective-permute-start(bf16[128,2304]{1,0:T(8,128)(2,1)S(1)} %convolution_convert_fusion.1), channel_id=1, source_target_pairs={{0,4},{4,0},{8,12},{12,8},{16,20},{20,16},{24,28},{28,24},{1,5},{5... | collective-permute-start | bytes 1769480 | tf_op jit(solution)/shard_map/ppermute | solution.py:19
  77.5 6.7 %collective-permute-start.33 = (bf16[32,2304]{1,0:T(8,128)(2,1)S(1)}, bf16[32,2304]{1,0:T(8,128)(2,1)S(1)}, u32[]{:S(2)}, u32[]{:S(2)}) collective-permute-start(bf16[32,2304]{1,0:T(8,128)(2,1)S(1)} %get-tuple-element.57), channel_id=1, source_target_pairs={{0,8},{4,12},{8,0},{12,4},{16,24},{20,28},{24,16},{28,20},{1,9},{5... | collective-permute-start | bytes 442376 | tf_op jit(solution)/shard_map/ppermute | solution.py:19
  78.9 9.5 %collective-permute-start.37 = (bf16[32,2304]{1,0:T(8,128)(2,1)S(1)}, bf16[32,2304]{1,0:T(8,128)(2,1)S(1)}, u32[]{:S(2)}, u32[]{:S(2)}) collective-permute-start(bf16[32,2304]{1,0:T(8,128)(2,1)S(1)} %get-tuple-element.59), channel_id=1, source_target_pairs={{0,16},{4,20},{8,24},{12,28},{16,0},{20,4},{24,8},{28,12},{1,17},{... | collective-permute-start | bytes 442376 | tf_op jit(solution)/shard_map/ppermute | solution.py:19
  79.5 9.0 %collective-permute-start.38 = (bf16[32,2304]{1,0:T(8,128)(2,1)S(1)}, bf16[32,2304]{1,0:T(8,128)(2,1)S(1)}, u32[]{:S(2)}, u32[]{:S(2)}) collective-permute-start(bf16[32,2304]{1,0:T(8,128)(2,1)S(1)} %get-tuple-element.58), channel_id=1, source_target_pairs={{0,24},{4,28},{8,16},{12,20},{16,8},{20,12},{24,0},{28,4},{1,25},{... | collective-permute-start | bytes 442376 | tf_op jit(solution)/shard_map/ppermute | solution.py:19
  84.8 15.5 %copy-start.7 = (f32[2304]{0:T(1024)S(1)}, f32[2304]{0:T(1024)}, u32[]{:S(2)}) copy-start(f32[2304]{0:T(1024)} %param.25) | copy-start | bytes 27652
  84.9 6.5 %collective-permute-start.34 = (bf16[32,2304]{1,0:T(8,128)(2,1)S(1)}, bf16[32,2304]{1,0:T(8,128)(2,1)S(1)}, u32[]{:S(2)}, u32[]{:S(2)}) collective-permute-start(bf16[32,2304]{1,0:T(8,128)(2,1)S(1)} %get-tuple-element.54), channel_id=1, source_target_pairs={{0,8},{4,12},{8,0},{12,4},{16,24},{20,28},{24,16},{28,20},{1,9},{5... | collective-permute-start | bytes 442376 | tf_op jit(solution)/shard_map/ppermute | solution.py:19
  86.3 7.6 %collective-permute-start.35 = (bf16[32,2304]{1,0:T(8,128)(2,1)S(1)}, bf16[32,2304]{1,0:T(8,128)(2,1)S(1)}, u32[]{:S(2)}, u32[]{:S(2)}) collective-permute-start(bf16[32,2304]{1,0:T(8,128)(2,1)S(1)} %get-tuple-element.56), channel_id=1, source_target_pairs={{0,16},{4,20},{8,24},{12,28},{16,0},{20,4},{24,8},{28,12},{1,17},{... | collective-permute-start | bytes 442376 | tf_op jit(solution)/shard_map/ppermute | solution.py:19
  86.8 7.2 %collective-permute-start.36 = (bf16[32,2304]{1,0:T(8,128)(2,1)S(1)}, bf16[32,2304]{1,0:T(8,128)(2,1)S(1)}, u32[]{:S(2)}, u32[]{:S(2)}) collective-permute-start(bf16[32,2304]{1,0:T(8,128)(2,1)S(1)} %get-tuple-element.55), channel_id=1, source_target_pairs={{0,24},{4,28},{8,16},{12,20},{16,8},{20,12},{24,0},{28,4},{1,25},{... | collective-permute-start | bytes 442376 | tf_op jit(solution)/shard_map/ppermute | solution.py:19
  88.5 5.4 %collective-permute-start.39 = (bf16[32,2304]{1,0:T(8,128)(2,1)S(1)}, bf16[32,2304]{1,0:T(8,128)(2,1)S(1)}, u32[]{:S(2)}, u32[]{:S(2)}) collective-permute-start(bf16[32,2304]{1,0:T(8,128)(2,1)S(1)} %add_convert_fusion.2), channel_id=1, source_target_pairs={{0,1},{1,0},{2,3},{3,2},{4,5},{5,4},{6,7},{7,6},{8,9},{9,8},{10,11... | collective-permute-start | bytes 442376 | tf_op jit(solution)/shard_map/ppermute | solution.py:19
  94.0 6.2 %collective-permute-start.40 = (bf16[16,2304]{1,0:T(8,128)(2,1)S(1)}, bf16[16,2304]{1,0:T(8,128)(2,1)S(1)}, u32[]{:S(2)}, u32[]{:S(2)}) collective-permute-start(bf16[16,2304]{1,0:T(8,128)(2,1)S(1)} %fusion.9), channel_id=1, source_target_pairs={{0,2},{1,3},{2,0},{3,1},{4,6},{5,7},{6,4},{7,5},{8,10},{9,11},{10,... | collective-permute-start | bytes 221192 | tf_op jit(solution)/shard_map/ppermute | solution.py:19
  (4 other events, 8.7 us)

commit v17 on v15

--- a/solution.py
+++ b/solution.py
@@ -316,7 +316,7 @@
         total = half(dot(features_far, decoder) + full(decoded) + zero)
         total = total.reshape(pairs, feats // 2 * own, width)
         blocks[chunk] = [total[0]] + [swap(total[p], "expert", 2 * p) for p in range(1, pairs)]
-        zero = 0.0 * full(blocks[chunk][1][:1])
+        zero = 0.0 * full(swap(total[1, :own, :LANES], "expert", 1)[:1, :1])
         both = jnp.stack([features_far, features_near])
         features[chunk] = both.reshape(2, pairs, feats // 2, 1, own, -1)
     arrived = swap(half(sum(full(block) for block in blocks[1])), "feat", feat_bits[0])

time: 101 us -> 102 us (level)
  waiting for transfers between devices: 29.1 us -> 27.8 us
    ppermute x41 -> x42, waiting for transfers between devices: 29.1 us -> 27.8 us  [swap(): lax.ppermute(value, axis, [(i, i ^ r) for i in range(lax.axis_size(axis))])]
    ppermute x41 -> x42, starting transfers between devices: 46.1 us -> 46.8 us  [swap(): lax.ppermute(value, axis, [(i, i ^ r) for i in range(lax.axis_size(axis))])]
  transfers between devices with their start and end apart: 41 -> 42, of which waited for: 15 -> 15; matrix products, arithmetic and copies ran while one was open for 6% -> 7% of each run, Pallas kernels for 12% -> 12%
where the time goes in v17:
time: 102 us
  starting transfers between devices  46.8 us (46%)
  waiting for transfers between devices  27.8 us (27%)
  Pallas kernels  15.5 us (15%)
  matrix products  5.52 us (5%)
  other arithmetic  2.22 us (2%)
  local copies, waits for them, and re-layouts  1.94 us (2%)
  between operations  1.94 us (2%)
    ppermute x42, starting transfers between devices, swap(): lax.ppermute(value, axis, [(i, i ^ r) for i in range(lax.axis_size(axis))])  46.8 us
    ppermute x42, waiting for transfers between devices, swap(): lax.ppermute(value, axis, [(i, i ^ r) for i in range(lax.axis_size(axis))])  27.8 us
    pallas_call x8, Pallas kernels, call(): pl.pallas_call(body, in_specs=specs, out_specs=[VMEM_SPEC] * len(outs), o...  15.5 us
    dot_general x8, matrix products, dot(): return jnp.dot(a, b, preferred_element_type=jnp.float32)  5.52 us
  transfers between devices with their start and end apart: 42, of which 15 were waited for; matrix products, arithmetic and copies ran while one was open for 7% of the time, Pallas kernels for 12%

profile of v17, /device:TPU:0, one launch (start us, length us, event | category | flops | bytes accessed | tf_op | source)
XLA Modules:
  0.0 101.7 jit_solution(12557389225391485437)
XLA Ops:
  0.6 0.9 pad_add_fusion.both
  1.7 2.9 %collective-permute-start = (bf16[16,128]{1,0:T(8,128)(2,1)S(1)}, bf16[16,128]{1,0:T(8,128)(2,1)S(1)}, u32[]{:S(2)}, u32[]{:S(2)}) collective-permute-start(bf16[16,128]{1,0:T(8,128)(2,1)S(1)} %shard_map.140), channel_id=1, source_target_pairs={{0,8},{4,12},{8,0},{12,4},{16,24},{20,28},{24,16},{28,20},{1,9},{5... | collective-permute-start | bytes 12296 | tf_op jit(solution)/shard_map/ppermute | solution.py:19
  4.6 1.5 %collective-permute-start.1 = (bf16[16,128]{1,0:T(8,128)(2,1)S(1)}, bf16[16,128]{1,0:T(8,128)(2,1)S(1)}, u32[]{:S(2)}, u32[]{:S(2)}) collective-permute-start(bf16[16,128]{1,0:T(8,128)(2,1)S(1)} %shard_map.140), channel_id=1, source_target_pairs={{0,16},{4,20},{8,24},{12,28},{16,0},{20,4},{24,8},{28,12},{1,17},{... | collective-permute-start | bytes 12296 | tf_op jit(solution)/shard_map/ppermute | solution.py:19
  6.2 2.0 %collective-permute-start.3 = (bf16[64,2304]{1,0:T(8,128)(2,1)}, bf16[64,2304]{1,0:T(8,128)(2,1)S(1)}, u32[]{:S(2)}, u32[]{:S(2)}) collective-permute-start(bf16[64,2304]{1,0:T(8,128)(2,1)} %refs_0_), channel_id=1, source_target_pairs={{0,8},{4,12},{8,0},{12,4},{16,24},{20,28},{24,16},{28,20},{1,9},{5... | collective-permute-start | bytes 884744 | tf_op jit(solution)/shard_map/ppermute | solution.py:19
  8.2 1.5 %collective-permute-start.4 = (bf16[64,2304]{1,0:T(8,128)(2,1)}, bf16[64,2304]{1,0:T(8,128)(2,1)S(1)}, u32[]{:S(2)}, u32[]{:S(2)}) collective-permute-start(bf16[64,2304]{1,0:T(8,128)(2,1)} %refs_0_), channel_id=1, source_target_pairs={{0,16},{4,20},{8,24},{12,28},{16,0},{20,4},{24,8},{28,12},{1,17},{... | collective-permute-start | bytes 884744 | tf_op jit(solution)/shard_map/ppermute | solution.py:19
  9.8 0.9 collective-permute-done.2
  10.7 1.6 %collective-permute-start.10 = (bf16[64,128]{1,0:T(8,128)(2,1)S(1)}, bf16[64,128]{1,0:T(8,128)(2,1)S(1)}, u32[]{:S(2)}, u32[]{:S(2)}) collective-permute-start(bf16[64,128]{1,0:T(8,128)(2,1)S(1)} %pad_maximum_fusion.3), channel_id=1, source_target_pairs={{0,1},{1,0},{2,3},{3,2},{4,5},{5,4},{6,7},{7,6},{8,9},{9,8},{10,11... | collective-permute-start | bytes 49160 | tf_op jit(solution)/shard_map/ppermute | solution.py:19
  12.3 1.0 copy-done.4
  13.3 3.9 %shard_map.141 = (bf16[64,2304]{1,0:T(8,128)(2,1)S(1)}, bf16[1,2304,1024]{2,1,0:T(8,128)(2,1)S(1)}, bf16[1,2304,1024]{2,1,0:T(8,128)(2,1)S(1)}) custom-call(bf16[64,2304]{1,0:T(8,128)(2,1)S(1)} %copy-done.4, bf16[1,2304,1024]{2,1,0:T(8,128)(2,1)} %refs_1_.1, bf16[1,2304,1024]{2,1,0:T(8,128)(2,1)} %refs_2_.1), custom_call_target="tpu_custom_call" | custom-call | flops 2676326400 | bytes 19464192 | tf_op jit(solution)/shard_map/pallas_call | solution.py:49
  17.2 2.7 %collective-permute-start.11 = (bf16[128,128]{1,0:T(8,128)(2,1)S(1)}, bf16[128,128]{1,0:T(8,128)(2,1)S(1)}, u32[]{:S(2)}, u32[]{:S(2)}) collective-permute-start(bf16[128,128]{1,0:T(8,128)(2,1)S(1)} %pad_maximum_fusion.2), channel_id=1, source_target_pairs={{0,2},{1,3},{2,0},{3,1},{4,6},{5,7},{6,4},{7,5},{8,10},{9,11},{10,... | collective-permute-start | bytes 98312 | tf_op jit(solution)/shard_map/ppermute | solution.py:19
  19.9 2.5 %collective-permute-done.4.refs_2_ = bf16[64,2304]{1,0:T(8,128)(2,1)S(1)} collective-permute-done((bf16[64,2304]{1,0:T(8,128)(2,1)}, bf16[64,2304]{1,0:T(8,128)(2,1)S(1)}, u32[]{:S(2)}, u32[]{:S(2)}) %collective-permute-start.4) | collective-permute-done | bytes 294944 | tf_op jit(solution)/shard_map/ppermute | solution.py:19
  22.9 2.7 %shard_map.142.hidden = bf16[256,1024]{1,0:T(8,128)(2,1)S(1)} custom-call(bf16[64,2304]{1,0:T(8,128)(2,1)S(1)} %get-tuple-element.30.refs_0_, bf16[64,2304]{1,0:T(8,128)(2,1)S(1)} %collective-permute-done.3.refs_1_, bf16[64,2304]{1,0:T(8,128)(2,1)S(1)} %collective-permute-done.4.refs_2_, bf16[64,2304]{1,0:T(8,128)(2,1)S(1)} %collective-permute-done.5.refs_3_, ...), custom_call_target="tpu_custom_call" | custom-call | flops 2415919104 | bytes 9437184 | tf_op jit(solution)/shard_map/pallas_call | solution.py:49
  25.7 2.0 %shard_map.144 = bf16[256,2304]{1,0:T(8,128)(2,1)S(1)} custom-call(s32[3]{0:T(128)S(1)} %pad_add_fusion.1.scalars, bf16[256,1024]{1,0:T(8,128)(2,1)S(1)} %shard_map.142.hidden, bf16[1,1024,2304]{2,1,0:T(8,128)(2,1)S(1)} %bitcast.61, bf16[256,128]{1,0:T(8,128)(2,1)S(1)} %constant_dynamic-update-slice_fusion.table), custom_call_target="tpu_custom_call" | custom-call | flops 1207959552 | bytes 4718592 | tf_op jit(solution)/shard_map/pallas_call | solution.py:49
  28.2 2.7 %shard_map.143.hidden = bf16[256,1024]{1,0:T(8,128)(2,1)S(1)} custom-call(bf16[64,2304]{1,0:T(8,128)(2,1)S(1)} %collective-permute-done.6.refs_0_.x, bf16[64,2304]{1,0:T(8,128)(2,1)S(1)} %collective-permute-done.7.refs_1_, bf16[64,2304]{1,0:T(8,128)(2,1)S(1)} %collective-permute-done.8.refs_2_, bf16[64,2304]{1,0:T(8,128)(2,1)S(1)} %collective-permute-done.9.refs_3_, ...), custom_call_target="tpu_custom_call" | custom-call | flops 2415919104 | bytes 9437184 | tf_op jit(solution)/shard_map/pallas_call | solution.py:49
  30.9 1.3 %shard_map.146 = (bf16[32,2304]{1,0:T(8,128)(2,1)S(1)}, bf16[32,2304]{1,0:T(8,128)(2,1)S(1)}, bf16[32,2304]{1,0:T(8,128)(2,1)S(1)}, bf16[32,2304]{1,0:T(8,128)(2,1)S(1)}) custom-call(s32[3]{0:T(128)S(1)} %pad_add_fusion.1.scalars, bf16[256,1024]{1,0:T(8,128)(2,1)S(1)} %shard_map.143.hidden, bf16[1,1024,2304]{2,1,0:T(8,128)(2,1)S(1)} %bitcast.61, ...), custom_call_target="tpu_custom_call" | custom-call | flops 1207959552 | bytes 4718592 | tf_op jit(solution)/shard_map/pallas_call | solution.py:49
  32.3 1.5 %collective-permute-start.17 = (bf16[32,2304]{1,0:T(8,128)(2,1)S(1)}, bf16[32,2304]{1,0:T(8,128)(2,1)S(1)}, u32[]{:S(2)}, u32[]{:S(2)}) collective-permute-start(bf16[32,2304]{1,0:T(8,128)(2,1)S(1)} %get-tuple-element.44), channel_id=1, source_target_pairs={{0,24},{4,28},{8,16},{12,20},{16,8},{20,12},{24,0},{28,4},{1,25},{... | collective-permute-start | bytes 442376 | tf_op jit(solution)/shard_map/ppermute | solution.py:19
  33.8 1.5 %collective-permute-start.18 = (bf16[32,2304]{1,0:T(8,128)(2,1)S(1)}, bf16[32,2304]{1,0:T(8,128)(2,1)S(1)}, u32[]{:S(2)}, u32[]{:S(2)}) collective-permute-start(bf16[32,2304]{1,0:T(8,128)(2,1)S(1)} %get-tuple-element.48), channel_id=1, source_target_pairs={{0,8},{4,12},{8,0},{12,4},{16,24},{20,28},{24,16},{28,20},{1,9},{5... | collective-permute-start | bytes 442376 | tf_op jit(solution)/shard_map/ppermute | solution.py:19
  35.9 1.4 %shard_map.145 = (bf16[32,2304]{1,0:T(8,128)(2,1)S(1)}, bf16[32,2304]{1,0:T(8,128)(2,1)S(1)}, bf16[32,2304]{1,0:T(8,128)(2,1)S(1)}, bf16[32,2304]{1,0:T(8,128)(2,1)S(1)}) custom-call(s32[3]{0:T(128)S(1)} %pad_add_fusion.1.scalars, bf16[256,1024]{1,0:T(8,128)(2,1)S(1)} %shard_map.143.hidden, bf16[1,1024,2304]{2,1,0:T(8,128)(2,1)S(1)} %bitcast.61, ...), custom_call_target="tpu_custom_call" | custom-call | flops 1207959552 | bytes 4718592 | tf_op jit(solution)/shard_map/pallas_call | solution.py:49
  37.2 0.9 collective-permute-start.14
  38.1 1.2 %collective-permute-start.15 = (bf16[32,2304]{1,0:T(8,128)(2,1)S(1)}, bf16[32,2304]{1,0:T(8,128)(2,1)S(1)}, u32[]{:S(2)}, u32[]{:S(2)}) collective-permute-start(bf16[32,2304]{1,0:T(8,128)(2,1)S(1)} %get-tuple-element.42), channel_id=1, source_target_pairs={{0,16},{4,20},{8,24},{12,28},{16,0},{20,4},{24,8},{28,12},{1,17},{... | collective-permute-start | bytes 442376 | tf_op jit(solution)/shard_map/ppermute | solution.py:19
  39.3 0.7 collective-permute-done.17
  40.0 1.4 %collective-permute-start.16 = (bf16[32,2304]{1,0:T(8,128)(2,1)S(1)}, bf16[32,2304]{1,0:T(8,128)(2,1)S(1)}, u32[]{:S(2)}, u32[]{:S(2)}) collective-permute-start(bf16[32,2304]{1,0:T(8,128)(2,1)S(1)} %get-tuple-element.43), channel_id=1, source_target_pairs={{0,24},{4,28},{8,16},{12,20},{16,8},{20,12},{24,0},{28,4},{1,25},{... | collective-permute-start | bytes 442376 | tf_op jit(solution)/shard_map/ppermute | solution.py:19
  41.4 1.4 %shard_map.147 = (f32[32,2304]{1,0:T(8,128)S(1)}, f32[32,2304]{1,0:T(8,128)S(1)}) custom-call(s32[3]{0:T(128)S(1)} %pad_add_fusion.1.scalars, bf16[64,2304]{1,0:T(8,128)(2,1)S(1)} %collective-permute-done.6.refs_0_.x, bf16[2304,256]{1,0:T(8,128)(2,1)S(1)} %copy-done.1, bf16[2304,256]{1,0:T(8,128)(2,1)S(1)} %copy-done.2, bf16[256,2304]{1,0:T(8,128)(2,1)S(1)} %copy-done.3), custom_call_target="tpu_custom_call" | custom-call | flops 226492416 | bytes 3538944 | tf_op jit(solution)/shard_map/pallas_call | solution.py:49
  43.3 1.6 %collective-permute-start.20 = (bf16[32,2304]{1,0:T(8,128)(2,1)S(1)}, bf16[32,2304]{1,0:T(8,128)(2,1)S(1)}, u32[]{:S(2)}, u32[]{:S(2)}) collective-permute-start(bf16[32,2304]{1,0:T(8,128)(2,1)S(1)} %add_convert_fusion.5), channel_id=1, source_target_pairs={{0,1},{1,0},{2,3},{3,2},{4,5},{5,4},{6,7},{7,6},{8,9},{9,8},{10,11... | collective-permute-start | bytes 442376 | tf_op jit(solution)/shard_map/ppermute | solution.py:19
  44.9 1.4 %collective-permute-done.14 = bf16[32,2304]{1,0:T(8,128)(2,1)S(1)} collective-permute-done((bf16[32,2304]{1,0:T(8,128)(2,1)S(1)}, bf16[32,2304]{1,0:T(8,128)(2,1)S(1)}, u32[]{:S(2)}, u32[]{:S(2)}) %collective-permute-start.14) | collective-permute-done | bytes 147488 | tf_op jit(solution)/shard_map/ppermute | solution.py:19
  46.3 2.2 %collective-permute-done.16 = bf16[32,2304]{1,0:T(8,128)(2,1)S(1)} collective-permute-done((bf16[32,2304]{1,0:T(8,128)(2,1)S(1)}, bf16[32,2304]{1,0:T(8,128)(2,1)S(1)}, u32[]{:S(2)}, u32[]{:S(2)}) %collective-permute-start.16) | collective-permute-done | bytes 147488 | tf_op jit(solution)/shard_map/ppermute | solution.py:19
  48.7 2.7 %collective-permute-start.21 = (bf16[2,16,2304]{2,1,0:T(8,128)(2,1)S(1)}, bf16[2,16,2304]{2,1,0:T(8,128)(2,1)S(1)}, u32[]{:S(2)}, u32[]{:S(2)}) collective-permute-start(bf16[2,16,2304]{2,1,0:T(8,128)(2,1)S(1)} %bitcast.110), channel_id=1, source_target_pairs={{0,2},{1,3},{2,0},{3,1},{4,6},{5,7},{6,4},{7,5},{8,10},{9,11},{10,... | collective-permute-start | bytes 442376 | tf_op jit(solution)/shard_map/ppermute | solution.py:19
  51.4 6.4 %collective-permute-done.21 = bf16[2,16,2304]{2,1,0:T(8,128)(2,1)S(1)} collective-permute-done((bf16[2,16,2304]{2,1,0:T(8,128)(2,1)S(1)}, bf16[2,16,2304]{2,1,0:T(8,128)(2,1)S(1)}, u32[]{:S(2)}, u32[]{:S(2)}) %collective-permute-start.21) | collective-permute-done | bytes 147488 | tf_op jit(solution)/shard_map/ppermute | solution.py:19
  57.8 0.8 collective-permute-start.22
  58.6 1.6 %collective-permute-start.27 = (bf16[32,2304]{1,0:T(8,128)(2,1)S(1)}, bf16[32,2304]{1,0:T(8,128)(2,1)S(1)}, u32[]{:S(2)}, u32[]{:S(2)}) collective-permute-start(bf16[32,2304]{1,0:T(8,128)(2,1)S(1)} %bitcast.106), channel_id=1, source_target_pairs={{0,8},{4,12},{8,0},{12,4},{16,24},{20,28},{24,16},{28,20},{1,9},{5... | collective-permute-start | bytes 442376 | tf_op jit(solution)/shard_map/ppermute | solution.py:19
  60.6 2.5 %collective-permute-done.22 = bf16[32,2304]{1,0:T(8,128)(2,1)S(1)} collective-permute-done((bf16[32,2304]{1,0:T(8,128)(2,1)S(1)}, bf16[32,2304]{1,0:T(8,128)(2,1)S(1)}, u32[]{:S(2)}, u32[]{:S(2)}) %collective-permute-start.22) | collective-permute-done | bytes 147488 | tf_op jit(solution)/shard_map/ppermute | solution.py:19
  63.0 1.4 %collective-permute-start.29 = (bf16[32,2304]{1,0:T(8,128)(2,1)S(1)}, bf16[32,2304]{1,0:T(8,128)(2,1)S(1)}, u32[]{:S(2)}, u32[]{:S(2)}) collective-permute-start(bf16[32,2304]{1,0:T(8,128)(2,1)S(1)} %bitcast.108), channel_id=1, source_target_pairs={{0,24},{4,28},{8,16},{12,20},{16,8},{20,12},{24,0},{28,4},{1,25},{... | collective-permute-start | bytes 442376 | tf_op jit(solution)/shard_map/ppermute | solution.py:19
  64.5 1.5 %collective-permute-start.25 = (bf16[32,2304]{1,0:T(8,128)(2,1)S(1)}, bf16[32,2304]{1,0:T(8,128)(2,1)S(1)}, u32[]{:S(2)}, u32[]{:S(2)}) collective-permute-start(bf16[32,2304]{1,0:T(8,128)(2,1)S(1)} %collective-permute-done.22), channel_id=1, source_target_pairs={{0,24},{4,28},{8,16},{12,20},{16,8},{20,12},{24,0},{28,4},{1,25},{... | collective-permute-start | bytes 442376 | tf_op jit(solution)/shard_map/ppermute | solution.py:19
  66.0 1.6 %collective-permute-start.23 = (bf16[32,2304]{1,0:T(8,128)(2,1)S(1)}, bf16[32,2304]{1,0:T(8,128)(2,1)S(1)}, u32[]{:S(2)}, u32[]{:S(2)}) collective-permute-start(bf16[32,2304]{1,0:T(8,128)(2,1)S(1)} %collective-permute-done.22), channel_id=1, source_target_pairs={{0,8},{4,12},{8,0},{12,4},{16,24},{20,28},{24,16},{28,20},{1,9},{5... | collective-permute-start | bytes 442376 | tf_op jit(solution)/shard_map/ppermute | solution.py:19
  68.0 2.1 %collective-permute-done.28 = bf16[32,2304]{1,0:T(8,128)(2,1)S(1)} collective-permute-done((bf16[32,2304]{1,0:T(8,128)(2,1)S(1)}, bf16[32,2304]{1,0:T(8,128)(2,1)S(1)}, u32[]{:S(2)}, u32[]{:S(2)}) %collective-permute-start.28) | collective-permute-done | bytes 147488 | tf_op jit(solution)/shard_map/ppermute | solution.py:19
  70.1 0.6 collective-permute-done.29
  70.9 2.1 %fusion.4 = bf16[128,512]{1,0:T(8,128)(2,1)S(1)} fusion(bf16[128,2304]{1,0:T(8,128)(2,1)S(1)} %bitcast.66, bf16[2304,512]{1,0:T(8,128)(2,1)} %param.22, f32[512]{0:T(512)S(1)} %copy-done.6), kind=kOutput, calls=%fused_computation.12 | convolution fusion | flops 302186496 | bytes 3082240 | tf_op jit(solution)/shard_map/dot_general | solution.py:23
  74.1 0.8 collective-permute-done.24
  77.7 1.4 %collective-permute-start.37 = (bf16[32,2304]{1,0:T(8,128)(2,1)S(1)}, bf16[32,2304]{1,0:T(8,128)(2,1)S(1)}, u32[]{:S(2)}, u32[]{:S(2)}) collective-permute-start(bf16[32,2304]{1,0:T(8,128)(2,1)S(1)} %get-tuple-element.57), channel_id=1, source_target_pairs={{0,8},{4,12},{8,0},{12,4},{16,24},{20,28},{24,16},{28,20},{1,9},{5... | collective-permute-start | bytes 442376 | tf_op jit(solution)/shard_map/ppermute | solution.py:19
  79.6 1.6 %collective-permute-start.39 = (bf16[32,2304]{1,0:T(8,128)(2,1)S(1)}, bf16[32,2304]{1,0:T(8,128)(2,1)S(1)}, u32[]{:S(2)}, u32[]{:S(2)}) collective-permute-start(bf16[32,2304]{1,0:T(8,128)(2,1)S(1)} %get-tuple-element.58), channel_id=1, source_target_pairs={{0,24},{4,28},{8,16},{12,20},{16,8},{20,12},{24,0},{28,4},{1,25},{... | collective-permute-start | bytes 442376 | tf_op jit(solution)/shard_map/ppermute | solution.py:19
  84.1 1.4 %collective-permute-start.34 = (bf16[32,2304]{1,0:T(8,128)(2,1)S(1)}, bf16[32,2304]{1,0:T(8,128)(2,1)S(1)}, u32[]{:S(2)}, u32[]{:S(2)}) collective-permute-start(bf16[32,2304]{1,0:T(8,128)(2,1)S(1)} %get-tuple-element.54), channel_id=1, source_target_pairs={{0,8},{4,12},{8,0},{12,4},{16,24},{20,28},{24,16},{28,20},{1,9},{5... | collective-permute-start | bytes 442376 | tf_op jit(solution)/shard_map/ppermute | solution.py:19
  86.0 1.6 %collective-permute-start.36 = (bf16[32,2304]{1,0:T(8,128)(2,1)S(1)}, bf16[32,2304]{1,0:T(8,128)(2,1)S(1)}, u32[]{:S(2)}, u32[]{:S(2)}) collective-permute-start(bf16[32,2304]{1,0:T(8,128)(2,1)S(1)} %get-tuple-element.55), channel_id=1, source_target_pairs={{0,24},{4,28},{8,16},{12,20},{16,8},{20,12},{24,0},{28,4},{1,25},{... | collective-permute-start | bytes 442376 | tf_op jit(solution)/shard_map/ppermute | solution.py:19
  87.6 0.8 collective-permute-done.38
  88.6 2.0 %collective-permute-start.40 = (bf16[32,2304]{1,0:T(8,128)(2,1)S(1)}, bf16[32,2304]{1,0:T(8,128)(2,1)S(1)}, u32[]{:S(2)}, u32[]{:S(2)}) collective-permute-start(bf16[32,2304]{1,0:T(8,128)(2,1)S(1)} %add_convert_fusion.2), channel_id=1, source_target_pairs={{0,1},{1,0},{2,3},{3,2},{4,5},{5,4},{6,7},{7,6},{8,9},{9,8},{10,11... | collective-permute-start | bytes 442376 | tf_op jit(solution)/shard_map/ppermute | solution.py:19
  90.9 3.6 %collective-permute-done.35 = bf16[32,2304]{1,0:T(8,128)(2,1)S(1)} collective-permute-done((bf16[32,2304]{1,0:T(8,128)(2,1)S(1)}, bf16[32,2304]{1,0:T(8,128)(2,1)S(1)}, u32[]{:S(2)}, u32[]{:S(2)}) %collective-permute-start.35) | collective-permute-done | bytes 147488 | tf_op jit(solution)/shard_map/ppermute | solution.py:19
  94.7 3.9 %collective-permute-start.41 = (bf16[16,2304]{1,0:T(8,128)(2,1)S(1)}, bf16[16,2304]{1,0:T(8,128)(2,1)S(1)}, u32[]{:S(2)}, u32[]{:S(2)}) collective-permute-start(bf16[16,2304]{1,0:T(8,128)(2,1)S(1)} %fusion.9), channel_id=1, source_target_pairs={{0,2},{1,3},{2,0},{3,1},{4,6},{5,7},{6,4},{7,5},{8,10},{9,11},{10,... | collective-permute-start | bytes 221192 | tf_op jit(solution)/shard_map/ppermute | solution.py:19
  98.6 2.4 %collective-permute-done.41 = bf16[16,2304]{1,0:T(8,128)(2,1)S(1)} collective-permute-done((bf16[16,2304]{1,0:T(8,128)(2,1)S(1)}, bf16[16,2304]{1,0:T(8,128)(2,1)S(1)}, u32[]{:S(2)}, u32[]{:S(2)}) %collective-permute-start.41) | collective-permute-done | bytes 73760 | tf_op jit(solution)/shard_map/ppermute | solution.py:19
  101.0 0.7 fusion.8
  (128 shorter events, 10.8 us)
Async XLA Ops:
  0.6 72.4 %copy-start = (bf16[512,2304]{1,0:T(8,128)(2,1)S(1)}, bf16[512,2304]{1,0:T(8,128)(2,1)}, u32[]{:S(2)}) copy-start(bf16[512,2304]{1,0:T(8,128)(2,1)} %param.24) | copy-start | bytes 7077892
  1.7 4.5 %collective-permute-start = (bf16[16,128]{1,0:T(8,128)(2,1)S(1)}, bf16[16,128]{1,0:T(8,128)(2,1)S(1)}, u32[]{:S(2)}, u32[]{:S(2)}) collective-permute-start(bf16[16,128]{1,0:T(8,128)(2,1)S(1)} %shard_map.140), channel_id=1, source_target_pairs={{0,8},{4,12},{8,0},{12,4},{16,24},{20,28},{24,16},{28,20},{1,9},{5... | collective-permute-start | bytes 12296 | tf_op jit(solution)/shard_map/ppermute | solution.py:19
  4.6 5.1 %collective-permute-start.1 = (bf16[16,128]{1,0:T(8,128)(2,1)S(1)}, bf16[16,128]{1,0:T(8,128)(2,1)S(1)}, u32[]{:S(2)}, u32[]{:S(2)}) collective-permute-start(bf16[16,128]{1,0:T(8,128)(2,1)S(1)} %shard_map.140), channel_id=1, source_target_pairs={{0,16},{4,20},{8,24},{12,28},{16,0},{20,4},{24,8},{28,12},{1,17},{... | collective-permute-start | bytes 12296 | tf_op jit(solution)/shard_map/ppermute | solution.py:19
  6.1 4.6 %collective-permute-start.2 = (bf16[16,128]{1,0:T(8,128)(2,1)S(1)}, bf16[16,128]{1,0:T(8,128)(2,1)S(1)}, u32[]{:S(2)}, u32[]{:S(2)}) collective-permute-start(bf16[16,128]{1,0:T(8,128)(2,1)S(1)} %shard_map.140), channel_id=1, source_target_pairs={{0,24},{4,28},{8,16},{12,20},{16,8},{20,12},{24,0},{28,4},{1,25},{... | collective-permute-start | bytes 12296 | tf_op jit(solution)/shard_map/ppermute | solution.py:19
  6.2 13.6 %collective-permute-start.3 = (bf16[64,2304]{1,0:T(8,128)(2,1)}, bf16[64,2304]{1,0:T(8,128)(2,1)S(1)}, u32[]{:S(2)}, u32[]{:S(2)}) collective-permute-start(bf16[64,2304]{1,0:T(8,128)(2,1)} %refs_0_), channel_id=1, source_target_pairs={{0,8},{4,12},{8,0},{12,4},{16,24},{20,28},{24,16},{28,20},{1,9},{5... | collective-permute-start | bytes 884744 | tf_op jit(solution)/shard_map/ppermute | solution.py:19
  8.2 14.2 %collective-permute-start.4 = (bf16[64,2304]{1,0:T(8,128)(2,1)}, bf16[64,2304]{1,0:T(8,128)(2,1)S(1)}, u32[]{:S(2)}, u32[]{:S(2)}) collective-permute-start(bf16[64,2304]{1,0:T(8,128)(2,1)} %refs_0_), channel_id=1, source_target_pairs={{0,16},{4,20},{8,24},{12,28},{16,0},{20,4},{24,8},{28,12},{1,17},{... | collective-permute-start | bytes 884744 | tf_op jit(solution)/shard_map/ppermute | solution.py:19
  9.8 12.7 %collective-permute-start.5 = (bf16[64,2304]{1,0:T(8,128)(2,1)}, bf16[64,2304]{1,0:T(8,128)(2,1)S(1)}, u32[]{:S(2)}, u32[]{:S(2)}) collective-permute-start(bf16[64,2304]{1,0:T(8,128)(2,1)} %refs_0_), channel_id=1, source_target_pairs={{0,24},{4,28},{8,16},{12,20},{16,8},{20,12},{24,0},{28,4},{1,25},{... | collective-permute-start | bytes 884744 | tf_op jit(solution)/shard_map/ppermute | solution.py:19
  9.8 15.9 %collective-permute-start.6 = (bf16[64,2304]{1,0:T(8,128)(2,1)}, bf16[64,2304]{1,0:T(8,128)(2,1)S(1)}, u32[]{:S(2)}, u32[]{:S(2)}) collective-permute-start(bf16[64,2304]{1,0:T(8,128)(2,1)} %refs_0_), channel_id=1, source_target_pairs={{0,4},{4,0},{8,12},{12,8},{16,20},{20,16},{24,28},{28,24},{1,5},{5... | collective-permute-start | bytes 884744 | tf_op jit(solution)/shard_map/ppermute | solution.py:19
  10.7 6.5 %collective-permute-start.10 = (bf16[64,128]{1,0:T(8,128)(2,1)S(1)}, bf16[64,128]{1,0:T(8,128)(2,1)S(1)}, u32[]{:S(2)}, u32[]{:S(2)}) collective-permute-start(bf16[64,128]{1,0:T(8,128)(2,1)S(1)} %pad_maximum_fusion.3), channel_id=1, source_target_pairs={{0,1},{1,0},{2,3},{3,2},{4,5},{5,4},{6,7},{7,6},{8,9},{9,8},{10,11... | collective-permute-start | bytes 49160 | tf_op jit(solution)/shard_map/ppermute | solution.py:19
  13.3 12.4 %slice-start = ((s8[4718592]{0:T(1024)(128)(4,1)}), s8[524288]{0:T(1024)(128)(4,1)S(1)}, s32[]{:S(2)}) async-start(s8[4718592]{0:T(1024)(128)(4,1)} %bitcast.60), calls=%async_computation | async-start | bytes 1048576
  17.2 5.7 %collective-permute-start.11 = (bf16[128,128]{1,0:T(8,128)(2,1)S(1)}, bf16[128,128]{1,0:T(8,128)(2,1)S(1)}, u32[]{:S(2)}, u32[]{:S(2)}) collective-permute-start(bf16[128,128]{1,0:T(8,128)(2,1)S(1)} %pad_maximum_fusion.2), channel_id=1, source_target_pairs={{0,2},{1,3},{2,0},{3,1},{4,6},{5,7},{6,4},{7,5},{8,10},{9,11},{10,... | collective-permute-start | bytes 98312 | tf_op jit(solution)/shard_map/ppermute | solution.py:19
  19.9 5.8 %collective-permute-start.7 = (bf16[64,2304]{1,0:T(8,128)(2,1)S(1)}, bf16[64,2304]{1,0:T(8,128)(2,1)S(1)}, u32[]{:S(2)}, u32[]{:S(2)}) collective-permute-start(bf16[64,2304]{1,0:T(8,128)(2,1)S(1)} %collective-permute-done.3.refs_1_), channel_id=1, source_target_pairs={{0,4},{4,0},{8,12},{12,8},{16,20},{20,16},{24,28},{28,24},{1,5},{5... | collective-permute-start | bytes 884744 | tf_op jit(solution)/shard_map/ppermute | solution.py:19
  22.4 3.2 %collective-permute-start.8 = (bf16[64,2304]{1,0:T(8,128)(2,1)S(1)}, bf16[64,2304]{1,0:T(8,128)(2,1)S(1)}, u32[]{:S(2)}, u32[]{:S(2)}) collective-permute-start(bf16[64,2304]{1,0:T(8,128)(2,1)S(1)} %collective-permute-done.4.refs_2_), channel_id=1, source_target_pairs={{0,4},{4,0},{8,12},{12,8},{16,20},{20,16},{24,28},{28,24},{1,5},{5... | collective-permute-start | bytes 884744 | tf_op jit(solution)/shard_map/ppermute | solution.py:19
  22.4 3.2 %collective-permute-start.9 = (bf16[64,2304]{1,0:T(8,128)(2,1)S(1)}, bf16[64,2304]{1,0:T(8,128)(2,1)S(1)}, u32[]{:S(2)}, u32[]{:S(2)}) collective-permute-start(bf16[64,2304]{1,0:T(8,128)(2,1)S(1)} %collective-permute-done.5.refs_3_), channel_id=1, source_target_pairs={{0,4},{4,0},{8,12},{12,8},{16,20},{20,16},{24,28},{28,24},{1,5},{5... | collective-permute-start | bytes 884744 | tf_op jit(solution)/shard_map/ppermute | solution.py:19
  27.7 3.3 %collective-permute-start.13 = (bf16[256,2304]{1,0:T(8,128)(2,1)S(1)}, bf16[256,2304]{1,0:T(8,128)(2,1)S(1)}, u32[]{:S(2)}, u32[]{:S(2)}) collective-permute-start(bf16[256,2304]{1,0:T(8,128)(2,1)S(1)} %shard_map.144), channel_id=1, source_target_pairs={{0,4},{4,0},{8,12},{12,8},{16,20},{20,16},{24,28},{28,24},{1,5},{5... | collective-permute-start | bytes 3538952 | tf_op jit(solution)/shard_map/ppermute | solution.py:19
  27.8 3.2 %collective-permute-start.12 = (bf16[256,128]{1,0:T(8,128)(2,1)S(1)}, bf16[256,128]{1,0:T(8,128)(2,1)S(1)}, u32[]{:S(2)}, u32[]{:S(2)}) collective-permute-start(bf16[256,128]{1,0:T(8,128)(2,1)S(1)} %constant_dynamic-update-slice_fusion.table), channel_id=1, source_target_pairs={{0,4},{4,0},{8,12},{12,8},{16,20},{20,16},{24,28},{28,24},{1,5},{5... | collective-permute-start | bytes 196616 | tf_op jit(solution)/shard_map/ppermute | solution.py:19
  32.3 7.7 %collective-permute-start.17 = (bf16[32,2304]{1,0:T(8,128)(2,1)S(1)}, bf16[32,2304]{1,0:T(8,128)(2,1)S(1)}, u32[]{:S(2)}, u32[]{:S(2)}) collective-permute-start(bf16[32,2304]{1,0:T(8,128)(2,1)S(1)} %get-tuple-element.44), channel_id=1, source_target_pairs={{0,24},{4,28},{8,16},{12,20},{16,8},{20,12},{24,0},{28,4},{1,25},{... | collective-permute-start | bytes 442376 | tf_op jit(solution)/shard_map/ppermute | solution.py:19
  33.8 9.4 %collective-permute-start.18 = (bf16[32,2304]{1,0:T(8,128)(2,1)S(1)}, bf16[32,2304]{1,0:T(8,128)(2,1)S(1)}, u32[]{:S(2)}, u32[]{:S(2)}) collective-permute-start(bf16[32,2304]{1,0:T(8,128)(2,1)S(1)} %get-tuple-element.48), channel_id=1, source_target_pairs={{0,8},{4,12},{8,0},{12,4},{16,24},{20,28},{24,16},{28,20},{1,9},{5... | collective-permute-start | bytes 442376 | tf_op jit(solution)/shard_map/ppermute | solution.py:19
  35.3 6.1 %copy-start.2 = (bf16[2304,256]{1,0:T(8,128)(2,1)S(1)}, bf16[2304,256]{1,0:T(8,128)(2,1)}, u32[]{:S(2)}) copy-start(bf16[2304,256]{1,0:T(8,128)(2,1)} %up.1) | copy-start | bytes 3538948
  35.3 6.1 %copy-start.3 = (bf16[256,2304]{1,0:T(8,128)(2,1)S(1)}, bf16[256,2304]{1,0:T(8,128)(2,1)}, u32[]{:S(2)}) copy-start(bf16[256,2304]{1,0:T(8,128)(2,1)} %down.7) | copy-start | bytes 3538948
  35.3 7.9 %collective-permute-start.19 = (bf16[32,2304]{1,0:T(8,128)(2,1)S(1)}, bf16[32,2304]{1,0:T(8,128)(2,1)S(1)}, u32[]{:S(2)}, u32[]{:S(2)}) collective-permute-start(bf16[32,2304]{1,0:T(8,128)(2,1)S(1)} %get-tuple-element.49), channel_id=1, source_target_pairs={{0,16},{4,20},{8,24},{12,28},{16,0},{20,4},{24,8},{28,12},{1,17},{... | collective-permute-start | bytes 442376 | tf_op jit(solution)/shard_map/ppermute | solution.py:19
  37.2 9.1 %collective-permute-start.14 = (bf16[32,2304]{1,0:T(8,128)(2,1)S(1)}, bf16[32,2304]{1,0:T(8,128)(2,1)S(1)}, u32[]{:S(2)}, u32[]{:S(2)}) collective-permute-start(bf16[32,2304]{1,0:T(8,128)(2,1)S(1)} %get-tuple-element.41), channel_id=1, source_target_pairs={{0,8},{4,12},{8,0},{12,4},{16,24},{20,28},{24,16},{28,20},{1,9},{5... | collective-permute-start | bytes 442376 | tf_op jit(solution)/shard_map/ppermute | solution.py:19
  38.1 8.2 %collective-permute-start.15 = (bf16[32,2304]{1,0:T(8,128)(2,1)S(1)}, bf16[32,2304]{1,0:T(8,128)(2,1)S(1)}, u32[]{:S(2)}, u32[]{:S(2)}) collective-permute-start(bf16[32,2304]{1,0:T(8,128)(2,1)S(1)} %get-tuple-element.42), channel_id=1, source_target_pairs={{0,16},{4,20},{8,24},{12,28},{16,0},{20,4},{24,8},{28,12},{1,17},{... | collective-permute-start | bytes 442376 | tf_op jit(solution)/shard_map/ppermute | solution.py:19
  40.0 8.6 %collective-permute-start.16 = (bf16[32,2304]{1,0:T(8,128)(2,1)S(1)}, bf16[32,2304]{1,0:T(8,128)(2,1)S(1)}, u32[]{:S(2)}, u32[]{:S(2)}) collective-permute-start(bf16[32,2304]{1,0:T(8,128)(2,1)S(1)} %get-tuple-element.43), channel_id=1, source_target_pairs={{0,24},{4,28},{8,16},{12,20},{16,8},{20,12},{24,0},{28,4},{1,25},{... | collective-permute-start | bytes 442376 | tf_op jit(solution)/shard_map/ppermute | solution.py:19
  42.8 28.1 %copy-start.6 = (f32[512]{0:T(512)S(1)}, f32[512]{0:T(512)}, u32[]{:S(2)}) copy-start(f32[512]{0:T(512)} %param.23) | copy-start | bytes 6148
  43.3 5.3 %collective-permute-start.20 = (bf16[32,2304]{1,0:T(8,128)(2,1)S(1)}, bf16[32,2304]{1,0:T(8,128)(2,1)S(1)}, u32[]{:S(2)}, u32[]{:S(2)}) collective-permute-start(bf16[32,2304]{1,0:T(8,128)(2,1)S(1)} %add_convert_fusion.5), channel_id=1, source_target_pairs={{0,1},{1,0},{2,3},{3,2},{4,5},{5,4},{6,7},{7,6},{8,9},{9,8},{10,11... | collective-permute-start | bytes 442376 | tf_op jit(solution)/shard_map/ppermute | solution.py:19
  48.7 9.1 %collective-permute-start.21 = (bf16[2,16,2304]{2,1,0:T(8,128)(2,1)S(1)}, bf16[2,16,2304]{2,1,0:T(8,128)(2,1)S(1)}, u32[]{:S(2)}, u32[]{:S(2)}) collective-permute-start(bf16[2,16,2304]{2,1,0:T(8,128)(2,1)S(1)} %bitcast.110), channel_id=1, source_target_pairs={{0,2},{1,3},{2,0},{3,1},{4,6},{5,7},{6,4},{7,5},{8,10},{9,11},{10,... | collective-permute-start | bytes 442376 | tf_op jit(solution)/shard_map/ppermute | solution.py:19
  57.8 5.2 %collective-permute-start.22 = (bf16[32,2304]{1,0:T(8,128)(2,1)S(1)}, bf16[32,2304]{1,0:T(8,128)(2,1)S(1)}, u32[]{:S(2)}, u32[]{:S(2)}) collective-permute-start(bf16[32,2304]{1,0:T(8,128)(2,1)S(1)} %bitcast.105), channel_id=1, source_target_pairs={{0,1},{1,0},{2,3},{3,2},{4,5},{5,4},{6,7},{7,6},{8,9},{9,8},{10,11... | collective-permute-start | bytes 442376 | tf_op jit(solution)/shard_map/ppermute | solution.py:19
  58.6 9.0 %collective-permute-start.27 = (bf16[32,2304]{1,0:T(8,128)(2,1)S(1)}, bf16[32,2304]{1,0:T(8,128)(2,1)S(1)}, u32[]{:S(2)}, u32[]{:S(2)}) collective-permute-start(bf16[32,2304]{1,0:T(8,128)(2,1)S(1)} %bitcast.106), channel_id=1, source_target_pairs={{0,8},{4,12},{8,0},{12,4},{16,24},{20,28},{24,16},{28,20},{1,9},{5... | collective-permute-start | bytes 442376 | tf_op jit(solution)/shard_map/ppermute | solution.py:19
  60.2 9.9 %collective-permute-start.28 = (bf16[32,2304]{1,0:T(8,128)(2,1)S(1)}, bf16[32,2304]{1,0:T(8,128)(2,1)S(1)}, u32[]{:S(2)}, u32[]{:S(2)}) collective-permute-start(bf16[32,2304]{1,0:T(8,128)(2,1)S(1)} %bitcast.107), channel_id=1, source_target_pairs={{0,16},{4,20},{8,24},{12,28},{16,0},{20,4},{24,8},{28,12},{1,17},{... | collective-permute-start | bytes 442376 | tf_op jit(solution)/shard_map/ppermute | solution.py:19
  63.0 7.7 %collective-permute-start.29 = (bf16[32,2304]{1,0:T(8,128)(2,1)S(1)}, bf16[32,2304]{1,0:T(8,128)(2,1)S(1)}, u32[]{:S(2)}, u32[]{:S(2)}) collective-permute-start(bf16[32,2304]{1,0:T(8,128)(2,1)S(1)} %bitcast.108), channel_id=1, source_target_pairs={{0,24},{4,28},{8,16},{12,20},{16,8},{20,12},{24,0},{28,4},{1,25},{... | collective-permute-start | bytes 442376 | tf_op jit(solution)/shard_map/ppermute | solution.py:19
  64.5 9.6 %collective-permute-start.25 = (bf16[32,2304]{1,0:T(8,128)(2,1)S(1)}, bf16[32,2304]{1,0:T(8,128)(2,1)S(1)}, u32[]{:S(2)}, u32[]{:S(2)}) collective-permute-start(bf16[32,2304]{1,0:T(8,128)(2,1)S(1)} %collective-permute-done.22), channel_id=1, source_target_pairs={{0,24},{4,28},{8,16},{12,20},{16,8},{20,12},{24,0},{28,4},{1,25},{... | collective-permute-start | bytes 442376 | tf_op jit(solution)/shard_map/ppermute | solution.py:19
  66.0 8.2 %collective-permute-start.23 = (bf16[32,2304]{1,0:T(8,128)(2,1)S(1)}, bf16[32,2304]{1,0:T(8,128)(2,1)S(1)}, u32[]{:S(2)}, u32[]{:S(2)}) collective-permute-start(bf16[32,2304]{1,0:T(8,128)(2,1)S(1)} %collective-permute-done.22), channel_id=1, source_target_pairs={{0,8},{4,12},{8,0},{12,4},{16,24},{20,28},{24,16},{28,20},{1,9},{5... | collective-permute-start | bytes 442376 | tf_op jit(solution)/shard_map/ppermute | solution.py:19
  67.6 7.3 %collective-permute-start.24 = (bf16[32,2304]{1,0:T(8,128)(2,1)S(1)}, bf16[32,2304]{1,0:T(8,128)(2,1)S(1)}, u32[]{:S(2)}, u32[]{:S(2)}) collective-permute-start(bf16[32,2304]{1,0:T(8,128)(2,1)S(1)} %collective-permute-done.22), channel_id=1, source_target_pairs={{0,16},{4,20},{8,24},{12,28},{16,0},{20,4},{24,8},{28,12},{1,17},{... | collective-permute-start | bytes 442376 | tf_op jit(solution)/shard_map/ppermute | solution.py:19
  70.8 5.8 %collective-permute-start.30 = (bf16[128,2304]{1,0:T(8,128)(2,1)S(1)}, bf16[128,2304]{1,0:T(8,128)(2,1)S(1)}, u32[]{:S(2)}, u32[]{:S(2)}) collective-permute-start(bf16[128,2304]{1,0:T(8,128)(2,1)S(1)} %bitcast.65), channel_id=1, source_target_pairs={{0,4},{4,0},{8,12},{12,8},{16,20},{20,16},{24,28},{28,24},{1,5},{5... | collective-permute-start | bytes 1769480 | tf_op jit(solution)/shard_map/ppermute | solution.py:19
  73.6 3.5 %collective-permute-start.32 = (bf16[128,2304]{1,0:T(8,128)(2,1)S(1)}, bf16[128,2304]{1,0:T(8,128)(2,1)S(1)}, u32[]{:S(2)}, u32[]{:S(2)}) collective-permute-start(bf16[128,2304]{1,0:T(8,128)(2,1)S(1)} %convolution_convert_fusion), channel_id=1, source_target_pairs={{0,4},{4,0},{8,12},{12,8},{16,20},{20,16},{24,28},{28,24},{1,5},{5... | collective-permute-start | bytes 1769480 | tf_op jit(solution)/shard_map/ppermute | solution.py:19
  75.0 4.7 %collective-permute-start.26 = (bf16[128,2304]{1,0:T(8,128)(2,1)S(1)}, bf16[128,2304]{1,0:T(8,128)(2,1)S(1)}, u32[]{:S(2)}, u32[]{:S(2)}) collective-permute-start(bf16[128,2304]{1,0:T(8,128)(2,1)S(1)} %bitcast.63), channel_id=1, source_target_pairs={{0,4},{4,0},{8,12},{12,8},{16,20},{20,16},{24,28},{28,24},{1,5},{5... | collective-permute-start | bytes 1769480 | tf_op jit(solution)/shard_map/ppermute | solution.py:19
  76.0 7.5 %collective-permute-start.31 = (bf16[128,2304]{1,0:T(8,128)(2,1)S(1)}, bf16[128,2304]{1,0:T(8,128)(2,1)S(1)}, u32[]{:S(2)}, u32[]{:S(2)}) collective-permute-start(bf16[128,2304]{1,0:T(8,128)(2,1)S(1)} %convolution_convert_fusion.1), channel_id=1, source_target_pairs={{0,4},{4,0},{8,12},{12,8},{16,20},{20,16},{24,28},{28,24},{1,5},{5... | collective-permute-start | bytes 1769480 | tf_op jit(solution)/shard_map/ppermute | solution.py:19
  77.6 4.8 %collective-permute-start.33 = (bf16[16,128]{1,0:T(8,128)(2,1)S(1)}, bf16[16,128]{1,0:T(8,128)(2,1)S(1)}, u32[]{:S(2)}, u32[]{:S(2)}) collective-permute-start(bf16[16,128]{1,0:T(8,128)(2,1)S(1)} %slice_bitcast_fusion), channel_id=1, source_target_pairs={{0,4},{4,0},{8,12},{12,8},{16,20},{20,16},{24,28},{28,24},{1,5},{5... | collective-permute-start | bytes 12296 | tf_op jit(solution)/shard_map/ppermute | solution.py:19
  77.7 8.3 %collective-permute-start.37 = (bf16[32,2304]{1,0:T(8,128)(2,1)S(1)}, bf16[32,2304]{1,0:T(8,128)(2,1)S(1)}, u32[]{:S(2)}, u32[]{:S(2)}) collective-permute-start(bf16[32,2304]{1,0:T(8,128)(2,1)S(1)} %get-tuple-element.57), channel_id=1, source_target_pairs={{0,8},{4,12},{8,0},{12,4},{16,24},{20,28},{24,16},{28,20},{1,9},{5... | collective-permute-start | bytes 442376 | tf_op jit(solution)/shard_map/ppermute | solution.py:19
  79.1 9.4 %collective-permute-start.38 = (bf16[32,2304]{1,0:T(8,128)(2,1)S(1)}, bf16[32,2304]{1,0:T(8,128)(2,1)S(1)}, u32[]{:S(2)}, u32[]{:S(2)}) collective-permute-start(bf16[32,2304]{1,0:T(8,128)(2,1)S(1)} %get-tuple-element.59), channel_id=1, source_target_pairs={{0,16},{4,20},{8,24},{12,28},{16,0},{20,4},{24,8},{28,12},{1,17},{... | collective-permute-start | bytes 442376 | tf_op jit(solution)/shard_map/ppermute | solution.py:19
  79.6 8.8 %collective-permute-start.39 = (bf16[32,2304]{1,0:T(8,128)(2,1)S(1)}, bf16[32,2304]{1,0:T(8,128)(2,1)S(1)}, u32[]{:S(2)}, u32[]{:S(2)}) collective-permute-start(bf16[32,2304]{1,0:T(8,128)(2,1)S(1)} %get-tuple-element.58), channel_id=1, source_target_pairs={{0,24},{4,28},{8,16},{12,20},{16,8},{20,12},{24,0},{28,4},{1,25},{... | collective-permute-start | bytes 442376 | tf_op jit(solution)/shard_map/ppermute | solution.py:19
  84.0 17.0 %copy-start.7 = (f32[2304]{0:T(1024)S(1)}, f32[2304]{0:T(1024)}, u32[]{:S(2)}) copy-start(f32[2304]{0:T(1024)} %param.25) | copy-start | bytes 27652
  84.1 6.9 %collective-permute-start.34 = (bf16[32,2304]{1,0:T(8,128)(2,1)S(1)}, bf16[32,2304]{1,0:T(8,128)(2,1)S(1)}, u32[]{:S(2)}, u32[]{:S(2)}) collective-permute-start(bf16[32,2304]{1,0:T(8,128)(2,1)S(1)} %get-tuple-element.54), channel_id=1, source_target_pairs={{0,8},{4,12},{8,0},{12,4},{16,24},{20,28},{24,16},{28,20},{1,9},{5... | collective-permute-start | bytes 442376 | tf_op jit(solution)/shard_map/ppermute | solution.py:19
  85.5 9.1 %collective-permute-start.35 = (bf16[32,2304]{1,0:T(8,128)(2,1)S(1)}, bf16[32,2304]{1,0:T(8,128)(2,1)S(1)}, u32[]{:S(2)}, u32[]{:S(2)}) collective-permute-start(bf16[32,2304]{1,0:T(8,128)(2,1)S(1)} %get-tuple-element.56), channel_id=1, source_target_pairs={{0,16},{4,20},{8,24},{12,28},{16,0},{20,4},{24,8},{28,12},{1,17},{... | collective-permute-start | bytes 442376 | tf_op jit(solution)/shard_map/ppermute | solution.py:19
  86.0 8.5 %collective-permute-start.36 = (bf16[32,2304]{1,0:T(8,128)(2,1)S(1)}, bf16[32,2304]{1,0:T(8,128)(2,1)S(1)}, u32[]{:S(2)}, u32[]{:S(2)}) collective-permute-start(bf16[32,2304]{1,0:T(8,128)(2,1)S(1)} %get-tuple-element.55), channel_id=1, source_target_pairs={{0,24},{4,28},{8,16},{12,20},{16,8},{20,12},{24,0},{28,4},{1,25},{... | collective-permute-start | bytes 442376 | tf_op jit(solution)/shard_map/ppermute | solution.py:19
  88.6 6.0 %collective-permute-start.40 = (bf16[32,2304]{1,0:T(8,128)(2,1)S(1)}, bf16[32,2304]{1,0:T(8,128)(2,1)S(1)}, u32[]{:S(2)}, u32[]{:S(2)}) collective-permute-start(bf16[32,2304]{1,0:T(8,128)(2,1)S(1)} %add_convert_fusion.2), channel_id=1, source_target_pairs={{0,1},{1,0},{2,3},{3,2},{4,5},{5,4},{6,7},{7,6},{8,9},{9,8},{10,11... | collective-permute-start | bytes 442376 | tf_op jit(solution)/shard_map/ppermute | solution.py:19
  94.7 6.3 %collective-permute-start.41 = (bf16[16,2304]{1,0:T(8,128)(2,1)S(1)}, bf16[16,2304]{1,0:T(8,128)(2,1)S(1)}, u32[]{:S(2)}, u32[]{:S(2)}) collective-permute-start(bf16[16,2304]{1,0:T(8,128)(2,1)S(1)} %fusion.9), channel_id=1, source_target_pairs={{0,2},{1,3},{2,0},{3,1},{4,6},{5,7},{6,4},{7,5},{8,10},{9,11},{10,... | collective-permute-start | bytes 221192 | tf_op jit(solution)/shard_map/ppermute | solution.py:19
  (5 other events, 14.9 us)
